TPU v7x, 32 devices: a whole 2x2x4 slice. The times are simulated.
32 devices in a mesh: groups: 2 (over y), tensor: 4 (over z), inner: 4 (over x, core).
Axes of the slice: x: 2, y: 2, z: 4, core: 2. Of those that a mesh axis runs over, the one named last changes fastest.
Arguments:
- states: bfloat16 [16, 8192], P(('groups', 'tensor'), 'inner'), parts along dimension 0, may hold values from -6 to 6
- attn_gain: bfloat16 [8192], P('inner'), may hold values from 0.5 to 1.5
- ffn_gain: bfloat16 [8192], P('inner'), may hold values from 0.5 to 1.5
- w_query: bfloat16 [8192, 4096], P('inner', 'tensor'), may hold values from -3 to 3
- w_kv: bfloat16 [8192, 1024], P('inner', 'tensor'), may hold values from -0.0625 to 0.0625
- w_out: bfloat16 [4096, 8192], P('tensor', 'inner'), may hold values from -0.1875 to 0.1875
- w_gate: bfloat16 [8192, 14336], P('inner', 'tensor'), may hold values from -0.0625 to 0.0625
- w_up: bfloat16 [8192, 14336], P('inner', 'tensor'), may hold values from -0.0625 to 0.0625
- w_down: bfloat16 [14336, 8192], P('tensor', 'inner'), may hold values from -0.046875 to 0.046875
- key_cache: bfloat16 [16, 4096, 4, 128], P(('groups', 'tensor'), 'inner'), parts along dimension 0, may hold values from -12 to 12
- value_cache: bfloat16 [16, 4096, 4, 128], P(('groups', 'tensor'), 'inner'), parts along dimension 0, may hold values from -6 to 6
- lengths: int32 [16], P('groups'), parts along dimension 0, may hold values from 1 to 4096, as said below
Outputs:
- result: bfloat16 [16, 8192], P(('groups', 'tensor'), 'inner'), parts along dimension 0
There are 2 independent parts, one for each index of `groups`. A program takes and returns all parts, laid end to end along the dimension named above; an argument that names none is the same for every part. Nothing has to cross between parts.
Inputs may be any that keep to these rules, and one draw needn't show every extreme that they name: `lengths`: some row has exactly 4096 and some row exactly 1.
All inputs are finite; a program needn't handle non-finite values.
Results may differ from a plain program's by a relative error of at most 0.02.
Values may be sent and summed in bfloat16 or wider, within the bound.
No kernel may reach another device: no remote copies, remote signals or barrier semaphores. Data moves between devices by JAX's collectives and lax.ppermute only.
A program may use at most 128 MiB of HBM per device.

v0:
```python
import math

import jax
import jax.numpy as jnp
from jax import lax
from jax.sharding import PartitionSpec as P

D = 8192
HEADS = 32
KV_HEADS = 4
HEAD_DIM = 128


epsilon = 1e-05
rope_base = 500000.0


def rotate(values, positions, pair_index):
    row_total = values.shape[0]
    paired = values.reshape(row_total, -1, 2)
    inverse = jnp.exp(pair_index.astype(jnp.float32) * (-2.0 / HEAD_DIM) * math.log(rope_base))
    angles = positions[:, None] * inverse[None, :]
    cosine = jnp.cos(angles)
    sines = jnp.sin(angles)
    lead_part = paired[:, :, 0]
    tail_part = paired[:, :, 1]
    turned = jnp.stack(
        [lead_part * cosine - tail_part * sines, lead_part * sines + tail_part * cosine], axis=-1
    )
    return turned.reshape(row_total, -1)


def normalize(shard, gain):
    widened = shard.astype(jnp.float32)
    square_sums = lax.psum(jnp.sum(widened * widened, axis=1), "inner")
    scaled = (
        widened * lax.rsqrt(square_sums / D + epsilon)[:, None] * gain.astype(jnp.float32)[None, :]
    )
    return lax.all_gather(scaled.astype(jnp.bfloat16), "tensor", axis=0, tiled=True)


def local(
    states,
    attn_gain,
    ffn_gain,
    w_query,
    w_kv,
    w_out,
    w_gate,
    w_up,
    w_down,
    key_cache,
    value_cache,
    lengths,
):
    tensor_index = lax.axis_index("tensor")
    tensor_count = lax.axis_size("tensor")
    inner_index = lax.axis_index("inner")
    positions = lengths.astype(jnp.float32)
    half_dim = HEAD_DIM // 2
    group_size = HEADS // KV_HEADS
    own_rows = states.shape[0]
    normed = normalize(states, attn_gain)
    query_cols = w_query.shape[1]
    kv_cols = w_kv.shape[1]
    joined = jnp.concatenate(
        [
            jnp.dot(normed, w_query, preferred_element_type=jnp.float32),
            jnp.dot(normed, w_kv, preferred_element_type=jnp.float32),
        ],
        axis=1,
    )
    joined = lax.psum(joined.astype(jnp.bfloat16), "inner").astype(jnp.float32)
    query_part = rotate(joined[:, :query_cols], positions, jnp.arange(query_cols // 2) % half_dim)
    kv_plain = joined[:, query_cols:]
    kv_pairs = (tensor_index * (kv_cols // 2) + jnp.arange(kv_cols // 2)) % half_dim
    kv_turned = rotate(kv_plain, positions, kv_pairs)
    kv_part = jnp.where(tensor_index * kv_cols < KV_HEADS * HEAD_DIM, kv_turned, kv_plain)
    packed = jnp.concatenate([query_part, kv_part], axis=1).astype(jnp.bfloat16)
    received = lax.all_to_all(packed, "tensor", split_axis=0, concat_axis=1, tiled=True)
    received = received.reshape(own_rows, tensor_count, query_cols + kv_cols)
    queries = received[:, :, :query_cols].reshape(own_rows, KV_HEADS, group_size, HEAD_DIM)
    kv_whole = received[:, :, query_cols:].reshape(own_rows, 2, KV_HEADS, HEAD_DIM)
    new_keys = kv_whole[:, 0]
    new_values = kv_whole[:, 1]
    my_lengths = lax.dynamic_slice_in_dim(lengths, tensor_index * own_rows, own_rows, 0)
    score_scale = HEAD_DIM ** (-0.5)
    slot_count = key_cache.shape[1]
    slot_places = inner_index * slot_count + jnp.arange(slot_count)
    usable = slot_places[None, :] < my_lengths[:, None]
    scores = (
        jnp.einsum("rgjd,rsgd->rgjs", queries, key_cache, preferred_element_type=jnp.float32)
        * score_scale
    )
    masked = jnp.where(usable[:, None, None, :], scores, -1e30)
    new_score = (
        jnp.einsum("rgjd,rgd->rgj", queries, new_keys, preferred_element_type=jnp.float32)
        * score_scale
    )
    far_peak = lax.pmax(jnp.max(masked, axis=3), "inner")
    row_peak = jnp.maximum(far_peak, new_score)
    weights = jnp.exp(masked - row_peak[..., None])
    totals = jnp.sum(weights, axis=3).reshape(own_rows, HEADS)
    mixture = jnp.einsum(
        "rgjs,rsgd->rgjd",
        weights.astype(jnp.bfloat16),
        value_cache,
        preferred_element_type=jnp.float32,
    ).reshape(own_rows, HEADS, HEAD_DIM)
    new_weight = jnp.exp(new_score - row_peak)
    new_terms = (
        new_weight.astype(jnp.bfloat16).astype(jnp.float32)[..., None]
        * new_values.astype(jnp.float32)[:, :, None, :]
    )
    new_terms = new_terms.reshape(own_rows, HEADS, HEAD_DIM)
    new_weight = new_weight.reshape(own_rows, HEADS)
    mixture, totals = (
        lax.psum(mixture.astype(jnp.bfloat16), "inner").astype(jnp.float32),
        lax.psum(totals.astype(jnp.bfloat16), "inner").astype(jnp.float32),
    )
    attended = ((mixture + new_terms) / (totals + new_weight)[..., None]).reshape(
        own_rows, HEADS * HEAD_DIM
    )
    attended = attended.astype(jnp.bfloat16)
    head_block = lax.all_to_all(attended, "tensor", split_axis=1, concat_axis=0, tiled=True)
    picked = head_block
    attn_sum = lax.psum_scatter(
        jnp.dot(picked, w_out, preferred_element_type=jnp.float32).astype(jnp.bfloat16),
        "tensor",
        scatter_dimension=0,
        tiled=True,
    ).astype(jnp.float32)
    updated = (states.astype(jnp.float32) + attn_sum).astype(jnp.bfloat16)
    normed_two = normalize(updated, ffn_gain)
    gate_part = jnp.dot(normed_two, w_gate, preferred_element_type=jnp.float32)
    upward_part = jnp.dot(normed_two, w_up, preferred_element_type=jnp.float32)
    gate, upward = (
        lax.psum(gate_part.astype(jnp.bfloat16), "inner").astype(jnp.float32),
        lax.psum(upward_part.astype(jnp.bfloat16), "inner").astype(jnp.float32),
    )
    hidden = (jax.nn.silu(gate) * upward).astype(jnp.bfloat16)
    picked = hidden
    down_sum = lax.psum_scatter(
        jnp.dot(picked, w_down, preferred_element_type=jnp.float32).astype(jnp.bfloat16),
        "tensor",
        scatter_dimension=0,
        tiled=True,
    ).astype(jnp.float32)
    return (updated.astype(jnp.float32) + down_sum).astype(jnp.bfloat16)


def solution(mesh):
    in_specs = (
        P(("groups", "tensor"), "inner"),
        P("inner"),
        P("inner"),
        P("inner", "tensor"),
        P("inner", "tensor"),
        P("tensor", "inner"),
        P("inner", "tensor"),
        P("inner", "tensor"),
        P("tensor", "inner"),
        P(("groups", "tensor"), "inner", None, None),
        P(("groups", "tensor"), "inner", None, None),
        P("groups"),
    )
    out_specs = P(("groups", "tensor"), "inner")
    return jax.shard_map(local, mesh=mesh, in_specs=in_specs, out_specs=out_specs, check_vma=False)
```

profile of v0, /device:TPU:0, one launch (start us, length us, event | category | flops | bytes accessed | tf_op | source)
XLA Modules:
  0.0 204.5 jit_solution(12646704145163433732)
XLA Ops:
  6.5 0.0 copy-start
  6.5 0.0 copy-start.1
  6.5 1.0 fusion.38
  7.5 0.7 convert_element_type.119
  8.2 8.3 %psum.49 = f32[2]{0:T(128)S(1)} all-reduce(f32[2]{0:T(128)S(1)} %fusion.38), channel_id=1, replica_groups=mesh['groups'=2,'tensor'=4,'inner'=4] {'inner'}, use_global_device_ids=true, to_apply=%region_1.0 | all-reduce | flops 2 | bytes 16 | tf_op jit(solution)/shard_map/psum | solution.py:35
  16.5 0.8 fusion.50
  17.3 13.4 %all-gather = bf16[4,2,2048]{2,1,0:T(2,128)(2,1)S(1)} all-gather(bf16[1,2,2048]{2,1,0:T(2,128)(2,1)S(1)} %fusion.50), channel_id=1, replica_groups=mesh['groups'=2,'tensor'=4,'inner'=4] {'tensor'}, dimensions={0}, use_global_device_ids=true | all-gather | bytes 40960 | tf_op jit(solution)/shard_map/all_gather | solution.py:39
  30.7 2.8 %convolution_convert_fusion.4 = bf16[8,1024]{1,0:T(8,128)(2,1)S(1)} fusion(bf16[8,2048]{1,0:T(8,128)(2,1)S(1)} %reshape.300, bf16[2048,1024]{1,0:T(8,128)(2,1)} %param.15), kind=kOutput, calls=%fused_computation.11 | convolution fusion | flops 33562624 | bytes 4243456 | tf_op jit(solution)/shard_map/dot_general | solution.py:68
  33.5 0.0 copy-done.1
  33.5 0.2 convolution_convert_fusion.5
  33.8 10.3 %psum.50 = bf16[8,1280]{1,0:T(8,128)(2,1)S(1)} all-reduce(bf16[8,1280]{1,0:T(8,128)(2,1)S(1)} %pad_maximum_fusion), channel_id=1, replica_groups=mesh['groups'=2,'tensor'=4,'inner'=4] {'inner'}, use_global_device_ids=true, to_apply=%region_2.0 | all-reduce | flops 10240 | bytes 40960 | tf_op jit(solution)/shard_map/psum | solution.py:73
  44.1 0.1 copy.55
  44.2 0.1 fusion.72
  44.4 0.1 copy.71
  44.5 0.0 copy-done.4
  44.5 0.1 fusion.55
  44.6 0.1 copy.58
  44.8 0.1 copy.59
  44.9 0.2 copy.51
  45.1 0.4 fusion.71
  45.5 0.0 copy-start.3
  45.5 0.0 copy-start.5
  45.5 0.1 copy.68
  45.6 0.1 copy.69
  45.7 0.2 fusion.35
  45.9 0.5 copy.54
  46.4 1.6 concatenate.14
  48.0 0.6 pad_maximum_fusion.1
  48.6 4.6 %all-to-all-start = ((bf16[4,2,1280]{2,1,0:T(2,128)(2,1)}), bf16[4,2,1280]{2,1,0:T(2,128)(2,1)S(1)}, u32[]{:S(2)}, u32[]{:S(2)}) async-start(bf16[4,2,1280]{2,1,0:T(2,128)(2,1)} %pad_maximum_fusion.1), calls=%async_computation | async-start | bytes 40960 | tf_op jit(solution)/shard_map/all_to_all | solution.py:80
  53.3 0.1 dynamic_slice.3
  53.4 0.1 broadcast_compare_fusion
  53.4 5.5 %all-to-all-done = bf16[4,2,1280]{2,1,0:T(2,128)(2,1)S(1)} async-done(((bf16[4,2,1280]{2,1,0:T(2,128)(2,1)}), bf16[4,2,1280]{2,1,0:T(2,128)(2,1)S(1)}, u32[]{:S(2)}, u32[]{:S(2)}) %all-to-all-start) | async-done | bytes 20512 | tf_op jit(solution)/shard_map/all_to_all | solution.py:80
  59.0 0.1 fusion.46
  59.1 0.0 copy-done
  59.1 0.7 fusion.73
  59.9 6.0 %pmax.7 = f32[2,4,8]{2,1,0:T(4,128)S(1)} all-reduce(f32[2,4,8]{2,1,0:T(4,128)S(1)} %get-tuple-element.24), channel_id=1, replica_groups=mesh['groups'=2,'tensor'=4,'inner'=4] {'inner'}, use_global_device_ids=true, to_apply=%region_4.5 | all-reduce | flops 64 | bytes 512 | tf_op jit(solution)/shard_map/pmax | solution.py:100
  65.8 0.2 fusion.16
  66.0 0.1 convert_element_type.133
  66.1 2.1 %fusion.13 = bf16[2,32,128]{2,1,0:T(8,128)(2,1)S(1)} fusion(bf16[2,1024,4,128]{3,2,1,0:T(4,128)(2,1)} %param.22, f32[2,4,8,1024]{3,2,1,0:T(8,128)S(1)} %get-tuple-element.25, f32[2,4,8]{2,1,0:T(4,128)S(1)} %get-tuple-element.21), kind=kOutput, calls=%fused_computation.12 | convolution fusion | flops 16916480 | bytes 2375936 | tf_op jit(solution)/shard_map/rgjs,rsgd->rgjd/dot_general | solution.py:104
  68.2 0.1 reshape.296
  68.3 0.1 reshape.297
  68.4 10.3 %all-reduce.3 = (bf16[2,32,128]{2,1,0:T(8,128)(2,1)S(1)}, bf16[2,32]{1,0:T(2,128)(2,1)S(1)}) all-reduce(bf16[2,32,128]{2,1,0:T(8,128)(2,1)S(1)} %fusion.13, bf16[2,32]{1,0:T(2,128)(2,1)S(1)} %convert_element_type.133), channel_id=1, replica_groups=mesh['groups'=2,'tensor'=4,'inner'=4] {'inner'}, use_global_device_ids=true, to_apply=%region_5.6 | all-reduce | flops 8256 | bytes 33024 | tf_op jit(solution)/shard_map/psum | solution.py:118
  78.6 0.1 fusion.29
  78.7 0.6 copy.64
  79.3 3.2 %all-to-all-start.1 = ((bf16[2,4,1024]{2,0,1:T(2,128)(2,1)}), bf16[2,4,1024]{2,0,1:T(2,128)(2,1)S(1)}, u32[]{:S(2)}, u32[]{:S(2)}) async-start(bf16[2,4,1024]{2,0,1:T(2,128)(2,1)} %copy.64), calls=%async_computation.1 | async-start | bytes 32768 | tf_op jit(solution)/shard_map/all_to_all | solution.py:125
  82.6 0.0 all-reduce.6.cloned.1.call-start
  82.7 0.0 copy-done.3
  82.7 0.0 copy-done.5
  82.7 0.6 dynamic-slice
  83.9 4.2 %all-to-all-done.1 = bf16[2,4,1024]{2,0,1:T(2,128)(2,1)S(1)} async-done(((bf16[2,4,1024]{2,0,1:T(2,128)(2,1)}), bf16[2,4,1024]{2,0,1:T(2,128)(2,1)S(1)}, u32[]{:S(2)}, u32[]{:S(2)}) %all-to-all-start.1) | async-done | bytes 16416 | tf_op jit(solution)/shard_map/all_to_all | solution.py:125
  88.2 2.8 %convolution_convert_fusion.3 = bf16[8,2048]{1,0:T(8,128)(2,1)S(1)} fusion(bf16[8,1024]{1,0:T(8,128)(2,1)S(1)} %all_to_all.26, bf16[1024,2048]{1,0:T(8,128)(2,1)} %param.17), kind=kOutput, calls=%fused_computation.3 | convolution fusion | flops 33570816 | bytes 4243456 | tf_op jit(solution)/shard_map/dot_general | solution.py:128
  91.0 16.3 %all-reduce = bf16[8,2048]{1,0:T(8,128)(2,1)S(1)} all-reduce(bf16[8,2048]{1,0:T(8,128)(2,1)S(1)} %convolution_convert_fusion.3), channel_id=2, replica_groups=mesh['groups'=2,'tensor'=4,'inner'=4] {'tensor'}, use_global_device_ids=true, to_apply=%region_8.9.clone | all-reduce | flops 16384 | bytes 65536
  107.3 0.0 copy-done.2
  107.4 0.1 fusion.42
  107.5 5.7 %psum.53 = f32[2]{0:T(128)S(1)} all-reduce(f32[2]{0:T(128)S(1)} %get-tuple-element.9), channel_id=1, replica_groups=mesh['groups'=2,'tensor'=4,'inner'=4] {'inner'}, use_global_device_ids=true, to_apply=%region_10.11 | all-reduce | flops 2 | bytes 16 | tf_op jit(solution)/shard_map/psum | solution.py:35
  113.2 0.1 fusion.49
  113.2 13.1 %all-gather.1 = bf16[4,2,2048]{2,1,0:T(2,128)(2,1)S(1)} all-gather(bf16[1,2,2048]{2,1,0:T(2,128)(2,1)S(1)} %fusion.49), channel_id=1, replica_groups=mesh['groups'=2,'tensor'=4,'inner'=4] {'tensor'}, dimensions={0}, use_global_device_ids=true | all-gather | bytes 40960 | tf_op jit(solution)/shard_map/all_gather | solution.py:39
  126.4 7.8 %convolution_convert_fusion = bf16[8,3584]{1,0:T(8,128)(2,1)} fusion(bf16[8,2048]{1,0:T(8,128)(2,1)S(1)} %reshape.302, bf16[2048,3584]{1,0:T(8,128)(2,1)} %param.19), kind=kOutput, calls=%fused_computation | convolution fusion | flops 117469184 | bytes 14770176 | tf_op jit(solution)/shard_map/dot_general | solution.py:136
  134.2 7.8 %convolution_convert_fusion.1 = bf16[8,3584]{1,0:T(8,128)(2,1)} fusion(bf16[8,2048]{1,0:T(8,128)(2,1)S(1)} %reshape.302, bf16[2048,3584]{1,0:T(8,128)(2,1)} %param.18), kind=kOutput, calls=%fused_computation.1 | convolution fusion | flops 117469184 | bytes 14770176 | tf_op jit(solution)/shard_map/dot_general | solution.py:135
  142.0 0.0 all-reduce.6.cloned.1.call-update
  142.0 28.8 %all-reduce.6.cloned.1.call-done = (bf16[8,3584]{1,0:T(8,128)(2,1)}, bf16[8,3584]{1,0:T(8,128)(2,1)}) async-done(((bf16[8,3584]{1,0:T(8,128)(2,1)}, bf16[8,3584]{1,0:T(8,128)(2,1)}), (bf16[8,3584]{1,0:T(8,128)(2,1)}, bf16[8,3584]{1,0:T(8,128)(2,1)})) %all-reduce.6.cloned.1.call-update) | async-done | bytes 114704 | tf_op jit(solution)/shard_map/psum | solution.py:139
  170.8 7.2 %convolution_convert_fusion.2 = bf16[8,2048]{1,0:T(8,128)(2,1)S(1)} fusion(bf16[3584,2048]{1,0:T(8,128)(2,1)} %param.20, bf16[8,3584]{1,0:T(8,128)(2,1)} %get-tuple-element.5, bf16[8,3584]{1,0:T(8,128)(2,1)} %get-tuple-element.6), kind=kOutput, calls=%fused_computation.2 | convolution fusion | flops 117686272 | bytes 14827520 | tf_op jit(solution)/shard_map/dot_general | solution.py:144
  178.0 19.0 %all-reduce.1 = bf16[8,2048]{1,0:T(8,128)(2,1)S(1)} all-reduce(bf16[8,2048]{1,0:T(8,128)(2,1)S(1)} %convolution_convert_fusion.2), channel_id=3, replica_groups=mesh['groups'=2,'tensor'=4,'inner'=4] {'tensor'}, use_global_device_ids=true, to_apply=%region_13.14.clone | all-reduce | flops 16384 | bytes 65536
  197.0 0.6 fusion.45
  (29 shorter events, 0.3 us)
Async XLA Ops:
  6.5 52.6 %copy-start = (bf16[2,1024,4,128]{3,2,1,0:T(4,128)(2,1)S(1)}, bf16[2,1024,4,128]{3,2,1,0:T(4,128)(2,1)}, u32[]{:S(2)}) copy-start(bf16[2,1024,4,128]{3,2,1,0:T(4,128)(2,1)} %param.21) | copy-start | bytes 6291460
  6.5 27.0 %copy-start.1 = (bf16[2048,256]{1,0:T(8,128)(2,1)S(1)}, bf16[2048,256]{1,0:T(8,128)(2,1)}, u32[]{:S(2)}) copy-start(bf16[2048,256]{1,0:T(8,128)(2,1)} %param.16) | copy-start | bytes 3145732
  6.5 38.0 %copy-start.4 = (s32[8]{0:T(128)S(1)}, s32[8]{0:T(128)}, u32[]{:S(2)}) copy-start(s32[8]{0:T(128)} %param.23) | copy-start | bytes 100
  45.5 37.2 %copy-start.3 = (bf16[2048]{0:T(1024)(128)(2,1)S(1)}, bf16[2048]{0:T(1024)(128)(2,1)}, u32[]{:S(2)}) copy-start(bf16[2048]{0:T(1024)(128)(2,1)} %param.14) | copy-start | bytes 12292
  45.5 37.2 %copy-start.5 = (u32[32]{0:T(128)S(1)}, u32[32]{0:T(128)}, u32[]{:S(2)}) copy-start(u32[32]{0:T(128)} %constant.74) | copy-start | bytes 388
  48.6 10.3 %all-to-all-start = ((bf16[4,2,1280]{2,1,0:T(2,128)(2,1)}), bf16[4,2,1280]{2,1,0:T(2,128)(2,1)S(1)}, u32[]{:S(2)}, u32[]{:S(2)}) async-start(bf16[4,2,1280]{2,1,0:T(2,128)(2,1)} %pad_maximum_fusion.1), calls=%async_computation | async-start | bytes 40960 | tf_op jit(solution)/shard_map/all_to_all | solution.py:80
  59.9 47.5 %copy-start.2 = (bf16[2,2048]{1,0:T(2,128)(2,1)S(1)}, bf16[2,2048]{1,0:T(2,128)(2,1)}, u32[]{:S(2)}) copy-start(bf16[2,2048]{1,0:T(2,128)(2,1)} %param.12) | copy-start | bytes 24580
  79.3 8.8 %all-to-all-start.1 = ((bf16[2,4,1024]{2,0,1:T(2,128)(2,1)}), bf16[2,4,1024]{2,0,1:T(2,128)(2,1)S(1)}, u32[]{:S(2)}, u32[]{:S(2)}) async-start(bf16[2,4,1024]{2,0,1:T(2,128)(2,1)} %copy.64), calls=%async_computation.1 | async-start | bytes 32768 | tf_op jit(solution)/shard_map/all_to_all | solution.py:125
  82.6 88.2 %all-reduce.6.cloned.1.call-start = ((), (), s32[]{:S(2)}) async-start(), calls=%async_computation.2 | async-start | bytes 229376 | tf_op jit(solution)/shard_map/psum | solution.py:139
Sparse Core Ops, SparseCore 0:
  142.1 28.6 all-reduce.5
where the time goes:
time: 205 us
  blocking collectives  102 us (50%)
  waiting for transfers between devices  38.5 us (19%)
  matrix products  31.7 us (15%)
  between operations  14.3 us (7%)
  starting transfers between devices  7.94 us (4%)
  local copies, waits for them, and re-layouts  5.14 us (3%)
  other arithmetic  4.66 us (2%)
    unnamed x2, blocking collectives  35.3 us
    psum x1, waiting for transfers between devices, local(): lax.psum(upward_part.astype(jnp.bfloat16), 'inner').astype(jnp.float32)  28.8 us
    all_gather x2, blocking collectives, normalize(): lax.all_gather(scaled.astype(jnp.bfloat16), 'tensor', axis=0, tiled=True)  26.5 us
    psum x2, blocking collectives, normalize(): square_sums = lax.psum(jnp.sum(widened * widened, axis=1), 'inner')  14 us
    psum x1, blocking collectives, local(): joined = lax.psum(joined.astype(jnp.bfloat16), 'inner').astype(jnp.float32)  10.3 us
    psum x1, blocking collectives, local(): lax.psum(mixture.astype(jnp.bfloat16), 'inner').astype(jnp.float32)  10.3 us
    dot_general x1, matrix products, local(): upward_part = jnp.dot(normed_two, w_up, preferred_element_type=jnp.float32)  7.79 us
    dot_general x1, matrix products, local(): gate_part = jnp.dot(normed_two, w_gate, preferred_element_type=jnp.float32)  7.79 us
  transfers between devices with their start and end apart: 3, of which 3 were waited for; matrix products, arithmetic and copies ran while one was open for 0% of the time, Pallas kernels for 0%

commit v1 on v0

v1 whole, which is shorter than its diff:
```python
import math

import jax
import jax.numpy as jnp
from jax import lax
from jax.sharding import PartitionSpec as P

D = 8192
HEADS = 32
KV_HEADS = 4
HEAD_DIM = 128

epsilon = 1e-05
rope_base = 500000.0


def swap_with(value, axis, step):
    count = lax.axis_size(axis)
    return lax.ppermute(value, axis, [(i, i ^ step) for i in range(count)])


def exchange(value, axis):
    return [value] + [swap_with(value, axis, k) for k in range(1, lax.axis_size(axis))]


def scatter_slots(pieces, axis):
    return [pieces[0]] + [swap_with(pieces[k], axis, k) for k in range(1, len(pieces))]


def unslot(stacked, index):
    count = stacked.shape[0]
    bit = 1
    while bit < count:
        shape = (count // (2 * bit), 2, bit) + stacked.shape[1:]
        turned = stacked.reshape(shape)[:, ::-1].reshape(stacked.shape)
        stacked = jnp.where((index & bit) != 0, turned, stacked)
        bit *= 2
    return stacked


def rotate(values, positions):
    inverse = jnp.exp(
        jnp.arange(HEAD_DIM // 2).astype(jnp.float32) * (-2.0 / HEAD_DIM) * math.log(rope_base)
    )
    angles = positions[:, None] * inverse[None, :]
    cosine = jnp.repeat(jnp.cos(angles), 2, axis=1)[:, None, :]
    sines = jnp.repeat(jnp.sin(angles), 2, axis=1)[:, None, :]
    even = (jnp.arange(HEAD_DIM) % 2 == 0)[None, None, :]
    other = jnp.where(even, -jnp.roll(values, -1, axis=-1), jnp.roll(values, 1, axis=-1))
    return values * cosine + other * sines


def local(
    states,
    attn_gain,
    ffn_gain,
    w_query,
    w_kv,
    w_out,
    w_gate,
    w_up,
    w_down,
    key_cache,
    value_cache,
    lengths,
):
    tensor_index = lax.axis_index("tensor")
    tensor_count = lax.axis_size("tensor")
    inner_index = lax.axis_index("inner")
    own_rows = states.shape[0]
    all_rows = own_rows * tensor_count
    group_size = HEADS // KV_HEADS
    query_cols = w_query.shape[1]

    own = states.astype(jnp.float32)
    squares = exchange(jnp.sum(own * own, axis=1), "inner")
    rows = jnp.concatenate(exchange(states, "tensor"), axis=0)
    scaled = (rows.astype(jnp.float32) * attn_gain.astype(jnp.float32)[None, :]).astype(jnp.bfloat16)
    joined = jnp.concatenate(
        [
            jnp.dot(scaled, w_query, preferred_element_type=jnp.float32),
            jnp.dot(scaled, w_kv, preferred_element_type=jnp.float32),
        ],
        axis=1,
    ).astype(jnp.bfloat16)
    joined = joined.reshape(tensor_count, own_rows, -1)
    got = scatter_slots([joined[k] for k in range(tensor_count)], "tensor")
    partial = exchange(jnp.stack(got), "inner")
    total = sum(p.astype(jnp.float32) for p in partial)
    scale = lax.rsqrt(sum(squares) / D + epsilon)
    total = unslot(total, tensor_index) * scale[None, :, None]
    total = total.transpose(1, 0, 2)
    my_lengths = lax.dynamic_slice_in_dim(lengths, tensor_index * own_rows, own_rows, 0)
    positions = my_lengths.astype(jnp.float32)
    queries = rotate(total[:, :, :query_cols].reshape(own_rows, HEADS, HEAD_DIM), positions)
    queries = queries.astype(jnp.bfloat16).reshape(own_rows, KV_HEADS, group_size, HEAD_DIM)
    kv_whole = total[:, :, query_cols:].reshape(own_rows, 2 * KV_HEADS, HEAD_DIM)
    new_keys = rotate(kv_whole[:, :KV_HEADS], positions).astype(jnp.bfloat16)
    new_values = kv_whole[:, KV_HEADS:].astype(jnp.bfloat16)

    score_scale = HEAD_DIM ** (-0.5)
    slot_count = key_cache.shape[1]
    slot_places = inner_index * slot_count + jnp.arange(slot_count)
    usable = slot_places[None, :] < my_lengths[:, None]
    scores = (
        jnp.einsum("rgjd,rsgd->rgjs", queries, key_cache, preferred_element_type=jnp.float32)
        * score_scale
    )
    masked = jnp.where(usable[:, None, None, :], scores, -1e30)
    new_score = (
        jnp.einsum("rgjd,rgd->rgj", queries, new_keys, preferred_element_type=jnp.float32)
        * score_scale
    )
    new_score = jnp.where(inner_index == 0, new_score, -1e30)
    peak = jnp.maximum(jnp.max(masked, axis=3), new_score)
    weights = jnp.exp(masked - peak[..., None])
    new_weight = jnp.exp(new_score - peak)
    totals = jnp.sum(weights, axis=3) + new_weight
    mixture = jnp.einsum(
        "rgjs,rsgd->rgjd",
        weights.astype(jnp.bfloat16),
        value_cache,
        preferred_element_type=jnp.float32,
    )
    mixture = mixture + (
        new_weight.astype(jnp.bfloat16).astype(jnp.float32)[..., None]
        * new_values.astype(jnp.float32)[:, :, None, :]
    )
    peak = peak.reshape(own_rows, HEADS, 1)
    totals = totals.reshape(own_rows, HEADS, 1)
    mixture = mixture.reshape(own_rows, HEADS, HEAD_DIM)
    wide = jnp.concatenate(
        [
            mixture,
            jnp.broadcast_to(totals, (own_rows, HEADS, HEAD_DIM // 2)),
            jnp.broadcast_to(peak, (own_rows, HEADS, HEAD_DIM // 2)),
        ],
        axis=2,
    )
    shards = exchange(wide, "inner")
    peaks = [s[:, :, HEAD_DIM + HEAD_DIM // 2 :][:, :, :1] for s in shards]
    top = peaks[0]
    for p in peaks[1:]:
        top = jnp.maximum(top, p)
    factors = [jnp.exp(p - top) for p in peaks]
    mixed = sum(s[:, :, :HEAD_DIM] * f for s, f in zip(shards, factors))
    denominator = sum(s[:, :, HEAD_DIM : HEAD_DIM + 1] * f for s, f in zip(shards, factors))
    attended = (mixed / denominator).astype(jnp.bfloat16)
    attended = attended.reshape(own_rows, tensor_count, -1).transpose(1, 0, 2)
    attended = unslot(attended, tensor_index)
    picked = scatter_slots([attended[k] for k in range(tensor_count)], "tensor")
    picked = jnp.concatenate(picked, axis=0)

    part = jnp.dot(picked, w_out, preferred_element_type=jnp.float32).astype(jnp.bfloat16)
    parts = exchange(part.reshape(tensor_count, own_rows, -1), "tensor")
    attn_sum = jnp.stack(
        [
            sum(parts[k][s ^ k].astype(jnp.float32) for k in range(tensor_count))
            for s in range(tensor_count)
        ]
    ).reshape(all_rows, -1)
    updated = (rows.astype(jnp.float32) + attn_sum).astype(jnp.bfloat16)
    wide_updated = updated.astype(jnp.float32)
    squares = exchange(jnp.sum(wide_updated * wide_updated, axis=1), "inner")
    scaled = (wide_updated * ffn_gain.astype(jnp.float32)[None, :]).astype(jnp.bfloat16)
    gates = exchange(
        jnp.dot(scaled, w_gate, preferred_element_type=jnp.float32).astype(jnp.bfloat16), "inner"
    )
    ups = exchange(
        jnp.dot(scaled, w_up, preferred_element_type=jnp.float32).astype(jnp.bfloat16), "inner"
    )
    scale = lax.rsqrt(sum(squares) / D + epsilon)[:, None]
    gate = sum(g.astype(jnp.float32) for g in gates) * scale
    upward = sum(u.astype(jnp.float32) for u in ups) * scale
    hidden = (jax.nn.silu(gate) * upward).astype(jnp.bfloat16)
    part = jnp.dot(hidden, w_down, preferred_element_type=jnp.float32).astype(jnp.bfloat16)
    part = part.reshape(tensor_count, own_rows, -1)
    parts = scatter_slots([part[k] for k in range(tensor_count)], "tensor")
    down_sum = sum(p.astype(jnp.float32) for p in parts)
    return (wide_updated[:own_rows] + down_sum).astype(jnp.bfloat16)


def solution(mesh):
    in_specs = (
        P(("groups", "tensor"), "inner"),
        P("inner"),
        P("inner"),
        P("inner", "tensor"),
        P("inner", "tensor"),
        P("tensor", "inner"),
        P("inner", "tensor"),
        P("inner", "tensor"),
        P("tensor", "inner"),
        P(("groups", "tensor"), "inner", None, None),
        P(("groups", "tensor"), "inner", None, None),
        P("groups"),
    )
    out_specs = P(("groups", "tensor"), "inner")
    return jax.shard_map(local, mesh=mesh, in_specs=in_specs, out_specs=out_specs, check_vma=False)
```

time: 205 us -> 93.6 us (0.46)
  blocking collectives: 102 us -> 0 us
  starting transfers between devices: 7.94 us -> 33.6 us
  between operations: 14.3 us -> 0.4 us
  waiting for transfers between devices: 38.5 us -> 26 us
  matrix products: 31.7 us -> 26.8 us
  local copies, waits for them, and re-layouts: 5.14 us -> 1.86 us
    unnamed x2 -> x0, blocking collectives: 35.3 us -> none
    psum x4 -> x0, blocking collectives: 34.5 us -> none  [the longest x2 14 us: normalize(): square_sums = lax.psum(jnp.sum(widened * widened, axis=1), 'inner')]
    ppermute x0 -> x33, starting transfers between devices: none -> 33.6 us  [swap_with(): return lax.ppermute(value, axis, [(i, i ^ step) for i in range(count)])]
    psum x1 -> x0, waiting for transfers between devices: 28.8 us -> none  [local(): lax.psum(upward_part.astype(jnp.bfloat16), 'inner').astype(jnp.float32)]
    all_gather x2 -> x0, blocking collectives: 26.5 us -> none  [normalize(): lax.all_gather(scaled.astype(jnp.bfloat16), 'tensor', axis=0, tiled=True)]
    ppermute x0 -> x33, waiting for transfers between devices: none -> 26 us  [swap_with(): return lax.ppermute(value, axis, [(i, i ^ step) for i in range(count)])]
    all_to_all x2 -> x0, waiting for transfers between devices: 9.71 us -> none  [the longest x1 5.47 us: local(): lax.all_to_all(packed, 'tensor', split_axis=0, concat_axis=1, tiled=True)]
    all_to_all x2 -> x0, starting transfers between devices: 7.89 us -> none  [the longest x1 4.65 us: local(): lax.all_to_all(packed, 'tensor', split_axis=0, concat_axis=1, tiled=True)]
  transfers between devices with their start and end apart: 3 -> 33, of which waited for: 3 -> 16; matrix products, arithmetic and copies ran while one was open for 0% -> 23% of each run, Pallas kernels for 0% -> 0%
where the time goes in v1:
time: 93.6 us; the launch traced here: 93.3 us
  starting transfers between devices  33.6 us (36%)
  matrix products  26.8 us (29%)
  waiting for transfers between devices  26 us (28%)
  other arithmetic  4.6 us (5%)
  local copies, waits for them, and re-layouts  1.86 us (2%)
    ppermute x33, starting transfers between devices, swap_with(): return lax.ppermute(value, axis, [(i, i ^ step) for i in range(count)])  33.6 us
    ppermute x33, waiting for transfers between devices, swap_with(): return lax.ppermute(value, axis, [(i, i ^ step) for i in range(count)])  26 us
    dot_general x1, matrix products, local(): jnp.dot(scaled, w_up, preferred_element_type=jnp.float32)  7.31 us
    dot_general x1, matrix products, local(): jnp.dot(scaled, w_gate, preferred_element_type=jnp.float32)  7.31 us
    dot_general x1, matrix products, local(): jnp.dot(scaled, w_query, preferred_element_type=jnp.float32)  2.87 us
    dot_general x1, matrix products, local(): jnp.dot(picked, w_out, preferred_element_type=jnp.float32)  2.84 us
    dot_general x1, matrix products, local(): jnp.einsum('rgjs,rsgd->rgjd', weights.astype(jnp.bfloat16), value_cache,...  2.08 us
    dot_general x1, matrix products, local(): jnp.dot(hidden, w_down, preferred_element_type=jnp.float32)  2.06 us
  transfers between devices with their start and end apart: 33, of which 16 were waited for; matrix products, arithmetic and copies ran while one was open for 23% of the time, Pallas kernels for 0%

profile of v1, /device:TPU:0, one launch (start us, length us, event | category | flops | bytes accessed | tf_op | source)
XLA Modules:
  0.0 93.3 jit_solution(10919759137106975877)
XLA Ops:
  0.0 1.0 %multiply_reduce_fusion.1 = f32[2]{0:T(128)S(1)} fusion(bf16[2,2048]{1,0:T(2,128)(2,1)} %param.12), kind=kLoop, calls=%fused_computation.93 | loop fusion | flops 12286 | bytes 8200 | tf_op jit(solution)/shard_map/reduce_sum | solution.py:76
  1.0 2.4 %collective-permute-start.11 = (f32[2]{0:T(128)S(1)}, f32[2]{0:T(128)S(1)}, u32[]{:S(2)}, u32[]{:S(2)}) collective-permute-start(f32[2]{0:T(128)S(1)} %multiply_reduce_fusion.1), channel_id=1, source_target_pairs={{0,3},{1,2},{2,1},{3,0},{4,7},{5,6},{6,5},{7,4},{8,11},{9,10},{10,... | collective-permute-start | bytes 32 | tf_op jit(solution)/shard_map/ppermute | solution.py:19
  3.4 0.6 collective-permute-start.10
  4.1 3.6 %collective-permute-start.2 = (bf16[2,2048]{1,0:T(2,128)(2,1)}, bf16[2,2048]{1,0:T(2,128)(2,1)S(1)}, u32[]{:S(2)}, u32[]{:S(2)}) collective-permute-start(bf16[2,2048]{1,0:T(2,128)(2,1)} %param.12), channel_id=1, source_target_pairs={{0,12},{4,8},{8,4},{12,0},{1,13},{5,9},{9,5},{13,1},{2,14},{6,10},... | collective-permute-start | bytes 24584 | tf_op jit(solution)/shard_map/ppermute | solution.py:19
  7.7 0.8 collective-permute-start
  8.5 0.7 fusion.79
  9.3 0.1 multiply_cosine_fusion
  9.4 0.7 convert_element_type.215
  10.1 2.3 %collective-permute-done.1 = bf16[2,2048]{1,0:T(2,128)(2,1)S(1)} collective-permute-done((bf16[2,2048]{1,0:T(2,128)(2,1)}, bf16[2,2048]{1,0:T(2,128)(2,1)S(1)}, u32[]{:S(2)}, u32[]{:S(2)}) %collective-permute-start.1) | collective-permute-done | bytes 8224 | tf_op jit(solution)/shard_map/ppermute | solution.py:19
  12.4 1.5 %convolution_convert_fusion.5 = bf16[8,256]{1,0:T(8,128)(2,1)S(1)} fusion(bf16[2048,256]{1,0:T(8,128)(2,1)} %param.16, f32[2048]{0:T(1024)S(1)} %convert_element_type.215, bf16[2,2048]{1,0:T(2,128)(2,1)S(1)} %collective-permute-done.2, bf16[2,2048]{1,0:T(2,128)(2,1)S(1)} %collective-permute-done.1, bf16[2,2048]{1,0:T(2,128)(2,1)S(1)} %collective-permute-done, ...), kind=kOutput, calls=%fused_computation.13 | convolution fusion | flops 8554496 | bytes 1093632 | tf_op jit(solution)/shard_map/dot_general | solution.py:82
  13.9 2.9 %convolution_convert_fusion.4 = bf16[8,1024]{1,0:T(8,128)(2,1)S(1)} fusion(bf16[2048,1024]{1,0:T(8,128)(2,1)} %param.15, f32[2048]{0:T(1024)S(1)} %convert_element_type.215, bf16[2,2048]{1,0:T(2,128)(2,1)S(1)} %collective-permute-done.2, bf16[2,2048]{1,0:T(2,128)(2,1)S(1)} %collective-permute-done.1, bf16[2,2048]{1,0:T(2,128)(2,1)S(1)} %collective-permute-done, ...), kind=kOutput, calls=%fused_computation.12 | convolution fusion | flops 33726464 | bytes 4251648 | tf_op jit(solution)/shard_map/dot_general | solution.py:81
  16.9 3.5 %collective-permute-start.5 = (bf16[2,1280]{1,0:T(2,128)(2,1)S(1)}, bf16[2,1280]{1,0:T(2,128)(2,1)S(1)}, u32[]{:S(2)}, u32[]{:S(2)}) collective-permute-start(bf16[2,1280]{1,0:T(2,128)(2,1)S(1)} %get-tuple-element.27), channel_id=1, source_target_pairs={{0,12},{4,8},{8,4},{12,0},{1,13},{5,9},{9,5},{13,1},{2,14},{6,10},... | collective-permute-start | bytes 15368 | tf_op jit(solution)/shard_map/ppermute | solution.py:19
  20.5 0.1 mul.220
  20.7 0.2 mul.223
  20.9 1.5 %collective-permute-done.5 = bf16[2,1280]{1,0:T(2,128)(2,1)S(1)} collective-permute-done((bf16[2,1280]{1,0:T(2,128)(2,1)S(1)}, bf16[2,1280]{1,0:T(2,128)(2,1)S(1)}, u32[]{:S(2)}, u32[]{:S(2)}) %collective-permute-start.5) | collective-permute-done | bytes 5152 | tf_op jit(solution)/shard_map/ppermute | solution.py:19
  22.4 2.5 %collective-permute-done.4 = bf16[2,1280]{1,0:T(2,128)(2,1)S(1)} collective-permute-done((bf16[2,1280]{1,0:T(2,128)(2,1)S(1)}, bf16[2,1280]{1,0:T(2,128)(2,1)S(1)}, u32[]{:S(2)}, u32[]{:S(2)}) %collective-permute-start.4) | collective-permute-done | bytes 5152 | tf_op jit(solution)/shard_map/ppermute | solution.py:19
  24.9 1.5 %collective-permute-start.7 = (bf16[4,2,1280]{2,1,0:T(2,128)(2,1)S(1)}, bf16[4,2,1280]{2,1,0:T(2,128)(2,1)S(1)}, u32[]{:S(2)}, u32[]{:S(2)}) collective-permute-start(bf16[4,2,1280]{2,1,0:T(2,128)(2,1)S(1)} %pad_maximum_fusion.3), channel_id=1, source_target_pairs={{0,2},{1,3},{2,0},{3,1},{4,6},{5,7},{6,4},{7,5},{8,10},{9,11},{10,... | collective-permute-start | bytes 61448 | tf_op jit(solution)/shard_map/ppermute | solution.py:19
  26.4 0.8 collective-permute-start.8
  27.2 1.6 %collective-permute-done.7 = bf16[4,2,1280]{2,1,0:T(2,128)(2,1)S(1)} collective-permute-done((bf16[4,2,1280]{2,1,0:T(2,128)(2,1)S(1)}, bf16[4,2,1280]{2,1,0:T(2,128)(2,1)S(1)}, u32[]{:S(2)}, u32[]{:S(2)}) %collective-permute-start.7) | collective-permute-done | bytes 20512 | tf_op jit(solution)/shard_map/ppermute | solution.py:19
  28.8 0.8 collective-permute-done.8
  29.7 0.1 fusion.24
  30.2 0.1 fusion.73
  30.3 0.1 fusion.37
  30.4 0.1 fusion.69
  30.5 0.7 fusion.84
  31.3 0.1 broadcast_in_dim.79
  31.4 0.2 fusion.16
  31.7 2.1 %fusion.13 = f32[2,32,128]{2,1,0:T(8,128)S(1)} fusion(bf16[2,1024,4,128]{3,2,1,0:T(4,128)(2,1)} %param.22, f32[2,4,8,1024]{3,2,1,0:T(8,128)S(1)} %get-tuple-element.42, f32[2,4,8]{2,1,0:T(4,128)S(1)} %fusion.71, f32[2,4,128]{2,1,0:T(4,128)S(1)} %fusion.72, f32[2,4,8]{2,1,0:T(4,128)S(1)} %get-tuple-element.33), kind=kOutput, calls=%fused_computation.11 | convolution fusion | flops 16924672 | bytes 2396672 | tf_op jit(solution)/shard_map/rgjs,rsgd->rgjd/dot_general | solution.py:119
  33.9 0.1 pad_maximum_fusion
  34.0 0.8 collective-permute-start.14
  34.8 1.4 %collective-permute-start.13 = (f32[2,32,256]{2,1,0:T(8,128)S(1)}, f32[2,32,256]{2,1,0:T(8,128)S(1)}, u32[]{:S(2)}, u32[]{:S(2)}) collective-permute-start(f32[2,32,256]{2,1,0:T(8,128)S(1)} %pad_maximum_fusion), channel_id=1, source_target_pairs={{0,2},{1,3},{2,0},{3,1},{4,6},{5,7},{6,4},{7,5},{8,10},{9,11},{10,... | collective-permute-start | bytes 196616 | tf_op jit(solution)/shard_map/ppermute | solution.py:19
  36.3 1.4 %collective-permute-done.14 = f32[2,32,256]{2,1,0:T(8,128)S(1)} collective-permute-done((f32[2,32,256]{2,1,0:T(8,128)S(1)}, f32[2,32,256]{2,1,0:T(8,128)S(1)}, u32[]{:S(2)}, u32[]{:S(2)}) %collective-permute-start.14) | collective-permute-done | bytes 65568 | tf_op jit(solution)/shard_map/ppermute | solution.py:19
  37.8 2.1 %collective-permute-done.13 = f32[2,32,256]{2,1,0:T(8,128)S(1)} collective-permute-done((f32[2,32,256]{2,1,0:T(8,128)S(1)}, f32[2,32,256]{2,1,0:T(8,128)S(1)}, u32[]{:S(2)}, u32[]{:S(2)}) %collective-permute-start.13) | collective-permute-done | bytes 65568 | tf_op jit(solution)/shard_map/ppermute | solution.py:19
  39.8 0.2 fusion.58
  40.0 0.1 fusion.38
  40.2 0.3 rev.14
  40.8 1.5 %collective-permute-start.16 = (bf16[2,1024]{1,0:T(2,128)(2,1)S(1)}, bf16[2,1024]{1,0:T(2,128)(2,1)S(1)}, u32[]{:S(2)}, u32[]{:S(2)}) collective-permute-start(bf16[2,1024]{1,0:T(2,128)(2,1)S(1)} %bitcast.103), channel_id=1, source_target_pairs={{0,8},{4,12},{8,0},{12,4},{1,9},{5,13},{9,1},{13,5},{2,10},{6,14},... | collective-permute-start | bytes 12296 | tf_op jit(solution)/shard_map/ppermute | solution.py:19
  42.2 2.9 %collective-permute-start.17 = (bf16[2,1024]{1,0:T(2,128)(2,1)S(1)}, bf16[2,1024]{1,0:T(2,128)(2,1)S(1)}, u32[]{:S(2)}, u32[]{:S(2)}) collective-permute-start(bf16[2,1024]{1,0:T(2,128)(2,1)S(1)} %bitcast.102), channel_id=1, source_target_pairs={{0,12},{4,8},{8,4},{12,0},{1,13},{5,9},{9,5},{13,1},{2,14},{6,10},... | collective-permute-start | bytes 12296 | tf_op jit(solution)/shard_map/ppermute | solution.py:19
  45.2 0.2 collective-permute-done.16
  45.4 2.3 %collective-permute-done.17 = bf16[2,1024]{1,0:T(2,128)(2,1)S(1)} collective-permute-done((bf16[2,1024]{1,0:T(2,128)(2,1)S(1)}, bf16[2,1024]{1,0:T(2,128)(2,1)S(1)}, u32[]{:S(2)}, u32[]{:S(2)}) %collective-permute-start.17) | collective-permute-done | bytes 4128 | tf_op jit(solution)/shard_map/ppermute | solution.py:19
  47.6 2.8 %convolution_convert_fusion.3 = bf16[8,2048]{1,0:T(8,128)(2,1)S(1)} fusion(bf16[1024,2048]{1,0:T(8,128)(2,1)} %param.17, bf16[2,1024]{1,0:T(2,128)(2,1)S(1)} %collective-permute-done.17, bf16[2,1024]{1,0:T(2,128)(2,1)S(1)} %collective-permute-done.16, bf16[2,1024]{1,0:T(2,128)(2,1)S(1)} %collective-permute-done.15, bf16[2,1024]{1,0:T(2,128)(2,1)S(1)} %bitcast.101), kind=kOutput, calls=%fused_computation.3 | convolution fusion | flops 33636352 | bytes 4243456 | tf_op jit(solution)/shard_map/dot_general | solution.py:154
  50.5 3.0 %collective-permute-start.20 = (bf16[4,2,2048]{2,1,0:T(2,128)(2,1)S(1)}, bf16[4,2,2048]{2,1,0:T(2,128)(2,1)S(1)}, u32[]{:S(2)}, u32[]{:S(2)}) collective-permute-start(bf16[4,2,2048]{2,1,0:T(2,128)(2,1)S(1)} %reshape.171), channel_id=1, source_target_pairs={{0,12},{4,8},{8,4},{12,0},{1,13},{5,9},{9,5},{13,1},{2,14},{6,10},... | collective-permute-start | bytes 98312 | tf_op jit(solution)/shard_map/ppermute | solution.py:19
  53.5 1.5 %collective-permute-start.18 = (bf16[4,2,2048]{2,1,0:T(2,128)(2,1)S(1)}, bf16[4,2,2048]{2,1,0:T(2,128)(2,1)S(1)}, u32[]{:S(2)}, u32[]{:S(2)}) collective-permute-start(bf16[4,2,2048]{2,1,0:T(2,128)(2,1)S(1)} %reshape.171), channel_id=1, source_target_pairs={{0,4},{4,0},{8,12},{12,8},{1,5},{5,1},{9,13},{13,9},{2,6},{6,2},{1... | collective-permute-start | bytes 98312 | tf_op jit(solution)/shard_map/ppermute | solution.py:19
  55.0 1.4 %collective-permute-done.20 = bf16[4,2,2048]{2,1,0:T(2,128)(2,1)S(1)} collective-permute-done((bf16[4,2,2048]{2,1,0:T(2,128)(2,1)S(1)}, bf16[4,2,2048]{2,1,0:T(2,128)(2,1)S(1)}, u32[]{:S(2)}, u32[]{:S(2)}) %collective-permute-start.20) | collective-permute-done | bytes 32800 | tf_op jit(solution)/shard_map/ppermute | solution.py:19
  56.4 2.0 %collective-permute-done.19 = bf16[4,2,2048]{2,1,0:T(2,128)(2,1)S(1)} collective-permute-done((bf16[4,2,2048]{2,1,0:T(2,128)(2,1)S(1)}, bf16[4,2,2048]{2,1,0:T(2,128)(2,1)S(1)}, u32[]{:S(2)}, u32[]{:S(2)}) %collective-permute-start.19) | collective-permute-done | bytes 32800 | tf_op jit(solution)/shard_map/ppermute | solution.py:19
  58.5 0.2 multiply_reduce_fusion
  58.7 0.9 collective-permute-start.25
  59.6 1.0 %collective-permute-start.24 = (f32[8]{0:T(128)S(1)}, f32[8]{0:T(128)S(1)}, u32[]{:S(2)}, u32[]{:S(2)}) collective-permute-start(f32[8]{0:T(128)S(1)} %get-tuple-element.10), channel_id=1, source_target_pairs={{0,1},{1,0},{2,3},{3,2},{4,5},{5,4},{6,7},{7,6},{8,9},{9,8},{10,11... | collective-permute-start | bytes 104 | tf_op jit(solution)/shard_map/ppermute | solution.py:19
  60.6 7.3 %convolution_convert_fusion.1 = bf16[8,3584]{1,0:T(8,128)(2,1)S(1)} fusion(bf16[2048,3584]{1,0:T(8,128)(2,1)} %param.18, f32[8,2048]{1,0:T(8,128)S(1)} %get-tuple-element.11, f32[2048]{0:T(1024)S(1)} %convert_element_type.254), kind=kOutput, calls=%fused_computation.1 | convolution fusion | flops 117501952 | bytes 14811136 | tf_op jit(solution)/shard_map/dot_general | solution.py:167
  67.9 0.4 collective-permute-start.23
  68.3 1.2 %collective-permute-start.22 = (bf16[8,3584]{1,0:T(8,128)(2,1)S(1)}, bf16[8,3584]{1,0:T(8,128)(2,1)S(1)}, u32[]{:S(2)}, u32[]{:S(2)}) collective-permute-start(bf16[8,3584]{1,0:T(8,128)(2,1)S(1)} %convolution_convert_fusion.1), channel_id=1, source_target_pairs={{0,2},{1,3},{2,0},{3,1},{4,6},{5,7},{6,4},{7,5},{8,10},{9,11},{10,... | collective-permute-start | bytes 172040 | tf_op jit(solution)/shard_map/ppermute | solution.py:19
  69.6 7.3 %convolution_convert_fusion = bf16[8,3584]{1,0:T(8,128)(2,1)S(1)} fusion(bf16[2048,3584]{1,0:T(8,128)(2,1)} %param.19, f32[8,2048]{1,0:T(8,128)S(1)} %get-tuple-element.11, f32[2048]{0:T(1024)S(1)} %convert_element_type.254), kind=kOutput, calls=%fused_computation | convolution fusion | flops 117501952 | bytes 14811136 | tf_op jit(solution)/shard_map/dot_general | solution.py:170
  76.9 0.1 collective-permute-start.21
  77.0 0.9 collective-permute-start.29
  77.8 1.2 %collective-permute-start.28 = (bf16[8,3584]{1,0:T(8,128)(2,1)S(1)}, bf16[8,3584]{1,0:T(8,128)(2,1)S(1)}, u32[]{:S(2)}, u32[]{:S(2)}) collective-permute-start(bf16[8,3584]{1,0:T(8,128)(2,1)S(1)} %convolution_convert_fusion), channel_id=1, source_target_pairs={{0,2},{1,3},{2,0},{3,1},{4,6},{5,7},{6,4},{7,5},{8,10},{9,11},{10,... | collective-permute-start | bytes 172040 | tf_op jit(solution)/shard_map/ppermute | solution.py:19
  79.1 1.5 %collective-permute-done.29 = bf16[8,3584]{1,0:T(8,128)(2,1)S(1)} collective-permute-done((bf16[8,3584]{1,0:T(8,128)(2,1)S(1)}, bf16[8,3584]{1,0:T(8,128)(2,1)S(1)}, u32[]{:S(2)}, u32[]{:S(2)}) %collective-permute-start.29) | collective-permute-done | bytes 57376 | tf_op jit(solution)/shard_map/ppermute | solution.py:19
  80.6 1.8 %collective-permute-done.28 = bf16[8,3584]{1,0:T(8,128)(2,1)S(1)} collective-permute-done((bf16[8,3584]{1,0:T(8,128)(2,1)S(1)}, bf16[8,3584]{1,0:T(8,128)(2,1)S(1)}, u32[]{:S(2)}, u32[]{:S(2)}) %collective-permute-start.28) | collective-permute-done | bytes 57376 | tf_op jit(solution)/shard_map/ppermute | solution.py:19
  82.5 2.1 %convolution_convert_fusion.2 = bf16[8,2048]{1,0:T(8,128)(2,1)S(1)} fusion(bf16[3584,2048]{1,0:T(8,128)(2,1)S(1)} %bitcast.84, bf16[8,3584]{1,0:T(8,128)(2,1)S(1)} %collective-permute-done.29, bf16[8,3584]{1,0:T(8,128)(2,1)S(1)} %collective-permute-done.28, bf16[8,3584]{1,0:T(8,128)(2,1)S(1)} %collective-permute-done.27, ...), kind=kOutput, calls=%fused_computation.2 | convolution fusion | flops 118087680 | bytes 15171616 | tf_op jit(solution)/shard_map/dot_general | solution.py:176
  84.5 0.6 collective-permute-start.30
  85.2 2.9 %collective-permute-start.32 = (bf16[2,2048]{1,0:T(2,128)(2,1)S(1)}, bf16[2,2048]{1,0:T(2,128)(2,1)S(1)}, u32[]{:S(2)}, u32[]{:S(2)}) collective-permute-start(bf16[2,2048]{1,0:T(2,128)(2,1)S(1)} %get-tuple-element.19), channel_id=1, source_target_pairs={{0,12},{4,8},{8,4},{12,0},{1,13},{5,9},{9,5},{13,1},{2,14},{6,10},... | collective-permute-start | bytes 24584 | tf_op jit(solution)/shard_map/ppermute | solution.py:19
  88.1 0.2 collective-permute-done.30
  88.3 2.4 %collective-permute-done.32 = bf16[2,2048]{1,0:T(2,128)(2,1)S(1)} collective-permute-done((bf16[2,2048]{1,0:T(2,128)(2,1)S(1)}, bf16[2,2048]{1,0:T(2,128)(2,1)S(1)}, u32[]{:S(2)}, u32[]{:S(2)}) %collective-permute-start.32) | collective-permute-done | bytes 8224 | tf_op jit(solution)/shard_map/ppermute | solution.py:19
  90.6 2.0 %collective-permute-done.31 = bf16[2,2048]{1,0:T(2,128)(2,1)S(1)} collective-permute-done((bf16[2,2048]{1,0:T(2,128)(2,1)S(1)}, bf16[2,2048]{1,0:T(2,128)(2,1)S(1)}, u32[]{:S(2)}, u32[]{:S(2)}) %collective-permute-start.31) | collective-permute-done | bytes 8224 | tf_op jit(solution)/shard_map/ppermute | solution.py:19
  92.6 0.6 fusion.41
  (95 shorter events, 1.9 us)
Async XLA Ops:
  0.0 30.5 %copy-start = (bf16[2,1024,4,128]{3,2,1,0:T(4,128)(2,1)S(1)}, bf16[2,1024,4,128]{3,2,1,0:T(4,128)(2,1)}, u32[]{:S(2)}) copy-start(bf16[2,1024,4,128]{3,2,1,0:T(4,128)(2,1)} %param.21) | copy-start | bytes 6291460
  1.0 25.4 %collective-permute-start.11 = (f32[2]{0:T(128)S(1)}, f32[2]{0:T(128)S(1)}, u32[]{:S(2)}, u32[]{:S(2)}) collective-permute-start(f32[2]{0:T(128)S(1)} %multiply_reduce_fusion.1), channel_id=1, source_target_pairs={{0,3},{1,2},{2,1},{3,0},{4,7},{5,6},{6,5},{7,4},{8,11},{9,10},{10,... | collective-permute-start | bytes 32 | tf_op jit(solution)/shard_map/ppermute | solution.py:19
  3.4 23.7 %collective-permute-start.10 = (f32[2]{0:T(128)S(1)}, f32[2]{0:T(128)S(1)}, u32[]{:S(2)}, u32[]{:S(2)}) collective-permute-start(f32[2]{0:T(128)S(1)} %multiply_reduce_fusion.1), channel_id=1, source_target_pairs={{0,2},{1,3},{2,0},{3,1},{4,6},{5,7},{6,4},{7,5},{8,10},{9,11},{10,... | collective-permute-start | bytes 32 | tf_op jit(solution)/shard_map/ppermute | solution.py:19
  4.1 6.0 %collective-permute-start.2 = (bf16[2,2048]{1,0:T(2,128)(2,1)}, bf16[2,2048]{1,0:T(2,128)(2,1)S(1)}, u32[]{:S(2)}, u32[]{:S(2)}) collective-permute-start(bf16[2,2048]{1,0:T(2,128)(2,1)} %param.12), channel_id=1, source_target_pairs={{0,12},{4,8},{8,4},{12,0},{1,13},{5,9},{9,5},{13,1},{2,14},{6,10},... | collective-permute-start | bytes 24584 | tf_op jit(solution)/shard_map/ppermute | solution.py:19
  7.7 4.8 %collective-permute-start.1 = (bf16[2,2048]{1,0:T(2,128)(2,1)}, bf16[2,2048]{1,0:T(2,128)(2,1)S(1)}, u32[]{:S(2)}, u32[]{:S(2)}) collective-permute-start(bf16[2,2048]{1,0:T(2,128)(2,1)} %param.12), channel_id=1, source_target_pairs={{0,8},{4,12},{8,0},{12,4},{1,9},{5,13},{9,1},{13,5},{2,10},{6,14},... | collective-permute-start | bytes 24584 | tf_op jit(solution)/shard_map/ppermute | solution.py:19
  7.7 4.8 %collective-permute-start = (bf16[2,2048]{1,0:T(2,128)(2,1)}, bf16[2,2048]{1,0:T(2,128)(2,1)S(1)}, u32[]{:S(2)}, u32[]{:S(2)}) collective-permute-start(bf16[2,2048]{1,0:T(2,128)(2,1)} %param.12), channel_id=1, source_target_pairs={{0,4},{4,0},{8,12},{12,8},{1,5},{5,1},{9,13},{13,9},{2,6},{6,2},{1... | collective-permute-start | bytes 24584 | tf_op jit(solution)/shard_map/ppermute | solution.py:19
  16.8 4.0 %collective-permute-start.3 = (bf16[2,1280]{1,0:T(2,128)(2,1)S(1)}, bf16[2,1280]{1,0:T(2,128)(2,1)S(1)}, u32[]{:S(2)}, u32[]{:S(2)}) collective-permute-start(bf16[2,1280]{1,0:T(2,128)(2,1)S(1)} %get-tuple-element.26), channel_id=1, source_target_pairs={{0,4},{4,0},{8,12},{12,8},{1,5},{5,1},{9,13},{13,9},{2,6},{6,2},{1... | collective-permute-start | bytes 15368 | tf_op jit(solution)/shard_map/ppermute | solution.py:19
  16.9 5.5 %collective-permute-start.5 = (bf16[2,1280]{1,0:T(2,128)(2,1)S(1)}, bf16[2,1280]{1,0:T(2,128)(2,1)S(1)}, u32[]{:S(2)}, u32[]{:S(2)}) collective-permute-start(bf16[2,1280]{1,0:T(2,128)(2,1)S(1)} %get-tuple-element.27), channel_id=1, source_target_pairs={{0,12},{4,8},{8,4},{12,0},{1,13},{5,9},{9,5},{13,1},{2,14},{6,10},... | collective-permute-start | bytes 15368 | tf_op jit(solution)/shard_map/ppermute | solution.py:19
  20.4 4.5 %collective-permute-start.4 = (bf16[2,1280]{1,0:T(2,128)(2,1)S(1)}, bf16[2,1280]{1,0:T(2,128)(2,1)S(1)}, u32[]{:S(2)}, u32[]{:S(2)}) collective-permute-start(bf16[2,1280]{1,0:T(2,128)(2,1)S(1)} %get-tuple-element.28), channel_id=1, source_target_pairs={{0,8},{4,12},{8,0},{12,4},{1,9},{5,13},{9,1},{13,5},{2,10},{6,14},... | collective-permute-start | bytes 15368 | tf_op jit(solution)/shard_map/ppermute | solution.py:19
  20.8 6.3 %collective-permute-start.9 = (f32[2]{0:T(128)S(1)}, f32[2]{0:T(128)S(1)}, u32[]{:S(2)}, u32[]{:S(2)}) collective-permute-start(f32[2]{0:T(128)S(1)} %multiply_reduce_fusion.1), channel_id=1, source_target_pairs={{0,1},{1,0},{2,3},{3,2},{4,5},{5,4},{6,7},{7,6},{8,9},{9,8},{10,11... | collective-permute-start | bytes 32 | tf_op jit(solution)/shard_map/ppermute | solution.py:19
  24.9 3.8 %collective-permute-start.7 = (bf16[4,2,1280]{2,1,0:T(2,128)(2,1)S(1)}, bf16[4,2,1280]{2,1,0:T(2,128)(2,1)S(1)}, u32[]{:S(2)}, u32[]{:S(2)}) collective-permute-start(bf16[4,2,1280]{2,1,0:T(2,128)(2,1)S(1)} %pad_maximum_fusion.3), channel_id=1, source_target_pairs={{0,2},{1,3},{2,0},{3,1},{4,6},{5,7},{6,4},{7,5},{8,10},{9,11},{10,... | collective-permute-start | bytes 61448 | tf_op jit(solution)/shard_map/ppermute | solution.py:19
  26.4 2.4 %collective-permute-start.6 = (bf16[4,2,1280]{2,1,0:T(2,128)(2,1)S(1)}, bf16[4,2,1280]{2,1,0:T(2,128)(2,1)S(1)}, u32[]{:S(2)}, u32[]{:S(2)}) collective-permute-start(bf16[4,2,1280]{2,1,0:T(2,128)(2,1)S(1)} %pad_maximum_fusion.3), channel_id=1, source_target_pairs={{0,1},{1,0},{2,3},{3,2},{4,5},{5,4},{6,7},{7,6},{8,9},{9,8},{10,11... | collective-permute-start | bytes 61448 | tf_op jit(solution)/shard_map/ppermute | solution.py:19
  26.4 3.2 %collective-permute-start.8 = (bf16[4,2,1280]{2,1,0:T(2,128)(2,1)S(1)}, bf16[4,2,1280]{2,1,0:T(2,128)(2,1)S(1)}, u32[]{:S(2)}, u32[]{:S(2)}) collective-permute-start(bf16[4,2,1280]{2,1,0:T(2,128)(2,1)S(1)} %pad_maximum_fusion.3), channel_id=1, source_target_pairs={{0,3},{1,2},{2,1},{3,0},{4,7},{5,6},{6,5},{7,4},{8,11},{9,10},{10,... | collective-permute-start | bytes 61448 | tf_op jit(solution)/shard_map/ppermute | solution.py:19
  31.3 23.7 %copy-start.2 = (bf16[2048]{0:T(1024)(128)(2,1)S(1)}, bf16[2048]{0:T(1024)(128)(2,1)}, u32[]{:S(2)}) copy-start(bf16[2048]{0:T(1024)(128)(2,1)} %param.14) | copy-start | bytes 12292
  31.7 26.8 %copy-start.1 = (bf16[2,2048]{1,0:T(2,128)(2,1)S(1)}, bf16[2,2048]{1,0:T(2,128)(2,1)}, u32[]{:S(2)}) copy-start(bf16[2,2048]{1,0:T(2,128)(2,1)} %param.12) | copy-start | bytes 24580
  34.0 3.8 %collective-permute-start.14 = (f32[2,32,256]{2,1,0:T(8,128)S(1)}, f32[2,32,256]{2,1,0:T(8,128)S(1)}, u32[]{:S(2)}, u32[]{:S(2)}) collective-permute-start(f32[2,32,256]{2,1,0:T(8,128)S(1)} %pad_maximum_fusion), channel_id=1, source_target_pairs={{0,3},{1,2},{2,1},{3,0},{4,7},{5,6},{6,5},{7,4},{8,11},{9,10},{10,... | collective-permute-start | bytes 196616 | tf_op jit(solution)/shard_map/ppermute | solution.py:19
  34.8 5.0 %collective-permute-start.13 = (f32[2,32,256]{2,1,0:T(8,128)S(1)}, f32[2,32,256]{2,1,0:T(8,128)S(1)}, u32[]{:S(2)}, u32[]{:S(2)}) collective-permute-start(f32[2,32,256]{2,1,0:T(8,128)S(1)} %pad_maximum_fusion), channel_id=1, source_target_pairs={{0,2},{1,3},{2,0},{3,1},{4,6},{5,7},{6,4},{7,5},{8,10},{9,11},{10,... | collective-permute-start | bytes 196616 | tf_op jit(solution)/shard_map/ppermute | solution.py:19
  36.2 3.7 %collective-permute-start.12 = (f32[2,32,256]{2,1,0:T(8,128)S(1)}, f32[2,32,256]{2,1,0:T(8,128)S(1)}, u32[]{:S(2)}, u32[]{:S(2)}) collective-permute-start(f32[2,32,256]{2,1,0:T(8,128)S(1)} %pad_maximum_fusion), channel_id=1, source_target_pairs={{0,1},{1,0},{2,3},{3,2},{4,5},{5,4},{6,7},{7,6},{8,9},{9,8},{10,11... | collective-permute-start | bytes 196616 | tf_op jit(solution)/shard_map/ppermute | solution.py:19
  40.7 4.5 %collective-permute-start.15 = (bf16[2,1024]{1,0:T(2,128)(2,1)S(1)}, bf16[2,1024]{1,0:T(2,128)(2,1)S(1)}, u32[]{:S(2)}, u32[]{:S(2)}) collective-permute-start(bf16[2,1024]{1,0:T(2,128)(2,1)S(1)} %bitcast.104), channel_id=1, source_target_pairs={{0,4},{4,0},{8,12},{12,8},{1,5},{5,1},{9,13},{13,9},{2,6},{6,2},{1... | collective-permute-start | bytes 12296 | tf_op jit(solution)/shard_map/ppermute | solution.py:19
  40.8 4.6 %collective-permute-start.16 = (bf16[2,1024]{1,0:T(2,128)(2,1)S(1)}, bf16[2,1024]{1,0:T(2,128)(2,1)S(1)}, u32[]{:S(2)}, u32[]{:S(2)}) collective-permute-start(bf16[2,1024]{1,0:T(2,128)(2,1)S(1)} %bitcast.103), channel_id=1, source_target_pairs={{0,8},{4,12},{8,0},{12,4},{1,9},{5,13},{9,1},{13,5},{2,10},{6,14},... | collective-permute-start | bytes 12296 | tf_op jit(solution)/shard_map/ppermute | solution.py:19
  42.2 5.4 %collective-permute-start.17 = (bf16[2,1024]{1,0:T(2,128)(2,1)S(1)}, bf16[2,1024]{1,0:T(2,128)(2,1)S(1)}, u32[]{:S(2)}, u32[]{:S(2)}) collective-permute-start(bf16[2,1024]{1,0:T(2,128)(2,1)S(1)} %bitcast.102), channel_id=1, source_target_pairs={{0,12},{4,8},{8,4},{12,0},{1,13},{5,9},{9,5},{13,1},{2,14},{6,10},... | collective-permute-start | bytes 12296 | tf_op jit(solution)/shard_map/ppermute | solution.py:19
  50.5 5.8 %collective-permute-start.20 = (bf16[4,2,2048]{2,1,0:T(2,128)(2,1)S(1)}, bf16[4,2,2048]{2,1,0:T(2,128)(2,1)S(1)}, u32[]{:S(2)}, u32[]{:S(2)}) collective-permute-start(bf16[4,2,2048]{2,1,0:T(2,128)(2,1)S(1)} %reshape.171), channel_id=1, source_target_pairs={{0,12},{4,8},{8,4},{12,0},{1,13},{5,9},{9,5},{13,1},{2,14},{6,10},... | collective-permute-start | bytes 98312 | tf_op jit(solution)/shard_map/ppermute | solution.py:19
  53.5 4.8 %collective-permute-start.19 = (bf16[4,2,2048]{2,1,0:T(2,128)(2,1)S(1)}, bf16[4,2,2048]{2,1,0:T(2,128)(2,1)S(1)}, u32[]{:S(2)}, u32[]{:S(2)}) collective-permute-start(bf16[4,2,2048]{2,1,0:T(2,128)(2,1)S(1)} %reshape.171), channel_id=1, source_target_pairs={{0,8},{4,12},{8,0},{12,4},{1,9},{5,13},{9,1},{13,5},{2,10},{6,14},... | collective-permute-start | bytes 98312 | tf_op jit(solution)/shard_map/ppermute | solution.py:19
  53.5 4.8 %collective-permute-start.18 = (bf16[4,2,2048]{2,1,0:T(2,128)(2,1)S(1)}, bf16[4,2,2048]{2,1,0:T(2,128)(2,1)S(1)}, u32[]{:S(2)}, u32[]{:S(2)}) collective-permute-start(bf16[4,2,2048]{2,1,0:T(2,128)(2,1)S(1)} %reshape.171), channel_id=1, source_target_pairs={{0,4},{4,0},{8,12},{12,8},{1,5},{5,1},{9,13},{13,9},{2,6},{6,2},{1... | collective-permute-start | bytes 98312 | tf_op jit(solution)/shard_map/ppermute | solution.py:19
  58.7 18.2 %collective-permute-start.26 = (f32[8]{0:T(128)S(1)}, f32[8]{0:T(128)S(1)}, u32[]{:S(2)}, u32[]{:S(2)}) collective-permute-start(f32[8]{0:T(128)S(1)} %get-tuple-element.10), channel_id=1, source_target_pairs={{0,3},{1,2},{2,1},{3,0},{4,7},{5,6},{6,5},{7,4},{8,11},{9,10},{10,... | collective-permute-start | bytes 104 | tf_op jit(solution)/shard_map/ppermute | solution.py:19
  58.7 18.2 %collective-permute-start.25 = (f32[8]{0:T(128)S(1)}, f32[8]{0:T(128)S(1)}, u32[]{:S(2)}, u32[]{:S(2)}) collective-permute-start(f32[8]{0:T(128)S(1)} %get-tuple-element.10), channel_id=1, source_target_pairs={{0,2},{1,3},{2,0},{3,1},{4,6},{5,7},{6,4},{7,5},{8,10},{9,11},{10,... | collective-permute-start | bytes 104 | tf_op jit(solution)/shard_map/ppermute | solution.py:19
  59.6 18.2 %collective-permute-start.24 = (f32[8]{0:T(128)S(1)}, f32[8]{0:T(128)S(1)}, u32[]{:S(2)}, u32[]{:S(2)}) collective-permute-start(f32[8]{0:T(128)S(1)} %get-tuple-element.10), channel_id=1, source_target_pairs={{0,1},{1,0},{2,3},{3,2},{4,5},{5,4},{6,7},{7,6},{8,9},{9,8},{10,11... | collective-permute-start | bytes 104 | tf_op jit(solution)/shard_map/ppermute | solution.py:19
  60.6 21.8 %slice-start = ((s8[14680064]{0:T(1024)(128)(4,1)}), s8[4194304]{0:T(1024)(128)(4,1)S(1)}, s32[]{:S(2)}) async-start(s8[14680064]{0:T(1024)(128)(4,1)} %bitcast.83), calls=%async_computation | async-start | bytes 8388608
  60.6 21.8 %slice-start.1 = ((s8[14680064]{0:T(1024)(128)(4,1)}), s8[4194304]{0:T(1024)(128)(4,1)S(1)}, s32[]{:S(2)}) async-start(s8[14680064]{0:T(1024)(128)(4,1)} %bitcast.83), calls=%async_computation.1 | async-start | bytes 8388608
  67.9 14.5 %slice-start.2 = ((s8[14680064]{0:T(1024)(128)(4,1)}), s8[4194304]{0:T(1024)(128)(4,1)S(1)}, s32[]{:S(2)}) async-start(s8[14680064]{0:T(1024)(128)(4,1)} %bitcast.83), calls=%async_computation.2 | async-start | bytes 8388608
  67.9 14.5 %slice-start.3 = ((s8[14680064]{0:T(1024)(128)(4,1)}), s8[2097152]{0:T(1024)(128)(4,1)S(1)}, s32[]{:S(2)}) async-start(s8[14680064]{0:T(1024)(128)(4,1)} %bitcast.83), calls=%async_computation.3 | async-start | bytes 4194304
  67.9 11.1 %collective-permute-start.23 = (bf16[8,3584]{1,0:T(8,128)(2,1)S(1)}, bf16[8,3584]{1,0:T(8,128)(2,1)S(1)}, u32[]{:S(2)}, u32[]{:S(2)}) collective-permute-start(bf16[8,3584]{1,0:T(8,128)(2,1)S(1)} %convolution_convert_fusion.1), channel_id=1, source_target_pairs={{0,3},{1,2},{2,1},{3,0},{4,7},{5,6},{6,5},{7,4},{8,11},{9,10},{10,... | collective-permute-start | bytes 172040 | tf_op jit(solution)/shard_map/ppermute | solution.py:19
  68.3 10.7 %collective-permute-start.22 = (bf16[8,3584]{1,0:T(8,128)(2,1)S(1)}, bf16[8,3584]{1,0:T(8,128)(2,1)S(1)}, u32[]{:S(2)}, u32[]{:S(2)}) collective-permute-start(bf16[8,3584]{1,0:T(8,128)(2,1)S(1)} %convolution_convert_fusion.1), channel_id=1, source_target_pairs={{0,2},{1,3},{2,0},{3,1},{4,6},{5,7},{6,4},{7,5},{8,10},{9,11},{10,... | collective-permute-start | bytes 172040 | tf_op jit(solution)/shard_map/ppermute | solution.py:19
  76.9 2.2 %collective-permute-start.21 = (bf16[8,3584]{1,0:T(8,128)(2,1)S(1)}, bf16[8,3584]{1,0:T(8,128)(2,1)S(1)}, u32[]{:S(2)}, u32[]{:S(2)}) collective-permute-start(bf16[8,3584]{1,0:T(8,128)(2,1)S(1)} %convolution_convert_fusion.1), channel_id=1, source_target_pairs={{0,1},{1,0},{2,3},{3,2},{4,5},{5,4},{6,7},{7,6},{8,9},{9,8},{10,11... | collective-permute-start | bytes 172040 | tf_op jit(solution)/shard_map/ppermute | solution.py:19
  77.0 3.6 %collective-permute-start.29 = (bf16[8,3584]{1,0:T(8,128)(2,1)S(1)}, bf16[8,3584]{1,0:T(8,128)(2,1)S(1)}, u32[]{:S(2)}, u32[]{:S(2)}) collective-permute-start(bf16[8,3584]{1,0:T(8,128)(2,1)S(1)} %convolution_convert_fusion), channel_id=1, source_target_pairs={{0,3},{1,2},{2,1},{3,0},{4,7},{5,6},{6,5},{7,4},{8,11},{9,10},{10,... | collective-permute-start | bytes 172040 | tf_op jit(solution)/shard_map/ppermute | solution.py:19
  77.8 4.6 %collective-permute-start.28 = (bf16[8,3584]{1,0:T(8,128)(2,1)S(1)}, bf16[8,3584]{1,0:T(8,128)(2,1)S(1)}, u32[]{:S(2)}, u32[]{:S(2)}) collective-permute-start(bf16[8,3584]{1,0:T(8,128)(2,1)S(1)} %convolution_convert_fusion), channel_id=1, source_target_pairs={{0,2},{1,3},{2,0},{3,1},{4,6},{5,7},{6,4},{7,5},{8,10},{9,11},{10,... | collective-permute-start | bytes 172040 | tf_op jit(solution)/shard_map/ppermute | solution.py:19
  79.1 3.4 %collective-permute-start.27 = (bf16[8,3584]{1,0:T(8,128)(2,1)S(1)}, bf16[8,3584]{1,0:T(8,128)(2,1)S(1)}, u32[]{:S(2)}, u32[]{:S(2)}) collective-permute-start(bf16[8,3584]{1,0:T(8,128)(2,1)S(1)} %convolution_convert_fusion), channel_id=1, source_target_pairs={{0,1},{1,0},{2,3},{3,2},{4,5},{5,4},{6,7},{7,6},{8,9},{9,8},{10,11... | collective-permute-start | bytes 172040 | tf_op jit(solution)/shard_map/ppermute | solution.py:19
  84.5 3.7 %collective-permute-start.30 = (bf16[2,2048]{1,0:T(2,128)(2,1)S(1)}, bf16[2,2048]{1,0:T(2,128)(2,1)S(1)}, u32[]{:S(2)}, u32[]{:S(2)}) collective-permute-start(bf16[2,2048]{1,0:T(2,128)(2,1)S(1)} %get-tuple-element.18), channel_id=1, source_target_pairs={{0,4},{4,0},{8,12},{12,8},{1,5},{5,1},{9,13},{13,9},{2,6},{6,2},{1... | collective-permute-start | bytes 24584 | tf_op jit(solution)/shard_map/ppermute | solution.py:19
  85.2 5.4 %collective-permute-start.32 = (bf16[2,2048]{1,0:T(2,128)(2,1)S(1)}, bf16[2,2048]{1,0:T(2,128)(2,1)S(1)}, u32[]{:S(2)}, u32[]{:S(2)}) collective-permute-start(bf16[2,2048]{1,0:T(2,128)(2,1)S(1)} %get-tuple-element.19), channel_id=1, source_target_pairs={{0,12},{4,8},{8,4},{12,0},{1,13},{5,9},{9,5},{13,1},{2,14},{6,10},... | collective-permute-start | bytes 24584 | tf_op jit(solution)/shard_map/ppermute | solution.py:19
  88.1 4.5 %collective-permute-start.31 = (bf16[2,2048]{1,0:T(2,128)(2,1)S(1)}, bf16[2,2048]{1,0:T(2,128)(2,1)S(1)}, u32[]{:S(2)}, u32[]{:S(2)}) collective-permute-start(bf16[2,2048]{1,0:T(2,128)(2,1)S(1)} %get-tuple-element.20), channel_id=1, source_target_pairs={{0,8},{4,12},{8,0},{12,4},{1,9},{5,13},{9,1},{13,5},{2,10},{6,14},... | collective-permute-start | bytes 24584 | tf_op jit(solution)/shard_map/ppermute | solution.py:19

commit v2 on v0

v2 whole, which is shorter than its diff:
```python
import functools
import math

import jax
import jax.numpy as jnp
from jax import lax
from jax.experimental import pallas as pl
from jax.experimental.pallas import tpu as pltpu
from jax.sharding import PartitionSpec as P

D = 8192
HEADS = 32
KV_HEADS = 4
HEAD_DIM = 128
GROUP = HEADS // KV_HEADS
LANES = 128
MIB = 2**20

epsilon = 1e-05
rope_base = 500000.0

in_vmem = pl.BlockSpec(memory_space=pltpu.VMEM)
in_smem = pl.BlockSpec(memory_space=pltpu.SMEM)
in_place = pl.BlockSpec(memory_space=pl.ANY)


def swap_with(value, axis, step):
    count = lax.axis_size(axis)
    return lax.ppermute(value, axis, [(i, i ^ step) for i in range(count)])


def exchange(value, axis):
    count = lax.axis_size(axis)
    got = {k: swap_with(value, axis, k) for k in reversed(range(1, count))}
    return [value] + [got[k] for k in range(1, count)]


def scatter_slots(pieces, axis):
    got = {k: swap_with(pieces[k], axis, k) for k in reversed(range(1, len(pieces)))}
    return [pieces[0]] + [got[k] for k in range(1, len(pieces))]


def pair_sums(value, axis):
    count = lax.axis_size(axis)
    step = 1
    while 2 * step < count:
        other = swap_with(value, axis, step)
        value = (value.astype(jnp.float32) + other.astype(jnp.float32)).astype(value.dtype)
        step *= 2
    return value, swap_with(value, axis, step)


def params(mib):
    return pltpu.CompilerParams(vmem_limit_bytes=mib * MIB)


def resident(weight):
    return pltpu.with_memory_space_constraint(weight, pltpu.VMEM)


def tile_of(columns):
    for tile in (512, 256, 128):
        if columns % tile == 0:
            return tile
    return columns


def product_tiles(left, weight_ref, store):
    columns = weight_ref.shape[1]
    tile = tile_of(columns)

    @pl.loop(0, columns // tile)
    def _(step):
        start = pl.multiple_of(step * tile, tile)
        store(
            start,
            tile,
            jnp.dot(left, weight_ref[:, pl.ds(start, tile)], preferred_element_type=jnp.float32),
        )


def three_parts(value):
    high = value.astype(jnp.bfloat16).astype(jnp.float32)
    rest = value - high
    middle = rest.astype(jnp.bfloat16).astype(jnp.float32)
    return high, middle, rest - middle


def spread(parts, lanes, first):
    out = 0.0
    for n, part in enumerate(parts):
        out = out + jnp.where(lanes == first + n, part, 0.0)
    return out


def squares_block(total, place):
    lanes = lax.broadcasted_iota(jnp.int32, (total.shape[0], LANES), 1)
    return spread(three_parts(total), lanes, place * 4).astype(jnp.bfloat16)


def load_kernel(count, *refs):
    sems = refs[-1]
    outs = refs[-1 - count : -1]
    copies = [pltpu.make_async_copy(refs[n], outs[n], sems.at[n]) for n in range(count)]
    for copy in copies:
        copy.start()
    for copy in copies:
        copy.wait()


def load(*weights, after):
    return pl.pallas_call(
        functools.partial(load_kernel, len(weights)),
        out_shape=tuple(pltpu.VMEM(w.shape, w.dtype) for w in weights),
        in_specs=[in_place] * (len(weights) + 1),
        out_specs=tuple(in_vmem for _ in weights),
        cost_estimate=pl.CostEstimate(
            flops=0, bytes_accessed=2 * sum(w.size for w in weights), transcendentals=0
        ),
        scratch_shapes=[pltpu.SemaphoreType.DMA((len(weights),))],
        compiler_params=params(1),
        name="load",
    )(*[pltpu.with_memory_space_constraint(w, pltpu.HBM) for w in weights], after)


def qkv_kernel(meta_ref, rows_ref, gain_ref, wq_ref, wkv_ref, out_ref):
    wide = rows_ref[...].astype(jnp.float32)
    total = jnp.sum(wide * wide, axis=1, keepdims=True)
    scaled = (wide * gain_ref[...].astype(jnp.float32)).astype(jnp.bfloat16)
    query_cols = wq_ref.shape[1]
    kv_cols = wkv_ref.shape[1]

    def store_query(start, size, value):
        out_ref[:, pl.ds(start, size)] = value.astype(jnp.bfloat16)

    product_tiles(scaled, wq_ref, store_query)
    out_ref[:, query_cols : query_cols + kv_cols] = jnp.dot(
        scaled, wkv_ref[...], preferred_element_type=jnp.float32
    ).astype(jnp.bfloat16)
    out_ref[:, query_cols + kv_cols :] = squares_block(total, meta_ref[1])


def project_qkv(meta, rows, gain, w_query, w_kv):
    columns = w_query.shape[1] + w_kv.shape[1] + LANES
    return pl.pallas_call(
        qkv_kernel,
        out_shape=jax.ShapeDtypeStruct((rows.shape[0], columns), jnp.bfloat16),
        in_specs=[in_smem] + [in_vmem] * 4,
        out_specs=in_vmem,
        compiler_params=params(2),
        name="project_qkv",
    )(meta, rows, gain, resident(w_query), resident(w_kv))


def attend_kernel(
    slots,
    meta_ref,
    cosine_ref,
    sine_ref,
    near_ref,
    far_ref,
    key_ref,
    value_ref,
    out_ref,
    query_s,
    kv_s,
    kv_wide_s,
    mixed_s,
    stats_s,
):
    all_rows = near_ref.shape[0]
    own_rows = all_rows // slots
    here = HEADS // slots
    query_cols = here * HEAD_DIM
    kv_cols = 2 * KV_HEADS * HEAD_DIM // slots
    columns = query_cols + kv_cols
    tensor_index = meta_ref[0]
    inner_index = meta_ref[1]
    positions = key_ref.shape[1] // KV_HEADS

    joined = near_ref[...].astype(jnp.float32) + far_ref[...].astype(jnp.float32)
    squares = jnp.sum(joined[:, columns:], axis=1, keepdims=True)
    joined = joined[:, :columns] * lax.rsqrt(squares / D + epsilon)
    cosine = cosine_ref[...]
    sine = sine_ref[...]

    def rotate(block):
        count = block.shape[0]
        even = lax.broadcasted_iota(jnp.int32, block.shape, 1) % 2 == 0
        other = jnp.where(
            even, pltpu.roll(block, HEAD_DIM - 1, axis=1), pltpu.roll(block, 1, axis=1)
        )
        return block * cosine[:count] + other * sine[:count]

    for j in range(here):
        block = rotate(joined[:, j * HEAD_DIM : (j + 1) * HEAD_DIM])
        query_s[j * all_rows : (j + 1) * all_rows, :] = block
    for s in range(slots):
        kv_s[s] = joined[s * own_rows : (s + 1) * own_rows, query_cols:]
    for d in range(slots):
        kv_wide_s[:, d * kv_cols : (d + 1) * kv_cols] = kv_s[d ^ tensor_index]
    new_keys = []
    new_values = []
    for g in range(KV_HEADS):
        block = kv_wide_s[:, g * HEAD_DIM : (g + 1) * HEAD_DIM]
        new_keys.append(rotate(block).astype(jnp.bfloat16).astype(jnp.float32))
        block = kv_wide_s[:, (KV_HEADS + g) * HEAD_DIM : (KV_HEADS + g + 1) * HEAD_DIM]
        new_values.append(block.astype(jnp.bfloat16).astype(jnp.float32))

    score_scale = HEAD_DIM ** (-0.5)
    row = lax.broadcasted_iota(jnp.int32, (HEADS, 1), 0)
    head = ((row % slots) ^ tensor_index) * here + row // slots
    kv_head = head // GROUP
    column = lax.broadcasted_iota(jnp.int32, (1, positions * KV_HEADS), 1)
    place = column // KV_HEADS + inner_index * positions
    column_head = column % KV_HEADS
    lanes = lax.broadcasted_iota(jnp.int32, (HEADS, LANES), 1)
    for r in range(own_rows):
        queries = query_s[pl.ds(r, HEADS, stride=own_rows), :].astype(jnp.bfloat16)
        scores = (
            lax.dot_general(
                queries,
                key_ref[r],
                (((1,), (1,)), ((), ())),
                preferred_element_type=jnp.float32,
            )
            * score_scale
        )
        used = jnp.where(place < meta_ref[2 + r], column_head, -1)
        masked = jnp.where(used == kv_head, scores, -1e30)
        key_rows = 0.0
        value_rows = 0.0
        for g in range(KV_HEADS):
            key_rows = key_rows + jnp.where(kv_head == g, new_keys[g][r : r + 1], 0.0)
            value_rows = value_rows + jnp.where(kv_head == g, new_values[g][r : r + 1], 0.0)
        new_score = (
            jnp.sum(queries.astype(jnp.float32) * key_rows, axis=1, keepdims=True) * score_scale
        )
        new_score = jnp.where(inner_index == 0, new_score, -1e30)
        peak = jnp.maximum(jnp.max(masked, axis=1, keepdims=True), new_score)
        weights = jnp.exp(masked - peak)
        new_weight = jnp.exp(new_score - peak)
        totals = jnp.sum(weights, axis=1, keepdims=True) + new_weight
        mixture = jnp.dot(
            weights.astype(jnp.bfloat16), value_ref[r], preferred_element_type=jnp.float32
        )
        mixture = mixture + new_weight.astype(jnp.bfloat16).astype(jnp.float32) * value_rows
        mixed_s[pl.ds(r, HEADS, stride=own_rows), :] = mixture
        stats_s[pl.ds(r, HEADS, stride=own_rows), :] = spread(
            three_parts(peak), lanes, 0
        ) + spread(three_parts(totals), lanes, 4)
    out_ref[:, :HEAD_DIM] = mixed_s[...].astype(jnp.bfloat16)
    out_ref[:, HEAD_DIM:] = stats_s[...].astype(jnp.bfloat16)


def attend(meta, cosine, sine, near, far, keys, values, slots):
    own_rows = near.shape[0] // slots
    kv_cols = 2 * KV_HEADS * HEAD_DIM // slots
    return pl.pallas_call(
        functools.partial(attend_kernel, slots),
        out_shape=jax.ShapeDtypeStruct((own_rows * HEADS, HEAD_DIM + LANES), jnp.bfloat16),
        in_specs=[in_smem] + [in_vmem] * 6,
        out_specs=in_vmem,
        scratch_shapes=[
            pltpu.VMEM((own_rows * HEADS, HEAD_DIM), jnp.float32),
            pltpu.VMEM((slots, own_rows, kv_cols), jnp.float32),
            pltpu.VMEM((own_rows, slots * kv_cols), jnp.float32),
            pltpu.VMEM((own_rows * HEADS, HEAD_DIM), jnp.float32),
            pltpu.VMEM((own_rows * HEADS, LANES), jnp.float32),
        ],
        compiler_params=params(6),
        name="attend",
    )(meta, cosine, sine, near, far, resident(keys), resident(values))


def combine_kernel(shards, all_rows, *refs):
    ins = refs[:shards]
    out_ref = refs[-1]
    peaks = []
    totals = []
    for ref in ins:
        stats = ref[:, HEAD_DIM:].astype(jnp.float32)
        peaks.append(stats[:, 0:1] + stats[:, 1:2] + stats[:, 2:3])
        totals.append(stats[:, 4:5] + stats[:, 5:6] + stats[:, 6:7])
    top = functools.reduce(jnp.maximum, peaks)
    mixed = 0.0
    denominator = 0.0
    for ref, peak, total in zip(ins, peaks, totals):
        factor = jnp.exp(peak - top)
        mixed = mixed + factor * ref[:, :HEAD_DIM].astype(jnp.float32)
        denominator = denominator + factor * total
    attended = mixed / denominator
    for j in range(attended.shape[0] // all_rows):
        out_ref[:, j * HEAD_DIM : (j + 1) * HEAD_DIM] = attended[
            j * all_rows : (j + 1) * all_rows
        ].astype(jnp.bfloat16)


def combine(parts, later, all_rows):
    count = len(parts)
    columns = parts[0].shape[0] // all_rows * HEAD_DIM
    return pl.pallas_call(
        functools.partial(combine_kernel, count, all_rows),
        out_shape=jax.ShapeDtypeStruct((all_rows, columns), jnp.bfloat16),
        in_specs=[in_vmem] * count + [in_place] * len(later),
        out_specs=in_vmem,
        compiler_params=params(2),
        name="combine",
    )(*parts, *[resident(w) for w in later])


def out_kernel(left_ref, weight_ref, later_ref, *outs):
    del later_ref
    left = left_ref[...]
    rows = outs[0].shape[0]

    def store(start, size, value):
        for k, ref in enumerate(outs):
            ref[:, pl.ds(start, size)] = value[k * rows : (k + 1) * rows].astype(jnp.bfloat16)

    product_tiles(left, weight_ref, store)


def project_out(left, weight, later, slots):
    rows = left.shape[0] // slots
    columns = weight.shape[1]
    return pl.pallas_call(
        out_kernel,
        out_shape=tuple([jax.ShapeDtypeStruct((rows, columns), jnp.bfloat16)] * slots),
        in_specs=[in_vmem, in_vmem, in_place],
        out_specs=tuple([in_vmem] * slots),
        compiler_params=params(2),
        name="project_out",
    )(left, resident(weight), resident(later))


def gate_up_kernel(slots, meta_ref, rows_ref, gain_ref, *refs):
    parts = refs[:slots]
    gate_ref, up_ref, out_ref, updated_ref = refs[slots:]
    own_rows = updated_ref.shape[0]
    total = parts[0][...].astype(jnp.float32)
    for ref in parts[1:]:
        total = total + ref[...].astype(jnp.float32)
    updated = (rows_ref[...].astype(jnp.float32) + total).astype(jnp.bfloat16)
    wide = updated.astype(jnp.float32)
    updated_ref[...] = wide[:own_rows]
    squares = jnp.sum(wide * wide, axis=1, keepdims=True)
    scaled = (wide * gain_ref[...].astype(jnp.float32)).astype(jnp.bfloat16)
    hidden = gate_ref.shape[1]

    def store_gate(start, size, value):
        out_ref[:, pl.ds(start, size)] = value.astype(jnp.bfloat16)

    def store_up(start, size, value):
        place = pl.multiple_of(start + hidden, math.gcd(hidden, size))
        out_ref[:, pl.ds(place, size)] = value.astype(jnp.bfloat16)

    product_tiles(scaled, gate_ref, store_gate)
    product_tiles(scaled, up_ref, store_up)
    out_ref[:, 2 * hidden :] = squares_block(squares, meta_ref[1])


def gate_up(meta, rows, gain, parts, w_gate, w_up, own_rows):
    hidden = w_gate.shape[1]
    slots = len(parts)
    return pl.pallas_call(
        functools.partial(gate_up_kernel, slots),
        out_shape=(
            jax.ShapeDtypeStruct((rows.shape[0], 2 * hidden + LANES), jnp.bfloat16),
            jax.ShapeDtypeStruct((own_rows, rows.shape[1]), jnp.float32),
        ),
        in_specs=[in_smem] + [in_vmem] * (4 + slots),
        out_specs=(in_vmem, in_vmem),
        compiler_params=params(3),
        name="gate_up",
    )(meta, rows, gain, *parts, resident(w_gate), resident(w_up))


def down_kernel(near_ref, far_ref, weight_ref, out_ref, hidden_s):
    hidden = weight_ref.shape[0]
    squares = jnp.sum(
        near_ref[:, 2 * hidden :].astype(jnp.float32) + far_ref[:, 2 * hidden :].astype(jnp.float32),
        axis=1,
        keepdims=True,
    )
    scale = lax.rsqrt(squares / D + epsilon)
    gate = near_ref[:, :hidden].astype(jnp.float32) + far_ref[:, :hidden].astype(jnp.float32)
    up = (
        near_ref[:, hidden : 2 * hidden].astype(jnp.float32)
        + far_ref[:, hidden : 2 * hidden].astype(jnp.float32)
    )
    gate = gate * scale
    hidden_s[...] = (gate / (1.0 + jnp.exp(-gate)) * (up * scale)).astype(jnp.bfloat16)

    def store(start, size, value):
        out_ref[:, pl.ds(start, size)] = value.astype(jnp.bfloat16)

    product_tiles(hidden_s[...], weight_ref, store)


def project_down(near, far, weight):
    rows = near.shape[0]
    return pl.pallas_call(
        down_kernel,
        out_shape=jax.ShapeDtypeStruct((rows, weight.shape[1]), jnp.bfloat16),
        in_specs=[in_vmem] * 3,
        out_specs=in_vmem,
        scratch_shapes=[pltpu.VMEM((rows, weight.shape[0]), jnp.bfloat16)],
        compiler_params=params(3),
        name="project_down",
    )(near, far, resident(weight))


def rotation_tables(positions, repeats):
    inverse = jnp.exp(
        (jnp.arange(HEAD_DIM) // 2).astype(jnp.float32) * (-2.0 / HEAD_DIM) * math.log(rope_base)
    )
    angles = positions[:, None] * inverse[None, :]
    sign = jnp.where(jnp.arange(HEAD_DIM) % 2 == 0, -1.0, 1.0)
    return (
        jnp.tile(jnp.cos(angles), (repeats, 1)),
        jnp.tile(jnp.sin(angles) * sign[None, :], (repeats, 1)),
    )


def local(
    states,
    attn_gain,
    ffn_gain,
    w_query,
    w_kv,
    w_out,
    w_gate,
    w_up,
    w_down,
    key_cache,
    value_cache,
    lengths,
):
    tensor_index = lax.axis_index("tensor")
    slots = lax.axis_size("tensor")
    inner_index = lax.axis_index("inner")
    own_rows = states.shape[0]
    all_rows = own_rows * slots

    rows = jnp.concatenate(exchange(states, "tensor"), axis=0)
    w_query, w_kv = load(w_query, w_kv, after=states)
    my_lengths = lax.dynamic_slice_in_dim(lengths, tensor_index * own_rows, own_rows, 0)
    meta = jnp.concatenate([jnp.stack([tensor_index, inner_index]).astype(jnp.int32), my_lengths])
    cosine, sine = rotation_tables(my_lengths.astype(jnp.float32), slots)

    flat = (own_rows, key_cache.shape[1] * KV_HEADS, HEAD_DIM)
    keys = key_cache.reshape(flat)
    values = value_cache.reshape(flat)
    joined = project_qkv(meta, rows, attn_gain[None, :], w_query, w_kv)
    keys, values = load(keys, values, after=joined)
    pieces = [joined[k * own_rows : (k + 1) * own_rows] for k in range(slots)]
    joined = jnp.concatenate(scatter_slots(pieces, "tensor"), axis=0)
    joined, keys, values = lax.optimization_barrier((joined, keys, values))
    near, far = pair_sums(joined, "inner")
    shard = attend(meta, cosine, sine, near, far, keys, values, slots)
    (w_out,) = load(w_out, after=shard)
    attended = combine(exchange(shard, "inner"), [w_out], all_rows)
    (w_up,) = load(w_up, after=attended)

    pieces = [attended[k * own_rows : (k + 1) * own_rows] for k in range(slots)]
    picked = scatter_slots(pieces, "tensor")
    left = jnp.concatenate([picked[s ^ k] for k in range(slots) for s in range(slots)], axis=0)
    parts = project_out(left, w_out, w_up, slots)
    (w_gate,) = load(w_gate, after=parts[0])
    parts = scatter_slots(parts, "tensor")
    joined, updated = gate_up(meta, rows, ffn_gain[None, :], parts, w_gate, w_up, own_rows)
    (w_down,) = load(w_down, after=joined)

    near, far = pair_sums(joined, "inner")
    part = project_down(near, far, w_down)
    pieces = [part[k * own_rows : (k + 1) * own_rows] for k in range(slots)]
    parts = scatter_slots(pieces, "tensor")
    down_sum = sum(p.astype(jnp.float32) for p in parts)
    return (updated + down_sum).astype(jnp.bfloat16)


def solution(mesh):
    in_specs = (
        P(("groups", "tensor"), "inner"),
        P("inner"),
        P("inner"),
        P("inner", "tensor"),
        P("inner", "tensor"),
        P("tensor", "inner"),
        P("inner", "tensor"),
        P("inner", "tensor"),
        P("tensor", "inner"),
        P(("groups", "tensor"), "inner", None, None),
        P(("groups", "tensor"), "inner", None, None),
        P("groups"),
    )
    out_specs = P(("groups", "tensor"), "inner")
    return jax.shard_map(local, mesh=mesh, in_specs=in_specs, out_specs=out_specs, check_vma=False)
```

time: 205 us -> 96.3 us (0.47)
  blocking collectives: 102 us -> 0 us
  Pallas kernels: 0 us -> 36.5 us
  matrix products: 31.7 us -> 0 us
  waiting for transfers between devices: 38.5 us -> 9.65 us
  starting transfers between devices: 7.94 us -> 27.7 us
  local copies, waits for them, and re-layouts: 5.14 us -> 20.2 us
  between operations: 14.3 us -> 0.3 us
  other arithmetic: 4.66 us -> 1.66 us
    pallas_call x0 -> x12, Pallas kernels: none -> 36.5 us  [the longest x6 22.6 us: load(): pl.pallas_call(functools.partial(load_kernel, len(weights)), out_shape=tu...]
    unnamed x2 -> x0, blocking collectives: 35.3 us -> none
    psum x4 -> x0, blocking collectives: 34.5 us -> none  [the longest x2 14 us: normalize(): square_sums = lax.psum(jnp.sum(widened * widened, axis=1), 'inner')]
    dot_general x9 -> x0, matrix products: 31.7 us -> none  [the longest x1 7.79 us: local(): upward_part = jnp.dot(normed_two, w_up, preferred_element_type=jnp.float32)]
    psum x1 -> x0, waiting for transfers between devices: 28.8 us -> none  [local(): lax.psum(upward_part.astype(jnp.bfloat16), 'inner').astype(jnp.float32)]
    ppermute x0 -> x22, starting transfers between devices: none -> 27.7 us  [swap_with(): return lax.ppermute(value, axis, [(i, i ^ step) for i in range(count)])]
    all_gather x2 -> x0, blocking collectives: 26.5 us -> none  [normalize(): lax.all_gather(scaled.astype(jnp.bfloat16), 'tensor', axis=0, tiled=True)]
    unnamed x19 -> x20, local copies, waits for them, and re-layouts: 0.96 us -> 19.2 us
  transfers between devices with their start and end apart: 3 -> 22, of which waited for: 3 -> 7; matrix products, arithmetic and copies ran while one was open for 0% -> 2% of each run, Pallas kernels for 0% -> 24%
where the time goes in v2:
time: 96.3 us; the launch traced here: 95.9 us
  Pallas kernels  36.5 us (38%)
  starting transfers between devices  27.7 us (29%)
  local copies, waits for them, and re-layouts  20.2 us (21%)
  waiting for transfers between devices  9.65 us (10%)
  other arithmetic  1.66 us (2%)
    ppermute x22, starting transfers between devices, swap_with(): return lax.ppermute(value, axis, [(i, i ^ step) for i in range(count)])  27.7 us
    pallas_call x6, Pallas kernels, load(): pl.pallas_call(functools.partial(load_kernel, len(weights)), out_shape=tu...  22.6 us
    unnamed x20, local copies, waits for them, and re-layouts  19.2 us
    ppermute x22, waiting for transfers between devices, swap_with(): return lax.ppermute(value, axis, [(i, i ^ step) for i in range(count)])  9.65 us
    pallas_call x1, Pallas kernels, gate_up(): pl.pallas_call(functools.partial(gate_up_kernel, slots), out_shape=(jax.S...  6.05 us
    pallas_call x1, Pallas kernels, project_down(): pl.pallas_call(down_kernel, out_shape=jax.ShapeDtypeStruct((rows, weight....  2.48 us
    pallas_call x1, Pallas kernels, attend(): pl.pallas_call(functools.partial(attend_kernel, slots), out_shape=jax.Sha...  2.27 us
  transfers between devices with their start and end apart: 22, of which 7 were waited for; matrix products, arithmetic and copies ran while one was open for 2% of the time, Pallas kernels for 24%

profile of v2, /device:TPU:0, one launch (start us, length us, event | category | flops | bytes accessed | tf_op | source)
XLA Modules:
  0.0 95.9 jit_solution(87485271690753538)
XLA Ops:
  0.0 5.0 %collective-permute-start.2 = (bf16[2,2048]{1,0:T(2,128)(2,1)}, bf16[2,2048]{1,0:T(2,128)(2,1)S(1)}, u32[]{:S(2)}, u32[]{:S(2)}) collective-permute-start(bf16[2,2048]{1,0:T(2,128)(2,1)} %refs_2_.1), channel_id=1, source_target_pairs={{0,12},{4,8},{8,4},{12,0},{1,13},{5,9},{9,5},{13,1},{2,14},{6,10},... | collective-permute-start | bytes 24584 | tf_op jit(solution)/shard_map/ppermute | solution.py:29
  5.1 0.6 collective-permute-start
  5.6 0.7 fusion.4
  6.3 0.1 pad_add_fusion.meta_ref
  6.4 0.7 broadcast_in_dim.20.gain_ref
  7.1 0.7 copy-done.4
  7.8 2.5 %load.6 = (bf16[2048,1024]{1,0:T(8,128)(2,1)S(1)}, bf16[2048,256]{1,0:T(8,128)(2,1)S(1)}) custom-call(bf16[2048,1024]{1,0:T(8,128)(2,1)} %refs_0_.5, bf16[2048,256]{1,0:T(8,128)(2,1)} %refs_1_.1, bf16[2,2048]{1,0:T(2,128)(2,1)S(1)} %copy-done.4), custom_call_target="tpu_custom_call" | custom-call | bytes 5242880 | tf_op jit(solution)/shard_map/load/pallas_call | solution.py:112
  10.3 0.0 collective-permute-done.2
  10.3 0.0 collective-permute-done
  10.4 1.6 %project_qkv.1.refs_2_ = bf16[8,1408]{1,0:T(8,128)(2,1)S(1)} custom-call(s32[4]{0:T(128)S(1)} %pad_add_fusion.meta_ref, bf16[8,2048]{1,0:T(8,128)(2,1)S(1)} %pad_maximum_fusion.rows_ref, bf16[1,2048]{1,0:T(2,128)(2,1)S(1)} %broadcast_in_dim.20.gain_ref, bf16[2048,1024]{1,0:T(8,128)(2,1)S(1)} %get-tuple-element.18.wq_ref, ...), custom_call_target="tpu_custom_call" | custom-call | tf_op jit(solution)/shard_map/project_qkv/pallas_call | solution.py:145
  12.1 3.9 %collective-permute-start.5 = (bf16[2,1408]{1,0:T(2,128)(2,1)S(1)}, bf16[2,1408]{1,0:T(2,128)(2,1)S(1)}, u32[]{:S(2)}, u32[]{:S(2)}) collective-permute-start(bf16[2,1408]{1,0:T(2,128)(2,1)S(1)} %get-tuple-element.37), channel_id=1, source_target_pairs={{0,12},{4,8},{8,4},{12,0},{1,13},{5,9},{9,5},{13,1},{2,14},{6,10},... | collective-permute-start | bytes 16904 | tf_op jit(solution)/shard_map/ppermute | solution.py:29
  16.0 0.0 collective-permute-start.4
  16.0 0.6 collective-permute-start.3
  16.6 2.2 %load.7 = (bf16[2,4096,128]{2,1,0:T(8,128)(2,1)S(1)}, bf16[2,4096,128]{2,1,0:T(8,128)(2,1)S(1)}) custom-call(bf16[2,4096,128]{2,1,0:T(8,128)(2,1)} %bitcast.10, bf16[2,4096,128]{2,1,0:T(8,128)(2,1)} %bitcast.11, bf16[8,1408]{1,0:T(8,128)(2,1)S(1)} %project_qkv.1.refs_2_), custom_call_target="tpu_custom_call" | custom-call | bytes 4194304 | tf_op jit(solution)/shard_map/load/pallas_call | solution.py:112
  18.9 1.6 %collective-permute-done.4 = bf16[2,1408]{1,0:T(2,128)(2,1)S(1)} collective-permute-done((bf16[2,1408]{1,0:T(2,128)(2,1)S(1)}, bf16[2,1408]{1,0:T(2,128)(2,1)S(1)}, u32[]{:S(2)}, u32[]{:S(2)}) %collective-permute-start.4) | collective-permute-done | bytes 5664 | tf_op jit(solution)/shard_map/ppermute | solution.py:29
  20.5 0.0 collective-permute-done.3
  20.5 0.1 collective-permute-start.6
  20.6 1.2 %collective-permute-done.6 = bf16[8,1408]{1,0:T(8,128)(2,1)S(1)} collective-permute-done((bf16[8,1408]{1,0:T(8,128)(2,1)S(1)}, bf16[8,1408]{1,0:T(8,128)(2,1)S(1)}, u32[]{:S(2)}, u32[]{:S(2)}) %collective-permute-start.6) | collective-permute-done | bytes 22560 | tf_op jit(solution)/shard_map/ppermute | solution.py:29
  21.8 1.6 %collective-permute-start.7 = (bf16[8,1408]{1,0:T(8,128)(2,1)S(1)}, bf16[8,1408]{1,0:T(8,128)(2,1)S(1)}, u32[]{:S(2)}, u32[]{:S(2)}) collective-permute-start(bf16[8,1408]{1,0:T(8,128)(2,1)S(1)} %add_convert_fusion.1.near_ref), channel_id=1, source_target_pairs={{0,2},{1,3},{2,0},{3,1},{4,6},{5,7},{6,4},{7,5},{8,10},{9,11},{10,... | collective-permute-start | bytes 67592 | tf_op jit(solution)/shard_map/ppermute | solution.py:29
  23.4 0.1 fusion
  23.5 2.2 %collective-permute-done.7.far_ref = bf16[8,1408]{1,0:T(8,128)(2,1)S(1)} collective-permute-done((bf16[8,1408]{1,0:T(8,128)(2,1)S(1)}, bf16[8,1408]{1,0:T(8,128)(2,1)S(1)}, u32[]{:S(2)}, u32[]{:S(2)}) %collective-permute-start.7) | collective-permute-done | bytes 22560 | tf_op jit(solution)/shard_map/ppermute | solution.py:29
  25.7 2.3 %attend.1.refs_1_.refs_0_ = bf16[64,256]{1,0:T(8,128)(2,1)S(1)} custom-call(s32[4]{0:T(128)S(1)} %pad_add_fusion.meta_ref, f32[8,128]{1,0:T(8,128)S(1)} %bitcast.9, f32[8,128]{1,0:T(8,128)S(1)} %bitcast.8, bf16[8,1408]{1,0:T(8,128)(2,1)S(1)} %add_convert_fusion.1.near_ref, bf16[8,1408]{1,0:T(8,128)(2,1)S(1)} %collective-permute-done.7.far_ref, ...), custom_call_target="tpu_custom_call" | custom-call | tf_op jit(solution)/shard_map/attend/pallas_call | solution.py:259
  27.9 0.2 collective-permute-start.10
  28.1 1.5 %collective-permute-start.9 = (bf16[64,256]{1,0:T(8,128)(2,1)S(1)}, bf16[64,256]{1,0:T(8,128)(2,1)S(1)}, u32[]{:S(2)}, u32[]{:S(2)}) collective-permute-start(bf16[64,256]{1,0:T(8,128)(2,1)S(1)} %attend.1.refs_1_.refs_0_), channel_id=1, source_target_pairs={{0,2},{1,3},{2,0},{3,1},{4,6},{5,7},{6,4},{7,5},{8,10},{9,11},{10,... | collective-permute-start | bytes 98312 | tf_op jit(solution)/shard_map/ppermute | solution.py:29
  29.6 0.3 collective-permute-start.8
  29.9 2.2 %load.8.refs_4_.weight_ref = bf16[1024,2048]{1,0:T(8,128)(2,1)S(1)} custom-call(bf16[1024,2048]{1,0:T(8,128)(2,1)} %refs_0_.6, bf16[64,256]{1,0:T(8,128)(2,1)S(1)} %attend.1.refs_1_.refs_0_), custom_call_target="tpu_custom_call" | custom-call | bytes 4194304 | tf_op jit(solution)/shard_map/load/pallas_call | solution.py:112
  32.1 0.0 collective-permute-done.8.refs_1_
  32.1 0.3 combine.1.refs_1_
  32.4 2.0 %copy-done.2 = bf16[1024,2048]{1,0:T(8,128)(2,1)} copy-done((bf16[1024,2048]{1,0:T(8,128)(2,1)}, bf16[1024,2048]{1,0:T(8,128)(2,1)S(1)}, u32[]{:S(2)}) %copy-start.2) | copy-done | bytes 4194328
  34.4 2.2 %collective-permute-start.13 = (bf16[2,1024]{1,0:T(2,128)(2,1)S(1)}, bf16[2,1024]{1,0:T(2,128)(2,1)S(1)}, u32[]{:S(2)}, u32[]{:S(2)}) collective-permute-start(bf16[2,1024]{1,0:T(2,128)(2,1)S(1)} %get-tuple-element.40), channel_id=1, source_target_pairs={{0,12},{4,8},{8,4},{12,0},{1,13},{5,9},{9,5},{13,1},{2,14},{6,10},... | collective-permute-start | bytes 12296 | tf_op jit(solution)/shard_map/ppermute | solution.py:29
  36.6 0.0 collective-permute-start.12
  36.6 2.2 %collective-permute-start.11 = (bf16[2,1024]{1,0:T(2,128)(2,1)S(1)}, bf16[2,1024]{1,0:T(2,128)(2,1)S(1)}, u32[]{:S(2)}, u32[]{:S(2)}) collective-permute-start(bf16[2,1024]{1,0:T(2,128)(2,1)S(1)} %get-tuple-element.42), channel_id=1, source_target_pairs={{0,4},{4,0},{8,12},{12,8},{1,5},{5,1},{9,13},{13,9},{2,6},{6,2},{1... | collective-permute-start | bytes 12296 | tf_op jit(solution)/shard_map/ppermute | solution.py:29
  38.8 5.2 %load.9.later_ref.refs_5_ = bf16[2048,3584]{1,0:T(8,128)(2,1)S(1)} custom-call(bf16[2048,3584]{1,0:T(8,128)(2,1)} %refs_0_.7, bf16[8,1024]{1,0:T(8,128)(2,1)S(1)} %combine.1.refs_1_), custom_call_target="tpu_custom_call" | custom-call | bytes 14680064 | tf_op jit(solution)/shard_map/load/pallas_call | solution.py:112
  44.0 5.2 %copy-done = bf16[2048,3584]{1,0:T(8,128)(2,1)} copy-done((bf16[2048,3584]{1,0:T(8,128)(2,1)}, bf16[2048,3584]{1,0:T(8,128)(2,1)S(1)}, u32[]{:S(2)}) %copy-start) | copy-done | bytes 14680088
  49.2 0.1 concatenate.15.left_ref
  49.4 5.2 %copy-done.1 = bf16[2048,3584]{1,0:T(8,128)(2,1)S(1)} copy-done((bf16[2048,3584]{1,0:T(8,128)(2,1)S(1)}, bf16[2048,3584]{1,0:T(8,128)(2,1)}, u32[]{:S(2)}) %copy-start.1) | copy-done | bytes 14680088
  54.5 2.2 %copy-done.3 = bf16[1024,2048]{1,0:T(8,128)(2,1)S(1)} copy-done((bf16[1024,2048]{1,0:T(8,128)(2,1)S(1)}, bf16[1024,2048]{1,0:T(8,128)(2,1)}, u32[]{:S(2)}) %copy-start.3) | copy-done | bytes 4194328
  56.7 1.1 %project_out.1 = (bf16[8,2048]{1,0:T(8,128)(2,1)S(1)}, bf16[8,2048]{1,0:T(8,128)(2,1)S(1)}, bf16[8,2048]{1,0:T(8,128)(2,1)S(1)}, bf16[8,2048]{1,0:T(8,128)(2,1)S(1)}) custom-call(bf16[32,1024]{1,0:T(8,128)(2,1)S(1)} %concatenate.15.left_ref, bf16[1024,2048]{1,0:T(8,128)(2,1)S(1)} %copy-done.3, bf16[2048,3584]{1,0:T(8,128)(2,1)S(1)} %copy-done.1), custom_call_target="tpu_custom_call" | custom-call | tf_op jit(solution)/shard_map/project_out/pallas_call | solution.py:327
  57.9 0.0 collective-permute-start.14
  57.9 2.7 %collective-permute-start.15 = (bf16[8,2048]{1,0:T(8,128)(2,1)S(1)}, bf16[8,2048]{1,0:T(8,128)(2,1)S(1)}, u32[]{:S(2)}, u32[]{:S(2)}) collective-permute-start(bf16[8,2048]{1,0:T(8,128)(2,1)S(1)} %get-tuple-element.27), channel_id=1, source_target_pairs={{0,8},{4,12},{8,0},{12,4},{1,9},{5,13},{9,1},{13,5},{2,10},{6,14},... | collective-permute-start | bytes 98312 | tf_op jit(solution)/shard_map/ppermute | solution.py:29
  60.6 1.7 %collective-permute-start.16 = (bf16[8,2048]{1,0:T(8,128)(2,1)S(1)}, bf16[8,2048]{1,0:T(8,128)(2,1)S(1)}, u32[]{:S(2)}, u32[]{:S(2)}) collective-permute-start(bf16[8,2048]{1,0:T(8,128)(2,1)S(1)} %get-tuple-element.28), channel_id=1, source_target_pairs={{0,12},{4,8},{8,4},{12,0},{1,13},{5,9},{9,5},{13,1},{2,14},{6,10},... | collective-permute-start | bytes 98312 | tf_op jit(solution)/shard_map/ppermute | solution.py:29
  62.3 0.0 slice-start
  62.3 0.0 slice-start.1
  62.3 0.0 slice-start.3
  62.3 5.3 %load.10.refs_4_ = bf16[2048,3584]{1,0:T(8,128)(2,1)S(1)} custom-call(bf16[2048,3584]{1,0:T(8,128)(2,1)} %refs_0_.8, bf16[8,2048]{1,0:T(8,128)(2,1)S(1)} %get-tuple-element.25.refs_1_.refs_0_), custom_call_target="tpu_custom_call" | custom-call | bytes 14680064 | tf_op jit(solution)/shard_map/load/pallas_call | solution.py:112
  67.7 0.0 collective-permute-done.15.refs_2_
  67.7 0.0 collective-permute-done.16.refs_3_
  67.7 0.9 slice-done
  68.7 1.3 %slice-done.1 = s8[4194304]{0:T(1024)(128)(4,1)S(1)} async-done(((s8[14680064]{0:T(1024)(128)(4,1)}), s8[4194304]{0:T(1024)(128)(4,1)S(1)}, s32[]{:S(2)}) %slice-start.1) | async-done | bytes 4194328
  69.9 1.2 %slice-done.2 = s8[4194304]{0:T(1024)(128)(4,1)S(1)} async-done(((s8[14680064]{0:T(1024)(128)(4,1)}), s8[4194304]{0:T(1024)(128)(4,1)S(1)}, s32[]{:S(2)}) %slice-start.2) | async-done | bytes 4194328
  71.1 0.6 slice-done.3
  71.7 6.0 %gate_up.1 = (bf16[8,7296]{1,0:T(8,128)(2,1)S(1)}, f32[2,2048]{1,0:T(2,128)S(1)}) custom-call(s32[4]{0:T(128)S(1)} %pad_add_fusion.meta_ref, bf16[8,2048]{1,0:T(8,128)(2,1)S(1)} %pad_maximum_fusion.rows_ref, bf16[1,2048]{1,0:T(2,128)(2,1)S(1)} %broadcast_in_dim.17.gain_ref, bf16[8,2048]{1,0:T(8,128)(2,1)S(1)} %get-tuple-element.25.refs_1_.refs_0_, ...), custom_call_target="tpu_custom_call" | custom-call | tf_op jit(solution)/shard_map/gate_up/pallas_call | solution.py:366
  77.8 0.0 collective-permute-start.17
  77.8 1.3 %collective-permute-done.17 = bf16[8,7296]{1,0:T(8,128)(2,1)S(1)} collective-permute-done((bf16[8,7296]{1,0:T(8,128)(2,1)S(1)}, bf16[8,7296]{1,0:T(8,128)(2,1)S(1)}, u32[]{:S(2)}, u32[]{:S(2)}) %collective-permute-start.17) | collective-permute-done | bytes 116768 | tf_op jit(solution)/shard_map/ppermute | solution.py:29
  79.2 1.6 %collective-permute-start.18 = (bf16[8,7296]{1,0:T(8,128)(2,1)S(1)}, bf16[8,7296]{1,0:T(8,128)(2,1)S(1)}, u32[]{:S(2)}, u32[]{:S(2)}) collective-permute-start(bf16[8,7296]{1,0:T(8,128)(2,1)S(1)} %add_convert_fusion.near_ref), channel_id=1, source_target_pairs={{0,2},{1,3},{2,0},{3,1},{4,6},{5,7},{6,4},{7,5},{8,10},{9,11},{10,... | collective-permute-start | bytes 350216 | tf_op jit(solution)/shard_map/ppermute | solution.py:29
  80.7 5.2 %load.11.weight_ref = bf16[3584,2048]{1,0:T(8,128)(2,1)S(1)} custom-call(bf16[3584,2048]{1,0:T(8,128)(2,1)} %refs_0_.9, bf16[8,7296]{1,0:T(8,128)(2,1)S(1)} %get-tuple-element.30.refs_1_), custom_call_target="tpu_custom_call" | custom-call | bytes 14680064 | tf_op jit(solution)/shard_map/load/pallas_call | solution.py:112
  85.9 2.5 %project_down.1 = bf16[8,2048]{1,0:T(8,128)(2,1)S(1)} custom-call(bf16[8,7296]{1,0:T(8,128)(2,1)S(1)} %add_convert_fusion.near_ref, bf16[8,7296]{1,0:T(8,128)(2,1)S(1)} %collective-permute-done.18.far_ref, bf16[3584,2048]{1,0:T(8,128)(2,1)S(1)} %load.11.weight_ref), custom_call_target="tpu_custom_call" | custom-call | tf_op jit(solution)/shard_map/project_down/pallas_call | solution.py:403
  88.4 0.1 collective-permute-start.19
  88.5 2.2 %collective-permute-start.21 = (bf16[2,2048]{1,0:T(2,128)(2,1)S(1)}, bf16[2,2048]{1,0:T(2,128)(2,1)S(1)}, u32[]{:S(2)}, u32[]{:S(2)}) collective-permute-start(bf16[2,2048]{1,0:T(2,128)(2,1)S(1)} %get-tuple-element.34), channel_id=1, source_target_pairs={{0,12},{4,8},{8,4},{12,0},{1,13},{5,9},{9,5},{13,1},{2,14},{6,10},... | collective-permute-start | bytes 24584 | tf_op jit(solution)/shard_map/ppermute | solution.py:29
  90.7 1.3 %collective-permute-start.20 = (bf16[2,2048]{1,0:T(2,128)(2,1)S(1)}, bf16[2,2048]{1,0:T(2,128)(2,1)S(1)}, u32[]{:S(2)}, u32[]{:S(2)}) collective-permute-start(bf16[2,2048]{1,0:T(2,128)(2,1)S(1)} %get-tuple-element.35), channel_id=1, source_target_pairs={{0,8},{4,12},{8,0},{12,4},{1,9},{5,13},{9,1},{13,5},{2,10},{6,14},... | collective-permute-start | bytes 24584 | tf_op jit(solution)/shard_map/ppermute | solution.py:29
  92.0 0.2 collective-permute-done.19
  92.2 1.9 %collective-permute-done.21 = bf16[2,2048]{1,0:T(2,128)(2,1)S(1)} collective-permute-done((bf16[2,2048]{1,0:T(2,128)(2,1)S(1)}, bf16[2,2048]{1,0:T(2,128)(2,1)S(1)}, u32[]{:S(2)}, u32[]{:S(2)}) %collective-permute-start.21) | collective-permute-done | bytes 8224 | tf_op jit(solution)/shard_map/ppermute | solution.py:29
  94.0 1.2 %collective-permute-done.20 = bf16[2,2048]{1,0:T(2,128)(2,1)S(1)} collective-permute-done((bf16[2,2048]{1,0:T(2,128)(2,1)S(1)}, bf16[2,2048]{1,0:T(2,128)(2,1)S(1)}, u32[]{:S(2)}, u32[]{:S(2)}) %collective-permute-start.20) | collective-permute-done | bytes 8224 | tf_op jit(solution)/shard_map/ppermute | solution.py:29
  95.3 0.6 add_convert_fusion.2
  (30 shorter events, 0.2 us)
Async XLA Ops:
  0.0 10.3 %collective-permute-start.2 = (bf16[2,2048]{1,0:T(2,128)(2,1)}, bf16[2,2048]{1,0:T(2,128)(2,1)S(1)}, u32[]{:S(2)}, u32[]{:S(2)}) collective-permute-start(bf16[2,2048]{1,0:T(2,128)(2,1)} %refs_2_.1), channel_id=1, source_target_pairs={{0,12},{4,8},{8,4},{12,0},{1,13},{5,9},{9,5},{13,1},{2,14},{6,10},... | collective-permute-start | bytes 24584 | tf_op jit(solution)/shard_map/ppermute | solution.py:29
  5.0 5.3 %collective-permute-start.1 = (bf16[2,2048]{1,0:T(2,128)(2,1)}, bf16[2,2048]{1,0:T(2,128)(2,1)S(1)}, u32[]{:S(2)}, u32[]{:S(2)}) collective-permute-start(bf16[2,2048]{1,0:T(2,128)(2,1)} %refs_2_.1), channel_id=1, source_target_pairs={{0,8},{4,12},{8,0},{12,4},{1,9},{5,13},{9,1},{13,5},{2,10},{6,14},... | collective-permute-start | bytes 24584 | tf_op jit(solution)/shard_map/ppermute | solution.py:29
  5.1 5.3 %collective-permute-start = (bf16[2,2048]{1,0:T(2,128)(2,1)}, bf16[2,2048]{1,0:T(2,128)(2,1)S(1)}, u32[]{:S(2)}, u32[]{:S(2)}) collective-permute-start(bf16[2,2048]{1,0:T(2,128)(2,1)} %refs_2_.1), channel_id=1, source_target_pairs={{0,4},{4,0},{8,12},{12,8},{1,5},{5,1},{9,13},{13,9},{2,6},{6,2},{1... | collective-permute-start | bytes 24584 | tf_op jit(solution)/shard_map/ppermute | solution.py:29
  7.1 0.7 copy-start.4
  12.1 6.8 %collective-permute-start.5 = (bf16[2,1408]{1,0:T(2,128)(2,1)S(1)}, bf16[2,1408]{1,0:T(2,128)(2,1)S(1)}, u32[]{:S(2)}, u32[]{:S(2)}) collective-permute-start(bf16[2,1408]{1,0:T(2,128)(2,1)S(1)} %get-tuple-element.37), channel_id=1, source_target_pairs={{0,12},{4,8},{8,4},{12,0},{1,13},{5,9},{9,5},{13,1},{2,14},{6,10},... | collective-permute-start | bytes 16904 | tf_op jit(solution)/shard_map/ppermute | solution.py:29
  16.0 4.5 %collective-permute-start.4 = (bf16[2,1408]{1,0:T(2,128)(2,1)S(1)}, bf16[2,1408]{1,0:T(2,128)(2,1)S(1)}, u32[]{:S(2)}, u32[]{:S(2)}) collective-permute-start(bf16[2,1408]{1,0:T(2,128)(2,1)S(1)} %get-tuple-element.38), channel_id=1, source_target_pairs={{0,8},{4,12},{8,0},{12,4},{1,9},{5,13},{9,1},{13,5},{2,10},{6,14},... | collective-permute-start | bytes 16904 | tf_op jit(solution)/shard_map/ppermute | solution.py:29
  16.0 4.5 %collective-permute-start.3 = (bf16[2,1408]{1,0:T(2,128)(2,1)S(1)}, bf16[2,1408]{1,0:T(2,128)(2,1)S(1)}, u32[]{:S(2)}, u32[]{:S(2)}) collective-permute-start(bf16[2,1408]{1,0:T(2,128)(2,1)S(1)} %get-tuple-element.39), channel_id=1, source_target_pairs={{0,4},{4,0},{8,12},{12,8},{1,5},{5,1},{9,13},{13,9},{2,6},{6,2},{1... | collective-permute-start | bytes 16904 | tf_op jit(solution)/shard_map/ppermute | solution.py:29
  20.5 1.3 %collective-permute-start.6 = (bf16[8,1408]{1,0:T(8,128)(2,1)S(1)}, bf16[8,1408]{1,0:T(8,128)(2,1)S(1)}, u32[]{:S(2)}, u32[]{:S(2)}) collective-permute-start(bf16[8,1408]{1,0:T(8,128)(2,1)S(1)} %pad_maximum_fusion.1), channel_id=1, source_target_pairs={{0,1},{1,0},{2,3},{3,2},{4,5},{5,4},{6,7},{7,6},{8,9},{9,8},{10,11... | collective-permute-start | bytes 67592 | tf_op jit(solution)/shard_map/ppermute | solution.py:29
  21.8 3.9 %collective-permute-start.7 = (bf16[8,1408]{1,0:T(8,128)(2,1)S(1)}, bf16[8,1408]{1,0:T(8,128)(2,1)S(1)}, u32[]{:S(2)}, u32[]{:S(2)}) collective-permute-start(bf16[8,1408]{1,0:T(8,128)(2,1)S(1)} %add_convert_fusion.1.near_ref), channel_id=1, source_target_pairs={{0,2},{1,3},{2,0},{3,1},{4,6},{5,7},{6,4},{7,5},{8,10},{9,11},{10,... | collective-permute-start | bytes 67592 | tf_op jit(solution)/shard_map/ppermute | solution.py:29
  27.9 4.1 %collective-permute-start.10 = (bf16[64,256]{1,0:T(8,128)(2,1)S(1)}, bf16[64,256]{1,0:T(8,128)(2,1)S(1)}, u32[]{:S(2)}, u32[]{:S(2)}) collective-permute-start(bf16[64,256]{1,0:T(8,128)(2,1)S(1)} %attend.1.refs_1_.refs_0_), channel_id=1, source_target_pairs={{0,3},{1,2},{2,1},{3,0},{4,7},{5,6},{6,5},{7,4},{8,11},{9,10},{10,... | collective-permute-start | bytes 98312 | tf_op jit(solution)/shard_map/ppermute | solution.py:29
  28.1 4.0 %collective-permute-start.9 = (bf16[64,256]{1,0:T(8,128)(2,1)S(1)}, bf16[64,256]{1,0:T(8,128)(2,1)S(1)}, u32[]{:S(2)}, u32[]{:S(2)}) collective-permute-start(bf16[64,256]{1,0:T(8,128)(2,1)S(1)} %attend.1.refs_1_.refs_0_), channel_id=1, source_target_pairs={{0,2},{1,3},{2,0},{3,1},{4,6},{5,7},{6,4},{7,5},{8,10},{9,11},{10,... | collective-permute-start | bytes 98312 | tf_op jit(solution)/shard_map/ppermute | solution.py:29
  29.6 2.5 %collective-permute-start.8 = (bf16[64,256]{1,0:T(8,128)(2,1)S(1)}, bf16[64,256]{1,0:T(8,128)(2,1)S(1)}, u32[]{:S(2)}, u32[]{:S(2)}) collective-permute-start(bf16[64,256]{1,0:T(8,128)(2,1)S(1)} %attend.1.refs_1_.refs_0_), channel_id=1, source_target_pairs={{0,1},{1,0},{2,3},{3,2},{4,5},{5,4},{6,7},{7,6},{8,9},{9,8},{10,11... | collective-permute-start | bytes 98312 | tf_op jit(solution)/shard_map/ppermute | solution.py:29
  32.4 2.0 %copy-start.2 = (bf16[1024,2048]{1,0:T(8,128)(2,1)}, bf16[1024,2048]{1,0:T(8,128)(2,1)S(1)}, u32[]{:S(2)}) copy-start(bf16[1024,2048]{1,0:T(8,128)(2,1)S(1)} %load.8.refs_4_.weight_ref) | copy-start | bytes 12582916
  34.4 14.8 %collective-permute-start.13 = (bf16[2,1024]{1,0:T(2,128)(2,1)S(1)}, bf16[2,1024]{1,0:T(2,128)(2,1)S(1)}, u32[]{:S(2)}, u32[]{:S(2)}) collective-permute-start(bf16[2,1024]{1,0:T(2,128)(2,1)S(1)} %get-tuple-element.40), channel_id=1, source_target_pairs={{0,12},{4,8},{8,4},{12,0},{1,13},{5,9},{9,5},{13,1},{2,14},{6,10},... | collective-permute-start | bytes 12296 | tf_op jit(solution)/shard_map/ppermute | solution.py:29
  36.6 12.6 %collective-permute-start.12 = (bf16[2,1024]{1,0:T(2,128)(2,1)S(1)}, bf16[2,1024]{1,0:T(2,128)(2,1)S(1)}, u32[]{:S(2)}, u32[]{:S(2)}) collective-permute-start(bf16[2,1024]{1,0:T(2,128)(2,1)S(1)} %get-tuple-element.41), channel_id=1, source_target_pairs={{0,8},{4,12},{8,0},{12,4},{1,9},{5,13},{9,1},{13,5},{2,10},{6,14},... | collective-permute-start | bytes 12296 | tf_op jit(solution)/shard_map/ppermute | solution.py:29
  36.6 12.6 %collective-permute-start.11 = (bf16[2,1024]{1,0:T(2,128)(2,1)S(1)}, bf16[2,1024]{1,0:T(2,128)(2,1)S(1)}, u32[]{:S(2)}, u32[]{:S(2)}) collective-permute-start(bf16[2,1024]{1,0:T(2,128)(2,1)S(1)} %get-tuple-element.42), channel_id=1, source_target_pairs={{0,4},{4,0},{8,12},{12,8},{1,5},{5,1},{9,13},{13,9},{2,6},{6,2},{1... | collective-permute-start | bytes 12296 | tf_op jit(solution)/shard_map/ppermute | solution.py:29
  44.0 5.2 %copy-start = (bf16[2048,3584]{1,0:T(8,128)(2,1)}, bf16[2048,3584]{1,0:T(8,128)(2,1)S(1)}, u32[]{:S(2)}) copy-start(bf16[2048,3584]{1,0:T(8,128)(2,1)S(1)} %load.9.later_ref.refs_5_) | copy-start | bytes 44040196
  49.4 5.2 %copy-start.1 = (bf16[2048,3584]{1,0:T(8,128)(2,1)S(1)}, bf16[2048,3584]{1,0:T(8,128)(2,1)}, u32[]{:S(2)}) copy-start(bf16[2048,3584]{1,0:T(8,128)(2,1)} %copy-done) | copy-start | bytes 44040196
  54.5 2.2 %copy-start.3 = (bf16[1024,2048]{1,0:T(8,128)(2,1)S(1)}, bf16[1024,2048]{1,0:T(8,128)(2,1)}, u32[]{:S(2)}) copy-start(bf16[1024,2048]{1,0:T(8,128)(2,1)} %copy-done.2) | copy-start | bytes 12582916
  56.7 5.6 %copy-start.5 = (bf16[2048]{0:T(1024)(128)(2,1)S(1)}, bf16[2048]{0:T(1024)(128)(2,1)}, u32[]{:S(2)}) copy-start(bf16[2048]{0:T(1024)(128)(2,1)} %param.14) | copy-start | bytes 12292
  57.9 9.8 %collective-permute-start.14 = (bf16[8,2048]{1,0:T(8,128)(2,1)S(1)}, bf16[8,2048]{1,0:T(8,128)(2,1)S(1)}, u32[]{:S(2)}, u32[]{:S(2)}) collective-permute-start(bf16[8,2048]{1,0:T(8,128)(2,1)S(1)} %get-tuple-element.26), channel_id=1, source_target_pairs={{0,4},{4,0},{8,12},{12,8},{1,5},{5,1},{9,13},{13,9},{2,6},{6,2},{1... | collective-permute-start | bytes 98312 | tf_op jit(solution)/shard_map/ppermute | solution.py:29
  57.9 9.8 %collective-permute-start.15 = (bf16[8,2048]{1,0:T(8,128)(2,1)S(1)}, bf16[8,2048]{1,0:T(8,128)(2,1)S(1)}, u32[]{:S(2)}, u32[]{:S(2)}) collective-permute-start(bf16[8,2048]{1,0:T(8,128)(2,1)S(1)} %get-tuple-element.27), channel_id=1, source_target_pairs={{0,8},{4,12},{8,0},{12,4},{1,9},{5,13},{9,1},{13,5},{2,10},{6,14},... | collective-permute-start | bytes 98312 | tf_op jit(solution)/shard_map/ppermute | solution.py:29
  60.6 7.1 %collective-permute-start.16 = (bf16[8,2048]{1,0:T(8,128)(2,1)S(1)}, bf16[8,2048]{1,0:T(8,128)(2,1)S(1)}, u32[]{:S(2)}, u32[]{:S(2)}) collective-permute-start(bf16[8,2048]{1,0:T(8,128)(2,1)S(1)} %get-tuple-element.28), channel_id=1, source_target_pairs={{0,12},{4,8},{8,4},{12,0},{1,13},{5,9},{9,5},{13,1},{2,14},{6,10},... | collective-permute-start | bytes 98312 | tf_op jit(solution)/shard_map/ppermute | solution.py:29
  62.3 6.4 %slice-start = ((s8[14680064]{0:T(1024)(128)(4,1)}), s8[4194304]{0:T(1024)(128)(4,1)S(1)}, s32[]{:S(2)}) async-start(s8[14680064]{0:T(1024)(128)(4,1)} %bitcast.6), calls=%async_computation | async-start | bytes 8388608
  62.3 7.6 %slice-start.1 = ((s8[14680064]{0:T(1024)(128)(4,1)}), s8[4194304]{0:T(1024)(128)(4,1)S(1)}, s32[]{:S(2)}) async-start(s8[14680064]{0:T(1024)(128)(4,1)} %bitcast.6), calls=%async_computation.1 | async-start | bytes 8388608
  62.3 8.8 %slice-start.2 = ((s8[14680064]{0:T(1024)(128)(4,1)}), s8[4194304]{0:T(1024)(128)(4,1)S(1)}, s32[]{:S(2)}) async-start(s8[14680064]{0:T(1024)(128)(4,1)} %bitcast.6), calls=%async_computation.2 | async-start | bytes 8388608
  62.3 9.4 %slice-start.3 = ((s8[14680064]{0:T(1024)(128)(4,1)}), s8[2097152]{0:T(1024)(128)(4,1)S(1)}, s32[]{:S(2)}) async-start(s8[14680064]{0:T(1024)(128)(4,1)} %bitcast.6), calls=%async_computation.3 | async-start | bytes 4194304
  77.8 1.3 %collective-permute-start.17 = (bf16[8,7296]{1,0:T(8,128)(2,1)S(1)}, bf16[8,7296]{1,0:T(8,128)(2,1)S(1)}, u32[]{:S(2)}, u32[]{:S(2)}) collective-permute-start(bf16[8,7296]{1,0:T(8,128)(2,1)S(1)} %get-tuple-element.30.refs_1_), channel_id=1, source_target_pairs={{0,1},{1,0},{2,3},{3,2},{4,5},{5,4},{6,7},{7,6},{8,9},{9,8},{10,11... | collective-permute-start | bytes 350216 | tf_op jit(solution)/shard_map/ppermute | solution.py:29
  79.2 6.8 %collective-permute-start.18 = (bf16[8,7296]{1,0:T(8,128)(2,1)S(1)}, bf16[8,7296]{1,0:T(8,128)(2,1)S(1)}, u32[]{:S(2)}, u32[]{:S(2)}) collective-permute-start(bf16[8,7296]{1,0:T(8,128)(2,1)S(1)} %add_convert_fusion.near_ref), channel_id=1, source_target_pairs={{0,2},{1,3},{2,0},{3,1},{4,6},{5,7},{6,4},{7,5},{8,10},{9,11},{10,... | collective-permute-start | bytes 350216 | tf_op jit(solution)/shard_map/ppermute | solution.py:29
  88.4 3.7 %collective-permute-start.19 = (bf16[2,2048]{1,0:T(2,128)(2,1)S(1)}, bf16[2,2048]{1,0:T(2,128)(2,1)S(1)}, u32[]{:S(2)}, u32[]{:S(2)}) collective-permute-start(bf16[2,2048]{1,0:T(2,128)(2,1)S(1)} %get-tuple-element.33), channel_id=1, source_target_pairs={{0,4},{4,0},{8,12},{12,8},{1,5},{5,1},{9,13},{13,9},{2,6},{6,2},{1... | collective-permute-start | bytes 24584 | tf_op jit(solution)/shard_map/ppermute | solution.py:29
  88.5 5.5 %collective-permute-start.21 = (bf16[2,2048]{1,0:T(2,128)(2,1)S(1)}, bf16[2,2048]{1,0:T(2,128)(2,1)S(1)}, u32[]{:S(2)}, u32[]{:S(2)}) collective-permute-start(bf16[2,2048]{1,0:T(2,128)(2,1)S(1)} %get-tuple-element.34), channel_id=1, source_target_pairs={{0,12},{4,8},{8,4},{12,0},{1,13},{5,9},{9,5},{13,1},{2,14},{6,10},... | collective-permute-start | bytes 24584 | tf_op jit(solution)/shard_map/ppermute | solution.py:29
  90.7 4.5 %collective-permute-start.20 = (bf16[2,2048]{1,0:T(2,128)(2,1)S(1)}, bf16[2,2048]{1,0:T(2,128)(2,1)S(1)}, u32[]{:S(2)}, u32[]{:S(2)}) collective-permute-start(bf16[2,2048]{1,0:T(2,128)(2,1)S(1)} %get-tuple-element.35), channel_id=1, source_target_pairs={{0,8},{4,12},{8,0},{12,4},{1,9},{5,13},{9,1},{13,5},{2,10},{6,14},... | collective-permute-start | bytes 24584 | tf_op jit(solution)/shard_map/ppermute | solution.py:29

commit v3 on v2

--- a/solution.py
+++ b/solution.py
@@ -309,10 +309,19 @@
     )(*parts, *[resident(w) for w in later])
 
 
-def out_kernel(left_ref, weight_ref, later_ref, *outs):
+def out_kernel(slots, weight_ref, later_ref, *refs):
     del later_ref
-    left = left_ref[...]
+    picked = refs[:slots]
+    outs = refs[slots : 2 * slots]
+    left_s = refs[2 * slots]
     rows = outs[0].shape[0]
+    own_rows = picked[0].shape[0]
+    values = [ref[...].astype(jnp.float32) for ref in picked]
+    for k in range(slots):
+        for s in range(slots):
+            place = (k * slots + s) * own_rows
+            left_s[place : place + own_rows, :] = values[s ^ k]
+    left = left_s[...].astype(jnp.bfloat16)
 
     def store(start, size, value):
         for k, ref in enumerate(outs):
@@ -321,17 +330,20 @@
     product_tiles(left, weight_ref, store)
 
 
-def project_out(left, weight, later, slots):
-    rows = left.shape[0] // slots
+def project_out(picked, weight, later):
+    slots = len(picked)
+    own_rows, depth = picked[0].shape
+    rows = own_rows * slots
     columns = weight.shape[1]
     return pl.pallas_call(
-        out_kernel,
+        functools.partial(out_kernel, slots),
         out_shape=tuple([jax.ShapeDtypeStruct((rows, columns), jnp.bfloat16)] * slots),
-        in_specs=[in_vmem, in_vmem, in_place],
+        in_specs=[in_vmem, in_place] + [in_vmem] * slots,
         out_specs=tuple([in_vmem] * slots),
-        compiler_params=params(2),
+        scratch_shapes=[pltpu.VMEM((slots * rows, depth), jnp.float32)],
+        compiler_params=params(3),
         name="project_out",
-    )(left, resident(weight), resident(later))
+    )(resident(weight), resident(later), *picked)
 
 
 def gate_up_kernel(slots, meta_ref, rows_ref, gain_ref, *refs):
@@ -460,14 +472,11 @@
     near, far = pair_sums(joined, "inner")
     shard = attend(meta, cosine, sine, near, far, keys, values, slots)
     (w_out,) = load(w_out, after=shard)
-    attended = combine(exchange(shard, "inner"), [w_out], all_rows)
-    (w_up,) = load(w_up, after=attended)
+    attended = combine(exchange(shard, "inner"), [w_out, w_gate], all_rows)
 
     pieces = [attended[k * own_rows : (k + 1) * own_rows] for k in range(slots)]
     picked = scatter_slots(pieces, "tensor")
-    left = jnp.concatenate([picked[s ^ k] for k in range(slots) for s in range(slots)], axis=0)
-    parts = project_out(left, w_out, w_up, slots)
-    (w_gate,) = load(w_gate, after=parts[0])
+    parts = project_out(picked, w_out, w_up)
     parts = scatter_slots(parts, "tensor")
     joined, updated = gate_up(meta, rows, ffn_gain[None, :], parts, w_gate, w_up, own_rows)
     (w_down,) = load(w_down, after=joined)

time: 96.3 us -> 73.1 us (0.76)
  local copies, waits for them, and re-layouts: 20.2 us -> 1.5 us
  Pallas kernels: 36.5 us -> 26.3 us
  waiting for transfers between devices: 9.65 us -> 15.4 us
    unnamed x20 -> x14, local copies, waits for them, and re-layouts: 19.2 us -> 0.73 us
    pallas_call x6 -> x4, Pallas kernels: 22.6 us -> 12.4 us  [load(): pl.pallas_call(functools.partial(load_kernel, len(weights)), out_shape=tu...]
    ppermute x22, waiting for transfers between devices: 9.65 us -> 15.4 us  [swap_with(): return lax.ppermute(value, axis, [(i, i ^ step) for i in range(count)])]
  transfers between devices with their start and end apart: 22 -> 22, of which waited for: 7 -> 11; matrix products, arithmetic and copies ran while one was open for 2% -> 2% of each run, Pallas kernels for 24% -> 17%
where the time goes in v3:
time: 73.1 us; the launch traced here: 72.8 us
  starting transfers between devices  27.7 us (38%)
  Pallas kernels  26.3 us (36%)
  waiting for transfers between devices  15.4 us (21%)
  other arithmetic  1.66 us (2%)
  local copies, waits for them, and re-layouts  1.5 us (2%)
    ppermute x22, starting transfers between devices, swap_with(): return lax.ppermute(value, axis, [(i, i ^ step) for i in range(count)])  27.7 us
    ppermute x22, waiting for transfers between devices, swap_with(): return lax.ppermute(value, axis, [(i, i ^ step) for i in range(count)])  15.4 us
    pallas_call x4, Pallas kernels, load(): pl.pallas_call(functools.partial(load_kernel, len(weights)), out_shape=tu...  12.4 us
    pallas_call x1, Pallas kernels, gate_up(): pl.pallas_call(functools.partial(gate_up_kernel, slots), out_shape=(jax.S...  6.05 us
    pallas_call x1, Pallas kernels, project_down(): pl.pallas_call(down_kernel, out_shape=jax.ShapeDtypeStruct((rows, weight....  2.48 us
    pallas_call x1, Pallas kernels, attend(): pl.pallas_call(functools.partial(attend_kernel, slots), out_shape=jax.Sha...  2.27 us
    pallas_call x1, Pallas kernels, project_qkv(): pl.pallas_call(qkv_kernel, out_shape=jax.ShapeDtypeStruct((rows.shape[0],...  1.64 us
  transfers between devices with their start and end apart: 22, of which 11 were waited for; matrix products, arithmetic and copies ran while one was open for 2% of the time, Pallas kernels for 17%

profile of v3, /device:TPU:0, one launch (start us, length us, event | category | flops | bytes accessed | tf_op | source)
XLA Modules:
  0.0 72.8 jit_solution(5633432695509516495)
XLA Ops:
  0.0 5.0 %collective-permute-start.2 = (bf16[2,2048]{1,0:T(2,128)(2,1)}, bf16[2,2048]{1,0:T(2,128)(2,1)S(1)}, u32[]{:S(2)}, u32[]{:S(2)}) collective-permute-start(bf16[2,2048]{1,0:T(2,128)(2,1)} %refs_2_.1), channel_id=1, source_target_pairs={{0,12},{4,8},{8,4},{12,0},{1,13},{5,9},{9,5},{13,1},{2,14},{6,10},... | collective-permute-start | bytes 24584 | tf_op jit(solution)/shard_map/ppermute | solution.py:29
  5.0 0.0 collective-permute-start.1
  5.1 0.6 collective-permute-start
  5.6 0.7 %fusion.4 = (f32[2]{0:T(128)S(1)}, s32[2]{0:T(128)S(1)}) fusion(s32[8]{0:T(128)} %param.23, s32[]{:T(128)S(6)} %select_n.31), kind=kLoop, calls=%fused_computation.18 | loop fusion | flops 2 | bytes 28 | tf_op jit(solution)/shard_map/convert_element_type | solution.py:462
  6.3 0.1 pad_add_fusion.meta_ref
  6.4 0.7 broadcast_in_dim.20.gain_ref
  7.1 0.7 copy-done.1
  7.8 2.5 %load.4 = (bf16[2048,1024]{1,0:T(8,128)(2,1)S(1)}, bf16[2048,256]{1,0:T(8,128)(2,1)S(1)}) custom-call(bf16[2048,1024]{1,0:T(8,128)(2,1)} %refs_0_.3, bf16[2048,256]{1,0:T(8,128)(2,1)} %refs_1_.1, bf16[2,2048]{1,0:T(2,128)(2,1)S(1)} %copy-done.1), custom_call_target="tpu_custom_call" | custom-call | bytes 5242880 | tf_op jit(solution)/shard_map/load/pallas_call | solution.py:112
  10.3 0.0 collective-permute-done.2
  10.3 0.0 collective-permute-done.1
  10.3 0.0 collective-permute-done
  10.4 1.6 %project_qkv.1.refs_2_ = bf16[8,1408]{1,0:T(8,128)(2,1)S(1)} custom-call(s32[4]{0:T(128)S(1)} %pad_add_fusion.meta_ref, bf16[8,2048]{1,0:T(8,128)(2,1)S(1)} %pad_maximum_fusion.rows_ref, bf16[1,2048]{1,0:T(2,128)(2,1)S(1)} %broadcast_in_dim.20.gain_ref, bf16[2048,1024]{1,0:T(8,128)(2,1)S(1)} %get-tuple-element.18.wq_ref, ...), custom_call_target="tpu_custom_call" | custom-call | tf_op jit(solution)/shard_map/project_qkv/pallas_call | solution.py:145
  12.1 3.9 %collective-permute-start.5 = (bf16[2,1408]{1,0:T(2,128)(2,1)S(1)}, bf16[2,1408]{1,0:T(2,128)(2,1)S(1)}, u32[]{:S(2)}, u32[]{:S(2)}) collective-permute-start(bf16[2,1408]{1,0:T(2,128)(2,1)S(1)} %get-tuple-element.37), channel_id=1, source_target_pairs={{0,12},{4,8},{8,4},{12,0},{1,13},{5,9},{9,5},{13,1},{2,14},{6,10},... | collective-permute-start | bytes 16904 | tf_op jit(solution)/shard_map/ppermute | solution.py:29
  16.0 0.0 collective-permute-start.4
  16.0 0.6 collective-permute-start.3
  16.6 2.4 %load.5 = (bf16[2,4096,128]{2,1,0:T(8,128)(2,1)S(1)}, bf16[2,4096,128]{2,1,0:T(8,128)(2,1)S(1)}) custom-call(bf16[2,4096,128]{2,1,0:T(8,128)(2,1)} %bitcast.10, bf16[2,4096,128]{2,1,0:T(8,128)(2,1)} %bitcast.11, bf16[8,1408]{1,0:T(8,128)(2,1)S(1)} %project_qkv.1.refs_2_), custom_call_target="tpu_custom_call" | custom-call | bytes 4194304 | tf_op jit(solution)/shard_map/load/pallas_call | solution.py:112
  19.0 0.0 collective-permute-done.5
  19.0 1.5 %collective-permute-done.4 = bf16[2,1408]{1,0:T(2,128)(2,1)S(1)} collective-permute-done((bf16[2,1408]{1,0:T(2,128)(2,1)S(1)}, bf16[2,1408]{1,0:T(2,128)(2,1)S(1)}, u32[]{:S(2)}, u32[]{:S(2)}) %collective-permute-start.4) | collective-permute-done | bytes 5664 | tf_op jit(solution)/shard_map/ppermute | solution.py:29
  20.5 0.0 collective-permute-done.3
  20.5 0.1 collective-permute-start.6
  20.6 1.2 %collective-permute-done.6 = bf16[8,1408]{1,0:T(8,128)(2,1)S(1)} collective-permute-done((bf16[8,1408]{1,0:T(8,128)(2,1)S(1)}, bf16[8,1408]{1,0:T(8,128)(2,1)S(1)}, u32[]{:S(2)}, u32[]{:S(2)}) %collective-permute-start.6) | collective-permute-done | bytes 22560 | tf_op jit(solution)/shard_map/ppermute | solution.py:29
  21.8 1.6 %collective-permute-start.7 = (bf16[8,1408]{1,0:T(8,128)(2,1)S(1)}, bf16[8,1408]{1,0:T(8,128)(2,1)S(1)}, u32[]{:S(2)}, u32[]{:S(2)}) collective-permute-start(bf16[8,1408]{1,0:T(8,128)(2,1)S(1)} %add_convert_fusion.1.near_ref), channel_id=1, source_target_pairs={{0,2},{1,3},{2,0},{3,1},{4,6},{5,7},{6,4},{7,5},{8,10},{9,11},{10,... | collective-permute-start | bytes 67592 | tf_op jit(solution)/shard_map/ppermute | solution.py:29
  23.4 0.1 fusion
  23.5 2.2 %collective-permute-done.7.far_ref = bf16[8,1408]{1,0:T(8,128)(2,1)S(1)} collective-permute-done((bf16[8,1408]{1,0:T(8,128)(2,1)S(1)}, bf16[8,1408]{1,0:T(8,128)(2,1)S(1)}, u32[]{:S(2)}, u32[]{:S(2)}) %collective-permute-start.7) | collective-permute-done | bytes 22560 | tf_op jit(solution)/shard_map/ppermute | solution.py:29
  25.7 2.3 %attend.1.refs_1_.refs_0_ = bf16[64,256]{1,0:T(8,128)(2,1)S(1)} custom-call(s32[4]{0:T(128)S(1)} %pad_add_fusion.meta_ref, f32[8,128]{1,0:T(8,128)S(1)} %bitcast.9, f32[8,128]{1,0:T(8,128)S(1)} %bitcast.8, bf16[8,1408]{1,0:T(8,128)(2,1)S(1)} %add_convert_fusion.1.near_ref, bf16[8,1408]{1,0:T(8,128)(2,1)S(1)} %collective-permute-done.7.far_ref, ...), custom_call_target="tpu_custom_call" | custom-call | tf_op jit(solution)/shard_map/attend/pallas_call | solution.py:259
  27.9 0.2 collective-permute-start.10
  28.1 1.5 %collective-permute-start.9 = (bf16[64,256]{1,0:T(8,128)(2,1)S(1)}, bf16[64,256]{1,0:T(8,128)(2,1)S(1)}, u32[]{:S(2)}, u32[]{:S(2)}) collective-permute-start(bf16[64,256]{1,0:T(8,128)(2,1)S(1)} %attend.1.refs_1_.refs_0_), channel_id=1, source_target_pairs={{0,2},{1,3},{2,0},{3,1},{4,6},{5,7},{6,4},{7,5},{8,10},{9,11},{10,... | collective-permute-start | bytes 98312 | tf_op jit(solution)/shard_map/ppermute | solution.py:29
  29.6 0.3 collective-permute-start.8
  29.9 2.3 %load.6.refs_4_.weight_ref = bf16[1024,2048]{1,0:T(8,128)(2,1)S(1)} custom-call(bf16[1024,2048]{1,0:T(8,128)(2,1)} %refs_0_.4, bf16[64,256]{1,0:T(8,128)(2,1)S(1)} %attend.1.refs_1_.refs_0_), custom_call_target="tpu_custom_call" | custom-call | bytes 4194304 | tf_op jit(solution)/shard_map/load/pallas_call | solution.py:112
  32.2 0.0 slice-start.2
  32.2 0.0 slice-start.3
  32.3 0.0 collective-permute-done.10.refs_3_
  32.3 0.0 collective-permute-done.9.refs_2_
  32.3 0.0 collective-permute-done.8.refs_1_
  32.3 0.0 copy-done
  32.3 0.3 combine.1
  32.6 2.4 %collective-permute-start.13 = (bf16[2,1024]{1,0:T(2,128)(2,1)S(1)}, bf16[2,1024]{1,0:T(2,128)(2,1)S(1)}, u32[]{:S(2)}, u32[]{:S(2)}) collective-permute-start(bf16[2,1024]{1,0:T(2,128)(2,1)S(1)} %get-tuple-element.40), channel_id=1, source_target_pairs={{0,12},{4,8},{8,4},{12,0},{1,13},{5,9},{9,5},{13,1},{2,14},{6,10},... | collective-permute-start | bytes 12296 | tf_op jit(solution)/shard_map/ppermute | solution.py:29
  34.9 0.0 collective-permute-start.12
  34.9 2.1 %collective-permute-start.11 = (bf16[2,1024]{1,0:T(2,128)(2,1)S(1)}, bf16[2,1024]{1,0:T(2,128)(2,1)S(1)}, u32[]{:S(2)}, u32[]{:S(2)}) collective-permute-start(bf16[2,1024]{1,0:T(2,128)(2,1)S(1)} %get-tuple-element.42), channel_id=1, source_target_pairs={{0,4},{4,0},{8,12},{12,8},{1,5},{5,1},{9,13},{13,9},{2,6},{6,2},{1... | collective-permute-start | bytes 12296 | tf_op jit(solution)/shard_map/ppermute | solution.py:29
  37.0 1.0 %collective-permute-done.13.refs_3_ = bf16[2,1024]{1,0:T(2,128)(2,1)S(1)} collective-permute-done((bf16[2,1024]{1,0:T(2,128)(2,1)S(1)}, bf16[2,1024]{1,0:T(2,128)(2,1)S(1)}, u32[]{:S(2)}, u32[]{:S(2)}) %collective-permute-start.13) | collective-permute-done | bytes 4128 | tf_op jit(solution)/shard_map/ppermute | solution.py:29
  38.1 1.4 %collective-permute-done.12.refs_2_ = bf16[2,1024]{1,0:T(2,128)(2,1)S(1)} collective-permute-done((bf16[2,1024]{1,0:T(2,128)(2,1)S(1)}, bf16[2,1024]{1,0:T(2,128)(2,1)S(1)}, u32[]{:S(2)}, u32[]{:S(2)}) %collective-permute-start.12) | collective-permute-done | bytes 4128 | tf_op jit(solution)/shard_map/ppermute | solution.py:29
  39.5 0.0 collective-permute-done.11.refs_1_
  39.5 0.0 copy-start.2
  39.5 1.2 %project_out.1 = (bf16[8,2048]{1,0:T(8,128)(2,1)S(1)}, bf16[8,2048]{1,0:T(8,128)(2,1)S(1)}, bf16[8,2048]{1,0:T(8,128)(2,1)S(1)}, bf16[8,2048]{1,0:T(8,128)(2,1)S(1)}) custom-call(bf16[1024,2048]{1,0:T(8,128)(2,1)S(1)} %load.6.refs_4_.weight_ref, bf16[2048,3584]{1,0:T(8,128)(2,1)S(1)} %bitcast.7, bf16[2,1024]{1,0:T(2,128)(2,1)S(1)} %get-tuple-element.43.refs_0_, ...), custom_call_target="tpu_custom_call" | custom-call | tf_op jit(solution)/shard_map/project_out/pallas_call | solution.py:338
  40.7 1.2 %collective-permute-start.14 = (bf16[8,2048]{1,0:T(8,128)(2,1)S(1)}, bf16[8,2048]{1,0:T(8,128)(2,1)S(1)}, u32[]{:S(2)}, u32[]{:S(2)}) collective-permute-start(bf16[8,2048]{1,0:T(8,128)(2,1)S(1)} %get-tuple-element.26), channel_id=1, source_target_pairs={{0,4},{4,0},{8,12},{12,8},{1,5},{5,1},{9,13},{13,9},{2,6},{6,2},{1... | collective-permute-start | bytes 98312 | tf_op jit(solution)/shard_map/ppermute | solution.py:29
  41.9 1.1 %collective-permute-start.15 = (bf16[8,2048]{1,0:T(8,128)(2,1)S(1)}, bf16[8,2048]{1,0:T(8,128)(2,1)S(1)}, u32[]{:S(2)}, u32[]{:S(2)}) collective-permute-start(bf16[8,2048]{1,0:T(8,128)(2,1)S(1)} %get-tuple-element.27), channel_id=1, source_target_pairs={{0,8},{4,12},{8,0},{12,4},{1,9},{5,13},{9,1},{13,5},{2,10},{6,14},... | collective-permute-start | bytes 98312 | tf_op jit(solution)/shard_map/ppermute | solution.py:29
  43.0 2.1 %collective-permute-start.16 = (bf16[8,2048]{1,0:T(8,128)(2,1)S(1)}, bf16[8,2048]{1,0:T(8,128)(2,1)S(1)}, u32[]{:S(2)}, u32[]{:S(2)}) collective-permute-start(bf16[8,2048]{1,0:T(8,128)(2,1)S(1)} %get-tuple-element.28), channel_id=1, source_target_pairs={{0,12},{4,8},{8,4},{12,0},{1,13},{5,9},{9,5},{13,1},{2,14},{6,10},... | collective-permute-start | bytes 98312 | tf_op jit(solution)/shard_map/ppermute | solution.py:29
  45.1 0.0 collective-permute-done.14.refs_1_
  45.1 1.6 %collective-permute-done.15.refs_2_ = bf16[8,2048]{1,0:T(8,128)(2,1)S(1)} collective-permute-done((bf16[8,2048]{1,0:T(8,128)(2,1)S(1)}, bf16[8,2048]{1,0:T(8,128)(2,1)S(1)}, u32[]{:S(2)}, u32[]{:S(2)}) %collective-permute-start.15) | collective-permute-done | bytes 32800 | tf_op jit(solution)/shard_map/ppermute | solution.py:29
  46.8 2.0 %collective-permute-done.16.refs_3_ = bf16[8,2048]{1,0:T(8,128)(2,1)S(1)} collective-permute-done((bf16[8,2048]{1,0:T(8,128)(2,1)S(1)}, bf16[8,2048]{1,0:T(8,128)(2,1)S(1)}, u32[]{:S(2)}, u32[]{:S(2)}) %collective-permute-start.16) | collective-permute-done | bytes 32800 | tf_op jit(solution)/shard_map/ppermute | solution.py:29
  48.7 6.0 %gate_up.1 = (bf16[8,7296]{1,0:T(8,128)(2,1)S(1)}, f32[2,2048]{1,0:T(2,128)S(1)}) custom-call(s32[4]{0:T(128)S(1)} %pad_add_fusion.meta_ref, bf16[8,2048]{1,0:T(8,128)(2,1)S(1)} %pad_maximum_fusion.rows_ref, bf16[1,2048]{1,0:T(2,128)(2,1)S(1)} %broadcast_in_dim.17.gain_ref, bf16[8,2048]{1,0:T(8,128)(2,1)S(1)} %get-tuple-element.25.refs_0_, ...), custom_call_target="tpu_custom_call" | custom-call | tf_op jit(solution)/shard_map/gate_up/pallas_call | solution.py:378
  54.8 0.0 collective-permute-start.17
  54.8 1.3 %collective-permute-done.17 = bf16[8,7296]{1,0:T(8,128)(2,1)S(1)} collective-permute-done((bf16[8,7296]{1,0:T(8,128)(2,1)S(1)}, bf16[8,7296]{1,0:T(8,128)(2,1)S(1)}, u32[]{:S(2)}, u32[]{:S(2)}) %collective-permute-start.17) | collective-permute-done | bytes 116768 | tf_op jit(solution)/shard_map/ppermute | solution.py:29
  56.2 1.6 %collective-permute-start.18 = (bf16[8,7296]{1,0:T(8,128)(2,1)S(1)}, bf16[8,7296]{1,0:T(8,128)(2,1)S(1)}, u32[]{:S(2)}, u32[]{:S(2)}) collective-permute-start(bf16[8,7296]{1,0:T(8,128)(2,1)S(1)} %add_convert_fusion.near_ref), channel_id=1, source_target_pairs={{0,2},{1,3},{2,0},{3,1},{4,6},{5,7},{6,4},{7,5},{8,10},{9,11},{10,... | collective-permute-start | bytes 350216 | tf_op jit(solution)/shard_map/ppermute | solution.py:29
  57.7 5.2 %load.7.weight_ref = bf16[3584,2048]{1,0:T(8,128)(2,1)S(1)} custom-call(bf16[3584,2048]{1,0:T(8,128)(2,1)} %refs_0_.5, bf16[8,7296]{1,0:T(8,128)(2,1)S(1)} %get-tuple-element.30.refs_1_), custom_call_target="tpu_custom_call" | custom-call | bytes 14680064 | tf_op jit(solution)/shard_map/load/pallas_call | solution.py:112
  62.9 0.0 collective-permute-done.18.far_ref
  62.9 2.5 %project_down.1 = bf16[8,2048]{1,0:T(8,128)(2,1)S(1)} custom-call(bf16[8,7296]{1,0:T(8,128)(2,1)S(1)} %add_convert_fusion.near_ref, bf16[8,7296]{1,0:T(8,128)(2,1)S(1)} %collective-permute-done.18.far_ref, bf16[3584,2048]{1,0:T(8,128)(2,1)S(1)} %load.7.weight_ref), custom_call_target="tpu_custom_call" | custom-call | tf_op jit(solution)/shard_map/project_down/pallas_call | solution.py:415
  65.4 0.1 collective-permute-start.19
  65.5 2.1 %collective-permute-start.21 = (bf16[2,2048]{1,0:T(2,128)(2,1)S(1)}, bf16[2,2048]{1,0:T(2,128)(2,1)S(1)}, u32[]{:S(2)}, u32[]{:S(2)}) collective-permute-start(bf16[2,2048]{1,0:T(2,128)(2,1)S(1)} %get-tuple-element.34), channel_id=1, source_target_pairs={{0,12},{4,8},{8,4},{12,0},{1,13},{5,9},{9,5},{13,1},{2,14},{6,10},... | collective-permute-start | bytes 24584 | tf_op jit(solution)/shard_map/ppermute | solution.py:29
  67.7 1.3 %collective-permute-start.20 = (bf16[2,2048]{1,0:T(2,128)(2,1)S(1)}, bf16[2,2048]{1,0:T(2,128)(2,1)S(1)}, u32[]{:S(2)}, u32[]{:S(2)}) collective-permute-start(bf16[2,2048]{1,0:T(2,128)(2,1)S(1)} %get-tuple-element.35), channel_id=1, source_target_pairs={{0,8},{4,12},{8,0},{12,4},{1,9},{5,13},{9,1},{13,5},{2,10},{6,14},... | collective-permute-start | bytes 24584 | tf_op jit(solution)/shard_map/ppermute | solution.py:29
  69.0 0.2 collective-permute-done.19
  69.2 2.0 %collective-permute-done.21 = bf16[2,2048]{1,0:T(2,128)(2,1)S(1)} collective-permute-done((bf16[2,2048]{1,0:T(2,128)(2,1)S(1)}, bf16[2,2048]{1,0:T(2,128)(2,1)S(1)}, u32[]{:S(2)}, u32[]{:S(2)}) %collective-permute-start.21) | collective-permute-done | bytes 8224 | tf_op jit(solution)/shard_map/ppermute | solution.py:29
  71.1 1.1 %collective-permute-done.20 = bf16[2,2048]{1,0:T(2,128)(2,1)S(1)} collective-permute-done((bf16[2,2048]{1,0:T(2,128)(2,1)S(1)}, bf16[2,2048]{1,0:T(2,128)(2,1)S(1)}, u32[]{:S(2)}, u32[]{:S(2)}) %collective-permute-start.20) | collective-permute-done | bytes 8224 | tf_op jit(solution)/shard_map/ppermute | solution.py:29
  72.2 0.6 add_convert_fusion.2
  (21 shorter events, 0.2 us)
Async XLA Ops:
  0.0 10.3 %collective-permute-start.2 = (bf16[2,2048]{1,0:T(2,128)(2,1)}, bf16[2,2048]{1,0:T(2,128)(2,1)S(1)}, u32[]{:S(2)}, u32[]{:S(2)}) collective-permute-start(bf16[2,2048]{1,0:T(2,128)(2,1)} %refs_2_.1), channel_id=1, source_target_pairs={{0,12},{4,8},{8,4},{12,0},{1,13},{5,9},{9,5},{13,1},{2,14},{6,10},... | collective-permute-start | bytes 24584 | tf_op jit(solution)/shard_map/ppermute | solution.py:29
  5.0 5.3 %collective-permute-start.1 = (bf16[2,2048]{1,0:T(2,128)(2,1)}, bf16[2,2048]{1,0:T(2,128)(2,1)S(1)}, u32[]{:S(2)}, u32[]{:S(2)}) collective-permute-start(bf16[2,2048]{1,0:T(2,128)(2,1)} %refs_2_.1), channel_id=1, source_target_pairs={{0,8},{4,12},{8,0},{12,4},{1,9},{5,13},{9,1},{13,5},{2,10},{6,14},... | collective-permute-start | bytes 24584 | tf_op jit(solution)/shard_map/ppermute | solution.py:29
  5.1 5.3 %collective-permute-start = (bf16[2,2048]{1,0:T(2,128)(2,1)}, bf16[2,2048]{1,0:T(2,128)(2,1)S(1)}, u32[]{:S(2)}, u32[]{:S(2)}) collective-permute-start(bf16[2,2048]{1,0:T(2,128)(2,1)} %refs_2_.1), channel_id=1, source_target_pairs={{0,4},{4,0},{8,12},{12,8},{1,5},{5,1},{9,13},{13,9},{2,6},{6,2},{1... | collective-permute-start | bytes 24584 | tf_op jit(solution)/shard_map/ppermute | solution.py:29
  7.1 0.7 copy-start.1
  12.1 6.9 %collective-permute-start.5 = (bf16[2,1408]{1,0:T(2,128)(2,1)S(1)}, bf16[2,1408]{1,0:T(2,128)(2,1)S(1)}, u32[]{:S(2)}, u32[]{:S(2)}) collective-permute-start(bf16[2,1408]{1,0:T(2,128)(2,1)S(1)} %get-tuple-element.37), channel_id=1, source_target_pairs={{0,12},{4,8},{8,4},{12,0},{1,13},{5,9},{9,5},{13,1},{2,14},{6,10},... | collective-permute-start | bytes 16904 | tf_op jit(solution)/shard_map/ppermute | solution.py:29
  16.0 4.5 %collective-permute-start.4 = (bf16[2,1408]{1,0:T(2,128)(2,1)S(1)}, bf16[2,1408]{1,0:T(2,128)(2,1)S(1)}, u32[]{:S(2)}, u32[]{:S(2)}) collective-permute-start(bf16[2,1408]{1,0:T(2,128)(2,1)S(1)} %get-tuple-element.38), channel_id=1, source_target_pairs={{0,8},{4,12},{8,0},{12,4},{1,9},{5,13},{9,1},{13,5},{2,10},{6,14},... | collective-permute-start | bytes 16904 | tf_op jit(solution)/shard_map/ppermute | solution.py:29
  16.0 4.5 %collective-permute-start.3 = (bf16[2,1408]{1,0:T(2,128)(2,1)S(1)}, bf16[2,1408]{1,0:T(2,128)(2,1)S(1)}, u32[]{:S(2)}, u32[]{:S(2)}) collective-permute-start(bf16[2,1408]{1,0:T(2,128)(2,1)S(1)} %get-tuple-element.39), channel_id=1, source_target_pairs={{0,4},{4,0},{8,12},{12,8},{1,5},{5,1},{9,13},{13,9},{2,6},{6,2},{1... | collective-permute-start | bytes 16904 | tf_op jit(solution)/shard_map/ppermute | solution.py:29
  16.6 15.7 %copy-start = (bf16[2048,3584]{1,0:T(8,128)(2,1)S(1)}, bf16[2048,3584]{1,0:T(8,128)(2,1)}, u32[]{:S(2)}) copy-start(bf16[2048,3584]{1,0:T(8,128)(2,1)} %refs_4_.1) | copy-start | bytes 44040196
  20.5 1.3 %collective-permute-start.6 = (bf16[8,1408]{1,0:T(8,128)(2,1)S(1)}, bf16[8,1408]{1,0:T(8,128)(2,1)S(1)}, u32[]{:S(2)}, u32[]{:S(2)}) collective-permute-start(bf16[8,1408]{1,0:T(8,128)(2,1)S(1)} %pad_maximum_fusion.1), channel_id=1, source_target_pairs={{0,1},{1,0},{2,3},{3,2},{4,5},{5,4},{6,7},{7,6},{8,9},{9,8},{10,11... | collective-permute-start | bytes 67592 | tf_op jit(solution)/shard_map/ppermute | solution.py:29
  21.8 3.9 %collective-permute-start.7 = (bf16[8,1408]{1,0:T(8,128)(2,1)S(1)}, bf16[8,1408]{1,0:T(8,128)(2,1)S(1)}, u32[]{:S(2)}, u32[]{:S(2)}) collective-permute-start(bf16[8,1408]{1,0:T(8,128)(2,1)S(1)} %add_convert_fusion.1.near_ref), channel_id=1, source_target_pairs={{0,2},{1,3},{2,0},{3,1},{4,6},{5,7},{6,4},{7,5},{8,10},{9,11},{10,... | collective-permute-start | bytes 67592 | tf_op jit(solution)/shard_map/ppermute | solution.py:29
  27.9 4.3 %collective-permute-start.10 = (bf16[64,256]{1,0:T(8,128)(2,1)S(1)}, bf16[64,256]{1,0:T(8,128)(2,1)S(1)}, u32[]{:S(2)}, u32[]{:S(2)}) collective-permute-start(bf16[64,256]{1,0:T(8,128)(2,1)S(1)} %attend.1.refs_1_.refs_0_), channel_id=1, source_target_pairs={{0,3},{1,2},{2,1},{3,0},{4,7},{5,6},{6,5},{7,4},{8,11},{9,10},{10,... | collective-permute-start | bytes 98312 | tf_op jit(solution)/shard_map/ppermute | solution.py:29
  28.1 4.1 %collective-permute-start.9 = (bf16[64,256]{1,0:T(8,128)(2,1)S(1)}, bf16[64,256]{1,0:T(8,128)(2,1)S(1)}, u32[]{:S(2)}, u32[]{:S(2)}) collective-permute-start(bf16[64,256]{1,0:T(8,128)(2,1)S(1)} %attend.1.refs_1_.refs_0_), channel_id=1, source_target_pairs={{0,2},{1,3},{2,0},{3,1},{4,6},{5,7},{6,4},{7,5},{8,10},{9,11},{10,... | collective-permute-start | bytes 98312 | tf_op jit(solution)/shard_map/ppermute | solution.py:29
  29.6 2.7 %collective-permute-start.8 = (bf16[64,256]{1,0:T(8,128)(2,1)S(1)}, bf16[64,256]{1,0:T(8,128)(2,1)S(1)}, u32[]{:S(2)}, u32[]{:S(2)}) collective-permute-start(bf16[64,256]{1,0:T(8,128)(2,1)S(1)} %attend.1.refs_1_.refs_0_), channel_id=1, source_target_pairs={{0,1},{1,0},{2,3},{3,2},{4,5},{5,4},{6,7},{7,6},{8,9},{9,8},{10,11... | collective-permute-start | bytes 98312 | tf_op jit(solution)/shard_map/ppermute | solution.py:29
  29.9 9.6 %slice-start = ((s8[14680064]{0:T(1024)(128)(4,1)}), s8[4194304]{0:T(1024)(128)(4,1)S(1)}, s32[]{:S(2)}) async-start(s8[14680064]{0:T(1024)(128)(4,1)} %bitcast.6), calls=%async_computation | async-start | bytes 8388608
  29.9 9.6 %slice-start.1 = ((s8[14680064]{0:T(1024)(128)(4,1)}), s8[4194304]{0:T(1024)(128)(4,1)S(1)}, s32[]{:S(2)}) async-start(s8[14680064]{0:T(1024)(128)(4,1)} %bitcast.6), calls=%async_computation.1 | async-start | bytes 8388608
  32.2 7.2 %slice-start.2 = ((s8[14680064]{0:T(1024)(128)(4,1)}), s8[4194304]{0:T(1024)(128)(4,1)S(1)}, s32[]{:S(2)}) async-start(s8[14680064]{0:T(1024)(128)(4,1)} %bitcast.6), calls=%async_computation.2 | async-start | bytes 8388608
  32.2 7.2 %slice-start.3 = ((s8[14680064]{0:T(1024)(128)(4,1)}), s8[2097152]{0:T(1024)(128)(4,1)S(1)}, s32[]{:S(2)}) async-start(s8[14680064]{0:T(1024)(128)(4,1)} %bitcast.6), calls=%async_computation.3 | async-start | bytes 4194304
  32.6 5.5 %collective-permute-start.13 = (bf16[2,1024]{1,0:T(2,128)(2,1)S(1)}, bf16[2,1024]{1,0:T(2,128)(2,1)S(1)}, u32[]{:S(2)}, u32[]{:S(2)}) collective-permute-start(bf16[2,1024]{1,0:T(2,128)(2,1)S(1)} %get-tuple-element.40), channel_id=1, source_target_pairs={{0,12},{4,8},{8,4},{12,0},{1,13},{5,9},{9,5},{13,1},{2,14},{6,10},... | collective-permute-start | bytes 12296 | tf_op jit(solution)/shard_map/ppermute | solution.py:29
  34.9 4.5 %collective-permute-start.12 = (bf16[2,1024]{1,0:T(2,128)(2,1)S(1)}, bf16[2,1024]{1,0:T(2,128)(2,1)S(1)}, u32[]{:S(2)}, u32[]{:S(2)}) collective-permute-start(bf16[2,1024]{1,0:T(2,128)(2,1)S(1)} %get-tuple-element.41), channel_id=1, source_target_pairs={{0,8},{4,12},{8,0},{12,4},{1,9},{5,13},{9,1},{13,5},{2,10},{6,14},... | collective-permute-start | bytes 12296 | tf_op jit(solution)/shard_map/ppermute | solution.py:29
  34.9 4.5 %collective-permute-start.11 = (bf16[2,1024]{1,0:T(2,128)(2,1)S(1)}, bf16[2,1024]{1,0:T(2,128)(2,1)S(1)}, u32[]{:S(2)}, u32[]{:S(2)}) collective-permute-start(bf16[2,1024]{1,0:T(2,128)(2,1)S(1)} %get-tuple-element.42), channel_id=1, source_target_pairs={{0,4},{4,0},{8,12},{12,8},{1,5},{5,1},{9,13},{13,9},{2,6},{6,2},{1... | collective-permute-start | bytes 12296 | tf_op jit(solution)/shard_map/ppermute | solution.py:29
  39.5 5.6 %copy-start.2 = (bf16[2048]{0:T(1024)(128)(2,1)S(1)}, bf16[2048]{0:T(1024)(128)(2,1)}, u32[]{:S(2)}) copy-start(bf16[2048]{0:T(1024)(128)(2,1)} %param.14) | copy-start | bytes 12292
  40.7 4.4 %collective-permute-start.14 = (bf16[8,2048]{1,0:T(8,128)(2,1)S(1)}, bf16[8,2048]{1,0:T(8,128)(2,1)S(1)}, u32[]{:S(2)}, u32[]{:S(2)}) collective-permute-start(bf16[8,2048]{1,0:T(8,128)(2,1)S(1)} %get-tuple-element.26), channel_id=1, source_target_pairs={{0,4},{4,0},{8,12},{12,8},{1,5},{5,1},{9,13},{13,9},{2,6},{6,2},{1... | collective-permute-start | bytes 98312 | tf_op jit(solution)/shard_map/ppermute | solution.py:29
  41.9 4.9 %collective-permute-start.15 = (bf16[8,2048]{1,0:T(8,128)(2,1)S(1)}, bf16[8,2048]{1,0:T(8,128)(2,1)S(1)}, u32[]{:S(2)}, u32[]{:S(2)}) collective-permute-start(bf16[8,2048]{1,0:T(8,128)(2,1)S(1)} %get-tuple-element.27), channel_id=1, source_target_pairs={{0,8},{4,12},{8,0},{12,4},{1,9},{5,13},{9,1},{13,5},{2,10},{6,14},... | collective-permute-start | bytes 98312 | tf_op jit(solution)/shard_map/ppermute | solution.py:29
  43.0 5.7 %collective-permute-start.16 = (bf16[8,2048]{1,0:T(8,128)(2,1)S(1)}, bf16[8,2048]{1,0:T(8,128)(2,1)S(1)}, u32[]{:S(2)}, u32[]{:S(2)}) collective-permute-start(bf16[8,2048]{1,0:T(8,128)(2,1)S(1)} %get-tuple-element.28), channel_id=1, source_target_pairs={{0,12},{4,8},{8,4},{12,0},{1,13},{5,9},{9,5},{13,1},{2,14},{6,10},... | collective-permute-start | bytes 98312 | tf_op jit(solution)/shard_map/ppermute | solution.py:29
  54.8 1.3 %collective-permute-start.17 = (bf16[8,7296]{1,0:T(8,128)(2,1)S(1)}, bf16[8,7296]{1,0:T(8,128)(2,1)S(1)}, u32[]{:S(2)}, u32[]{:S(2)}) collective-permute-start(bf16[8,7296]{1,0:T(8,128)(2,1)S(1)} %get-tuple-element.30.refs_1_), channel_id=1, source_target_pairs={{0,1},{1,0},{2,3},{3,2},{4,5},{5,4},{6,7},{7,6},{8,9},{9,8},{10,11... | collective-permute-start | bytes 350216 | tf_op jit(solution)/shard_map/ppermute | solution.py:29
  56.2 6.7 %collective-permute-start.18 = (bf16[8,7296]{1,0:T(8,128)(2,1)S(1)}, bf16[8,7296]{1,0:T(8,128)(2,1)S(1)}, u32[]{:S(2)}, u32[]{:S(2)}) collective-permute-start(bf16[8,7296]{1,0:T(8,128)(2,1)S(1)} %add_convert_fusion.near_ref), channel_id=1, source_target_pairs={{0,2},{1,3},{2,0},{3,1},{4,6},{5,7},{6,4},{7,5},{8,10},{9,11},{10,... | collective-permute-start | bytes 350216 | tf_op jit(solution)/shard_map/ppermute | solution.py:29
  65.4 3.7 %collective-permute-start.19 = (bf16[2,2048]{1,0:T(2,128)(2,1)S(1)}, bf16[2,2048]{1,0:T(2,128)(2,1)S(1)}, u32[]{:S(2)}, u32[]{:S(2)}) collective-permute-start(bf16[2,2048]{1,0:T(2,128)(2,1)S(1)} %get-tuple-element.33), channel_id=1, source_target_pairs={{0,4},{4,0},{8,12},{12,8},{1,5},{5,1},{9,13},{13,9},{2,6},{6,2},{1... | collective-permute-start | bytes 24584 | tf_op jit(solution)/shard_map/ppermute | solution.py:29
  65.5 5.6 %collective-permute-start.21 = (bf16[2,2048]{1,0:T(2,128)(2,1)S(1)}, bf16[2,2048]{1,0:T(2,128)(2,1)S(1)}, u32[]{:S(2)}, u32[]{:S(2)}) collective-permute-start(bf16[2,2048]{1,0:T(2,128)(2,1)S(1)} %get-tuple-element.34), channel_id=1, source_target_pairs={{0,12},{4,8},{8,4},{12,0},{1,13},{5,9},{9,5},{13,1},{2,14},{6,10},... | collective-permute-start | bytes 24584 | tf_op jit(solution)/shard_map/ppermute | solution.py:29
  67.7 4.5 %collective-permute-start.20 = (bf16[2,2048]{1,0:T(2,128)(2,1)S(1)}, bf16[2,2048]{1,0:T(2,128)(2,1)S(1)}, u32[]{:S(2)}, u32[]{:S(2)}) collective-permute-start(bf16[2,2048]{1,0:T(2,128)(2,1)S(1)} %get-tuple-element.35), channel_id=1, source_target_pairs={{0,8},{4,12},{8,0},{12,4},{1,9},{5,13},{9,1},{13,5},{2,10},{6,14},... | collective-permute-start | bytes 24584 | tf_op jit(solution)/shard_map/ppermute | solution.py:29

commit v4 on v2

v4 whole, which is shorter than its diff:
```python
import functools
import math

import jax
import jax.numpy as jnp
from jax import lax
from jax.experimental import pallas as pl
from jax.experimental.pallas import tpu as pltpu
from jax.sharding import PartitionSpec as P

D = 8192
HEADS = 32
KV_HEADS = 4
HEAD_DIM = 128
GROUP = HEADS // KV_HEADS
LANES = 128
MIB = 2**20
COPIES = 4

epsilon = 1e-05
rope_base = 500000.0

in_vmem = pl.BlockSpec(memory_space=pltpu.VMEM)
in_smem = pl.BlockSpec(memory_space=pltpu.SMEM)
in_place = pl.BlockSpec(memory_space=pl.ANY)


def swap_with(value, axis, step):
    count = lax.axis_size(axis)
    return lax.ppermute(value, axis, [(i, i ^ step) for i in range(count)])


def exchange(value, axis):
    count = lax.axis_size(axis)
    got = {k: swap_with(value, axis, k) for k in reversed(range(1, count))}
    return [value] + [got[k] for k in range(1, count)]


def steps_up(count):
    return [1 << n for n in range(count.bit_length() - 1)]


def gather_rows(value, axis, beside):
    for step in steps_up(lax.axis_size(axis)):
        other = swap_with(value, axis, step)
        value = beside(step, value)
        value = jnp.concatenate([value, other], axis=0)
    return value


def scatter_rows(near, far, axis, beside):
    count = lax.axis_size(axis)
    rows = (near.shape[0] + far.shape[0]) // count
    cut = lambda array, n: array[n * rows : (n + 1) * rows]
    half = count // 2
    held = [[cut(near, n)] for n in range(half)] + [[cut(far, n)] for n in range(half)]
    order = [0]
    step = half
    while step:
        if step == half:
            sent = far
        else:
            sent = jnp.concatenate([p for n in range(step, 2 * step) for p in held[n]], axis=0)
        got = swap_with(sent, axis, step)
        got = beside(step, got)
        each = len(held[0])
        for n in range(step):
            held[n] = held[n] + [cut(got, n * each + m) for m in range(each)]
        held = held[:step]
        order = order + [n ^ step for n in order]
        step //= 2
    return [held[0][order.index(n)] for n in range(count)]


def params(mib):
    return pltpu.CompilerParams(vmem_limit_bytes=mib * MIB)


def resident(weight):
    return pltpu.with_memory_space_constraint(weight, pltpu.VMEM)


def tile_of(columns):
    for tile in (1792, 1024, 896, 512, 256, 128):
        if columns % tile == 0:
            return tile
    return columns


def product_tiles(left, weight_ref, store):
    columns = weight_ref.shape[1]
    tile = tile_of(columns)

    @pl.loop(0, columns // tile)
    def _(step):
        start = pl.multiple_of(step * tile, tile)
        store(
            start,
            tile,
            jnp.dot(left, weight_ref[:, pl.ds(start, tile)], preferred_element_type=jnp.float32),
        )


def three_parts(value):
    high = value.astype(jnp.bfloat16).astype(jnp.float32)
    rest = value - high
    middle = rest.astype(jnp.bfloat16).astype(jnp.float32)
    return high, middle, rest - middle


def spread(parts, lanes, first):
    out = 0.0
    for n, part in enumerate(parts):
        out = out + jnp.where(lanes == first + n, part, 0.0)
    return out


def squares_block(total):
    lanes = lax.broadcasted_iota(jnp.int32, (total.shape[0], LANES), 1)
    return spread(three_parts(total), lanes, lax.axis_index("inner") * 4)


def load_kernel(spans, *refs):
    count = len(spans)
    outs = refs[count + 1 : 2 * count + 1]
    sems = refs[-1]
    copies = []
    for n, (start, size) in enumerate(spans):
        cuts = COPIES if len(refs[n].shape) > 1 and size % (16 * COPIES) == 0 else 1
        each = size // cuts
        for m in range(cuts):
            copies.append(
                pltpu.make_async_copy(
                    refs[n].at[pl.ds(start + m * each, each)],
                    outs[n].at[pl.ds(m * each, each)],
                    sems.at[n, m],
                )
            )
    for copy in copies:
        copy.start()
    for copy in copies:
        copy.wait()


def load(*arrays, after, spans=None):
    spans = spans or [(0, a.shape[0]) for a in arrays]
    shapes = [(size,) + a.shape[1:] for a, (_, size) in zip(arrays, spans)]
    return pl.pallas_call(
        functools.partial(load_kernel, spans),
        out_shape=tuple(pltpu.VMEM(shape, a.dtype) for shape, a in zip(shapes, arrays)),
        in_specs=[in_place] * (len(arrays) + 1),
        out_specs=tuple(in_vmem for _ in arrays),
        cost_estimate=pl.CostEstimate(
            flops=0, bytes_accessed=2 * sum(math.prod(shape) for shape in shapes), transcendentals=0
        ),
        scratch_shapes=[pltpu.SemaphoreType.DMA((len(arrays), COPIES))],
        compiler_params=params(1),
        name="load",
    )(*[pltpu.with_memory_space_constraint(a, pltpu.HBM) for a in arrays], after)


def qkv_kernel(rows_ref, gain_ref, wq_ref, wkv_ref, near_ref, far_ref, out_s):
    wide = rows_ref[...].astype(jnp.float32)
    total = jnp.sum(wide * wide, axis=1, keepdims=True)
    gain = gain_ref[...].astype(jnp.float32)[None, :]
    scaled = (wide * gain).astype(jnp.bfloat16)
    query_cols = wq_ref.shape[1]
    kv_cols = wkv_ref.shape[1]

    def store_query(start, size, value):
        out_s[:, pl.ds(start, size)] = value

    product_tiles(scaled, wq_ref, store_query)
    out_s[:, query_cols : query_cols + kv_cols] = jnp.dot(
        scaled, wkv_ref[...], preferred_element_type=jnp.float32
    )
    out_s[:, query_cols + kv_cols :] = squares_block(total)
    half = near_ref.shape[0]
    near_ref[...] = out_s[:half, :].astype(jnp.bfloat16)
    far_ref[...] = out_s[half:, :].astype(jnp.bfloat16)


def project_qkv(rows, gain, w_query, w_kv):
    count = rows.shape[0]
    columns = w_query.shape[1] + w_kv.shape[1] + LANES
    return pl.pallas_call(
        qkv_kernel,
        out_shape=(jax.ShapeDtypeStruct((count // 2, columns), jnp.bfloat16),) * 2,
        in_specs=[in_vmem] * 4,
        out_specs=(in_vmem,) * 2,
        scratch_shapes=[pltpu.VMEM((count, columns), jnp.float32)],
        compiler_params=params(2),
        name="project_qkv",
    )(rows, gain, resident(w_query), resident(w_kv))


def attend_kernel(
    slots,
    shards,
    lengths_ref,
    cosine_ref,
    sine_ref,
    key_ref,
    value_ref,
    *refs,
):
    parts = refs[:shards]
    out_ref, query_s, kv_s, kv_wide_s, mixed_s, stats_s = refs[shards:]
    all_rows = parts[0].shape[0]
    own_rows = all_rows // slots
    here = HEADS // slots
    query_cols = here * HEAD_DIM
    kv_cols = 2 * KV_HEADS * HEAD_DIM // slots
    columns = query_cols + kv_cols
    tensor_index = lax.axis_index("tensor")
    inner_index = lax.axis_index("inner")
    positions = key_ref.shape[1] // KV_HEADS

    joined = functools.reduce(jnp.add, [ref[...].astype(jnp.float32) for ref in parts])
    squares = jnp.sum(joined[:, columns:], axis=1, keepdims=True)
    joined = joined[:, :columns] * lax.rsqrt(squares / D + epsilon)
    cosine = cosine_ref[...]
    sine = sine_ref[...]

    def rotate(block):
        count = block.shape[0]
        even = lax.broadcasted_iota(jnp.int32, block.shape, 1) % 2 == 0
        other = jnp.where(
            even, pltpu.roll(block, HEAD_DIM - 1, axis=1), pltpu.roll(block, 1, axis=1)
        )
        return block * cosine[:count] + other * sine[:count]

    for j in range(here):
        block = rotate(joined[:, j * HEAD_DIM : (j + 1) * HEAD_DIM])
        query_s[j * all_rows : (j + 1) * all_rows, :] = block
    for s in range(slots):
        kv_s[s] = joined[s * own_rows : (s + 1) * own_rows, query_cols:]
    for d in range(slots):
        kv_wide_s[:, d * kv_cols : (d + 1) * kv_cols] = kv_s[d ^ tensor_index]
    new_keys = []
    new_values = []
    for g in range(KV_HEADS):
        block = kv_wide_s[:, g * HEAD_DIM : (g + 1) * HEAD_DIM]
        new_keys.append(rotate(block).astype(jnp.bfloat16).astype(jnp.float32))
        block = kv_wide_s[:, (KV_HEADS + g) * HEAD_DIM : (KV_HEADS + g + 1) * HEAD_DIM]
        new_values.append(block.astype(jnp.bfloat16).astype(jnp.float32))

    score_scale = HEAD_DIM ** (-0.5)
    row = lax.broadcasted_iota(jnp.int32, (HEADS, 1), 0)
    head = ((row % slots) ^ tensor_index) * here + row // slots
    kv_head = head // GROUP
    column = lax.broadcasted_iota(jnp.int32, (1, positions * KV_HEADS), 1)
    place = column // KV_HEADS + inner_index * positions
    column_head = column % KV_HEADS
    lanes = lax.broadcasted_iota(jnp.int32, (HEADS, LANES), 1)
    for r in range(own_rows):
        queries = query_s[pl.ds(r, HEADS, stride=own_rows), :].astype(jnp.bfloat16)
        scores = (
            lax.dot_general(
                queries,
                key_ref[r],
                (((1,), (1,)), ((), ())),
                preferred_element_type=jnp.float32,
            )
            * score_scale
        )
        used = jnp.where(place < lengths_ref[r : r + 1, 0:1], column_head, -1)
        masked = jnp.where(used == kv_head, scores, -1e30)
        key_rows = 0.0
        value_rows = 0.0
        for g in range(KV_HEADS):
            key_rows = key_rows + jnp.where(kv_head == g, new_keys[g][r : r + 1], 0.0)
            value_rows = value_rows + jnp.where(kv_head == g, new_values[g][r : r + 1], 0.0)
        new_score = (
            jnp.sum(queries.astype(jnp.float32) * key_rows, axis=1, keepdims=True) * score_scale
        )
        new_score = jnp.where(inner_index == 0, new_score, -1e30)
        peak = jnp.maximum(jnp.max(masked, axis=1, keepdims=True), new_score)
        weights = jnp.exp(masked - peak)
        new_weight = jnp.exp(new_score - peak)
        totals = jnp.sum(weights, axis=1, keepdims=True) + new_weight
        mixture = jnp.dot(
            weights.astype(jnp.bfloat16), value_ref[r], preferred_element_type=jnp.float32
        )
        mixture = mixture + new_weight.astype(jnp.bfloat16).astype(jnp.float32) * value_rows
        mixed_s[pl.ds(r, HEADS, stride=own_rows), :] = mixture
        stats_s[pl.ds(r, HEADS, stride=own_rows), :] = spread(
            three_parts(peak), lanes, 0
        ) + spread(three_parts(totals), lanes, 4)
    out_ref[:, :HEAD_DIM] = mixed_s[...].astype(jnp.bfloat16)
    out_ref[:, HEAD_DIM:] = stats_s[...].astype(jnp.bfloat16)


def attend(lengths, cosine, sine, parts, keys, values, slots):
    own_rows = parts[0].shape[0] // slots
    kv_cols = 2 * KV_HEADS * HEAD_DIM // slots
    return pl.pallas_call(
        functools.partial(attend_kernel, slots, len(parts)),
        out_shape=jax.ShapeDtypeStruct((own_rows * HEADS, HEAD_DIM + LANES), jnp.bfloat16),
        in_specs=[in_vmem] * (5 + len(parts)),
        out_specs=in_vmem,
        scratch_shapes=[
            pltpu.VMEM((own_rows * HEADS, HEAD_DIM), jnp.float32),
            pltpu.VMEM((slots, own_rows, kv_cols), jnp.float32),
            pltpu.VMEM((own_rows, slots * kv_cols), jnp.float32),
            pltpu.VMEM((own_rows * HEADS, HEAD_DIM), jnp.float32),
            pltpu.VMEM((own_rows * HEADS, LANES), jnp.float32),
        ],
        compiler_params=params(6),
        name="attend",
    )(lengths, cosine, sine, resident(keys), resident(values), *parts)


def combine_kernel(shards, all_rows, *refs):
    ins = refs[:shards]
    near_ref, far_ref = refs[-2:]
    half = all_rows // 2
    peaks = []
    totals = []
    for ref in ins:
        stats = ref[:, HEAD_DIM:].astype(jnp.float32)
        peaks.append(stats[:, 0:1] + stats[:, 1:2] + stats[:, 2:3])
        totals.append(stats[:, 4:5] + stats[:, 5:6] + stats[:, 6:7])
    top = functools.reduce(jnp.maximum, peaks)
    mixed = 0.0
    denominator = 0.0
    for ref, peak, total in zip(ins, peaks, totals):
        factor = jnp.exp(peak - top)
        mixed = mixed + factor * ref[:, :HEAD_DIM].astype(jnp.float32)
        denominator = denominator + factor * total
    attended = mixed / denominator
    for j in range(attended.shape[0] // all_rows):
        block = attended[j * all_rows : (j + 1) * all_rows]
        near_ref[:, j * HEAD_DIM : (j + 1) * HEAD_DIM] = block[:half].astype(jnp.bfloat16)
        far_ref[:, j * HEAD_DIM : (j + 1) * HEAD_DIM] = block[half:].astype(jnp.bfloat16)


def combine(parts, later, all_rows):
    count = len(parts)
    columns = parts[0].shape[0] // all_rows * HEAD_DIM
    return pl.pallas_call(
        functools.partial(combine_kernel, count, all_rows),
        out_shape=(jax.ShapeDtypeStruct((all_rows // 2, columns), jnp.bfloat16),) * 2,
        in_specs=[in_vmem] * count + [in_place] * len(later),
        out_specs=(in_vmem,) * 2,
        compiler_params=params(2),
        name="combine",
    )(*parts, *[resident(w) for w in later])


def turned(block, step, own_rows):
    count = block.shape[0]
    span = step * own_rows
    row = lax.broadcasted_iota(jnp.int32, (count, 1), 0)
    return jnp.where(
        (row // span) % 2 == 0,
        pltpu.roll(block, count - span, axis=0),
        pltpu.roll(block, span, axis=0),
    )


def out_kernel(own_rows, left_ref, weight_ref, later_ref, part_ref, sent_ref):
    del later_ref
    rows = left_ref.shape[0]
    left = left_ref[...].astype(jnp.float32)
    left = jnp.concatenate([left, turned(left, 1, own_rows)], axis=0).astype(jnp.bfloat16)

    def store(start, size, value):
        part_ref[:, pl.ds(start, size)] = value[:rows].astype(jnp.bfloat16)
        sent_ref[:, pl.ds(start, size)] = value[rows:].astype(jnp.bfloat16)

    product_tiles(left, weight_ref, store)


def project_out(left, weight, later, own_rows):
    shape = jax.ShapeDtypeStruct((left.shape[0], weight.shape[1]), jnp.bfloat16)
    return pl.pallas_call(
        functools.partial(out_kernel, own_rows),
        out_shape=(shape, shape),
        in_specs=[in_vmem, in_vmem, in_place],
        out_specs=(in_vmem, in_vmem),
        compiler_params=params(3),
        name="project_out",
    )(left, resident(weight), resident(later))


def pair_kernel(step, own_rows, first_ref, second_ref, *refs):
    total = first_ref[...].astype(jnp.float32) + second_ref[...].astype(jnp.float32)
    if step is None:
        refs[-1][...] = total.astype(jnp.bfloat16)
    else:
        refs[-2][...] = total.astype(jnp.bfloat16)
        refs[-1][...] = turned(total, step, own_rows).astype(jnp.bfloat16)


def pair_sum(first, second, step=None, own_rows=None, later=()):
    shape = jax.ShapeDtypeStruct(first.shape, first.dtype)
    return pl.pallas_call(
        functools.partial(pair_kernel, step, own_rows),
        out_shape=shape if step is None else (shape, shape),
        in_specs=[in_vmem] * 2 + [in_place] * len(later),
        out_specs=in_vmem if step is None else (in_vmem, in_vmem),
        compiler_params=params(2),
        name="pair_sum",
    )(first, second, *[resident(w) for w in later])


def gate_up_kernel(
    rows_ref, gain_ref, first_ref, second_ref, gate_ref, up_ref, out_ref, updated_ref
):
    own_rows = updated_ref.shape[0]
    total = first_ref[...].astype(jnp.float32) + second_ref[...].astype(jnp.float32)
    updated = (rows_ref[...].astype(jnp.float32) + total).astype(jnp.bfloat16)
    wide = updated.astype(jnp.float32)
    updated_ref[...] = wide[:own_rows]
    squares = jnp.sum(wide * wide, axis=1, keepdims=True)
    scaled = (wide * gain_ref[...].astype(jnp.float32)[None, :]).astype(jnp.bfloat16)
    hidden = gate_ref.shape[1]

    def store_gate(start, size, value):
        out_ref[:, pl.ds(start, size)] = value.astype(jnp.bfloat16)

    def store_up(start, size, value):
        place = pl.multiple_of(start + hidden, math.gcd(hidden, size))
        out_ref[:, pl.ds(place, size)] = value.astype(jnp.bfloat16)

    product_tiles(scaled, gate_ref, store_gate)
    product_tiles(scaled, up_ref, store_up)
    out_ref[:, 2 * hidden :] = squares_block(squares).astype(jnp.bfloat16)


def gate_up(rows, gain, first, second, w_gate, w_up, own_rows):
    hidden = w_gate.shape[1]
    return pl.pallas_call(
        gate_up_kernel,
        out_shape=(
            jax.ShapeDtypeStruct((rows.shape[0], 2 * hidden + LANES), jnp.bfloat16),
            jax.ShapeDtypeStruct((own_rows, rows.shape[1]), jnp.float32),
        ),
        in_specs=[in_vmem] * 6,
        out_specs=(in_vmem, in_vmem),
        compiler_params=params(3),
        name="gate_up",
    )(rows, gain, first, second, resident(w_gate), resident(w_up))


def down_kernel(near_ref, far_ref, upper_ref, lower_ref, low_ref, high_ref, hidden_s, out_s):
    hidden = hidden_s.shape[1]
    cut = upper_ref.shape[0]
    squares = jnp.sum(
        near_ref[:, 2 * hidden :].astype(jnp.float32) + far_ref[:, 2 * hidden :].astype(jnp.float32),
        axis=1,
        keepdims=True,
    )
    scale = lax.rsqrt(squares / D + epsilon)
    gate = near_ref[:, :hidden].astype(jnp.float32) + far_ref[:, :hidden].astype(jnp.float32)
    up = (
        near_ref[:, hidden : 2 * hidden].astype(jnp.float32)
        + far_ref[:, hidden : 2 * hidden].astype(jnp.float32)
    )
    gate = gate * scale
    hidden_s[...] = (gate / (1.0 + jnp.exp(-gate)) * (up * scale)).astype(jnp.bfloat16)
    columns = upper_ref.shape[1]
    tile = tile_of(columns)

    @pl.loop(0, columns // tile)
    def _(step):
        span = pl.ds(pl.multiple_of(step * tile, tile), tile)
        out_s[:, span] = jnp.dot(
            hidden_s[:, :cut], upper_ref[:, span], preferred_element_type=jnp.float32
        ) + jnp.dot(hidden_s[:, cut:], lower_ref[:, span], preferred_element_type=jnp.float32)

    half = low_ref.shape[0]
    low_ref[...] = out_s[:half, :].astype(jnp.bfloat16)
    high_ref[...] = out_s[half:, :].astype(jnp.bfloat16)


def project_down(near, far, upper, lower):
    rows = near.shape[0]
    columns = upper.shape[1]
    return pl.pallas_call(
        down_kernel,
        out_shape=(jax.ShapeDtypeStruct((rows // 2, columns), jnp.bfloat16),) * 2,
        in_specs=[in_vmem] * 4,
        out_specs=(in_vmem,) * 2,
        scratch_shapes=[
            pltpu.VMEM((rows, upper.shape[0] + lower.shape[0]), jnp.bfloat16),
            pltpu.VMEM((rows, columns), jnp.float32),
        ],
        compiler_params=params(3),
        name="project_down",
    )(near, far, resident(upper), resident(lower))


def rotation_tables(positions, repeats):
    inverse = jnp.exp(
        (jnp.arange(HEAD_DIM) // 2).astype(jnp.float32) * (-2.0 / HEAD_DIM) * math.log(rope_base)
    )
    angles = positions[:, None] * inverse[None, :]
    sign = jnp.where(jnp.arange(HEAD_DIM) % 2 == 0, -1.0, 1.0)
    return (
        jnp.tile(jnp.cos(angles), (repeats, 1)),
        jnp.tile(jnp.sin(angles) * sign[None, :], (repeats, 1)),
    )


def local(
    states,
    attn_gain,
    ffn_gain,
    w_query,
    w_kv,
    w_out,
    w_gate,
    w_up,
    w_down,
    key_cache,
    value_cache,
    lengths,
):
    tensor_index = lax.axis_index("tensor")
    slots = lax.axis_size("tensor")
    own_rows = states.shape[0]
    all_rows = own_rows * slots

    loaded = {}

    def during_gather(step, value):
        if step == 1:
            value, loaded["attn_gain"], loaded["ffn_gain"], loaded["w_kv"] = load(
                value, attn_gain, ffn_gain, w_kv, after=value
            )
        if step == slots // 2:
            (loaded["w_query"],) = load(w_query, after=value)
        return value

    rows = gather_rows(states, "tensor", during_gather)
    near, far = project_qkv(rows, loaded["attn_gain"], loaded["w_query"], loaded["w_kv"])
    near, lengths = lax.optimization_barrier((near, lengths))
    my_lengths = lax.dynamic_slice_in_dim(lengths, tensor_index * own_rows, own_rows, 0)
    cosine, sine = rotation_tables(my_lengths.astype(jnp.float32), slots)
    my_lengths = jnp.broadcast_to(my_lengths[:, None], (own_rows, LANES))
    flat = (own_rows, key_cache.shape[1] * KV_HEADS, HEAD_DIM)

    def during_scatter(step, got):
        if step == slots // 2:
            (keys,) = load(key_cache.reshape(flat), after=near)
            got, loaded["keys"] = lax.optimization_barrier((got, keys))
        if step == 1:
            (values,) = load(value_cache.reshape(flat), after=loaded["keys"])
            got, loaded["values"] = lax.optimization_barrier((got, values))
        return got

    joined = jnp.concatenate(scatter_rows(near, far, "tensor", during_scatter), axis=0)
    shard = attend(
        my_lengths,
        cosine,
        sine,
        exchange(joined, "inner"),
        loaded["keys"],
        loaded["values"],
        slots,
    )
    (w_out,) = load(w_out, after=shard)
    near, far = combine(exchange(shard, "inner"), [w_out, w_gate], all_rows)

    alone = lambda step, value: value
    picked = jnp.concatenate(scatter_rows(near, far, "tensor", alone), axis=0)
    part, sent = project_out(picked, w_out, w_up, own_rows)
    steps = steps_up(slots)
    for step, following in zip(steps, steps[1:] + [None]):
        other = swap_with(sent, "tensor", step)
        if following:
            part, sent = pair_sum(part, other, following, own_rows)
    joined, updated = gate_up(rows, loaded["ffn_gain"], part, other, w_gate, w_up, own_rows)

    steps = steps_up(lax.axis_size("inner"))
    cut = w_down.shape[0] // 64 * 16
    (upper,) = load(w_down, after=joined, spans=[(0, cut)])
    for step in steps[:-1]:
        joined = pair_sum(joined, swap_with(joined, "inner", step), later=[upper])
    (lower,) = load(w_down, after=joined, spans=[(cut, w_down.shape[0] - cut)])
    other = swap_with(joined, "inner", steps[-1])
    near, far = project_down(joined, other, upper, lower)
    parts = scatter_rows(near, far, "tensor", alone)
    down_sum = sum(p.astype(jnp.float32) for p in parts)
    return (updated + down_sum).astype(jnp.bfloat16)


def solution(mesh):
    in_specs = (
        P(("groups", "tensor"), "inner"),
        P("inner"),
        P("inner"),
        P("inner", "tensor"),
        P("inner", "tensor"),
        P("tensor", "inner"),
        P("inner", "tensor"),
        P("inner", "tensor"),
        P("tensor", "inner"),
        P(("groups", "tensor"), "inner", None, None),
        P(("groups", "tensor"), "inner", None, None),
        P("groups"),
    )
    out_specs = P(("groups", "tensor"), "inner")
    return jax.shard_map(local, mesh=mesh, in_specs=in_specs, out_specs=out_specs, check_vma=False)
```

time: 96.3 us -> 72.7 us (0.75)
  local copies, waits for them, and re-layouts: 20.2 us -> 0.21 us
  Pallas kernels: 36.5 us -> 26.2 us
  waiting for transfers between devices: 9.65 us -> 16 us
  starting transfers between devices: 27.7 us -> 28.7 us
    unnamed x20 -> x18, local copies, waits for them, and re-layouts: 19.2 us -> 0.05 us
    pallas_call x11 -> x14, Pallas kernels: 36.2 us -> 25.9 us  [the longest x7 15.9 us: load(): pl.pallas_call(functools.partial(load_kernel, spans), out_shape=tuple((pl...]
    ppermute x22 -> x18, waiting for transfers between devices: 9.65 us -> 16 us  [swap_with(): return lax.ppermute(value, axis, [(i, i ^ step) for i in range(count)])]
    ppermute x22 -> x18, starting transfers between devices: 27.7 us -> 28.7 us  [swap_with(): return lax.ppermute(value, axis, [(i, i ^ step) for i in range(count)])]
  transfers between devices with their start and end apart: 22 -> 18, of which waited for: 7 -> 12; matrix products, arithmetic and copies ran while one was open for 2% -> 0% of each run, Pallas kernels for 24% -> 22%
where the time goes in v4:
time: 72.7 us; the launch traced here: 72.5 us
  starting transfers between devices  28.7 us (39%)
  Pallas kernels  26.2 us (36%)
  waiting for transfers between devices  16 us (22%)
  other arithmetic  0.99 us (1%)
    ppermute x18, starting transfers between devices, swap_with(): return lax.ppermute(value, axis, [(i, i ^ step) for i in range(count)])  28.7 us
    ppermute x18, waiting for transfers between devices, swap_with(): return lax.ppermute(value, axis, [(i, i ^ step) for i in range(count)])  16 us
    pallas_call x7, Pallas kernels, load(): pl.pallas_call(functools.partial(load_kernel, spans), out_shape=tuple((pl...  15.9 us
    pallas_call x1, Pallas kernels, gate_up(): pl.pallas_call(gate_up_kernel, out_shape=(jax.ShapeDtypeStruct((rows.shap...  4.37 us
    pallas_call x1, Pallas kernels, project_down(): pl.pallas_call(down_kernel, out_shape=(jax.ShapeDtypeStruct((rows // 2, c...  2.27 us
    pallas_call x1, Pallas kernels, attend(): pl.pallas_call(functools.partial(attend_kernel, slots, len(parts)), out_s...  1.74 us
  transfers between devices with their start and end apart: 18, of which 12 were waited for; matrix products, arithmetic and copies ran while one was open for 0% of the time, Pallas kernels for 22%

profile of v4, /device:TPU:0, one launch (start us, length us, event | category | flops | bytes accessed | tf_op | source)
XLA Modules:
  0.0 72.5 jit_solution(172882131766969002)
XLA Ops:
  0.0 3.0 %collective-permute-start = (bf16[2,2048]{1,0:T(2,128)(2,1)}, bf16[2,2048]{1,0:T(2,128)(2,1)S(1)}, u32[]{:S(2)}, u32[]{:S(2)}) collective-permute-start(bf16[2,2048]{1,0:T(2,128)(2,1)} %refs_4_.1), channel_id=1, source_target_pairs={{0,4},{4,0},{8,12},{12,8},{1,5},{5,1},{9,13},{13,9},{2,6},{6,2},{1... | collective-permute-start | bytes 24584 | tf_op jit(solution)/shard_map/ppermute | solution.py:30
  3.0 1.4 %load.7 = (bf16[2,2048]{1,0:T(2,128)(2,1)S(1)}, bf16[2048]{0:T(1024)(128)(2,1)S(1)}, bf16[2048]{0:T(1024)(128)(2,1)S(1)}, bf16[2048,256]{1,0:T(8,128)(2,1)S(1)}) custom-call(bf16[2,2048]{1,0:T(2,128)(2,1)} %refs_4_.1, bf16[2048]{0:T(1024)(128)(2,1)} %refs_1_.1, bf16[2048]{0:T(1024)(128)(2,1)} %refs_2_.1, bf16[2048,256]{1,0:T(8,128)(2,1)} %refs_3_.1, ...), custom_call_target="tpu_custom_call" | custom-call | bytes 1064960 | tf_op jit(solution)/shard_map/load/pallas_call | solution.py:148
  4.4 0.5 collective-permute-done
  4.9 3.1 %collective-permute-start.1 = (bf16[4,2048]{1,0:T(4,128)(2,1)S(1)}, bf16[4,2048]{1,0:T(4,128)(2,1)S(1)}, u32[]{:S(2)}, u32[]{:S(2)}) collective-permute-start(bf16[4,2048]{1,0:T(4,128)(2,1)S(1)} %pad_maximum_fusion.2.refs_1_), channel_id=1, source_target_pairs={{0,8},{4,12},{8,0},{12,4},{1,9},{5,13},{9,1},{13,5},{2,10},{6,14},... | collective-permute-start | bytes 49160 | tf_op jit(solution)/shard_map/ppermute | solution.py:30
  8.0 2.2 %load.8.wq_ref = bf16[2048,1024]{1,0:T(8,128)(2,1)S(1)} custom-call(bf16[2048,1024]{1,0:T(8,128)(2,1)} %refs_0_.6, bf16[4,2048]{1,0:T(4,128)(2,1)S(1)} %pad_maximum_fusion.2.refs_1_), custom_call_target="tpu_custom_call" | custom-call | bytes 4194304 | tf_op jit(solution)/shard_map/load/pallas_call | solution.py:148
  10.2 0.0 collective-permute-done.1
  10.3 0.0 copy-start
  10.3 0.0 slice-start
  10.3 0.8 %project_qkv.1 = (bf16[4,1408]{1,0:T(4,128)(2,1)S(1)}, bf16[4,1408]{1,0:T(4,128)(2,1)S(1)}) custom-call(bf16[8,2048]{1,0:T(8,128)(2,1)S(1)} %pad_maximum_fusion.rows_ref, bf16[2048]{0:T(1024)(128)(2,1)S(1)} %get-tuple-element.29.gain_ref, bf16[2048,1024]{1,0:T(8,128)(2,1)S(1)} %load.8.wq_ref, bf16[2048,256]{1,0:T(8,128)(2,1)S(1)} %get-tuple-element.30.wkv_ref), custom_call_target="tpu_custom_call" | custom-call | tf_op jit(solution)/shard_map/project_qkv/pallas_call | solution.py:186
  11.1 2.4 %collective-permute-start.2 = (bf16[4,1408]{1,0:T(4,128)(2,1)S(1)}, bf16[4,1408]{1,0:T(4,128)(2,1)S(1)}, u32[]{:S(2)}, u32[]{:S(2)}) collective-permute-start(bf16[4,1408]{1,0:T(4,128)(2,1)S(1)} %get-tuple-element.33), channel_id=1, source_target_pairs={{0,8},{4,12},{8,0},{12,4},{1,9},{5,13},{9,1},{13,5},{2,10},{6,14},... | collective-permute-start | bytes 33800 | tf_op jit(solution)/shard_map/ppermute | solution.py:30
  13.5 1.8 %load.9.refs_1_.key_ref = bf16[2,4096,128]{2,1,0:T(8,128)(2,1)S(1)} custom-call(bf16[2,4096,128]{2,1,0:T(8,128)(2,1)} %bitcast.11, bf16[4,1408]{1,0:T(4,128)(2,1)S(1)} %get-tuple-element.34.refs_1_), custom_call_target="tpu_custom_call" | custom-call | bytes 2097152 | tf_op jit(solution)/shard_map/load/pallas_call | solution.py:148
  15.3 0.4 collective-permute-done.2
  15.7 1.7 %collective-permute-start.3 = (bf16[4,1408]{1,0:T(4,128)(2,1)S(1)}, bf16[4,1408]{1,0:T(4,128)(2,1)S(1)}, u32[]{:S(2)}, u32[]{:S(2)}) collective-permute-start(bf16[4,1408]{1,0:T(4,128)(2,1)S(1)} %pad_maximum_fusion.5), channel_id=1, source_target_pairs={{0,4},{4,0},{8,12},{12,8},{1,5},{5,1},{9,13},{13,9},{2,6},{6,2},{1... | collective-permute-start | bytes 33800 | tf_op jit(solution)/shard_map/ppermute | solution.py:30
  17.4 0.0 copy-done
  17.4 0.1 fusion.4
  17.5 1.8 %load.10.value_ref = bf16[2,4096,128]{2,1,0:T(8,128)(2,1)S(1)} custom-call(bf16[2,4096,128]{2,1,0:T(8,128)(2,1)} %bitcast.10, bf16[2,4096,128]{2,1,0:T(8,128)(2,1)S(1)} %load.9.refs_1_.key_ref), custom_call_target="tpu_custom_call" | custom-call | bytes 2097152 | tf_op jit(solution)/shard_map/load/pallas_call | solution.py:148
  19.3 0.2 collective-permute-done.3
  19.5 0.1 collective-permute-start.6
  19.6 1.6 %collective-permute-start.5 = (bf16[8,1408]{1,0:T(8,128)(2,1)S(1)}, bf16[8,1408]{1,0:T(8,128)(2,1)S(1)}, u32[]{:S(2)}, u32[]{:S(2)}) collective-permute-start(bf16[8,1408]{1,0:T(8,128)(2,1)S(1)} %pad_maximum_fusion.1.refs_0_), channel_id=1, source_target_pairs={{0,2},{1,3},{2,0},{3,1},{4,6},{5,7},{6,4},{7,5},{8,10},{9,11},{10,... | collective-permute-start | bytes 67592 | tf_op jit(solution)/shard_map/ppermute | solution.py:30
  21.2 0.3 collective-permute-start.4
  21.5 0.1 fusion
  21.6 1.4 %collective-permute-done.6.refs_3_ = bf16[8,1408]{1,0:T(8,128)(2,1)S(1)} collective-permute-done((bf16[8,1408]{1,0:T(8,128)(2,1)S(1)}, bf16[8,1408]{1,0:T(8,128)(2,1)S(1)}, u32[]{:S(2)}, u32[]{:S(2)}) %collective-permute-start.6) | collective-permute-done | bytes 22560 | tf_op jit(solution)/shard_map/ppermute | solution.py:30
  23.0 0.5 collective-permute-done.5.refs_2_
  23.5 0.0 collective-permute-done.4.refs_1_
  23.5 0.1 broadcast_in_dim.10.lengths_ref
  23.6 1.7 %attend.1.refs_1_.refs_0_ = bf16[64,256]{1,0:T(8,128)(2,1)S(1)} custom-call(s32[2,128]{1,0:T(2,128)S(1)} %broadcast_in_dim.10.lengths_ref, f32[8,128]{1,0:T(8,128)S(1)} %bitcast.9, f32[8,128]{1,0:T(8,128)S(1)} %bitcast.8, bf16[2,4096,128]{2,1,0:T(8,128)(2,1)S(1)} %load.9.refs_1_.key_ref, bf16[2,4096,128]{2,1,0:T(8,128)(2,1)S(1)} %load.10.value_ref, ...), custom_call_target="tpu_custom_call" | custom-call | tf_op jit(solution)/shard_map/attend/pallas_call | solution.py:297
  25.3 0.0 slice-start.3
  25.3 0.0 slice-start.5
  25.3 0.6 collective-permute-start.9
  25.9 1.5 %collective-permute-start.8 = (bf16[64,256]{1,0:T(8,128)(2,1)S(1)}, bf16[64,256]{1,0:T(8,128)(2,1)S(1)}, u32[]{:S(2)}, u32[]{:S(2)}) collective-permute-start(bf16[64,256]{1,0:T(8,128)(2,1)S(1)} %attend.1.refs_1_.refs_0_), channel_id=1, source_target_pairs={{0,2},{1,3},{2,0},{3,1},{4,6},{5,7},{6,4},{7,5},{8,10},{9,11},{10,... | collective-permute-start | bytes 98312 | tf_op jit(solution)/shard_map/ppermute | solution.py:30
  27.4 0.0 collective-permute-start.7
  27.4 2.5 %load.11.refs_4_.weight_ref = bf16[1024,2048]{1,0:T(8,128)(2,1)S(1)} custom-call(bf16[1024,2048]{1,0:T(8,128)(2,1)} %refs_0_.7, bf16[64,256]{1,0:T(8,128)(2,1)S(1)} %attend.1.refs_1_.refs_0_), custom_call_target="tpu_custom_call" | custom-call | bytes 4194304 | tf_op jit(solution)/shard_map/load/pallas_call | solution.py:148
  29.9 0.0 slice-start.6
  29.9 0.0 slice-start.7
  29.9 0.0 collective-permute-done.9.refs_3_
  29.9 0.2 collective-permute-done.8.refs_2_
  30.1 0.0 collective-permute-done.7.refs_1_
  30.1 0.0 slice-done
  30.1 0.0 slice-done.1
  30.1 0.0 slice-done.2
  30.2 0.0 slice-done.3
  30.2 0.3 combine.1
  30.4 2.5 %collective-permute-start.10 = (bf16[4,1024]{1,0:T(4,128)(2,1)S(1)}, bf16[4,1024]{1,0:T(4,128)(2,1)S(1)}, u32[]{:S(2)}, u32[]{:S(2)}) collective-permute-start(bf16[4,1024]{1,0:T(4,128)(2,1)S(1)} %get-tuple-element.40), channel_id=1, source_target_pairs={{0,8},{4,12},{8,0},{12,4},{1,9},{5,13},{9,1},{13,5},{2,10},{6,14},... | collective-permute-start | bytes 24584 | tf_op jit(solution)/shard_map/ppermute | solution.py:30
  32.9 2.1 %collective-permute-done.10 = bf16[4,1024]{1,0:T(4,128)(2,1)S(1)} collective-permute-done((bf16[4,1024]{1,0:T(4,128)(2,1)S(1)}, bf16[4,1024]{1,0:T(4,128)(2,1)S(1)}, u32[]{:S(2)}, u32[]{:S(2)}) %collective-permute-start.10) | collective-permute-done | bytes 8224 | tf_op jit(solution)/shard_map/ppermute | solution.py:30
  35.1 1.7 %collective-permute-start.11 = (bf16[4,1024]{1,0:T(4,128)(2,1)S(1)}, bf16[4,1024]{1,0:T(4,128)(2,1)S(1)}, u32[]{:S(2)}, u32[]{:S(2)}) collective-permute-start(bf16[4,1024]{1,0:T(4,128)(2,1)S(1)} %pad_maximum_fusion.6), channel_id=1, source_target_pairs={{0,4},{4,0},{8,12},{12,8},{1,5},{5,1},{9,13},{13,9},{2,6},{6,2},{1... | collective-permute-start | bytes 24584 | tf_op jit(solution)/shard_map/ppermute | solution.py:30
  36.8 2.0 %collective-permute-done.11 = bf16[4,1024]{1,0:T(4,128)(2,1)S(1)} collective-permute-done((bf16[4,1024]{1,0:T(4,128)(2,1)S(1)}, bf16[4,1024]{1,0:T(4,128)(2,1)S(1)}, u32[]{:S(2)}, u32[]{:S(2)}) %collective-permute-start.11) | collective-permute-done | bytes 8224 | tf_op jit(solution)/shard_map/ppermute | solution.py:30
  38.9 0.8 %project_out.1 = (bf16[8,2048]{1,0:T(8,128)(2,1)S(1)}, bf16[8,2048]{1,0:T(8,128)(2,1)S(1)}) custom-call(bf16[8,1024]{1,0:T(8,128)(2,1)S(1)} %pad_maximum_fusion.3.left_ref, bf16[1024,2048]{1,0:T(8,128)(2,1)S(1)} %load.11.refs_4_.weight_ref, bf16[2048,3584]{1,0:T(8,128)(2,1)S(1)} %bitcast.7), custom_call_target="tpu_custom_call" | custom-call | tf_op jit(solution)/shard_map/project_out/pallas_call | solution.py:377
  39.7 1.7 %collective-permute-start.12 = (bf16[8,2048]{1,0:T(8,128)(2,1)S(1)}, bf16[8,2048]{1,0:T(8,128)(2,1)S(1)}, u32[]{:S(2)}, u32[]{:S(2)}) collective-permute-start(bf16[8,2048]{1,0:T(8,128)(2,1)S(1)} %get-tuple-element.42), channel_id=1, source_target_pairs={{0,4},{4,0},{8,12},{12,8},{1,5},{5,1},{9,13},{13,9},{2,6},{6,2},{1... | collective-permute-start | bytes 98312 | tf_op jit(solution)/shard_map/ppermute | solution.py:30
  41.3 2.3 %collective-permute-done.12.second_ref = bf16[8,2048]{1,0:T(8,128)(2,1)S(1)} collective-permute-done((bf16[8,2048]{1,0:T(8,128)(2,1)S(1)}, bf16[8,2048]{1,0:T(8,128)(2,1)S(1)}, u32[]{:S(2)}, u32[]{:S(2)}) %collective-permute-start.12) | collective-permute-done | bytes 32800 | tf_op jit(solution)/shard_map/ppermute | solution.py:30
  43.6 2.8 %collective-permute-start.13 = (bf16[8,2048]{1,0:T(8,128)(2,1)S(1)}, bf16[8,2048]{1,0:T(8,128)(2,1)S(1)}, u32[]{:S(2)}, u32[]{:S(2)}) collective-permute-start(bf16[8,2048]{1,0:T(8,128)(2,1)S(1)} %get-tuple-element.44), channel_id=1, source_target_pairs={{0,8},{4,12},{8,0},{12,4},{1,9},{5,13},{9,1},{13,5},{2,10},{6,14},... | collective-permute-start | bytes 98312 | tf_op jit(solution)/shard_map/ppermute | solution.py:30
  46.4 2.1 %collective-permute-done.13.second_ref = bf16[8,2048]{1,0:T(8,128)(2,1)S(1)} collective-permute-done((bf16[8,2048]{1,0:T(8,128)(2,1)S(1)}, bf16[8,2048]{1,0:T(8,128)(2,1)S(1)}, u32[]{:S(2)}, u32[]{:S(2)}) %collective-permute-start.13) | collective-permute-done | bytes 32800 | tf_op jit(solution)/shard_map/ppermute | solution.py:30
  48.5 4.4 %gate_up.1 = (bf16[8,7296]{1,0:T(8,128)(2,1)S(1)}, f32[2,2048]{1,0:T(2,128)S(1)}) custom-call(bf16[8,2048]{1,0:T(8,128)(2,1)S(1)} %pad_maximum_fusion.rows_ref, bf16[2048]{0:T(1024)(128)(2,1)S(1)} %get-tuple-element.28.gain_ref, bf16[8,2048]{1,0:T(8,128)(2,1)S(1)} %get-tuple-element.43.first_ref, bf16[8,2048]{1,0:T(8,128)(2,1)S(1)} %collective-permute-done.13.second_ref, ...), custom_call_target="tpu_custom_call" | custom-call | tf_op jit(solution)/shard_map/gate_up/pallas_call | solution.py:434
  52.9 0.0 collective-permute-start.14
  52.9 2.0 %load.12.refs_0_.upper_ref = bf16[896,2048]{1,0:T(8,128)(2,1)S(1)} custom-call(bf16[3584,2048]{1,0:T(8,128)(2,1)} %refs_0_.9, bf16[8,7296]{1,0:T(8,128)(2,1)S(1)} %get-tuple-element.46.refs_1_.first_ref), custom_call_target="tpu_custom_call" | custom-call | bytes 3670016 | tf_op jit(solution)/shard_map/load/pallas_call | solution.py:148
  54.9 0.0 collective-permute-done.14.second_ref
  55.0 1.7 %collective-permute-start.15 = (bf16[8,7296]{1,0:T(8,128)(2,1)S(1)}, bf16[8,7296]{1,0:T(8,128)(2,1)S(1)}, u32[]{:S(2)}, u32[]{:S(2)}) collective-permute-start(bf16[8,7296]{1,0:T(8,128)(2,1)S(1)} %pair_sum.3.refs_1_.near_ref), channel_id=1, source_target_pairs={{0,2},{1,3},{2,0},{3,1},{4,6},{5,7},{6,4},{7,5},{8,10},{9,11},{10,... | collective-permute-start | bytes 350216 | tf_op jit(solution)/shard_map/ppermute | solution.py:30
  56.7 4.2 %load.13.lower_ref = bf16[2688,2048]{1,0:T(8,128)(2,1)S(1)} custom-call(bf16[3584,2048]{1,0:T(8,128)(2,1)} %refs_0_.9, bf16[8,7296]{1,0:T(8,128)(2,1)S(1)} %pair_sum.3.refs_1_.near_ref), custom_call_target="tpu_custom_call" | custom-call | bytes 11010048 | tf_op jit(solution)/shard_map/load/pallas_call | solution.py:148
  61.0 0.0 collective-permute-done.15.far_ref
  61.0 2.3 %project_down.1 = (bf16[4,2048]{1,0:T(4,128)(2,1)S(1)}, bf16[4,2048]{1,0:T(4,128)(2,1)S(1)}) custom-call(bf16[8,7296]{1,0:T(8,128)(2,1)S(1)} %pair_sum.3.refs_1_.near_ref, bf16[8,7296]{1,0:T(8,128)(2,1)S(1)} %collective-permute-done.15.far_ref, bf16[896,2048]{1,0:T(8,128)(2,1)S(1)} %load.12.refs_0_.upper_ref, bf16[2688,2048]{1,0:T(8,128)(2,1)S(1)} %load.13.lower_ref), custom_call_target="tpu_custom_call" | custom-call | tf_op jit(solution)/shard_map/project_down/pallas_call | solution.py:481
  63.3 2.5 %collective-permute-start.16 = (bf16[4,2048]{1,0:T(4,128)(2,1)S(1)}, bf16[4,2048]{1,0:T(4,128)(2,1)S(1)}, u32[]{:S(2)}, u32[]{:S(2)}) collective-permute-start(bf16[4,2048]{1,0:T(4,128)(2,1)S(1)} %get-tuple-element.48), channel_id=1, source_target_pairs={{0,8},{4,12},{8,0},{12,4},{1,9},{5,13},{9,1},{13,5},{2,10},{6,14},... | collective-permute-start | bytes 49160 | tf_op jit(solution)/shard_map/ppermute | solution.py:30
  65.8 2.2 %collective-permute-done.16 = bf16[4,2048]{1,0:T(4,128)(2,1)S(1)} collective-permute-done((bf16[4,2048]{1,0:T(4,128)(2,1)S(1)}, bf16[4,2048]{1,0:T(4,128)(2,1)S(1)}, u32[]{:S(2)}, u32[]{:S(2)}) %collective-permute-start.16) | collective-permute-done | bytes 16416 | tf_op jit(solution)/shard_map/ppermute | solution.py:30
  68.0 1.6 %collective-permute-start.17 = (bf16[4,2048]{1,0:T(4,128)(2,1)S(1)}, bf16[4,2048]{1,0:T(4,128)(2,1)S(1)}, u32[]{:S(2)}, u32[]{:S(2)}) collective-permute-start(bf16[4,2048]{1,0:T(4,128)(2,1)S(1)} %pad_maximum_fusion.4), channel_id=1, source_target_pairs={{0,4},{4,0},{8,12},{12,8},{1,5},{5,1},{9,13},{13,9},{2,6},{6,2},{1... | collective-permute-start | bytes 49160 | tf_op jit(solution)/shard_map/ppermute | solution.py:30
  69.7 2.2 %collective-permute-done.17 = bf16[4,2048]{1,0:T(4,128)(2,1)S(1)} collective-permute-done((bf16[4,2048]{1,0:T(4,128)(2,1)S(1)}, bf16[4,2048]{1,0:T(4,128)(2,1)S(1)}, u32[]{:S(2)}, u32[]{:S(2)}) %collective-permute-start.17) | collective-permute-done | bytes 16416 | tf_op jit(solution)/shard_map/ppermute | solution.py:30
  71.8 0.6 add_convert_fusion
  (28 shorter events, 0.3 us)
Async XLA Ops:
  0.0 4.9 %collective-permute-start = (bf16[2,2048]{1,0:T(2,128)(2,1)}, bf16[2,2048]{1,0:T(2,128)(2,1)S(1)}, u32[]{:S(2)}, u32[]{:S(2)}) collective-permute-start(bf16[2,2048]{1,0:T(2,128)(2,1)} %refs_4_.1), channel_id=1, source_target_pairs={{0,4},{4,0},{8,12},{12,8},{1,5},{5,1},{9,13},{13,9},{2,6},{6,2},{1... | collective-permute-start | bytes 24584 | tf_op jit(solution)/shard_map/ppermute | solution.py:30
  4.9 5.3 %collective-permute-start.1 = (bf16[4,2048]{1,0:T(4,128)(2,1)S(1)}, bf16[4,2048]{1,0:T(4,128)(2,1)S(1)}, u32[]{:S(2)}, u32[]{:S(2)}) collective-permute-start(bf16[4,2048]{1,0:T(4,128)(2,1)S(1)} %pad_maximum_fusion.2.refs_1_), channel_id=1, source_target_pairs={{0,8},{4,12},{8,0},{12,4},{1,9},{5,13},{9,1},{13,5},{2,10},{6,14},... | collective-permute-start | bytes 49160 | tf_op jit(solution)/shard_map/ppermute | solution.py:30
  10.3 7.2 %copy-start = (s32[8]{0:T(128)S(1)}, s32[8]{0:T(128)}, u32[]{:S(2)}) copy-start(s32[8]{0:T(128)} %param.23) | copy-start | bytes 100
  10.3 19.9 %slice-start = ((s8[14680064]{0:T(1024)(128)(4,1)}), s8[2097152]{0:T(1024)(128)(4,1)S(1)}, s32[]{:S(2)}) async-start(s8[14680064]{0:T(1024)(128)(4,1)} %bitcast.4), calls=%async_computation | async-start | bytes 4194304
  11.1 4.6 %collective-permute-start.2 = (bf16[4,1408]{1,0:T(4,128)(2,1)S(1)}, bf16[4,1408]{1,0:T(4,128)(2,1)S(1)}, u32[]{:S(2)}, u32[]{:S(2)}) collective-permute-start(bf16[4,1408]{1,0:T(4,128)(2,1)S(1)} %get-tuple-element.33), channel_id=1, source_target_pairs={{0,8},{4,12},{8,0},{12,4},{1,9},{5,13},{9,1},{13,5},{2,10},{6,14},... | collective-permute-start | bytes 33800 | tf_op jit(solution)/shard_map/ppermute | solution.py:30
  13.5 16.6 %slice-start.1 = ((s8[14680064]{0:T(1024)(128)(4,1)}), s8[4194304]{0:T(1024)(128)(4,1)S(1)}, s32[]{:S(2)}) async-start(s8[14680064]{0:T(1024)(128)(4,1)} %bitcast.4), calls=%async_computation.1 | async-start | bytes 8388608
  15.7 3.7 %collective-permute-start.3 = (bf16[4,1408]{1,0:T(4,128)(2,1)S(1)}, bf16[4,1408]{1,0:T(4,128)(2,1)S(1)}, u32[]{:S(2)}, u32[]{:S(2)}) collective-permute-start(bf16[4,1408]{1,0:T(4,128)(2,1)S(1)} %pad_maximum_fusion.5), channel_id=1, source_target_pairs={{0,4},{4,0},{8,12},{12,8},{1,5},{5,1},{9,13},{13,9},{2,6},{6,2},{1... | collective-permute-start | bytes 33800 | tf_op jit(solution)/shard_map/ppermute | solution.py:30
  17.5 12.6 %slice-start.2 = ((s8[14680064]{0:T(1024)(128)(4,1)}), s8[4194304]{0:T(1024)(128)(4,1)S(1)}, s32[]{:S(2)}) async-start(s8[14680064]{0:T(1024)(128)(4,1)} %bitcast.4), calls=%async_computation.2 | async-start | bytes 8388608
  19.5 3.5 %collective-permute-start.6 = (bf16[8,1408]{1,0:T(8,128)(2,1)S(1)}, bf16[8,1408]{1,0:T(8,128)(2,1)S(1)}, u32[]{:S(2)}, u32[]{:S(2)}) collective-permute-start(bf16[8,1408]{1,0:T(8,128)(2,1)S(1)} %pad_maximum_fusion.1.refs_0_), channel_id=1, source_target_pairs={{0,3},{1,2},{2,1},{3,0},{4,7},{5,6},{6,5},{7,4},{8,11},{9,10},{10,... | collective-permute-start | bytes 67592 | tf_op jit(solution)/shard_map/ppermute | solution.py:30
  19.6 3.9 %collective-permute-start.5 = (bf16[8,1408]{1,0:T(8,128)(2,1)S(1)}, bf16[8,1408]{1,0:T(8,128)(2,1)S(1)}, u32[]{:S(2)}, u32[]{:S(2)}) collective-permute-start(bf16[8,1408]{1,0:T(8,128)(2,1)S(1)} %pad_maximum_fusion.1.refs_0_), channel_id=1, source_target_pairs={{0,2},{1,3},{2,0},{3,1},{4,6},{5,7},{6,4},{7,5},{8,10},{9,11},{10,... | collective-permute-start | bytes 67592 | tf_op jit(solution)/shard_map/ppermute | solution.py:30
  21.2 2.3 %collective-permute-start.4 = (bf16[8,1408]{1,0:T(8,128)(2,1)S(1)}, bf16[8,1408]{1,0:T(8,128)(2,1)S(1)}, u32[]{:S(2)}, u32[]{:S(2)}) collective-permute-start(bf16[8,1408]{1,0:T(8,128)(2,1)S(1)} %pad_maximum_fusion.1.refs_0_), channel_id=1, source_target_pairs={{0,1},{1,0},{2,3},{3,2},{4,5},{5,4},{6,7},{7,6},{8,9},{9,8},{10,11... | collective-permute-start | bytes 67592 | tf_op jit(solution)/shard_map/ppermute | solution.py:30
  23.6 15.3 %slice-start.4 = ((s8[14680064]{0:T(1024)(128)(4,1)}), s8[4194304]{0:T(1024)(128)(4,1)S(1)}, s32[]{:S(2)}) async-start(s8[14680064]{0:T(1024)(128)(4,1)} %bitcast.6), calls=%async_computation.4 | async-start | bytes 8388608
  25.3 4.9 %slice-start.3 = ((s8[14680064]{0:T(1024)(128)(4,1)}), s8[4194304]{0:T(1024)(128)(4,1)S(1)}, s32[]{:S(2)}) async-start(s8[14680064]{0:T(1024)(128)(4,1)} %bitcast.4), calls=%async_computation.3 | async-start | bytes 8388608
  25.3 13.5 %slice-start.5 = ((s8[14680064]{0:T(1024)(128)(4,1)}), s8[4194304]{0:T(1024)(128)(4,1)S(1)}, s32[]{:S(2)}) async-start(s8[14680064]{0:T(1024)(128)(4,1)} %bitcast.6), calls=%async_computation.5 | async-start | bytes 8388608
  25.3 4.6 %collective-permute-start.9 = (bf16[64,256]{1,0:T(8,128)(2,1)S(1)}, bf16[64,256]{1,0:T(8,128)(2,1)S(1)}, u32[]{:S(2)}, u32[]{:S(2)}) collective-permute-start(bf16[64,256]{1,0:T(8,128)(2,1)S(1)} %attend.1.refs_1_.refs_0_), channel_id=1, source_target_pairs={{0,3},{1,2},{2,1},{3,0},{4,7},{5,6},{6,5},{7,4},{8,11},{9,10},{10,... | collective-permute-start | bytes 98312 | tf_op jit(solution)/shard_map/ppermute | solution.py:30
  25.9 4.2 %collective-permute-start.8 = (bf16[64,256]{1,0:T(8,128)(2,1)S(1)}, bf16[64,256]{1,0:T(8,128)(2,1)S(1)}, u32[]{:S(2)}, u32[]{:S(2)}) collective-permute-start(bf16[64,256]{1,0:T(8,128)(2,1)S(1)} %attend.1.refs_1_.refs_0_), channel_id=1, source_target_pairs={{0,2},{1,3},{2,0},{3,1},{4,6},{5,7},{6,4},{7,5},{8,10},{9,11},{10,... | collective-permute-start | bytes 98312 | tf_op jit(solution)/shard_map/ppermute | solution.py:30
  27.4 2.7 %collective-permute-start.7 = (bf16[64,256]{1,0:T(8,128)(2,1)S(1)}, bf16[64,256]{1,0:T(8,128)(2,1)S(1)}, u32[]{:S(2)}, u32[]{:S(2)}) collective-permute-start(bf16[64,256]{1,0:T(8,128)(2,1)S(1)} %attend.1.refs_1_.refs_0_), channel_id=1, source_target_pairs={{0,1},{1,0},{2,3},{3,2},{4,5},{5,4},{6,7},{7,6},{8,9},{9,8},{10,11... | collective-permute-start | bytes 98312 | tf_op jit(solution)/shard_map/ppermute | solution.py:30
  29.9 9.0 %slice-start.6 = ((s8[14680064]{0:T(1024)(128)(4,1)}), s8[4194304]{0:T(1024)(128)(4,1)S(1)}, s32[]{:S(2)}) async-start(s8[14680064]{0:T(1024)(128)(4,1)} %bitcast.6), calls=%async_computation.6 | async-start | bytes 8388608
  29.9 9.0 %slice-start.7 = ((s8[14680064]{0:T(1024)(128)(4,1)}), s8[2097152]{0:T(1024)(128)(4,1)S(1)}, s32[]{:S(2)}) async-start(s8[14680064]{0:T(1024)(128)(4,1)} %bitcast.6), calls=%async_computation.7 | async-start | bytes 4194304
  30.4 4.6 %collective-permute-start.10 = (bf16[4,1024]{1,0:T(4,128)(2,1)S(1)}, bf16[4,1024]{1,0:T(4,128)(2,1)S(1)}, u32[]{:S(2)}, u32[]{:S(2)}) collective-permute-start(bf16[4,1024]{1,0:T(4,128)(2,1)S(1)} %get-tuple-element.40), channel_id=1, source_target_pairs={{0,8},{4,12},{8,0},{12,4},{1,9},{5,13},{9,1},{13,5},{2,10},{6,14},... | collective-permute-start | bytes 24584 | tf_op jit(solution)/shard_map/ppermute | solution.py:30
  35.1 3.7 %collective-permute-start.11 = (bf16[4,1024]{1,0:T(4,128)(2,1)S(1)}, bf16[4,1024]{1,0:T(4,128)(2,1)S(1)}, u32[]{:S(2)}, u32[]{:S(2)}) collective-permute-start(bf16[4,1024]{1,0:T(4,128)(2,1)S(1)} %pad_maximum_fusion.6), channel_id=1, source_target_pairs={{0,4},{4,0},{8,12},{12,8},{1,5},{5,1},{9,13},{13,9},{2,6},{6,2},{1... | collective-permute-start | bytes 24584 | tf_op jit(solution)/shard_map/ppermute | solution.py:30
  39.7 3.9 %collective-permute-start.12 = (bf16[8,2048]{1,0:T(8,128)(2,1)S(1)}, bf16[8,2048]{1,0:T(8,128)(2,1)S(1)}, u32[]{:S(2)}, u32[]{:S(2)}) collective-permute-start(bf16[8,2048]{1,0:T(8,128)(2,1)S(1)} %get-tuple-element.42), channel_id=1, source_target_pairs={{0,4},{4,0},{8,12},{12,8},{1,5},{5,1},{9,13},{13,9},{2,6},{6,2},{1... | collective-permute-start | bytes 98312 | tf_op jit(solution)/shard_map/ppermute | solution.py:30
  43.6 4.9 %collective-permute-start.13 = (bf16[8,2048]{1,0:T(8,128)(2,1)S(1)}, bf16[8,2048]{1,0:T(8,128)(2,1)S(1)}, u32[]{:S(2)}, u32[]{:S(2)}) collective-permute-start(bf16[8,2048]{1,0:T(8,128)(2,1)S(1)} %get-tuple-element.44), channel_id=1, source_target_pairs={{0,8},{4,12},{8,0},{12,4},{1,9},{5,13},{9,1},{13,5},{2,10},{6,14},... | collective-permute-start | bytes 98312 | tf_op jit(solution)/shard_map/ppermute | solution.py:30
  52.9 2.1 %collective-permute-start.14 = (bf16[8,7296]{1,0:T(8,128)(2,1)S(1)}, bf16[8,7296]{1,0:T(8,128)(2,1)S(1)}, u32[]{:S(2)}, u32[]{:S(2)}) collective-permute-start(bf16[8,7296]{1,0:T(8,128)(2,1)S(1)} %get-tuple-element.46.refs_1_.first_ref), channel_id=1, source_target_pairs={{0,1},{1,0},{2,3},{3,2},{4,5},{5,4},{6,7},{7,6},{8,9},{9,8},{10,11... | collective-permute-start | bytes 350216 | tf_op jit(solution)/shard_map/ppermute | solution.py:30
  55.0 6.0 %collective-permute-start.15 = (bf16[8,7296]{1,0:T(8,128)(2,1)S(1)}, bf16[8,7296]{1,0:T(8,128)(2,1)S(1)}, u32[]{:S(2)}, u32[]{:S(2)}) collective-permute-start(bf16[8,7296]{1,0:T(8,128)(2,1)S(1)} %pair_sum.3.refs_1_.near_ref), channel_id=1, source_target_pairs={{0,2},{1,3},{2,0},{3,1},{4,6},{5,7},{6,4},{7,5},{8,10},{9,11},{10,... | collective-permute-start | bytes 350216 | tf_op jit(solution)/shard_map/ppermute | solution.py:30
  63.3 4.7 %collective-permute-start.16 = (bf16[4,2048]{1,0:T(4,128)(2,1)S(1)}, bf16[4,2048]{1,0:T(4,128)(2,1)S(1)}, u32[]{:S(2)}, u32[]{:S(2)}) collective-permute-start(bf16[4,2048]{1,0:T(4,128)(2,1)S(1)} %get-tuple-element.48), channel_id=1, source_target_pairs={{0,8},{4,12},{8,0},{12,4},{1,9},{5,13},{9,1},{13,5},{2,10},{6,14},... | collective-permute-start | bytes 49160 | tf_op jit(solution)/shard_map/ppermute | solution.py:30
  68.0 3.8 %collective-permute-start.17 = (bf16[4,2048]{1,0:T(4,128)(2,1)S(1)}, bf16[4,2048]{1,0:T(4,128)(2,1)S(1)}, u32[]{:S(2)}, u32[]{:S(2)}) collective-permute-start(bf16[4,2048]{1,0:T(4,128)(2,1)S(1)} %pad_maximum_fusion.4), channel_id=1, source_target_pairs={{0,4},{4,0},{8,12},{12,8},{1,5},{5,1},{9,13},{13,9},{2,6},{6,2},{1... | collective-permute-start | bytes 49160 | tf_op jit(solution)/shard_map/ppermute | solution.py:30

commit v5 on v4

--- a/solution.py
+++ b/solution.py
@@ -36,48 +36,34 @@
     return [value] + [got[k] for k in range(1, count)]
 
 
+def scatter_slots(pieces, cross):
+    count = lax.axis_size("tensor")
+    width = lax.axis_size("inner")
+    got = [pieces[0]]
+    for k in range(1, count):
+        pairs = [
+            (t * width + i, (t ^ k) * width + (i ^ cross))
+            for t in range(count)
+            for i in range(width)
+        ]
+        got.append(lax.ppermute(pieces[k], ("tensor", "inner"), pairs))
+    return got
+
+
 def steps_up(count):
     return [1 << n for n in range(count.bit_length() - 1)]
 
 
-def gather_rows(value, axis, beside):
-    for step in steps_up(lax.axis_size(axis)):
-        other = swap_with(value, axis, step)
-        value = beside(step, value)
-        value = jnp.concatenate([value, other], axis=0)
-    return value
-
-
-def scatter_rows(near, far, axis, beside):
-    count = lax.axis_size(axis)
-    rows = (near.shape[0] + far.shape[0]) // count
-    cut = lambda array, n: array[n * rows : (n + 1) * rows]
-    half = count // 2
-    held = [[cut(near, n)] for n in range(half)] + [[cut(far, n)] for n in range(half)]
-    order = [0]
-    step = half
-    while step:
-        if step == half:
-            sent = far
-        else:
-            sent = jnp.concatenate([p for n in range(step, 2 * step) for p in held[n]], axis=0)
-        got = swap_with(sent, axis, step)
-        got = beside(step, got)
-        each = len(held[0])
-        for n in range(step):
-            held[n] = held[n] + [cut(got, n * each + m) for m in range(each)]
-        held = held[:step]
-        order = order + [n ^ step for n in order]
-        step //= 2
-    return [held[0][order.index(n)] for n in range(count)]
-
-
 def params(mib):
     return pltpu.CompilerParams(vmem_limit_bytes=mib * MIB)
 
 
 def resident(weight):
     return pltpu.with_memory_space_constraint(weight, pltpu.VMEM)
+
+
+def in_hbm(weight):
+    return pltpu.with_memory_space_constraint(weight, pltpu.HBM)
 
 
 def tile_of(columns):
@@ -120,22 +106,25 @@
     return spread(three_parts(total), lanes, lax.axis_index("inner") * 4)
 
 
+def copies_of(source, start, target, sems):
+    size = target.shape[0]
+    cuts = COPIES if len(target.shape) > 1 and size % (16 * COPIES) == 0 else 1
+    each = size // cuts
+    return [
+        pltpu.make_async_copy(
+            source.at[pl.ds(start + m * each, each)], target.at[pl.ds(m * each, each)], sems.at[m]
+        )
+        for m in range(cuts)
+    ]
+
+
 def load_kernel(spans, *refs):
     count = len(spans)
     outs = refs[count + 1 : 2 * count + 1]
     sems = refs[-1]
     copies = []
-    for n, (start, size) in enumerate(spans):
-        cuts = COPIES if len(refs[n].shape) > 1 and size % (16 * COPIES) == 0 else 1
-        each = size // cuts
-        for m in range(cuts):
-            copies.append(
-                pltpu.make_async_copy(
-                    refs[n].at[pl.ds(start + m * each, each)],
-                    outs[n].at[pl.ds(m * each, each)],
-                    sems.at[n, m],
-                )
-            )
+    for n, (start, _) in enumerate(spans):
+        copies += copies_of(refs[n], start, outs[n], sems.at[n])
     for copy in copies:
         copy.start()
     for copy in copies:
@@ -156,10 +145,10 @@
         scratch_shapes=[pltpu.SemaphoreType.DMA((len(arrays), COPIES))],
         compiler_params=params(1),
         name="load",
-    )(*[pltpu.with_memory_space_constraint(a, pltpu.HBM) for a in arrays], after)
-
-
-def qkv_kernel(rows_ref, gain_ref, wq_ref, wkv_ref, near_ref, far_ref, out_s):
+    )(*[in_hbm(a) for a in arrays], after)
+
+
+def qkv_kernel(rows_ref, gain_ref, wq_ref, wkv_ref, out_ref):
     wide = rows_ref[...].astype(jnp.float32)
     total = jnp.sum(wide * wide, axis=1, keepdims=True)
     gain = gain_ref[...].astype(jnp.float32)[None, :]
@@ -168,16 +157,13 @@
     kv_cols = wkv_ref.shape[1]
 
     def store_query(start, size, value):
-        out_s[:, pl.ds(start, size)] = value
+        out_ref[:, pl.ds(start, size)] = value.astype(jnp.bfloat16)
 
     product_tiles(scaled, wq_ref, store_query)
-    out_s[:, query_cols : query_cols + kv_cols] = jnp.dot(
+    out_ref[:, query_cols : query_cols + kv_cols] = jnp.dot(
         scaled, wkv_ref[...], preferred_element_type=jnp.float32
-    )
-    out_s[:, query_cols + kv_cols :] = squares_block(total)
-    half = near_ref.shape[0]
-    near_ref[...] = out_s[:half, :].astype(jnp.bfloat16)
-    far_ref[...] = out_s[half:, :].astype(jnp.bfloat16)
+    ).astype(jnp.bfloat16)
+    out_ref[:, query_cols + kv_cols :] = squares_block(total).astype(jnp.bfloat16)
 
 
 def project_qkv(rows, gain, w_query, w_kv):
@@ -185,10 +171,9 @@
     columns = w_query.shape[1] + w_kv.shape[1] + LANES
     return pl.pallas_call(
         qkv_kernel,
-        out_shape=(jax.ShapeDtypeStruct((count // 2, columns), jnp.bfloat16),) * 2,
+        out_shape=jax.ShapeDtypeStruct((count, columns), jnp.bfloat16),
         in_specs=[in_vmem] * 4,
-        out_specs=(in_vmem,) * 2,
-        scratch_shapes=[pltpu.VMEM((count, columns), jnp.float32)],
+        out_specs=in_vmem,
         compiler_params=params(2),
         name="project_qkv",
     )(rows, gain, resident(w_query), resident(w_kv))
@@ -202,10 +187,14 @@
     sine_ref,
     key_ref,
     value_ref,
+    later_ref,
     *refs,
 ):
     parts = refs[:shards]
-    out_ref, query_s, kv_s, kv_wide_s, mixed_s, stats_s = refs[shards:]
+    out_ref, loaded_ref, query_s, kv_s, kv_wide_s, mixed_s, stats_s, sems = refs[shards:]
+    copies = copies_of(later_ref, 0, loaded_ref, sems)
+    for copy in copies:
+        copy.start()
     all_rows = parts[0].shape[0]
     own_rows = all_rows // slots
     here = HEADS // slots
@@ -289,32 +278,37 @@
         ) + spread(three_parts(totals), lanes, 4)
     out_ref[:, :HEAD_DIM] = mixed_s[...].astype(jnp.bfloat16)
     out_ref[:, HEAD_DIM:] = stats_s[...].astype(jnp.bfloat16)
-
-
-def attend(lengths, cosine, sine, parts, keys, values, slots):
+    for copy in copies:
+        copy.wait()
+
+
+def attend(lengths, cosine, sine, parts, keys, values, later, slots):
     own_rows = parts[0].shape[0] // slots
     kv_cols = 2 * KV_HEADS * HEAD_DIM // slots
     return pl.pallas_call(
         functools.partial(attend_kernel, slots, len(parts)),
-        out_shape=jax.ShapeDtypeStruct((own_rows * HEADS, HEAD_DIM + LANES), jnp.bfloat16),
-        in_specs=[in_vmem] * (5 + len(parts)),
-        out_specs=in_vmem,
+        out_shape=(
+            jax.ShapeDtypeStruct((own_rows * HEADS, HEAD_DIM + LANES), jnp.bfloat16),
+            pltpu.VMEM(later.shape, later.dtype),
+        ),
+        in_specs=[in_vmem] * 5 + [in_place] + [in_vmem] * len(parts),
+        out_specs=(in_vmem, in_vmem),
         scratch_shapes=[
             pltpu.VMEM((own_rows * HEADS, HEAD_DIM), jnp.float32),
             pltpu.VMEM((slots, own_rows, kv_cols), jnp.float32),
             pltpu.VMEM((own_rows, slots * kv_cols), jnp.float32),
             pltpu.VMEM((own_rows * HEADS, HEAD_DIM), jnp.float32),
             pltpu.VMEM((own_rows * HEADS, LANES), jnp.float32),
+            pltpu.SemaphoreType.DMA((COPIES,)),
         ],
         compiler_params=params(6),
         name="attend",
-    )(lengths, cosine, sine, resident(keys), resident(values), *parts)
+    )(lengths, cosine, sine, resident(keys), resident(values), in_hbm(later), *parts)
 
 
 def combine_kernel(shards, all_rows, *refs):
     ins = refs[:shards]
-    near_ref, far_ref = refs[-2:]
-    half = all_rows // 2
+    out_ref = refs[-1]
     peaks = []
     totals = []
     for ref in ins:
@@ -331,8 +325,7 @@
     attended = mixed / denominator
     for j in range(attended.shape[0] // all_rows):
         block = attended[j * all_rows : (j + 1) * all_rows]
-        near_ref[:, j * HEAD_DIM : (j + 1) * HEAD_DIM] = block[:half].astype(jnp.bfloat16)
-        far_ref[:, j * HEAD_DIM : (j + 1) * HEAD_DIM] = block[half:].astype(jnp.bfloat16)
+        out_ref[:, j * HEAD_DIM : (j + 1) * HEAD_DIM] = block.astype(jnp.bfloat16)
 
 
 def combine(parts, later, all_rows):
@@ -340,9 +333,9 @@
     columns = parts[0].shape[0] // all_rows * HEAD_DIM
     return pl.pallas_call(
         functools.partial(combine_kernel, count, all_rows),
-        out_shape=(jax.ShapeDtypeStruct((all_rows // 2, columns), jnp.bfloat16),) * 2,
+        out_shape=jax.ShapeDtypeStruct((all_rows, columns), jnp.bfloat16),
         in_specs=[in_vmem] * count + [in_place] * len(later),
-        out_specs=(in_vmem,) * 2,
+        out_specs=in_vmem,
         compiler_params=params(2),
         name="combine",
     )(*parts, *[resident(w) for w in later])
@@ -359,57 +352,60 @@
     )
 
 
-def out_kernel(own_rows, left_ref, weight_ref, later_ref, part_ref, sent_ref):
+def out_kernel(own_rows, left_ref, weight_ref, later_ref, *outs):
     del later_ref
     rows = left_ref.shape[0]
-    left = left_ref[...].astype(jnp.float32)
-    left = jnp.concatenate([left, turned(left, 1, own_rows)], axis=0).astype(jnp.bfloat16)
+    lefts = [left_ref[...].astype(jnp.float32)]
+    for k in range(1, len(outs)):
+        low = k & -k
+        lefts.append(turned(lefts[k ^ low], low, own_rows))
+    left = jnp.concatenate(lefts, axis=0).astype(jnp.bfloat16)
 
     def store(start, size, value):
-        part_ref[:, pl.ds(start, size)] = value[:rows].astype(jnp.bfloat16)
-        sent_ref[:, pl.ds(start, size)] = value[rows:].astype(jnp.bfloat16)
+        for k, ref in enumerate(outs):
+            ref[:, pl.ds(start, size)] = value[k * rows : (k + 1) * rows].astype(jnp.bfloat16)
 
     product_tiles(left, weight_ref, store)
 
 
 def project_out(left, weight, later, own_rows):
-    shape = jax.ShapeDtypeStruct((left.shape[0], weight.shape[1]), jnp.bfloat16)
+    rows = left.shape[0]
+    count = rows // own_rows
+    shape = jax.ShapeDtypeStruct((rows, weight.shape[1]), jnp.bfloat16)
     return pl.pallas_call(
         functools.partial(out_kernel, own_rows),
-        out_shape=(shape, shape),
+        out_shape=(shape,) * count,
         in_specs=[in_vmem, in_vmem, in_place],
-        out_specs=(in_vmem, in_vmem),
+        out_specs=(in_vmem,) * count,
         compiler_params=params(3),
         name="project_out",
     )(left, resident(weight), resident(later))
 
 
-def pair_kernel(step, own_rows, first_ref, second_ref, *refs):
+def pair_kernel(first_ref, second_ref, out_ref):
     total = first_ref[...].astype(jnp.float32) + second_ref[...].astype(jnp.float32)
-    if step is None:
-        refs[-1][...] = total.astype(jnp.bfloat16)
-    else:
-        refs[-2][...] = total.astype(jnp.bfloat16)
-        refs[-1][...] = turned(total, step, own_rows).astype(jnp.bfloat16)
-
-
-def pair_sum(first, second, step=None, own_rows=None, later=()):
-    shape = jax.ShapeDtypeStruct(first.shape, first.dtype)
-    return pl.pallas_call(
-        functools.partial(pair_kernel, step, own_rows),
-        out_shape=shape if step is None else (shape, shape),
-        in_specs=[in_vmem] * 2 + [in_place] * len(later),
-        out_specs=in_vmem if step is None else (in_vmem, in_vmem),
+    out_ref[...] = total.astype(jnp.bfloat16)
+
+
+def pair_sum(first, second):
+    return pl.pallas_call(
+        pair_kernel,
+        out_shape=jax.ShapeDtypeStruct(first.shape, first.dtype),
+        in_specs=[in_vmem] * 2,
+        out_specs=in_vmem,
         compiler_params=params(2),
         name="pair_sum",
-    )(first, second, *[resident(w) for w in later])
-
-
-def gate_up_kernel(
-    rows_ref, gain_ref, first_ref, second_ref, gate_ref, up_ref, out_ref, updated_ref
-):
+    )(first, second)
+
+
+def gate_up_kernel(slots, rows_ref, gain_ref, gate_ref, up_ref, later_ref, *refs):
+    parts = refs[:slots]
+    out_ref, updated_ref, loaded_ref, sems = refs[slots:]
+    copies = copies_of(later_ref, 0, loaded_ref, sems)
+    for copy in copies:
+        copy.start()
     own_rows = updated_ref.shape[0]
-    total = first_ref[...].astype(jnp.float32) + second_ref[...].astype(jnp.float32)
+    total = functools.reduce(jnp.add, [ref[...].astype(jnp.float32) for ref in parts])
     updated = (rows_ref[...].astype(jnp.float32) + total).astype(jnp.bfloat16)
     wide = updated.astype(jnp.float32)
     updated_ref[...] = wide[:own_rows]
@@ -427,24 +423,29 @@
     product_tiles(scaled, gate_ref, store_gate)
     product_tiles(scaled, up_ref, store_up)
     out_ref[:, 2 * hidden :] = squares_block(squares).astype(jnp.bfloat16)
-
-
-def gate_up(rows, gain, first, second, w_gate, w_up, own_rows):
+    for copy in copies:
+        copy.wait()
+
+
+def gate_up(rows, gain, parts, w_gate, w_up, later, cut, own_rows):
     hidden = w_gate.shape[1]
-    return pl.pallas_call(
-        gate_up_kernel,
+    slots = len(parts)
+    return pl.pallas_call(
+        functools.partial(gate_up_kernel, slots),
         out_shape=(
             jax.ShapeDtypeStruct((rows.shape[0], 2 * hidden + LANES), jnp.bfloat16),
             jax.ShapeDtypeStruct((own_rows, rows.shape[1]), jnp.float32),
+            pltpu.VMEM((cut, later.shape[1]), later.dtype),
         ),
-        in_specs=[in_vmem] * 6,
-        out_specs=(in_vmem, in_vmem),
+        in_specs=[in_vmem] * 4 + [in_place] + [in_vmem] * slots,
+        out_specs=(in_vmem,) * 3,
+        scratch_shapes=[pltpu.SemaphoreType.DMA((COPIES,))],
         compiler_params=params(3),
         name="gate_up",
-    )(rows, gain, first, second, resident(w_gate), resident(w_up))
-
-
-def down_kernel(near_ref, far_ref, upper_ref, lower_ref, low_ref, high_ref, hidden_s, out_s):
+    )(rows, gain, resident(w_gate), resident(w_up), in_hbm(later), *parts)
+
+
+def down_kernel(near_ref, far_ref, upper_ref, lower_ref, out_ref, hidden_s):
     hidden = hidden_s.shape[1]
     cut = upper_ref.shape[0]
     squares = jnp.sum(
@@ -466,13 +467,10 @@
     @pl.loop(0, columns // tile)
     def _(step):
         span = pl.ds(pl.multiple_of(step * tile, tile), tile)
-        out_s[:, span] = jnp.dot(
+        total = jnp.dot(
             hidden_s[:, :cut], upper_ref[:, span], preferred_element_type=jnp.float32
         ) + jnp.dot(hidden_s[:, cut:], lower_ref[:, span], preferred_element_type=jnp.float32)
-
-    half = low_ref.shape[0]
-    low_ref[...] = out_s[:half, :].astype(jnp.bfloat16)
-    high_ref[...] = out_s[half:, :].astype(jnp.bfloat16)
+        out_ref[:, span] = total.astype(jnp.bfloat16)
 
 
 def project_down(near, far, upper, lower):
@@ -480,12 +478,11 @@
     columns = upper.shape[1]
     return pl.pallas_call(
         down_kernel,
-        out_shape=(jax.ShapeDtypeStruct((rows // 2, columns), jnp.bfloat16),) * 2,
+        out_shape=jax.ShapeDtypeStruct((rows, columns), jnp.bfloat16),
         in_specs=[in_vmem] * 4,
-        out_specs=(in_vmem,) * 2,
+        out_specs=in_vmem,
         scratch_shapes=[
             pltpu.VMEM((rows, upper.shape[0] + lower.shape[0]), jnp.bfloat16),
-            pltpu.VMEM((rows, columns), jnp.float32),
         ],
         compiler_params=params(3),
         name="project_down",
@@ -523,66 +520,42 @@
     own_rows = states.shape[0]
     all_rows = own_rows * slots
 
-    loaded = {}
-
-    def during_gather(step, value):
-        if step == 1:
-            value, loaded["attn_gain"], loaded["ffn_gain"], loaded["w_kv"] = load(
-                value, attn_gain, ffn_gain, w_kv, after=value
-            )
-        if step == slots // 2:
-            (loaded["w_query"],) = load(w_query, after=value)
-        return value
-
-    rows = gather_rows(states, "tensor", during_gather)
-    near, far = project_qkv(rows, loaded["attn_gain"], loaded["w_query"], loaded["w_kv"])
-    near, lengths = lax.optimization_barrier((near, lengths))
+    cut = lambda array: [array[k * own_rows : (k + 1) * own_rows] for k in range(slots)]
+
+    got = exchange(states, "tensor")
+    own, attn_gain, ffn_gain, w_kv, w_query = load(
+        states, attn_gain, ffn_gain, w_kv, w_query, after=states
+    )
+    rows = jnp.concatenate([own] + got[1:], axis=0)
+    joined = project_qkv(rows, attn_gain, w_query, w_kv)
+
+    joined, lengths = lax.optimization_barrier((joined, lengths))
     my_lengths = lax.dynamic_slice_in_dim(lengths, tensor_index * own_rows, own_rows, 0)
     cosine, sine = rotation_tables(my_lengths.astype(jnp.float32), slots)
     my_lengths = jnp.broadcast_to(my_lengths[:, None], (own_rows, LANES))
     flat = (own_rows, key_cache.shape[1] * KV_HEADS, HEAD_DIM)
-
-    def during_scatter(step, got):
-        if step == slots // 2:
-            (keys,) = load(key_cache.reshape(flat), after=near)
-            got, loaded["keys"] = lax.optimization_barrier((got, keys))
-        if step == 1:
-            (values,) = load(value_cache.reshape(flat), after=loaded["keys"])
-            got, loaded["values"] = lax.optimization_barrier((got, values))
-        return got
-
-    joined = jnp.concatenate(scatter_rows(near, far, "tensor", during_scatter), axis=0)
-    shard = attend(
-        my_lengths,
-        cosine,
-        sine,
-        exchange(joined, "inner"),
-        loaded["keys"],
-        loaded["values"],
-        slots,
-    )
-    (w_out,) = load(w_out, after=shard)
-    near, far = combine(exchange(shard, "inner"), [w_out, w_gate], all_rows)
-
-    alone = lambda step, value: value
-    picked = jnp.concatenate(scatter_rows(near, far, "tensor", alone), axis=0)
-    part, sent = project_out(picked, w_out, w_up, own_rows)
-    steps = steps_up(slots)
-    for step, following in zip(steps, steps[1:] + [None]):
-        other = swap_with(sent, "tensor", step)
-        if following:
-            part, sent = pair_sum(part, other, following, own_rows)
-    joined, updated = gate_up(rows, loaded["ffn_gain"], part, other, w_gate, w_up, own_rows)
+    keys, values = load(key_cache.reshape(flat), value_cache.reshape(flat), after=joined)
+    joined = jnp.concatenate(scatter_slots(cut(joined), 1), axis=0)
+    joined, keys, values = lax.optimization_barrier((joined, keys, values))
+    shard, w_out = attend(
+        my_lengths, cosine, sine, exchange(joined, "inner"), keys, values, w_out, slots
+    )
+    attended = combine(exchange(shard, "inner"), [w_gate], all_rows)
+    picked = jnp.concatenate(scatter_slots(cut(attended), 1), axis=0)
+    parts = project_out(picked, w_out, w_up, own_rows)
+    parts = scatter_slots(parts, 0)
+    first = w_down.shape[0] // 128 * 96
+    joined, updated, upper = gate_up(
+        rows, ffn_gain, parts, w_gate, w_up, w_down, first, own_rows
+    )
 
     steps = steps_up(lax.axis_size("inner"))
-    cut = w_down.shape[0] // 64 * 16
-    (upper,) = load(w_down, after=joined, spans=[(0, cut)])
     for step in steps[:-1]:
-        joined = pair_sum(joined, swap_with(joined, "inner", step), later=[upper])
-    (lower,) = load(w_down, after=joined, spans=[(cut, w_down.shape[0] - cut)])
+        joined = pair_sum(joined, swap_with(joined, "inner", step))
+    (lower,) = load(w_down, after=joined, spans=[(first, w_down.shape[0] - first)])
     other = swap_with(joined, "inner", steps[-1])
-    near, far = project_down(joined, other, upper, lower)
-    parts = scatter_rows(near, far, "tensor", alone)
+    part = project_down(joined, other, upper, lower)
+    parts = scatter_slots(cut(part), 0)
     down_sum = sum(p.astype(jnp.float32) for p in parts)
     return (updated + down_sum).astype(jnp.bfloat16)
 

time: 72.7 us -> 65.5 us (0.901)
  Pallas kernels: 26.2 us -> 19.3 us
  starting transfers between devices: 28.7 us -> 25.7 us
  waiting for transfers between devices: 16 us -> 19 us
    ppermute x18 -> x11, starting transfers between devices: 28.7 us -> 11.7 us  [swap_with(): return lax.ppermute(value, axis, [(i, i ^ step) for i in range(count)])]
    ppermute x0 -> x12, starting transfers between devices: none -> 14 us  [scatter_slots(): got.append(lax.ppermute(pieces[k], ('tensor', 'inner'), pairs))]
    ppermute x0 -> x12, waiting for transfers between devices: none -> 8.29 us  [scatter_slots(): got.append(lax.ppermute(pieces[k], ('tensor', 'inner'), pairs))]
    pallas_call x7 -> x3, Pallas kernels: 15.9 us -> 7.81 us  [load(): pl.pallas_call(functools.partial(load_kernel, spans), out_shape=tuple((pl...]
    ppermute x18 -> x11, waiting for transfers between devices: 16 us -> 10.7 us  [swap_with(): return lax.ppermute(value, axis, [(i, i ^ step) for i in range(count)])]
    pallas_call x1, Pallas kernels: 1.74 us -> 2.82 us  [attend(): pl.pallas_call(functools.partial(attend_kernel, slots, len(parts)), out_s...]
    pallas_call x5 -> x4, Pallas kernels: 7.49 us -> 7.5 us  [the longest x1 4.43 us: gate_up(): pl.pallas_call(functools.partial(gate_up_kernel, slots), out_shape=(jax.S...]
  transfers between devices with their start and end apart: 18 -> 23, of which waited for: 12 -> 15; matrix products, arithmetic and copies ran while one was open for 0% -> 0% of each run, Pallas kernels for 22% -> 12%
where the time goes in v5:
time: 65.5 us; the launch traced here: 65.4 us
  starting transfers between devices  25.7 us (39%)
  Pallas kernels  19.3 us (29%)
  waiting for transfers between devices  19 us (29%)
  other arithmetic  0.92 us (1%)
    ppermute x12, starting transfers between devices, scatter_slots(): got.append(lax.ppermute(pieces[k], ('tensor', 'inner'), pairs))  14 us
    ppermute x11, starting transfers between devices, swap_with(): return lax.ppermute(value, axis, [(i, i ^ step) for i in range(count)])  11.7 us
    ppermute x11, waiting for transfers between devices, swap_with(): return lax.ppermute(value, axis, [(i, i ^ step) for i in range(count)])  10.7 us
    ppermute x12, waiting for transfers between devices, scatter_slots(): got.append(lax.ppermute(pieces[k], ('tensor', 'inner'), pairs))  8.29 us
    pallas_call x3, Pallas kernels, load(): pl.pallas_call(functools.partial(load_kernel, spans), out_shape=tuple((pl...  7.81 us
    pallas_call x1, Pallas kernels, gate_up(): pl.pallas_call(functools.partial(gate_up_kernel, slots), out_shape=(jax.S...  4.43 us
    pallas_call x1, Pallas kernels, attend(): pl.pallas_call(functools.partial(attend_kernel, slots, len(parts)), out_s...  2.82 us
    pallas_call x1, Pallas kernels, project_down(): pl.pallas_call(down_kernel, out_shape=jax.ShapeDtypeStruct((rows, columns...  2.24 us
  transfers between devices with their start and end apart: 23, of which 15 were waited for; matrix products, arithmetic and copies ran while one was open for 0% of the time, Pallas kernels for 12%

profile of v5, /device:TPU:0, one launch (start us, length us, event | category | flops | bytes accessed | tf_op | source)
XLA Modules:
  0.0 65.4 jit_solution(5604820531738992352)
XLA Ops:
  0.0 3.0 %collective-permute-start = (bf16[2,2048]{1,0:T(2,128)(2,1)}, bf16[2,2048]{1,0:T(2,128)(2,1)S(1)}, u32[]{:S(2)}, u32[]{:S(2)}) collective-permute-start(bf16[2,2048]{1,0:T(2,128)(2,1)} %refs_5_.1), channel_id=1, source_target_pairs={{0,4},{4,0},{8,12},{12,8},{1,5},{5,1},{9,13},{13,9},{2,6},{6,2},{1... | collective-permute-start | bytes 24584 | tf_op jit(solution)/shard_map/ppermute | solution.py:30
  3.0 2.5 %collective-permute-start.2 = (bf16[2,2048]{1,0:T(2,128)(2,1)}, bf16[2,2048]{1,0:T(2,128)(2,1)S(1)}, u32[]{:S(2)}, u32[]{:S(2)}) collective-permute-start(bf16[2,2048]{1,0:T(2,128)(2,1)} %refs_5_.1), channel_id=1, source_target_pairs={{0,12},{4,8},{8,4},{12,0},{1,13},{5,9},{9,5},{13,1},{2,14},{6,10},... | collective-permute-start | bytes 24584 | tf_op jit(solution)/shard_map/ppermute | solution.py:30
  5.5 0.1 collective-permute-start.1
  5.6 2.7 %load.3 = (bf16[2,2048]{1,0:T(2,128)(2,1)S(1)}, bf16[2048]{0:T(1024)(128)(2,1)S(1)}, bf16[2048]{0:T(1024)(128)(2,1)S(1)}, bf16[2048,256]{1,0:T(8,128)(2,1)S(1)}, bf16[2048,1024]{1,0:T(8,128)(2,1)S(1)}) custom-call(bf16[2,2048]{1,0:T(2,128)(2,1)} %refs_5_.1, bf16[2048]{0:T(1024)(128)(2,1)} %refs_1_.1, bf16[2048]{0:T(1024)(128)(2,1)} %refs_2_.1, ...), custom_call_target="tpu_custom_call" | custom-call | bytes 5259264 | tf_op jit(solution)/shard_map/load/pallas_call | solution.py:137
  8.4 0.0 collective-permute-done
  8.4 0.4 collective-permute-done.2
  8.8 1.5 %collective-permute-done.1 = bf16[2,2048]{1,0:T(2,128)(2,1)S(1)} collective-permute-done((bf16[2,2048]{1,0:T(2,128)(2,1)}, bf16[2,2048]{1,0:T(2,128)(2,1)S(1)}, u32[]{:S(2)}, u32[]{:S(2)}) %collective-permute-start.1) | collective-permute-done | bytes 8224 | tf_op jit(solution)/shard_map/ppermute | solution.py:30
  10.3 0.0 copy-start
  10.3 0.8 %project_qkv.1.refs_2_ = bf16[8,1408]{1,0:T(8,128)(2,1)S(1)} custom-call(bf16[8,2048]{1,0:T(8,128)(2,1)S(1)} %pad_maximum_fusion.rows_ref, bf16[2048]{0:T(1024)(128)(2,1)S(1)} %get-tuple-element.28.gain_ref, bf16[2048,1024]{1,0:T(8,128)(2,1)S(1)} %get-tuple-element.29.wq_ref, bf16[2048,256]{1,0:T(8,128)(2,1)S(1)} %get-tuple-element.30.wkv_ref), custom_call_target="tpu_custom_call" | custom-call | tf_op jit(solution)/shard_map/project_qkv/pallas_call | solution.py:172
  11.1 0.1 collective-permute-start.5
  11.2 1.8 %collective-permute-start.4 = (bf16[2,1408]{1,0:T(2,128)(2,1)S(1)}, bf16[2,1408]{1,0:T(2,128)(2,1)S(1)}, u32[]{:S(2)}, u32[]{:S(2)}) collective-permute-start(bf16[2,1408]{1,0:T(2,128)(2,1)S(1)} %get-tuple-element.54), channel_id=1, source_target_pairs={{0,9},{1,8},{2,11},{3,10},{4,13},{5,12},{6,15},{7,14},{8,1},{9,0},... | collective-permute-start | bytes 16904 | tf_op jit(solution)/shard_map/ppermute | solution.py:49
  13.1 0.3 collective-permute-start.3
  13.3 0.0 copy-done.3
  13.3 0.1 fusion.4
  13.4 3.0 %load.4 = (bf16[2,4096,128]{2,1,0:T(8,128)(2,1)S(1)}, bf16[2,4096,128]{2,1,0:T(8,128)(2,1)S(1)}) custom-call(bf16[2,4096,128]{2,1,0:T(8,128)(2,1)} %bitcast.6, bf16[2,4096,128]{2,1,0:T(8,128)(2,1)} %bitcast.7, bf16[8,1408]{1,0:T(8,128)(2,1)S(1)} %project_qkv.1.refs_2_), custom_call_target="tpu_custom_call" | custom-call | bytes 4194304 | tf_op jit(solution)/shard_map/load/pallas_call | solution.py:137
  16.5 0.0 collective-permute-done.5
  16.5 0.0 collective-permute-done.4
  16.5 0.0 collective-permute-done.3
  16.5 2.5 %collective-permute-start.8 = (bf16[8,1408]{1,0:T(8,128)(2,1)S(1)}, bf16[8,1408]{1,0:T(8,128)(2,1)S(1)}, u32[]{:S(2)}, u32[]{:S(2)}) collective-permute-start(bf16[8,1408]{1,0:T(8,128)(2,1)S(1)} %pad_maximum_fusion.1.refs_0_), channel_id=1, source_target_pairs={{0,3},{1,2},{2,1},{3,0},{4,7},{5,6},{6,5},{7,4},{8,11},{9,10},{10,... | collective-permute-start | bytes 67592 | tf_op jit(solution)/shard_map/ppermute | solution.py:30
  19.0 0.5 collective-permute-start.7
  19.6 0.0 collective-permute-start.6
  19.6 0.1 fusion
  19.7 0.9 %collective-permute-done.8.refs_3_ = bf16[8,1408]{1,0:T(8,128)(2,1)S(1)} collective-permute-done((bf16[8,1408]{1,0:T(8,128)(2,1)S(1)}, bf16[8,1408]{1,0:T(8,128)(2,1)S(1)}, u32[]{:S(2)}, u32[]{:S(2)}) %collective-permute-start.8) | collective-permute-done | bytes 22560 | tf_op jit(solution)/shard_map/ppermute | solution.py:30
  20.5 2.3 %collective-permute-done.7.refs_2_ = bf16[8,1408]{1,0:T(8,128)(2,1)S(1)} collective-permute-done((bf16[8,1408]{1,0:T(8,128)(2,1)S(1)}, bf16[8,1408]{1,0:T(8,128)(2,1)S(1)}, u32[]{:S(2)}, u32[]{:S(2)}) %collective-permute-start.7) | collective-permute-done | bytes 22560 | tf_op jit(solution)/shard_map/ppermute | solution.py:30
  22.9 0.0 collective-permute-done.6.refs_1_
  22.9 0.1 broadcast_in_dim.10.lengths_ref
  22.9 2.8 %attend.1 = (bf16[64,256]{1,0:T(8,128)(2,1)S(1)}, bf16[1024,2048]{1,0:T(8,128)(2,1)S(1)}) custom-call(s32[2,128]{1,0:T(2,128)S(1)} %broadcast_in_dim.10.lengths_ref, f32[8,128]{1,0:T(8,128)S(1)} %bitcast.5, f32[8,128]{1,0:T(8,128)S(1)} %bitcast.4, bf16[2,4096,128]{2,1,0:T(8,128)(2,1)S(1)} %get-tuple-element.35.key_ref, ...), custom_call_target="tpu_custom_call" | custom-call | tf_op jit(solution)/shard_map/attend/pallas_call | solution.py:288
  25.8 0.0 copy-start.1
  25.8 0.1 collective-permute-start.11
  25.8 0.6 collective-permute-start.10
  26.4 1.2 %collective-permute-start.9 = (bf16[64,256]{1,0:T(8,128)(2,1)S(1)}, bf16[64,256]{1,0:T(8,128)(2,1)S(1)}, u32[]{:S(2)}, u32[]{:S(2)}) collective-permute-start(bf16[64,256]{1,0:T(8,128)(2,1)S(1)} %get-tuple-element.38.refs_0_), channel_id=1, source_target_pairs={{0,1},{1,0},{2,3},{3,2},{4,5},{5,4},{6,7},{7,6},{8,9},{9,8},{10,11... | collective-permute-start | bytes 98312 | tf_op jit(solution)/shard_map/ppermute | solution.py:30
  27.7 1.5 %collective-permute-done.11.refs_3_ = bf16[64,256]{1,0:T(8,128)(2,1)S(1)} collective-permute-done((bf16[64,256]{1,0:T(8,128)(2,1)S(1)}, bf16[64,256]{1,0:T(8,128)(2,1)S(1)}, u32[]{:S(2)}, u32[]{:S(2)}) %collective-permute-start.11) | collective-permute-done | bytes 32800 | tf_op jit(solution)/shard_map/ppermute | solution.py:30
  29.2 0.7 %collective-permute-done.10.refs_2_ = bf16[64,256]{1,0:T(8,128)(2,1)S(1)} collective-permute-done((bf16[64,256]{1,0:T(8,128)(2,1)S(1)}, bf16[64,256]{1,0:T(8,128)(2,1)S(1)}, u32[]{:S(2)}, u32[]{:S(2)}) %collective-permute-start.10) | collective-permute-done | bytes 32800 | tf_op jit(solution)/shard_map/ppermute | solution.py:30
  29.9 0.0 collective-permute-done.9.refs_1_
  29.9 0.3 combine.1
  30.2 0.9 %collective-permute-start.14 = (bf16[2,1024]{1,0:T(2,128)(2,1)S(1)}, bf16[2,1024]{1,0:T(2,128)(2,1)S(1)}, u32[]{:S(2)}, u32[]{:S(2)}) collective-permute-start(bf16[2,1024]{1,0:T(2,128)(2,1)S(1)} %get-tuple-element.57), channel_id=1, source_target_pairs={{0,13},{1,12},{2,15},{3,14},{4,9},{5,8},{6,11},{7,10},{8,5},{9,4},... | collective-permute-start | bytes 12296 | tf_op jit(solution)/shard_map/ppermute | solution.py:49
  31.0 0.6 collective-permute-start.13
  31.6 2.2 %collective-permute-start.12 = (bf16[2,1024]{1,0:T(2,128)(2,1)S(1)}, bf16[2,1024]{1,0:T(2,128)(2,1)S(1)}, u32[]{:S(2)}, u32[]{:S(2)}) collective-permute-start(bf16[2,1024]{1,0:T(2,128)(2,1)S(1)} %get-tuple-element.59), channel_id=1, source_target_pairs={{0,5},{1,4},{2,7},{3,6},{4,1},{5,0},{6,3},{7,2},{8,13},{9,12},{10,... | collective-permute-start | bytes 12296 | tf_op jit(solution)/shard_map/ppermute | solution.py:49
  33.8 1.3 %collective-permute-done.14 = bf16[2,1024]{1,0:T(2,128)(2,1)S(1)} collective-permute-done((bf16[2,1024]{1,0:T(2,128)(2,1)S(1)}, bf16[2,1024]{1,0:T(2,128)(2,1)S(1)}, u32[]{:S(2)}, u32[]{:S(2)}) %collective-permute-start.14) | collective-permute-done | bytes 4128 | tf_op jit(solution)/shard_map/ppermute | solution.py:49
  35.1 0.0 collective-permute-done.13
  35.1 0.1 collective-permute-done.12
  35.2 0.0 copy-done.1
  35.2 0.0 copy-start.2
  35.2 0.9 %project_out.1 = (bf16[8,2048]{1,0:T(8,128)(2,1)S(1)}, bf16[8,2048]{1,0:T(8,128)(2,1)S(1)}, bf16[8,2048]{1,0:T(8,128)(2,1)S(1)}, bf16[8,2048]{1,0:T(8,128)(2,1)S(1)}) custom-call(bf16[8,1024]{1,0:T(8,128)(2,1)S(1)} %pad_maximum_fusion.2.left_ref, bf16[1024,2048]{1,0:T(8,128)(2,1)S(1)} %get-tuple-element.39.weight_ref, bf16[2048,3584]{1,0:T(8,128)(2,1)S(1)} %copy-done.1), custom_call_target="tpu_custom_call" | custom-call | tf_op jit(solution)/shard_map/project_out/pallas_call | solution.py:375
  36.1 2.2 %collective-permute-start.15 = (bf16[8,2048]{1,0:T(8,128)(2,1)S(1)}, bf16[8,2048]{1,0:T(8,128)(2,1)S(1)}, u32[]{:S(2)}, u32[]{:S(2)}) collective-permute-start(bf16[8,2048]{1,0:T(8,128)(2,1)S(1)} %get-tuple-element.41), channel_id=1, source_target_pairs={{0,4},{1,5},{2,6},{3,7},{4,0},{5,1},{6,2},{7,3},{8,12},{9,13},{10,... | collective-permute-start | bytes 98312 | tf_op jit(solution)/shard_map/ppermute | solution.py:49
  38.4 0.7 %collective-permute-start.16 = (bf16[8,2048]{1,0:T(8,128)(2,1)S(1)}, bf16[8,2048]{1,0:T(8,128)(2,1)S(1)}, u32[]{:S(2)}, u32[]{:S(2)}) collective-permute-start(bf16[8,2048]{1,0:T(8,128)(2,1)S(1)} %get-tuple-element.42), channel_id=1, source_target_pairs={{0,8},{1,9},{2,10},{3,11},{4,12},{5,13},{6,14},{7,15},{8,0},{9,1},... | collective-permute-start | bytes 98312 | tf_op jit(solution)/shard_map/ppermute | solution.py:49
  39.0 1.8 %collective-permute-start.17 = (bf16[8,2048]{1,0:T(8,128)(2,1)S(1)}, bf16[8,2048]{1,0:T(8,128)(2,1)S(1)}, u32[]{:S(2)}, u32[]{:S(2)}) collective-permute-start(bf16[8,2048]{1,0:T(8,128)(2,1)S(1)} %get-tuple-element.43), channel_id=1, source_target_pairs={{0,12},{1,13},{2,14},{3,15},{4,8},{5,9},{6,10},{7,11},{8,4},{9,5},... | collective-permute-start | bytes 98312 | tf_op jit(solution)/shard_map/ppermute | solution.py:49
  40.8 0.0 collective-permute-done.15.refs_1_
  40.8 2.5 %collective-permute-done.16.refs_2_ = bf16[8,2048]{1,0:T(8,128)(2,1)S(1)} collective-permute-done((bf16[8,2048]{1,0:T(8,128)(2,1)S(1)}, bf16[8,2048]{1,0:T(8,128)(2,1)S(1)}, u32[]{:S(2)}, u32[]{:S(2)}) %collective-permute-start.16) | collective-permute-done | bytes 32800 | tf_op jit(solution)/shard_map/ppermute | solution.py:49
  43.4 1.4 %collective-permute-done.17.refs_3_ = bf16[8,2048]{1,0:T(8,128)(2,1)S(1)} collective-permute-done((bf16[8,2048]{1,0:T(8,128)(2,1)S(1)}, bf16[8,2048]{1,0:T(8,128)(2,1)S(1)}, u32[]{:S(2)}, u32[]{:S(2)}) %collective-permute-start.17) | collective-permute-done | bytes 32800 | tf_op jit(solution)/shard_map/ppermute | solution.py:49
  44.8 4.4 %gate_up.1 = (bf16[8,7296]{1,0:T(8,128)(2,1)S(1)}, f32[2,2048]{1,0:T(2,128)S(1)}, bf16[2688,2048]{1,0:T(8,128)(2,1)S(1)}) custom-call(bf16[8,2048]{1,0:T(8,128)(2,1)S(1)} %pad_maximum_fusion.rows_ref, bf16[2048]{0:T(1024)(128)(2,1)S(1)} %get-tuple-element.27.gain_ref, bf16[2048,3584]{1,0:T(8,128)(2,1)S(1)} %copy-done, bf16[2048,3584]{1,0:T(8,128)(2,1)S(1)} %copy-done.2, ...), custom_call_target="tpu_custom_call" | custom-call | tf_op jit(solution)/shard_map/gate_up/pallas_call | solution.py:433
  49.2 0.1 collective-permute-start.18
  49.3 1.3 %collective-permute-done.18.second_ref = bf16[8,7296]{1,0:T(8,128)(2,1)S(1)} collective-permute-done((bf16[8,7296]{1,0:T(8,128)(2,1)S(1)}, bf16[8,7296]{1,0:T(8,128)(2,1)S(1)}, u32[]{:S(2)}, u32[]{:S(2)}) %collective-permute-start.18) | collective-permute-done | bytes 116768 | tf_op jit(solution)/shard_map/ppermute | solution.py:30
  50.6 1.1 %collective-permute-start.19 = (bf16[8,7296]{1,0:T(8,128)(2,1)S(1)}, bf16[8,7296]{1,0:T(8,128)(2,1)S(1)}, u32[]{:S(2)}, u32[]{:S(2)}) collective-permute-start(bf16[8,7296]{1,0:T(8,128)(2,1)S(1)} %pair_sum.1.refs_1_.near_ref), channel_id=1, source_target_pairs={{0,2},{1,3},{2,0},{3,1},{4,6},{5,7},{6,4},{7,5},{8,10},{9,11},{10,... | collective-permute-start | bytes 350216 | tf_op jit(solution)/shard_map/ppermute | solution.py:30
  51.7 2.0 %load.5.lower_ref = bf16[896,2048]{1,0:T(8,128)(2,1)S(1)} custom-call(bf16[3584,2048]{1,0:T(8,128)(2,1)} %refs_0_.3, bf16[8,7296]{1,0:T(8,128)(2,1)S(1)} %pair_sum.1.refs_1_.near_ref), custom_call_target="tpu_custom_call" | custom-call | bytes 3670016 | tf_op jit(solution)/shard_map/load/pallas_call | solution.py:137
  53.7 2.2 %collective-permute-done.19.far_ref = bf16[8,7296]{1,0:T(8,128)(2,1)S(1)} collective-permute-done((bf16[8,7296]{1,0:T(8,128)(2,1)S(1)}, bf16[8,7296]{1,0:T(8,128)(2,1)S(1)}, u32[]{:S(2)}, u32[]{:S(2)}) %collective-permute-start.19) | collective-permute-done | bytes 116768 | tf_op jit(solution)/shard_map/ppermute | solution.py:30
  55.9 2.2 %project_down.1 = bf16[8,2048]{1,0:T(8,128)(2,1)S(1)} custom-call(bf16[8,7296]{1,0:T(8,128)(2,1)S(1)} %pair_sum.1.refs_1_.near_ref, bf16[8,7296]{1,0:T(8,128)(2,1)S(1)} %collective-permute-done.19.far_ref, bf16[2688,2048]{1,0:T(8,128)(2,1)S(1)} %get-tuple-element.46.upper_ref, bf16[896,2048]{1,0:T(8,128)(2,1)S(1)} %load.5.lower_ref), custom_call_target="tpu_custom_call" | custom-call | tf_op jit(solution)/shard_map/project_down/pallas_call | solution.py:479
  58.2 0.1 collective-permute-start.20
  58.3 1.9 %collective-permute-start.22 = (bf16[2,2048]{1,0:T(2,128)(2,1)S(1)}, bf16[2,2048]{1,0:T(2,128)(2,1)S(1)}, u32[]{:S(2)}, u32[]{:S(2)}) collective-permute-start(bf16[2,2048]{1,0:T(2,128)(2,1)S(1)} %get-tuple-element.50), channel_id=1, source_target_pairs={{0,12},{1,13},{2,14},{3,15},{4,8},{5,9},{6,10},{7,11},{8,4},{9,5},... | collective-permute-start | bytes 24584 | tf_op jit(solution)/shard_map/ppermute | solution.py:49
  60.2 1.6 %collective-permute-start.21 = (bf16[2,2048]{1,0:T(2,128)(2,1)S(1)}, bf16[2,2048]{1,0:T(2,128)(2,1)S(1)}, u32[]{:S(2)}, u32[]{:S(2)}) collective-permute-start(bf16[2,2048]{1,0:T(2,128)(2,1)S(1)} %get-tuple-element.51), channel_id=1, source_target_pairs={{0,8},{1,9},{2,10},{3,11},{4,12},{5,13},{6,14},{7,15},{8,0},{9,1},... | collective-permute-start | bytes 24584 | tf_op jit(solution)/shard_map/ppermute | solution.py:49
  61.8 0.2 collective-permute-done.20
  61.9 1.9 %collective-permute-done.22 = bf16[2,2048]{1,0:T(2,128)(2,1)S(1)} collective-permute-done((bf16[2,2048]{1,0:T(2,128)(2,1)S(1)}, bf16[2,2048]{1,0:T(2,128)(2,1)S(1)}, u32[]{:S(2)}, u32[]{:S(2)}) %collective-permute-start.22) | collective-permute-done | bytes 8224 | tf_op jit(solution)/shard_map/ppermute | solution.py:49
  63.8 1.0 %collective-permute-done.21 = bf16[2,2048]{1,0:T(2,128)(2,1)S(1)} collective-permute-done((bf16[2,2048]{1,0:T(2,128)(2,1)S(1)}, bf16[2,2048]{1,0:T(2,128)(2,1)S(1)}, u32[]{:S(2)}, u32[]{:S(2)}) %collective-permute-start.21) | collective-permute-done | bytes 8224 | tf_op jit(solution)/shard_map/ppermute | solution.py:49
  64.8 0.6 add_convert_fusion
  (13 shorter events, 0.2 us)
Async XLA Ops:
  0.0 8.4 %collective-permute-start = (bf16[2,2048]{1,0:T(2,128)(2,1)}, bf16[2,2048]{1,0:T(2,128)(2,1)S(1)}, u32[]{:S(2)}, u32[]{:S(2)}) collective-permute-start(bf16[2,2048]{1,0:T(2,128)(2,1)} %refs_5_.1), channel_id=1, source_target_pairs={{0,4},{4,0},{8,12},{12,8},{1,5},{5,1},{9,13},{13,9},{2,6},{6,2},{1... | collective-permute-start | bytes 24584 | tf_op jit(solution)/shard_map/ppermute | solution.py:30
  3.0 5.7 %collective-permute-start.2 = (bf16[2,2048]{1,0:T(2,128)(2,1)}, bf16[2,2048]{1,0:T(2,128)(2,1)S(1)}, u32[]{:S(2)}, u32[]{:S(2)}) collective-permute-start(bf16[2,2048]{1,0:T(2,128)(2,1)} %refs_5_.1), channel_id=1, source_target_pairs={{0,12},{4,8},{8,4},{12,0},{1,13},{5,9},{9,5},{13,1},{2,14},{6,10},... | collective-permute-start | bytes 24584 | tf_op jit(solution)/shard_map/ppermute | solution.py:30
  5.5 4.8 %collective-permute-start.1 = (bf16[2,2048]{1,0:T(2,128)(2,1)}, bf16[2,2048]{1,0:T(2,128)(2,1)S(1)}, u32[]{:S(2)}, u32[]{:S(2)}) collective-permute-start(bf16[2,2048]{1,0:T(2,128)(2,1)} %refs_5_.1), channel_id=1, source_target_pairs={{0,8},{4,12},{8,0},{12,4},{1,9},{5,13},{9,1},{13,5},{2,10},{6,14},... | collective-permute-start | bytes 24584 | tf_op jit(solution)/shard_map/ppermute | solution.py:30
  5.6 7.7 %copy-start.3 = (s32[8]{0:T(128)S(1)}, s32[8]{0:T(128)}, u32[]{:S(2)}) copy-start(s32[8]{0:T(128)} %param.23) | copy-start | bytes 100
  10.3 19.6 %copy-start = (bf16[2048,3584]{1,0:T(8,128)(2,1)S(1)}, bf16[2048,3584]{1,0:T(8,128)(2,1)}, u32[]{:S(2)}) copy-start(bf16[2048,3584]{1,0:T(8,128)(2,1)} %gate_ref.1) | copy-start | bytes 44040196
  11.1 5.3 %collective-permute-start.5 = (bf16[2,1408]{1,0:T(2,128)(2,1)S(1)}, bf16[2,1408]{1,0:T(2,128)(2,1)S(1)}, u32[]{:S(2)}, u32[]{:S(2)}) collective-permute-start(bf16[2,1408]{1,0:T(2,128)(2,1)S(1)} %get-tuple-element.53), channel_id=1, source_target_pairs={{0,13},{1,12},{2,15},{3,14},{4,9},{5,8},{6,11},{7,10},{8,5},{9,4},... | collective-permute-start | bytes 16904 | tf_op jit(solution)/shard_map/ppermute | solution.py:49
  11.2 5.3 %collective-permute-start.4 = (bf16[2,1408]{1,0:T(2,128)(2,1)S(1)}, bf16[2,1408]{1,0:T(2,128)(2,1)S(1)}, u32[]{:S(2)}, u32[]{:S(2)}) collective-permute-start(bf16[2,1408]{1,0:T(2,128)(2,1)S(1)} %get-tuple-element.54), channel_id=1, source_target_pairs={{0,9},{1,8},{2,11},{3,10},{4,13},{5,12},{6,15},{7,14},{8,1},{9,0},... | collective-permute-start | bytes 16904 | tf_op jit(solution)/shard_map/ppermute | solution.py:49
  13.1 3.4 %collective-permute-start.3 = (bf16[2,1408]{1,0:T(2,128)(2,1)S(1)}, bf16[2,1408]{1,0:T(2,128)(2,1)S(1)}, u32[]{:S(2)}, u32[]{:S(2)}) collective-permute-start(bf16[2,1408]{1,0:T(2,128)(2,1)S(1)} %get-tuple-element.55), channel_id=1, source_target_pairs={{0,5},{1,4},{2,7},{3,6},{4,1},{5,0},{6,3},{7,2},{8,13},{9,12},{10,... | collective-permute-start | bytes 16904 | tf_op jit(solution)/shard_map/ppermute | solution.py:49
  16.5 4.0 %collective-permute-start.8 = (bf16[8,1408]{1,0:T(8,128)(2,1)S(1)}, bf16[8,1408]{1,0:T(8,128)(2,1)S(1)}, u32[]{:S(2)}, u32[]{:S(2)}) collective-permute-start(bf16[8,1408]{1,0:T(8,128)(2,1)S(1)} %pad_maximum_fusion.1.refs_0_), channel_id=1, source_target_pairs={{0,3},{1,2},{2,1},{3,0},{4,7},{5,6},{6,5},{7,4},{8,11},{9,10},{10,... | collective-permute-start | bytes 67592 | tf_op jit(solution)/shard_map/ppermute | solution.py:30
  19.0 3.8 %collective-permute-start.7 = (bf16[8,1408]{1,0:T(8,128)(2,1)S(1)}, bf16[8,1408]{1,0:T(8,128)(2,1)S(1)}, u32[]{:S(2)}, u32[]{:S(2)}) collective-permute-start(bf16[8,1408]{1,0:T(8,128)(2,1)S(1)} %pad_maximum_fusion.1.refs_0_), channel_id=1, source_target_pairs={{0,2},{1,3},{2,0},{3,1},{4,6},{5,7},{6,4},{7,5},{8,10},{9,11},{10,... | collective-permute-start | bytes 67592 | tf_op jit(solution)/shard_map/ppermute | solution.py:30
  19.6 3.3 %collective-permute-start.6 = (bf16[8,1408]{1,0:T(8,128)(2,1)S(1)}, bf16[8,1408]{1,0:T(8,128)(2,1)S(1)}, u32[]{:S(2)}, u32[]{:S(2)}) collective-permute-start(bf16[8,1408]{1,0:T(8,128)(2,1)S(1)} %pad_maximum_fusion.1.refs_0_), channel_id=1, source_target_pairs={{0,1},{1,0},{2,3},{3,2},{4,5},{5,4},{6,7},{7,6},{8,9},{9,8},{10,11... | collective-permute-start | bytes 67592 | tf_op jit(solution)/shard_map/ppermute | solution.py:30
  25.8 9.4 %copy-start.1 = (bf16[2048,3584]{1,0:T(8,128)(2,1)S(1)}, bf16[2048,3584]{1,0:T(8,128)(2,1)}, u32[]{:S(2)}) copy-start(bf16[2048,3584]{1,0:T(8,128)(2,1)} %up_ref.1) | copy-start | bytes 44040196
  25.8 3.4 %collective-permute-start.11 = (bf16[64,256]{1,0:T(8,128)(2,1)S(1)}, bf16[64,256]{1,0:T(8,128)(2,1)S(1)}, u32[]{:S(2)}, u32[]{:S(2)}) collective-permute-start(bf16[64,256]{1,0:T(8,128)(2,1)S(1)} %get-tuple-element.38.refs_0_), channel_id=1, source_target_pairs={{0,3},{1,2},{2,1},{3,0},{4,7},{5,6},{6,5},{7,4},{8,11},{9,10},{10,... | collective-permute-start | bytes 98312 | tf_op jit(solution)/shard_map/ppermute | solution.py:30
  25.8 4.0 %collective-permute-start.10 = (bf16[64,256]{1,0:T(8,128)(2,1)S(1)}, bf16[64,256]{1,0:T(8,128)(2,1)S(1)}, u32[]{:S(2)}, u32[]{:S(2)}) collective-permute-start(bf16[64,256]{1,0:T(8,128)(2,1)S(1)} %get-tuple-element.38.refs_0_), channel_id=1, source_target_pairs={{0,2},{1,3},{2,0},{3,1},{4,6},{5,7},{6,4},{7,5},{8,10},{9,11},{10,... | collective-permute-start | bytes 98312 | tf_op jit(solution)/shard_map/ppermute | solution.py:30
  26.4 3.4 %collective-permute-start.9 = (bf16[64,256]{1,0:T(8,128)(2,1)S(1)}, bf16[64,256]{1,0:T(8,128)(2,1)S(1)}, u32[]{:S(2)}, u32[]{:S(2)}) collective-permute-start(bf16[64,256]{1,0:T(8,128)(2,1)S(1)} %get-tuple-element.38.refs_0_), channel_id=1, source_target_pairs={{0,1},{1,0},{2,3},{3,2},{4,5},{5,4},{6,7},{7,6},{8,9},{9,8},{10,11... | collective-permute-start | bytes 98312 | tf_op jit(solution)/shard_map/ppermute | solution.py:30
  30.2 4.9 %collective-permute-start.14 = (bf16[2,1024]{1,0:T(2,128)(2,1)S(1)}, bf16[2,1024]{1,0:T(2,128)(2,1)S(1)}, u32[]{:S(2)}, u32[]{:S(2)}) collective-permute-start(bf16[2,1024]{1,0:T(2,128)(2,1)S(1)} %get-tuple-element.57), channel_id=1, source_target_pairs={{0,13},{1,12},{2,15},{3,14},{4,9},{5,8},{6,11},{7,10},{8,5},{9,4},... | collective-permute-start | bytes 12296 | tf_op jit(solution)/shard_map/ppermute | solution.py:49
  31.0 4.0 %collective-permute-start.13 = (bf16[2,1024]{1,0:T(2,128)(2,1)S(1)}, bf16[2,1024]{1,0:T(2,128)(2,1)S(1)}, u32[]{:S(2)}, u32[]{:S(2)}) collective-permute-start(bf16[2,1024]{1,0:T(2,128)(2,1)S(1)} %get-tuple-element.58), channel_id=1, source_target_pairs={{0,9},{1,8},{2,11},{3,10},{4,13},{5,12},{6,15},{7,14},{8,1},{9,0},... | collective-permute-start | bytes 12296 | tf_op jit(solution)/shard_map/ppermute | solution.py:49
  31.6 3.5 %collective-permute-start.12 = (bf16[2,1024]{1,0:T(2,128)(2,1)S(1)}, bf16[2,1024]{1,0:T(2,128)(2,1)S(1)}, u32[]{:S(2)}, u32[]{:S(2)}) collective-permute-start(bf16[2,1024]{1,0:T(2,128)(2,1)S(1)} %get-tuple-element.59), channel_id=1, source_target_pairs={{0,5},{1,4},{2,7},{3,6},{4,1},{5,0},{6,3},{7,2},{8,13},{9,12},{10,... | collective-permute-start | bytes 12296 | tf_op jit(solution)/shard_map/ppermute | solution.py:49
  35.2 9.6 %copy-start.2 = (bf16[2048,3584]{1,0:T(8,128)(2,1)S(1)}, bf16[2048,3584]{1,0:T(8,128)(2,1)}, u32[]{:S(2)}) copy-start(bf16[2048,3584]{1,0:T(8,128)(2,1)} %up_ref.1) | copy-start | bytes 44040196
  36.1 4.7 %collective-permute-start.15 = (bf16[8,2048]{1,0:T(8,128)(2,1)S(1)}, bf16[8,2048]{1,0:T(8,128)(2,1)S(1)}, u32[]{:S(2)}, u32[]{:S(2)}) collective-permute-start(bf16[8,2048]{1,0:T(8,128)(2,1)S(1)} %get-tuple-element.41), channel_id=1, source_target_pairs={{0,4},{1,5},{2,6},{3,7},{4,0},{5,1},{6,2},{7,3},{8,12},{9,13},{10,... | collective-permute-start | bytes 98312 | tf_op jit(solution)/shard_map/ppermute | solution.py:49
  38.4 5.0 %collective-permute-start.16 = (bf16[8,2048]{1,0:T(8,128)(2,1)S(1)}, bf16[8,2048]{1,0:T(8,128)(2,1)S(1)}, u32[]{:S(2)}, u32[]{:S(2)}) collective-permute-start(bf16[8,2048]{1,0:T(8,128)(2,1)S(1)} %get-tuple-element.42), channel_id=1, source_target_pairs={{0,8},{1,9},{2,10},{3,11},{4,12},{5,13},{6,14},{7,15},{8,0},{9,1},... | collective-permute-start | bytes 98312 | tf_op jit(solution)/shard_map/ppermute | solution.py:49
  39.0 5.7 %collective-permute-start.17 = (bf16[8,2048]{1,0:T(8,128)(2,1)S(1)}, bf16[8,2048]{1,0:T(8,128)(2,1)S(1)}, u32[]{:S(2)}, u32[]{:S(2)}) collective-permute-start(bf16[8,2048]{1,0:T(8,128)(2,1)S(1)} %get-tuple-element.43), channel_id=1, source_target_pairs={{0,12},{1,13},{2,14},{3,15},{4,8},{5,9},{6,10},{7,11},{8,4},{9,5},... | collective-permute-start | bytes 98312 | tf_op jit(solution)/shard_map/ppermute | solution.py:49
  49.2 1.4 %collective-permute-start.18 = (bf16[8,7296]{1,0:T(8,128)(2,1)S(1)}, bf16[8,7296]{1,0:T(8,128)(2,1)S(1)}, u32[]{:S(2)}, u32[]{:S(2)}) collective-permute-start(bf16[8,7296]{1,0:T(8,128)(2,1)S(1)} %get-tuple-element.45.first_ref), channel_id=1, source_target_pairs={{0,1},{1,0},{2,3},{3,2},{4,5},{5,4},{6,7},{7,6},{8,9},{9,8},{10,11... | collective-permute-start | bytes 350216 | tf_op jit(solution)/shard_map/ppermute | solution.py:30
  50.6 5.3 %collective-permute-start.19 = (bf16[8,7296]{1,0:T(8,128)(2,1)S(1)}, bf16[8,7296]{1,0:T(8,128)(2,1)S(1)}, u32[]{:S(2)}, u32[]{:S(2)}) collective-permute-start(bf16[8,7296]{1,0:T(8,128)(2,1)S(1)} %pair_sum.1.refs_1_.near_ref), channel_id=1, source_target_pairs={{0,2},{1,3},{2,0},{3,1},{4,6},{5,7},{6,4},{7,5},{8,10},{9,11},{10,... | collective-permute-start | bytes 350216 | tf_op jit(solution)/shard_map/ppermute | solution.py:30
  58.2 3.7 %collective-permute-start.20 = (bf16[2,2048]{1,0:T(2,128)(2,1)S(1)}, bf16[2,2048]{1,0:T(2,128)(2,1)S(1)}, u32[]{:S(2)}, u32[]{:S(2)}) collective-permute-start(bf16[2,2048]{1,0:T(2,128)(2,1)S(1)} %get-tuple-element.49), channel_id=1, source_target_pairs={{0,4},{1,5},{2,6},{3,7},{4,0},{5,1},{6,2},{7,3},{8,12},{9,13},{10,... | collective-permute-start | bytes 24584 | tf_op jit(solution)/shard_map/ppermute | solution.py:49
  58.3 5.5 %collective-permute-start.22 = (bf16[2,2048]{1,0:T(2,128)(2,1)S(1)}, bf16[2,2048]{1,0:T(2,128)(2,1)S(1)}, u32[]{:S(2)}, u32[]{:S(2)}) collective-permute-start(bf16[2,2048]{1,0:T(2,128)(2,1)S(1)} %get-tuple-element.50), channel_id=1, source_target_pairs={{0,12},{1,13},{2,14},{3,15},{4,8},{5,9},{6,10},{7,11},{8,4},{9,5},... | collective-permute-start | bytes 24584 | tf_op jit(solution)/shard_map/ppermute | solution.py:49
  60.2 4.5 %collective-permute-start.21 = (bf16[2,2048]{1,0:T(2,128)(2,1)S(1)}, bf16[2,2048]{1,0:T(2,128)(2,1)S(1)}, u32[]{:S(2)}, u32[]{:S(2)}) collective-permute-start(bf16[2,2048]{1,0:T(2,128)(2,1)S(1)} %get-tuple-element.51), channel_id=1, source_target_pairs={{0,8},{1,9},{2,10},{3,11},{4,12},{5,13},{6,14},{7,15},{8,0},{9,1},... | collective-permute-start | bytes 24584 | tf_op jit(solution)/shard_map/ppermute | solution.py:49

commit v6 on v5

--- a/solution.py
+++ b/solution.py
@@ -66,6 +66,12 @@
     return pltpu.with_memory_space_constraint(weight, pltpu.HBM)
 
 
+def product_cost(depth, columns):
+    return pl.CostEstimate(
+        flops=16 * depth * columns, bytes_accessed=2 * depth * columns, transcendentals=0
+    )
+
+
 def tile_of(columns):
     for tile in (1792, 1024, 896, 512, 256, 128):
         if columns % tile == 0:
@@ -73,17 +79,18 @@
     return columns
 
 
-def product_tiles(left, weight_ref, store):
-    columns = weight_ref.shape[1]
+def product_tiles(left, weight_ref, store, first=0, columns=None):
+    columns = columns or weight_ref.shape[1]
     tile = tile_of(columns)
 
     @pl.loop(0, columns // tile)
     def _(step):
         start = pl.multiple_of(step * tile, tile)
+        span = pl.ds(pl.multiple_of(first + start, math.gcd(first, tile)), tile)
         store(
             start,
             tile,
-            jnp.dot(left, weight_ref[:, pl.ds(start, tile)], preferred_element_type=jnp.float32),
+            jnp.dot(left, weight_ref[:, span], preferred_element_type=jnp.float32),
         )
 
 
@@ -187,14 +194,10 @@
     sine_ref,
     key_ref,
     value_ref,
-    later_ref,
     *refs,
 ):
     parts = refs[:shards]
-    out_ref, loaded_ref, query_s, kv_s, kv_wide_s, mixed_s, stats_s, sems = refs[shards:]
-    copies = copies_of(later_ref, 0, loaded_ref, sems)
-    for copy in copies:
-        copy.start()
+    out_ref, query_s, kv_s, kv_wide_s, mixed_s, stats_s = refs[shards:]
     all_rows = parts[0].shape[0]
     own_rows = all_rows // slots
     here = HEADS // slots
@@ -278,32 +281,26 @@
         ) + spread(three_parts(totals), lanes, 4)
     out_ref[:, :HEAD_DIM] = mixed_s[...].astype(jnp.bfloat16)
     out_ref[:, HEAD_DIM:] = stats_s[...].astype(jnp.bfloat16)
-    for copy in copies:
-        copy.wait()
-
-
-def attend(lengths, cosine, sine, parts, keys, values, later, slots):
+
+
+def attend(lengths, cosine, sine, parts, keys, values, slots):
     own_rows = parts[0].shape[0] // slots
     kv_cols = 2 * KV_HEADS * HEAD_DIM // slots
     return pl.pallas_call(
         functools.partial(attend_kernel, slots, len(parts)),
-        out_shape=(
-            jax.ShapeDtypeStruct((own_rows * HEADS, HEAD_DIM + LANES), jnp.bfloat16),
-            pltpu.VMEM(later.shape, later.dtype),
-        ),
-        in_specs=[in_vmem] * 5 + [in_place] + [in_vmem] * len(parts),
-        out_specs=(in_vmem, in_vmem),
+        out_shape=jax.ShapeDtypeStruct((own_rows * HEADS, HEAD_DIM + LANES), jnp.bfloat16),
+        in_specs=[in_vmem] * (5 + len(parts)),
+        out_specs=in_vmem,
         scratch_shapes=[
             pltpu.VMEM((own_rows * HEADS, HEAD_DIM), jnp.float32),
             pltpu.VMEM((slots, own_rows, kv_cols), jnp.float32),
             pltpu.VMEM((own_rows, slots * kv_cols), jnp.float32),
             pltpu.VMEM((own_rows * HEADS, HEAD_DIM), jnp.float32),
             pltpu.VMEM((own_rows * HEADS, LANES), jnp.float32),
-            pltpu.SemaphoreType.DMA((COPIES,)),
         ],
         compiler_params=params(6),
         name="attend",
-    )(lengths, cosine, sine, resident(keys), resident(values), in_hbm(later), *parts)
+    )(lengths, cosine, sine, resident(keys), resident(values), *parts)
 
 
 def combine_kernel(shards, all_rows, *refs):
@@ -398,9 +395,21 @@
     )(first, second)
 
 
-def gate_up_kernel(slots, rows_ref, gain_ref, gate_ref, up_ref, later_ref, *refs):
+def gate_up_tiles(scaled, gate_ref, up_ref, out_ref, first, count):
+    def store(offset):
+        def place(start, size, value):
+            start = pl.multiple_of(offset + start, math.gcd(offset, size))
+            out_ref[:, pl.ds(start, size)] = value.astype(jnp.bfloat16)
+
+        return place
+
+    product_tiles(scaled, gate_ref, store(0), first, count)
+    product_tiles(scaled, up_ref, store(count), first, count)
+
+
+def first_gate_up_kernel(slots, count, rows_ref, gain_ref, gate_ref, up_ref, later_ref, *refs):
     parts = refs[:slots]
-    out_ref, updated_ref, loaded_ref, sems = refs[slots:]
+    out_ref, updated_ref, scaled_ref, loaded_ref, sems = refs[slots:]
     copies = copies_of(later_ref, 0, loaded_ref, sems)
     for copy in copies:
         copy.start()
@@ -410,83 +419,122 @@
     wide = updated.astype(jnp.float32)
     updated_ref[...] = wide[:own_rows]
     squares = jnp.sum(wide * wide, axis=1, keepdims=True)
+    out_ref[:, 2 * count :] = squares_block(squares).astype(jnp.bfloat16)
     scaled = (wide * gain_ref[...].astype(jnp.float32)[None, :]).astype(jnp.bfloat16)
-    hidden = gate_ref.shape[1]
-
-    def store_gate(start, size, value):
-        out_ref[:, pl.ds(start, size)] = value.astype(jnp.bfloat16)
-
-    def store_up(start, size, value):
-        place = pl.multiple_of(start + hidden, math.gcd(hidden, size))
-        out_ref[:, pl.ds(place, size)] = value.astype(jnp.bfloat16)
-
-    product_tiles(scaled, gate_ref, store_gate)
-    product_tiles(scaled, up_ref, store_up)
-    out_ref[:, 2 * hidden :] = squares_block(squares).astype(jnp.bfloat16)
+    scaled_ref[...] = scaled
+    gate_up_tiles(scaled, gate_ref, up_ref, out_ref, 0, count)
     for copy in copies:
         copy.wait()
 
 
-def gate_up(rows, gain, parts, w_gate, w_up, later, cut, own_rows):
-    hidden = w_gate.shape[1]
+def first_gate_up(rows, gain, parts, w_gate, w_up, w_down, count, own_rows):
     slots = len(parts)
     return pl.pallas_call(
-        functools.partial(gate_up_kernel, slots),
+        functools.partial(first_gate_up_kernel, slots, count),
         out_shape=(
-            jax.ShapeDtypeStruct((rows.shape[0], 2 * hidden + LANES), jnp.bfloat16),
+            jax.ShapeDtypeStruct((rows.shape[0], 2 * count + LANES), jnp.bfloat16),
             jax.ShapeDtypeStruct((own_rows, rows.shape[1]), jnp.float32),
-            pltpu.VMEM((cut, later.shape[1]), later.dtype),
+            jax.ShapeDtypeStruct(rows.shape, jnp.bfloat16),
+            pltpu.VMEM((count, w_down.shape[1]), w_down.dtype),
         ),
         in_specs=[in_vmem] * 4 + [in_place] + [in_vmem] * slots,
-        out_specs=(in_vmem,) * 3,
+        out_specs=(in_vmem,) * 4,
         scratch_shapes=[pltpu.SemaphoreType.DMA((COPIES,))],
         compiler_params=params(3),
-        name="gate_up",
-    )(rows, gain, resident(w_gate), resident(w_up), in_hbm(later), *parts)
-
-
-def down_kernel(near_ref, far_ref, upper_ref, lower_ref, out_ref, hidden_s):
-    hidden = hidden_s.shape[1]
-    cut = upper_ref.shape[0]
+        cost_estimate=product_cost(w_gate.shape[0], 2 * count),
+        name="first_gate_up",
+    )(rows, gain, resident(w_gate), resident(w_up), in_hbm(w_down), *parts)
+
+
+def second_gate_up_kernel(
+    first, scaled_ref, gate_ref, up_ref, later_ref, out_ref, loaded_ref, sems
+):
+    copies = copies_of(later_ref, first, loaded_ref, sems)
+    for copy in copies:
+        copy.start()
+    count = loaded_ref.shape[0]
+    gate_up_tiles(scaled_ref[...], gate_ref, up_ref, out_ref, first, count)
+    for copy in copies:
+        copy.wait()
+
+
+def second_gate_up(scaled, w_gate, w_up, w_down, first):
+    count = w_down.shape[0] - first
+    return pl.pallas_call(
+        functools.partial(second_gate_up_kernel, first),
+        out_shape=(
+            jax.ShapeDtypeStruct((scaled.shape[0], 2 * count), jnp.bfloat16),
+            pltpu.VMEM((count, w_down.shape[1]), w_down.dtype),
+        ),
+        in_specs=[in_vmem] * 3 + [in_place],
+        out_specs=(in_vmem,) * 2,
+        scratch_shapes=[pltpu.SemaphoreType.DMA((COPIES,))],
+        compiler_params=params(3),
+        cost_estimate=product_cost(w_gate.shape[0], 2 * count),
+        name="second_gate_up",
+    )(scaled, resident(w_gate), resident(w_up), in_hbm(w_down))
+
+
+def hidden_of(near_ref, far_ref, scale, count):
+    def total(start):
+        span = slice(start, start + count)
+        return (near_ref[:, span].astype(jnp.float32) + far_ref[:, span].astype(jnp.float32)) * scale
+
+    gate = total(0)
+    return (gate / (1.0 + jnp.exp(-gate)) * total(count)).astype(jnp.bfloat16)
+
+
+def first_down_kernel(near_ref, far_ref, weight_ref, out_ref, scale_ref):
+    count = weight_ref.shape[0]
     squares = jnp.sum(
-        near_ref[:, 2 * hidden :].astype(jnp.float32) + far_ref[:, 2 * hidden :].astype(jnp.float32),
+        near_ref[:, 2 * count :].astype(jnp.float32) + far_ref[:, 2 * count :].astype(jnp.float32),
         axis=1,
         keepdims=True,
     )
     scale = lax.rsqrt(squares / D + epsilon)
-    gate = near_ref[:, :hidden].astype(jnp.float32) + far_ref[:, :hidden].astype(jnp.float32)
-    up = (
-        near_ref[:, hidden : 2 * hidden].astype(jnp.float32)
-        + far_ref[:, hidden : 2 * hidden].astype(jnp.float32)
-    )
-    gate = gate * scale
-    hidden_s[...] = (gate / (1.0 + jnp.exp(-gate)) * (up * scale)).astype(jnp.bfloat16)
-    columns = upper_ref.shape[1]
-    tile = tile_of(columns)
-
-    @pl.loop(0, columns // tile)
-    def _(step):
-        span = pl.ds(pl.multiple_of(step * tile, tile), tile)
-        total = jnp.dot(
-            hidden_s[:, :cut], upper_ref[:, span], preferred_element_type=jnp.float32
-        ) + jnp.dot(hidden_s[:, cut:], lower_ref[:, span], preferred_element_type=jnp.float32)
-        out_ref[:, span] = total.astype(jnp.bfloat16)
-
-
-def project_down(near, far, upper, lower):
+    scale_ref[...] = jnp.broadcast_to(scale, scale_ref.shape)
+
+    def store(start, size, value):
+        out_ref[:, pl.ds(start, size)] = value
+
+    product_tiles(hidden_of(near_ref, far_ref, scale, count), weight_ref, store)
+
+
+def first_down(near, far, weight):
     rows = near.shape[0]
-    columns = upper.shape[1]
-    return pl.pallas_call(
-        down_kernel,
-        out_shape=jax.ShapeDtypeStruct((rows, columns), jnp.bfloat16),
-        in_specs=[in_vmem] * 4,
+    return pl.pallas_call(
+        first_down_kernel,
+        out_shape=(
+            jax.ShapeDtypeStruct((rows, weight.shape[1]), jnp.float32),
+            jax.ShapeDtypeStruct((rows, LANES), jnp.float32),
+        ),
+        in_specs=[in_vmem] * 3,
+        out_specs=(in_vmem,) * 2,
+        compiler_params=params(3),
+        cost_estimate=product_cost(*weight.shape),
+        name="first_down",
+    )(near, far, resident(weight))
+
+
+def second_down_kernel(near_ref, far_ref, weight_ref, part_ref, scale_ref, out_ref):
+    count = weight_ref.shape[0]
+
+    def store(start, size, value):
+        span = pl.ds(start, size)
+        out_ref[:, span] = (part_ref[:, span] + value).astype(jnp.bfloat16)
+
+    product_tiles(hidden_of(near_ref, far_ref, scale_ref[:, 0:1], count), weight_ref, store)
+
+
+def second_down(near, far, weight, part, scale):
+    return pl.pallas_call(
+        second_down_kernel,
+        out_shape=jax.ShapeDtypeStruct(part.shape, jnp.bfloat16),
+        in_specs=[in_vmem] * 5,
         out_specs=in_vmem,
-        scratch_shapes=[
-            pltpu.VMEM((rows, upper.shape[0] + lower.shape[0]), jnp.bfloat16),
-        ],
         compiler_params=params(3),
-        name="project_down",
-    )(near, far, resident(upper), resident(lower))
+        name="second_down",
+    )(near, far, resident(weight), part, scale)
 
 
 def rotation_tables(positions, repeats):
@@ -536,25 +584,27 @@
     flat = (own_rows, key_cache.shape[1] * KV_HEADS, HEAD_DIM)
     keys, values = load(key_cache.reshape(flat), value_cache.reshape(flat), after=joined)
     joined = jnp.concatenate(scatter_slots(cut(joined), 1), axis=0)
-    joined, keys, values = lax.optimization_barrier((joined, keys, values))
-    shard, w_out = attend(
-        my_lengths, cosine, sine, exchange(joined, "inner"), keys, values, w_out, slots
-    )
+    joined, keys, values, w_gate = lax.optimization_barrier((joined, keys, values, w_gate))
+    (w_out,) = load(w_out, after=joined)
+    parts, w_out = lax.optimization_barrier((exchange(joined, "inner"), w_out))
+    shard = attend(my_lengths, cosine, sine, parts, keys, values, slots)
+
     attended = combine(exchange(shard, "inner"), [w_gate], all_rows)
     picked = jnp.concatenate(scatter_slots(cut(attended), 1), axis=0)
-    parts = project_out(picked, w_out, w_up, own_rows)
-    parts = scatter_slots(parts, 0)
-    first = w_down.shape[0] // 128 * 96
-    joined, updated, upper = gate_up(
+    parts = scatter_slots(project_out(picked, w_out, w_up, own_rows), 0)
+
+    tiles = w_gate.shape[1] // LANES
+    first = (tiles + 1) // 2 * LANES
+    one, updated, scaled, upper = first_gate_up(
         rows, ffn_gain, parts, w_gate, w_up, w_down, first, own_rows
     )
-
+    two, lower = second_gate_up(scaled, w_gate, w_up, w_down, first)
     steps = steps_up(lax.axis_size("inner"))
     for step in steps[:-1]:
-        joined = pair_sum(joined, swap_with(joined, "inner", step))
-    (lower,) = load(w_down, after=joined, spans=[(first, w_down.shape[0] - first)])
-    other = swap_with(joined, "inner", steps[-1])
-    part = project_down(joined, other, upper, lower)
+        one = pair_sum(one, swap_with(one, "inner", step))
+        two = pair_sum(two, swap_with(two, "inner", step))
+    part, scale = first_down(one, swap_with(one, "inner", steps[-1]), upper)
+    part = second_down(two, swap_with(two, "inner", steps[-1]), lower, part, scale)
     parts = scatter_slots(cut(part), 0)
     down_sum = sum(p.astype(jnp.float32) for p in parts)
     return (updated + down_sum).astype(jnp.bfloat16)

time: 65.5 us -> 67.1 us (1.024)
  Pallas kernels: 19.3 us -> 20.6 us
  starting transfers between devices: 25.7 us -> 26.7 us
    pallas_call x2 -> x4, Pallas kernels: 6.67 us -> 9.42 us  [the longest x1 3.59 us: first_gate_up(): pl.pallas_call(functools.partial(first_gate_up_kernel, slots, count), out...]
    ppermute x11 -> x13, starting transfers between devices: 11.7 us -> 13.7 us  [swap_with(): return lax.ppermute(value, axis, [(i, i ^ step) for i in range(count)])]
    ppermute x11 -> x13, waiting for transfers between devices: 10.7 us -> 8.79 us  [swap_with(): return lax.ppermute(value, axis, [(i, i ^ step) for i in range(count)])]
    ppermute x12, waiting for transfers between devices: 8.29 us -> 9.64 us  [scatter_slots(): got.append(lax.ppermute(pieces[k], ('tensor', 'inner'), pairs))]
    ppermute x12, starting transfers between devices: 14 us -> 12.9 us  [scatter_slots(): got.append(lax.ppermute(pieces[k], ('tensor', 'inner'), pairs))]
    pallas_call x1, Pallas kernels: 2.82 us -> 1.74 us  [attend(): pl.pallas_call(functools.partial(attend_kernel, slots, len(parts)), out_s...]
  transfers between devices with their start and end apart: 23 -> 25, of which waited for: 15 -> 15; matrix products, arithmetic and copies ran while one was open for 0% -> 0% of each run, Pallas kernels for 12% -> 18%
where the time goes in v6:
time: 67.1 us; the launch traced here: 66.9 us
  starting transfers between devices  26.7 us (40%)
  Pallas kernels  20.6 us (31%)
  waiting for transfers between devices  18.4 us (27%)
  other arithmetic  0.91 us (1%)
    ppermute x13, starting transfers between devices, swap_with(): return lax.ppermute(value, axis, [(i, i ^ step) for i in range(count)])  13.7 us
    ppermute x12, starting transfers between devices, scatter_slots(): got.append(lax.ppermute(pieces[k], ('tensor', 'inner'), pairs))  12.9 us
    ppermute x12, waiting for transfers between devices, scatter_slots(): got.append(lax.ppermute(pieces[k], ('tensor', 'inner'), pairs))  9.64 us
    ppermute x13, waiting for transfers between devices, swap_with(): return lax.ppermute(value, axis, [(i, i ^ step) for i in range(count)])  8.79 us
    pallas_call x3, Pallas kernels, load(): pl.pallas_call(functools.partial(load_kernel, spans), out_shape=tuple((pl...  7.38 us
    pallas_call x1, Pallas kernels, first_gate_up(): pl.pallas_call(functools.partial(first_gate_up_kernel, slots, count), out...  3.59 us
    pallas_call x1, Pallas kernels, second_gate_up(): pl.pallas_call(functools.partial(second_gate_up_kernel, first), out_shape...  3.25 us
    pallas_call x1, Pallas kernels, attend(): pl.pallas_call(functools.partial(attend_kernel, slots, len(parts)), out_s...  1.74 us
  transfers between devices with their start and end apart: 25, of which 15 were waited for; matrix products, arithmetic and copies ran while one was open for 0% of the time, Pallas kernels for 18%

profile of v6, /device:TPU:0, one launch (start us, length us, event | category | flops | bytes accessed | tf_op | source)
XLA Modules:
  0.0 66.9 jit_solution(11726282970923096991)
XLA Ops:
  0.0 3.0 %collective-permute-start = (bf16[2,2048]{1,0:T(2,128)(2,1)}, bf16[2,2048]{1,0:T(2,128)(2,1)S(1)}, u32[]{:S(2)}, u32[]{:S(2)}) collective-permute-start(bf16[2,2048]{1,0:T(2,128)(2,1)} %refs_5_.1), channel_id=1, source_target_pairs={{0,4},{4,0},{8,12},{12,8},{1,5},{5,1},{9,13},{13,9},{2,6},{6,2},{1... | collective-permute-start | bytes 24584 | tf_op jit(solution)/shard_map/ppermute | solution.py:30
  3.0 2.5 %collective-permute-start.2 = (bf16[2,2048]{1,0:T(2,128)(2,1)}, bf16[2,2048]{1,0:T(2,128)(2,1)S(1)}, u32[]{:S(2)}, u32[]{:S(2)}) collective-permute-start(bf16[2,2048]{1,0:T(2,128)(2,1)} %refs_5_.1), channel_id=1, source_target_pairs={{0,12},{4,8},{8,4},{12,0},{1,13},{5,9},{9,5},{13,1},{2,14},{6,10},... | collective-permute-start | bytes 24584 | tf_op jit(solution)/shard_map/ppermute | solution.py:30
  5.5 0.1 collective-permute-start.1
  5.6 2.7 %load.3 = (bf16[2,2048]{1,0:T(2,128)(2,1)S(1)}, bf16[2048]{0:T(1024)(128)(2,1)S(1)}, bf16[2048]{0:T(1024)(128)(2,1)S(1)}, bf16[2048,256]{1,0:T(8,128)(2,1)S(1)}, bf16[2048,1024]{1,0:T(8,128)(2,1)S(1)}) custom-call(bf16[2,2048]{1,0:T(2,128)(2,1)} %refs_5_.1, bf16[2048]{0:T(1024)(128)(2,1)} %refs_1_.1, bf16[2048]{0:T(1024)(128)(2,1)} %refs_2_.1, ...), custom_call_target="tpu_custom_call" | custom-call | bytes 5259264 | tf_op jit(solution)/shard_map/load/pallas_call | solution.py:144
  8.4 0.0 collective-permute-done
  8.4 0.4 collective-permute-done.2
  8.8 1.5 %collective-permute-done.1 = bf16[2,2048]{1,0:T(2,128)(2,1)S(1)} collective-permute-done((bf16[2,2048]{1,0:T(2,128)(2,1)}, bf16[2,2048]{1,0:T(2,128)(2,1)S(1)}, u32[]{:S(2)}, u32[]{:S(2)}) %collective-permute-start.1) | collective-permute-done | bytes 8224 | tf_op jit(solution)/shard_map/ppermute | solution.py:30
  10.3 0.8 %project_qkv.1.refs_2_ = bf16[8,1408]{1,0:T(8,128)(2,1)S(1)} custom-call(bf16[8,2048]{1,0:T(8,128)(2,1)S(1)} %pad_maximum_fusion.rows_ref, bf16[2048]{0:T(1024)(128)(2,1)S(1)} %get-tuple-element.37.gain_ref, bf16[2048,1024]{1,0:T(8,128)(2,1)S(1)} %get-tuple-element.38.wq_ref, bf16[2048,256]{1,0:T(8,128)(2,1)S(1)} %get-tuple-element.39.wkv_ref), custom_call_target="tpu_custom_call" | custom-call | tf_op jit(solution)/shard_map/project_qkv/pallas_call | solution.py:179
  11.1 0.1 collective-permute-start.5
  11.2 1.8 %collective-permute-start.4 = (bf16[2,1408]{1,0:T(2,128)(2,1)S(1)}, bf16[2,1408]{1,0:T(2,128)(2,1)S(1)}, u32[]{:S(2)}, u32[]{:S(2)}) collective-permute-start(bf16[2,1408]{1,0:T(2,128)(2,1)S(1)} %get-tuple-element.72), channel_id=1, source_target_pairs={{0,9},{1,8},{2,11},{3,10},{4,13},{5,12},{6,15},{7,14},{8,1},{9,0},... | collective-permute-start | bytes 16904 | tf_op jit(solution)/shard_map/ppermute | solution.py:49
  13.1 0.3 collective-permute-start.3
  13.3 0.1 fusion.4
  13.4 2.4 %load.4 = (bf16[2,4096,128]{2,1,0:T(8,128)(2,1)S(1)}, bf16[2,4096,128]{2,1,0:T(8,128)(2,1)S(1)}) custom-call(bf16[2,4096,128]{2,1,0:T(8,128)(2,1)} %bitcast.6, bf16[2,4096,128]{2,1,0:T(8,128)(2,1)} %bitcast.7, bf16[8,1408]{1,0:T(8,128)(2,1)S(1)} %project_qkv.1.refs_2_), custom_call_target="tpu_custom_call" | custom-call | bytes 4194304 | tf_op jit(solution)/shard_map/load/pallas_call | solution.py:144
  15.9 0.2 collective-permute-done.5
  16.0 0.0 collective-permute-done.4
  16.0 0.1 collective-permute-done.3
  16.1 3.0 %collective-permute-start.8 = (bf16[8,1408]{1,0:T(8,128)(2,1)S(1)}, bf16[8,1408]{1,0:T(8,128)(2,1)S(1)}, u32[]{:S(2)}, u32[]{:S(2)}) collective-permute-start(bf16[8,1408]{1,0:T(8,128)(2,1)S(1)} %pad_maximum_fusion.1.refs_1_.refs_0_), channel_id=1, source_target_pairs={{0,3},{1,2},{2,1},{3,0},{4,7},{5,6},{6,5},{7,4},{8,11},{9,10},{10,... | collective-permute-start | bytes 67592 | tf_op jit(solution)/shard_map/ppermute | solution.py:30
  19.2 0.5 collective-permute-start.7
  19.7 0.0 collective-permute-start.6
  19.7 0.1 fusion
  19.8 2.2 %load.5.weight_ref = bf16[1024,2048]{1,0:T(8,128)(2,1)S(1)} custom-call(bf16[1024,2048]{1,0:T(8,128)(2,1)} %refs_0_.3, bf16[8,1408]{1,0:T(8,128)(2,1)S(1)} %pad_maximum_fusion.1.refs_1_.refs_0_), custom_call_target="tpu_custom_call" | custom-call | bytes 4194304 | tf_op jit(solution)/shard_map/load/pallas_call | solution.py:144
  22.1 0.0 collective-permute-done.8.refs_3_
  22.1 0.9 %collective-permute-done.7.refs_2_ = bf16[8,1408]{1,0:T(8,128)(2,1)S(1)} collective-permute-done((bf16[8,1408]{1,0:T(8,128)(2,1)S(1)}, bf16[8,1408]{1,0:T(8,128)(2,1)S(1)}, u32[]{:S(2)}, u32[]{:S(2)}) %collective-permute-start.7) | collective-permute-done | bytes 22560 | tf_op jit(solution)/shard_map/ppermute | solution.py:30
  23.0 0.0 collective-permute-done.6.refs_1_
  23.0 0.1 broadcast_in_dim.10.lengths_ref
  23.1 1.7 %attend.1.refs_0_ = bf16[64,256]{1,0:T(8,128)(2,1)S(1)} custom-call(s32[2,128]{1,0:T(2,128)S(1)} %broadcast_in_dim.10.lengths_ref, f32[8,128]{1,0:T(8,128)S(1)} %bitcast.5, f32[8,128]{1,0:T(8,128)S(1)} %bitcast.4, bf16[2,4096,128]{2,1,0:T(8,128)(2,1)S(1)} %get-tuple-element.45.key_ref, bf16[2,4096,128]{2,1,0:T(8,128)(2,1)S(1)} %get-tuple-element.46.value_ref, ...), custom_call_target="tpu_custom_call" | custom-call | tf_op jit(solution)/shard_map/attend/pallas_call | solution.py:289
  24.8 0.0 copy-start.1
  24.8 1.3 %collective-permute-start.11 = (bf16[64,256]{1,0:T(8,128)(2,1)S(1)}, bf16[64,256]{1,0:T(8,128)(2,1)S(1)}, u32[]{:S(2)}, u32[]{:S(2)}) collective-permute-start(bf16[64,256]{1,0:T(8,128)(2,1)S(1)} %attend.1.refs_0_), channel_id=1, source_target_pairs={{0,3},{1,2},{2,1},{3,0},{4,7},{5,6},{6,5},{7,4},{8,11},{9,10},{10,... | collective-permute-start | bytes 98312 | tf_op jit(solution)/shard_map/ppermute | solution.py:30
  26.2 0.5 collective-permute-start.10
  26.7 0.0 collective-permute-start.9
  26.8 1.5 %collective-permute-done.11.refs_3_ = bf16[64,256]{1,0:T(8,128)(2,1)S(1)} collective-permute-done((bf16[64,256]{1,0:T(8,128)(2,1)S(1)}, bf16[64,256]{1,0:T(8,128)(2,1)S(1)}, u32[]{:S(2)}, u32[]{:S(2)}) %collective-permute-start.11) | collective-permute-done | bytes 32800 | tf_op jit(solution)/shard_map/ppermute | solution.py:30
  28.2 1.9 %collective-permute-done.10.refs_2_ = bf16[64,256]{1,0:T(8,128)(2,1)S(1)} collective-permute-done((bf16[64,256]{1,0:T(8,128)(2,1)S(1)}, bf16[64,256]{1,0:T(8,128)(2,1)S(1)}, u32[]{:S(2)}, u32[]{:S(2)}) %collective-permute-start.10) | collective-permute-done | bytes 32800 | tf_op jit(solution)/shard_map/ppermute | solution.py:30
  30.1 0.3 combine.1
  30.4 0.1 collective-permute-start.14
  30.5 0.9 %collective-permute-start.13 = (bf16[2,1024]{1,0:T(2,128)(2,1)S(1)}, bf16[2,1024]{1,0:T(2,128)(2,1)S(1)}, u32[]{:S(2)}, u32[]{:S(2)}) collective-permute-start(bf16[2,1024]{1,0:T(2,128)(2,1)S(1)} %get-tuple-element.76), channel_id=1, source_target_pairs={{0,9},{1,8},{2,11},{3,10},{4,13},{5,12},{6,15},{7,14},{8,1},{9,0},... | collective-permute-start | bytes 12296 | tf_op jit(solution)/shard_map/ppermute | solution.py:49
  31.4 1.4 %collective-permute-start.12 = (bf16[2,1024]{1,0:T(2,128)(2,1)S(1)}, bf16[2,1024]{1,0:T(2,128)(2,1)S(1)}, u32[]{:S(2)}, u32[]{:S(2)}) collective-permute-start(bf16[2,1024]{1,0:T(2,128)(2,1)S(1)} %get-tuple-element.77), channel_id=1, source_target_pairs={{0,5},{1,4},{2,7},{3,6},{4,1},{5,0},{6,3},{7,2},{8,13},{9,12},{10,... | collective-permute-start | bytes 12296 | tf_op jit(solution)/shard_map/ppermute | solution.py:49
  32.8 2.5 %collective-permute-done.14 = bf16[2,1024]{1,0:T(2,128)(2,1)S(1)} collective-permute-done((bf16[2,1024]{1,0:T(2,128)(2,1)S(1)}, bf16[2,1024]{1,0:T(2,128)(2,1)S(1)}, u32[]{:S(2)}, u32[]{:S(2)}) %collective-permute-start.14) | collective-permute-done | bytes 4128 | tf_op jit(solution)/shard_map/ppermute | solution.py:49
  35.3 0.0 collective-permute-done.12
  35.3 0.0 copy-start.2
  35.3 0.9 %project_out.1 = (bf16[8,2048]{1,0:T(8,128)(2,1)S(1)}, bf16[8,2048]{1,0:T(8,128)(2,1)S(1)}, bf16[8,2048]{1,0:T(8,128)(2,1)S(1)}, bf16[8,2048]{1,0:T(8,128)(2,1)S(1)}) custom-call(bf16[8,1024]{1,0:T(8,128)(2,1)S(1)} %pad_maximum_fusion.2.left_ref, bf16[1024,2048]{1,0:T(8,128)(2,1)S(1)} %load.5.weight_ref, bf16[2048,3584]{1,0:T(8,128)(2,1)S(1)} %copy-done.1), custom_call_target="tpu_custom_call" | custom-call | tf_op jit(solution)/shard_map/project_out/pallas_call | solution.py:372
  36.3 2.3 %collective-permute-start.15 = (bf16[8,2048]{1,0:T(8,128)(2,1)S(1)}, bf16[8,2048]{1,0:T(8,128)(2,1)S(1)}, u32[]{:S(2)}, u32[]{:S(2)}) collective-permute-start(bf16[8,2048]{1,0:T(8,128)(2,1)S(1)} %get-tuple-element.54), channel_id=1, source_target_pairs={{0,4},{1,5},{2,6},{3,7},{4,0},{5,1},{6,2},{7,3},{8,12},{9,13},{10,... | collective-permute-start | bytes 98312 | tf_op jit(solution)/shard_map/ppermute | solution.py:49
  38.6 0.0 collective-permute-start.16
  38.6 2.4 %collective-permute-start.17 = (bf16[8,2048]{1,0:T(8,128)(2,1)S(1)}, bf16[8,2048]{1,0:T(8,128)(2,1)S(1)}, u32[]{:S(2)}, u32[]{:S(2)}) collective-permute-start(bf16[8,2048]{1,0:T(8,128)(2,1)S(1)} %get-tuple-element.56), channel_id=1, source_target_pairs={{0,12},{1,13},{2,14},{3,15},{4,8},{5,9},{6,10},{7,11},{8,4},{9,5},... | collective-permute-start | bytes 98312 | tf_op jit(solution)/shard_map/ppermute | solution.py:49
  41.0 2.4 %collective-permute-done.16.refs_2_ = bf16[8,2048]{1,0:T(8,128)(2,1)S(1)} collective-permute-done((bf16[8,2048]{1,0:T(8,128)(2,1)S(1)}, bf16[8,2048]{1,0:T(8,128)(2,1)S(1)}, u32[]{:S(2)}, u32[]{:S(2)}) %collective-permute-start.16) | collective-permute-done | bytes 32800 | tf_op jit(solution)/shard_map/ppermute | solution.py:49
  43.4 1.1 %collective-permute-done.17.refs_3_ = bf16[8,2048]{1,0:T(8,128)(2,1)S(1)} collective-permute-done((bf16[8,2048]{1,0:T(8,128)(2,1)S(1)}, bf16[8,2048]{1,0:T(8,128)(2,1)S(1)}, u32[]{:S(2)}, u32[]{:S(2)}) %collective-permute-start.17) | collective-permute-done | bytes 32800 | tf_op jit(solution)/shard_map/ppermute | solution.py:49
  44.5 3.6 %first_gate_up.1 = (bf16[8,3712]{1,0:T(8,128)(2,1)S(1)}, f32[2,2048]{1,0:T(2,128)S(1)}, bf16[8,2048]{1,0:T(8,128)(2,1)S(1)}, bf16[1792,2048]{1,0:T(8,128)(2,1)S(1)}) custom-call(bf16[8,2048]{1,0:T(8,128)(2,1)S(1)} %pad_maximum_fusion.rows_ref, bf16[2048]{0:T(1024)(128)(2,1)S(1)} %get-tuple-element.36.gain_ref, bf16[2048,3584]{1,0:T(8,128)(2,1)S(1)} %copy-done, ...), custom_call_target="tpu_custom_call" | custom-call | flops 117440512 | bytes 14680064 | tf_op jit(solution)/shard_map/first_gate_up/pallas_call | solution.py:432
  48.1 0.1 collective-permute-start.20
  48.2 3.3 %second_gate_up.1 = (bf16[8,3584]{1,0:T(8,128)(2,1)S(1)}, bf16[1792,2048]{1,0:T(8,128)(2,1)S(1)}) custom-call(bf16[8,2048]{1,0:T(8,128)(2,1)S(1)} %get-tuple-element.58.scaled_ref, bf16[2048,3584]{1,0:T(8,128)(2,1)S(1)} %copy-done, bf16[2048,3584]{1,0:T(8,128)(2,1)S(1)} %copy-done.2, bf16[3584,2048]{1,0:T(8,128)(2,1)} %later_ref.5), custom_call_target="tpu_custom_call" | custom-call | flops 117440512 | bytes 14680064 | tf_op jit(solution)/shard_map/second_gate_up/pallas_call | solution.py:463
  51.5 0.6 collective-permute-start.18
  52.0 0.0 collective-permute-done.20.second_ref
  52.1 0.7 %collective-permute-start.21 = (bf16[8,3712]{1,0:T(8,128)(2,1)S(1)}, bf16[8,3712]{1,0:T(8,128)(2,1)S(1)}, u32[]{:S(2)}, u32[]{:S(2)}) collective-permute-start(bf16[8,3712]{1,0:T(8,128)(2,1)S(1)} %pair_sum.3.near_ref), channel_id=1, source_target_pairs={{0,2},{1,3},{2,0},{3,1},{4,6},{5,7},{6,4},{7,5},{8,10},{9,11},{10,... | collective-permute-start | bytes 178184 | tf_op jit(solution)/shard_map/ppermute | solution.py:30
  52.8 0.2 collective-permute-done.18.second_ref
  52.9 1.3 %collective-permute-start.19 = (bf16[8,3584]{1,0:T(8,128)(2,1)S(1)}, bf16[8,3584]{1,0:T(8,128)(2,1)S(1)}, u32[]{:S(2)}, u32[]{:S(2)}) collective-permute-start(bf16[8,3584]{1,0:T(8,128)(2,1)S(1)} %pair_sum.2.near_ref), channel_id=1, source_target_pairs={{0,2},{1,3},{2,0},{3,1},{4,6},{5,7},{6,4},{7,5},{8,10},{9,11},{10,... | collective-permute-start | bytes 172040 | tf_op jit(solution)/shard_map/ppermute | solution.py:30
  54.2 2.5 %collective-permute-done.21.far_ref = bf16[8,3712]{1,0:T(8,128)(2,1)S(1)} collective-permute-done((bf16[8,3712]{1,0:T(8,128)(2,1)S(1)}, bf16[8,3712]{1,0:T(8,128)(2,1)S(1)}, u32[]{:S(2)}, u32[]{:S(2)}) %collective-permute-start.21) | collective-permute-done | bytes 59424 | tf_op jit(solution)/shard_map/ppermute | solution.py:30
  56.7 1.3 %first_down.1 = (f32[8,2048]{1,0:T(8,128)S(1)}, f32[8,128]{1,0:T(8,128)S(1)}) custom-call(bf16[8,3712]{1,0:T(8,128)(2,1)S(1)} %pair_sum.3.near_ref, bf16[8,3712]{1,0:T(8,128)(2,1)S(1)} %collective-permute-done.21.far_ref, bf16[1792,2048]{1,0:T(8,128)(2,1)S(1)} %get-tuple-element.62.weight_ref), custom_call_target="tpu_custom_call" | custom-call | flops 58720256 | bytes 7340032 | tf_op jit(solution)/shard_map/first_down/pallas_call | solution.py:505
  58.0 0.0 collective-permute-done.19.far_ref
  58.0 1.3 %second_down.1 = bf16[8,2048]{1,0:T(8,128)(2,1)S(1)} custom-call(bf16[8,3584]{1,0:T(8,128)(2,1)S(1)} %pair_sum.2.near_ref, bf16[8,3584]{1,0:T(8,128)(2,1)S(1)} %collective-permute-done.19.far_ref, bf16[1792,2048]{1,0:T(8,128)(2,1)S(1)} %get-tuple-element.60.weight_ref, f32[8,2048]{1,0:T(8,128)S(1)} %get-tuple-element.63.part_ref, ...), custom_call_target="tpu_custom_call" | custom-call | tf_op jit(solution)/shard_map/second_down/pallas_call | solution.py:530
  59.3 0.7 collective-permute-start.22
  60.0 1.8 %collective-permute-start.24 = (bf16[2,2048]{1,0:T(2,128)(2,1)S(1)}, bf16[2,2048]{1,0:T(2,128)(2,1)S(1)}, u32[]{:S(2)}, u32[]{:S(2)}) collective-permute-start(bf16[2,2048]{1,0:T(2,128)(2,1)S(1)} %get-tuple-element.68), channel_id=1, source_target_pairs={{0,12},{1,13},{2,14},{3,15},{4,8},{5,9},{6,10},{7,11},{8,4},{9,5},... | collective-permute-start | bytes 24584 | tf_op jit(solution)/shard_map/ppermute | solution.py:49
  61.7 1.1 %collective-permute-start.23 = (bf16[2,2048]{1,0:T(2,128)(2,1)S(1)}, bf16[2,2048]{1,0:T(2,128)(2,1)S(1)}, u32[]{:S(2)}, u32[]{:S(2)}) collective-permute-start(bf16[2,2048]{1,0:T(2,128)(2,1)S(1)} %get-tuple-element.69), channel_id=1, source_target_pairs={{0,8},{1,9},{2,10},{3,11},{4,12},{5,13},{6,14},{7,15},{8,0},{9,1},... | collective-permute-start | bytes 24584 | tf_op jit(solution)/shard_map/ppermute | solution.py:49
  62.9 0.2 collective-permute-done.22
  63.0 2.4 %collective-permute-done.24 = bf16[2,2048]{1,0:T(2,128)(2,1)S(1)} collective-permute-done((bf16[2,2048]{1,0:T(2,128)(2,1)S(1)}, bf16[2,2048]{1,0:T(2,128)(2,1)S(1)}, u32[]{:S(2)}, u32[]{:S(2)}) %collective-permute-start.24) | collective-permute-done | bytes 8224 | tf_op jit(solution)/shard_map/ppermute | solution.py:49
  65.4 0.9 %collective-permute-done.23 = bf16[2,2048]{1,0:T(2,128)(2,1)S(1)} collective-permute-done((bf16[2,2048]{1,0:T(2,128)(2,1)S(1)}, bf16[2,2048]{1,0:T(2,128)(2,1)S(1)}, u32[]{:S(2)}, u32[]{:S(2)}) %collective-permute-start.23) | collective-permute-done | bytes 8224 | tf_op jit(solution)/shard_map/ppermute | solution.py:49
  66.3 0.6 add_convert_fusion
  (20 shorter events, 0.2 us)
Async XLA Ops:
  0.0 8.4 %collective-permute-start = (bf16[2,2048]{1,0:T(2,128)(2,1)}, bf16[2,2048]{1,0:T(2,128)(2,1)S(1)}, u32[]{:S(2)}, u32[]{:S(2)}) collective-permute-start(bf16[2,2048]{1,0:T(2,128)(2,1)} %refs_5_.1), channel_id=1, source_target_pairs={{0,4},{4,0},{8,12},{12,8},{1,5},{5,1},{9,13},{13,9},{2,6},{6,2},{1... | collective-permute-start | bytes 24584 | tf_op jit(solution)/shard_map/ppermute | solution.py:30
  3.0 5.7 %collective-permute-start.2 = (bf16[2,2048]{1,0:T(2,128)(2,1)}, bf16[2,2048]{1,0:T(2,128)(2,1)S(1)}, u32[]{:S(2)}, u32[]{:S(2)}) collective-permute-start(bf16[2,2048]{1,0:T(2,128)(2,1)} %refs_5_.1), channel_id=1, source_target_pairs={{0,12},{4,8},{8,4},{12,0},{1,13},{5,9},{9,5},{13,1},{2,14},{6,10},... | collective-permute-start | bytes 24584 | tf_op jit(solution)/shard_map/ppermute | solution.py:30
  5.5 4.8 %collective-permute-start.1 = (bf16[2,2048]{1,0:T(2,128)(2,1)}, bf16[2,2048]{1,0:T(2,128)(2,1)S(1)}, u32[]{:S(2)}, u32[]{:S(2)}) collective-permute-start(bf16[2,2048]{1,0:T(2,128)(2,1)} %refs_5_.1), channel_id=1, source_target_pairs={{0,8},{4,12},{8,0},{12,4},{1,9},{5,13},{9,1},{13,5},{2,10},{6,14},... | collective-permute-start | bytes 24584 | tf_op jit(solution)/shard_map/ppermute | solution.py:30
  5.6 7.7 %copy-start.3 = (s32[8]{0:T(128)S(1)}, s32[8]{0:T(128)}, u32[]{:S(2)}) copy-start(s32[8]{0:T(128)} %param.23) | copy-start | bytes 100
  11.1 4.9 %collective-permute-start.5 = (bf16[2,1408]{1,0:T(2,128)(2,1)S(1)}, bf16[2,1408]{1,0:T(2,128)(2,1)S(1)}, u32[]{:S(2)}, u32[]{:S(2)}) collective-permute-start(bf16[2,1408]{1,0:T(2,128)(2,1)S(1)} %get-tuple-element.71), channel_id=1, source_target_pairs={{0,13},{1,12},{2,15},{3,14},{4,9},{5,8},{6,11},{7,10},{8,5},{9,4},... | collective-permute-start | bytes 16904 | tf_op jit(solution)/shard_map/ppermute | solution.py:49
  11.2 4.8 %collective-permute-start.4 = (bf16[2,1408]{1,0:T(2,128)(2,1)S(1)}, bf16[2,1408]{1,0:T(2,128)(2,1)S(1)}, u32[]{:S(2)}, u32[]{:S(2)}) collective-permute-start(bf16[2,1408]{1,0:T(2,128)(2,1)S(1)} %get-tuple-element.72), channel_id=1, source_target_pairs={{0,9},{1,8},{2,11},{3,10},{4,13},{5,12},{6,15},{7,14},{8,1},{9,0},... | collective-permute-start | bytes 16904 | tf_op jit(solution)/shard_map/ppermute | solution.py:49
  13.1 3.0 %collective-permute-start.3 = (bf16[2,1408]{1,0:T(2,128)(2,1)S(1)}, bf16[2,1408]{1,0:T(2,128)(2,1)S(1)}, u32[]{:S(2)}, u32[]{:S(2)}) collective-permute-start(bf16[2,1408]{1,0:T(2,128)(2,1)S(1)} %get-tuple-element.73), channel_id=1, source_target_pairs={{0,5},{1,4},{2,7},{3,6},{4,1},{5,0},{6,3},{7,2},{8,13},{9,12},{10,... | collective-permute-start | bytes 16904 | tf_op jit(solution)/shard_map/ppermute | solution.py:49
  13.4 16.7 %copy-start = (bf16[2048,3584]{1,0:T(8,128)(2,1)S(1)}, bf16[2048,3584]{1,0:T(8,128)(2,1)}, u32[]{:S(2)}) copy-start(bf16[2048,3584]{1,0:T(8,128)(2,1)} %gate_ref.1) | copy-start | bytes 44040196
  16.1 5.9 %collective-permute-start.8 = (bf16[8,1408]{1,0:T(8,128)(2,1)S(1)}, bf16[8,1408]{1,0:T(8,128)(2,1)S(1)}, u32[]{:S(2)}, u32[]{:S(2)}) collective-permute-start(bf16[8,1408]{1,0:T(8,128)(2,1)S(1)} %pad_maximum_fusion.1.refs_1_.refs_0_), channel_id=1, source_target_pairs={{0,3},{1,2},{2,1},{3,0},{4,7},{5,6},{6,5},{7,4},{8,11},{9,10},{10,... | collective-permute-start | bytes 67592 | tf_op jit(solution)/shard_map/ppermute | solution.py:30
  19.2 3.8 %collective-permute-start.7 = (bf16[8,1408]{1,0:T(8,128)(2,1)S(1)}, bf16[8,1408]{1,0:T(8,128)(2,1)S(1)}, u32[]{:S(2)}, u32[]{:S(2)}) collective-permute-start(bf16[8,1408]{1,0:T(8,128)(2,1)S(1)} %pad_maximum_fusion.1.refs_1_.refs_0_), channel_id=1, source_target_pairs={{0,2},{1,3},{2,0},{3,1},{4,6},{5,7},{6,4},{7,5},{8,10},{9,11},{10,... | collective-permute-start | bytes 67592 | tf_op jit(solution)/shard_map/ppermute | solution.py:30
  19.7 3.3 %collective-permute-start.6 = (bf16[8,1408]{1,0:T(8,128)(2,1)S(1)}, bf16[8,1408]{1,0:T(8,128)(2,1)S(1)}, u32[]{:S(2)}, u32[]{:S(2)}) collective-permute-start(bf16[8,1408]{1,0:T(8,128)(2,1)S(1)} %pad_maximum_fusion.1.refs_1_.refs_0_), channel_id=1, source_target_pairs={{0,1},{1,0},{2,3},{3,2},{4,5},{5,4},{6,7},{7,6},{8,9},{9,8},{10,11... | collective-permute-start | bytes 67592 | tf_op jit(solution)/shard_map/ppermute | solution.py:30
  24.8 10.5 %copy-start.1 = (bf16[2048,3584]{1,0:T(8,128)(2,1)S(1)}, bf16[2048,3584]{1,0:T(8,128)(2,1)}, u32[]{:S(2)}) copy-start(bf16[2048,3584]{1,0:T(8,128)(2,1)} %up_ref.3) | copy-start | bytes 44040196
  24.8 3.4 %collective-permute-start.11 = (bf16[64,256]{1,0:T(8,128)(2,1)S(1)}, bf16[64,256]{1,0:T(8,128)(2,1)S(1)}, u32[]{:S(2)}, u32[]{:S(2)}) collective-permute-start(bf16[64,256]{1,0:T(8,128)(2,1)S(1)} %attend.1.refs_0_), channel_id=1, source_target_pairs={{0,3},{1,2},{2,1},{3,0},{4,7},{5,6},{6,5},{7,4},{8,11},{9,10},{10,... | collective-permute-start | bytes 98312 | tf_op jit(solution)/shard_map/ppermute | solution.py:30
  26.2 3.9 %collective-permute-start.10 = (bf16[64,256]{1,0:T(8,128)(2,1)S(1)}, bf16[64,256]{1,0:T(8,128)(2,1)S(1)}, u32[]{:S(2)}, u32[]{:S(2)}) collective-permute-start(bf16[64,256]{1,0:T(8,128)(2,1)S(1)} %attend.1.refs_0_), channel_id=1, source_target_pairs={{0,2},{1,3},{2,0},{3,1},{4,6},{5,7},{6,4},{7,5},{8,10},{9,11},{10,... | collective-permute-start | bytes 98312 | tf_op jit(solution)/shard_map/ppermute | solution.py:30
  26.7 3.4 %collective-permute-start.9 = (bf16[64,256]{1,0:T(8,128)(2,1)S(1)}, bf16[64,256]{1,0:T(8,128)(2,1)S(1)}, u32[]{:S(2)}, u32[]{:S(2)}) collective-permute-start(bf16[64,256]{1,0:T(8,128)(2,1)S(1)} %attend.1.refs_0_), channel_id=1, source_target_pairs={{0,1},{1,0},{2,3},{3,2},{4,5},{5,4},{6,7},{7,6},{8,9},{9,8},{10,11... | collective-permute-start | bytes 98312 | tf_op jit(solution)/shard_map/ppermute | solution.py:30
  30.4 4.9 %collective-permute-start.14 = (bf16[2,1024]{1,0:T(2,128)(2,1)S(1)}, bf16[2,1024]{1,0:T(2,128)(2,1)S(1)}, u32[]{:S(2)}, u32[]{:S(2)}) collective-permute-start(bf16[2,1024]{1,0:T(2,128)(2,1)S(1)} %get-tuple-element.75), channel_id=1, source_target_pairs={{0,13},{1,12},{2,15},{3,14},{4,9},{5,8},{6,11},{7,10},{8,5},{9,4},... | collective-permute-start | bytes 12296 | tf_op jit(solution)/shard_map/ppermute | solution.py:49
  30.5 4.8 %collective-permute-start.13 = (bf16[2,1024]{1,0:T(2,128)(2,1)S(1)}, bf16[2,1024]{1,0:T(2,128)(2,1)S(1)}, u32[]{:S(2)}, u32[]{:S(2)}) collective-permute-start(bf16[2,1024]{1,0:T(2,128)(2,1)S(1)} %get-tuple-element.76), channel_id=1, source_target_pairs={{0,9},{1,8},{2,11},{3,10},{4,13},{5,12},{6,15},{7,14},{8,1},{9,0},... | collective-permute-start | bytes 12296 | tf_op jit(solution)/shard_map/ppermute | solution.py:49
  31.4 3.9 %collective-permute-start.12 = (bf16[2,1024]{1,0:T(2,128)(2,1)S(1)}, bf16[2,1024]{1,0:T(2,128)(2,1)S(1)}, u32[]{:S(2)}, u32[]{:S(2)}) collective-permute-start(bf16[2,1024]{1,0:T(2,128)(2,1)S(1)} %get-tuple-element.77), channel_id=1, source_target_pairs={{0,5},{1,4},{2,7},{3,6},{4,1},{5,0},{6,3},{7,2},{8,13},{9,12},{10,... | collective-permute-start | bytes 12296 | tf_op jit(solution)/shard_map/ppermute | solution.py:49
  35.3 9.2 %copy-start.2 = (bf16[2048,3584]{1,0:T(8,128)(2,1)S(1)}, bf16[2048,3584]{1,0:T(8,128)(2,1)}, u32[]{:S(2)}) copy-start(bf16[2048,3584]{1,0:T(8,128)(2,1)} %up_ref.3) | copy-start | bytes 44040196
  36.3 4.7 %collective-permute-start.15 = (bf16[8,2048]{1,0:T(8,128)(2,1)S(1)}, bf16[8,2048]{1,0:T(8,128)(2,1)S(1)}, u32[]{:S(2)}, u32[]{:S(2)}) collective-permute-start(bf16[8,2048]{1,0:T(8,128)(2,1)S(1)} %get-tuple-element.54), channel_id=1, source_target_pairs={{0,4},{1,5},{2,6},{3,7},{4,0},{5,1},{6,2},{7,3},{8,12},{9,13},{10,... | collective-permute-start | bytes 98312 | tf_op jit(solution)/shard_map/ppermute | solution.py:49
  38.6 4.8 %collective-permute-start.16 = (bf16[8,2048]{1,0:T(8,128)(2,1)S(1)}, bf16[8,2048]{1,0:T(8,128)(2,1)S(1)}, u32[]{:S(2)}, u32[]{:S(2)}) collective-permute-start(bf16[8,2048]{1,0:T(8,128)(2,1)S(1)} %get-tuple-element.55), channel_id=1, source_target_pairs={{0,8},{1,9},{2,10},{3,11},{4,12},{5,13},{6,14},{7,15},{8,0},{9,1},... | collective-permute-start | bytes 98312 | tf_op jit(solution)/shard_map/ppermute | solution.py:49
  38.6 5.9 %collective-permute-start.17 = (bf16[8,2048]{1,0:T(8,128)(2,1)S(1)}, bf16[8,2048]{1,0:T(8,128)(2,1)S(1)}, u32[]{:S(2)}, u32[]{:S(2)}) collective-permute-start(bf16[8,2048]{1,0:T(8,128)(2,1)S(1)} %get-tuple-element.56), channel_id=1, source_target_pairs={{0,12},{1,13},{2,14},{3,15},{4,8},{5,9},{6,10},{7,11},{8,4},{9,5},... | collective-permute-start | bytes 98312 | tf_op jit(solution)/shard_map/ppermute | solution.py:49
  48.1 3.9 %collective-permute-start.20 = (bf16[8,3712]{1,0:T(8,128)(2,1)S(1)}, bf16[8,3712]{1,0:T(8,128)(2,1)S(1)}, u32[]{:S(2)}, u32[]{:S(2)}) collective-permute-start(bf16[8,3712]{1,0:T(8,128)(2,1)S(1)} %get-tuple-element.61.first_ref), channel_id=1, source_target_pairs={{0,1},{1,0},{2,3},{3,2},{4,5},{5,4},{6,7},{7,6},{8,9},{9,8},{10,11... | collective-permute-start | bytes 178184 | tf_op jit(solution)/shard_map/ppermute | solution.py:30
  51.5 1.5 %collective-permute-start.18 = (bf16[8,3584]{1,0:T(8,128)(2,1)S(1)}, bf16[8,3584]{1,0:T(8,128)(2,1)S(1)}, u32[]{:S(2)}, u32[]{:S(2)}) collective-permute-start(bf16[8,3584]{1,0:T(8,128)(2,1)S(1)} %get-tuple-element.59.first_ref), channel_id=1, source_target_pairs={{0,1},{1,0},{2,3},{3,2},{4,5},{5,4},{6,7},{7,6},{8,9},{9,8},{10,11... | collective-permute-start | bytes 172040 | tf_op jit(solution)/shard_map/ppermute | solution.py:30
  52.1 4.6 %collective-permute-start.21 = (bf16[8,3712]{1,0:T(8,128)(2,1)S(1)}, bf16[8,3712]{1,0:T(8,128)(2,1)S(1)}, u32[]{:S(2)}, u32[]{:S(2)}) collective-permute-start(bf16[8,3712]{1,0:T(8,128)(2,1)S(1)} %pair_sum.3.near_ref), channel_id=1, source_target_pairs={{0,2},{1,3},{2,0},{3,1},{4,6},{5,7},{6,4},{7,5},{8,10},{9,11},{10,... | collective-permute-start | bytes 178184 | tf_op jit(solution)/shard_map/ppermute | solution.py:30
  52.9 5.0 %collective-permute-start.19 = (bf16[8,3584]{1,0:T(8,128)(2,1)S(1)}, bf16[8,3584]{1,0:T(8,128)(2,1)S(1)}, u32[]{:S(2)}, u32[]{:S(2)}) collective-permute-start(bf16[8,3584]{1,0:T(8,128)(2,1)S(1)} %pair_sum.2.near_ref), channel_id=1, source_target_pairs={{0,2},{1,3},{2,0},{3,1},{4,6},{5,7},{6,4},{7,5},{8,10},{9,11},{10,... | collective-permute-start | bytes 172040 | tf_op jit(solution)/shard_map/ppermute | solution.py:30
  59.3 3.7 %collective-permute-start.22 = (bf16[2,2048]{1,0:T(2,128)(2,1)S(1)}, bf16[2,2048]{1,0:T(2,128)(2,1)S(1)}, u32[]{:S(2)}, u32[]{:S(2)}) collective-permute-start(bf16[2,2048]{1,0:T(2,128)(2,1)S(1)} %get-tuple-element.67), channel_id=1, source_target_pairs={{0,4},{1,5},{2,6},{3,7},{4,0},{5,1},{6,2},{7,3},{8,12},{9,13},{10,... | collective-permute-start | bytes 24584 | tf_op jit(solution)/shard_map/ppermute | solution.py:49
  60.0 5.4 %collective-permute-start.24 = (bf16[2,2048]{1,0:T(2,128)(2,1)S(1)}, bf16[2,2048]{1,0:T(2,128)(2,1)S(1)}, u32[]{:S(2)}, u32[]{:S(2)}) collective-permute-start(bf16[2,2048]{1,0:T(2,128)(2,1)S(1)} %get-tuple-element.68), channel_id=1, source_target_pairs={{0,12},{1,13},{2,14},{3,15},{4,8},{5,9},{6,10},{7,11},{8,4},{9,5},... | collective-permute-start | bytes 24584 | tf_op jit(solution)/shard_map/ppermute | solution.py:49
  61.7 4.5 %collective-permute-start.23 = (bf16[2,2048]{1,0:T(2,128)(2,1)S(1)}, bf16[2,2048]{1,0:T(2,128)(2,1)S(1)}, u32[]{:S(2)}, u32[]{:S(2)}) collective-permute-start(bf16[2,2048]{1,0:T(2,128)(2,1)S(1)} %get-tuple-element.69), channel_id=1, source_target_pairs={{0,8},{1,9},{2,10},{3,11},{4,12},{5,13},{6,14},{7,15},{8,0},{9,1},... | collective-permute-start | bytes 24584 | tf_op jit(solution)/shard_map/ppermute | solution.py:49

commit v7 on v6

--- a/solution.py
+++ b/solution.py
@@ -155,8 +155,24 @@
     )(*[in_hbm(a) for a in arrays], after)
 
 
-def qkv_kernel(rows_ref, gain_ref, wq_ref, wkv_ref, out_ref):
-    wide = rows_ref[...].astype(jnp.float32)
+def join_rows(refs, target):
+    rows = refs[0].shape[0]
+    for n, ref in enumerate(refs):
+        target[n * rows : (n + 1) * rows, :] = ref[...].astype(jnp.float32)
+    return target[...]
+
+
+def part_rows(source, refs):
+    rows = refs[0].shape[0]
+    for n, ref in enumerate(refs):
+        ref[...] = source[n * rows : (n + 1) * rows, :].astype(ref.dtype)
+
+
+def qkv_kernel(slots, gain_ref, wq_ref, wkv_ref, *refs):
+    rows_ref = refs[slots]
+    out_s, rows_s = refs[-2:]
+    wide = join_rows(refs[:slots], rows_s)
+    rows_ref[...] = wide
     total = jnp.sum(wide * wide, axis=1, keepdims=True)
     gain = gain_ref[...].astype(jnp.float32)[None, :]
     scaled = (wide * gain).astype(jnp.bfloat16)
@@ -164,26 +180,52 @@
     kv_cols = wkv_ref.shape[1]
 
     def store_query(start, size, value):
-        out_ref[:, pl.ds(start, size)] = value.astype(jnp.bfloat16)
+        out_s[:, pl.ds(start, size)] = value
 
     product_tiles(scaled, wq_ref, store_query)
-    out_ref[:, query_cols : query_cols + kv_cols] = jnp.dot(
+    out_s[:, query_cols : query_cols + kv_cols] = jnp.dot(
         scaled, wkv_ref[...], preferred_element_type=jnp.float32
-    ).astype(jnp.bfloat16)
-    out_ref[:, query_cols + kv_cols :] = squares_block(total).astype(jnp.bfloat16)
+    )
+    out_s[:, query_cols + kv_cols :] = squares_block(total)
+    part_rows(out_s, refs[slots + 1 : 2 * slots + 1])
 
 
 def project_qkv(rows, gain, w_query, w_kv):
-    count = rows.shape[0]
+    slots = len(rows)
+    own_rows, depth = rows[0].shape
     columns = w_query.shape[1] + w_kv.shape[1] + LANES
     return pl.pallas_call(
-        qkv_kernel,
-        out_shape=jax.ShapeDtypeStruct((count, columns), jnp.bfloat16),
-        in_specs=[in_vmem] * 4,
-        out_specs=in_vmem,
+        functools.partial(qkv_kernel, slots),
+        out_shape=(
+            jax.ShapeDtypeStruct((own_rows * slots, depth), jnp.float32),
+            *[jax.ShapeDtypeStruct((own_rows, columns), jnp.bfloat16)] * slots,
+        ),
+        in_specs=[in_vmem] * (3 + slots),
+        out_specs=(in_vmem,) * (1 + slots),
+        scratch_shapes=[
+            pltpu.VMEM((own_rows * slots, columns), jnp.float32),
+            pltpu.VMEM((own_rows * slots, depth), jnp.float32),
+        ],
         compiler_params=params(2),
         name="project_qkv",
-    )(rows, gain, resident(w_query), resident(w_kv))
+    )(gain, resident(w_query), resident(w_kv), *rows)
+
+
+def stack_kernel(*refs):
+    refs[-2][...] = join_rows(refs[:-2], refs[-1]).astype(refs[-2].dtype)
+
+
+def stack(pieces):
+    shape = (len(pieces) * pieces[0].shape[0], pieces[0].shape[1])
+    return pl.pallas_call(
+        stack_kernel,
+        out_shape=jax.ShapeDtypeStruct(shape, pieces[0].dtype),
+        in_specs=[in_vmem] * len(pieces),
+        out_specs=in_vmem,
+        scratch_shapes=[pltpu.VMEM(shape, jnp.float32)],
+        compiler_params=params(1),
+        name="stack",
+    )(*pieces)
 
 
 def attend_kernel(
@@ -303,9 +345,10 @@
     )(lengths, cosine, sine, resident(keys), resident(values), *parts)
 
 
-def combine_kernel(shards, all_rows, *refs):
+def combine_kernel(shards, slots, *refs):
     ins = refs[:shards]
-    out_ref = refs[-1]
+    out_s = refs[-1]
+    all_rows = out_s.shape[0]
     peaks = []
     totals = []
     for ref in ins:
@@ -322,17 +365,19 @@
     attended = mixed / denominator
     for j in range(attended.shape[0] // all_rows):
         block = attended[j * all_rows : (j + 1) * all_rows]
-        out_ref[:, j * HEAD_DIM : (j + 1) * HEAD_DIM] = block.astype(jnp.bfloat16)
-
-
-def combine(parts, later, all_rows):
+        out_s[:, j * HEAD_DIM : (j + 1) * HEAD_DIM] = block
+    part_rows(out_s, refs[-1 - slots : -1])
+
+
+def combine(parts, later, all_rows, slots):
     count = len(parts)
     columns = parts[0].shape[0] // all_rows * HEAD_DIM
     return pl.pallas_call(
-        functools.partial(combine_kernel, count, all_rows),
-        out_shape=jax.ShapeDtypeStruct((all_rows, columns), jnp.bfloat16),
+        functools.partial(combine_kernel, count, slots),
+        out_shape=(jax.ShapeDtypeStruct((all_rows // slots, columns), jnp.bfloat16),) * slots,
         in_specs=[in_vmem] * count + [in_place] * len(later),
-        out_specs=in_vmem,
+        out_specs=(in_vmem,) * slots,
+        scratch_shapes=[pltpu.VMEM((all_rows, columns), jnp.float32)],
         compiler_params=params(2),
         name="combine",
     )(*parts, *[resident(w) for w in later])
@@ -349,11 +394,14 @@
     )
 
 
-def out_kernel(own_rows, left_ref, weight_ref, later_ref, *outs):
-    del later_ref
-    rows = left_ref.shape[0]
-    lefts = [left_ref[...].astype(jnp.float32)]
-    for k in range(1, len(outs)):
+def out_kernel(slots, later, weight_ref, *refs):
+    pieces = refs[:slots]
+    outs = refs[slots + later : 2 * slots + later]
+    left_s = refs[-1]
+    own_rows = pieces[0].shape[0]
+    rows = left_s.shape[0]
+    lefts = [join_rows(pieces, left_s)]
+    for k in range(1, slots):
         low = k & -k
         lefts.append(turned(lefts[k ^ low], low, own_rows))
     left = jnp.concatenate(lefts, axis=0).astype(jnp.bfloat16)
@@ -365,18 +413,19 @@
     product_tiles(left, weight_ref, store)
 
 
-def project_out(left, weight, later, own_rows):
-    rows = left.shape[0]
-    count = rows // own_rows
-    shape = jax.ShapeDtypeStruct((rows, weight.shape[1]), jnp.bfloat16)
-    return pl.pallas_call(
-        functools.partial(out_kernel, own_rows),
-        out_shape=(shape,) * count,
-        in_specs=[in_vmem, in_vmem, in_place],
-        out_specs=(in_vmem,) * count,
+def project_out(pieces, weight, later):
+    slots = len(pieces)
+    own_rows, depth = pieces[0].shape
+    shape = jax.ShapeDtypeStruct((own_rows * slots, weight.shape[1]), jnp.bfloat16)
+    return pl.pallas_call(
+        functools.partial(out_kernel, slots, len(later)),
+        out_shape=(shape,) * slots,
+        in_specs=[in_vmem] * (1 + slots) + [in_place] * len(later),
+        out_specs=(in_vmem,) * slots,
+        scratch_shapes=[pltpu.VMEM((own_rows * slots, depth), jnp.float32)],
         compiler_params=params(3),
         name="project_out",
-    )(left, resident(weight), resident(later))
+    )(resident(weight), *pieces, *[resident(w) for w in later])
 
 
 def pair_kernel(first_ref, second_ref, out_ref):
@@ -407,15 +456,17 @@
     product_tiles(scaled, up_ref, store(count), first, count)
 
 
-def first_gate_up_kernel(slots, count, rows_ref, gain_ref, gate_ref, up_ref, later_ref, *refs):
+def first_gate_up_kernel(
+    slots, count, start, rows_ref, gain_ref, gate_ref, up_ref, down_ref, *refs
+):
     parts = refs[:slots]
-    out_ref, updated_ref, scaled_ref, loaded_ref, sems = refs[slots:]
-    copies = copies_of(later_ref, 0, loaded_ref, sems)
+    out_ref, updated_ref, scaled_ref, loaded_ref, sems = refs[-5:]
+    copies = copies_of(down_ref, start, loaded_ref, sems)
     for copy in copies:
         copy.start()
     own_rows = updated_ref.shape[0]
     total = functools.reduce(jnp.add, [ref[...].astype(jnp.float32) for ref in parts])
-    updated = (rows_ref[...].astype(jnp.float32) + total).astype(jnp.bfloat16)
+    updated = (rows_ref[...] + total).astype(jnp.bfloat16)
     wide = updated.astype(jnp.float32)
     updated_ref[...] = wide[:own_rows]
     squares = jnp.sum(wide * wide, axis=1, keepdims=True)
@@ -427,44 +478,53 @@
         copy.wait()
 
 
-def first_gate_up(rows, gain, parts, w_gate, w_up, w_down, count, own_rows):
+def first_gate_up(rows, gain, parts, w_gate, w_up, w_down, span, later, count, own_rows):
     slots = len(parts)
-    return pl.pallas_call(
-        functools.partial(first_gate_up_kernel, slots, count),
+    start, size = span
+    return pl.pallas_call(
+        functools.partial(first_gate_up_kernel, slots, count, start),
         out_shape=(
             jax.ShapeDtypeStruct((rows.shape[0], 2 * count + LANES), jnp.bfloat16),
             jax.ShapeDtypeStruct((own_rows, rows.shape[1]), jnp.float32),
             jax.ShapeDtypeStruct(rows.shape, jnp.bfloat16),
-            pltpu.VMEM((count, w_down.shape[1]), w_down.dtype),
+            pltpu.VMEM((size, w_down.shape[1]), w_down.dtype),
         ),
-        in_specs=[in_vmem] * 4 + [in_place] + [in_vmem] * slots,
+        in_specs=[in_vmem] * 4 + [in_place] + [in_vmem] * slots + [in_place] * len(later),
         out_specs=(in_vmem,) * 4,
         scratch_shapes=[pltpu.SemaphoreType.DMA((COPIES,))],
         compiler_params=params(3),
         cost_estimate=product_cost(w_gate.shape[0], 2 * count),
         name="first_gate_up",
-    )(rows, gain, resident(w_gate), resident(w_up), in_hbm(w_down), *parts)
+    )(
+        rows,
+        gain,
+        resident(w_gate),
+        resident(w_up),
+        in_hbm(w_down),
+        *parts,
+        *[resident(w) for w in later],
+    )
 
 
 def second_gate_up_kernel(
-    first, scaled_ref, gate_ref, up_ref, later_ref, out_ref, loaded_ref, sems
+    first, count, start, scaled_ref, gate_ref, up_ref, down_ref, out_ref, loaded_ref, sems
 ):
-    copies = copies_of(later_ref, first, loaded_ref, sems)
+    copies = copies_of(down_ref, start, loaded_ref, sems)
     for copy in copies:
         copy.start()
-    count = loaded_ref.shape[0]
     gate_up_tiles(scaled_ref[...], gate_ref, up_ref, out_ref, first, count)
     for copy in copies:
         copy.wait()
 
 
-def second_gate_up(scaled, w_gate, w_up, w_down, first):
-    count = w_down.shape[0] - first
-    return pl.pallas_call(
-        functools.partial(second_gate_up_kernel, first),
+def second_gate_up(scaled, w_gate, w_up, w_down, span, first):
+    count = w_gate.shape[1] - first
+    start, size = span
+    return pl.pallas_call(
+        functools.partial(second_gate_up_kernel, first, count, start),
         out_shape=(
             jax.ShapeDtypeStruct((scaled.shape[0], 2 * count), jnp.bfloat16),
-            pltpu.VMEM((count, w_down.shape[1]), w_down.dtype),
+            pltpu.VMEM((size, w_down.shape[1]), w_down.dtype),
         ),
         in_specs=[in_vmem] * 3 + [in_place],
         out_specs=(in_vmem,) * 2,
@@ -484,8 +544,10 @@
     return (gate / (1.0 + jnp.exp(-gate)) * total(count)).astype(jnp.bfloat16)
 
 
-def first_down_kernel(near_ref, far_ref, weight_ref, out_ref, scale_ref):
-    count = weight_ref.shape[0]
+def first_down_kernel(near_ref, far_ref, one_ref, two_ref, later_ref, out_ref, scale_ref):
+    del later_ref
+    cut = one_ref.shape[0]
+    count = (near_ref.shape[1] - LANES) // 2
     squares = jnp.sum(
         near_ref[:, 2 * count :].astype(jnp.float32) + far_ref[:, 2 * count :].astype(jnp.float32),
         axis=1,
@@ -493,48 +555,64 @@
     )
     scale = lax.rsqrt(squares / D + epsilon)
     scale_ref[...] = jnp.broadcast_to(scale, scale_ref.shape)
+    hidden = hidden_of(near_ref, far_ref, scale, count)
+    lower_ref = two_ref.at[: count - cut]
 
     def store(start, size, value):
-        out_ref[:, pl.ds(start, size)] = value
-
-    product_tiles(hidden_of(near_ref, far_ref, scale, count), weight_ref, store)
-
-
-def first_down(near, far, weight):
+        span = pl.ds(start, size)
+        out_ref[:, span] = value + jnp.dot(
+            hidden[:, cut:], lower_ref[:, span], preferred_element_type=jnp.float32
+        )
+
+    product_tiles(hidden[:, :cut], one_ref, store)
+
+
+def first_down(near, far, one, two, later):
     rows = near.shape[0]
+    columns = one.shape[1]
     return pl.pallas_call(
         first_down_kernel,
         out_shape=(
-            jax.ShapeDtypeStruct((rows, weight.shape[1]), jnp.float32),
+            jax.ShapeDtypeStruct((rows, columns), jnp.float32),
             jax.ShapeDtypeStruct((rows, LANES), jnp.float32),
         ),
-        in_specs=[in_vmem] * 3,
+        in_specs=[in_vmem] * 4 + [in_place],
         out_specs=(in_vmem,) * 2,
         compiler_params=params(3),
-        cost_estimate=product_cost(*weight.shape),
+        cost_estimate=product_cost((near.shape[1] - LANES) // 2, columns),
         name="first_down",
-    )(near, far, resident(weight))
-
-
-def second_down_kernel(near_ref, far_ref, weight_ref, part_ref, scale_ref, out_ref):
-    count = weight_ref.shape[0]
+    )(near, far, resident(one), resident(two), resident(later))
+
+
+def second_down_kernel(near_ref, far_ref, two_ref, three_ref, part_ref, scale_ref, *refs):
+    out_s = refs[-1]
+    count = near_ref.shape[1] // 2
+    cut = count - three_ref.shape[0]
+    hidden = hidden_of(near_ref, far_ref, scale_ref[:, 0:1], count)
+    upper_ref = two_ref.at[two_ref.shape[0] - cut :]
 
     def store(start, size, value):
         span = pl.ds(start, size)
-        out_ref[:, span] = (part_ref[:, span] + value).astype(jnp.bfloat16)
-
-    product_tiles(hidden_of(near_ref, far_ref, scale_ref[:, 0:1], count), weight_ref, store)
-
-
-def second_down(near, far, weight, part, scale):
+        out_s[:, span] = part_ref[:, span] + (
+            value
+            + jnp.dot(hidden[:, :cut], upper_ref[:, span], preferred_element_type=jnp.float32)
+        )
+
+    product_tiles(hidden[:, cut:], three_ref, store)
+    part_rows(out_s, refs[:-1])
+
+
+def second_down(near, far, two, three, part, scale, slots):
+    rows, columns = part.shape
     return pl.pallas_call(
         second_down_kernel,
-        out_shape=jax.ShapeDtypeStruct(part.shape, jnp.bfloat16),
-        in_specs=[in_vmem] * 5,
-        out_specs=in_vmem,
+        out_shape=(jax.ShapeDtypeStruct((rows // slots, columns), jnp.bfloat16),) * slots,
+        in_specs=[in_vmem] * 6,
+        out_specs=(in_vmem,) * slots,
+        scratch_shapes=[pltpu.VMEM(part.shape, jnp.float32)],
         compiler_params=params(3),
         name="second_down",
-    )(near, far, resident(weight), part, scale)
+    )(near, far, resident(two), resident(three), part, scale)
 
 
 def rotation_tables(positions, repeats):
@@ -568,44 +646,49 @@
     own_rows = states.shape[0]
     all_rows = own_rows * slots
 
-    cut = lambda array: [array[k * own_rows : (k + 1) * own_rows] for k in range(slots)]
-
     got = exchange(states, "tensor")
     own, attn_gain, ffn_gain, w_kv, w_query = load(
         states, attn_gain, ffn_gain, w_kv, w_query, after=states
     )
-    rows = jnp.concatenate([own] + got[1:], axis=0)
-    joined = project_qkv(rows, attn_gain, w_query, w_kv)
-
-    joined, lengths = lax.optimization_barrier((joined, lengths))
+    rows, *pieces = project_qkv([own] + got[1:], attn_gain, w_query, w_kv)
+
+    rows, lengths = lax.optimization_barrier((rows, lengths))
     my_lengths = lax.dynamic_slice_in_dim(lengths, tensor_index * own_rows, own_rows, 0)
     cosine, sine = rotation_tables(my_lengths.astype(jnp.float32), slots)
     my_lengths = jnp.broadcast_to(my_lengths[:, None], (own_rows, LANES))
     flat = (own_rows, key_cache.shape[1] * KV_HEADS, HEAD_DIM)
-    keys, values = load(key_cache.reshape(flat), value_cache.reshape(flat), after=joined)
-    joined = jnp.concatenate(scatter_slots(cut(joined), 1), axis=0)
-    joined, keys, values, w_gate = lax.optimization_barrier((joined, keys, values, w_gate))
+    keys, values = load(key_cache.reshape(flat), value_cache.reshape(flat), after=rows)
+    joined = stack(scatter_slots(pieces, 1))
+    joined, keys, values = lax.optimization_barrier((joined, keys, values))
     (w_out,) = load(w_out, after=joined)
     parts, w_out = lax.optimization_barrier((exchange(joined, "inner"), w_out))
     shard = attend(my_lengths, cosine, sine, parts, keys, values, slots)
 
-    attended = combine(exchange(shard, "inner"), [w_gate], all_rows)
-    picked = jnp.concatenate(scatter_slots(cut(attended), 1), axis=0)
-    parts = scatter_slots(project_out(picked, w_out, w_up, own_rows), 0)
+    pieces = combine(exchange(shard, "inner"), [], all_rows, slots)
+    parts = scatter_slots(project_out(scatter_slots(pieces, 1), w_out, [w_up]), 0)
 
     tiles = w_gate.shape[1] // LANES
-    first = (tiles + 1) // 2 * LANES
-    one, updated, scaled, upper = first_gate_up(
-        rows, ffn_gain, parts, w_gate, w_up, w_down, first, own_rows
-    )
-    two, lower = second_gate_up(scaled, w_gate, w_up, w_down, first)
+    half = (tiles + 1) // 2
+    span = tiles * 9 // 28
+    first = half * LANES
+    starts = [0, span * LANES, (span + max(span, half - span + 1)) * LANES, tiles * LANES]
+    spans = [(a, b - a) for a, b in zip(starts, starts[1:])]
+    one, updated, scaled, down_one = first_gate_up(
+        rows, ffn_gain, parts, w_gate, w_up, w_down, spans[0], [], first, own_rows
+    )
+    two, down_two = second_gate_up(scaled, w_gate, w_up, w_down, spans[1], first)
     steps = steps_up(lax.axis_size("inner"))
     for step in steps[:-1]:
         one = pair_sum(one, swap_with(one, "inner", step))
         two = pair_sum(two, swap_with(two, "inner", step))
-    part, scale = first_down(one, swap_with(one, "inner", steps[-1]), upper)
-    part = second_down(two, swap_with(two, "inner", steps[-1]), lower, part, scale)
-    parts = scatter_slots(cut(part), 0)
+    (down_three,) = load(w_down, after=two, spans=[spans[2]])
+    part, scale = first_down(
+        one, swap_with(one, "inner", steps[-1]), down_one, down_two, down_three
+    )
+    pieces = second_down(
+        two, swap_with(two, "inner", steps[-1]), down_two, down_three, part, scale, slots
+    )
+    parts = scatter_slots(pieces, 0)
     down_sum = sum(p.astype(jnp.float32) for p in parts)
     return (updated + down_sum).astype(jnp.bfloat16)
 

time: 67.1 us -> 69.5 us (1.036)
  Pallas kernels: 20.6 us -> 22 us
  starting transfers between devices: 26.7 us -> 28 us
    ppermute x13, waiting for transfers between devices: 8.79 us -> 6.12 us  [swap_with(): return lax.ppermute(value, axis, [(i, i ^ step) for i in range(count)])]
    pallas_call x3 -> x4, Pallas kernels: 7.38 us -> 9.9 us  [load(): pl.pallas_call(functools.partial(load_kernel, spans), out_shape=tuple((pl...]
    ppermute x12, waiting for transfers between devices: 9.64 us -> 12 us  [scatter_slots(): got.append(lax.ppermute(pieces[k], ('tensor', 'inner'), pairs))]
    ppermute x12, starting transfers between devices: 12.9 us -> 15 us  [scatter_slots(): got.append(lax.ppermute(pieces[k], ('tensor', 'inner'), pairs))]
    pallas_call x6 -> x7, Pallas kernels: 10.1 us -> 9.08 us  [the longest x1 3.26 us: first_gate_up(): pl.pallas_call(functools.partial(first_gate_up_kernel, slots, count, star...]
  transfers between devices with their start and end apart: 25 -> 25, of which waited for: 15 -> 9; matrix products, arithmetic and copies ran while one was open for 0% -> 0% of each run, Pallas kernels for 18% -> 20%
where the time goes in v7:
time: 69.5 us; the launch traced here: 69.3 us
  starting transfers between devices  28 us (40%)
  Pallas kernels  22 us (32%)
  waiting for transfers between devices  18.1 us (26%)
  other arithmetic  0.81 us (1%)
    ppermute x12, starting transfers between devices, scatter_slots(): got.append(lax.ppermute(pieces[k], ('tensor', 'inner'), pairs))  15 us
    ppermute x13, starting transfers between devices, swap_with(): return lax.ppermute(value, axis, [(i, i ^ step) for i in range(count)])  13.1 us
    ppermute x12, waiting for transfers between devices, scatter_slots(): got.append(lax.ppermute(pieces[k], ('tensor', 'inner'), pairs))  12 us
    pallas_call x4, Pallas kernels, load(): pl.pallas_call(functools.partial(load_kernel, spans), out_shape=tuple((pl...  9.9 us
    ppermute x13, waiting for transfers between devices, swap_with(): return lax.ppermute(value, axis, [(i, i ^ step) for i in range(count)])  6.12 us
    pallas_call x1, Pallas kernels, first_gate_up(): pl.pallas_call(functools.partial(first_gate_up_kernel, slots, count, star...  3.26 us
    pallas_call x1, Pallas kernels, second_gate_up(): pl.pallas_call(functools.partial(second_gate_up_kernel, first, count, sta...  2.44 us
    pallas_call x1, Pallas kernels, attend(): pl.pallas_call(functools.partial(attend_kernel, slots, len(parts)), out_s...  1.73 us
  transfers between devices with their start and end apart: 25, of which 9 were waited for; matrix products, arithmetic and copies ran while one was open for 0% of the time, Pallas kernels for 20%

profile of v7, /device:TPU:0, one launch (start us, length us, event | category | flops | bytes accessed | tf_op | source)
XLA Modules:
  0.0 69.3 jit_solution(5858423117684547035)
XLA Ops:
  0.0 3.0 %collective-permute-start = (bf16[2,2048]{1,0:T(2,128)(2,1)}, bf16[2,2048]{1,0:T(2,128)(2,1)S(1)}, u32[]{:S(2)}, u32[]{:S(2)}) collective-permute-start(bf16[2,2048]{1,0:T(2,128)(2,1)} %refs_5_.1), channel_id=1, source_target_pairs={{0,4},{4,0},{8,12},{12,8},{1,5},{5,1},{9,13},{13,9},{2,6},{6,2},{1... | collective-permute-start | bytes 24584 | tf_op jit(solution)/shard_map/ppermute | solution.py:30
  3.0 2.6 %collective-permute-start.1 = (bf16[2,2048]{1,0:T(2,128)(2,1)}, bf16[2,2048]{1,0:T(2,128)(2,1)S(1)}, u32[]{:S(2)}, u32[]{:S(2)}) collective-permute-start(bf16[2,2048]{1,0:T(2,128)(2,1)} %refs_5_.1), channel_id=1, source_target_pairs={{0,8},{4,12},{8,0},{12,4},{1,9},{5,13},{9,1},{13,5},{2,10},{6,14},... | collective-permute-start | bytes 24584 | tf_op jit(solution)/shard_map/ppermute | solution.py:30
  5.6 0.0 collective-permute-start.2
  5.6 0.0 copy-start.2
  5.6 2.7 %load.4 = (bf16[2,2048]{1,0:T(2,128)(2,1)S(1)}, bf16[2048]{0:T(1024)(128)(2,1)S(1)}, bf16[2048]{0:T(1024)(128)(2,1)S(1)}, bf16[2048,256]{1,0:T(8,128)(2,1)S(1)}, bf16[2048,1024]{1,0:T(8,128)(2,1)S(1)}) custom-call(bf16[2,2048]{1,0:T(2,128)(2,1)} %refs_5_.1, bf16[2048]{0:T(1024)(128)(2,1)} %refs_1_.1, bf16[2048]{0:T(1024)(128)(2,1)} %refs_2_.1, ...), custom_call_target="tpu_custom_call" | custom-call | bytes 5259264 | tf_op jit(solution)/shard_map/load/pallas_call | solution.py:144
  8.4 0.0 collective-permute-done.refs_1_
  8.4 0.0 collective-permute-done.1.refs_2_
  8.4 2.9 %collective-permute-done.2.refs_3_ = bf16[2,2048]{1,0:T(2,128)(2,1)S(1)} collective-permute-done((bf16[2,2048]{1,0:T(2,128)(2,1)}, bf16[2,2048]{1,0:T(2,128)(2,1)S(1)}, u32[]{:S(2)}, u32[]{:S(2)}) %collective-permute-start.2) | collective-permute-done | bytes 8224 | tf_op jit(solution)/shard_map/ppermute | solution.py:30
  11.3 0.8 %project_qkv.1 = (f32[8,2048]{1,0:T(8,128)S(1)}, bf16[2,1408]{1,0:T(2,128)(2,1)S(1)}, bf16[2,1408]{1,0:T(2,128)(2,1)S(1)}, bf16[2,1408]{1,0:T(2,128)(2,1)S(1)}, bf16[2,1408]{1,0:T(2,128)(2,1)S(1)}) custom-call(bf16[2048]{0:T(1024)(128)(2,1)S(1)} %get-tuple-element.47.gain_ref, bf16[2048,1024]{1,0:T(8,128)(2,1)S(1)} %get-tuple-element.48.wq_ref, ...), custom_call_target="tpu_custom_call" | custom-call | tf_op jit(solution)/shard_map/project_qkv/pallas_call | solution.py:197
  12.1 0.1 collective-permute-start.3
  12.2 1.2 %collective-permute-start.4 = (bf16[2,1408]{1,0:T(2,128)(2,1)S(1)}, bf16[2,1408]{1,0:T(2,128)(2,1)S(1)}, u32[]{:S(2)}, u32[]{:S(2)}) collective-permute-start(bf16[2,1408]{1,0:T(2,128)(2,1)S(1)} %get-tuple-element.56), channel_id=1, source_target_pairs={{0,9},{1,8},{2,11},{3,10},{4,13},{5,12},{6,15},{7,14},{8,1},{9,0},... | collective-permute-start | bytes 16904 | tf_op jit(solution)/shard_map/ppermute | solution.py:49
  13.4 0.6 collective-permute-start.5
  14.0 0.1 fusion.4
  14.1 2.4 %load.5 = (bf16[2,4096,128]{2,1,0:T(8,128)(2,1)S(1)}, bf16[2,4096,128]{2,1,0:T(8,128)(2,1)S(1)}) custom-call(bf16[2,4096,128]{2,1,0:T(8,128)(2,1)} %bitcast.6, bf16[2,4096,128]{2,1,0:T(8,128)(2,1)} %bitcast.7, f32[8,2048]{1,0:T(8,128)S(1)} %get-tuple-element.52.refs_2_.rows_ref), custom_call_target="tpu_custom_call" | custom-call | bytes 4194304 | tf_op jit(solution)/shard_map/load/pallas_call | solution.py:144
  16.5 0.0 collective-permute-done.3.refs_1_
  16.5 0.0 collective-permute-done.4.refs_2_
  16.6 1.7 %collective-permute-done.5.refs_3_ = bf16[2,1408]{1,0:T(2,128)(2,1)S(1)} collective-permute-done((bf16[2,1408]{1,0:T(2,128)(2,1)S(1)}, bf16[2,1408]{1,0:T(2,128)(2,1)S(1)}, u32[]{:S(2)}, u32[]{:S(2)}) %collective-permute-start.5) | collective-permute-done | bytes 5664 | tf_op jit(solution)/shard_map/ppermute | solution.py:49
  18.3 0.8 %collective-permute-start.6 = (bf16[8,1408]{1,0:T(8,128)(2,1)S(1)}, bf16[8,1408]{1,0:T(8,128)(2,1)S(1)}, u32[]{:S(2)}, u32[]{:S(2)}) collective-permute-start(bf16[8,1408]{1,0:T(8,128)(2,1)S(1)} %stack.1.refs_1_.refs_0_), channel_id=1, source_target_pairs={{0,1},{1,0},{2,3},{3,2},{4,5},{5,4},{6,7},{7,6},{8,9},{9,8},{10,11... | collective-permute-start | bytes 67592 | tf_op jit(solution)/shard_map/ppermute | solution.py:30
  19.0 1.5 %collective-permute-start.7 = (bf16[8,1408]{1,0:T(8,128)(2,1)S(1)}, bf16[8,1408]{1,0:T(8,128)(2,1)S(1)}, u32[]{:S(2)}, u32[]{:S(2)}) collective-permute-start(bf16[8,1408]{1,0:T(8,128)(2,1)S(1)} %stack.1.refs_1_.refs_0_), channel_id=1, source_target_pairs={{0,2},{1,3},{2,0},{3,1},{4,6},{5,7},{6,4},{7,5},{8,10},{9,11},{10,... | collective-permute-start | bytes 67592 | tf_op jit(solution)/shard_map/ppermute | solution.py:30
  20.5 0.0 collective-permute-start.8
  20.5 0.1 fusion
  20.6 2.2 %load.6.weight_ref = bf16[1024,2048]{1,0:T(8,128)(2,1)S(1)} custom-call(bf16[1024,2048]{1,0:T(8,128)(2,1)} %refs_0_.4, bf16[8,1408]{1,0:T(8,128)(2,1)S(1)} %stack.1.refs_1_.refs_0_), custom_call_target="tpu_custom_call" | custom-call | bytes 4194304 | tf_op jit(solution)/shard_map/load/pallas_call | solution.py:144
  22.9 0.0 collective-permute-done.6.refs_1_
  22.9 0.0 collective-permute-done.7.refs_2_
  22.9 1.1 %collective-permute-done.8.refs_3_ = bf16[8,1408]{1,0:T(8,128)(2,1)S(1)} collective-permute-done((bf16[8,1408]{1,0:T(8,128)(2,1)S(1)}, bf16[8,1408]{1,0:T(8,128)(2,1)S(1)}, u32[]{:S(2)}, u32[]{:S(2)}) %collective-permute-start.8) | collective-permute-done | bytes 22560 | tf_op jit(solution)/shard_map/ppermute | solution.py:30
  24.0 0.1 broadcast_in_dim.10.lengths_ref
  24.1 1.7 %attend.1.refs_0_ = bf16[64,256]{1,0:T(8,128)(2,1)S(1)} custom-call(s32[2,128]{1,0:T(2,128)S(1)} %broadcast_in_dim.10.lengths_ref, f32[8,128]{1,0:T(8,128)S(1)} %bitcast.4, f32[8,128]{1,0:T(8,128)S(1)} %bitcast.5, bf16[2,4096,128]{2,1,0:T(8,128)(2,1)S(1)} %get-tuple-element.63.key_ref, bf16[2,4096,128]{2,1,0:T(8,128)(2,1)S(1)} %get-tuple-element.64.value_ref, ...), custom_call_target="tpu_custom_call" | custom-call | tf_op jit(solution)/shard_map/attend/pallas_call | solution.py:331
  25.8 0.6 collective-permute-start.10
  26.4 1.0 %collective-permute-start.11 = (bf16[64,256]{1,0:T(8,128)(2,1)S(1)}, bf16[64,256]{1,0:T(8,128)(2,1)S(1)}, u32[]{:S(2)}, u32[]{:S(2)}) collective-permute-start(bf16[64,256]{1,0:T(8,128)(2,1)S(1)} %attend.1.refs_0_), channel_id=1, source_target_pairs={{0,3},{1,2},{2,1},{3,0},{4,7},{5,6},{6,5},{7,4},{8,11},{9,10},{10,... | collective-permute-start | bytes 98312 | tf_op jit(solution)/shard_map/ppermute | solution.py:30
  27.4 0.6 collective-permute-start.9
  28.0 2.1 %collective-permute-done.10.refs_2_ = bf16[64,256]{1,0:T(8,128)(2,1)S(1)} collective-permute-done((bf16[64,256]{1,0:T(8,128)(2,1)S(1)}, bf16[64,256]{1,0:T(8,128)(2,1)S(1)}, u32[]{:S(2)}, u32[]{:S(2)}) %collective-permute-start.10) | collective-permute-done | bytes 32800 | tf_op jit(solution)/shard_map/ppermute | solution.py:30
  30.1 0.0 collective-permute-done.11.refs_3_
  30.1 0.0 collective-permute-done.9.refs_1_
  30.1 0.3 combine.1
  30.4 0.1 collective-permute-start.12
  30.5 2.5 %collective-permute-start.13 = (bf16[2,1024]{1,0:T(2,128)(2,1)S(1)}, bf16[2,1024]{1,0:T(2,128)(2,1)S(1)}, u32[]{:S(2)}, u32[]{:S(2)}) collective-permute-start(bf16[2,1024]{1,0:T(2,128)(2,1)S(1)} %get-tuple-element.71), channel_id=1, source_target_pairs={{0,9},{1,8},{2,11},{3,10},{4,13},{5,12},{6,15},{7,14},{8,1},{9,0},... | collective-permute-start | bytes 12296 | tf_op jit(solution)/shard_map/ppermute | solution.py:49
  32.9 1.7 %collective-permute-start.14 = (bf16[2,1024]{1,0:T(2,128)(2,1)S(1)}, bf16[2,1024]{1,0:T(2,128)(2,1)S(1)}, u32[]{:S(2)}, u32[]{:S(2)}) collective-permute-start(bf16[2,1024]{1,0:T(2,128)(2,1)S(1)} %get-tuple-element.72), channel_id=1, source_target_pairs={{0,13},{1,12},{2,15},{3,14},{4,9},{5,8},{6,11},{7,10},{8,5},{9,4},... | collective-permute-start | bytes 12296 | tf_op jit(solution)/shard_map/ppermute | solution.py:49
  34.7 0.0 collective-permute-done.12.refs_1_
  34.7 0.0 collective-permute-done.13.refs_2_
  34.7 3.1 %collective-permute-done.14.refs_3_ = bf16[2,1024]{1,0:T(2,128)(2,1)S(1)} collective-permute-done((bf16[2,1024]{1,0:T(2,128)(2,1)S(1)}, bf16[2,1024]{1,0:T(2,128)(2,1)S(1)}, u32[]{:S(2)}, u32[]{:S(2)}) %collective-permute-start.14) | collective-permute-done | bytes 4128 | tf_op jit(solution)/shard_map/ppermute | solution.py:49
  37.8 0.9 %project_out.1 = (bf16[8,2048]{1,0:T(8,128)(2,1)S(1)}, bf16[8,2048]{1,0:T(8,128)(2,1)S(1)}, bf16[8,2048]{1,0:T(8,128)(2,1)S(1)}, bf16[8,2048]{1,0:T(8,128)(2,1)S(1)}) custom-call(bf16[1024,2048]{1,0:T(8,128)(2,1)S(1)} %load.6.weight_ref, bf16[2,1024]{1,0:T(2,128)(2,1)S(1)} %get-tuple-element.69.refs_0_, bf16[2,1024]{1,0:T(2,128)(2,1)S(1)} %collective-permute-done.12.refs_1_, ...), custom_call_target="tpu_custom_call" | custom-call | tf_op jit(solution)/shard_map/project_out/pallas_call | solution.py:420
  38.7 0.0 collective-permute-start.15
  38.7 2.2 %collective-permute-start.16 = (bf16[8,2048]{1,0:T(8,128)(2,1)S(1)}, bf16[8,2048]{1,0:T(8,128)(2,1)S(1)}, u32[]{:S(2)}, u32[]{:S(2)}) collective-permute-start(bf16[8,2048]{1,0:T(8,128)(2,1)S(1)} %get-tuple-element.75), channel_id=1, source_target_pairs={{0,8},{1,9},{2,10},{3,11},{4,12},{5,13},{6,14},{7,15},{8,0},{9,1},... | collective-permute-start | bytes 98312 | tf_op jit(solution)/shard_map/ppermute | solution.py:49
  40.9 2.2 %collective-permute-start.17 = (bf16[8,2048]{1,0:T(8,128)(2,1)S(1)}, bf16[8,2048]{1,0:T(8,128)(2,1)S(1)}, u32[]{:S(2)}, u32[]{:S(2)}) collective-permute-start(bf16[8,2048]{1,0:T(8,128)(2,1)S(1)} %get-tuple-element.76), channel_id=1, source_target_pairs={{0,12},{1,13},{2,14},{3,15},{4,8},{5,9},{6,10},{7,11},{8,4},{9,5},... | collective-permute-start | bytes 98312 | tf_op jit(solution)/shard_map/ppermute | solution.py:49
  43.1 0.0 collective-permute-done.15.refs_1_
  43.1 1.1 %collective-permute-done.16.refs_2_ = bf16[8,2048]{1,0:T(8,128)(2,1)S(1)} collective-permute-done((bf16[8,2048]{1,0:T(8,128)(2,1)S(1)}, bf16[8,2048]{1,0:T(8,128)(2,1)S(1)}, u32[]{:S(2)}, u32[]{:S(2)}) %collective-permute-start.16) | collective-permute-done | bytes 32800 | tf_op jit(solution)/shard_map/ppermute | solution.py:49
  44.3 2.4 %collective-permute-done.17.refs_3_ = bf16[8,2048]{1,0:T(8,128)(2,1)S(1)} collective-permute-done((bf16[8,2048]{1,0:T(8,128)(2,1)S(1)}, bf16[8,2048]{1,0:T(8,128)(2,1)S(1)}, u32[]{:S(2)}, u32[]{:S(2)}) %collective-permute-start.17) | collective-permute-done | bytes 32800 | tf_op jit(solution)/shard_map/ppermute | solution.py:49
  46.7 3.3 %first_gate_up.1 = (bf16[8,3712]{1,0:T(8,128)(2,1)S(1)}, f32[2,2048]{1,0:T(2,128)S(1)}, bf16[8,2048]{1,0:T(8,128)(2,1)S(1)}, bf16[1152,2048]{1,0:T(8,128)(2,1)S(1)}) custom-call(f32[8,2048]{1,0:T(8,128)S(1)} %get-tuple-element.52.refs_2_.rows_ref, bf16[2048]{0:T(1024)(128)(2,1)S(1)} %get-tuple-element.53.gain_ref, bf16[2048,3584]{1,0:T(8,128)(2,1)S(1)} %copy-done.1, ...), custom_call_target="tpu_custom_call" | custom-call | flops 117440512 | bytes 14680064 | tf_op jit(solution)/shard_map/first_gate_up/pallas_call | solution.py:484
  49.9 0.1 collective-permute-start.20
  50.0 2.4 %second_gate_up.1 = (bf16[8,3584]{1,0:T(8,128)(2,1)S(1)}, bf16[1152,2048]{1,0:T(8,128)(2,1)S(1)}) custom-call(bf16[8,2048]{1,0:T(8,128)(2,1)S(1)} %get-tuple-element.78.scaled_ref, bf16[2048,3584]{1,0:T(8,128)(2,1)S(1)} %copy-done.1, bf16[2048,3584]{1,0:T(8,128)(2,1)S(1)} %copy-done, bf16[3584,2048]{1,0:T(8,128)(2,1)} %refs_0_.5), custom_call_target="tpu_custom_call" | custom-call | flops 117440512 | bytes 14680064 | tf_op jit(solution)/shard_map/second_gate_up/pallas_call | solution.py:523
  52.5 0.6 collective-permute-start.18
  53.0 0.0 collective-permute-done.20.second_ref
  53.0 1.5 %collective-permute-start.21 = (bf16[8,3712]{1,0:T(8,128)(2,1)S(1)}, bf16[8,3712]{1,0:T(8,128)(2,1)S(1)}, u32[]{:S(2)}, u32[]{:S(2)}) collective-permute-start(bf16[8,3712]{1,0:T(8,128)(2,1)S(1)} %pair_sum.3.near_ref), channel_id=1, source_target_pairs={{0,2},{1,3},{2,0},{3,1},{4,6},{5,7},{6,4},{7,5},{8,10},{9,11},{10,... | collective-permute-start | bytes 178184 | tf_op jit(solution)/shard_map/ppermute | solution.py:30
  54.5 0.9 %collective-permute-start.19 = (bf16[8,3584]{1,0:T(8,128)(2,1)S(1)}, bf16[8,3584]{1,0:T(8,128)(2,1)S(1)}, u32[]{:S(2)}, u32[]{:S(2)}) collective-permute-start(bf16[8,3584]{1,0:T(8,128)(2,1)S(1)} %pair_sum.2.refs_1_.near_ref), channel_id=1, source_target_pairs={{0,2},{1,3},{2,0},{3,1},{4,6},{5,7},{6,4},{7,5},{8,10},{9,11},{10,... | collective-permute-start | bytes 172040 | tf_op jit(solution)/shard_map/ppermute | solution.py:30
  55.4 2.5 %load.7.later_ref.three_ref = bf16[1280,2048]{1,0:T(8,128)(2,1)S(1)} custom-call(bf16[3584,2048]{1,0:T(8,128)(2,1)} %refs_0_.5, bf16[8,3584]{1,0:T(8,128)(2,1)S(1)} %pair_sum.2.refs_1_.near_ref), custom_call_target="tpu_custom_call" | custom-call | bytes 5242880 | tf_op jit(solution)/shard_map/load/pallas_call | solution.py:144
  58.0 1.3 %first_down.1 = (f32[8,2048]{1,0:T(8,128)S(1)}, f32[8,128]{1,0:T(8,128)S(1)}) custom-call(bf16[8,3712]{1,0:T(8,128)(2,1)S(1)} %pair_sum.3.near_ref, bf16[8,3712]{1,0:T(8,128)(2,1)S(1)} %collective-permute-done.21.far_ref, bf16[1152,2048]{1,0:T(8,128)(2,1)S(1)} %get-tuple-element.82.one_ref, bf16[1152,2048]{1,0:T(8,128)(2,1)S(1)} %get-tuple-element.80.two_ref, ...), custom_call_target="tpu_custom_call" | custom-call | flops 58720256 | bytes 7340032 | tf_op jit(solution)/shard_map/first_down/pallas_call | solution.py:573
  59.2 1.3 %second_down.1 = (bf16[2,2048]{1,0:T(2,128)(2,1)S(1)}, bf16[2,2048]{1,0:T(2,128)(2,1)S(1)}, bf16[2,2048]{1,0:T(2,128)(2,1)S(1)}, bf16[2,2048]{1,0:T(2,128)(2,1)S(1)}) custom-call(bf16[8,3584]{1,0:T(8,128)(2,1)S(1)} %pair_sum.2.refs_1_.near_ref, bf16[8,3584]{1,0:T(8,128)(2,1)S(1)} %collective-permute-done.19.far_ref, ...), custom_call_target="tpu_custom_call" | custom-call | tf_op jit(solution)/shard_map/second_down/pallas_call | solution.py:607
  60.6 0.1 collective-permute-start.22
  60.6 2.6 %collective-permute-start.23 = (bf16[2,2048]{1,0:T(2,128)(2,1)S(1)}, bf16[2,2048]{1,0:T(2,128)(2,1)S(1)}, u32[]{:S(2)}, u32[]{:S(2)}) collective-permute-start(bf16[2,2048]{1,0:T(2,128)(2,1)S(1)} %get-tuple-element.87), channel_id=1, source_target_pairs={{0,8},{1,9},{2,10},{3,11},{4,12},{5,13},{6,14},{7,15},{8,0},{9,1},... | collective-permute-start | bytes 24584 | tf_op jit(solution)/shard_map/ppermute | solution.py:49
  63.2 1.8 %collective-permute-start.24 = (bf16[2,2048]{1,0:T(2,128)(2,1)S(1)}, bf16[2,2048]{1,0:T(2,128)(2,1)S(1)}, u32[]{:S(2)}, u32[]{:S(2)}) collective-permute-start(bf16[2,2048]{1,0:T(2,128)(2,1)S(1)} %get-tuple-element.88), channel_id=1, source_target_pairs={{0,12},{1,13},{2,14},{3,15},{4,8},{5,9},{6,10},{7,11},{8,4},{9,5},... | collective-permute-start | bytes 24584 | tf_op jit(solution)/shard_map/ppermute | solution.py:49
  65.0 0.0 collective-permute-done.22
  65.0 0.3 collective-permute-done.23
  65.3 3.4 %collective-permute-done.24 = bf16[2,2048]{1,0:T(2,128)(2,1)S(1)} collective-permute-done((bf16[2,2048]{1,0:T(2,128)(2,1)S(1)}, bf16[2,2048]{1,0:T(2,128)(2,1)S(1)}, u32[]{:S(2)}, u32[]{:S(2)}) %collective-permute-start.24) | collective-permute-done | bytes 8224 | tf_op jit(solution)/shard_map/ppermute | solution.py:49
  68.7 0.6 add_convert_fusion
  (14 shorter events, 0.1 us)
Async XLA Ops:
  0.0 8.4 %collective-permute-start = (bf16[2,2048]{1,0:T(2,128)(2,1)}, bf16[2,2048]{1,0:T(2,128)(2,1)S(1)}, u32[]{:S(2)}, u32[]{:S(2)}) collective-permute-start(bf16[2,2048]{1,0:T(2,128)(2,1)} %refs_5_.1), channel_id=1, source_target_pairs={{0,4},{4,0},{8,12},{12,8},{1,5},{5,1},{9,13},{13,9},{2,6},{6,2},{1... | collective-permute-start | bytes 24584 | tf_op jit(solution)/shard_map/ppermute | solution.py:30
  3.0 5.4 %collective-permute-start.1 = (bf16[2,2048]{1,0:T(2,128)(2,1)}, bf16[2,2048]{1,0:T(2,128)(2,1)S(1)}, u32[]{:S(2)}, u32[]{:S(2)}) collective-permute-start(bf16[2,2048]{1,0:T(2,128)(2,1)} %refs_5_.1), channel_id=1, source_target_pairs={{0,8},{4,12},{8,0},{12,4},{1,9},{5,13},{9,1},{13,5},{2,10},{6,14},... | collective-permute-start | bytes 24584 | tf_op jit(solution)/shard_map/ppermute | solution.py:30
  5.6 5.7 %collective-permute-start.2 = (bf16[2,2048]{1,0:T(2,128)(2,1)}, bf16[2,2048]{1,0:T(2,128)(2,1)S(1)}, u32[]{:S(2)}, u32[]{:S(2)}) collective-permute-start(bf16[2,2048]{1,0:T(2,128)(2,1)} %refs_5_.1), channel_id=1, source_target_pairs={{0,12},{4,8},{8,4},{12,0},{1,13},{5,9},{9,5},{13,1},{2,14},{6,10},... | collective-permute-start | bytes 24584 | tf_op jit(solution)/shard_map/ppermute | solution.py:30
  5.6 8.4 %copy-start.2 = (s32[8]{0:T(128)S(1)}, s32[8]{0:T(128)}, u32[]{:S(2)}) copy-start(s32[8]{0:T(128)} %param.23) | copy-start | bytes 100
  12.1 4.4 %collective-permute-start.3 = (bf16[2,1408]{1,0:T(2,128)(2,1)S(1)}, bf16[2,1408]{1,0:T(2,128)(2,1)S(1)}, u32[]{:S(2)}, u32[]{:S(2)}) collective-permute-start(bf16[2,1408]{1,0:T(2,128)(2,1)S(1)} %get-tuple-element.55), channel_id=1, source_target_pairs={{0,5},{1,4},{2,7},{3,6},{4,1},{5,0},{6,3},{7,2},{8,13},{9,12},{10,... | collective-permute-start | bytes 16904 | tf_op jit(solution)/shard_map/ppermute | solution.py:49
  12.2 4.4 %collective-permute-start.4 = (bf16[2,1408]{1,0:T(2,128)(2,1)S(1)}, bf16[2,1408]{1,0:T(2,128)(2,1)S(1)}, u32[]{:S(2)}, u32[]{:S(2)}) collective-permute-start(bf16[2,1408]{1,0:T(2,128)(2,1)S(1)} %get-tuple-element.56), channel_id=1, source_target_pairs={{0,9},{1,8},{2,11},{3,10},{4,13},{5,12},{6,15},{7,14},{8,1},{9,0},... | collective-permute-start | bytes 16904 | tf_op jit(solution)/shard_map/ppermute | solution.py:49
  13.4 4.8 %collective-permute-start.5 = (bf16[2,1408]{1,0:T(2,128)(2,1)S(1)}, bf16[2,1408]{1,0:T(2,128)(2,1)S(1)}, u32[]{:S(2)}, u32[]{:S(2)}) collective-permute-start(bf16[2,1408]{1,0:T(2,128)(2,1)S(1)} %get-tuple-element.57), channel_id=1, source_target_pairs={{0,13},{1,12},{2,15},{3,14},{4,9},{5,8},{6,11},{7,10},{8,5},{9,4},... | collective-permute-start | bytes 16904 | tf_op jit(solution)/shard_map/ppermute | solution.py:49
  14.1 23.7 %copy-start = (bf16[2048,3584]{1,0:T(8,128)(2,1)S(1)}, bf16[2048,3584]{1,0:T(8,128)(2,1)}, u32[]{:S(2)}) copy-start(bf16[2048,3584]{1,0:T(8,128)(2,1)} %up_ref.3) | copy-start | bytes 44040196
  18.3 4.6 %collective-permute-start.6 = (bf16[8,1408]{1,0:T(8,128)(2,1)S(1)}, bf16[8,1408]{1,0:T(8,128)(2,1)S(1)}, u32[]{:S(2)}, u32[]{:S(2)}) collective-permute-start(bf16[8,1408]{1,0:T(8,128)(2,1)S(1)} %stack.1.refs_1_.refs_0_), channel_id=1, source_target_pairs={{0,1},{1,0},{2,3},{3,2},{4,5},{5,4},{6,7},{7,6},{8,9},{9,8},{10,11... | collective-permute-start | bytes 67592 | tf_op jit(solution)/shard_map/ppermute | solution.py:30
  19.0 3.8 %collective-permute-start.7 = (bf16[8,1408]{1,0:T(8,128)(2,1)S(1)}, bf16[8,1408]{1,0:T(8,128)(2,1)S(1)}, u32[]{:S(2)}, u32[]{:S(2)}) collective-permute-start(bf16[8,1408]{1,0:T(8,128)(2,1)S(1)} %stack.1.refs_1_.refs_0_), channel_id=1, source_target_pairs={{0,2},{1,3},{2,0},{3,1},{4,6},{5,7},{6,4},{7,5},{8,10},{9,11},{10,... | collective-permute-start | bytes 67592 | tf_op jit(solution)/shard_map/ppermute | solution.py:30
  20.5 3.4 %collective-permute-start.8 = (bf16[8,1408]{1,0:T(8,128)(2,1)S(1)}, bf16[8,1408]{1,0:T(8,128)(2,1)S(1)}, u32[]{:S(2)}, u32[]{:S(2)}) collective-permute-start(bf16[8,1408]{1,0:T(8,128)(2,1)S(1)} %stack.1.refs_1_.refs_0_), channel_id=1, source_target_pairs={{0,3},{1,2},{2,1},{3,0},{4,7},{5,6},{6,5},{7,4},{8,11},{9,10},{10,... | collective-permute-start | bytes 67592 | tf_op jit(solution)/shard_map/ppermute | solution.py:30
  25.8 4.3 %collective-permute-start.10 = (bf16[64,256]{1,0:T(8,128)(2,1)S(1)}, bf16[64,256]{1,0:T(8,128)(2,1)S(1)}, u32[]{:S(2)}, u32[]{:S(2)}) collective-permute-start(bf16[64,256]{1,0:T(8,128)(2,1)S(1)} %attend.1.refs_0_), channel_id=1, source_target_pairs={{0,2},{1,3},{2,0},{3,1},{4,6},{5,7},{6,4},{7,5},{8,10},{9,11},{10,... | collective-permute-start | bytes 98312 | tf_op jit(solution)/shard_map/ppermute | solution.py:30
  26.4 3.7 %collective-permute-start.11 = (bf16[64,256]{1,0:T(8,128)(2,1)S(1)}, bf16[64,256]{1,0:T(8,128)(2,1)S(1)}, u32[]{:S(2)}, u32[]{:S(2)}) collective-permute-start(bf16[64,256]{1,0:T(8,128)(2,1)S(1)} %attend.1.refs_0_), channel_id=1, source_target_pairs={{0,3},{1,2},{2,1},{3,0},{4,7},{5,6},{6,5},{7,4},{8,11},{9,10},{10,... | collective-permute-start | bytes 98312 | tf_op jit(solution)/shard_map/ppermute | solution.py:30
  27.4 2.7 %collective-permute-start.9 = (bf16[64,256]{1,0:T(8,128)(2,1)S(1)}, bf16[64,256]{1,0:T(8,128)(2,1)S(1)}, u32[]{:S(2)}, u32[]{:S(2)}) collective-permute-start(bf16[64,256]{1,0:T(8,128)(2,1)S(1)} %attend.1.refs_0_), channel_id=1, source_target_pairs={{0,1},{1,0},{2,3},{3,2},{4,5},{5,4},{6,7},{7,6},{8,9},{9,8},{10,11... | collective-permute-start | bytes 98312 | tf_op jit(solution)/shard_map/ppermute | solution.py:30
  30.4 4.3 %collective-permute-start.12 = (bf16[2,1024]{1,0:T(2,128)(2,1)S(1)}, bf16[2,1024]{1,0:T(2,128)(2,1)S(1)}, u32[]{:S(2)}, u32[]{:S(2)}) collective-permute-start(bf16[2,1024]{1,0:T(2,128)(2,1)S(1)} %get-tuple-element.70), channel_id=1, source_target_pairs={{0,5},{1,4},{2,7},{3,6},{4,1},{5,0},{6,3},{7,2},{8,13},{9,12},{10,... | collective-permute-start | bytes 12296 | tf_op jit(solution)/shard_map/ppermute | solution.py:49
  30.5 4.2 %collective-permute-start.13 = (bf16[2,1024]{1,0:T(2,128)(2,1)S(1)}, bf16[2,1024]{1,0:T(2,128)(2,1)S(1)}, u32[]{:S(2)}, u32[]{:S(2)}) collective-permute-start(bf16[2,1024]{1,0:T(2,128)(2,1)S(1)} %get-tuple-element.71), channel_id=1, source_target_pairs={{0,9},{1,8},{2,11},{3,10},{4,13},{5,12},{6,15},{7,14},{8,1},{9,0},... | collective-permute-start | bytes 12296 | tf_op jit(solution)/shard_map/ppermute | solution.py:49
  32.9 4.8 %collective-permute-start.14 = (bf16[2,1024]{1,0:T(2,128)(2,1)S(1)}, bf16[2,1024]{1,0:T(2,128)(2,1)S(1)}, u32[]{:S(2)}, u32[]{:S(2)}) collective-permute-start(bf16[2,1024]{1,0:T(2,128)(2,1)S(1)} %get-tuple-element.72), channel_id=1, source_target_pairs={{0,13},{1,12},{2,15},{3,14},{4,9},{5,8},{6,11},{7,10},{8,5},{9,4},... | collective-permute-start | bytes 12296 | tf_op jit(solution)/shard_map/ppermute | solution.py:49
  37.8 8.9 %copy-start.1 = (bf16[2048,3584]{1,0:T(8,128)(2,1)S(1)}, bf16[2048,3584]{1,0:T(8,128)(2,1)}, u32[]{:S(2)}) copy-start(bf16[2048,3584]{1,0:T(8,128)(2,1)} %gate_ref.3) | copy-start | bytes 44040196
  38.7 4.4 %collective-permute-start.15 = (bf16[8,2048]{1,0:T(8,128)(2,1)S(1)}, bf16[8,2048]{1,0:T(8,128)(2,1)S(1)}, u32[]{:S(2)}, u32[]{:S(2)}) collective-permute-start(bf16[8,2048]{1,0:T(8,128)(2,1)S(1)} %get-tuple-element.74), channel_id=1, source_target_pairs={{0,4},{1,5},{2,6},{3,7},{4,0},{5,1},{6,2},{7,3},{8,12},{9,13},{10,... | collective-permute-start | bytes 98312 | tf_op jit(solution)/shard_map/ppermute | solution.py:49
  38.7 5.5 %collective-permute-start.16 = (bf16[8,2048]{1,0:T(8,128)(2,1)S(1)}, bf16[8,2048]{1,0:T(8,128)(2,1)S(1)}, u32[]{:S(2)}, u32[]{:S(2)}) collective-permute-start(bf16[8,2048]{1,0:T(8,128)(2,1)S(1)} %get-tuple-element.75), channel_id=1, source_target_pairs={{0,8},{1,9},{2,10},{3,11},{4,12},{5,13},{6,14},{7,15},{8,0},{9,1},... | collective-permute-start | bytes 98312 | tf_op jit(solution)/shard_map/ppermute | solution.py:49
  40.9 5.7 %collective-permute-start.17 = (bf16[8,2048]{1,0:T(8,128)(2,1)S(1)}, bf16[8,2048]{1,0:T(8,128)(2,1)S(1)}, u32[]{:S(2)}, u32[]{:S(2)}) collective-permute-start(bf16[8,2048]{1,0:T(8,128)(2,1)S(1)} %get-tuple-element.76), channel_id=1, source_target_pairs={{0,12},{1,13},{2,14},{3,15},{4,8},{5,9},{6,10},{7,11},{8,4},{9,5},... | collective-permute-start | bytes 98312 | tf_op jit(solution)/shard_map/ppermute | solution.py:49
  49.9 3.1 %collective-permute-start.20 = (bf16[8,3712]{1,0:T(8,128)(2,1)S(1)}, bf16[8,3712]{1,0:T(8,128)(2,1)S(1)}, u32[]{:S(2)}, u32[]{:S(2)}) collective-permute-start(bf16[8,3712]{1,0:T(8,128)(2,1)S(1)} %get-tuple-element.81.first_ref), channel_id=1, source_target_pairs={{0,1},{1,0},{2,3},{3,2},{4,5},{5,4},{6,7},{7,6},{8,9},{9,8},{10,11... | collective-permute-start | bytes 178184 | tf_op jit(solution)/shard_map/ppermute | solution.py:30
  52.5 2.1 %collective-permute-start.18 = (bf16[8,3584]{1,0:T(8,128)(2,1)S(1)}, bf16[8,3584]{1,0:T(8,128)(2,1)S(1)}, u32[]{:S(2)}, u32[]{:S(2)}) collective-permute-start(bf16[8,3584]{1,0:T(8,128)(2,1)S(1)} %get-tuple-element.79.first_ref), channel_id=1, source_target_pairs={{0,1},{1,0},{2,3},{3,2},{4,5},{5,4},{6,7},{7,6},{8,9},{9,8},{10,11... | collective-permute-start | bytes 172040 | tf_op jit(solution)/shard_map/ppermute | solution.py:30
  53.0 4.9 %collective-permute-start.21 = (bf16[8,3712]{1,0:T(8,128)(2,1)S(1)}, bf16[8,3712]{1,0:T(8,128)(2,1)S(1)}, u32[]{:S(2)}, u32[]{:S(2)}) collective-permute-start(bf16[8,3712]{1,0:T(8,128)(2,1)S(1)} %pair_sum.3.near_ref), channel_id=1, source_target_pairs={{0,2},{1,3},{2,0},{3,1},{4,6},{5,7},{6,4},{7,5},{8,10},{9,11},{10,... | collective-permute-start | bytes 178184 | tf_op jit(solution)/shard_map/ppermute | solution.py:30
  54.5 4.7 %collective-permute-start.19 = (bf16[8,3584]{1,0:T(8,128)(2,1)S(1)}, bf16[8,3584]{1,0:T(8,128)(2,1)S(1)}, u32[]{:S(2)}, u32[]{:S(2)}) collective-permute-start(bf16[8,3584]{1,0:T(8,128)(2,1)S(1)} %pair_sum.2.refs_1_.near_ref), channel_id=1, source_target_pairs={{0,2},{1,3},{2,0},{3,1},{4,6},{5,7},{6,4},{7,5},{8,10},{9,11},{10,... | collective-permute-start | bytes 172040 | tf_op jit(solution)/shard_map/ppermute | solution.py:30
  60.6 4.5 %collective-permute-start.22 = (bf16[2,2048]{1,0:T(2,128)(2,1)S(1)}, bf16[2,2048]{1,0:T(2,128)(2,1)S(1)}, u32[]{:S(2)}, u32[]{:S(2)}) collective-permute-start(bf16[2,2048]{1,0:T(2,128)(2,1)S(1)} %get-tuple-element.86), channel_id=1, source_target_pairs={{0,4},{1,5},{2,6},{3,7},{4,0},{5,1},{6,2},{7,3},{8,12},{9,13},{10,... | collective-permute-start | bytes 24584 | tf_op jit(solution)/shard_map/ppermute | solution.py:49
  60.6 4.7 %collective-permute-start.23 = (bf16[2,2048]{1,0:T(2,128)(2,1)S(1)}, bf16[2,2048]{1,0:T(2,128)(2,1)S(1)}, u32[]{:S(2)}, u32[]{:S(2)}) collective-permute-start(bf16[2,2048]{1,0:T(2,128)(2,1)S(1)} %get-tuple-element.87), channel_id=1, source_target_pairs={{0,8},{1,9},{2,10},{3,11},{4,12},{5,13},{6,14},{7,15},{8,0},{9,1},... | collective-permute-start | bytes 24584 | tf_op jit(solution)/shard_map/ppermute | solution.py:49
  63.2 5.4 %collective-permute-start.24 = (bf16[2,2048]{1,0:T(2,128)(2,1)S(1)}, bf16[2,2048]{1,0:T(2,128)(2,1)S(1)}, u32[]{:S(2)}, u32[]{:S(2)}) collective-permute-start(bf16[2,2048]{1,0:T(2,128)(2,1)S(1)} %get-tuple-element.88), channel_id=1, source_target_pairs={{0,12},{1,13},{2,14},{3,15},{4,8},{5,9},{6,10},{7,11},{8,4},{9,5},... | collective-permute-start | bytes 24584 | tf_op jit(solution)/shard_map/ppermute | solution.py:49

commit v8 on v7

--- a/solution.py
+++ b/solution.py
@@ -171,11 +171,10 @@
 def qkv_kernel(slots, gain_ref, wq_ref, wkv_ref, *refs):
     rows_ref = refs[slots]
     out_s, rows_s = refs[-2:]
-    wide = join_rows(refs[:slots], rows_s)
+    wide = join_rows(refs[:slots][::-1], rows_s)
     rows_ref[...] = wide
     total = jnp.sum(wide * wide, axis=1, keepdims=True)
-    gain = gain_ref[...].astype(jnp.float32)[None, :]
-    scaled = (wide * gain).astype(jnp.bfloat16)
+    scaled = (wide * gain_ref[...].astype(jnp.float32)).astype(jnp.bfloat16)
     query_cols = wq_ref.shape[1]
     kv_cols = wkv_ref.shape[1]
 
@@ -208,11 +207,11 @@
         ],
         compiler_params=params(2),
         name="project_qkv",
-    )(gain, resident(w_query), resident(w_kv), *rows)
+    )(gain, resident(w_query), resident(w_kv), *rows[::-1])
 
 
 def stack_kernel(*refs):
-    refs[-2][...] = join_rows(refs[:-2], refs[-1]).astype(refs[-2].dtype)
+    refs[-2][...] = join_rows(refs[:-2][::-1], refs[-1]).astype(refs[-2].dtype)
 
 
 def stack(pieces):
@@ -225,7 +224,7 @@
         scratch_shapes=[pltpu.VMEM(shape, jnp.float32)],
         compiler_params=params(1),
         name="stack",
-    )(*pieces)
+    )(*pieces[::-1])
 
 
 def attend_kernel(
@@ -342,7 +341,7 @@
         ],
         compiler_params=params(6),
         name="attend",
-    )(lengths, cosine, sine, resident(keys), resident(values), *parts)
+    )(lengths, cosine, sine, resident(keys), resident(values), *parts[::-1])
 
 
 def combine_kernel(shards, slots, *refs):
@@ -380,7 +379,7 @@
         scratch_shapes=[pltpu.VMEM((all_rows, columns), jnp.float32)],
         compiler_params=params(2),
         name="combine",
-    )(*parts, *[resident(w) for w in later])
+    )(*parts[::-1], *[resident(w) for w in later])
 
 
 def turned(block, step, own_rows):
@@ -395,7 +394,7 @@
 
 
 def out_kernel(slots, later, weight_ref, *refs):
-    pieces = refs[:slots]
+    pieces = refs[:slots][::-1]
     outs = refs[slots + later : 2 * slots + later]
     left_s = refs[-1]
     own_rows = pieces[0].shape[0]
@@ -425,7 +424,7 @@
         scratch_shapes=[pltpu.VMEM((own_rows * slots, depth), jnp.float32)],
         compiler_params=params(3),
         name="project_out",
-    )(resident(weight), *pieces, *[resident(w) for w in later])
+    )(resident(weight), *pieces[::-1], *[resident(w) for w in later])
 
 
 def pair_kernel(first_ref, second_ref, out_ref):
@@ -471,7 +470,7 @@
     updated_ref[...] = wide[:own_rows]
     squares = jnp.sum(wide * wide, axis=1, keepdims=True)
     out_ref[:, 2 * count :] = squares_block(squares).astype(jnp.bfloat16)
-    scaled = (wide * gain_ref[...].astype(jnp.float32)[None, :]).astype(jnp.bfloat16)
+    scaled = (wide * gain_ref[...].astype(jnp.float32)).astype(jnp.bfloat16)
     scaled_ref[...] = scaled
     gate_up_tiles(scaled, gate_ref, up_ref, out_ref, 0, count)
     for copy in copies:
@@ -501,7 +500,7 @@
         resident(w_gate),
         resident(w_up),
         in_hbm(w_down),
-        *parts,
+        *parts[::-1],
         *[resident(w) for w in later],
     )
 
@@ -650,7 +649,7 @@
     own, attn_gain, ffn_gain, w_kv, w_query = load(
         states, attn_gain, ffn_gain, w_kv, w_query, after=states
     )
-    rows, *pieces = project_qkv([own] + got[1:], attn_gain, w_query, w_kv)
+    rows, *pieces = project_qkv([own] + got[1:], attn_gain[None, :], w_query, w_kv)
 
     rows, lengths = lax.optimization_barrier((rows, lengths))
     my_lengths = lax.dynamic_slice_in_dim(lengths, tensor_index * own_rows, own_rows, 0)
@@ -661,7 +660,7 @@
     joined = stack(scatter_slots(pieces, 1))
     joined, keys, values = lax.optimization_barrier((joined, keys, values))
     (w_out,) = load(w_out, after=joined)
-    parts, w_out = lax.optimization_barrier((exchange(joined, "inner"), w_out))
+    parts, w_out = lax.optimization_barrier((exchange(joined, "inner")[::-1], w_out))
     shard = attend(my_lengths, cosine, sine, parts, keys, values, slots)
 
     pieces = combine(exchange(shard, "inner"), [], all_rows, slots)
@@ -669,12 +668,12 @@
 
     tiles = w_gate.shape[1] // LANES
     half = (tiles + 1) // 2
-    span = tiles * 9 // 28
     first = half * LANES
-    starts = [0, span * LANES, (span + max(span, half - span + 1)) * LANES, tiles * LANES]
+    span = tiles // 4
+    starts = [0, span * LANES, (span + max(tiles * 9 // 28, half - span + 1)) * LANES, tiles * LANES]
     spans = [(a, b - a) for a, b in zip(starts, starts[1:])]
     one, updated, scaled, down_one = first_gate_up(
-        rows, ffn_gain, parts, w_gate, w_up, w_down, spans[0], [], first, own_rows
+        rows, ffn_gain[None, :], parts, w_gate, w_up, w_down, spans[0], [], first, own_rows
     )
     two, down_two = second_gate_up(scaled, w_gate, w_up, w_down, spans[1], first)
     steps = steps_up(lax.axis_size("inner"))
@@ -689,7 +688,7 @@
         two, swap_with(two, "inner", steps[-1]), down_two, down_three, part, scale, slots
     )
     parts = scatter_slots(pieces, 0)
-    down_sum = sum(p.astype(jnp.float32) for p in parts)
+    down_sum = sum(p.astype(jnp.float32) for p in parts[::-1])
     return (updated + down_sum).astype(jnp.bfloat16)
 
 

time: 69.5 us -> 69.4 us (level)
  waiting for transfers between devices: 18.1 us -> 11.2 us
  local copies, waits for them, and re-layouts: 0.09 us -> 4.25 us
  starting transfers between devices: 28 us -> 30.4 us
    unnamed x6 -> x10, local copies, waits for them, and re-layouts: 0.01 us -> 4.16 us
    ppermute x12, waiting for transfers between devices: 12 us -> 8.01 us  [scatter_slots(): got.append(lax.ppermute(pieces[k], ('tensor', 'inner'), pairs))]
    ppermute x13, waiting for transfers between devices: 6.12 us -> 3.23 us  [swap_with(): return lax.ppermute(value, axis, [(i, i ^ step) for i in range(count)])]
    ppermute x12, starting transfers between devices: 15 us -> 17.1 us  [scatter_slots(): got.append(lax.ppermute(pieces[k], ('tensor', 'inner'), pairs))]
  transfers between devices with their start and end apart: 25 -> 25, of which waited for: 9 -> 11; matrix products, arithmetic and copies ran while one was open for 0% -> 0% of each run, Pallas kernels for 20% -> 20%
where the time goes in v8:
time: 69.4 us; the launch traced here: 69.2 us
  starting transfers between devices  30.4 us (44%)
  Pallas kernels  22.4 us (32%)
  waiting for transfers between devices  11.2 us (16%)
  local copies, waits for them, and re-layouts  4.25 us (6%)
  other arithmetic  0.81 us (1%)
    ppermute x12, starting transfers between devices, scatter_slots(): got.append(lax.ppermute(pieces[k], ('tensor', 'inner'), pairs))  17.1 us
    ppermute x13, starting transfers between devices, swap_with(): return lax.ppermute(value, axis, [(i, i ^ step) for i in range(count)])  13.3 us
    pallas_call x4, Pallas kernels, load(): pl.pallas_call(functools.partial(load_kernel, spans), out_shape=tuple((pl...  10.2 us
    ppermute x12, waiting for transfers between devices, scatter_slots(): got.append(lax.ppermute(pieces[k], ('tensor', 'inner'), pairs))  8.01 us
    unnamed x10, local copies, waits for them, and re-layouts  4.16 us
    ppermute x13, waiting for transfers between devices, swap_with(): return lax.ppermute(value, axis, [(i, i ^ step) for i in range(count)])  3.23 us
    pallas_call x1, Pallas kernels, first_gate_up(): pl.pallas_call(functools.partial(first_gate_up_kernel, slots, count, star...  3.22 us
    pallas_call x1, Pallas kernels, second_gate_up(): pl.pallas_call(functools.partial(second_gate_up_kernel, first, count, sta...  2.44 us
  transfers between devices with their start and end apart: 25, of which 11 were waited for; matrix products, arithmetic and copies ran while one was open for 0% of the time, Pallas kernels for 20%

profile of v8, /device:TPU:0, one launch (start us, length us, event | category | flops | bytes accessed | tf_op | source)
XLA Modules:
  0.0 69.2 jit_solution(12250787300407880402)
XLA Ops:
  0.0 5.0 %collective-permute-start = (bf16[2,2048]{1,0:T(2,128)(2,1)}, bf16[2,2048]{1,0:T(2,128)(2,1)S(1)}, u32[]{:S(2)}, u32[]{:S(2)}) collective-permute-start(bf16[2,2048]{1,0:T(2,128)(2,1)} %refs_5_.1), channel_id=1, source_target_pairs={{0,12},{4,8},{8,4},{12,0},{1,13},{5,9},{9,5},{13,1},{2,14},{6,10},... | collective-permute-start | bytes 24584 | tf_op jit(solution)/shard_map/ppermute | solution.py:30
  5.0 0.0 collective-permute-start.1
  5.1 0.6 collective-permute-start.2
  5.6 2.7 %load.4 = (bf16[2,2048]{1,0:T(2,128)(2,1)S(1)}, bf16[2048]{0:T(1024)(128)(2,1)S(1)}, bf16[2048]{0:T(1024)(128)(2,1)S(1)}, bf16[2048,256]{1,0:T(8,128)(2,1)S(1)}, bf16[2048,1024]{1,0:T(8,128)(2,1)S(1)}) custom-call(bf16[2,2048]{1,0:T(2,128)(2,1)} %refs_5_.1, bf16[2048]{0:T(1024)(128)(2,1)} %refs_1_.1, bf16[2048]{0:T(1024)(128)(2,1)} %refs_2_.1, ...), custom_call_target="tpu_custom_call" | custom-call | bytes 5259264 | tf_op jit(solution)/shard_map/load/pallas_call | solution.py:144
  8.4 2.0 %copy-done.2 = bf16[2048,1024]{1,0:T(8,128)(2,1)} copy-done((bf16[2048,1024]{1,0:T(8,128)(2,1)}, bf16[2048,1024]{1,0:T(8,128)(2,1)S(1)}, u32[]{:S(2)}) %copy-start.2) | copy-done | bytes 4194328
  10.3 0.0 collective-permute-done.refs_0_
  10.4 0.0 collective-permute-done.1.refs_1_
  10.4 0.0 collective-permute-done.2.refs_2_
  10.4 2.2 %copy-done.3 = bf16[2048,1024]{1,0:T(8,128)(2,1)S(1)} copy-done((bf16[2048,1024]{1,0:T(8,128)(2,1)S(1)}, bf16[2048,1024]{1,0:T(8,128)(2,1)}, u32[]{:S(2)}) %copy-start.3) | copy-done | bytes 4194328
  12.6 0.8 %project_qkv.1 = (f32[8,2048]{1,0:T(8,128)S(1)}, bf16[2,1408]{1,0:T(2,128)(2,1)S(1)}, bf16[2,1408]{1,0:T(2,128)(2,1)S(1)}, bf16[2,1408]{1,0:T(2,128)(2,1)S(1)}, bf16[2,1408]{1,0:T(2,128)(2,1)S(1)}) custom-call(bf16[1,2048]{1,0:T(2,128)(2,1)S(1)} %broadcast_in_dim.23.gain_ref, bf16[2048,1024]{1,0:T(8,128)(2,1)S(1)} %copy-done.3, ...), custom_call_target="tpu_custom_call" | custom-call | tf_op jit(solution)/shard_map/project_qkv/pallas_call | solution.py:196
  13.4 2.5 %collective-permute-start.3 = (bf16[2,1408]{1,0:T(2,128)(2,1)S(1)}, bf16[2,1408]{1,0:T(2,128)(2,1)S(1)}, u32[]{:S(2)}, u32[]{:S(2)}) collective-permute-start(bf16[2,1408]{1,0:T(2,128)(2,1)S(1)} %get-tuple-element.54), channel_id=1, source_target_pairs={{0,13},{1,12},{2,15},{3,14},{4,9},{5,8},{6,11},{7,10},{8,5},{9,4},... | collective-permute-start | bytes 16904 | tf_op jit(solution)/shard_map/ppermute | solution.py:49
  15.9 0.2 collective-permute-start.4
  16.1 1.5 %collective-permute-start.5 = (bf16[2,1408]{1,0:T(2,128)(2,1)S(1)}, bf16[2,1408]{1,0:T(2,128)(2,1)S(1)}, u32[]{:S(2)}, u32[]{:S(2)}) collective-permute-start(bf16[2,1408]{1,0:T(2,128)(2,1)S(1)} %get-tuple-element.56), channel_id=1, source_target_pairs={{0,5},{1,4},{2,7},{3,6},{4,1},{5,0},{6,3},{7,2},{8,13},{9,12},{10,... | collective-permute-start | bytes 16904 | tf_op jit(solution)/shard_map/ppermute | solution.py:49
  17.7 0.1 fusion.4
  17.7 2.4 %load.5 = (bf16[2,4096,128]{2,1,0:T(8,128)(2,1)S(1)}, bf16[2,4096,128]{2,1,0:T(8,128)(2,1)S(1)}) custom-call(bf16[2,4096,128]{2,1,0:T(8,128)(2,1)} %bitcast.6, bf16[2,4096,128]{2,1,0:T(8,128)(2,1)} %bitcast.7, f32[8,2048]{1,0:T(8,128)S(1)} %get-tuple-element.52.refs_2_.rows_ref), custom_call_target="tpu_custom_call" | custom-call | bytes 4194304 | tf_op jit(solution)/shard_map/load/pallas_call | solution.py:144
  20.2 0.0 collective-permute-done.3.refs_0_
  20.2 0.0 collective-permute-done.4.refs_1_
  20.2 2.3 %collective-permute-start.6 = (bf16[8,1408]{1,0:T(8,128)(2,1)S(1)}, bf16[8,1408]{1,0:T(8,128)(2,1)S(1)}, u32[]{:S(2)}, u32[]{:S(2)}) collective-permute-start(bf16[8,1408]{1,0:T(8,128)(2,1)S(1)} %stack.1.refs_1_.refs_0_), channel_id=1, source_target_pairs={{0,3},{1,2},{2,1},{3,0},{4,7},{5,6},{6,5},{7,4},{8,11},{9,10},{10,... | collective-permute-start | bytes 67592 | tf_op jit(solution)/shard_map/ppermute | solution.py:30
  22.5 0.5 collective-permute-start.7
  23.1 0.0 collective-permute-start.8
  23.1 0.1 fusion
  23.2 2.2 %load.6.weight_ref = bf16[1024,2048]{1,0:T(8,128)(2,1)S(1)} custom-call(bf16[1024,2048]{1,0:T(8,128)(2,1)} %refs_0_.4, bf16[8,1408]{1,0:T(8,128)(2,1)S(1)} %stack.1.refs_1_.refs_0_), custom_call_target="tpu_custom_call" | custom-call | bytes 4194304 | tf_op jit(solution)/shard_map/load/pallas_call | solution.py:144
  25.4 0.9 %collective-permute-done.7.refs_2_ = bf16[8,1408]{1,0:T(8,128)(2,1)S(1)} collective-permute-done((bf16[8,1408]{1,0:T(8,128)(2,1)S(1)}, bf16[8,1408]{1,0:T(8,128)(2,1)S(1)}, u32[]{:S(2)}, u32[]{:S(2)}) %collective-permute-start.7) | collective-permute-done | bytes 22560 | tf_op jit(solution)/shard_map/ppermute | solution.py:30
  26.4 0.0 collective-permute-done.8.refs_1_
  26.4 0.1 broadcast_in_dim.25.lengths_ref
  26.4 1.7 %attend.1.refs_3_ = bf16[64,256]{1,0:T(8,128)(2,1)S(1)} custom-call(s32[2,128]{1,0:T(2,128)S(1)} %broadcast_in_dim.25.lengths_ref, f32[8,128]{1,0:T(8,128)S(1)} %bitcast.4, f32[8,128]{1,0:T(8,128)S(1)} %bitcast.5, bf16[2,4096,128]{2,1,0:T(8,128)(2,1)S(1)} %get-tuple-element.63.key_ref, bf16[2,4096,128]{2,1,0:T(8,128)(2,1)S(1)} %get-tuple-element.64.value_ref, ...), custom_call_target="tpu_custom_call" | custom-call | tf_op jit(solution)/shard_map/attend/pallas_call | solution.py:330
  28.2 0.7 collective-permute-start.10
  28.8 0.2 collective-permute-start.11
  29.1 1.3 %collective-permute-start.9 = (bf16[64,256]{1,0:T(8,128)(2,1)S(1)}, bf16[64,256]{1,0:T(8,128)(2,1)S(1)}, u32[]{:S(2)}, u32[]{:S(2)}) collective-permute-start(bf16[64,256]{1,0:T(8,128)(2,1)S(1)} %attend.1.refs_3_), channel_id=1, source_target_pairs={{0,3},{1,2},{2,1},{3,0},{4,7},{5,6},{6,5},{7,4},{8,11},{9,10},{10,... | collective-permute-start | bytes 98312 | tf_op jit(solution)/shard_map/ppermute | solution.py:30
  30.4 1.9 %collective-permute-done.10.refs_1_ = bf16[64,256]{1,0:T(8,128)(2,1)S(1)} collective-permute-done((bf16[64,256]{1,0:T(8,128)(2,1)S(1)}, bf16[64,256]{1,0:T(8,128)(2,1)S(1)}, u32[]{:S(2)}, u32[]{:S(2)}) %collective-permute-start.10) | collective-permute-done | bytes 32800 | tf_op jit(solution)/shard_map/ppermute | solution.py:30
  32.3 0.0 collective-permute-done.11.refs_2_
  32.3 0.2 collective-permute-done.9.refs_0_
  32.5 0.3 combine.1
  32.8 3.2 %collective-permute-start.12 = (bf16[2,1024]{1,0:T(2,128)(2,1)S(1)}, bf16[2,1024]{1,0:T(2,128)(2,1)S(1)}, u32[]{:S(2)}, u32[]{:S(2)}) collective-permute-start(bf16[2,1024]{1,0:T(2,128)(2,1)S(1)} %get-tuple-element.69), channel_id=1, source_target_pairs={{0,13},{1,12},{2,15},{3,14},{4,9},{5,8},{6,11},{7,10},{8,5},{9,4},... | collective-permute-start | bytes 12296 | tf_op jit(solution)/shard_map/ppermute | solution.py:49
  36.0 0.0 collective-permute-start.13
  36.0 0.8 %collective-permute-start.14 = (bf16[2,1024]{1,0:T(2,128)(2,1)S(1)}, bf16[2,1024]{1,0:T(2,128)(2,1)S(1)}, u32[]{:S(2)}, u32[]{:S(2)}) collective-permute-start(bf16[2,1024]{1,0:T(2,128)(2,1)S(1)} %get-tuple-element.71), channel_id=1, source_target_pairs={{0,5},{1,4},{2,7},{3,6},{4,1},{5,0},{6,3},{7,2},{8,13},{9,12},{10,... | collective-permute-start | bytes 12296 | tf_op jit(solution)/shard_map/ppermute | solution.py:49
  36.7 0.9 %collective-permute-done.12.refs_0_ = bf16[2,1024]{1,0:T(2,128)(2,1)S(1)} collective-permute-done((bf16[2,1024]{1,0:T(2,128)(2,1)S(1)}, bf16[2,1024]{1,0:T(2,128)(2,1)S(1)}, u32[]{:S(2)}, u32[]{:S(2)}) %collective-permute-start.12) | collective-permute-done | bytes 4128 | tf_op jit(solution)/shard_map/ppermute | solution.py:49
  37.7 2.2 %collective-permute-done.13.refs_1_ = bf16[2,1024]{1,0:T(2,128)(2,1)S(1)} collective-permute-done((bf16[2,1024]{1,0:T(2,128)(2,1)S(1)}, bf16[2,1024]{1,0:T(2,128)(2,1)S(1)}, u32[]{:S(2)}, u32[]{:S(2)}) %collective-permute-start.13) | collective-permute-done | bytes 4128 | tf_op jit(solution)/shard_map/ppermute | solution.py:49
  39.9 0.0 collective-permute-done.14.refs_2_
  39.9 1.0 %project_out.1 = (bf16[8,2048]{1,0:T(8,128)(2,1)S(1)}, bf16[8,2048]{1,0:T(8,128)(2,1)S(1)}, bf16[8,2048]{1,0:T(8,128)(2,1)S(1)}, bf16[8,2048]{1,0:T(8,128)(2,1)S(1)}) custom-call(bf16[1024,2048]{1,0:T(8,128)(2,1)S(1)} %load.6.weight_ref, bf16[2,1024]{1,0:T(2,128)(2,1)S(1)} %collective-permute-done.12.refs_0_, ...), custom_call_target="tpu_custom_call" | custom-call | tf_op jit(solution)/shard_map/project_out/pallas_call | solution.py:419
  40.8 1.5 %collective-permute-start.15 = (bf16[8,2048]{1,0:T(8,128)(2,1)S(1)}, bf16[8,2048]{1,0:T(8,128)(2,1)S(1)}, u32[]{:S(2)}, u32[]{:S(2)}) collective-permute-start(bf16[8,2048]{1,0:T(8,128)(2,1)S(1)} %get-tuple-element.73), channel_id=1, source_target_pairs={{0,12},{1,13},{2,14},{3,15},{4,8},{5,9},{6,10},{7,11},{8,4},{9,5},... | collective-permute-start | bytes 98312 | tf_op jit(solution)/shard_map/ppermute | solution.py:49
  42.4 0.6 collective-permute-start.16
  43.0 2.3 %collective-permute-start.17 = (bf16[8,2048]{1,0:T(8,128)(2,1)S(1)}, bf16[8,2048]{1,0:T(8,128)(2,1)S(1)}, u32[]{:S(2)}, u32[]{:S(2)}) collective-permute-start(bf16[8,2048]{1,0:T(8,128)(2,1)S(1)} %get-tuple-element.75), channel_id=1, source_target_pairs={{0,4},{1,5},{2,6},{3,7},{4,0},{5,1},{6,2},{7,3},{8,12},{9,13},{10,... | collective-permute-start | bytes 98312 | tf_op jit(solution)/shard_map/ppermute | solution.py:49
  45.3 1.6 %collective-permute-done.15.refs_0_ = bf16[8,2048]{1,0:T(8,128)(2,1)S(1)} collective-permute-done((bf16[8,2048]{1,0:T(8,128)(2,1)S(1)}, bf16[8,2048]{1,0:T(8,128)(2,1)S(1)}, u32[]{:S(2)}, u32[]{:S(2)}) %collective-permute-start.15) | collective-permute-done | bytes 32800 | tf_op jit(solution)/shard_map/ppermute | solution.py:49
  46.9 0.6 collective-permute-done.16.refs_1_
  47.5 0.3 collective-permute-done.17.refs_2_
  47.8 3.2 %first_gate_up.1 = (bf16[8,3712]{1,0:T(8,128)(2,1)S(1)}, f32[2,2048]{1,0:T(2,128)S(1)}, bf16[8,2048]{1,0:T(8,128)(2,1)S(1)}, bf16[896,2048]{1,0:T(8,128)(2,1)S(1)}) custom-call(f32[8,2048]{1,0:T(8,128)S(1)} %get-tuple-element.52.refs_2_.rows_ref, bf16[1,2048]{1,0:T(2,128)(2,1)S(1)} %broadcast_in_dim.24.gain_ref, bf16[2048,3584]{1,0:T(8,128)(2,1)S(1)} %copy-done.1, ...), custom_call_target="tpu_custom_call" | custom-call | flops 117440512 | bytes 14680064 | tf_op jit(solution)/shard_map/first_gate_up/pallas_call | solution.py:483
  51.0 0.1 collective-permute-start.20
  51.1 2.4 %second_gate_up.1 = (bf16[8,3584]{1,0:T(8,128)(2,1)S(1)}, bf16[1152,2048]{1,0:T(8,128)(2,1)S(1)}) custom-call(bf16[8,2048]{1,0:T(8,128)(2,1)S(1)} %get-tuple-element.78.scaled_ref, bf16[2048,3584]{1,0:T(8,128)(2,1)S(1)} %copy-done.1, bf16[2048,3584]{1,0:T(8,128)(2,1)S(1)} %copy-done, bf16[3584,2048]{1,0:T(8,128)(2,1)} %refs_0_.5), custom_call_target="tpu_custom_call" | custom-call | flops 117440512 | bytes 14680064 | tf_op jit(solution)/shard_map/second_gate_up/pallas_call | solution.py:522
  53.6 0.6 collective-permute-start.18
  54.1 0.7 %collective-permute-start.21 = (bf16[8,3712]{1,0:T(8,128)(2,1)S(1)}, bf16[8,3712]{1,0:T(8,128)(2,1)S(1)}, u32[]{:S(2)}, u32[]{:S(2)}) collective-permute-start(bf16[8,3712]{1,0:T(8,128)(2,1)S(1)} %pair_sum.3.near_ref), channel_id=1, source_target_pairs={{0,2},{1,3},{2,0},{3,1},{4,6},{5,7},{6,4},{7,5},{8,10},{9,11},{10,... | collective-permute-start | bytes 178184 | tf_op jit(solution)/shard_map/ppermute | solution.py:30
  54.9 0.2 collective-permute-done.18.second_ref
  55.0 1.3 %collective-permute-start.19 = (bf16[8,3584]{1,0:T(8,128)(2,1)S(1)}, bf16[8,3584]{1,0:T(8,128)(2,1)S(1)}, u32[]{:S(2)}, u32[]{:S(2)}) collective-permute-start(bf16[8,3584]{1,0:T(8,128)(2,1)S(1)} %pair_sum.2.refs_1_.near_ref), channel_id=1, source_target_pairs={{0,2},{1,3},{2,0},{3,1},{4,6},{5,7},{6,4},{7,5},{8,10},{9,11},{10,... | collective-permute-start | bytes 172040 | tf_op jit(solution)/shard_map/ppermute | solution.py:30
  56.3 2.9 %load.7.later_ref.three_ref = bf16[1536,2048]{1,0:T(8,128)(2,1)S(1)} custom-call(bf16[3584,2048]{1,0:T(8,128)(2,1)} %refs_0_.5, bf16[8,3584]{1,0:T(8,128)(2,1)S(1)} %pair_sum.2.refs_1_.near_ref), custom_call_target="tpu_custom_call" | custom-call | bytes 6291456 | tf_op jit(solution)/shard_map/load/pallas_call | solution.py:144
  59.2 1.3 %first_down.1 = (f32[8,2048]{1,0:T(8,128)S(1)}, f32[8,128]{1,0:T(8,128)S(1)}) custom-call(bf16[8,3712]{1,0:T(8,128)(2,1)S(1)} %pair_sum.3.near_ref, bf16[8,3712]{1,0:T(8,128)(2,1)S(1)} %collective-permute-done.21.far_ref, bf16[896,2048]{1,0:T(8,128)(2,1)S(1)} %get-tuple-element.82.one_ref, bf16[1152,2048]{1,0:T(8,128)(2,1)S(1)} %get-tuple-element.80.two_ref, ...), custom_call_target="tpu_custom_call" | custom-call | flops 58720256 | bytes 7340032 | tf_op jit(solution)/shard_map/first_down/pallas_call | solution.py:572
  60.5 0.0 collective-permute-done.19.far_ref
  60.5 1.3 %second_down.1 = (bf16[2,2048]{1,0:T(2,128)(2,1)S(1)}, bf16[2,2048]{1,0:T(2,128)(2,1)S(1)}, bf16[2,2048]{1,0:T(2,128)(2,1)S(1)}, bf16[2,2048]{1,0:T(2,128)(2,1)S(1)}) custom-call(bf16[8,3584]{1,0:T(8,128)(2,1)S(1)} %pair_sum.2.refs_1_.near_ref, bf16[8,3584]{1,0:T(8,128)(2,1)S(1)} %collective-permute-done.19.far_ref, ...), custom_call_target="tpu_custom_call" | custom-call | tf_op jit(solution)/shard_map/second_down/pallas_call | solution.py:606
  61.8 2.2 %collective-permute-start.22 = (bf16[2,2048]{1,0:T(2,128)(2,1)S(1)}, bf16[2,2048]{1,0:T(2,128)(2,1)S(1)}, u32[]{:S(2)}, u32[]{:S(2)}) collective-permute-start(bf16[2,2048]{1,0:T(2,128)(2,1)S(1)} %get-tuple-element.85), channel_id=1, source_target_pairs={{0,12},{1,13},{2,14},{3,15},{4,8},{5,9},{6,10},{7,11},{8,4},{9,5},... | collective-permute-start | bytes 24584 | tf_op jit(solution)/shard_map/ppermute | solution.py:49
  64.0 0.7 collective-permute-start.23
  64.7 1.6 %collective-permute-start.24 = (bf16[2,2048]{1,0:T(2,128)(2,1)S(1)}, bf16[2,2048]{1,0:T(2,128)(2,1)S(1)}, u32[]{:S(2)}, u32[]{:S(2)}) collective-permute-start(bf16[2,2048]{1,0:T(2,128)(2,1)S(1)} %get-tuple-element.87), channel_id=1, source_target_pairs={{0,4},{1,5},{2,6},{3,7},{4,0},{5,1},{6,2},{7,3},{8,12},{9,13},{10,... | collective-permute-start | bytes 24584 | tf_op jit(solution)/shard_map/ppermute | solution.py:49
  66.3 1.1 %collective-permute-done.22 = bf16[2,2048]{1,0:T(2,128)(2,1)S(1)} collective-permute-done((bf16[2,2048]{1,0:T(2,128)(2,1)S(1)}, bf16[2,2048]{1,0:T(2,128)(2,1)S(1)}, u32[]{:S(2)}, u32[]{:S(2)}) %collective-permute-start.22) | collective-permute-done | bytes 8224 | tf_op jit(solution)/shard_map/ppermute | solution.py:49
  67.3 1.2 %collective-permute-done.23 = bf16[2,2048]{1,0:T(2,128)(2,1)S(1)} collective-permute-done((bf16[2,2048]{1,0:T(2,128)(2,1)S(1)}, bf16[2,2048]{1,0:T(2,128)(2,1)S(1)}, u32[]{:S(2)}, u32[]{:S(2)}) %collective-permute-start.23) | collective-permute-done | bytes 8224 | tf_op jit(solution)/shard_map/ppermute | solution.py:49
  68.6 0.0 collective-permute-done.24
  68.6 0.6 add_convert_fusion
  (20 shorter events, 0.1 us)
Async XLA Ops:
  0.0 10.3 %collective-permute-start = (bf16[2,2048]{1,0:T(2,128)(2,1)}, bf16[2,2048]{1,0:T(2,128)(2,1)S(1)}, u32[]{:S(2)}, u32[]{:S(2)}) collective-permute-start(bf16[2,2048]{1,0:T(2,128)(2,1)} %refs_5_.1), channel_id=1, source_target_pairs={{0,12},{4,8},{8,4},{12,0},{1,13},{5,9},{9,5},{13,1},{2,14},{6,10},... | collective-permute-start | bytes 24584 | tf_op jit(solution)/shard_map/ppermute | solution.py:30
  5.0 5.3 %collective-permute-start.1 = (bf16[2,2048]{1,0:T(2,128)(2,1)}, bf16[2,2048]{1,0:T(2,128)(2,1)S(1)}, u32[]{:S(2)}, u32[]{:S(2)}) collective-permute-start(bf16[2,2048]{1,0:T(2,128)(2,1)} %refs_5_.1), channel_id=1, source_target_pairs={{0,8},{4,12},{8,0},{12,4},{1,9},{5,13},{9,1},{13,5},{2,10},{6,14},... | collective-permute-start | bytes 24584 | tf_op jit(solution)/shard_map/ppermute | solution.py:30
  5.1 5.3 %collective-permute-start.2 = (bf16[2,2048]{1,0:T(2,128)(2,1)}, bf16[2,2048]{1,0:T(2,128)(2,1)S(1)}, u32[]{:S(2)}, u32[]{:S(2)}) collective-permute-start(bf16[2,2048]{1,0:T(2,128)(2,1)} %refs_5_.1), channel_id=1, source_target_pairs={{0,4},{4,0},{8,12},{12,8},{1,5},{5,1},{9,13},{13,9},{2,6},{6,2},{1... | collective-permute-start | bytes 24584 | tf_op jit(solution)/shard_map/ppermute | solution.py:30
  5.6 12.0 %copy-start.4 = (s32[8]{0:T(128)S(1)}, s32[8]{0:T(128)}, u32[]{:S(2)}) copy-start(s32[8]{0:T(128)} %param.23) | copy-start | bytes 100
  8.4 2.0 %copy-start.2 = (bf16[2048,1024]{1,0:T(8,128)(2,1)}, bf16[2048,1024]{1,0:T(8,128)(2,1)S(1)}, u32[]{:S(2)}) copy-start(bf16[2048,1024]{1,0:T(8,128)(2,1)S(1)} %get-tuple-element.48.wq_ref) | copy-start | bytes 12582916
  10.4 2.2 %copy-start.3 = (bf16[2048,1024]{1,0:T(8,128)(2,1)S(1)}, bf16[2048,1024]{1,0:T(8,128)(2,1)}, u32[]{:S(2)}) copy-start(bf16[2048,1024]{1,0:T(8,128)(2,1)} %copy-done.2) | copy-start | bytes 12582916
  13.4 6.8 %collective-permute-start.3 = (bf16[2,1408]{1,0:T(2,128)(2,1)S(1)}, bf16[2,1408]{1,0:T(2,128)(2,1)S(1)}, u32[]{:S(2)}, u32[]{:S(2)}) collective-permute-start(bf16[2,1408]{1,0:T(2,128)(2,1)S(1)} %get-tuple-element.54), channel_id=1, source_target_pairs={{0,13},{1,12},{2,15},{3,14},{4,9},{5,8},{6,11},{7,10},{8,5},{9,4},... | collective-permute-start | bytes 16904 | tf_op jit(solution)/shard_map/ppermute | solution.py:49
  15.9 4.3 %collective-permute-start.4 = (bf16[2,1408]{1,0:T(2,128)(2,1)S(1)}, bf16[2,1408]{1,0:T(2,128)(2,1)S(1)}, u32[]{:S(2)}, u32[]{:S(2)}) collective-permute-start(bf16[2,1408]{1,0:T(2,128)(2,1)S(1)} %get-tuple-element.55), channel_id=1, source_target_pairs={{0,9},{1,8},{2,11},{3,10},{4,13},{5,12},{6,15},{7,14},{8,1},{9,0},... | collective-permute-start | bytes 16904 | tf_op jit(solution)/shard_map/ppermute | solution.py:49
  16.1 4.1 %collective-permute-start.5 = (bf16[2,1408]{1,0:T(2,128)(2,1)S(1)}, bf16[2,1408]{1,0:T(2,128)(2,1)S(1)}, u32[]{:S(2)}, u32[]{:S(2)}) collective-permute-start(bf16[2,1408]{1,0:T(2,128)(2,1)S(1)} %get-tuple-element.56), channel_id=1, source_target_pairs={{0,5},{1,4},{2,7},{3,6},{4,1},{5,0},{6,3},{7,2},{8,13},{9,12},{10,... | collective-permute-start | bytes 16904 | tf_op jit(solution)/shard_map/ppermute | solution.py:49
  17.7 22.2 %copy-start = (bf16[2048,3584]{1,0:T(8,128)(2,1)S(1)}, bf16[2048,3584]{1,0:T(8,128)(2,1)}, u32[]{:S(2)}) copy-start(bf16[2048,3584]{1,0:T(8,128)(2,1)} %up_ref.3) | copy-start | bytes 44040196
  20.2 5.2 %collective-permute-start.6 = (bf16[8,1408]{1,0:T(8,128)(2,1)S(1)}, bf16[8,1408]{1,0:T(8,128)(2,1)S(1)}, u32[]{:S(2)}, u32[]{:S(2)}) collective-permute-start(bf16[8,1408]{1,0:T(8,128)(2,1)S(1)} %stack.1.refs_1_.refs_0_), channel_id=1, source_target_pairs={{0,3},{1,2},{2,1},{3,0},{4,7},{5,6},{6,5},{7,4},{8,11},{9,10},{10,... | collective-permute-start | bytes 67592 | tf_op jit(solution)/shard_map/ppermute | solution.py:30
  22.5 3.8 %collective-permute-start.7 = (bf16[8,1408]{1,0:T(8,128)(2,1)S(1)}, bf16[8,1408]{1,0:T(8,128)(2,1)S(1)}, u32[]{:S(2)}, u32[]{:S(2)}) collective-permute-start(bf16[8,1408]{1,0:T(8,128)(2,1)S(1)} %stack.1.refs_1_.refs_0_), channel_id=1, source_target_pairs={{0,2},{1,3},{2,0},{3,1},{4,6},{5,7},{6,4},{7,5},{8,10},{9,11},{10,... | collective-permute-start | bytes 67592 | tf_op jit(solution)/shard_map/ppermute | solution.py:30
  23.1 3.3 %collective-permute-start.8 = (bf16[8,1408]{1,0:T(8,128)(2,1)S(1)}, bf16[8,1408]{1,0:T(8,128)(2,1)S(1)}, u32[]{:S(2)}, u32[]{:S(2)}) collective-permute-start(bf16[8,1408]{1,0:T(8,128)(2,1)S(1)} %stack.1.refs_1_.refs_0_), channel_id=1, source_target_pairs={{0,1},{1,0},{2,3},{3,2},{4,5},{5,4},{6,7},{7,6},{8,9},{9,8},{10,11... | collective-permute-start | bytes 67592 | tf_op jit(solution)/shard_map/ppermute | solution.py:30
  28.2 4.1 %collective-permute-start.10 = (bf16[64,256]{1,0:T(8,128)(2,1)S(1)}, bf16[64,256]{1,0:T(8,128)(2,1)S(1)}, u32[]{:S(2)}, u32[]{:S(2)}) collective-permute-start(bf16[64,256]{1,0:T(8,128)(2,1)S(1)} %attend.1.refs_3_), channel_id=1, source_target_pairs={{0,2},{1,3},{2,0},{3,1},{4,6},{5,7},{6,4},{7,5},{8,10},{9,11},{10,... | collective-permute-start | bytes 98312 | tf_op jit(solution)/shard_map/ppermute | solution.py:30
  28.8 3.4 %collective-permute-start.11 = (bf16[64,256]{1,0:T(8,128)(2,1)S(1)}, bf16[64,256]{1,0:T(8,128)(2,1)S(1)}, u32[]{:S(2)}, u32[]{:S(2)}) collective-permute-start(bf16[64,256]{1,0:T(8,128)(2,1)S(1)} %attend.1.refs_3_), channel_id=1, source_target_pairs={{0,1},{1,0},{2,3},{3,2},{4,5},{5,4},{6,7},{7,6},{8,9},{9,8},{10,11... | collective-permute-start | bytes 98312 | tf_op jit(solution)/shard_map/ppermute | solution.py:30
  29.1 3.4 %collective-permute-start.9 = (bf16[64,256]{1,0:T(8,128)(2,1)S(1)}, bf16[64,256]{1,0:T(8,128)(2,1)S(1)}, u32[]{:S(2)}, u32[]{:S(2)}) collective-permute-start(bf16[64,256]{1,0:T(8,128)(2,1)S(1)} %attend.1.refs_3_), channel_id=1, source_target_pairs={{0,3},{1,2},{2,1},{3,0},{4,7},{5,6},{6,5},{7,4},{8,11},{9,10},{10,... | collective-permute-start | bytes 98312 | tf_op jit(solution)/shard_map/ppermute | solution.py:30
  32.8 4.9 %collective-permute-start.12 = (bf16[2,1024]{1,0:T(2,128)(2,1)S(1)}, bf16[2,1024]{1,0:T(2,128)(2,1)S(1)}, u32[]{:S(2)}, u32[]{:S(2)}) collective-permute-start(bf16[2,1024]{1,0:T(2,128)(2,1)S(1)} %get-tuple-element.69), channel_id=1, source_target_pairs={{0,13},{1,12},{2,15},{3,14},{4,9},{5,8},{6,11},{7,10},{8,5},{9,4},... | collective-permute-start | bytes 12296 | tf_op jit(solution)/shard_map/ppermute | solution.py:49
  36.0 3.9 %collective-permute-start.13 = (bf16[2,1024]{1,0:T(2,128)(2,1)S(1)}, bf16[2,1024]{1,0:T(2,128)(2,1)S(1)}, u32[]{:S(2)}, u32[]{:S(2)}) collective-permute-start(bf16[2,1024]{1,0:T(2,128)(2,1)S(1)} %get-tuple-element.70), channel_id=1, source_target_pairs={{0,9},{1,8},{2,11},{3,10},{4,13},{5,12},{6,15},{7,14},{8,1},{9,0},... | collective-permute-start | bytes 12296 | tf_op jit(solution)/shard_map/ppermute | solution.py:49
  36.0 3.9 %collective-permute-start.14 = (bf16[2,1024]{1,0:T(2,128)(2,1)S(1)}, bf16[2,1024]{1,0:T(2,128)(2,1)S(1)}, u32[]{:S(2)}, u32[]{:S(2)}) collective-permute-start(bf16[2,1024]{1,0:T(2,128)(2,1)S(1)} %get-tuple-element.71), channel_id=1, source_target_pairs={{0,5},{1,4},{2,7},{3,6},{4,1},{5,0},{6,3},{7,2},{8,13},{9,12},{10,... | collective-permute-start | bytes 12296 | tf_op jit(solution)/shard_map/ppermute | solution.py:49
  39.9 7.9 %copy-start.1 = (bf16[2048,3584]{1,0:T(8,128)(2,1)S(1)}, bf16[2048,3584]{1,0:T(8,128)(2,1)}, u32[]{:S(2)}) copy-start(bf16[2048,3584]{1,0:T(8,128)(2,1)} %gate_ref.3) | copy-start | bytes 44040196
  40.8 6.1 %collective-permute-start.15 = (bf16[8,2048]{1,0:T(8,128)(2,1)S(1)}, bf16[8,2048]{1,0:T(8,128)(2,1)S(1)}, u32[]{:S(2)}, u32[]{:S(2)}) collective-permute-start(bf16[8,2048]{1,0:T(8,128)(2,1)S(1)} %get-tuple-element.73), channel_id=1, source_target_pairs={{0,12},{1,13},{2,14},{3,15},{4,8},{5,9},{6,10},{7,11},{8,4},{9,5},... | collective-permute-start | bytes 98312 | tf_op jit(solution)/shard_map/ppermute | solution.py:49
  42.4 5.1 %collective-permute-start.16 = (bf16[8,2048]{1,0:T(8,128)(2,1)S(1)}, bf16[8,2048]{1,0:T(8,128)(2,1)S(1)}, u32[]{:S(2)}, u32[]{:S(2)}) collective-permute-start(bf16[8,2048]{1,0:T(8,128)(2,1)S(1)} %get-tuple-element.74), channel_id=1, source_target_pairs={{0,8},{1,9},{2,10},{3,11},{4,12},{5,13},{6,14},{7,15},{8,0},{9,1},... | collective-permute-start | bytes 98312 | tf_op jit(solution)/shard_map/ppermute | solution.py:49
  43.0 4.8 %collective-permute-start.17 = (bf16[8,2048]{1,0:T(8,128)(2,1)S(1)}, bf16[8,2048]{1,0:T(8,128)(2,1)S(1)}, u32[]{:S(2)}, u32[]{:S(2)}) collective-permute-start(bf16[8,2048]{1,0:T(8,128)(2,1)S(1)} %get-tuple-element.75), channel_id=1, source_target_pairs={{0,4},{1,5},{2,6},{3,7},{4,0},{5,1},{6,2},{7,3},{8,12},{9,13},{10,... | collective-permute-start | bytes 98312 | tf_op jit(solution)/shard_map/ppermute | solution.py:49
  51.0 3.1 %collective-permute-start.20 = (bf16[8,3712]{1,0:T(8,128)(2,1)S(1)}, bf16[8,3712]{1,0:T(8,128)(2,1)S(1)}, u32[]{:S(2)}, u32[]{:S(2)}) collective-permute-start(bf16[8,3712]{1,0:T(8,128)(2,1)S(1)} %get-tuple-element.81.first_ref), channel_id=1, source_target_pairs={{0,1},{1,0},{2,3},{3,2},{4,5},{5,4},{6,7},{7,6},{8,9},{9,8},{10,11... | collective-permute-start | bytes 178184 | tf_op jit(solution)/shard_map/ppermute | solution.py:30
  53.6 1.5 %collective-permute-start.18 = (bf16[8,3584]{1,0:T(8,128)(2,1)S(1)}, bf16[8,3584]{1,0:T(8,128)(2,1)S(1)}, u32[]{:S(2)}, u32[]{:S(2)}) collective-permute-start(bf16[8,3584]{1,0:T(8,128)(2,1)S(1)} %get-tuple-element.79.first_ref), channel_id=1, source_target_pairs={{0,1},{1,0},{2,3},{3,2},{4,5},{5,4},{6,7},{7,6},{8,9},{9,8},{10,11... | collective-permute-start | bytes 172040 | tf_op jit(solution)/shard_map/ppermute | solution.py:30
  54.1 5.1 %collective-permute-start.21 = (bf16[8,3712]{1,0:T(8,128)(2,1)S(1)}, bf16[8,3712]{1,0:T(8,128)(2,1)S(1)}, u32[]{:S(2)}, u32[]{:S(2)}) collective-permute-start(bf16[8,3712]{1,0:T(8,128)(2,1)S(1)} %pair_sum.3.near_ref), channel_id=1, source_target_pairs={{0,2},{1,3},{2,0},{3,1},{4,6},{5,7},{6,4},{7,5},{8,10},{9,11},{10,... | collective-permute-start | bytes 178184 | tf_op jit(solution)/shard_map/ppermute | solution.py:30
  55.0 5.5 %collective-permute-start.19 = (bf16[8,3584]{1,0:T(8,128)(2,1)S(1)}, bf16[8,3584]{1,0:T(8,128)(2,1)S(1)}, u32[]{:S(2)}, u32[]{:S(2)}) collective-permute-start(bf16[8,3584]{1,0:T(8,128)(2,1)S(1)} %pair_sum.2.refs_1_.near_ref), channel_id=1, source_target_pairs={{0,2},{1,3},{2,0},{3,1},{4,6},{5,7},{6,4},{7,5},{8,10},{9,11},{10,... | collective-permute-start | bytes 172040 | tf_op jit(solution)/shard_map/ppermute | solution.py:30
  61.8 5.5 %collective-permute-start.22 = (bf16[2,2048]{1,0:T(2,128)(2,1)S(1)}, bf16[2,2048]{1,0:T(2,128)(2,1)S(1)}, u32[]{:S(2)}, u32[]{:S(2)}) collective-permute-start(bf16[2,2048]{1,0:T(2,128)(2,1)S(1)} %get-tuple-element.85), channel_id=1, source_target_pairs={{0,12},{1,13},{2,14},{3,15},{4,8},{5,9},{6,10},{7,11},{8,4},{9,5},... | collective-permute-start | bytes 24584 | tf_op jit(solution)/shard_map/ppermute | solution.py:49
  64.0 4.5 %collective-permute-start.23 = (bf16[2,2048]{1,0:T(2,128)(2,1)S(1)}, bf16[2,2048]{1,0:T(2,128)(2,1)S(1)}, u32[]{:S(2)}, u32[]{:S(2)}) collective-permute-start(bf16[2,2048]{1,0:T(2,128)(2,1)S(1)} %get-tuple-element.86), channel_id=1, source_target_pairs={{0,8},{1,9},{2,10},{3,11},{4,12},{5,13},{6,14},{7,15},{8,0},{9,1},... | collective-permute-start | bytes 24584 | tf_op jit(solution)/shard_map/ppermute | solution.py:49
  64.7 3.9 %collective-permute-start.24 = (bf16[2,2048]{1,0:T(2,128)(2,1)S(1)}, bf16[2,2048]{1,0:T(2,128)(2,1)S(1)}, u32[]{:S(2)}, u32[]{:S(2)}) collective-permute-start(bf16[2,2048]{1,0:T(2,128)(2,1)S(1)} %get-tuple-element.87), channel_id=1, source_target_pairs={{0,4},{1,5},{2,6},{3,7},{4,0},{5,1},{6,2},{7,3},{8,12},{9,13},{10,... | collective-permute-start | bytes 24584 | tf_op jit(solution)/shard_map/ppermute | solution.py:49

commit v9 on v8

--- a/solution.py
+++ b/solution.py
@@ -174,7 +174,7 @@
     wide = join_rows(refs[:slots][::-1], rows_s)
     rows_ref[...] = wide
     total = jnp.sum(wide * wide, axis=1, keepdims=True)
-    scaled = (wide * gain_ref[...].astype(jnp.float32)).astype(jnp.bfloat16)
+    scaled = (wide * gain_ref[...].astype(jnp.float32)[None, :]).astype(jnp.bfloat16)
     query_cols = wq_ref.shape[1]
     kv_cols = wkv_ref.shape[1]
 
@@ -470,7 +470,7 @@
     updated_ref[...] = wide[:own_rows]
     squares = jnp.sum(wide * wide, axis=1, keepdims=True)
     out_ref[:, 2 * count :] = squares_block(squares).astype(jnp.bfloat16)
-    scaled = (wide * gain_ref[...].astype(jnp.float32)).astype(jnp.bfloat16)
+    scaled = (wide * gain_ref[...].astype(jnp.float32)[None, :]).astype(jnp.bfloat16)
     scaled_ref[...] = scaled
     gate_up_tiles(scaled, gate_ref, up_ref, out_ref, 0, count)
     for copy in copies:
@@ -649,7 +649,7 @@
     own, attn_gain, ffn_gain, w_kv, w_query = load(
         states, attn_gain, ffn_gain, w_kv, w_query, after=states
     )
-    rows, *pieces = project_qkv([own] + got[1:], attn_gain[None, :], w_query, w_kv)
+    rows, *pieces = project_qkv([own] + got[1:], attn_gain, w_query, w_kv)
 
     rows, lengths = lax.optimization_barrier((rows, lengths))
     my_lengths = lax.dynamic_slice_in_dim(lengths, tensor_index * own_rows, own_rows, 0)
@@ -673,7 +673,7 @@
     starts = [0, span * LANES, (span + max(tiles * 9 // 28, half - span + 1)) * LANES, tiles * LANES]
     spans = [(a, b - a) for a, b in zip(starts, starts[1:])]
     one, updated, scaled, down_one = first_gate_up(
-        rows, ffn_gain[None, :], parts, w_gate, w_up, w_down, spans[0], [], first, own_rows
+        rows, ffn_gain, parts, w_gate, w_up, w_down, spans[0], [], first, own_rows
     )
     two, down_two = second_gate_up(scaled, w_gate, w_up, w_down, spans[1], first)
     steps = steps_up(lax.axis_size("inner"))

time: 69.4 us -> 65.1 us (0.938)
  local copies, waits for them, and re-layouts: 4.25 us -> 0.09 us
  waiting for transfers between devices: 11.2 us -> 12.4 us
  starting transfers between devices: 30.4 us -> 29.2 us
    unnamed x10 -> x6, local copies, waits for them, and re-layouts: 4.16 us -> 0.01 us
    ppermute x13, waiting for transfers between devices: 3.23 us -> 5.33 us  [swap_with(): return lax.ppermute(value, axis, [(i, i ^ step) for i in range(count)])]
    ppermute x12, starting transfers between devices: 17.1 us -> 15.6 us  [scatter_slots(): got.append(lax.ppermute(pieces[k], ('tensor', 'inner'), pairs))]
    ppermute x12, waiting for transfers between devices: 8.01 us -> 7.1 us  [scatter_slots(): got.append(lax.ppermute(pieces[k], ('tensor', 'inner'), pairs))]
  transfers between devices with their start and end apart: 25 -> 25, of which waited for: 11 -> 12; matrix products, arithmetic and copies ran while one was open for 0% -> 0% of each run, Pallas kernels for 20% -> 22%
where the time goes in v9:
time: 65.1 us; the launch traced here: 65 us
  starting transfers between devices  29.2 us (45%)
  Pallas kernels  22.3 us (34%)
  waiting for transfers between devices  12.4 us (19%)
  other arithmetic  0.81 us (1%)
    ppermute x12, starting transfers between devices, scatter_slots(): got.append(lax.ppermute(pieces[k], ('tensor', 'inner'), pairs))  15.6 us
    ppermute x13, starting transfers between devices, swap_with(): return lax.ppermute(value, axis, [(i, i ^ step) for i in range(count)])  13.6 us
    pallas_call x4, Pallas kernels, load(): pl.pallas_call(functools.partial(load_kernel, spans), out_shape=tuple((pl...  10.2 us
    ppermute x12, waiting for transfers between devices, scatter_slots(): got.append(lax.ppermute(pieces[k], ('tensor', 'inner'), pairs))  7.1 us
    ppermute x13, waiting for transfers between devices, swap_with(): return lax.ppermute(value, axis, [(i, i ^ step) for i in range(count)])  5.33 us
    pallas_call x1, Pallas kernels, first_gate_up(): pl.pallas_call(functools.partial(first_gate_up_kernel, slots, count, star...  3.15 us
    pallas_call x1, Pallas kernels, second_gate_up(): pl.pallas_call(functools.partial(second_gate_up_kernel, first, count, sta...  2.44 us
    pallas_call x1, Pallas kernels, attend(): pl.pallas_call(functools.partial(attend_kernel, slots, len(parts)), out_s...  1.73 us
  transfers between devices with their start and end apart: 25, of which 12 were waited for; matrix products, arithmetic and copies ran while one was open for 0% of the time, Pallas kernels for 22%

profile of v9, /device:TPU:0, one launch (start us, length us, event | category | flops | bytes accessed | tf_op | source)
XLA Modules:
  0.0 65.0 jit_solution(4807785498241456448)
XLA Ops:
  0.0 5.0 %collective-permute-start = (bf16[2,2048]{1,0:T(2,128)(2,1)}, bf16[2,2048]{1,0:T(2,128)(2,1)S(1)}, u32[]{:S(2)}, u32[]{:S(2)}) collective-permute-start(bf16[2,2048]{1,0:T(2,128)(2,1)} %refs_5_.1), channel_id=1, source_target_pairs={{0,12},{4,8},{8,4},{12,0},{1,13},{5,9},{9,5},{13,1},{2,14},{6,10},... | collective-permute-start | bytes 24584 | tf_op jit(solution)/shard_map/ppermute | solution.py:30
  5.0 0.0 collective-permute-start.1
  5.1 0.6 collective-permute-start.2
  5.6 2.7 %load.4 = (bf16[2,2048]{1,0:T(2,128)(2,1)S(1)}, bf16[2048]{0:T(1024)(128)(2,1)S(1)}, bf16[2048]{0:T(1024)(128)(2,1)S(1)}, bf16[2048,256]{1,0:T(8,128)(2,1)S(1)}, bf16[2048,1024]{1,0:T(8,128)(2,1)S(1)}) custom-call(bf16[2,2048]{1,0:T(2,128)(2,1)} %refs_5_.1, bf16[2048]{0:T(1024)(128)(2,1)} %refs_1_.1, bf16[2048]{0:T(1024)(128)(2,1)} %refs_2_.1, ...), custom_call_target="tpu_custom_call" | custom-call | bytes 5259264 | tf_op jit(solution)/shard_map/load/pallas_call | solution.py:144
  8.4 0.0 collective-permute-done.refs_0_
  8.4 1.4 %collective-permute-done.1.refs_1_ = bf16[2,2048]{1,0:T(2,128)(2,1)S(1)} collective-permute-done((bf16[2,2048]{1,0:T(2,128)(2,1)}, bf16[2,2048]{1,0:T(2,128)(2,1)S(1)}, u32[]{:S(2)}, u32[]{:S(2)}) %collective-permute-start.1) | collective-permute-done | bytes 8224 | tf_op jit(solution)/shard_map/ppermute | solution.py:30
  9.8 0.0 collective-permute-done.2.refs_2_
  9.8 0.8 %project_qkv.1 = (f32[8,2048]{1,0:T(8,128)S(1)}, bf16[2,1408]{1,0:T(2,128)(2,1)S(1)}, bf16[2,1408]{1,0:T(2,128)(2,1)S(1)}, bf16[2,1408]{1,0:T(2,128)(2,1)S(1)}, bf16[2,1408]{1,0:T(2,128)(2,1)S(1)}) custom-call(bf16[2048]{0:T(1024)(128)(2,1)S(1)} %get-tuple-element.47.gain_ref, bf16[2048,1024]{1,0:T(8,128)(2,1)S(1)} %get-tuple-element.48.wq_ref, ...), custom_call_target="tpu_custom_call" | custom-call | tf_op jit(solution)/shard_map/project_qkv/pallas_call | solution.py:196
  10.6 1.1 %collective-permute-start.3 = (bf16[2,1408]{1,0:T(2,128)(2,1)S(1)}, bf16[2,1408]{1,0:T(2,128)(2,1)S(1)}, u32[]{:S(2)}, u32[]{:S(2)}) collective-permute-start(bf16[2,1408]{1,0:T(2,128)(2,1)S(1)} %get-tuple-element.54), channel_id=1, source_target_pairs={{0,13},{1,12},{2,15},{3,14},{4,9},{5,8},{6,11},{7,10},{8,5},{9,4},... | collective-permute-start | bytes 16904 | tf_op jit(solution)/shard_map/ppermute | solution.py:49
  11.7 0.2 collective-permute-start.4
  11.9 1.5 %collective-permute-start.5 = (bf16[2,1408]{1,0:T(2,128)(2,1)S(1)}, bf16[2,1408]{1,0:T(2,128)(2,1)S(1)}, u32[]{:S(2)}, u32[]{:S(2)}) collective-permute-start(bf16[2,1408]{1,0:T(2,128)(2,1)S(1)} %get-tuple-element.56), channel_id=1, source_target_pairs={{0,5},{1,4},{2,7},{3,6},{4,1},{5,0},{6,3},{7,2},{8,13},{9,12},{10,... | collective-permute-start | bytes 16904 | tf_op jit(solution)/shard_map/ppermute | solution.py:49
  13.5 0.1 fusion.4
  13.6 2.4 %load.5 = (bf16[2,4096,128]{2,1,0:T(8,128)(2,1)S(1)}, bf16[2,4096,128]{2,1,0:T(8,128)(2,1)S(1)}) custom-call(bf16[2,4096,128]{2,1,0:T(8,128)(2,1)} %bitcast.6, bf16[2,4096,128]{2,1,0:T(8,128)(2,1)} %bitcast.7, f32[8,2048]{1,0:T(8,128)S(1)} %get-tuple-element.52.refs_2_.rows_ref), custom_call_target="tpu_custom_call" | custom-call | bytes 4194304 | tf_op jit(solution)/shard_map/load/pallas_call | solution.py:144
  16.0 0.0 collective-permute-done.3.refs_0_
  16.0 0.0 collective-permute-done.4.refs_1_
  16.0 0.0 collective-permute-done.5.refs_2_
  16.1 2.6 %collective-permute-start.6 = (bf16[8,1408]{1,0:T(8,128)(2,1)S(1)}, bf16[8,1408]{1,0:T(8,128)(2,1)S(1)}, u32[]{:S(2)}, u32[]{:S(2)}) collective-permute-start(bf16[8,1408]{1,0:T(8,128)(2,1)S(1)} %stack.1.refs_1_.refs_0_), channel_id=1, source_target_pairs={{0,3},{1,2},{2,1},{3,0},{4,7},{5,6},{6,5},{7,4},{8,11},{9,10},{10,... | collective-permute-start | bytes 67592 | tf_op jit(solution)/shard_map/ppermute | solution.py:30
  18.7 0.5 collective-permute-start.7
  19.2 0.0 collective-permute-start.8
  19.2 0.1 fusion
  19.3 2.2 %load.6.weight_ref = bf16[1024,2048]{1,0:T(8,128)(2,1)S(1)} custom-call(bf16[1024,2048]{1,0:T(8,128)(2,1)} %refs_0_.4, bf16[8,1408]{1,0:T(8,128)(2,1)S(1)} %stack.1.refs_1_.refs_0_), custom_call_target="tpu_custom_call" | custom-call | bytes 4194304 | tf_op jit(solution)/shard_map/load/pallas_call | solution.py:144
  21.5 0.0 collective-permute-done.6.refs_3_
  21.6 0.9 %collective-permute-done.7.refs_2_ = bf16[8,1408]{1,0:T(8,128)(2,1)S(1)} collective-permute-done((bf16[8,1408]{1,0:T(8,128)(2,1)S(1)}, bf16[8,1408]{1,0:T(8,128)(2,1)S(1)}, u32[]{:S(2)}, u32[]{:S(2)}) %collective-permute-start.7) | collective-permute-done | bytes 22560 | tf_op jit(solution)/shard_map/ppermute | solution.py:30
  22.5 0.1 broadcast_in_dim.10.lengths_ref
  22.6 1.7 %attend.1.refs_3_ = bf16[64,256]{1,0:T(8,128)(2,1)S(1)} custom-call(s32[2,128]{1,0:T(2,128)S(1)} %broadcast_in_dim.10.lengths_ref, f32[8,128]{1,0:T(8,128)S(1)} %bitcast.4, f32[8,128]{1,0:T(8,128)S(1)} %bitcast.5, bf16[2,4096,128]{2,1,0:T(8,128)(2,1)S(1)} %get-tuple-element.63.key_ref, bf16[2,4096,128]{2,1,0:T(8,128)(2,1)S(1)} %get-tuple-element.64.value_ref, ...), custom_call_target="tpu_custom_call" | custom-call | tf_op jit(solution)/shard_map/attend/pallas_call | solution.py:330
  24.3 0.7 %collective-permute-start.10 = (bf16[64,256]{1,0:T(8,128)(2,1)S(1)}, bf16[64,256]{1,0:T(8,128)(2,1)S(1)}, u32[]{:S(2)}, u32[]{:S(2)}) collective-permute-start(bf16[64,256]{1,0:T(8,128)(2,1)S(1)} %attend.1.refs_3_), channel_id=1, source_target_pairs={{0,2},{1,3},{2,0},{3,1},{4,6},{5,7},{6,4},{7,5},{8,10},{9,11},{10,... | collective-permute-start | bytes 98312 | tf_op jit(solution)/shard_map/ppermute | solution.py:30
  25.0 0.8 %collective-permute-start.11 = (bf16[64,256]{1,0:T(8,128)(2,1)S(1)}, bf16[64,256]{1,0:T(8,128)(2,1)S(1)}, u32[]{:S(2)}, u32[]{:S(2)}) collective-permute-start(bf16[64,256]{1,0:T(8,128)(2,1)S(1)} %attend.1.refs_3_), channel_id=1, source_target_pairs={{0,1},{1,0},{2,3},{3,2},{4,5},{5,4},{6,7},{7,6},{8,9},{9,8},{10,11... | collective-permute-start | bytes 98312 | tf_op jit(solution)/shard_map/ppermute | solution.py:30
  25.8 0.7 %collective-permute-start.9 = (bf16[64,256]{1,0:T(8,128)(2,1)S(1)}, bf16[64,256]{1,0:T(8,128)(2,1)S(1)}, u32[]{:S(2)}, u32[]{:S(2)}) collective-permute-start(bf16[64,256]{1,0:T(8,128)(2,1)S(1)} %attend.1.refs_3_), channel_id=1, source_target_pairs={{0,3},{1,2},{2,1},{3,0},{4,7},{5,6},{6,5},{7,4},{8,11},{9,10},{10,... | collective-permute-start | bytes 98312 | tf_op jit(solution)/shard_map/ppermute | solution.py:30
  26.5 1.8 %collective-permute-done.10.refs_1_ = bf16[64,256]{1,0:T(8,128)(2,1)S(1)} collective-permute-done((bf16[64,256]{1,0:T(8,128)(2,1)S(1)}, bf16[64,256]{1,0:T(8,128)(2,1)S(1)}, u32[]{:S(2)}, u32[]{:S(2)}) %collective-permute-start.10) | collective-permute-done | bytes 32800 | tf_op jit(solution)/shard_map/ppermute | solution.py:30
  28.3 0.0 collective-permute-done.11.refs_2_
  28.3 1.0 %collective-permute-done.9.refs_0_ = bf16[64,256]{1,0:T(8,128)(2,1)S(1)} collective-permute-done((bf16[64,256]{1,0:T(8,128)(2,1)S(1)}, bf16[64,256]{1,0:T(8,128)(2,1)S(1)}, u32[]{:S(2)}, u32[]{:S(2)}) %collective-permute-start.9) | collective-permute-done | bytes 32800 | tf_op jit(solution)/shard_map/ppermute | solution.py:30
  29.3 0.3 combine.1
  29.6 2.2 %collective-permute-start.12 = (bf16[2,1024]{1,0:T(2,128)(2,1)S(1)}, bf16[2,1024]{1,0:T(2,128)(2,1)S(1)}, u32[]{:S(2)}, u32[]{:S(2)}) collective-permute-start(bf16[2,1024]{1,0:T(2,128)(2,1)S(1)} %get-tuple-element.69), channel_id=1, source_target_pairs={{0,13},{1,12},{2,15},{3,14},{4,9},{5,8},{6,11},{7,10},{8,5},{9,4},... | collective-permute-start | bytes 12296 | tf_op jit(solution)/shard_map/ppermute | solution.py:49
  31.8 1.7 %collective-permute-start.14 = (bf16[2,1024]{1,0:T(2,128)(2,1)S(1)}, bf16[2,1024]{1,0:T(2,128)(2,1)S(1)}, u32[]{:S(2)}, u32[]{:S(2)}) collective-permute-start(bf16[2,1024]{1,0:T(2,128)(2,1)S(1)} %get-tuple-element.71), channel_id=1, source_target_pairs={{0,5},{1,4},{2,7},{3,6},{4,1},{5,0},{6,3},{7,2},{8,13},{9,12},{10,... | collective-permute-start | bytes 12296 | tf_op jit(solution)/shard_map/ppermute | solution.py:49
  33.5 1.0 %collective-permute-done.12.refs_0_ = bf16[2,1024]{1,0:T(2,128)(2,1)S(1)} collective-permute-done((bf16[2,1024]{1,0:T(2,128)(2,1)S(1)}, bf16[2,1024]{1,0:T(2,128)(2,1)S(1)}, u32[]{:S(2)}, u32[]{:S(2)}) %collective-permute-start.12) | collective-permute-done | bytes 4128 | tf_op jit(solution)/shard_map/ppermute | solution.py:49
  34.5 1.2 %collective-permute-done.13.refs_1_ = bf16[2,1024]{1,0:T(2,128)(2,1)S(1)} collective-permute-done((bf16[2,1024]{1,0:T(2,128)(2,1)S(1)}, bf16[2,1024]{1,0:T(2,128)(2,1)S(1)}, u32[]{:S(2)}, u32[]{:S(2)}) %collective-permute-start.13) | collective-permute-done | bytes 4128 | tf_op jit(solution)/shard_map/ppermute | solution.py:49
  35.7 0.0 collective-permute-done.14.refs_2_
  35.7 1.0 %project_out.1 = (bf16[8,2048]{1,0:T(8,128)(2,1)S(1)}, bf16[8,2048]{1,0:T(8,128)(2,1)S(1)}, bf16[8,2048]{1,0:T(8,128)(2,1)S(1)}, bf16[8,2048]{1,0:T(8,128)(2,1)S(1)}) custom-call(bf16[1024,2048]{1,0:T(8,128)(2,1)S(1)} %load.6.weight_ref, bf16[2,1024]{1,0:T(2,128)(2,1)S(1)} %collective-permute-done.12.refs_0_, ...), custom_call_target="tpu_custom_call" | custom-call | tf_op jit(solution)/shard_map/project_out/pallas_call | solution.py:419
  36.7 1.5 %collective-permute-start.15 = (bf16[8,2048]{1,0:T(8,128)(2,1)S(1)}, bf16[8,2048]{1,0:T(8,128)(2,1)S(1)}, u32[]{:S(2)}, u32[]{:S(2)}) collective-permute-start(bf16[8,2048]{1,0:T(8,128)(2,1)S(1)} %get-tuple-element.73), channel_id=1, source_target_pairs={{0,12},{1,13},{2,14},{3,15},{4,8},{5,9},{6,10},{7,11},{8,4},{9,5},... | collective-permute-start | bytes 98312 | tf_op jit(solution)/shard_map/ppermute | solution.py:49
  38.2 1.0 %collective-permute-start.16 = (bf16[8,2048]{1,0:T(8,128)(2,1)S(1)}, bf16[8,2048]{1,0:T(8,128)(2,1)S(1)}, u32[]{:S(2)}, u32[]{:S(2)}) collective-permute-start(bf16[8,2048]{1,0:T(8,128)(2,1)S(1)} %get-tuple-element.74), channel_id=1, source_target_pairs={{0,8},{1,9},{2,10},{3,11},{4,12},{5,13},{6,14},{7,15},{8,0},{9,1},... | collective-permute-start | bytes 98312 | tf_op jit(solution)/shard_map/ppermute | solution.py:49
  39.3 1.8 %collective-permute-start.17 = (bf16[8,2048]{1,0:T(8,128)(2,1)S(1)}, bf16[8,2048]{1,0:T(8,128)(2,1)S(1)}, u32[]{:S(2)}, u32[]{:S(2)}) collective-permute-start(bf16[8,2048]{1,0:T(8,128)(2,1)S(1)} %get-tuple-element.75), channel_id=1, source_target_pairs={{0,4},{1,5},{2,6},{3,7},{4,0},{5,1},{6,2},{7,3},{8,12},{9,13},{10,... | collective-permute-start | bytes 98312 | tf_op jit(solution)/shard_map/ppermute | solution.py:49
  41.1 1.7 %collective-permute-done.15.refs_0_ = bf16[8,2048]{1,0:T(8,128)(2,1)S(1)} collective-permute-done((bf16[8,2048]{1,0:T(8,128)(2,1)S(1)}, bf16[8,2048]{1,0:T(8,128)(2,1)S(1)}, u32[]{:S(2)}, u32[]{:S(2)}) %collective-permute-start.15) | collective-permute-done | bytes 32800 | tf_op jit(solution)/shard_map/ppermute | solution.py:49
  42.7 0.6 collective-permute-done.16.refs_1_
  43.3 0.3 collective-permute-done.17.refs_2_
  43.6 3.2 %first_gate_up.1 = (bf16[8,3712]{1,0:T(8,128)(2,1)S(1)}, f32[2,2048]{1,0:T(2,128)S(1)}, bf16[8,2048]{1,0:T(8,128)(2,1)S(1)}, bf16[896,2048]{1,0:T(8,128)(2,1)S(1)}) custom-call(f32[8,2048]{1,0:T(8,128)S(1)} %get-tuple-element.52.refs_2_.rows_ref, bf16[2048]{0:T(1024)(128)(2,1)S(1)} %get-tuple-element.53.gain_ref, bf16[2048,3584]{1,0:T(8,128)(2,1)S(1)} %copy-done.1, ...), custom_call_target="tpu_custom_call" | custom-call | flops 117440512 | bytes 14680064 | tf_op jit(solution)/shard_map/first_gate_up/pallas_call | solution.py:483
  46.8 0.1 collective-permute-start.20
  46.9 2.4 %second_gate_up.1 = (bf16[8,3584]{1,0:T(8,128)(2,1)S(1)}, bf16[1152,2048]{1,0:T(8,128)(2,1)S(1)}) custom-call(bf16[8,2048]{1,0:T(8,128)(2,1)S(1)} %get-tuple-element.78.scaled_ref, bf16[2048,3584]{1,0:T(8,128)(2,1)S(1)} %copy-done.1, bf16[2048,3584]{1,0:T(8,128)(2,1)S(1)} %copy-done, bf16[3584,2048]{1,0:T(8,128)(2,1)} %refs_0_.5), custom_call_target="tpu_custom_call" | custom-call | flops 117440512 | bytes 14680064 | tf_op jit(solution)/shard_map/second_gate_up/pallas_call | solution.py:522
  49.3 0.6 collective-permute-start.18
  49.9 0.0 collective-permute-done.20.second_ref
  49.9 0.7 %collective-permute-start.21 = (bf16[8,3712]{1,0:T(8,128)(2,1)S(1)}, bf16[8,3712]{1,0:T(8,128)(2,1)S(1)}, u32[]{:S(2)}, u32[]{:S(2)}) collective-permute-start(bf16[8,3712]{1,0:T(8,128)(2,1)S(1)} %pair_sum.3.near_ref), channel_id=1, source_target_pairs={{0,2},{1,3},{2,0},{3,1},{4,6},{5,7},{6,4},{7,5},{8,10},{9,11},{10,... | collective-permute-start | bytes 178184 | tf_op jit(solution)/shard_map/ppermute | solution.py:30
  50.6 0.2 collective-permute-done.18.second_ref
  50.8 1.3 %collective-permute-start.19 = (bf16[8,3584]{1,0:T(8,128)(2,1)S(1)}, bf16[8,3584]{1,0:T(8,128)(2,1)S(1)}, u32[]{:S(2)}, u32[]{:S(2)}) collective-permute-start(bf16[8,3584]{1,0:T(8,128)(2,1)S(1)} %pair_sum.2.refs_1_.near_ref), channel_id=1, source_target_pairs={{0,2},{1,3},{2,0},{3,1},{4,6},{5,7},{6,4},{7,5},{8,10},{9,11},{10,... | collective-permute-start | bytes 172040 | tf_op jit(solution)/shard_map/ppermute | solution.py:30
  52.1 2.9 %load.7.later_ref.three_ref = bf16[1536,2048]{1,0:T(8,128)(2,1)S(1)} custom-call(bf16[3584,2048]{1,0:T(8,128)(2,1)} %refs_0_.5, bf16[8,3584]{1,0:T(8,128)(2,1)S(1)} %pair_sum.2.refs_1_.near_ref), custom_call_target="tpu_custom_call" | custom-call | bytes 6291456 | tf_op jit(solution)/shard_map/load/pallas_call | solution.py:144
  54.9 0.0 collective-permute-done.21.far_ref
  55.0 1.3 %first_down.1 = (f32[8,2048]{1,0:T(8,128)S(1)}, f32[8,128]{1,0:T(8,128)S(1)}) custom-call(bf16[8,3712]{1,0:T(8,128)(2,1)S(1)} %pair_sum.3.near_ref, bf16[8,3712]{1,0:T(8,128)(2,1)S(1)} %collective-permute-done.21.far_ref, bf16[896,2048]{1,0:T(8,128)(2,1)S(1)} %get-tuple-element.82.one_ref, bf16[1152,2048]{1,0:T(8,128)(2,1)S(1)} %get-tuple-element.80.two_ref, ...), custom_call_target="tpu_custom_call" | custom-call | flops 58720256 | bytes 7340032 | tf_op jit(solution)/shard_map/first_down/pallas_call | solution.py:572
  56.2 0.0 collective-permute-done.19.far_ref
  56.2 1.3 %second_down.1 = (bf16[2,2048]{1,0:T(2,128)(2,1)S(1)}, bf16[2,2048]{1,0:T(2,128)(2,1)S(1)}, bf16[2,2048]{1,0:T(2,128)(2,1)S(1)}, bf16[2,2048]{1,0:T(2,128)(2,1)S(1)}) custom-call(bf16[8,3584]{1,0:T(8,128)(2,1)S(1)} %pair_sum.2.refs_1_.near_ref, bf16[8,3584]{1,0:T(8,128)(2,1)S(1)} %collective-permute-done.19.far_ref, ...), custom_call_target="tpu_custom_call" | custom-call | tf_op jit(solution)/shard_map/second_down/pallas_call | solution.py:606
  57.6 2.2 %collective-permute-start.22 = (bf16[2,2048]{1,0:T(2,128)(2,1)S(1)}, bf16[2,2048]{1,0:T(2,128)(2,1)S(1)}, u32[]{:S(2)}, u32[]{:S(2)}) collective-permute-start(bf16[2,2048]{1,0:T(2,128)(2,1)S(1)} %get-tuple-element.85), channel_id=1, source_target_pairs={{0,12},{1,13},{2,14},{3,15},{4,8},{5,9},{6,10},{7,11},{8,4},{9,5},... | collective-permute-start | bytes 24584 | tf_op jit(solution)/shard_map/ppermute | solution.py:49
  59.8 0.7 %collective-permute-start.23 = (bf16[2,2048]{1,0:T(2,128)(2,1)S(1)}, bf16[2,2048]{1,0:T(2,128)(2,1)S(1)}, u32[]{:S(2)}, u32[]{:S(2)}) collective-permute-start(bf16[2,2048]{1,0:T(2,128)(2,1)S(1)} %get-tuple-element.86), channel_id=1, source_target_pairs={{0,8},{1,9},{2,10},{3,11},{4,12},{5,13},{6,14},{7,15},{8,0},{9,1},... | collective-permute-start | bytes 24584 | tf_op jit(solution)/shard_map/ppermute | solution.py:49
  60.5 1.6 %collective-permute-start.24 = (bf16[2,2048]{1,0:T(2,128)(2,1)S(1)}, bf16[2,2048]{1,0:T(2,128)(2,1)S(1)}, u32[]{:S(2)}, u32[]{:S(2)}) collective-permute-start(bf16[2,2048]{1,0:T(2,128)(2,1)S(1)} %get-tuple-element.87), channel_id=1, source_target_pairs={{0,4},{1,5},{2,6},{3,7},{4,0},{5,1},{6,2},{7,3},{8,12},{9,13},{10,... | collective-permute-start | bytes 24584 | tf_op jit(solution)/shard_map/ppermute | solution.py:49
  62.0 1.1 %collective-permute-done.22 = bf16[2,2048]{1,0:T(2,128)(2,1)S(1)} collective-permute-done((bf16[2,2048]{1,0:T(2,128)(2,1)S(1)}, bf16[2,2048]{1,0:T(2,128)(2,1)S(1)}, u32[]{:S(2)}, u32[]{:S(2)}) %collective-permute-start.22) | collective-permute-done | bytes 8224 | tf_op jit(solution)/shard_map/ppermute | solution.py:49
  63.1 1.2 %collective-permute-done.23 = bf16[2,2048]{1,0:T(2,128)(2,1)S(1)} collective-permute-done((bf16[2,2048]{1,0:T(2,128)(2,1)S(1)}, bf16[2,2048]{1,0:T(2,128)(2,1)S(1)}, u32[]{:S(2)}, u32[]{:S(2)}) %collective-permute-start.23) | collective-permute-done | bytes 8224 | tf_op jit(solution)/shard_map/ppermute | solution.py:49
  64.3 0.0 collective-permute-done.24
  64.3 0.6 add_convert_fusion
  (14 shorter events, 0.1 us)
Async XLA Ops:
  0.0 8.4 %collective-permute-start = (bf16[2,2048]{1,0:T(2,128)(2,1)}, bf16[2,2048]{1,0:T(2,128)(2,1)S(1)}, u32[]{:S(2)}, u32[]{:S(2)}) collective-permute-start(bf16[2,2048]{1,0:T(2,128)(2,1)} %refs_5_.1), channel_id=1, source_target_pairs={{0,12},{4,8},{8,4},{12,0},{1,13},{5,9},{9,5},{13,1},{2,14},{6,10},... | collective-permute-start | bytes 24584 | tf_op jit(solution)/shard_map/ppermute | solution.py:30
  5.0 4.8 %collective-permute-start.1 = (bf16[2,2048]{1,0:T(2,128)(2,1)}, bf16[2,2048]{1,0:T(2,128)(2,1)S(1)}, u32[]{:S(2)}, u32[]{:S(2)}) collective-permute-start(bf16[2,2048]{1,0:T(2,128)(2,1)} %refs_5_.1), channel_id=1, source_target_pairs={{0,8},{4,12},{8,0},{12,4},{1,9},{5,13},{9,1},{13,5},{2,10},{6,14},... | collective-permute-start | bytes 24584 | tf_op jit(solution)/shard_map/ppermute | solution.py:30
  5.1 4.8 %collective-permute-start.2 = (bf16[2,2048]{1,0:T(2,128)(2,1)}, bf16[2,2048]{1,0:T(2,128)(2,1)S(1)}, u32[]{:S(2)}, u32[]{:S(2)}) collective-permute-start(bf16[2,2048]{1,0:T(2,128)(2,1)} %refs_5_.1), channel_id=1, source_target_pairs={{0,4},{4,0},{8,12},{12,8},{1,5},{5,1},{9,13},{13,9},{2,6},{6,2},{1... | collective-permute-start | bytes 24584 | tf_op jit(solution)/shard_map/ppermute | solution.py:30
  5.6 7.8 %copy-start.2 = (s32[8]{0:T(128)S(1)}, s32[8]{0:T(128)}, u32[]{:S(2)}) copy-start(s32[8]{0:T(128)} %param.23) | copy-start | bytes 100
  10.6 5.4 %collective-permute-start.3 = (bf16[2,1408]{1,0:T(2,128)(2,1)S(1)}, bf16[2,1408]{1,0:T(2,128)(2,1)S(1)}, u32[]{:S(2)}, u32[]{:S(2)}) collective-permute-start(bf16[2,1408]{1,0:T(2,128)(2,1)S(1)} %get-tuple-element.54), channel_id=1, source_target_pairs={{0,13},{1,12},{2,15},{3,14},{4,9},{5,8},{6,11},{7,10},{8,5},{9,4},... | collective-permute-start | bytes 16904 | tf_op jit(solution)/shard_map/ppermute | solution.py:49
  11.7 4.3 %collective-permute-start.4 = (bf16[2,1408]{1,0:T(2,128)(2,1)S(1)}, bf16[2,1408]{1,0:T(2,128)(2,1)S(1)}, u32[]{:S(2)}, u32[]{:S(2)}) collective-permute-start(bf16[2,1408]{1,0:T(2,128)(2,1)S(1)} %get-tuple-element.55), channel_id=1, source_target_pairs={{0,9},{1,8},{2,11},{3,10},{4,13},{5,12},{6,15},{7,14},{8,1},{9,0},... | collective-permute-start | bytes 16904 | tf_op jit(solution)/shard_map/ppermute | solution.py:49
  11.9 4.1 %collective-permute-start.5 = (bf16[2,1408]{1,0:T(2,128)(2,1)S(1)}, bf16[2,1408]{1,0:T(2,128)(2,1)S(1)}, u32[]{:S(2)}, u32[]{:S(2)}) collective-permute-start(bf16[2,1408]{1,0:T(2,128)(2,1)S(1)} %get-tuple-element.56), channel_id=1, source_target_pairs={{0,5},{1,4},{2,7},{3,6},{4,1},{5,0},{6,3},{7,2},{8,13},{9,12},{10,... | collective-permute-start | bytes 16904 | tf_op jit(solution)/shard_map/ppermute | solution.py:49
  13.6 22.2 %copy-start = (bf16[2048,3584]{1,0:T(8,128)(2,1)S(1)}, bf16[2048,3584]{1,0:T(8,128)(2,1)}, u32[]{:S(2)}) copy-start(bf16[2048,3584]{1,0:T(8,128)(2,1)} %up_ref.3) | copy-start | bytes 44040196
  16.1 5.5 %collective-permute-start.6 = (bf16[8,1408]{1,0:T(8,128)(2,1)S(1)}, bf16[8,1408]{1,0:T(8,128)(2,1)S(1)}, u32[]{:S(2)}, u32[]{:S(2)}) collective-permute-start(bf16[8,1408]{1,0:T(8,128)(2,1)S(1)} %stack.1.refs_1_.refs_0_), channel_id=1, source_target_pairs={{0,3},{1,2},{2,1},{3,0},{4,7},{5,6},{6,5},{7,4},{8,11},{9,10},{10,... | collective-permute-start | bytes 67592 | tf_op jit(solution)/shard_map/ppermute | solution.py:30
  18.7 3.8 %collective-permute-start.7 = (bf16[8,1408]{1,0:T(8,128)(2,1)S(1)}, bf16[8,1408]{1,0:T(8,128)(2,1)S(1)}, u32[]{:S(2)}, u32[]{:S(2)}) collective-permute-start(bf16[8,1408]{1,0:T(8,128)(2,1)S(1)} %stack.1.refs_1_.refs_0_), channel_id=1, source_target_pairs={{0,2},{1,3},{2,0},{3,1},{4,6},{5,7},{6,4},{7,5},{8,10},{9,11},{10,... | collective-permute-start | bytes 67592 | tf_op jit(solution)/shard_map/ppermute | solution.py:30
  19.2 3.3 %collective-permute-start.8 = (bf16[8,1408]{1,0:T(8,128)(2,1)S(1)}, bf16[8,1408]{1,0:T(8,128)(2,1)S(1)}, u32[]{:S(2)}, u32[]{:S(2)}) collective-permute-start(bf16[8,1408]{1,0:T(8,128)(2,1)S(1)} %stack.1.refs_1_.refs_0_), channel_id=1, source_target_pairs={{0,1},{1,0},{2,3},{3,2},{4,5},{5,4},{6,7},{7,6},{8,9},{9,8},{10,11... | collective-permute-start | bytes 67592 | tf_op jit(solution)/shard_map/ppermute | solution.py:30
  24.3 4.0 %collective-permute-start.10 = (bf16[64,256]{1,0:T(8,128)(2,1)S(1)}, bf16[64,256]{1,0:T(8,128)(2,1)S(1)}, u32[]{:S(2)}, u32[]{:S(2)}) collective-permute-start(bf16[64,256]{1,0:T(8,128)(2,1)S(1)} %attend.1.refs_3_), channel_id=1, source_target_pairs={{0,2},{1,3},{2,0},{3,1},{4,6},{5,7},{6,4},{7,5},{8,10},{9,11},{10,... | collective-permute-start | bytes 98312 | tf_op jit(solution)/shard_map/ppermute | solution.py:30
  25.0 3.3 %collective-permute-start.11 = (bf16[64,256]{1,0:T(8,128)(2,1)S(1)}, bf16[64,256]{1,0:T(8,128)(2,1)S(1)}, u32[]{:S(2)}, u32[]{:S(2)}) collective-permute-start(bf16[64,256]{1,0:T(8,128)(2,1)S(1)} %attend.1.refs_3_), channel_id=1, source_target_pairs={{0,1},{1,0},{2,3},{3,2},{4,5},{5,4},{6,7},{7,6},{8,9},{9,8},{10,11... | collective-permute-start | bytes 98312 | tf_op jit(solution)/shard_map/ppermute | solution.py:30
  25.8 3.5 %collective-permute-start.9 = (bf16[64,256]{1,0:T(8,128)(2,1)S(1)}, bf16[64,256]{1,0:T(8,128)(2,1)S(1)}, u32[]{:S(2)}, u32[]{:S(2)}) collective-permute-start(bf16[64,256]{1,0:T(8,128)(2,1)S(1)} %attend.1.refs_3_), channel_id=1, source_target_pairs={{0,3},{1,2},{2,1},{3,0},{4,7},{5,6},{6,5},{7,4},{8,11},{9,10},{10,... | collective-permute-start | bytes 98312 | tf_op jit(solution)/shard_map/ppermute | solution.py:30
  29.6 4.9 %collective-permute-start.12 = (bf16[2,1024]{1,0:T(2,128)(2,1)S(1)}, bf16[2,1024]{1,0:T(2,128)(2,1)S(1)}, u32[]{:S(2)}, u32[]{:S(2)}) collective-permute-start(bf16[2,1024]{1,0:T(2,128)(2,1)S(1)} %get-tuple-element.69), channel_id=1, source_target_pairs={{0,13},{1,12},{2,15},{3,14},{4,9},{5,8},{6,11},{7,10},{8,5},{9,4},... | collective-permute-start | bytes 12296 | tf_op jit(solution)/shard_map/ppermute | solution.py:49
  31.8 3.9 %collective-permute-start.13 = (bf16[2,1024]{1,0:T(2,128)(2,1)S(1)}, bf16[2,1024]{1,0:T(2,128)(2,1)S(1)}, u32[]{:S(2)}, u32[]{:S(2)}) collective-permute-start(bf16[2,1024]{1,0:T(2,128)(2,1)S(1)} %get-tuple-element.70), channel_id=1, source_target_pairs={{0,9},{1,8},{2,11},{3,10},{4,13},{5,12},{6,15},{7,14},{8,1},{9,0},... | collective-permute-start | bytes 12296 | tf_op jit(solution)/shard_map/ppermute | solution.py:49
  31.8 3.9 %collective-permute-start.14 = (bf16[2,1024]{1,0:T(2,128)(2,1)S(1)}, bf16[2,1024]{1,0:T(2,128)(2,1)S(1)}, u32[]{:S(2)}, u32[]{:S(2)}) collective-permute-start(bf16[2,1024]{1,0:T(2,128)(2,1)S(1)} %get-tuple-element.71), channel_id=1, source_target_pairs={{0,5},{1,4},{2,7},{3,6},{4,1},{5,0},{6,3},{7,2},{8,13},{9,12},{10,... | collective-permute-start | bytes 12296 | tf_op jit(solution)/shard_map/ppermute | solution.py:49
  35.7 7.9 %copy-start.1 = (bf16[2048,3584]{1,0:T(8,128)(2,1)S(1)}, bf16[2048,3584]{1,0:T(8,128)(2,1)}, u32[]{:S(2)}) copy-start(bf16[2048,3584]{1,0:T(8,128)(2,1)} %gate_ref.3) | copy-start | bytes 44040196
  36.7 6.1 %collective-permute-start.15 = (bf16[8,2048]{1,0:T(8,128)(2,1)S(1)}, bf16[8,2048]{1,0:T(8,128)(2,1)S(1)}, u32[]{:S(2)}, u32[]{:S(2)}) collective-permute-start(bf16[8,2048]{1,0:T(8,128)(2,1)S(1)} %get-tuple-element.73), channel_id=1, source_target_pairs={{0,12},{1,13},{2,14},{3,15},{4,8},{5,9},{6,10},{7,11},{8,4},{9,5},... | collective-permute-start | bytes 98312 | tf_op jit(solution)/shard_map/ppermute | solution.py:49
  38.2 5.1 %collective-permute-start.16 = (bf16[8,2048]{1,0:T(8,128)(2,1)S(1)}, bf16[8,2048]{1,0:T(8,128)(2,1)S(1)}, u32[]{:S(2)}, u32[]{:S(2)}) collective-permute-start(bf16[8,2048]{1,0:T(8,128)(2,1)S(1)} %get-tuple-element.74), channel_id=1, source_target_pairs={{0,8},{1,9},{2,10},{3,11},{4,12},{5,13},{6,14},{7,15},{8,0},{9,1},... | collective-permute-start | bytes 98312 | tf_op jit(solution)/shard_map/ppermute | solution.py:49
  39.3 4.4 %collective-permute-start.17 = (bf16[8,2048]{1,0:T(8,128)(2,1)S(1)}, bf16[8,2048]{1,0:T(8,128)(2,1)S(1)}, u32[]{:S(2)}, u32[]{:S(2)}) collective-permute-start(bf16[8,2048]{1,0:T(8,128)(2,1)S(1)} %get-tuple-element.75), channel_id=1, source_target_pairs={{0,4},{1,5},{2,6},{3,7},{4,0},{5,1},{6,2},{7,3},{8,12},{9,13},{10,... | collective-permute-start | bytes 98312 | tf_op jit(solution)/shard_map/ppermute | solution.py:49
  46.8 3.1 %collective-permute-start.20 = (bf16[8,3712]{1,0:T(8,128)(2,1)S(1)}, bf16[8,3712]{1,0:T(8,128)(2,1)S(1)}, u32[]{:S(2)}, u32[]{:S(2)}) collective-permute-start(bf16[8,3712]{1,0:T(8,128)(2,1)S(1)} %get-tuple-element.81.first_ref), channel_id=1, source_target_pairs={{0,1},{1,0},{2,3},{3,2},{4,5},{5,4},{6,7},{7,6},{8,9},{9,8},{10,11... | collective-permute-start | bytes 178184 | tf_op jit(solution)/shard_map/ppermute | solution.py:30
  49.3 1.5 %collective-permute-start.18 = (bf16[8,3584]{1,0:T(8,128)(2,1)S(1)}, bf16[8,3584]{1,0:T(8,128)(2,1)S(1)}, u32[]{:S(2)}, u32[]{:S(2)}) collective-permute-start(bf16[8,3584]{1,0:T(8,128)(2,1)S(1)} %get-tuple-element.79.first_ref), channel_id=1, source_target_pairs={{0,1},{1,0},{2,3},{3,2},{4,5},{5,4},{6,7},{7,6},{8,9},{9,8},{10,11... | collective-permute-start | bytes 172040 | tf_op jit(solution)/shard_map/ppermute | solution.py:30
  49.9 5.1 %collective-permute-start.21 = (bf16[8,3712]{1,0:T(8,128)(2,1)S(1)}, bf16[8,3712]{1,0:T(8,128)(2,1)S(1)}, u32[]{:S(2)}, u32[]{:S(2)}) collective-permute-start(bf16[8,3712]{1,0:T(8,128)(2,1)S(1)} %pair_sum.3.near_ref), channel_id=1, source_target_pairs={{0,2},{1,3},{2,0},{3,1},{4,6},{5,7},{6,4},{7,5},{8,10},{9,11},{10,... | collective-permute-start | bytes 178184 | tf_op jit(solution)/shard_map/ppermute | solution.py:30
  50.8 5.5 %collective-permute-start.19 = (bf16[8,3584]{1,0:T(8,128)(2,1)S(1)}, bf16[8,3584]{1,0:T(8,128)(2,1)S(1)}, u32[]{:S(2)}, u32[]{:S(2)}) collective-permute-start(bf16[8,3584]{1,0:T(8,128)(2,1)S(1)} %pair_sum.2.refs_1_.near_ref), channel_id=1, source_target_pairs={{0,2},{1,3},{2,0},{3,1},{4,6},{5,7},{6,4},{7,5},{8,10},{9,11},{10,... | collective-permute-start | bytes 172040 | tf_op jit(solution)/shard_map/ppermute | solution.py:30
  57.6 5.5 %collective-permute-start.22 = (bf16[2,2048]{1,0:T(2,128)(2,1)S(1)}, bf16[2,2048]{1,0:T(2,128)(2,1)S(1)}, u32[]{:S(2)}, u32[]{:S(2)}) collective-permute-start(bf16[2,2048]{1,0:T(2,128)(2,1)S(1)} %get-tuple-element.85), channel_id=1, source_target_pairs={{0,12},{1,13},{2,14},{3,15},{4,8},{5,9},{6,10},{7,11},{8,4},{9,5},... | collective-permute-start | bytes 24584 | tf_op jit(solution)/shard_map/ppermute | solution.py:49
  59.8 4.5 %collective-permute-start.23 = (bf16[2,2048]{1,0:T(2,128)(2,1)S(1)}, bf16[2,2048]{1,0:T(2,128)(2,1)S(1)}, u32[]{:S(2)}, u32[]{:S(2)}) collective-permute-start(bf16[2,2048]{1,0:T(2,128)(2,1)S(1)} %get-tuple-element.86), channel_id=1, source_target_pairs={{0,8},{1,9},{2,10},{3,11},{4,12},{5,13},{6,14},{7,15},{8,0},{9,1},... | collective-permute-start | bytes 24584 | tf_op jit(solution)/shard_map/ppermute | solution.py:49
  60.5 3.9 %collective-permute-start.24 = (bf16[2,2048]{1,0:T(2,128)(2,1)S(1)}, bf16[2,2048]{1,0:T(2,128)(2,1)S(1)}, u32[]{:S(2)}, u32[]{:S(2)}) collective-permute-start(bf16[2,2048]{1,0:T(2,128)(2,1)S(1)} %get-tuple-element.87), channel_id=1, source_target_pairs={{0,4},{1,5},{2,6},{3,7},{4,0},{5,1},{6,2},{7,3},{8,12},{9,13},{10,... | collective-permute-start | bytes 24584 | tf_op jit(solution)/shard_map/ppermute | solution.py:49

commit v10 on v9

--- a/solution.py
+++ b/solution.py
@@ -174,7 +174,8 @@
     wide = join_rows(refs[:slots][::-1], rows_s)
     rows_ref[...] = wide
     total = jnp.sum(wide * wide, axis=1, keepdims=True)
-    scaled = (wide * gain_ref[...].astype(jnp.float32)[None, :]).astype(jnp.bfloat16)
+    gain = gain_ref[...].astype(jnp.float32)[None, :]
+    scaled = (wide * gain).astype(jnp.bfloat16)
     query_cols = wq_ref.shape[1]
     kv_cols = wkv_ref.shape[1]
 
@@ -238,7 +239,7 @@
     *refs,
 ):
     parts = refs[:shards]
-    out_ref, query_s, kv_s, kv_wide_s, mixed_s, stats_s = refs[shards:]
+    out_ref, query_s, kv_s, kv_wide_s, mixed_s, stats_s = refs[-6:]
     all_rows = parts[0].shape[0]
     own_rows = all_rows // slots
     here = HEADS // slots
@@ -324,13 +325,13 @@
     out_ref[:, HEAD_DIM:] = stats_s[...].astype(jnp.bfloat16)
 
 
-def attend(lengths, cosine, sine, parts, keys, values, slots):
+def attend(lengths, cosine, sine, parts, keys, values, later, slots):
     own_rows = parts[0].shape[0] // slots
     kv_cols = 2 * KV_HEADS * HEAD_DIM // slots
     return pl.pallas_call(
         functools.partial(attend_kernel, slots, len(parts)),
         out_shape=jax.ShapeDtypeStruct((own_rows * HEADS, HEAD_DIM + LANES), jnp.bfloat16),
-        in_specs=[in_vmem] * (5 + len(parts)),
+        in_specs=[in_vmem] * (5 + len(parts)) + [in_place] * len(later),
         out_specs=in_vmem,
         scratch_shapes=[
             pltpu.VMEM((own_rows * HEADS, HEAD_DIM), jnp.float32),
@@ -341,7 +342,7 @@
         ],
         compiler_params=params(6),
         name="attend",
-    )(lengths, cosine, sine, resident(keys), resident(values), *parts[::-1])
+    )(lengths, cosine, sine, resident(keys), resident(values), *parts[::-1], *[resident(w) for w in later])
 
 
 def combine_kernel(shards, slots, *refs):
@@ -455,14 +456,9 @@
     product_tiles(scaled, up_ref, store(count), first, count)
 
 
-def first_gate_up_kernel(
-    slots, count, start, rows_ref, gain_ref, gate_ref, up_ref, down_ref, *refs
-):
+def first_gate_up_kernel(slots, count, rows_ref, gain_ref, gate_ref, up_ref, *refs):
     parts = refs[:slots]
-    out_ref, updated_ref, scaled_ref, loaded_ref, sems = refs[-5:]
-    copies = copies_of(down_ref, start, loaded_ref, sems)
-    for copy in copies:
-        copy.start()
+    out_ref, updated_ref, scaled_ref = refs[-3:]
     own_rows = updated_ref.shape[0]
     total = functools.reduce(jnp.add, [ref[...].astype(jnp.float32) for ref in parts])
     updated = (rows_ref[...] + total).astype(jnp.bfloat16)
@@ -473,65 +469,41 @@
     scaled = (wide * gain_ref[...].astype(jnp.float32)[None, :]).astype(jnp.bfloat16)
     scaled_ref[...] = scaled
     gate_up_tiles(scaled, gate_ref, up_ref, out_ref, 0, count)
-    for copy in copies:
-        copy.wait()
-
-
-def first_gate_up(rows, gain, parts, w_gate, w_up, w_down, span, later, count, own_rows):
+
+
+def first_gate_up(rows, gain, parts, w_gate, w_up, later, count, own_rows):
     slots = len(parts)
-    start, size = span
-    return pl.pallas_call(
-        functools.partial(first_gate_up_kernel, slots, count, start),
+    return pl.pallas_call(
+        functools.partial(first_gate_up_kernel, slots, count),
         out_shape=(
             jax.ShapeDtypeStruct((rows.shape[0], 2 * count + LANES), jnp.bfloat16),
             jax.ShapeDtypeStruct((own_rows, rows.shape[1]), jnp.float32),
             jax.ShapeDtypeStruct(rows.shape, jnp.bfloat16),
-            pltpu.VMEM((size, w_down.shape[1]), w_down.dtype),
         ),
-        in_specs=[in_vmem] * 4 + [in_place] + [in_vmem] * slots + [in_place] * len(later),
-        out_specs=(in_vmem,) * 4,
-        scratch_shapes=[pltpu.SemaphoreType.DMA((COPIES,))],
+        in_specs=[in_vmem] * (4 + slots) + [in_place] * len(later),
+        out_specs=(in_vmem,) * 3,
         compiler_params=params(3),
         cost_estimate=product_cost(w_gate.shape[0], 2 * count),
         name="first_gate_up",
-    )(
-        rows,
-        gain,
-        resident(w_gate),
-        resident(w_up),
-        in_hbm(w_down),
-        *parts[::-1],
-        *[resident(w) for w in later],
-    )
-
-
-def second_gate_up_kernel(
-    first, count, start, scaled_ref, gate_ref, up_ref, down_ref, out_ref, loaded_ref, sems
-):
-    copies = copies_of(down_ref, start, loaded_ref, sems)
-    for copy in copies:
-        copy.start()
+    )(rows, gain, resident(w_gate), resident(w_up), *parts[::-1], *[resident(w) for w in later])
+
+
+def second_gate_up_kernel(first, count, scaled_ref, gate_ref, up_ref, *refs):
+    out_ref = refs[-1]
     gate_up_tiles(scaled_ref[...], gate_ref, up_ref, out_ref, first, count)
-    for copy in copies:
-        copy.wait()
-
-
-def second_gate_up(scaled, w_gate, w_up, w_down, span, first):
+
+
+def second_gate_up(scaled, w_gate, w_up, later, first):
     count = w_gate.shape[1] - first
-    start, size = span
-    return pl.pallas_call(
-        functools.partial(second_gate_up_kernel, first, count, start),
-        out_shape=(
-            jax.ShapeDtypeStruct((scaled.shape[0], 2 * count), jnp.bfloat16),
-            pltpu.VMEM((size, w_down.shape[1]), w_down.dtype),
-        ),
-        in_specs=[in_vmem] * 3 + [in_place],
-        out_specs=(in_vmem,) * 2,
-        scratch_shapes=[pltpu.SemaphoreType.DMA((COPIES,))],
+    return pl.pallas_call(
+        functools.partial(second_gate_up_kernel, first, count),
+        out_shape=jax.ShapeDtypeStruct((scaled.shape[0], 2 * count), jnp.bfloat16),
+        in_specs=[in_vmem] * 3 + [in_place] * len(later),
+        out_specs=in_vmem,
         compiler_params=params(3),
         cost_estimate=product_cost(w_gate.shape[0], 2 * count),
         name="second_gate_up",
-    )(scaled, resident(w_gate), resident(w_up), in_hbm(w_down))
+    )(scaled, resident(w_gate), resident(w_up), *[resident(w) for w in later])
 
 
 def hidden_of(near_ref, far_ref, scale, count):
@@ -543,10 +515,7 @@
     return (gate / (1.0 + jnp.exp(-gate)) * total(count)).astype(jnp.bfloat16)
 
 
-def first_down_kernel(near_ref, far_ref, one_ref, two_ref, later_ref, out_ref, scale_ref):
-    del later_ref
-    cut = one_ref.shape[0]
-    count = (near_ref.shape[1] - LANES) // 2
+def first_down_kernel(count, near_ref, far_ref, weight_ref, out_ref, scale_ref):
     squares = jnp.sum(
         near_ref[:, 2 * count :].astype(jnp.float32) + far_ref[:, 2 * count :].astype(jnp.float32),
         axis=1,
@@ -554,64 +523,70 @@
     )
     scale = lax.rsqrt(squares / D + epsilon)
     scale_ref[...] = jnp.broadcast_to(scale, scale_ref.shape)
-    hidden = hidden_of(near_ref, far_ref, scale, count)
-    lower_ref = two_ref.at[: count - cut]
+
+    def store(start, size, value):
+        out_ref[:, pl.ds(start, size)] = value
+
+    product_tiles(hidden_of(near_ref, far_ref, scale, count), weight_ref.at[:count], store)
+
+
+def first_down(near, far, weight, count):
+    rows = near.shape[0]
+    return pl.pallas_call(
+        functools.partial(first_down_kernel, count),
+        out_shape=(
+            jax.ShapeDtypeStruct((rows, weight.shape[1]), jnp.float32),
+            jax.ShapeDtypeStruct((rows, LANES), jnp.float32),
+        ),
+        in_specs=[in_vmem] * 3,
+        out_specs=(in_vmem,) * 2,
+        compiler_params=params(3),
+        cost_estimate=product_cost(count, weight.shape[1]),
+        name="first_down",
+    )(near, far, resident(weight))
+
+
+def second_down_kernel(count, near_ref, far_ref, weight_ref, part_ref, scale_ref, *refs):
+    out_s = refs[-1]
+    first = weight_ref.shape[0] - count
 
     def store(start, size, value):
         span = pl.ds(start, size)
-        out_ref[:, span] = value + jnp.dot(
-            hidden[:, cut:], lower_ref[:, span], preferred_element_type=jnp.float32
-        )
-
-    product_tiles(hidden[:, :cut], one_ref, store)
-
-
-def first_down(near, far, one, two, later):
-    rows = near.shape[0]
-    columns = one.shape[1]
-    return pl.pallas_call(
-        first_down_kernel,
-        out_shape=(
-            jax.ShapeDtypeStruct((rows, columns), jnp.float32),
-            jax.ShapeDtypeStruct((rows, LANES), jnp.float32),
-        ),
-        in_specs=[in_vmem] * 4 + [in_place],
-        out_specs=(in_vmem,) * 2,
-        compiler_params=params(3),
-        cost_estimate=product_cost((near.shape[1] - LANES) // 2, columns),
-        name="first_down",
-    )(near, far, resident(one), resident(two), resident(later))
-
-
-def second_down_kernel(near_ref, far_ref, two_ref, three_ref, part_ref, scale_ref, *refs):
-    out_s = refs[-1]
-    count = near_ref.shape[1] // 2
-    cut = count - three_ref.shape[0]
+        out_s[:, span] = part_ref[:, span] + value
+
     hidden = hidden_of(near_ref, far_ref, scale_ref[:, 0:1], count)
-    upper_ref = two_ref.at[two_ref.shape[0] - cut :]
-
-    def store(start, size, value):
-        span = pl.ds(start, size)
-        out_s[:, span] = part_ref[:, span] + (
-            value
-            + jnp.dot(hidden[:, :cut], upper_ref[:, span], preferred_element_type=jnp.float32)
-        )
-
-    product_tiles(hidden[:, cut:], three_ref, store)
+    product_tiles(hidden, weight_ref.at[first:], store)
     part_rows(out_s, refs[:-1])
 
 
-def second_down(near, far, two, three, part, scale, slots):
+def second_down(near, far, weight, part, scale, slots):
     rows, columns = part.shape
-    return pl.pallas_call(
-        second_down_kernel,
+    count = near.shape[1] // 2
+    return pl.pallas_call(
+        functools.partial(second_down_kernel, count),
         out_shape=(jax.ShapeDtypeStruct((rows // slots, columns), jnp.bfloat16),) * slots,
-        in_specs=[in_vmem] * 6,
+        in_specs=[in_vmem] * 5,
         out_specs=(in_vmem,) * slots,
         scratch_shapes=[pltpu.VMEM(part.shape, jnp.float32)],
         compiler_params=params(3),
         name="second_down",
-    )(near, far, resident(two), resident(three), part, scale)
+    )(near, far, resident(weight), part, scale)
+
+
+def finish_kernel(updated_ref, *refs):
+    total = functools.reduce(jnp.add, [ref[...].astype(jnp.float32) for ref in refs[:-1]])
+    refs[-1][...] = (updated_ref[...] + total).astype(jnp.bfloat16)
+
+
+def finish(updated, parts):
+    return pl.pallas_call(
+        finish_kernel,
+        out_shape=jax.ShapeDtypeStruct(updated.shape, jnp.bfloat16),
+        in_specs=[in_vmem] * (1 + len(parts)),
+        out_specs=in_vmem,
+        compiler_params=params(1),
+        name="finish",
+    )(updated, *parts[::-1])
 
 
 def rotation_tables(positions, repeats):
@@ -661,35 +636,25 @@
     joined, keys, values = lax.optimization_barrier((joined, keys, values))
     (w_out,) = load(w_out, after=joined)
     parts, w_out = lax.optimization_barrier((exchange(joined, "inner")[::-1], w_out))
-    shard = attend(my_lengths, cosine, sine, parts, keys, values, slots)
-
-    pieces = combine(exchange(shard, "inner"), [], all_rows, slots)
-    parts = scatter_slots(project_out(scatter_slots(pieces, 1), w_out, [w_up]), 0)
+    shard = attend(my_lengths, cosine, sine, parts, keys, values, [w_gate], slots)
+
+    pieces = combine(exchange(shard, "inner"), [w_up], all_rows, slots)
+    parts = scatter_slots(project_out(scatter_slots(pieces, 1), w_out, [w_down]), 0)
 
     tiles = w_gate.shape[1] // LANES
-    half = (tiles + 1) // 2
-    first = half * LANES
-    span = tiles // 4
-    starts = [0, span * LANES, (span + max(tiles * 9 // 28, half - span + 1)) * LANES, tiles * LANES]
-    spans = [(a, b - a) for a, b in zip(starts, starts[1:])]
-    one, updated, scaled, down_one = first_gate_up(
-        rows, ffn_gain, parts, w_gate, w_up, w_down, spans[0], [], first, own_rows
-    )
-    two, down_two = second_gate_up(scaled, w_gate, w_up, w_down, spans[1], first)
+    first = (tiles + 1) // 2 * LANES
+    one, updated, scaled = first_gate_up(
+        rows, ffn_gain, parts, w_gate, w_up, [], first, own_rows
+    )
+    two = second_gate_up(scaled, w_gate, w_up, [], first)
     steps = steps_up(lax.axis_size("inner"))
     for step in steps[:-1]:
         one = pair_sum(one, swap_with(one, "inner", step))
         two = pair_sum(two, swap_with(two, "inner", step))
-    (down_three,) = load(w_down, after=two, spans=[spans[2]])
-    part, scale = first_down(
-        one, swap_with(one, "inner", steps[-1]), down_one, down_two, down_three
-    )
-    pieces = second_down(
-        two, swap_with(two, "inner", steps[-1]), down_two, down_three, part, scale, slots
-    )
+    part, scale = first_down(one, swap_with(one, "inner", steps[-1]), w_down, first)
+    pieces = second_down(two, swap_with(two, "inner", steps[-1]), w_down, part, scale, slots)
     parts = scatter_slots(pieces, 0)
-    down_sum = sum(p.astype(jnp.float32) for p in parts[::-1])
-    return (updated + down_sum).astype(jnp.bfloat16)
+    return finish(updated, parts)
 
 
 def solution(mesh):

time: 65.1 us -> 68.7 us (1.055)
  local copies, waits for them, and re-layouts: 0.09 us -> 5.8 us
  Pallas kernels: 22.3 us -> 18.4 us
  waiting for transfers between devices: 12.4 us -> 16 us
  starting transfers between devices: 29.2 us -> 27.9 us
    unnamed x6 -> x28, local copies, waits for them, and re-layouts: 0.01 us -> 5.73 us
    pallas_call x4 -> x3, Pallas kernels: 10.2 us -> 7.38 us  [load(): pl.pallas_call(functools.partial(load_kernel, spans), out_shape=tuple((pl...]
    ppermute x13, waiting for transfers between devices: 5.33 us -> 7.87 us  [swap_with(): return lax.ppermute(value, axis, [(i, i ^ step) for i in range(count)])]
    ppermute x12, starting transfers between devices: 15.6 us -> 14.5 us  [scatter_slots(): got.append(lax.ppermute(pieces[k], ('tensor', 'inner'), pairs))]
    ppermute x12, waiting for transfers between devices: 7.1 us -> 8.11 us  [scatter_slots(): got.append(lax.ppermute(pieces[k], ('tensor', 'inner'), pairs))]
    pallas_call x4 -> x5, Pallas kernels: 8.19 us -> 7.24 us  [the longest x1 2.01 us: second_gate_up(): pl.pallas_call(functools.partial(second_gate_up_kernel, first, count), ou...]
  transfers between devices with their start and end apart: 25 -> 25, of which waited for: 12 -> 11; matrix products, arithmetic and copies ran while one was open for 0% -> 0% of each run, Pallas kernels for 22% -> 16%
where the time goes in v10:
time: 68.7 us; the launch traced here: 68.6 us
  starting transfers between devices  27.9 us (41%)
  Pallas kernels  18.4 us (27%)
  waiting for transfers between devices  16 us (23%)
  local copies, waits for them, and re-layouts  5.8 us (8%)
    ppermute x12, starting transfers between devices, scatter_slots(): got.append(lax.ppermute(pieces[k], ('tensor', 'inner'), pairs))  14.5 us
    ppermute x13, starting transfers between devices, swap_with(): return lax.ppermute(value, axis, [(i, i ^ step) for i in range(count)])  13.4 us
    ppermute x12, waiting for transfers between devices, scatter_slots(): got.append(lax.ppermute(pieces[k], ('tensor', 'inner'), pairs))  8.11 us
    ppermute x13, waiting for transfers between devices, swap_with(): return lax.ppermute(value, axis, [(i, i ^ step) for i in range(count)])  7.87 us
    pallas_call x3, Pallas kernels, load(): pl.pallas_call(functools.partial(load_kernel, spans), out_shape=tuple((pl...  7.38 us
    unnamed x28, local copies, waits for them, and re-layouts  5.73 us
    pallas_call x1, Pallas kernels, second_gate_up(): pl.pallas_call(functools.partial(second_gate_up_kernel, first, count), ou...  2.01 us
    pallas_call x1, Pallas kernels, first_gate_up(): pl.pallas_call(functools.partial(first_gate_up_kernel, slots, count), out...  2 us
  transfers between devices with their start and end apart: 25, of which 11 were waited for; matrix products, arithmetic and copies ran while one was open for 0% of the time, Pallas kernels for 16%

profile of v10, /device:TPU:0, one launch (start us, length us, event | category | flops | bytes accessed | tf_op | source)
XLA Modules:
  0.0 68.6 jit_solution(15872375318722243418)
XLA Ops:
  0.0 5.0 %collective-permute-start = (bf16[2,2048]{1,0:T(2,128)(2,1)}, bf16[2,2048]{1,0:T(2,128)(2,1)S(1)}, u32[]{:S(2)}, u32[]{:S(2)}) collective-permute-start(bf16[2,2048]{1,0:T(2,128)(2,1)} %refs_5_.1), channel_id=1, source_target_pairs={{0,12},{4,8},{8,4},{12,0},{1,13},{5,9},{9,5},{13,1},{2,14},{6,10},... | collective-permute-start | bytes 24584 | tf_op jit(solution)/shard_map/ppermute | solution.py:30
  5.0 0.0 collective-permute-start.1
  5.1 0.6 collective-permute-start.2
  5.6 2.7 %load.3 = (bf16[2,2048]{1,0:T(2,128)(2,1)S(1)}, bf16[2048]{0:T(1024)(128)(2,1)S(1)}, bf16[2048]{0:T(1024)(128)(2,1)S(1)}, bf16[2048,256]{1,0:T(8,128)(2,1)S(1)}, bf16[2048,1024]{1,0:T(8,128)(2,1)S(1)}) custom-call(bf16[2,2048]{1,0:T(2,128)(2,1)} %refs_5_.1, bf16[2048]{0:T(1024)(128)(2,1)} %refs_1_.1, bf16[2048]{0:T(1024)(128)(2,1)} %refs_2_.1, ...), custom_call_target="tpu_custom_call" | custom-call | bytes 5259264 | tf_op jit(solution)/shard_map/load/pallas_call | solution.py:144
  8.4 1.4 %collective-permute-done.1.refs_1_ = bf16[2,2048]{1,0:T(2,128)(2,1)S(1)} collective-permute-done((bf16[2,2048]{1,0:T(2,128)(2,1)}, bf16[2,2048]{1,0:T(2,128)(2,1)S(1)}, u32[]{:S(2)}, u32[]{:S(2)}) %collective-permute-start.1) | collective-permute-done | bytes 8224 | tf_op jit(solution)/shard_map/ppermute | solution.py:30
  9.8 0.8 %project_qkv.1 = (f32[8,2048]{1,0:T(8,128)S(1)}, bf16[2,1408]{1,0:T(2,128)(2,1)S(1)}, bf16[2,1408]{1,0:T(2,128)(2,1)S(1)}, bf16[2,1408]{1,0:T(2,128)(2,1)S(1)}, bf16[2,1408]{1,0:T(2,128)(2,1)S(1)}) custom-call(bf16[2048]{0:T(1024)(128)(2,1)S(1)} %get-tuple-element.44.gain_ref, bf16[2048,1024]{1,0:T(8,128)(2,1)S(1)} %get-tuple-element.45.wq_ref, ...), custom_call_target="tpu_custom_call" | custom-call | tf_op jit(solution)/shard_map/project_qkv/pallas_call | solution.py:197
  10.6 1.1 %collective-permute-start.3 = (bf16[2,1408]{1,0:T(2,128)(2,1)S(1)}, bf16[2,1408]{1,0:T(2,128)(2,1)S(1)}, u32[]{:S(2)}, u32[]{:S(2)}) collective-permute-start(bf16[2,1408]{1,0:T(2,128)(2,1)S(1)} %get-tuple-element.51), channel_id=1, source_target_pairs={{0,13},{1,12},{2,15},{3,14},{4,9},{5,8},{6,11},{7,10},{8,5},{9,4},... | collective-permute-start | bytes 16904 | tf_op jit(solution)/shard_map/ppermute | solution.py:49
  11.7 0.2 collective-permute-start.4
  11.9 1.5 %collective-permute-start.5 = (bf16[2,1408]{1,0:T(2,128)(2,1)S(1)}, bf16[2,1408]{1,0:T(2,128)(2,1)S(1)}, u32[]{:S(2)}, u32[]{:S(2)}) collective-permute-start(bf16[2,1408]{1,0:T(2,128)(2,1)S(1)} %get-tuple-element.53), channel_id=1, source_target_pairs={{0,5},{1,4},{2,7},{3,6},{4,1},{5,0},{6,3},{7,2},{8,13},{9,12},{10,... | collective-permute-start | bytes 16904 | tf_op jit(solution)/shard_map/ppermute | solution.py:49
  13.5 0.1 fusion.4
  13.6 2.3 %load.4 = (bf16[2,4096,128]{2,1,0:T(8,128)(2,1)S(1)}, bf16[2,4096,128]{2,1,0:T(8,128)(2,1)S(1)}) custom-call(bf16[2,4096,128]{2,1,0:T(8,128)(2,1)} %bitcast.12, bf16[2,4096,128]{2,1,0:T(8,128)(2,1)} %bitcast.13, f32[8,2048]{1,0:T(8,128)S(1)} %get-tuple-element.49.refs_2_.rows_ref), custom_call_target="tpu_custom_call" | custom-call | bytes 4194304 | tf_op jit(solution)/shard_map/load/pallas_call | solution.py:144
  15.8 0.0 collective-permute-done.3.refs_0_
  15.9 0.0 collective-permute-done.4.refs_1_
  15.9 2.6 %collective-permute-start.6 = (bf16[8,1408]{1,0:T(8,128)(2,1)S(1)}, bf16[8,1408]{1,0:T(8,128)(2,1)S(1)}, u32[]{:S(2)}, u32[]{:S(2)}) collective-permute-start(bf16[8,1408]{1,0:T(8,128)(2,1)S(1)} %stack.1.refs_1_.refs_0_), channel_id=1, source_target_pairs={{0,3},{1,2},{2,1},{3,0},{4,7},{5,6},{6,5},{7,4},{8,11},{9,10},{10,... | collective-permute-start | bytes 67592 | tf_op jit(solution)/shard_map/ppermute | solution.py:30
  18.5 0.5 collective-permute-start.7
  19.1 0.1 fusion
  19.2 0.0 slice-start
  19.2 0.0 slice-start.1
  19.2 2.4 %load.5.weight_ref = bf16[1024,2048]{1,0:T(8,128)(2,1)S(1)} custom-call(bf16[1024,2048]{1,0:T(8,128)(2,1)} %refs_0_.3, bf16[8,1408]{1,0:T(8,128)(2,1)S(1)} %stack.1.refs_1_.refs_0_), custom_call_target="tpu_custom_call" | custom-call | bytes 4194304 | tf_op jit(solution)/shard_map/load/pallas_call | solution.py:144
  21.6 0.8 %collective-permute-done.7.refs_2_ = bf16[8,1408]{1,0:T(8,128)(2,1)S(1)} collective-permute-done((bf16[8,1408]{1,0:T(8,128)(2,1)S(1)}, bf16[8,1408]{1,0:T(8,128)(2,1)S(1)}, u32[]{:S(2)}, u32[]{:S(2)}) %collective-permute-start.7) | collective-permute-done | bytes 22560 | tf_op jit(solution)/shard_map/ppermute | solution.py:30
  22.3 0.1 broadcast_in_dim.10.lengths_ref
  22.4 5.7 %copy-done = bf16[2048,3584]{1,0:T(8,128)(2,1)S(1)} copy-done((bf16[2048,3584]{1,0:T(8,128)(2,1)S(1)}, bf16[2048,3584]{1,0:T(8,128)(2,1)}, u32[]{:S(2)}) %copy-start) | copy-done | bytes 14680088
  28.1 0.0 slice-start.6
  28.1 1.7 %attend.1.refs_3_ = bf16[64,256]{1,0:T(8,128)(2,1)S(1)} custom-call(s32[2,128]{1,0:T(2,128)S(1)} %broadcast_in_dim.10.lengths_ref, f32[8,128]{1,0:T(8,128)S(1)} %bitcast.10, f32[8,128]{1,0:T(8,128)S(1)} %bitcast.11, bf16[2,4096,128]{2,1,0:T(8,128)(2,1)S(1)} %get-tuple-element.60.key_ref, bf16[2,4096,128]{2,1,0:T(8,128)(2,1)S(1)} %get-tuple-element.61.value_ref, ...), custom_call_target="tpu_custom_call" | custom-call | tf_op jit(solution)/shard_map/attend/pallas_call | solution.py:331
  29.8 0.0 slice-start.7
  29.8 1.2 %collective-permute-start.9 = (bf16[64,256]{1,0:T(8,128)(2,1)S(1)}, bf16[64,256]{1,0:T(8,128)(2,1)S(1)}, u32[]{:S(2)}, u32[]{:S(2)}) collective-permute-start(bf16[64,256]{1,0:T(8,128)(2,1)S(1)} %attend.1.refs_3_), channel_id=1, source_target_pairs={{0,3},{1,2},{2,1},{3,0},{4,7},{5,6},{6,5},{7,4},{8,11},{9,10},{10,... | collective-permute-start | bytes 98312 | tf_op jit(solution)/shard_map/ppermute | solution.py:30
  31.1 0.5 collective-permute-start.10
  31.6 0.2 collective-permute-start.11
  31.8 1.6 %collective-permute-done.9.refs_0_ = bf16[64,256]{1,0:T(8,128)(2,1)S(1)} collective-permute-done((bf16[64,256]{1,0:T(8,128)(2,1)S(1)}, bf16[64,256]{1,0:T(8,128)(2,1)S(1)}, u32[]{:S(2)}, u32[]{:S(2)}) %collective-permute-start.9) | collective-permute-done | bytes 32800 | tf_op jit(solution)/shard_map/ppermute | solution.py:30
  33.4 1.6 %collective-permute-done.10.refs_1_ = bf16[64,256]{1,0:T(8,128)(2,1)S(1)} collective-permute-done((bf16[64,256]{1,0:T(8,128)(2,1)S(1)}, bf16[64,256]{1,0:T(8,128)(2,1)S(1)}, u32[]{:S(2)}, u32[]{:S(2)}) %collective-permute-start.10) | collective-permute-done | bytes 32800 | tf_op jit(solution)/shard_map/ppermute | solution.py:30
  35.0 0.0 collective-permute-done.11.refs_2_
  35.0 0.0 slice-start.8
  35.0 0.0 slice-start.9
  35.0 0.3 combine.1
  35.3 0.9 %collective-permute-start.12 = (bf16[2,1024]{1,0:T(2,128)(2,1)S(1)}, bf16[2,1024]{1,0:T(2,128)(2,1)S(1)}, u32[]{:S(2)}, u32[]{:S(2)}) collective-permute-start(bf16[2,1024]{1,0:T(2,128)(2,1)S(1)} %get-tuple-element.66), channel_id=1, source_target_pairs={{0,13},{1,12},{2,15},{3,14},{4,9},{5,8},{6,11},{7,10},{8,5},{9,4},... | collective-permute-start | bytes 12296 | tf_op jit(solution)/shard_map/ppermute | solution.py:49
  36.2 0.6 collective-permute-start.13
  36.8 1.3 %collective-permute-start.14 = (bf16[2,1024]{1,0:T(2,128)(2,1)S(1)}, bf16[2,1024]{1,0:T(2,128)(2,1)S(1)}, u32[]{:S(2)}, u32[]{:S(2)}) collective-permute-start(bf16[2,1024]{1,0:T(2,128)(2,1)S(1)} %get-tuple-element.68), channel_id=1, source_target_pairs={{0,5},{1,4},{2,7},{3,6},{4,1},{5,0},{6,3},{7,2},{8,13},{9,12},{10,... | collective-permute-start | bytes 12296 | tf_op jit(solution)/shard_map/ppermute | solution.py:49
  38.1 2.1 %collective-permute-done.12.refs_0_ = bf16[2,1024]{1,0:T(2,128)(2,1)S(1)} collective-permute-done((bf16[2,1024]{1,0:T(2,128)(2,1)S(1)}, bf16[2,1024]{1,0:T(2,128)(2,1)S(1)}, u32[]{:S(2)}, u32[]{:S(2)}) %collective-permute-start.12) | collective-permute-done | bytes 4128 | tf_op jit(solution)/shard_map/ppermute | solution.py:49
  40.2 0.0 collective-permute-done.13.refs_1_
  40.2 0.0 collective-permute-done.14.refs_2_
  40.3 0.0 slice-start.10
  40.3 1.0 %project_out.1 = (bf16[8,2048]{1,0:T(8,128)(2,1)S(1)}, bf16[8,2048]{1,0:T(8,128)(2,1)S(1)}, bf16[8,2048]{1,0:T(8,128)(2,1)S(1)}, bf16[8,2048]{1,0:T(8,128)(2,1)S(1)}) custom-call(bf16[1024,2048]{1,0:T(8,128)(2,1)S(1)} %load.5.weight_ref, bf16[2,1024]{1,0:T(2,128)(2,1)S(1)} %collective-permute-done.12.refs_0_, ...), custom_call_target="tpu_custom_call" | custom-call | tf_op jit(solution)/shard_map/project_out/pallas_call | solution.py:420
  41.2 2.4 %collective-permute-start.15 = (bf16[8,2048]{1,0:T(8,128)(2,1)S(1)}, bf16[8,2048]{1,0:T(8,128)(2,1)S(1)}, u32[]{:S(2)}, u32[]{:S(2)}) collective-permute-start(bf16[8,2048]{1,0:T(8,128)(2,1)S(1)} %get-tuple-element.70), channel_id=1, source_target_pairs={{0,12},{1,13},{2,14},{3,15},{4,8},{5,9},{6,10},{7,11},{8,4},{9,5},... | collective-permute-start | bytes 98312 | tf_op jit(solution)/shard_map/ppermute | solution.py:49
  43.7 1.3 %collective-permute-start.16 = (bf16[8,2048]{1,0:T(8,128)(2,1)S(1)}, bf16[8,2048]{1,0:T(8,128)(2,1)S(1)}, u32[]{:S(2)}, u32[]{:S(2)}) collective-permute-start(bf16[8,2048]{1,0:T(8,128)(2,1)S(1)} %get-tuple-element.71), channel_id=1, source_target_pairs={{0,8},{1,9},{2,10},{3,11},{4,12},{5,13},{6,14},{7,15},{8,0},{9,1},... | collective-permute-start | bytes 98312 | tf_op jit(solution)/shard_map/ppermute | solution.py:49
  45.0 0.6 collective-permute-start.17
  45.7 1.4 %collective-permute-done.15.refs_0_ = bf16[8,2048]{1,0:T(8,128)(2,1)S(1)} collective-permute-done((bf16[8,2048]{1,0:T(8,128)(2,1)S(1)}, bf16[8,2048]{1,0:T(8,128)(2,1)S(1)}, u32[]{:S(2)}, u32[]{:S(2)}) %collective-permute-start.15) | collective-permute-done | bytes 32800 | tf_op jit(solution)/shard_map/ppermute | solution.py:49
  47.1 1.6 %collective-permute-done.16.refs_1_ = bf16[8,2048]{1,0:T(8,128)(2,1)S(1)} collective-permute-done((bf16[8,2048]{1,0:T(8,128)(2,1)S(1)}, bf16[8,2048]{1,0:T(8,128)(2,1)S(1)}, u32[]{:S(2)}, u32[]{:S(2)}) %collective-permute-start.16) | collective-permute-done | bytes 32800 | tf_op jit(solution)/shard_map/ppermute | solution.py:49
  48.7 0.3 collective-permute-done.17.refs_2_
  49.0 2.0 %first_gate_up.1 = (bf16[8,3712]{1,0:T(8,128)(2,1)S(1)}, f32[2,2048]{1,0:T(2,128)S(1)}, bf16[8,2048]{1,0:T(8,128)(2,1)S(1)}) custom-call(f32[8,2048]{1,0:T(8,128)S(1)} %get-tuple-element.49.refs_2_.rows_ref, bf16[2048]{0:T(1024)(128)(2,1)S(1)} %get-tuple-element.50.gain_ref, bf16[2048,3584]{1,0:T(8,128)(2,1)S(1)} %bitcast.9, bf16[2048,3584]{1,0:T(8,128)(2,1)S(1)} %bitcast.5, ...), custom_call_target="tpu_custom_call" | custom-call | flops 117440512 | bytes 14680064 | tf_op jit(solution)/shard_map/first_gate_up/pallas_call | solution.py:476
  51.0 0.0 collective-permute-start.20
  51.0 2.0 %second_gate_up.1.first_ref = bf16[8,3584]{1,0:T(8,128)(2,1)S(1)} custom-call(bf16[8,2048]{1,0:T(8,128)(2,1)S(1)} %get-tuple-element.75.scaled_ref, bf16[2048,3584]{1,0:T(8,128)(2,1)S(1)} %bitcast.9, bf16[2048,3584]{1,0:T(8,128)(2,1)S(1)} %bitcast.5), custom_call_target="tpu_custom_call" | custom-call | flops 117440512 | bytes 14680064 | tf_op jit(solution)/shard_map/second_gate_up/pallas_call | solution.py:498
  53.1 0.5 collective-permute-start.18
  53.6 1.1 %collective-permute-start.21 = (bf16[8,3712]{1,0:T(8,128)(2,1)S(1)}, bf16[8,3712]{1,0:T(8,128)(2,1)S(1)}, u32[]{:S(2)}, u32[]{:S(2)}) collective-permute-start(bf16[8,3712]{1,0:T(8,128)(2,1)S(1)} %pair_sum.3.near_ref), channel_id=1, source_target_pairs={{0,2},{1,3},{2,0},{3,1},{4,6},{5,7},{6,4},{7,5},{8,10},{9,11},{10,... | collective-permute-start | bytes 178184 | tf_op jit(solution)/shard_map/ppermute | solution.py:30
  54.7 0.0 collective-permute-done.18.second_ref
  54.8 1.0 %collective-permute-start.19 = (bf16[8,3584]{1,0:T(8,128)(2,1)S(1)}, bf16[8,3584]{1,0:T(8,128)(2,1)S(1)}, u32[]{:S(2)}, u32[]{:S(2)}) collective-permute-start(bf16[8,3584]{1,0:T(8,128)(2,1)S(1)} %pair_sum.2.near_ref), channel_id=1, source_target_pairs={{0,2},{1,3},{2,0},{3,1},{4,6},{5,7},{6,4},{7,5},{8,10},{9,11},{10,... | collective-permute-start | bytes 172040 | tf_op jit(solution)/shard_map/ppermute | solution.py:30
  55.8 2.5 %collective-permute-done.21.far_ref = bf16[8,3712]{1,0:T(8,128)(2,1)S(1)} collective-permute-done((bf16[8,3712]{1,0:T(8,128)(2,1)S(1)}, bf16[8,3712]{1,0:T(8,128)(2,1)S(1)}, u32[]{:S(2)}, u32[]{:S(2)}) %collective-permute-start.21) | collective-permute-done | bytes 59424 | tf_op jit(solution)/shard_map/ppermute | solution.py:30
  58.2 1.3 %first_down.1 = (f32[8,2048]{1,0:T(8,128)S(1)}, f32[8,128]{1,0:T(8,128)S(1)}) custom-call(bf16[8,3712]{1,0:T(8,128)(2,1)S(1)} %pair_sum.3.near_ref, bf16[8,3712]{1,0:T(8,128)(2,1)S(1)} %collective-permute-done.21.far_ref, bf16[3584,2048]{1,0:T(8,128)(2,1)S(1)} %bitcast.7), custom_call_target="tpu_custom_call" | custom-call | flops 58720256 | bytes 7340032 | tf_op jit(solution)/shard_map/first_down/pallas_call | solution.py:535
  59.5 0.0 collective-permute-done.19.far_ref
  59.5 1.3 %second_down.1 = (bf16[2,2048]{1,0:T(2,128)(2,1)S(1)}, bf16[2,2048]{1,0:T(2,128)(2,1)S(1)}, bf16[2,2048]{1,0:T(2,128)(2,1)S(1)}, bf16[2,2048]{1,0:T(2,128)(2,1)S(1)}) custom-call(bf16[8,3584]{1,0:T(8,128)(2,1)S(1)} %pair_sum.2.near_ref, bf16[8,3584]{1,0:T(8,128)(2,1)S(1)} %collective-permute-done.19.far_ref, bf16[3584,2048]{1,0:T(8,128)(2,1)S(1)} %bitcast.7, ...), custom_call_target="tpu_custom_call" | custom-call | tf_op jit(solution)/shard_map/second_down/pallas_call | solution.py:565
  60.9 2.6 %collective-permute-start.22 = (bf16[2,2048]{1,0:T(2,128)(2,1)S(1)}, bf16[2,2048]{1,0:T(2,128)(2,1)S(1)}, u32[]{:S(2)}, u32[]{:S(2)}) collective-permute-start(bf16[2,2048]{1,0:T(2,128)(2,1)S(1)} %get-tuple-element.79), channel_id=1, source_target_pairs={{0,12},{1,13},{2,14},{3,15},{4,8},{5,9},{6,10},{7,11},{8,4},{9,5},... | collective-permute-start | bytes 24584 | tf_op jit(solution)/shard_map/ppermute | solution.py:49
  63.4 1.9 %collective-permute-start.24 = (bf16[2,2048]{1,0:T(2,128)(2,1)S(1)}, bf16[2,2048]{1,0:T(2,128)(2,1)S(1)}, u32[]{:S(2)}, u32[]{:S(2)}) collective-permute-start(bf16[2,2048]{1,0:T(2,128)(2,1)S(1)} %get-tuple-element.81), channel_id=1, source_target_pairs={{0,4},{1,5},{2,6},{3,7},{4,0},{5,1},{6,2},{7,3},{8,12},{9,13},{10,... | collective-permute-start | bytes 24584 | tf_op jit(solution)/shard_map/ppermute | solution.py:49
  65.3 1.1 %collective-permute-done.22.refs_0_ = bf16[2,2048]{1,0:T(2,128)(2,1)S(1)} collective-permute-done((bf16[2,2048]{1,0:T(2,128)(2,1)S(1)}, bf16[2,2048]{1,0:T(2,128)(2,1)S(1)}, u32[]{:S(2)}, u32[]{:S(2)}) %collective-permute-start.22) | collective-permute-done | bytes 8224 | tf_op jit(solution)/shard_map/ppermute | solution.py:49
  66.4 1.6 %collective-permute-done.23.refs_1_ = bf16[2,2048]{1,0:T(2,128)(2,1)S(1)} collective-permute-done((bf16[2,2048]{1,0:T(2,128)(2,1)S(1)}, bf16[2,2048]{1,0:T(2,128)(2,1)S(1)}, u32[]{:S(2)}, u32[]{:S(2)}) %collective-permute-start.23) | collective-permute-done | bytes 8224 | tf_op jit(solution)/shard_map/ppermute | solution.py:49
  68.0 0.6 finish.1
  (38 shorter events, 0.1 us)
Async XLA Ops:
  0.0 8.4 %collective-permute-start = (bf16[2,2048]{1,0:T(2,128)(2,1)}, bf16[2,2048]{1,0:T(2,128)(2,1)S(1)}, u32[]{:S(2)}, u32[]{:S(2)}) collective-permute-start(bf16[2,2048]{1,0:T(2,128)(2,1)} %refs_5_.1), channel_id=1, source_target_pairs={{0,12},{4,8},{8,4},{12,0},{1,13},{5,9},{9,5},{13,1},{2,14},{6,10},... | collective-permute-start | bytes 24584 | tf_op jit(solution)/shard_map/ppermute | solution.py:30
  5.0 4.8 %collective-permute-start.1 = (bf16[2,2048]{1,0:T(2,128)(2,1)}, bf16[2,2048]{1,0:T(2,128)(2,1)S(1)}, u32[]{:S(2)}, u32[]{:S(2)}) collective-permute-start(bf16[2,2048]{1,0:T(2,128)(2,1)} %refs_5_.1), channel_id=1, source_target_pairs={{0,8},{4,12},{8,0},{12,4},{1,9},{5,13},{9,1},{13,5},{2,10},{6,14},... | collective-permute-start | bytes 24584 | tf_op jit(solution)/shard_map/ppermute | solution.py:30
  5.1 4.8 %collective-permute-start.2 = (bf16[2,2048]{1,0:T(2,128)(2,1)}, bf16[2,2048]{1,0:T(2,128)(2,1)S(1)}, u32[]{:S(2)}, u32[]{:S(2)}) collective-permute-start(bf16[2,2048]{1,0:T(2,128)(2,1)} %refs_5_.1), channel_id=1, source_target_pairs={{0,4},{4,0},{8,12},{12,8},{1,5},{5,1},{9,13},{13,9},{2,6},{6,2},{1... | collective-permute-start | bytes 24584 | tf_op jit(solution)/shard_map/ppermute | solution.py:30
  5.6 7.8 %copy-start.1 = (s32[8]{0:T(128)S(1)}, s32[8]{0:T(128)}, u32[]{:S(2)}) copy-start(s32[8]{0:T(128)} %param.23) | copy-start | bytes 100
  10.6 5.2 %collective-permute-start.3 = (bf16[2,1408]{1,0:T(2,128)(2,1)S(1)}, bf16[2,1408]{1,0:T(2,128)(2,1)S(1)}, u32[]{:S(2)}, u32[]{:S(2)}) collective-permute-start(bf16[2,1408]{1,0:T(2,128)(2,1)S(1)} %get-tuple-element.51), channel_id=1, source_target_pairs={{0,13},{1,12},{2,15},{3,14},{4,9},{5,8},{6,11},{7,10},{8,5},{9,4},... | collective-permute-start | bytes 16904 | tf_op jit(solution)/shard_map/ppermute | solution.py:49
  11.7 4.2 %collective-permute-start.4 = (bf16[2,1408]{1,0:T(2,128)(2,1)S(1)}, bf16[2,1408]{1,0:T(2,128)(2,1)S(1)}, u32[]{:S(2)}, u32[]{:S(2)}) collective-permute-start(bf16[2,1408]{1,0:T(2,128)(2,1)S(1)} %get-tuple-element.52), channel_id=1, source_target_pairs={{0,9},{1,8},{2,11},{3,10},{4,13},{5,12},{6,15},{7,14},{8,1},{9,0},... | collective-permute-start | bytes 16904 | tf_op jit(solution)/shard_map/ppermute | solution.py:49
  11.9 3.9 %collective-permute-start.5 = (bf16[2,1408]{1,0:T(2,128)(2,1)S(1)}, bf16[2,1408]{1,0:T(2,128)(2,1)S(1)}, u32[]{:S(2)}, u32[]{:S(2)}) collective-permute-start(bf16[2,1408]{1,0:T(2,128)(2,1)S(1)} %get-tuple-element.53), channel_id=1, source_target_pairs={{0,5},{1,4},{2,7},{3,6},{4,1},{5,0},{6,3},{7,2},{8,13},{9,12},{10,... | collective-permute-start | bytes 16904 | tf_op jit(solution)/shard_map/ppermute | solution.py:49
  15.9 5.7 %collective-permute-start.6 = (bf16[8,1408]{1,0:T(8,128)(2,1)S(1)}, bf16[8,1408]{1,0:T(8,128)(2,1)S(1)}, u32[]{:S(2)}, u32[]{:S(2)}) collective-permute-start(bf16[8,1408]{1,0:T(8,128)(2,1)S(1)} %stack.1.refs_1_.refs_0_), channel_id=1, source_target_pairs={{0,3},{1,2},{2,1},{3,0},{4,7},{5,6},{6,5},{7,4},{8,11},{9,10},{10,... | collective-permute-start | bytes 67592 | tf_op jit(solution)/shard_map/ppermute | solution.py:30
  18.5 3.8 %collective-permute-start.7 = (bf16[8,1408]{1,0:T(8,128)(2,1)S(1)}, bf16[8,1408]{1,0:T(8,128)(2,1)S(1)}, u32[]{:S(2)}, u32[]{:S(2)}) collective-permute-start(bf16[8,1408]{1,0:T(8,128)(2,1)S(1)} %stack.1.refs_1_.refs_0_), channel_id=1, source_target_pairs={{0,2},{1,3},{2,0},{3,1},{4,6},{5,7},{6,4},{7,5},{8,10},{9,11},{10,... | collective-permute-start | bytes 67592 | tf_op jit(solution)/shard_map/ppermute | solution.py:30
  19.1 3.3 %collective-permute-start.8 = (bf16[8,1408]{1,0:T(8,128)(2,1)S(1)}, bf16[8,1408]{1,0:T(8,128)(2,1)S(1)}, u32[]{:S(2)}, u32[]{:S(2)}) collective-permute-start(bf16[8,1408]{1,0:T(8,128)(2,1)S(1)} %stack.1.refs_1_.refs_0_), channel_id=1, source_target_pairs={{0,1},{1,0},{2,3},{3,2},{4,5},{5,4},{6,7},{7,6},{8,9},{9,8},{10,11... | collective-permute-start | bytes 67592 | tf_op jit(solution)/shard_map/ppermute | solution.py:30
  19.2 15.8 %slice-start = ((s8[14680064]{0:T(1024)(128)(4,1)}), s8[4194304]{0:T(1024)(128)(4,1)S(1)}, s32[]{:S(2)}) async-start(s8[14680064]{0:T(1024)(128)(4,1)} %bitcast.4), calls=%async_computation | async-start | bytes 8388608
  19.2 15.8 %slice-start.1 = ((s8[14680064]{0:T(1024)(128)(4,1)}), s8[4194304]{0:T(1024)(128)(4,1)S(1)}, s32[]{:S(2)}) async-start(s8[14680064]{0:T(1024)(128)(4,1)} %bitcast.4), calls=%async_computation.1 | async-start | bytes 8388608
  22.4 5.7 %copy-start = (bf16[2048,3584]{1,0:T(8,128)(2,1)S(1)}, bf16[2048,3584]{1,0:T(8,128)(2,1)}, u32[]{:S(2)}) copy-start(bf16[2048,3584]{1,0:T(8,128)(2,1)} %gate_ref.3) | copy-start | bytes 44040196
  28.1 6.9 %slice-start.2 = ((s8[14680064]{0:T(1024)(128)(4,1)}), s8[4194304]{0:T(1024)(128)(4,1)S(1)}, s32[]{:S(2)}) async-start(s8[14680064]{0:T(1024)(128)(4,1)} %bitcast.4), calls=%async_computation.2 | async-start | bytes 8388608
  28.1 6.9 %slice-start.3 = ((s8[14680064]{0:T(1024)(128)(4,1)}), s8[2097152]{0:T(1024)(128)(4,1)S(1)}, s32[]{:S(2)}) async-start(s8[14680064]{0:T(1024)(128)(4,1)} %bitcast.4), calls=%async_computation.3 | async-start | bytes 4194304
  28.1 12.2 %slice-start.4 = ((s8[14680064]{0:T(1024)(128)(4,1)}), s8[4194304]{0:T(1024)(128)(4,1)S(1)}, s32[]{:S(2)}) async-start(s8[14680064]{0:T(1024)(128)(4,1)} %bitcast.6), calls=%async_computation.4 | async-start | bytes 8388608
  28.1 12.2 %slice-start.5 = ((s8[14680064]{0:T(1024)(128)(4,1)}), s8[4194304]{0:T(1024)(128)(4,1)S(1)}, s32[]{:S(2)}) async-start(s8[14680064]{0:T(1024)(128)(4,1)} %bitcast.6), calls=%async_computation.5 | async-start | bytes 8388608
  28.1 12.2 %slice-start.6 = ((s8[14680064]{0:T(1024)(128)(4,1)}), s8[4194304]{0:T(1024)(128)(4,1)S(1)}, s32[]{:S(2)}) async-start(s8[14680064]{0:T(1024)(128)(4,1)} %bitcast.6), calls=%async_computation.6 | async-start | bytes 8388608
  29.8 10.4 %slice-start.7 = ((s8[14680064]{0:T(1024)(128)(4,1)}), s8[2097152]{0:T(1024)(128)(4,1)S(1)}, s32[]{:S(2)}) async-start(s8[14680064]{0:T(1024)(128)(4,1)} %bitcast.6), calls=%async_computation.7 | async-start | bytes 4194304
  29.8 3.5 %collective-permute-start.9 = (bf16[64,256]{1,0:T(8,128)(2,1)S(1)}, bf16[64,256]{1,0:T(8,128)(2,1)S(1)}, u32[]{:S(2)}, u32[]{:S(2)}) collective-permute-start(bf16[64,256]{1,0:T(8,128)(2,1)S(1)} %attend.1.refs_3_), channel_id=1, source_target_pairs={{0,3},{1,2},{2,1},{3,0},{4,7},{5,6},{6,5},{7,4},{8,11},{9,10},{10,... | collective-permute-start | bytes 98312 | tf_op jit(solution)/shard_map/ppermute | solution.py:30
  31.1 3.9 %collective-permute-start.10 = (bf16[64,256]{1,0:T(8,128)(2,1)S(1)}, bf16[64,256]{1,0:T(8,128)(2,1)S(1)}, u32[]{:S(2)}, u32[]{:S(2)}) collective-permute-start(bf16[64,256]{1,0:T(8,128)(2,1)S(1)} %attend.1.refs_3_), channel_id=1, source_target_pairs={{0,2},{1,3},{2,0},{3,1},{4,6},{5,7},{6,4},{7,5},{8,10},{9,11},{10,... | collective-permute-start | bytes 98312 | tf_op jit(solution)/shard_map/ppermute | solution.py:30
  31.6 3.4 %collective-permute-start.11 = (bf16[64,256]{1,0:T(8,128)(2,1)S(1)}, bf16[64,256]{1,0:T(8,128)(2,1)S(1)}, u32[]{:S(2)}, u32[]{:S(2)}) collective-permute-start(bf16[64,256]{1,0:T(8,128)(2,1)S(1)} %attend.1.refs_3_), channel_id=1, source_target_pairs={{0,1},{1,0},{2,3},{3,2},{4,5},{5,4},{6,7},{7,6},{8,9},{9,8},{10,11... | collective-permute-start | bytes 98312 | tf_op jit(solution)/shard_map/ppermute | solution.py:30
  35.0 14.0 %slice-start.8 = ((s8[14680064]{0:T(1024)(128)(4,1)}), s8[4194304]{0:T(1024)(128)(4,1)S(1)}, s32[]{:S(2)}) async-start(s8[14680064]{0:T(1024)(128)(4,1)} %bitcast.8), calls=%async_computation.8 | async-start | bytes 8388608
  35.0 14.0 %slice-start.9 = ((s8[14680064]{0:T(1024)(128)(4,1)}), s8[4194304]{0:T(1024)(128)(4,1)S(1)}, s32[]{:S(2)}) async-start(s8[14680064]{0:T(1024)(128)(4,1)} %bitcast.8), calls=%async_computation.9 | async-start | bytes 8388608
  35.3 4.9 %collective-permute-start.12 = (bf16[2,1024]{1,0:T(2,128)(2,1)S(1)}, bf16[2,1024]{1,0:T(2,128)(2,1)S(1)}, u32[]{:S(2)}, u32[]{:S(2)}) collective-permute-start(bf16[2,1024]{1,0:T(2,128)(2,1)S(1)} %get-tuple-element.66), channel_id=1, source_target_pairs={{0,13},{1,12},{2,15},{3,14},{4,9},{5,8},{6,11},{7,10},{8,5},{9,4},... | collective-permute-start | bytes 12296 | tf_op jit(solution)/shard_map/ppermute | solution.py:49
  36.2 4.0 %collective-permute-start.13 = (bf16[2,1024]{1,0:T(2,128)(2,1)S(1)}, bf16[2,1024]{1,0:T(2,128)(2,1)S(1)}, u32[]{:S(2)}, u32[]{:S(2)}) collective-permute-start(bf16[2,1024]{1,0:T(2,128)(2,1)S(1)} %get-tuple-element.67), channel_id=1, source_target_pairs={{0,9},{1,8},{2,11},{3,10},{4,13},{5,12},{6,15},{7,14},{8,1},{9,0},... | collective-permute-start | bytes 12296 | tf_op jit(solution)/shard_map/ppermute | solution.py:49
  36.8 3.4 %collective-permute-start.14 = (bf16[2,1024]{1,0:T(2,128)(2,1)S(1)}, bf16[2,1024]{1,0:T(2,128)(2,1)S(1)}, u32[]{:S(2)}, u32[]{:S(2)}) collective-permute-start(bf16[2,1024]{1,0:T(2,128)(2,1)S(1)} %get-tuple-element.68), channel_id=1, source_target_pairs={{0,5},{1,4},{2,7},{3,6},{4,1},{5,0},{6,3},{7,2},{8,13},{9,12},{10,... | collective-permute-start | bytes 12296 | tf_op jit(solution)/shard_map/ppermute | solution.py:49
  40.3 8.8 %slice-start.10 = ((s8[14680064]{0:T(1024)(128)(4,1)}), s8[4194304]{0:T(1024)(128)(4,1)S(1)}, s32[]{:S(2)}) async-start(s8[14680064]{0:T(1024)(128)(4,1)} %bitcast.8), calls=%async_computation.10 | async-start | bytes 8388608
  40.3 8.7 %slice-start.11 = ((s8[14680064]{0:T(1024)(128)(4,1)}), s8[2097152]{0:T(1024)(128)(4,1)S(1)}, s32[]{:S(2)}) async-start(s8[14680064]{0:T(1024)(128)(4,1)} %bitcast.8), calls=%async_computation.11 | async-start | bytes 4194304
  41.2 5.8 %collective-permute-start.15 = (bf16[8,2048]{1,0:T(8,128)(2,1)S(1)}, bf16[8,2048]{1,0:T(8,128)(2,1)S(1)}, u32[]{:S(2)}, u32[]{:S(2)}) collective-permute-start(bf16[8,2048]{1,0:T(8,128)(2,1)S(1)} %get-tuple-element.70), channel_id=1, source_target_pairs={{0,12},{1,13},{2,14},{3,15},{4,8},{5,9},{6,10},{7,11},{8,4},{9,5},... | collective-permute-start | bytes 98312 | tf_op jit(solution)/shard_map/ppermute | solution.py:49
  43.7 5.0 %collective-permute-start.16 = (bf16[8,2048]{1,0:T(8,128)(2,1)S(1)}, bf16[8,2048]{1,0:T(8,128)(2,1)S(1)}, u32[]{:S(2)}, u32[]{:S(2)}) collective-permute-start(bf16[8,2048]{1,0:T(8,128)(2,1)S(1)} %get-tuple-element.71), channel_id=1, source_target_pairs={{0,8},{1,9},{2,10},{3,11},{4,12},{5,13},{6,14},{7,15},{8,0},{9,1},... | collective-permute-start | bytes 98312 | tf_op jit(solution)/shard_map/ppermute | solution.py:49
  45.0 4.0 %collective-permute-start.17 = (bf16[8,2048]{1,0:T(8,128)(2,1)S(1)}, bf16[8,2048]{1,0:T(8,128)(2,1)S(1)}, u32[]{:S(2)}, u32[]{:S(2)}) collective-permute-start(bf16[8,2048]{1,0:T(8,128)(2,1)S(1)} %get-tuple-element.72), channel_id=1, source_target_pairs={{0,4},{1,5},{2,6},{3,7},{4,0},{5,1},{6,2},{7,3},{8,12},{9,13},{10,... | collective-permute-start | bytes 98312 | tf_op jit(solution)/shard_map/ppermute | solution.py:49
  51.0 2.5 %collective-permute-start.20 = (bf16[8,3712]{1,0:T(8,128)(2,1)S(1)}, bf16[8,3712]{1,0:T(8,128)(2,1)S(1)}, u32[]{:S(2)}, u32[]{:S(2)}) collective-permute-start(bf16[8,3712]{1,0:T(8,128)(2,1)S(1)} %get-tuple-element.76.first_ref), channel_id=1, source_target_pairs={{0,1},{1,0},{2,3},{3,2},{4,5},{5,4},{6,7},{7,6},{8,9},{9,8},{10,11... | collective-permute-start | bytes 178184 | tf_op jit(solution)/shard_map/ppermute | solution.py:30
  53.1 1.7 %collective-permute-start.18 = (bf16[8,3584]{1,0:T(8,128)(2,1)S(1)}, bf16[8,3584]{1,0:T(8,128)(2,1)S(1)}, u32[]{:S(2)}, u32[]{:S(2)}) collective-permute-start(bf16[8,3584]{1,0:T(8,128)(2,1)S(1)} %second_gate_up.1.first_ref), channel_id=1, source_target_pairs={{0,1},{1,0},{2,3},{3,2},{4,5},{5,4},{6,7},{7,6},{8,9},{9,8},{10,11... | collective-permute-start | bytes 172040 | tf_op jit(solution)/shard_map/ppermute | solution.py:30
  53.6 4.6 %collective-permute-start.21 = (bf16[8,3712]{1,0:T(8,128)(2,1)S(1)}, bf16[8,3712]{1,0:T(8,128)(2,1)S(1)}, u32[]{:S(2)}, u32[]{:S(2)}) collective-permute-start(bf16[8,3712]{1,0:T(8,128)(2,1)S(1)} %pair_sum.3.near_ref), channel_id=1, source_target_pairs={{0,2},{1,3},{2,0},{3,1},{4,6},{5,7},{6,4},{7,5},{8,10},{9,11},{10,... | collective-permute-start | bytes 178184 | tf_op jit(solution)/shard_map/ppermute | solution.py:30
  54.8 4.8 %collective-permute-start.19 = (bf16[8,3584]{1,0:T(8,128)(2,1)S(1)}, bf16[8,3584]{1,0:T(8,128)(2,1)S(1)}, u32[]{:S(2)}, u32[]{:S(2)}) collective-permute-start(bf16[8,3584]{1,0:T(8,128)(2,1)S(1)} %pair_sum.2.near_ref), channel_id=1, source_target_pairs={{0,2},{1,3},{2,0},{3,1},{4,6},{5,7},{6,4},{7,5},{8,10},{9,11},{10,... | collective-permute-start | bytes 172040 | tf_op jit(solution)/shard_map/ppermute | solution.py:30
  60.9 5.5 %collective-permute-start.22 = (bf16[2,2048]{1,0:T(2,128)(2,1)S(1)}, bf16[2,2048]{1,0:T(2,128)(2,1)S(1)}, u32[]{:S(2)}, u32[]{:S(2)}) collective-permute-start(bf16[2,2048]{1,0:T(2,128)(2,1)S(1)} %get-tuple-element.79), channel_id=1, source_target_pairs={{0,12},{1,13},{2,14},{3,15},{4,8},{5,9},{6,10},{7,11},{8,4},{9,5},... | collective-permute-start | bytes 24584 | tf_op jit(solution)/shard_map/ppermute | solution.py:49
  63.4 4.5 %collective-permute-start.23 = (bf16[2,2048]{1,0:T(2,128)(2,1)S(1)}, bf16[2,2048]{1,0:T(2,128)(2,1)S(1)}, u32[]{:S(2)}, u32[]{:S(2)}) collective-permute-start(bf16[2,2048]{1,0:T(2,128)(2,1)S(1)} %get-tuple-element.80), channel_id=1, source_target_pairs={{0,8},{1,9},{2,10},{3,11},{4,12},{5,13},{6,14},{7,15},{8,0},{9,1},... | collective-permute-start | bytes 24584 | tf_op jit(solution)/shard_map/ppermute | solution.py:49
  63.4 4.5 %collective-permute-start.24 = (bf16[2,2048]{1,0:T(2,128)(2,1)S(1)}, bf16[2,2048]{1,0:T(2,128)(2,1)S(1)}, u32[]{:S(2)}, u32[]{:S(2)}) collective-permute-start(bf16[2,2048]{1,0:T(2,128)(2,1)S(1)} %get-tuple-element.81), channel_id=1, source_target_pairs={{0,4},{1,5},{2,6},{3,7},{4,0},{5,1},{6,2},{7,3},{8,12},{9,13},{10,... | collective-permute-start | bytes 24584 | tf_op jit(solution)/shard_map/ppermute | solution.py:49

commit v11 on v10

--- a/solution.py
+++ b/solution.py
@@ -515,62 +515,41 @@
     return (gate / (1.0 + jnp.exp(-gate)) * total(count)).astype(jnp.bfloat16)
 
 
-def first_down_kernel(count, near_ref, far_ref, weight_ref, out_ref, scale_ref):
+def down_kernel(one_near, one_far, two_near, two_far, weight_ref, *refs):
+    hidden_s, out_s = refs[-2:]
+    first = (one_near.shape[1] - LANES) // 2
+    second = two_near.shape[1] // 2
     squares = jnp.sum(
-        near_ref[:, 2 * count :].astype(jnp.float32) + far_ref[:, 2 * count :].astype(jnp.float32),
+        one_near[:, 2 * first :].astype(jnp.float32) + one_far[:, 2 * first :].astype(jnp.float32),
         axis=1,
         keepdims=True,
     )
     scale = lax.rsqrt(squares / D + epsilon)
-    scale_ref[...] = jnp.broadcast_to(scale, scale_ref.shape)
+    hidden_s[:, :first] = hidden_of(one_near, one_far, scale, first)
+    hidden_s[:, first:] = hidden_of(two_near, two_far, scale, second)
 
     def store(start, size, value):
-        out_ref[:, pl.ds(start, size)] = value
-
-    product_tiles(hidden_of(near_ref, far_ref, scale, count), weight_ref.at[:count], store)
-
-
-def first_down(near, far, weight, count):
-    rows = near.shape[0]
-    return pl.pallas_call(
-        functools.partial(first_down_kernel, count),
-        out_shape=(
-            jax.ShapeDtypeStruct((rows, weight.shape[1]), jnp.float32),
-            jax.ShapeDtypeStruct((rows, LANES), jnp.float32),
-        ),
-        in_specs=[in_vmem] * 3,
-        out_specs=(in_vmem,) * 2,
-        compiler_params=params(3),
-        cost_estimate=product_cost(count, weight.shape[1]),
-        name="first_down",
-    )(near, far, resident(weight))
-
-
-def second_down_kernel(count, near_ref, far_ref, weight_ref, part_ref, scale_ref, *refs):
-    out_s = refs[-1]
-    first = weight_ref.shape[0] - count
-
-    def store(start, size, value):
-        span = pl.ds(start, size)
-        out_s[:, span] = part_ref[:, span] + value
-
-    hidden = hidden_of(near_ref, far_ref, scale_ref[:, 0:1], count)
-    product_tiles(hidden, weight_ref.at[first:], store)
-    part_rows(out_s, refs[:-1])
-
-
-def second_down(near, far, weight, part, scale, slots):
-    rows, columns = part.shape
-    count = near.shape[1] // 2
-    return pl.pallas_call(
-        functools.partial(second_down_kernel, count),
+        out_s[:, pl.ds(start, size)] = value
+
+    product_tiles(hidden_s[...], weight_ref, store)
+    part_rows(out_s, refs[:-2])
+
+
+def project_down(one, two, weight, slots):
+    rows = one[0].shape[0]
+    depth, columns = weight.shape
+    return pl.pallas_call(
+        down_kernel,
         out_shape=(jax.ShapeDtypeStruct((rows // slots, columns), jnp.bfloat16),) * slots,
         in_specs=[in_vmem] * 5,
         out_specs=(in_vmem,) * slots,
-        scratch_shapes=[pltpu.VMEM(part.shape, jnp.float32)],
+        scratch_shapes=[
+            pltpu.VMEM((rows, depth), jnp.bfloat16),
+            pltpu.VMEM((rows, columns), jnp.float32),
+        ],
         compiler_params=params(3),
-        name="second_down",
-    )(near, far, resident(weight), part, scale)
+        name="project_down",
+    )(*one, *two, resident(weight))
 
 
 def finish_kernel(updated_ref, *refs):
@@ -636,10 +615,10 @@
     joined, keys, values = lax.optimization_barrier((joined, keys, values))
     (w_out,) = load(w_out, after=joined)
     parts, w_out = lax.optimization_barrier((exchange(joined, "inner")[::-1], w_out))
-    shard = attend(my_lengths, cosine, sine, parts, keys, values, [w_gate], slots)
-
-    pieces = combine(exchange(shard, "inner"), [w_up], all_rows, slots)
-    parts = scatter_slots(project_out(scatter_slots(pieces, 1), w_out, [w_down]), 0)
+    shard = attend(my_lengths, cosine, sine, parts, keys, values, [], slots)
+
+    pieces = combine(exchange(shard, "inner"), [w_gate], all_rows, slots)
+    parts = scatter_slots(project_out(scatter_slots(pieces, 1), w_out, [w_up]), 0)
 
     tiles = w_gate.shape[1] // LANES
     first = (tiles + 1) // 2 * LANES
@@ -651,8 +630,9 @@
     for step in steps[:-1]:
         one = pair_sum(one, swap_with(one, "inner", step))
         two = pair_sum(two, swap_with(two, "inner", step))
-    part, scale = first_down(one, swap_with(one, "inner", steps[-1]), w_down, first)
-    pieces = second_down(two, swap_with(two, "inner", steps[-1]), w_down, part, scale, slots)
+    one = (one, swap_with(one, "inner", steps[-1]))
+    two = (two, swap_with(two, "inner", steps[-1]))
+    pieces = project_down(one, two, w_down, slots)
     parts = scatter_slots(pieces, 0)
     return finish(updated, parts)
 

time: 68.7 us -> 63.8 us (0.929)
  local copies, waits for them, and re-layouts: 5.8 us -> 0.11 us
  waiting for transfers between devices: 16 us -> 17.2 us
    unnamed x28 -> x14, local copies, waits for them, and re-layouts: 5.73 us -> 0.04 us
    ppermute x13, waiting for transfers between devices: 7.87 us -> 9.04 us  [swap_with(): return lax.ppermute(value, axis, [(i, i ^ step) for i in range(count)])]
    pallas_call x2 -> x1, Pallas kernels: 2.6 us -> 2.28 us  [project_down(): pl.pallas_call(down_kernel, out_shape=(jax.ShapeDtypeStruct((rows // slot...]
  transfers between devices with their start and end apart: 25 -> 25, of which waited for: 11 -> 11; matrix products, arithmetic and copies ran while one was open for 0% -> 0% of each run, Pallas kernels for 16% -> 15%
where the time goes in v11:
time: 63.8 us; the launch traced here: 63.7 us
  starting transfers between devices  27.9 us (44%)
  Pallas kernels  18.1 us (28%)
  waiting for transfers between devices  17.2 us (27%)
    ppermute x12, starting transfers between devices, scatter_slots(): got.append(lax.ppermute(pieces[k], ('tensor', 'inner'), pairs))  14.5 us
    ppermute x13, starting transfers between devices, swap_with(): return lax.ppermute(value, axis, [(i, i ^ step) for i in range(count)])  13.4 us
    ppermute x13, waiting for transfers between devices, swap_with(): return lax.ppermute(value, axis, [(i, i ^ step) for i in range(count)])  9.04 us
    ppermute x12, waiting for transfers between devices, scatter_slots(): got.append(lax.ppermute(pieces[k], ('tensor', 'inner'), pairs))  8.12 us
    pallas_call x3, Pallas kernels, load(): pl.pallas_call(functools.partial(load_kernel, spans), out_shape=tuple((pl...  7.38 us
    pallas_call x1, Pallas kernels, project_down(): pl.pallas_call(down_kernel, out_shape=(jax.ShapeDtypeStruct((rows // slot...  2.28 us
    pallas_call x1, Pallas kernels, second_gate_up(): pl.pallas_call(functools.partial(second_gate_up_kernel, first, count), ou...  2 us
    pallas_call x1, Pallas kernels, first_gate_up(): pl.pallas_call(functools.partial(first_gate_up_kernel, slots, count), out...  2 us
  transfers between devices with their start and end apart: 25, of which 11 were waited for; matrix products, arithmetic and copies ran while one was open for 0% of the time, Pallas kernels for 15%

profile of v11, /device:TPU:0, one launch (start us, length us, event | category | flops | bytes accessed | tf_op | source)
XLA Modules:
  0.0 63.7 jit_solution(15040056032293654040)
XLA Ops:
  0.0 5.0 %collective-permute-start = (bf16[2,2048]{1,0:T(2,128)(2,1)}, bf16[2,2048]{1,0:T(2,128)(2,1)S(1)}, u32[]{:S(2)}, u32[]{:S(2)}) collective-permute-start(bf16[2,2048]{1,0:T(2,128)(2,1)} %refs_5_.1), channel_id=1, source_target_pairs={{0,12},{4,8},{8,4},{12,0},{1,13},{5,9},{9,5},{13,1},{2,14},{6,10},... | collective-permute-start | bytes 24584 | tf_op jit(solution)/shard_map/ppermute | solution.py:30
  5.0 0.0 collective-permute-start.1
  5.1 0.6 collective-permute-start.2
  5.6 2.7 %load.3 = (bf16[2,2048]{1,0:T(2,128)(2,1)S(1)}, bf16[2048]{0:T(1024)(128)(2,1)S(1)}, bf16[2048]{0:T(1024)(128)(2,1)S(1)}, bf16[2048,256]{1,0:T(8,128)(2,1)S(1)}, bf16[2048,1024]{1,0:T(8,128)(2,1)S(1)}) custom-call(bf16[2,2048]{1,0:T(2,128)(2,1)} %refs_5_.1, bf16[2048]{0:T(1024)(128)(2,1)} %refs_1_.1, bf16[2048]{0:T(1024)(128)(2,1)} %refs_2_.1, ...), custom_call_target="tpu_custom_call" | custom-call | bytes 5259264 | tf_op jit(solution)/shard_map/load/pallas_call | solution.py:144
  8.4 0.0 collective-permute-done.refs_0_
  8.4 1.4 %collective-permute-done.1.refs_1_ = bf16[2,2048]{1,0:T(2,128)(2,1)S(1)} collective-permute-done((bf16[2,2048]{1,0:T(2,128)(2,1)}, bf16[2,2048]{1,0:T(2,128)(2,1)S(1)}, u32[]{:S(2)}, u32[]{:S(2)}) %collective-permute-start.1) | collective-permute-done | bytes 8224 | tf_op jit(solution)/shard_map/ppermute | solution.py:30
  9.8 0.0 collective-permute-done.2.refs_2_
  9.8 0.8 %project_qkv.1 = (f32[8,2048]{1,0:T(8,128)S(1)}, bf16[2,1408]{1,0:T(2,128)(2,1)S(1)}, bf16[2,1408]{1,0:T(2,128)(2,1)S(1)}, bf16[2,1408]{1,0:T(2,128)(2,1)S(1)}, bf16[2,1408]{1,0:T(2,128)(2,1)S(1)}) custom-call(bf16[2048]{0:T(1024)(128)(2,1)S(1)} %get-tuple-element.42.gain_ref, bf16[2048,1024]{1,0:T(8,128)(2,1)S(1)} %get-tuple-element.43.wq_ref, ...), custom_call_target="tpu_custom_call" | custom-call | tf_op jit(solution)/shard_map/project_qkv/pallas_call | solution.py:197
  10.6 1.1 %collective-permute-start.3 = (bf16[2,1408]{1,0:T(2,128)(2,1)S(1)}, bf16[2,1408]{1,0:T(2,128)(2,1)S(1)}, u32[]{:S(2)}, u32[]{:S(2)}) collective-permute-start(bf16[2,1408]{1,0:T(2,128)(2,1)S(1)} %get-tuple-element.49), channel_id=1, source_target_pairs={{0,13},{1,12},{2,15},{3,14},{4,9},{5,8},{6,11},{7,10},{8,5},{9,4},... | collective-permute-start | bytes 16904 | tf_op jit(solution)/shard_map/ppermute | solution.py:49
  11.7 0.2 collective-permute-start.4
  11.9 1.5 %collective-permute-start.5 = (bf16[2,1408]{1,0:T(2,128)(2,1)S(1)}, bf16[2,1408]{1,0:T(2,128)(2,1)S(1)}, u32[]{:S(2)}, u32[]{:S(2)}) collective-permute-start(bf16[2,1408]{1,0:T(2,128)(2,1)S(1)} %get-tuple-element.51), channel_id=1, source_target_pairs={{0,5},{1,4},{2,7},{3,6},{4,1},{5,0},{6,3},{7,2},{8,13},{9,12},{10,... | collective-permute-start | bytes 16904 | tf_op jit(solution)/shard_map/ppermute | solution.py:49
  13.5 0.1 fusion.4
  13.6 2.4 %load.4 = (bf16[2,4096,128]{2,1,0:T(8,128)(2,1)S(1)}, bf16[2,4096,128]{2,1,0:T(8,128)(2,1)S(1)}) custom-call(bf16[2,4096,128]{2,1,0:T(8,128)(2,1)} %bitcast.8, bf16[2,4096,128]{2,1,0:T(8,128)(2,1)} %bitcast.9, f32[8,2048]{1,0:T(8,128)S(1)} %get-tuple-element.47.refs_2_.rows_ref), custom_call_target="tpu_custom_call" | custom-call | bytes 4194304 | tf_op jit(solution)/shard_map/load/pallas_call | solution.py:144
  16.0 0.0 collective-permute-done.3.refs_0_
  16.0 0.0 collective-permute-done.4.refs_1_
  16.1 2.6 %collective-permute-start.6 = (bf16[8,1408]{1,0:T(8,128)(2,1)S(1)}, bf16[8,1408]{1,0:T(8,128)(2,1)S(1)}, u32[]{:S(2)}, u32[]{:S(2)}) collective-permute-start(bf16[8,1408]{1,0:T(8,128)(2,1)S(1)} %stack.1.refs_1_.refs_0_), channel_id=1, source_target_pairs={{0,3},{1,2},{2,1},{3,0},{4,7},{5,6},{6,5},{7,4},{8,11},{9,10},{10,... | collective-permute-start | bytes 67592 | tf_op jit(solution)/shard_map/ppermute | solution.py:30
  18.7 0.5 collective-permute-start.7
  19.2 0.0 collective-permute-start.8
  19.2 0.1 fusion
  19.3 2.2 %load.5.weight_ref = bf16[1024,2048]{1,0:T(8,128)(2,1)S(1)} custom-call(bf16[1024,2048]{1,0:T(8,128)(2,1)} %refs_0_.3, bf16[8,1408]{1,0:T(8,128)(2,1)S(1)} %stack.1.refs_1_.refs_0_), custom_call_target="tpu_custom_call" | custom-call | bytes 4194304 | tf_op jit(solution)/shard_map/load/pallas_call | solution.py:144
  21.6 0.9 %collective-permute-done.7.refs_2_ = bf16[8,1408]{1,0:T(8,128)(2,1)S(1)} collective-permute-done((bf16[8,1408]{1,0:T(8,128)(2,1)S(1)}, bf16[8,1408]{1,0:T(8,128)(2,1)S(1)}, u32[]{:S(2)}, u32[]{:S(2)}) %collective-permute-start.7) | collective-permute-done | bytes 22560 | tf_op jit(solution)/shard_map/ppermute | solution.py:30
  22.5 0.0 collective-permute-done.8.refs_1_
  22.5 0.1 broadcast_in_dim.10.lengths_ref
  22.6 1.7 %attend.1.refs_3_ = bf16[64,256]{1,0:T(8,128)(2,1)S(1)} custom-call(s32[2,128]{1,0:T(2,128)S(1)} %broadcast_in_dim.10.lengths_ref, f32[8,128]{1,0:T(8,128)S(1)} %bitcast.6, f32[8,128]{1,0:T(8,128)S(1)} %bitcast.7, bf16[2,4096,128]{2,1,0:T(8,128)(2,1)S(1)} %get-tuple-element.58.key_ref, bf16[2,4096,128]{2,1,0:T(8,128)(2,1)S(1)} %get-tuple-element.59.value_ref, ...), custom_call_target="tpu_custom_call" | custom-call | tf_op jit(solution)/shard_map/attend/pallas_call | solution.py:331
  24.3 0.0 copy-start.1
  24.3 1.4 %collective-permute-start.9 = (bf16[64,256]{1,0:T(8,128)(2,1)S(1)}, bf16[64,256]{1,0:T(8,128)(2,1)S(1)}, u32[]{:S(2)}, u32[]{:S(2)}) collective-permute-start(bf16[64,256]{1,0:T(8,128)(2,1)S(1)} %attend.1.refs_3_), channel_id=1, source_target_pairs={{0,3},{1,2},{2,1},{3,0},{4,7},{5,6},{6,5},{7,4},{8,11},{9,10},{10,... | collective-permute-start | bytes 98312 | tf_op jit(solution)/shard_map/ppermute | solution.py:30
  25.7 0.5 collective-permute-start.10
  26.2 0.0 collective-permute-start.11
  26.3 1.5 %collective-permute-done.9.refs_0_ = bf16[64,256]{1,0:T(8,128)(2,1)S(1)} collective-permute-done((bf16[64,256]{1,0:T(8,128)(2,1)S(1)}, bf16[64,256]{1,0:T(8,128)(2,1)S(1)}, u32[]{:S(2)}, u32[]{:S(2)}) %collective-permute-start.9) | collective-permute-done | bytes 32800 | tf_op jit(solution)/shard_map/ppermute | solution.py:30
  27.7 1.9 %collective-permute-done.10.refs_1_ = bf16[64,256]{1,0:T(8,128)(2,1)S(1)} collective-permute-done((bf16[64,256]{1,0:T(8,128)(2,1)S(1)}, bf16[64,256]{1,0:T(8,128)(2,1)S(1)}, u32[]{:S(2)}, u32[]{:S(2)}) %collective-permute-start.10) | collective-permute-done | bytes 32800 | tf_op jit(solution)/shard_map/ppermute | solution.py:30
  29.6 0.0 collective-permute-done.11.refs_2_
  29.6 0.3 combine.1
  29.9 0.7 %collective-permute-start.12 = (bf16[2,1024]{1,0:T(2,128)(2,1)S(1)}, bf16[2,1024]{1,0:T(2,128)(2,1)S(1)}, u32[]{:S(2)}, u32[]{:S(2)}) collective-permute-start(bf16[2,1024]{1,0:T(2,128)(2,1)S(1)} %get-tuple-element.64), channel_id=1, source_target_pairs={{0,13},{1,12},{2,15},{3,14},{4,9},{5,8},{6,11},{7,10},{8,5},{9,4},... | collective-permute-start | bytes 12296 | tf_op jit(solution)/shard_map/ppermute | solution.py:49
  30.6 0.3 collective-permute-start.13
  30.9 1.8 %collective-permute-start.14 = (bf16[2,1024]{1,0:T(2,128)(2,1)S(1)}, bf16[2,1024]{1,0:T(2,128)(2,1)S(1)}, u32[]{:S(2)}, u32[]{:S(2)}) collective-permute-start(bf16[2,1024]{1,0:T(2,128)(2,1)S(1)} %get-tuple-element.66), channel_id=1, source_target_pairs={{0,5},{1,4},{2,7},{3,6},{4,1},{5,0},{6,3},{7,2},{8,13},{9,12},{10,... | collective-permute-start | bytes 12296 | tf_op jit(solution)/shard_map/ppermute | solution.py:49
  32.7 2.1 %collective-permute-done.12.refs_0_ = bf16[2,1024]{1,0:T(2,128)(2,1)S(1)} collective-permute-done((bf16[2,1024]{1,0:T(2,128)(2,1)S(1)}, bf16[2,1024]{1,0:T(2,128)(2,1)S(1)}, u32[]{:S(2)}, u32[]{:S(2)}) %collective-permute-start.12) | collective-permute-done | bytes 4128 | tf_op jit(solution)/shard_map/ppermute | solution.py:49
  34.8 0.0 collective-permute-done.13.refs_1_
  34.8 0.0 collective-permute-done.14.refs_2_
  34.8 1.0 %project_out.1 = (bf16[8,2048]{1,0:T(8,128)(2,1)S(1)}, bf16[8,2048]{1,0:T(8,128)(2,1)S(1)}, bf16[8,2048]{1,0:T(8,128)(2,1)S(1)}, bf16[8,2048]{1,0:T(8,128)(2,1)S(1)}) custom-call(bf16[1024,2048]{1,0:T(8,128)(2,1)S(1)} %load.5.weight_ref, bf16[2,1024]{1,0:T(2,128)(2,1)S(1)} %collective-permute-done.12.refs_0_, ...), custom_call_target="tpu_custom_call" | custom-call | tf_op jit(solution)/shard_map/project_out/pallas_call | solution.py:420
  35.7 2.4 %collective-permute-start.15 = (bf16[8,2048]{1,0:T(8,128)(2,1)S(1)}, bf16[8,2048]{1,0:T(8,128)(2,1)S(1)}, u32[]{:S(2)}, u32[]{:S(2)}) collective-permute-start(bf16[8,2048]{1,0:T(8,128)(2,1)S(1)} %get-tuple-element.68), channel_id=1, source_target_pairs={{0,12},{1,13},{2,14},{3,15},{4,8},{5,9},{6,10},{7,11},{8,4},{9,5},... | collective-permute-start | bytes 98312 | tf_op jit(solution)/shard_map/ppermute | solution.py:49
  38.2 1.4 %collective-permute-start.16 = (bf16[8,2048]{1,0:T(8,128)(2,1)S(1)}, bf16[8,2048]{1,0:T(8,128)(2,1)S(1)}, u32[]{:S(2)}, u32[]{:S(2)}) collective-permute-start(bf16[8,2048]{1,0:T(8,128)(2,1)S(1)} %get-tuple-element.69), channel_id=1, source_target_pairs={{0,8},{1,9},{2,10},{3,11},{4,12},{5,13},{6,14},{7,15},{8,0},{9,1},... | collective-permute-start | bytes 98312 | tf_op jit(solution)/shard_map/ppermute | solution.py:49
  39.5 0.6 collective-permute-start.17
  40.1 1.4 %collective-permute-done.15.refs_0_ = bf16[8,2048]{1,0:T(8,128)(2,1)S(1)} collective-permute-done((bf16[8,2048]{1,0:T(8,128)(2,1)S(1)}, bf16[8,2048]{1,0:T(8,128)(2,1)S(1)}, u32[]{:S(2)}, u32[]{:S(2)}) %collective-permute-start.15) | collective-permute-done | bytes 32800 | tf_op jit(solution)/shard_map/ppermute | solution.py:49
  41.6 1.6 %collective-permute-done.16.refs_1_ = bf16[8,2048]{1,0:T(8,128)(2,1)S(1)} collective-permute-done((bf16[8,2048]{1,0:T(8,128)(2,1)S(1)}, bf16[8,2048]{1,0:T(8,128)(2,1)S(1)}, u32[]{:S(2)}, u32[]{:S(2)}) %collective-permute-start.16) | collective-permute-done | bytes 32800 | tf_op jit(solution)/shard_map/ppermute | solution.py:49
  43.2 0.3 collective-permute-done.17.refs_2_
  43.5 2.0 %first_gate_up.1 = (bf16[8,3712]{1,0:T(8,128)(2,1)S(1)}, f32[2,2048]{1,0:T(2,128)S(1)}, bf16[8,2048]{1,0:T(8,128)(2,1)S(1)}) custom-call(f32[8,2048]{1,0:T(8,128)S(1)} %get-tuple-element.47.refs_2_.rows_ref, bf16[2048]{0:T(1024)(128)(2,1)S(1)} %get-tuple-element.48.gain_ref, bf16[2048,3584]{1,0:T(8,128)(2,1)S(1)} %copy-done, ...), custom_call_target="tpu_custom_call" | custom-call | flops 117440512 | bytes 14680064 | tf_op jit(solution)/shard_map/first_gate_up/pallas_call | solution.py:476
  45.5 0.0 collective-permute-start.18
  45.5 0.0 slice-start.1
  45.5 0.0 slice-start.2
  45.6 2.0 %second_gate_up.1.first_ref = bf16[8,3584]{1,0:T(8,128)(2,1)S(1)} custom-call(bf16[8,2048]{1,0:T(8,128)(2,1)S(1)} %get-tuple-element.74.scaled_ref, bf16[2048,3584]{1,0:T(8,128)(2,1)S(1)} %copy-done, bf16[2048,3584]{1,0:T(8,128)(2,1)S(1)} %copy-done.1), custom_call_target="tpu_custom_call" | custom-call | flops 117440512 | bytes 14680064 | tf_op jit(solution)/shard_map/second_gate_up/pallas_call | solution.py:498
  47.6 0.5 collective-permute-start.20
  48.1 0.9 %collective-permute-start.19 = (bf16[8,3712]{1,0:T(8,128)(2,1)S(1)}, bf16[8,3712]{1,0:T(8,128)(2,1)S(1)}, u32[]{:S(2)}, u32[]{:S(2)}) collective-permute-start(bf16[8,3712]{1,0:T(8,128)(2,1)S(1)} %pair_sum.2.one_near), channel_id=1, source_target_pairs={{0,2},{1,3},{2,0},{3,1},{4,6},{5,7},{6,4},{7,5},{8,10},{9,11},{10,... | collective-permute-start | bytes 178184 | tf_op jit(solution)/shard_map/ppermute | solution.py:30
  49.0 0.0 collective-permute-done.20.second_ref
  49.0 1.2 %collective-permute-start.21 = (bf16[8,3584]{1,0:T(8,128)(2,1)S(1)}, bf16[8,3584]{1,0:T(8,128)(2,1)S(1)}, u32[]{:S(2)}, u32[]{:S(2)}) collective-permute-start(bf16[8,3584]{1,0:T(8,128)(2,1)S(1)} %pair_sum.3.two_near), channel_id=1, source_target_pairs={{0,2},{1,3},{2,0},{3,1},{4,6},{5,7},{6,4},{7,5},{8,10},{9,11},{10,... | collective-permute-start | bytes 172040 | tf_op jit(solution)/shard_map/ppermute | solution.py:30
  50.3 3.3 %collective-permute-done.21.two_far = bf16[8,3584]{1,0:T(8,128)(2,1)S(1)} collective-permute-done((bf16[8,3584]{1,0:T(8,128)(2,1)S(1)}, bf16[8,3584]{1,0:T(8,128)(2,1)S(1)}, u32[]{:S(2)}, u32[]{:S(2)}) %collective-permute-start.21) | collective-permute-done | bytes 57376 | tf_op jit(solution)/shard_map/ppermute | solution.py:30
  53.6 0.0 collective-permute-done.19.one_far
  53.6 2.3 %project_down.1 = (bf16[2,2048]{1,0:T(2,128)(2,1)S(1)}, bf16[2,2048]{1,0:T(2,128)(2,1)S(1)}, bf16[2,2048]{1,0:T(2,128)(2,1)S(1)}, bf16[2,2048]{1,0:T(2,128)(2,1)S(1)}) custom-call(bf16[8,3712]{1,0:T(8,128)(2,1)S(1)} %pair_sum.2.one_near, bf16[8,3712]{1,0:T(8,128)(2,1)S(1)} %collective-permute-done.19.one_far, bf16[8,3584]{1,0:T(8,128)(2,1)S(1)} %pair_sum.3.two_near, ...), custom_call_target="tpu_custom_call" | custom-call | tf_op jit(solution)/shard_map/project_down/pallas_call | solution.py:541
  55.9 2.6 %collective-permute-start.22 = (bf16[2,2048]{1,0:T(2,128)(2,1)S(1)}, bf16[2,2048]{1,0:T(2,128)(2,1)S(1)}, u32[]{:S(2)}, u32[]{:S(2)}) collective-permute-start(bf16[2,2048]{1,0:T(2,128)(2,1)S(1)} %get-tuple-element.75), channel_id=1, source_target_pairs={{0,12},{1,13},{2,14},{3,15},{4,8},{5,9},{6,10},{7,11},{8,4},{9,5},... | collective-permute-start | bytes 24584 | tf_op jit(solution)/shard_map/ppermute | solution.py:49
  58.5 0.0 collective-permute-start.23
  58.5 1.9 %collective-permute-start.24 = (bf16[2,2048]{1,0:T(2,128)(2,1)S(1)}, bf16[2,2048]{1,0:T(2,128)(2,1)S(1)}, u32[]{:S(2)}, u32[]{:S(2)}) collective-permute-start(bf16[2,2048]{1,0:T(2,128)(2,1)S(1)} %get-tuple-element.77), channel_id=1, source_target_pairs={{0,4},{1,5},{2,6},{3,7},{4,0},{5,1},{6,2},{7,3},{8,12},{9,13},{10,... | collective-permute-start | bytes 24584 | tf_op jit(solution)/shard_map/ppermute | solution.py:49
  60.4 1.1 %collective-permute-done.22.refs_0_ = bf16[2,2048]{1,0:T(2,128)(2,1)S(1)} collective-permute-done((bf16[2,2048]{1,0:T(2,128)(2,1)S(1)}, bf16[2,2048]{1,0:T(2,128)(2,1)S(1)}, u32[]{:S(2)}, u32[]{:S(2)}) %collective-permute-start.22) | collective-permute-done | bytes 8224 | tf_op jit(solution)/shard_map/ppermute | solution.py:49
  61.4 1.6 %collective-permute-done.23.refs_1_ = bf16[2,2048]{1,0:T(2,128)(2,1)S(1)} collective-permute-done((bf16[2,2048]{1,0:T(2,128)(2,1)S(1)}, bf16[2,2048]{1,0:T(2,128)(2,1)S(1)}, u32[]{:S(2)}, u32[]{:S(2)}) %collective-permute-start.23) | collective-permute-done | bytes 8224 | tf_op jit(solution)/shard_map/ppermute | solution.py:49
  63.0 0.0 collective-permute-done.24.refs_2_
  63.0 0.6 finish.1
  (21 shorter events, 0.1 us)
Async XLA Ops:
  0.0 8.4 %collective-permute-start = (bf16[2,2048]{1,0:T(2,128)(2,1)}, bf16[2,2048]{1,0:T(2,128)(2,1)S(1)}, u32[]{:S(2)}, u32[]{:S(2)}) collective-permute-start(bf16[2,2048]{1,0:T(2,128)(2,1)} %refs_5_.1), channel_id=1, source_target_pairs={{0,12},{4,8},{8,4},{12,0},{1,13},{5,9},{9,5},{13,1},{2,14},{6,10},... | collective-permute-start | bytes 24584 | tf_op jit(solution)/shard_map/ppermute | solution.py:30
  5.0 4.8 %collective-permute-start.1 = (bf16[2,2048]{1,0:T(2,128)(2,1)}, bf16[2,2048]{1,0:T(2,128)(2,1)S(1)}, u32[]{:S(2)}, u32[]{:S(2)}) collective-permute-start(bf16[2,2048]{1,0:T(2,128)(2,1)} %refs_5_.1), channel_id=1, source_target_pairs={{0,8},{4,12},{8,0},{12,4},{1,9},{5,13},{9,1},{13,5},{2,10},{6,14},... | collective-permute-start | bytes 24584 | tf_op jit(solution)/shard_map/ppermute | solution.py:30
  5.1 4.8 %collective-permute-start.2 = (bf16[2,2048]{1,0:T(2,128)(2,1)}, bf16[2,2048]{1,0:T(2,128)(2,1)S(1)}, u32[]{:S(2)}, u32[]{:S(2)}) collective-permute-start(bf16[2,2048]{1,0:T(2,128)(2,1)} %refs_5_.1), channel_id=1, source_target_pairs={{0,4},{4,0},{8,12},{12,8},{1,5},{5,1},{9,13},{13,9},{2,6},{6,2},{1... | collective-permute-start | bytes 24584 | tf_op jit(solution)/shard_map/ppermute | solution.py:30
  5.6 7.8 %copy-start.2 = (s32[8]{0:T(128)S(1)}, s32[8]{0:T(128)}, u32[]{:S(2)}) copy-start(s32[8]{0:T(128)} %param.23) | copy-start | bytes 100
  10.6 5.4 %collective-permute-start.3 = (bf16[2,1408]{1,0:T(2,128)(2,1)S(1)}, bf16[2,1408]{1,0:T(2,128)(2,1)S(1)}, u32[]{:S(2)}, u32[]{:S(2)}) collective-permute-start(bf16[2,1408]{1,0:T(2,128)(2,1)S(1)} %get-tuple-element.49), channel_id=1, source_target_pairs={{0,13},{1,12},{2,15},{3,14},{4,9},{5,8},{6,11},{7,10},{8,5},{9,4},... | collective-permute-start | bytes 16904 | tf_op jit(solution)/shard_map/ppermute | solution.py:49
  11.7 4.3 %collective-permute-start.4 = (bf16[2,1408]{1,0:T(2,128)(2,1)S(1)}, bf16[2,1408]{1,0:T(2,128)(2,1)S(1)}, u32[]{:S(2)}, u32[]{:S(2)}) collective-permute-start(bf16[2,1408]{1,0:T(2,128)(2,1)S(1)} %get-tuple-element.50), channel_id=1, source_target_pairs={{0,9},{1,8},{2,11},{3,10},{4,13},{5,12},{6,15},{7,14},{8,1},{9,0},... | collective-permute-start | bytes 16904 | tf_op jit(solution)/shard_map/ppermute | solution.py:49
  11.9 4.1 %collective-permute-start.5 = (bf16[2,1408]{1,0:T(2,128)(2,1)S(1)}, bf16[2,1408]{1,0:T(2,128)(2,1)S(1)}, u32[]{:S(2)}, u32[]{:S(2)}) collective-permute-start(bf16[2,1408]{1,0:T(2,128)(2,1)S(1)} %get-tuple-element.51), channel_id=1, source_target_pairs={{0,5},{1,4},{2,7},{3,6},{4,1},{5,0},{6,3},{7,2},{8,13},{9,12},{10,... | collective-permute-start | bytes 16904 | tf_op jit(solution)/shard_map/ppermute | solution.py:49
  13.6 16.1 %copy-start = (bf16[2048,3584]{1,0:T(8,128)(2,1)S(1)}, bf16[2048,3584]{1,0:T(8,128)(2,1)}, u32[]{:S(2)}) copy-start(bf16[2048,3584]{1,0:T(8,128)(2,1)} %gate_ref.3) | copy-start | bytes 44040196
  16.1 5.5 %collective-permute-start.6 = (bf16[8,1408]{1,0:T(8,128)(2,1)S(1)}, bf16[8,1408]{1,0:T(8,128)(2,1)S(1)}, u32[]{:S(2)}, u32[]{:S(2)}) collective-permute-start(bf16[8,1408]{1,0:T(8,128)(2,1)S(1)} %stack.1.refs_1_.refs_0_), channel_id=1, source_target_pairs={{0,3},{1,2},{2,1},{3,0},{4,7},{5,6},{6,5},{7,4},{8,11},{9,10},{10,... | collective-permute-start | bytes 67592 | tf_op jit(solution)/shard_map/ppermute | solution.py:30
  18.7 3.8 %collective-permute-start.7 = (bf16[8,1408]{1,0:T(8,128)(2,1)S(1)}, bf16[8,1408]{1,0:T(8,128)(2,1)S(1)}, u32[]{:S(2)}, u32[]{:S(2)}) collective-permute-start(bf16[8,1408]{1,0:T(8,128)(2,1)S(1)} %stack.1.refs_1_.refs_0_), channel_id=1, source_target_pairs={{0,2},{1,3},{2,0},{3,1},{4,6},{5,7},{6,4},{7,5},{8,10},{9,11},{10,... | collective-permute-start | bytes 67592 | tf_op jit(solution)/shard_map/ppermute | solution.py:30
  19.2 3.3 %collective-permute-start.8 = (bf16[8,1408]{1,0:T(8,128)(2,1)S(1)}, bf16[8,1408]{1,0:T(8,128)(2,1)S(1)}, u32[]{:S(2)}, u32[]{:S(2)}) collective-permute-start(bf16[8,1408]{1,0:T(8,128)(2,1)S(1)} %stack.1.refs_1_.refs_0_), channel_id=1, source_target_pairs={{0,1},{1,0},{2,3},{3,2},{4,5},{5,4},{6,7},{7,6},{8,9},{9,8},{10,11... | collective-permute-start | bytes 67592 | tf_op jit(solution)/shard_map/ppermute | solution.py:30
  24.3 10.5 %copy-start.1 = (bf16[2048,3584]{1,0:T(8,128)(2,1)S(1)}, bf16[2048,3584]{1,0:T(8,128)(2,1)}, u32[]{:S(2)}) copy-start(bf16[2048,3584]{1,0:T(8,128)(2,1)} %up_ref.3) | copy-start | bytes 44040196
  24.3 3.4 %collective-permute-start.9 = (bf16[64,256]{1,0:T(8,128)(2,1)S(1)}, bf16[64,256]{1,0:T(8,128)(2,1)S(1)}, u32[]{:S(2)}, u32[]{:S(2)}) collective-permute-start(bf16[64,256]{1,0:T(8,128)(2,1)S(1)} %attend.1.refs_3_), channel_id=1, source_target_pairs={{0,3},{1,2},{2,1},{3,0},{4,7},{5,6},{6,5},{7,4},{8,11},{9,10},{10,... | collective-permute-start | bytes 98312 | tf_op jit(solution)/shard_map/ppermute | solution.py:30
  25.7 3.9 %collective-permute-start.10 = (bf16[64,256]{1,0:T(8,128)(2,1)S(1)}, bf16[64,256]{1,0:T(8,128)(2,1)S(1)}, u32[]{:S(2)}, u32[]{:S(2)}) collective-permute-start(bf16[64,256]{1,0:T(8,128)(2,1)S(1)} %attend.1.refs_3_), channel_id=1, source_target_pairs={{0,2},{1,3},{2,0},{3,1},{4,6},{5,7},{6,4},{7,5},{8,10},{9,11},{10,... | collective-permute-start | bytes 98312 | tf_op jit(solution)/shard_map/ppermute | solution.py:30
  26.2 3.4 %collective-permute-start.11 = (bf16[64,256]{1,0:T(8,128)(2,1)S(1)}, bf16[64,256]{1,0:T(8,128)(2,1)S(1)}, u32[]{:S(2)}, u32[]{:S(2)}) collective-permute-start(bf16[64,256]{1,0:T(8,128)(2,1)S(1)} %attend.1.refs_3_), channel_id=1, source_target_pairs={{0,1},{1,0},{2,3},{3,2},{4,5},{5,4},{6,7},{7,6},{8,9},{9,8},{10,11... | collective-permute-start | bytes 98312 | tf_op jit(solution)/shard_map/ppermute | solution.py:30
  29.9 4.9 %collective-permute-start.12 = (bf16[2,1024]{1,0:T(2,128)(2,1)S(1)}, bf16[2,1024]{1,0:T(2,128)(2,1)S(1)}, u32[]{:S(2)}, u32[]{:S(2)}) collective-permute-start(bf16[2,1024]{1,0:T(2,128)(2,1)S(1)} %get-tuple-element.64), channel_id=1, source_target_pairs={{0,13},{1,12},{2,15},{3,14},{4,9},{5,8},{6,11},{7,10},{8,5},{9,4},... | collective-permute-start | bytes 12296 | tf_op jit(solution)/shard_map/ppermute | solution.py:49
  30.6 4.2 %collective-permute-start.13 = (bf16[2,1024]{1,0:T(2,128)(2,1)S(1)}, bf16[2,1024]{1,0:T(2,128)(2,1)S(1)}, u32[]{:S(2)}, u32[]{:S(2)}) collective-permute-start(bf16[2,1024]{1,0:T(2,128)(2,1)S(1)} %get-tuple-element.65), channel_id=1, source_target_pairs={{0,9},{1,8},{2,11},{3,10},{4,13},{5,12},{6,15},{7,14},{8,1},{9,0},... | collective-permute-start | bytes 12296 | tf_op jit(solution)/shard_map/ppermute | solution.py:49
  30.9 3.8 %collective-permute-start.14 = (bf16[2,1024]{1,0:T(2,128)(2,1)S(1)}, bf16[2,1024]{1,0:T(2,128)(2,1)S(1)}, u32[]{:S(2)}, u32[]{:S(2)}) collective-permute-start(bf16[2,1024]{1,0:T(2,128)(2,1)S(1)} %get-tuple-element.66), channel_id=1, source_target_pairs={{0,5},{1,4},{2,7},{3,6},{4,1},{5,0},{6,3},{7,2},{8,13},{9,12},{10,... | collective-permute-start | bytes 12296 | tf_op jit(solution)/shard_map/ppermute | solution.py:49
  35.7 5.8 %collective-permute-start.15 = (bf16[8,2048]{1,0:T(8,128)(2,1)S(1)}, bf16[8,2048]{1,0:T(8,128)(2,1)S(1)}, u32[]{:S(2)}, u32[]{:S(2)}) collective-permute-start(bf16[8,2048]{1,0:T(8,128)(2,1)S(1)} %get-tuple-element.68), channel_id=1, source_target_pairs={{0,12},{1,13},{2,14},{3,15},{4,8},{5,9},{6,10},{7,11},{8,4},{9,5},... | collective-permute-start | bytes 98312 | tf_op jit(solution)/shard_map/ppermute | solution.py:49
  38.2 5.0 %collective-permute-start.16 = (bf16[8,2048]{1,0:T(8,128)(2,1)S(1)}, bf16[8,2048]{1,0:T(8,128)(2,1)S(1)}, u32[]{:S(2)}, u32[]{:S(2)}) collective-permute-start(bf16[8,2048]{1,0:T(8,128)(2,1)S(1)} %get-tuple-element.69), channel_id=1, source_target_pairs={{0,8},{1,9},{2,10},{3,11},{4,12},{5,13},{6,14},{7,15},{8,0},{9,1},... | collective-permute-start | bytes 98312 | tf_op jit(solution)/shard_map/ppermute | solution.py:49
  39.5 4.0 %collective-permute-start.17 = (bf16[8,2048]{1,0:T(8,128)(2,1)S(1)}, bf16[8,2048]{1,0:T(8,128)(2,1)S(1)}, u32[]{:S(2)}, u32[]{:S(2)}) collective-permute-start(bf16[8,2048]{1,0:T(8,128)(2,1)S(1)} %get-tuple-element.70), channel_id=1, source_target_pairs={{0,4},{1,5},{2,6},{3,7},{4,0},{5,1},{6,2},{7,3},{8,12},{9,13},{10,... | collective-permute-start | bytes 98312 | tf_op jit(solution)/shard_map/ppermute | solution.py:49
  45.5 2.6 %collective-permute-start.18 = (bf16[8,3712]{1,0:T(8,128)(2,1)S(1)}, bf16[8,3712]{1,0:T(8,128)(2,1)S(1)}, u32[]{:S(2)}, u32[]{:S(2)}) collective-permute-start(bf16[8,3712]{1,0:T(8,128)(2,1)S(1)} %get-tuple-element.73.first_ref), channel_id=1, source_target_pairs={{0,1},{1,0},{2,3},{3,2},{4,5},{5,4},{6,7},{7,6},{8,9},{9,8},{10,11... | collective-permute-start | bytes 178184 | tf_op jit(solution)/shard_map/ppermute | solution.py:30
  45.5 8.1 %slice-start = ((s8[14680064]{0:T(1024)(128)(4,1)}), s8[4194304]{0:T(1024)(128)(4,1)S(1)}, s32[]{:S(2)}) async-start(s8[14680064]{0:T(1024)(128)(4,1)} %bitcast.4), calls=%async_computation | async-start | bytes 8388608
  45.5 8.1 %slice-start.1 = ((s8[14680064]{0:T(1024)(128)(4,1)}), s8[4194304]{0:T(1024)(128)(4,1)S(1)}, s32[]{:S(2)}) async-start(s8[14680064]{0:T(1024)(128)(4,1)} %bitcast.4), calls=%async_computation.1 | async-start | bytes 8388608
  45.5 8.1 %slice-start.2 = ((s8[14680064]{0:T(1024)(128)(4,1)}), s8[4194304]{0:T(1024)(128)(4,1)S(1)}, s32[]{:S(2)}) async-start(s8[14680064]{0:T(1024)(128)(4,1)} %bitcast.4), calls=%async_computation.2 | async-start | bytes 8388608
  45.5 8.1 %slice-start.3 = ((s8[14680064]{0:T(1024)(128)(4,1)}), s8[2097152]{0:T(1024)(128)(4,1)S(1)}, s32[]{:S(2)}) async-start(s8[14680064]{0:T(1024)(128)(4,1)} %bitcast.4), calls=%async_computation.3 | async-start | bytes 4194304
  47.6 1.5 %collective-permute-start.20 = (bf16[8,3584]{1,0:T(8,128)(2,1)S(1)}, bf16[8,3584]{1,0:T(8,128)(2,1)S(1)}, u32[]{:S(2)}, u32[]{:S(2)}) collective-permute-start(bf16[8,3584]{1,0:T(8,128)(2,1)S(1)} %second_gate_up.1.first_ref), channel_id=1, source_target_pairs={{0,1},{1,0},{2,3},{3,2},{4,5},{5,4},{6,7},{7,6},{8,9},{9,8},{10,11... | collective-permute-start | bytes 172040 | tf_op jit(solution)/shard_map/ppermute | solution.py:30
  48.1 5.5 %collective-permute-start.19 = (bf16[8,3712]{1,0:T(8,128)(2,1)S(1)}, bf16[8,3712]{1,0:T(8,128)(2,1)S(1)}, u32[]{:S(2)}, u32[]{:S(2)}) collective-permute-start(bf16[8,3712]{1,0:T(8,128)(2,1)S(1)} %pair_sum.2.one_near), channel_id=1, source_target_pairs={{0,2},{1,3},{2,0},{3,1},{4,6},{5,7},{6,4},{7,5},{8,10},{9,11},{10,... | collective-permute-start | bytes 178184 | tf_op jit(solution)/shard_map/ppermute | solution.py:30
  49.0 4.5 %collective-permute-start.21 = (bf16[8,3584]{1,0:T(8,128)(2,1)S(1)}, bf16[8,3584]{1,0:T(8,128)(2,1)S(1)}, u32[]{:S(2)}, u32[]{:S(2)}) collective-permute-start(bf16[8,3584]{1,0:T(8,128)(2,1)S(1)} %pair_sum.3.two_near), channel_id=1, source_target_pairs={{0,2},{1,3},{2,0},{3,1},{4,6},{5,7},{6,4},{7,5},{8,10},{9,11},{10,... | collective-permute-start | bytes 172040 | tf_op jit(solution)/shard_map/ppermute | solution.py:30
  55.9 5.5 %collective-permute-start.22 = (bf16[2,2048]{1,0:T(2,128)(2,1)S(1)}, bf16[2,2048]{1,0:T(2,128)(2,1)S(1)}, u32[]{:S(2)}, u32[]{:S(2)}) collective-permute-start(bf16[2,2048]{1,0:T(2,128)(2,1)S(1)} %get-tuple-element.75), channel_id=1, source_target_pairs={{0,12},{1,13},{2,14},{3,15},{4,8},{5,9},{6,10},{7,11},{8,4},{9,5},... | collective-permute-start | bytes 24584 | tf_op jit(solution)/shard_map/ppermute | solution.py:49
  58.5 4.5 %collective-permute-start.23 = (bf16[2,2048]{1,0:T(2,128)(2,1)S(1)}, bf16[2,2048]{1,0:T(2,128)(2,1)S(1)}, u32[]{:S(2)}, u32[]{:S(2)}) collective-permute-start(bf16[2,2048]{1,0:T(2,128)(2,1)S(1)} %get-tuple-element.76), channel_id=1, source_target_pairs={{0,8},{1,9},{2,10},{3,11},{4,12},{5,13},{6,14},{7,15},{8,0},{9,1},... | collective-permute-start | bytes 24584 | tf_op jit(solution)/shard_map/ppermute | solution.py:49
  58.5 4.5 %collective-permute-start.24 = (bf16[2,2048]{1,0:T(2,128)(2,1)S(1)}, bf16[2,2048]{1,0:T(2,128)(2,1)S(1)}, u32[]{:S(2)}, u32[]{:S(2)}) collective-permute-start(bf16[2,2048]{1,0:T(2,128)(2,1)S(1)} %get-tuple-element.77), channel_id=1, source_target_pairs={{0,4},{1,5},{2,6},{3,7},{4,0},{5,1},{6,2},{7,3},{8,12},{9,13},{10,... | collective-permute-start | bytes 24584 | tf_op jit(solution)/shard_map/ppermute | solution.py:49

commit v12 on v11

--- a/solution.py
+++ b/solution.py
@@ -16,6 +16,7 @@
 LANES = 128
 MIB = 2**20
 COPIES = 4
+STATS = 8
 
 epsilon = 1e-05
 rope_base = 500000.0
@@ -321,8 +322,16 @@
         stats_s[pl.ds(r, HEADS, stride=own_rows), :] = spread(
             three_parts(peak), lanes, 0
         ) + spread(three_parts(totals), lanes, 4)
-    out_ref[:, :HEAD_DIM] = mixed_s[...].astype(jnp.bfloat16)
-    out_ref[:, HEAD_DIM:] = stats_s[...].astype(jnp.bfloat16)
+    heads = own_rows * HEADS
+    out_ref[:heads, :] = mixed_s[...].astype(jnp.bfloat16)
+    packed = stats_s[:all_rows, :]
+    for j in range(1, here):
+        block = stats_s[j * all_rows : (j + 1) * all_rows, :]
+        packed = packed + pltpu.roll(block, j * STATS, axis=1)
+    spare = out_ref.shape[0] - heads - all_rows
+    if spare:
+        packed = jnp.concatenate([packed, jnp.zeros((spare, LANES), jnp.float32)], axis=0)
+    out_ref[heads:, :] = packed.astype(jnp.bfloat16)
 
 
 def attend(lengths, cosine, sine, parts, keys, values, later, slots):
@@ -330,7 +339,9 @@
     kv_cols = 2 * KV_HEADS * HEAD_DIM // slots
     return pl.pallas_call(
         functools.partial(attend_kernel, slots, len(parts)),
-        out_shape=jax.ShapeDtypeStruct((own_rows * HEADS, HEAD_DIM + LANES), jnp.bfloat16),
+        out_shape=jax.ShapeDtypeStruct(
+            (own_rows * HEADS + max(16, own_rows * slots), HEAD_DIM), jnp.bfloat16
+        ),
         in_specs=[in_vmem] * (5 + len(parts)) + [in_place] * len(later),
         out_specs=in_vmem,
         scratch_shapes=[
@@ -346,32 +357,33 @@
 
 
 def combine_kernel(shards, slots, *refs):
-    ins = refs[:shards]
     out_s = refs[-1]
-    all_rows = out_s.shape[0]
-    peaks = []
-    totals = []
-    for ref in ins:
-        stats = ref[:, HEAD_DIM:].astype(jnp.float32)
-        peaks.append(stats[:, 0:1] + stats[:, 1:2] + stats[:, 2:3])
-        totals.append(stats[:, 4:5] + stats[:, 5:6] + stats[:, 6:7])
-    top = functools.reduce(jnp.maximum, peaks)
-    mixed = 0.0
-    denominator = 0.0
-    for ref, peak, total in zip(ins, peaks, totals):
-        factor = jnp.exp(peak - top)
-        mixed = mixed + factor * ref[:, :HEAD_DIM].astype(jnp.float32)
-        denominator = denominator + factor * total
-    attended = mixed / denominator
-    for j in range(attended.shape[0] // all_rows):
-        block = attended[j * all_rows : (j + 1) * all_rows]
-        out_s[:, j * HEAD_DIM : (j + 1) * HEAD_DIM] = block
+    all_rows, columns = out_s.shape
+    here = columns // HEAD_DIM
+    heads = here * all_rows
+    mixtures = [ref[:heads, :].astype(jnp.float32) for ref in refs[:shards]]
+    stats = [ref[heads:, :].astype(jnp.float32)[:all_rows] for ref in refs[:shards]]
+    for j in range(here):
+
+        def whole(block, first):
+            lane = j * STATS + first
+            return block[:, lane : lane + 1] + block[:, lane + 1 : lane + 2] + block[:, lane + 2 : lane + 3]
+
+        peaks = [whole(block, 0) for block in stats]
+        top = functools.reduce(jnp.maximum, peaks)
+        mixed = 0.0
+        denominator = 0.0
+        for mixture, block, peak in zip(mixtures, stats, peaks):
+            factor = jnp.exp(peak - top)
+            mixed = mixed + factor * mixture[j * all_rows : (j + 1) * all_rows]
+            denominator = denominator + factor * whole(block, 4)
+        out_s[:, j * HEAD_DIM : (j + 1) * HEAD_DIM] = mixed / denominator
     part_rows(out_s, refs[-1 - slots : -1])
 
 
 def combine(parts, later, all_rows, slots):
     count = len(parts)
-    columns = parts[0].shape[0] // all_rows * HEAD_DIM
+    columns = HEADS // slots * HEAD_DIM
     return pl.pallas_call(
         functools.partial(combine_kernel, count, slots),
         out_shape=(jax.ShapeDtypeStruct((all_rows // slots, columns), jnp.bfloat16),) * slots,
@@ -610,14 +622,16 @@
     cosine, sine = rotation_tables(my_lengths.astype(jnp.float32), slots)
     my_lengths = jnp.broadcast_to(my_lengths[:, None], (own_rows, LANES))
     flat = (own_rows, key_cache.shape[1] * KV_HEADS, HEAD_DIM)
-    keys, values = load(key_cache.reshape(flat), value_cache.reshape(flat), after=rows)
+    (keys,) = load(key_cache.reshape(flat), after=rows)
     joined = stack(scatter_slots(pieces, 1))
-    joined, keys, values = lax.optimization_barrier((joined, keys, values))
-    (w_out,) = load(w_out, after=joined)
-    parts, w_out = lax.optimization_barrier((exchange(joined, "inner")[::-1], w_out))
+    joined, keys = lax.optimization_barrier((joined, keys))
+    (values,) = load(value_cache.reshape(flat), after=joined)
+    parts, values = lax.optimization_barrier((exchange(joined, "inner")[::-1], values))
     shard = attend(my_lengths, cosine, sine, parts, keys, values, [], slots)
 
-    pieces = combine(exchange(shard, "inner"), [w_gate], all_rows, slots)
+    (w_out,) = load(w_out, after=shard)
+    shards, w_out = lax.optimization_barrier((exchange(shard, "inner")[::-1], w_out))
+    pieces = combine(shards[::-1], [w_gate], all_rows, slots)
     parts = scatter_slots(project_out(scatter_slots(pieces, 1), w_out, [w_up]), 0)
 
     tiles = w_gate.shape[1] // LANES

time: 63.8 us -> 62.4 us (0.978)
  waiting for transfers between devices: 17.2 us -> 13.1 us
  starting transfers between devices: 27.9 us -> 29.3 us
  Pallas kernels: 18.1 us -> 19.2 us
    ppermute x13, waiting for transfers between devices: 9.04 us -> 6.02 us  [swap_with(): return lax.ppermute(value, axis, [(i, i ^ step) for i in range(count)])]
    ppermute x12, starting transfers between devices: 14.5 us -> 15.6 us  [scatter_slots(): got.append(lax.ppermute(pieces[k], ('tensor', 'inner'), pairs))]
    pallas_call x3 -> x4, Pallas kernels: 7.38 us -> 8.48 us  [load(): pl.pallas_call(functools.partial(load_kernel, spans), out_shape=tuple((pl...]
    ppermute x12, waiting for transfers between devices: 8.12 us -> 7.03 us  [scatter_slots(): got.append(lax.ppermute(pieces[k], ('tensor', 'inner'), pairs))]
  transfers between devices with their start and end apart: 25 -> 25, of which waited for: 11 -> 11; matrix products, arithmetic and copies ran while one was open for 0% -> 0% of each run, Pallas kernels for 15% -> 17%
where the time goes in v12:
time: 62.4 us; the launch traced here: 62.2 us
  starting transfers between devices  29.3 us (47%)
  Pallas kernels  19.2 us (31%)
  waiting for transfers between devices  13.1 us (21%)
    ppermute x12, starting transfers between devices, scatter_slots(): got.append(lax.ppermute(pieces[k], ('tensor', 'inner'), pairs))  15.6 us
    ppermute x13, starting transfers between devices, swap_with(): return lax.ppermute(value, axis, [(i, i ^ step) for i in range(count)])  13.7 us
    pallas_call x4, Pallas kernels, load(): pl.pallas_call(functools.partial(load_kernel, spans), out_shape=tuple((pl...  8.48 us
    ppermute x12, waiting for transfers between devices, scatter_slots(): got.append(lax.ppermute(pieces[k], ('tensor', 'inner'), pairs))  7.03 us
    ppermute x13, waiting for transfers between devices, swap_with(): return lax.ppermute(value, axis, [(i, i ^ step) for i in range(count)])  6.02 us
    pallas_call x1, Pallas kernels, project_down(): pl.pallas_call(down_kernel, out_shape=(jax.ShapeDtypeStruct((rows // slot...  2.28 us
    pallas_call x1, Pallas kernels, first_gate_up(): pl.pallas_call(functools.partial(first_gate_up_kernel, slots, count), out...  2 us
    pallas_call x1, Pallas kernels, second_gate_up(): pl.pallas_call(functools.partial(second_gate_up_kernel, first, count), ou...  2 us
  transfers between devices with their start and end apart: 25, of which 11 were waited for; matrix products, arithmetic and copies ran while one was open for 0% of the time, Pallas kernels for 17%

profile of v12, /device:TPU:0, one launch (start us, length us, event | category | flops | bytes accessed | tf_op | source)
XLA Modules:
  0.0 62.2 jit_solution(7023252222864974611)
XLA Ops:
  0.0 5.0 %collective-permute-start = (bf16[2,2048]{1,0:T(2,128)(2,1)}, bf16[2,2048]{1,0:T(2,128)(2,1)S(1)}, u32[]{:S(2)}, u32[]{:S(2)}) collective-permute-start(bf16[2,2048]{1,0:T(2,128)(2,1)} %refs_5_.1), channel_id=1, source_target_pairs={{0,12},{4,8},{8,4},{12,0},{1,13},{5,9},{9,5},{13,1},{2,14},{6,10},... | collective-permute-start | bytes 24584 | tf_op jit(solution)/shard_map/ppermute | solution.py:31
  5.0 0.0 collective-permute-start.1
  5.1 0.6 collective-permute-start.2
  5.6 2.9 %load.4 = (bf16[2,2048]{1,0:T(2,128)(2,1)S(1)}, bf16[2048]{0:T(1024)(128)(2,1)S(1)}, bf16[2048]{0:T(1024)(128)(2,1)S(1)}, bf16[2048,256]{1,0:T(8,128)(2,1)S(1)}, bf16[2048,1024]{1,0:T(8,128)(2,1)S(1)}) custom-call(bf16[2,2048]{1,0:T(2,128)(2,1)} %refs_5_.1, bf16[2048]{0:T(1024)(128)(2,1)} %refs_1_.1, bf16[2048]{0:T(1024)(128)(2,1)} %refs_2_.1, ...), custom_call_target="tpu_custom_call" | custom-call | bytes 5259264 | tf_op jit(solution)/shard_map/load/pallas_call | solution.py:145
  8.5 0.0 collective-permute-done.refs_0_
  8.5 1.3 %collective-permute-done.1.refs_1_ = bf16[2,2048]{1,0:T(2,128)(2,1)S(1)} collective-permute-done((bf16[2,2048]{1,0:T(2,128)(2,1)}, bf16[2,2048]{1,0:T(2,128)(2,1)S(1)}, u32[]{:S(2)}, u32[]{:S(2)}) %collective-permute-start.1) | collective-permute-done | bytes 8224 | tf_op jit(solution)/shard_map/ppermute | solution.py:31
  9.8 0.0 collective-permute-done.2.refs_2_
  9.8 0.8 %project_qkv.1 = (f32[8,2048]{1,0:T(8,128)S(1)}, bf16[2,1408]{1,0:T(2,128)(2,1)S(1)}, bf16[2,1408]{1,0:T(2,128)(2,1)S(1)}, bf16[2,1408]{1,0:T(2,128)(2,1)S(1)}, bf16[2,1408]{1,0:T(2,128)(2,1)S(1)}) custom-call(bf16[2048]{0:T(1024)(128)(2,1)S(1)} %get-tuple-element.44.gain_ref, bf16[2048,1024]{1,0:T(8,128)(2,1)S(1)} %get-tuple-element.45.wq_ref, ...), custom_call_target="tpu_custom_call" | custom-call | tf_op jit(solution)/shard_map/project_qkv/pallas_call | solution.py:198
  10.6 1.2 %collective-permute-start.3 = (bf16[2,1408]{1,0:T(2,128)(2,1)S(1)}, bf16[2,1408]{1,0:T(2,128)(2,1)S(1)}, u32[]{:S(2)}, u32[]{:S(2)}) collective-permute-start(bf16[2,1408]{1,0:T(2,128)(2,1)S(1)} %get-tuple-element.52), channel_id=1, source_target_pairs={{0,13},{1,12},{2,15},{3,14},{4,9},{5,8},{6,11},{7,10},{8,5},{9,4},... | collective-permute-start | bytes 16904 | tf_op jit(solution)/shard_map/ppermute | solution.py:50
  11.9 0.2 collective-permute-start.4
  12.1 1.5 %collective-permute-start.5 = (bf16[2,1408]{1,0:T(2,128)(2,1)S(1)}, bf16[2,1408]{1,0:T(2,128)(2,1)S(1)}, u32[]{:S(2)}, u32[]{:S(2)}) collective-permute-start(bf16[2,1408]{1,0:T(2,128)(2,1)S(1)} %get-tuple-element.54), channel_id=1, source_target_pairs={{0,5},{1,4},{2,7},{3,6},{4,1},{5,0},{6,3},{7,2},{8,13},{9,12},{10,... | collective-permute-start | bytes 16904 | tf_op jit(solution)/shard_map/ppermute | solution.py:50
  13.7 0.1 fusion.4
  13.7 1.6 %load.5.key_ref = bf16[2,4096,128]{2,1,0:T(8,128)(2,1)S(1)} custom-call(bf16[2,4096,128]{2,1,0:T(8,128)(2,1)} %bitcast.12, f32[8,2048]{1,0:T(8,128)S(1)} %get-tuple-element.49.refs_1_.rows_ref), custom_call_target="tpu_custom_call" | custom-call | bytes 2097152 | tf_op jit(solution)/shard_map/load/pallas_call | solution.py:145
  15.4 0.2 collective-permute-done.3.refs_0_
  15.6 0.3 collective-permute-done.4.refs_1_
  15.8 0.0 collective-permute-done.5.refs_2_
  15.9 2.7 %collective-permute-start.6 = (bf16[8,1408]{1,0:T(8,128)(2,1)S(1)}, bf16[8,1408]{1,0:T(8,128)(2,1)S(1)}, u32[]{:S(2)}, u32[]{:S(2)}) collective-permute-start(bf16[8,1408]{1,0:T(8,128)(2,1)S(1)} %stack.1.refs_1_.refs_0_), channel_id=1, source_target_pairs={{0,3},{1,2},{2,1},{3,0},{4,7},{5,6},{6,5},{7,4},{8,11},{9,10},{10,... | collective-permute-start | bytes 67592 | tf_op jit(solution)/shard_map/ppermute | solution.py:31
  18.5 0.5 collective-permute-start.7
  19.1 0.0 collective-permute-start.8
  19.1 0.1 fusion
  19.2 0.0 slice-start.2
  19.2 0.0 slice-start.5
  19.2 1.8 %load.6.value_ref = bf16[2,4096,128]{2,1,0:T(8,128)(2,1)S(1)} custom-call(bf16[2,4096,128]{2,1,0:T(8,128)(2,1)} %bitcast.13, bf16[8,1408]{1,0:T(8,128)(2,1)S(1)} %stack.1.refs_1_.refs_0_), custom_call_target="tpu_custom_call" | custom-call | bytes 2097152 | tf_op jit(solution)/shard_map/load/pallas_call | solution.py:145
  21.0 0.0 collective-permute-done.6.refs_3_
  21.0 1.3 %collective-permute-done.7.refs_2_ = bf16[8,1408]{1,0:T(8,128)(2,1)S(1)} collective-permute-done((bf16[8,1408]{1,0:T(8,128)(2,1)S(1)}, bf16[8,1408]{1,0:T(8,128)(2,1)S(1)}, u32[]{:S(2)}, u32[]{:S(2)}) %collective-permute-start.7) | collective-permute-done | bytes 22560 | tf_op jit(solution)/shard_map/ppermute | solution.py:31
  22.3 0.0 collective-permute-done.8.refs_1_
  22.4 0.1 broadcast_in_dim.10.lengths_ref
  22.4 1.7 %attend.1.refs_1_.refs_3_ = bf16[80,128]{1,0:T(8,128)(2,1)S(1)} custom-call(s32[2,128]{1,0:T(2,128)S(1)} %broadcast_in_dim.10.lengths_ref, f32[8,128]{1,0:T(8,128)S(1)} %bitcast.10, f32[8,128]{1,0:T(8,128)S(1)} %bitcast.11, bf16[2,4096,128]{2,1,0:T(8,128)(2,1)S(1)} %load.5.key_ref, bf16[2,4096,128]{2,1,0:T(8,128)(2,1)S(1)} %load.6.value_ref, ...), custom_call_target="tpu_custom_call" | custom-call | tf_op jit(solution)/shard_map/attend/pallas_call | solution.py:340
  24.2 0.0 slice-start.3
  24.2 0.0 slice-start.6
  24.2 0.6 collective-permute-start.10
  24.8 0.0 collective-permute-start.11
  24.8 1.6 %collective-permute-start.9 = (bf16[80,128]{1,0:T(8,128)(2,1)S(1)}, bf16[80,128]{1,0:T(8,128)(2,1)S(1)}, u32[]{:S(2)}, u32[]{:S(2)}) collective-permute-start(bf16[80,128]{1,0:T(8,128)(2,1)S(1)} %attend.1.refs_1_.refs_3_), channel_id=1, source_target_pairs={{0,3},{1,2},{2,1},{3,0},{4,7},{5,6},{6,5},{7,4},{8,11},{9,10},{10,... | collective-permute-start | bytes 61448 | tf_op jit(solution)/shard_map/ppermute | solution.py:31
  26.4 2.2 %load.7.weight_ref = bf16[1024,2048]{1,0:T(8,128)(2,1)S(1)} custom-call(bf16[1024,2048]{1,0:T(8,128)(2,1)} %refs_0_.3, bf16[80,128]{1,0:T(8,128)(2,1)S(1)} %attend.1.refs_1_.refs_3_), custom_call_target="tpu_custom_call" | custom-call | bytes 4194304 | tf_op jit(solution)/shard_map/load/pallas_call | solution.py:145
  28.6 0.0 slice-start.7
  28.6 0.0 collective-permute-done.10.refs_1_
  28.6 0.0 collective-permute-done.9.refs_0_
  28.7 0.3 combine.1
  29.0 1.6 %collective-permute-start.12 = (bf16[2,1024]{1,0:T(2,128)(2,1)S(1)}, bf16[2,1024]{1,0:T(2,128)(2,1)S(1)}, u32[]{:S(2)}, u32[]{:S(2)}) collective-permute-start(bf16[2,1024]{1,0:T(2,128)(2,1)S(1)} %get-tuple-element.68), channel_id=1, source_target_pairs={{0,13},{1,12},{2,15},{3,14},{4,9},{5,8},{6,11},{7,10},{8,5},{9,4},... | collective-permute-start | bytes 12296 | tf_op jit(solution)/shard_map/ppermute | solution.py:50
  30.5 0.0 collective-permute-start.13
  30.6 2.2 %collective-permute-start.14 = (bf16[2,1024]{1,0:T(2,128)(2,1)S(1)}, bf16[2,1024]{1,0:T(2,128)(2,1)S(1)}, u32[]{:S(2)}, u32[]{:S(2)}) collective-permute-start(bf16[2,1024]{1,0:T(2,128)(2,1)S(1)} %get-tuple-element.70), channel_id=1, source_target_pairs={{0,5},{1,4},{2,7},{3,6},{4,1},{5,0},{6,3},{7,2},{8,13},{9,12},{10,... | collective-permute-start | bytes 12296 | tf_op jit(solution)/shard_map/ppermute | solution.py:50
  32.8 1.1 %collective-permute-done.12.refs_0_ = bf16[2,1024]{1,0:T(2,128)(2,1)S(1)} collective-permute-done((bf16[2,1024]{1,0:T(2,128)(2,1)S(1)}, bf16[2,1024]{1,0:T(2,128)(2,1)S(1)}, u32[]{:S(2)}, u32[]{:S(2)}) %collective-permute-start.12) | collective-permute-done | bytes 4128 | tf_op jit(solution)/shard_map/ppermute | solution.py:50
  33.9 0.6 collective-permute-done.13.refs_1_
  34.5 1.0 %project_out.1 = (bf16[8,2048]{1,0:T(8,128)(2,1)S(1)}, bf16[8,2048]{1,0:T(8,128)(2,1)S(1)}, bf16[8,2048]{1,0:T(8,128)(2,1)S(1)}, bf16[8,2048]{1,0:T(8,128)(2,1)S(1)}) custom-call(bf16[1024,2048]{1,0:T(8,128)(2,1)S(1)} %load.7.weight_ref, bf16[2,1024]{1,0:T(2,128)(2,1)S(1)} %collective-permute-done.12.refs_0_, ...), custom_call_target="tpu_custom_call" | custom-call | tf_op jit(solution)/shard_map/project_out/pallas_call | solution.py:432
  35.5 1.9 %collective-permute-start.15 = (bf16[8,2048]{1,0:T(8,128)(2,1)S(1)}, bf16[8,2048]{1,0:T(8,128)(2,1)S(1)}, u32[]{:S(2)}, u32[]{:S(2)}) collective-permute-start(bf16[8,2048]{1,0:T(8,128)(2,1)S(1)} %get-tuple-element.72), channel_id=1, source_target_pairs={{0,12},{1,13},{2,14},{3,15},{4,8},{5,9},{6,10},{7,11},{8,4},{9,5},... | collective-permute-start | bytes 98312 | tf_op jit(solution)/shard_map/ppermute | solution.py:50
  37.4 1.2 %collective-permute-start.16 = (bf16[8,2048]{1,0:T(8,128)(2,1)S(1)}, bf16[8,2048]{1,0:T(8,128)(2,1)S(1)}, u32[]{:S(2)}, u32[]{:S(2)}) collective-permute-start(bf16[8,2048]{1,0:T(8,128)(2,1)S(1)} %get-tuple-element.73), channel_id=1, source_target_pairs={{0,8},{1,9},{2,10},{3,11},{4,12},{5,13},{6,14},{7,15},{8,0},{9,1},... | collective-permute-start | bytes 98312 | tf_op jit(solution)/shard_map/ppermute | solution.py:50
  38.6 1.2 %collective-permute-start.17 = (bf16[8,2048]{1,0:T(8,128)(2,1)S(1)}, bf16[8,2048]{1,0:T(8,128)(2,1)S(1)}, u32[]{:S(2)}, u32[]{:S(2)}) collective-permute-start(bf16[8,2048]{1,0:T(8,128)(2,1)S(1)} %get-tuple-element.74), channel_id=1, source_target_pairs={{0,4},{1,5},{2,6},{3,7},{4,0},{5,1},{6,2},{7,3},{8,12},{9,13},{10,... | collective-permute-start | bytes 98312 | tf_op jit(solution)/shard_map/ppermute | solution.py:50
  39.9 1.6 %collective-permute-done.15.refs_0_ = bf16[8,2048]{1,0:T(8,128)(2,1)S(1)} collective-permute-done((bf16[8,2048]{1,0:T(8,128)(2,1)S(1)}, bf16[8,2048]{1,0:T(8,128)(2,1)S(1)}, u32[]{:S(2)}, u32[]{:S(2)}) %collective-permute-start.15) | collective-permute-done | bytes 32800 | tf_op jit(solution)/shard_map/ppermute | solution.py:50
  41.5 1.2 %collective-permute-done.16.refs_1_ = bf16[8,2048]{1,0:T(8,128)(2,1)S(1)} collective-permute-done((bf16[8,2048]{1,0:T(8,128)(2,1)S(1)}, bf16[8,2048]{1,0:T(8,128)(2,1)S(1)}, u32[]{:S(2)}, u32[]{:S(2)}) %collective-permute-start.16) | collective-permute-done | bytes 32800 | tf_op jit(solution)/shard_map/ppermute | solution.py:50
  42.6 0.0 collective-permute-done.17.refs_2_
  42.7 2.0 %first_gate_up.1 = (bf16[8,3712]{1,0:T(8,128)(2,1)S(1)}, f32[2,2048]{1,0:T(2,128)S(1)}, bf16[8,2048]{1,0:T(8,128)(2,1)S(1)}) custom-call(f32[8,2048]{1,0:T(8,128)S(1)} %get-tuple-element.49.refs_1_.rows_ref, bf16[2048]{0:T(1024)(128)(2,1)S(1)} %get-tuple-element.50.gain_ref, bf16[2048,3584]{1,0:T(8,128)(2,1)S(1)} %bitcast.5, bf16[2048,3584]{1,0:T(8,128)(2,1)S(1)} %bitcast.7, ...), custom_call_target="tpu_custom_call" | custom-call | flops 117440512 | bytes 14680064 | tf_op jit(solution)/shard_map/first_gate_up/pallas_call | solution.py:488
  44.7 0.0 slice-start.9
  44.7 2.0 %second_gate_up.1.first_ref = bf16[8,3584]{1,0:T(8,128)(2,1)S(1)} custom-call(bf16[8,2048]{1,0:T(8,128)(2,1)S(1)} %get-tuple-element.78.scaled_ref, bf16[2048,3584]{1,0:T(8,128)(2,1)S(1)} %bitcast.5, bf16[2048,3584]{1,0:T(8,128)(2,1)S(1)} %bitcast.7), custom_call_target="tpu_custom_call" | custom-call | flops 117440512 | bytes 14680064 | tf_op jit(solution)/shard_map/second_gate_up/pallas_call | solution.py:510
  46.7 0.5 collective-permute-start.20
  47.2 1.3 %collective-permute-start.19 = (bf16[8,3712]{1,0:T(8,128)(2,1)S(1)}, bf16[8,3712]{1,0:T(8,128)(2,1)S(1)}, u32[]{:S(2)}, u32[]{:S(2)}) collective-permute-start(bf16[8,3712]{1,0:T(8,128)(2,1)S(1)} %pair_sum.2.one_near), channel_id=1, source_target_pairs={{0,2},{1,3},{2,0},{3,1},{4,6},{5,7},{6,4},{7,5},{8,10},{9,11},{10,... | collective-permute-start | bytes 178184 | tf_op jit(solution)/shard_map/ppermute | solution.py:31
  48.5 0.9 %collective-permute-start.21 = (bf16[8,3584]{1,0:T(8,128)(2,1)S(1)}, bf16[8,3584]{1,0:T(8,128)(2,1)S(1)}, u32[]{:S(2)}, u32[]{:S(2)}) collective-permute-start(bf16[8,3584]{1,0:T(8,128)(2,1)S(1)} %pair_sum.3.two_near), channel_id=1, source_target_pairs={{0,2},{1,3},{2,0},{3,1},{4,6},{5,7},{6,4},{7,5},{8,10},{9,11},{10,... | collective-permute-start | bytes 172040 | tf_op jit(solution)/shard_map/ppermute | solution.py:31
  49.4 3.4 %collective-permute-done.21.two_far = bf16[8,3584]{1,0:T(8,128)(2,1)S(1)} collective-permute-done((bf16[8,3584]{1,0:T(8,128)(2,1)S(1)}, bf16[8,3584]{1,0:T(8,128)(2,1)S(1)}, u32[]{:S(2)}, u32[]{:S(2)}) %collective-permute-start.21) | collective-permute-done | bytes 57376 | tf_op jit(solution)/shard_map/ppermute | solution.py:31
  52.8 2.3 %project_down.1 = (bf16[2,2048]{1,0:T(2,128)(2,1)S(1)}, bf16[2,2048]{1,0:T(2,128)(2,1)S(1)}, bf16[2,2048]{1,0:T(2,128)(2,1)S(1)}, bf16[2,2048]{1,0:T(2,128)(2,1)S(1)}) custom-call(bf16[8,3712]{1,0:T(8,128)(2,1)S(1)} %pair_sum.2.one_near, bf16[8,3712]{1,0:T(8,128)(2,1)S(1)} %collective-permute-done.19.one_far, bf16[8,3584]{1,0:T(8,128)(2,1)S(1)} %pair_sum.3.two_near, ...), custom_call_target="tpu_custom_call" | custom-call | tf_op jit(solution)/shard_map/project_down/pallas_call | solution.py:553
  55.1 2.0 %collective-permute-start.22 = (bf16[2,2048]{1,0:T(2,128)(2,1)S(1)}, bf16[2,2048]{1,0:T(2,128)(2,1)S(1)}, u32[]{:S(2)}, u32[]{:S(2)}) collective-permute-start(bf16[2,2048]{1,0:T(2,128)(2,1)S(1)} %get-tuple-element.79), channel_id=1, source_target_pairs={{0,12},{1,13},{2,14},{3,15},{4,8},{5,9},{6,10},{7,11},{8,4},{9,5},... | collective-permute-start | bytes 24584 | tf_op jit(solution)/shard_map/ppermute | solution.py:50
  57.1 0.8 %collective-permute-start.23 = (bf16[2,2048]{1,0:T(2,128)(2,1)S(1)}, bf16[2,2048]{1,0:T(2,128)(2,1)S(1)}, u32[]{:S(2)}, u32[]{:S(2)}) collective-permute-start(bf16[2,2048]{1,0:T(2,128)(2,1)S(1)} %get-tuple-element.80), channel_id=1, source_target_pairs={{0,8},{1,9},{2,10},{3,11},{4,12},{5,13},{6,14},{7,15},{8,0},{9,1},... | collective-permute-start | bytes 24584 | tf_op jit(solution)/shard_map/ppermute | solution.py:50
  57.9 1.7 %collective-permute-start.24 = (bf16[2,2048]{1,0:T(2,128)(2,1)S(1)}, bf16[2,2048]{1,0:T(2,128)(2,1)S(1)}, u32[]{:S(2)}, u32[]{:S(2)}) collective-permute-start(bf16[2,2048]{1,0:T(2,128)(2,1)S(1)} %get-tuple-element.81), channel_id=1, source_target_pairs={{0,4},{1,5},{2,6},{3,7},{4,0},{5,1},{6,2},{7,3},{8,12},{9,13},{10,... | collective-permute-start | bytes 24584 | tf_op jit(solution)/shard_map/ppermute | solution.py:50
  59.6 1.1 %collective-permute-done.22.refs_0_ = bf16[2,2048]{1,0:T(2,128)(2,1)S(1)} collective-permute-done((bf16[2,2048]{1,0:T(2,128)(2,1)S(1)}, bf16[2,2048]{1,0:T(2,128)(2,1)S(1)}, u32[]{:S(2)}, u32[]{:S(2)}) %collective-permute-start.22) | collective-permute-done | bytes 8224 | tf_op jit(solution)/shard_map/ppermute | solution.py:50
  60.6 1.0 %collective-permute-done.23.refs_1_ = bf16[2,2048]{1,0:T(2,128)(2,1)S(1)} collective-permute-done((bf16[2,2048]{1,0:T(2,128)(2,1)S(1)}, bf16[2,2048]{1,0:T(2,128)(2,1)S(1)}, u32[]{:S(2)}, u32[]{:S(2)}) %collective-permute-start.23) | collective-permute-done | bytes 8224 | tf_op jit(solution)/shard_map/ppermute | solution.py:50
  61.6 0.6 finish.1
  (36 shorter events, 0.1 us)
Async XLA Ops:
  0.0 8.5 %collective-permute-start = (bf16[2,2048]{1,0:T(2,128)(2,1)}, bf16[2,2048]{1,0:T(2,128)(2,1)S(1)}, u32[]{:S(2)}, u32[]{:S(2)}) collective-permute-start(bf16[2,2048]{1,0:T(2,128)(2,1)} %refs_5_.1), channel_id=1, source_target_pairs={{0,12},{4,8},{8,4},{12,0},{1,13},{5,9},{9,5},{13,1},{2,14},{6,10},... | collective-permute-start | bytes 24584 | tf_op jit(solution)/shard_map/ppermute | solution.py:31
  5.0 4.8 %collective-permute-start.1 = (bf16[2,2048]{1,0:T(2,128)(2,1)}, bf16[2,2048]{1,0:T(2,128)(2,1)S(1)}, u32[]{:S(2)}, u32[]{:S(2)}) collective-permute-start(bf16[2,2048]{1,0:T(2,128)(2,1)} %refs_5_.1), channel_id=1, source_target_pairs={{0,8},{4,12},{8,0},{12,4},{1,9},{5,13},{9,1},{13,5},{2,10},{6,14},... | collective-permute-start | bytes 24584 | tf_op jit(solution)/shard_map/ppermute | solution.py:31
  5.1 4.8 %collective-permute-start.2 = (bf16[2,2048]{1,0:T(2,128)(2,1)}, bf16[2,2048]{1,0:T(2,128)(2,1)S(1)}, u32[]{:S(2)}, u32[]{:S(2)}) collective-permute-start(bf16[2,2048]{1,0:T(2,128)(2,1)} %refs_5_.1), channel_id=1, source_target_pairs={{0,4},{4,0},{8,12},{12,8},{1,5},{5,1},{9,13},{13,9},{2,6},{6,2},{1... | collective-permute-start | bytes 24584 | tf_op jit(solution)/shard_map/ppermute | solution.py:31
  5.6 8.0 %copy-start = (s32[8]{0:T(128)S(1)}, s32[8]{0:T(128)}, u32[]{:S(2)}) copy-start(s32[8]{0:T(128)} %param.23) | copy-start | bytes 100
  5.6 23.0 %slice-start = ((s8[14680064]{0:T(1024)(128)(4,1)}), s8[4194304]{0:T(1024)(128)(4,1)S(1)}, s32[]{:S(2)}) async-start(s8[14680064]{0:T(1024)(128)(4,1)} %bitcast.4), calls=%async_computation | async-start | bytes 8388608
  9.8 18.9 %slice-start.1 = ((s8[14680064]{0:T(1024)(128)(4,1)}), s8[4194304]{0:T(1024)(128)(4,1)S(1)}, s32[]{:S(2)}) async-start(s8[14680064]{0:T(1024)(128)(4,1)} %bitcast.4), calls=%async_computation.1 | async-start | bytes 8388608
  9.8 24.7 %slice-start.4 = ((s8[14680064]{0:T(1024)(128)(4,1)}), s8[4194304]{0:T(1024)(128)(4,1)S(1)}, s32[]{:S(2)}) async-start(s8[14680064]{0:T(1024)(128)(4,1)} %bitcast.6), calls=%async_computation.4 | async-start | bytes 8388608
  10.6 4.9 %collective-permute-start.3 = (bf16[2,1408]{1,0:T(2,128)(2,1)S(1)}, bf16[2,1408]{1,0:T(2,128)(2,1)S(1)}, u32[]{:S(2)}, u32[]{:S(2)}) collective-permute-start(bf16[2,1408]{1,0:T(2,128)(2,1)S(1)} %get-tuple-element.52), channel_id=1, source_target_pairs={{0,13},{1,12},{2,15},{3,14},{4,9},{5,8},{6,11},{7,10},{8,5},{9,4},... | collective-permute-start | bytes 16904 | tf_op jit(solution)/shard_map/ppermute | solution.py:50
  11.9 3.9 %collective-permute-start.4 = (bf16[2,1408]{1,0:T(2,128)(2,1)S(1)}, bf16[2,1408]{1,0:T(2,128)(2,1)S(1)}, u32[]{:S(2)}, u32[]{:S(2)}) collective-permute-start(bf16[2,1408]{1,0:T(2,128)(2,1)S(1)} %get-tuple-element.53), channel_id=1, source_target_pairs={{0,9},{1,8},{2,11},{3,10},{4,13},{5,12},{6,15},{7,14},{8,1},{9,0},... | collective-permute-start | bytes 16904 | tf_op jit(solution)/shard_map/ppermute | solution.py:50
  12.1 3.7 %collective-permute-start.5 = (bf16[2,1408]{1,0:T(2,128)(2,1)S(1)}, bf16[2,1408]{1,0:T(2,128)(2,1)S(1)}, u32[]{:S(2)}, u32[]{:S(2)}) collective-permute-start(bf16[2,1408]{1,0:T(2,128)(2,1)S(1)} %get-tuple-element.54), channel_id=1, source_target_pairs={{0,5},{1,4},{2,7},{3,6},{4,1},{5,0},{6,3},{7,2},{8,13},{9,12},{10,... | collective-permute-start | bytes 16904 | tf_op jit(solution)/shard_map/ppermute | solution.py:50
  15.9 5.1 %collective-permute-start.6 = (bf16[8,1408]{1,0:T(8,128)(2,1)S(1)}, bf16[8,1408]{1,0:T(8,128)(2,1)S(1)}, u32[]{:S(2)}, u32[]{:S(2)}) collective-permute-start(bf16[8,1408]{1,0:T(8,128)(2,1)S(1)} %stack.1.refs_1_.refs_0_), channel_id=1, source_target_pairs={{0,3},{1,2},{2,1},{3,0},{4,7},{5,6},{6,5},{7,4},{8,11},{9,10},{10,... | collective-permute-start | bytes 67592 | tf_op jit(solution)/shard_map/ppermute | solution.py:31
  18.5 3.8 %collective-permute-start.7 = (bf16[8,1408]{1,0:T(8,128)(2,1)S(1)}, bf16[8,1408]{1,0:T(8,128)(2,1)S(1)}, u32[]{:S(2)}, u32[]{:S(2)}) collective-permute-start(bf16[8,1408]{1,0:T(8,128)(2,1)S(1)} %stack.1.refs_1_.refs_0_), channel_id=1, source_target_pairs={{0,2},{1,3},{2,0},{3,1},{4,6},{5,7},{6,4},{7,5},{8,10},{9,11},{10,... | collective-permute-start | bytes 67592 | tf_op jit(solution)/shard_map/ppermute | solution.py:31
  19.1 3.3 %collective-permute-start.8 = (bf16[8,1408]{1,0:T(8,128)(2,1)S(1)}, bf16[8,1408]{1,0:T(8,128)(2,1)S(1)}, u32[]{:S(2)}, u32[]{:S(2)}) collective-permute-start(bf16[8,1408]{1,0:T(8,128)(2,1)S(1)} %stack.1.refs_1_.refs_0_), channel_id=1, source_target_pairs={{0,1},{1,0},{2,3},{3,2},{4,5},{5,4},{6,7},{7,6},{8,9},{9,8},{10,11... | collective-permute-start | bytes 67592 | tf_op jit(solution)/shard_map/ppermute | solution.py:31
  19.2 9.5 %slice-start.2 = ((s8[14680064]{0:T(1024)(128)(4,1)}), s8[4194304]{0:T(1024)(128)(4,1)S(1)}, s32[]{:S(2)}) async-start(s8[14680064]{0:T(1024)(128)(4,1)} %bitcast.4), calls=%async_computation.2 | async-start | bytes 8388608
  19.2 15.3 %slice-start.5 = ((s8[14680064]{0:T(1024)(128)(4,1)}), s8[4194304]{0:T(1024)(128)(4,1)S(1)}, s32[]{:S(2)}) async-start(s8[14680064]{0:T(1024)(128)(4,1)} %bitcast.6), calls=%async_computation.5 | async-start | bytes 8388608
  24.2 4.5 %slice-start.3 = ((s8[14680064]{0:T(1024)(128)(4,1)}), s8[2097152]{0:T(1024)(128)(4,1)S(1)}, s32[]{:S(2)}) async-start(s8[14680064]{0:T(1024)(128)(4,1)} %bitcast.4), calls=%async_computation.3 | async-start | bytes 4194304
  24.2 10.3 %slice-start.6 = ((s8[14680064]{0:T(1024)(128)(4,1)}), s8[4194304]{0:T(1024)(128)(4,1)S(1)}, s32[]{:S(2)}) async-start(s8[14680064]{0:T(1024)(128)(4,1)} %bitcast.6), calls=%async_computation.6 | async-start | bytes 8388608
  24.2 4.4 %collective-permute-start.10 = (bf16[80,128]{1,0:T(8,128)(2,1)S(1)}, bf16[80,128]{1,0:T(8,128)(2,1)S(1)}, u32[]{:S(2)}, u32[]{:S(2)}) collective-permute-start(bf16[80,128]{1,0:T(8,128)(2,1)S(1)} %attend.1.refs_1_.refs_3_), channel_id=1, source_target_pairs={{0,2},{1,3},{2,0},{3,1},{4,6},{5,7},{6,4},{7,5},{8,10},{9,11},{10,... | collective-permute-start | bytes 61448 | tf_op jit(solution)/shard_map/ppermute | solution.py:31
  24.8 3.8 %collective-permute-start.11 = (bf16[80,128]{1,0:T(8,128)(2,1)S(1)}, bf16[80,128]{1,0:T(8,128)(2,1)S(1)}, u32[]{:S(2)}, u32[]{:S(2)}) collective-permute-start(bf16[80,128]{1,0:T(8,128)(2,1)S(1)} %attend.1.refs_1_.refs_3_), channel_id=1, source_target_pairs={{0,1},{1,0},{2,3},{3,2},{4,5},{5,4},{6,7},{7,6},{8,9},{9,8},{10,11... | collective-permute-start | bytes 61448 | tf_op jit(solution)/shard_map/ppermute | solution.py:31
  24.8 3.9 %collective-permute-start.9 = (bf16[80,128]{1,0:T(8,128)(2,1)S(1)}, bf16[80,128]{1,0:T(8,128)(2,1)S(1)}, u32[]{:S(2)}, u32[]{:S(2)}) collective-permute-start(bf16[80,128]{1,0:T(8,128)(2,1)S(1)} %attend.1.refs_1_.refs_3_), channel_id=1, source_target_pairs={{0,3},{1,2},{2,1},{3,0},{4,7},{5,6},{6,5},{7,4},{8,11},{9,10},{10,... | collective-permute-start | bytes 61448 | tf_op jit(solution)/shard_map/ppermute | solution.py:31
  28.6 5.9 %slice-start.7 = ((s8[14680064]{0:T(1024)(128)(4,1)}), s8[2097152]{0:T(1024)(128)(4,1)S(1)}, s32[]{:S(2)}) async-start(s8[14680064]{0:T(1024)(128)(4,1)} %bitcast.6), calls=%async_computation.7 | async-start | bytes 4194304
  29.0 4.9 %collective-permute-start.12 = (bf16[2,1024]{1,0:T(2,128)(2,1)S(1)}, bf16[2,1024]{1,0:T(2,128)(2,1)S(1)}, u32[]{:S(2)}, u32[]{:S(2)}) collective-permute-start(bf16[2,1024]{1,0:T(2,128)(2,1)S(1)} %get-tuple-element.68), channel_id=1, source_target_pairs={{0,13},{1,12},{2,15},{3,14},{4,9},{5,8},{6,11},{7,10},{8,5},{9,4},... | collective-permute-start | bytes 12296 | tf_op jit(solution)/shard_map/ppermute | solution.py:50
  30.5 3.9 %collective-permute-start.13 = (bf16[2,1024]{1,0:T(2,128)(2,1)S(1)}, bf16[2,1024]{1,0:T(2,128)(2,1)S(1)}, u32[]{:S(2)}, u32[]{:S(2)}) collective-permute-start(bf16[2,1024]{1,0:T(2,128)(2,1)S(1)} %get-tuple-element.69), channel_id=1, source_target_pairs={{0,9},{1,8},{2,11},{3,10},{4,13},{5,12},{6,15},{7,14},{8,1},{9,0},... | collective-permute-start | bytes 12296 | tf_op jit(solution)/shard_map/ppermute | solution.py:50
  30.6 3.9 %collective-permute-start.14 = (bf16[2,1024]{1,0:T(2,128)(2,1)S(1)}, bf16[2,1024]{1,0:T(2,128)(2,1)S(1)}, u32[]{:S(2)}, u32[]{:S(2)}) collective-permute-start(bf16[2,1024]{1,0:T(2,128)(2,1)S(1)} %get-tuple-element.70), channel_id=1, source_target_pairs={{0,5},{1,4},{2,7},{3,6},{4,1},{5,0},{6,3},{7,2},{8,13},{9,12},{10,... | collective-permute-start | bytes 12296 | tf_op jit(solution)/shard_map/ppermute | solution.py:50
  35.5 6.0 %collective-permute-start.15 = (bf16[8,2048]{1,0:T(8,128)(2,1)S(1)}, bf16[8,2048]{1,0:T(8,128)(2,1)S(1)}, u32[]{:S(2)}, u32[]{:S(2)}) collective-permute-start(bf16[8,2048]{1,0:T(8,128)(2,1)S(1)} %get-tuple-element.72), channel_id=1, source_target_pairs={{0,12},{1,13},{2,14},{3,15},{4,8},{5,9},{6,10},{7,11},{8,4},{9,5},... | collective-permute-start | bytes 98312 | tf_op jit(solution)/shard_map/ppermute | solution.py:50
  37.4 5.2 %collective-permute-start.16 = (bf16[8,2048]{1,0:T(8,128)(2,1)S(1)}, bf16[8,2048]{1,0:T(8,128)(2,1)S(1)}, u32[]{:S(2)}, u32[]{:S(2)}) collective-permute-start(bf16[8,2048]{1,0:T(8,128)(2,1)S(1)} %get-tuple-element.73), channel_id=1, source_target_pairs={{0,8},{1,9},{2,10},{3,11},{4,12},{5,13},{6,14},{7,15},{8,0},{9,1},... | collective-permute-start | bytes 98312 | tf_op jit(solution)/shard_map/ppermute | solution.py:50
  38.6 4.0 %collective-permute-start.17 = (bf16[8,2048]{1,0:T(8,128)(2,1)S(1)}, bf16[8,2048]{1,0:T(8,128)(2,1)S(1)}, u32[]{:S(2)}, u32[]{:S(2)}) collective-permute-start(bf16[8,2048]{1,0:T(8,128)(2,1)S(1)} %get-tuple-element.74), channel_id=1, source_target_pairs={{0,4},{1,5},{2,6},{3,7},{4,0},{5,1},{6,2},{7,3},{8,12},{9,13},{10,... | collective-permute-start | bytes 98312 | tf_op jit(solution)/shard_map/ppermute | solution.py:50
  44.7 2.6 %collective-permute-start.18 = (bf16[8,3712]{1,0:T(8,128)(2,1)S(1)}, bf16[8,3712]{1,0:T(8,128)(2,1)S(1)}, u32[]{:S(2)}, u32[]{:S(2)}) collective-permute-start(bf16[8,3712]{1,0:T(8,128)(2,1)S(1)} %get-tuple-element.77.first_ref), channel_id=1, source_target_pairs={{0,1},{1,0},{2,3},{3,2},{4,5},{5,4},{6,7},{7,6},{8,9},{9,8},{10,11... | collective-permute-start | bytes 178184 | tf_op jit(solution)/shard_map/ppermute | solution.py:31
  44.7 8.1 %slice-start.8 = ((s8[14680064]{0:T(1024)(128)(4,1)}), s8[4194304]{0:T(1024)(128)(4,1)S(1)}, s32[]{:S(2)}) async-start(s8[14680064]{0:T(1024)(128)(4,1)} %bitcast.8), calls=%async_computation.8 | async-start | bytes 8388608
  44.7 8.1 %slice-start.9 = ((s8[14680064]{0:T(1024)(128)(4,1)}), s8[4194304]{0:T(1024)(128)(4,1)S(1)}, s32[]{:S(2)}) async-start(s8[14680064]{0:T(1024)(128)(4,1)} %bitcast.8), calls=%async_computation.9 | async-start | bytes 8388608
  44.7 8.1 %slice-start.10 = ((s8[14680064]{0:T(1024)(128)(4,1)}), s8[4194304]{0:T(1024)(128)(4,1)S(1)}, s32[]{:S(2)}) async-start(s8[14680064]{0:T(1024)(128)(4,1)} %bitcast.8), calls=%async_computation.10 | async-start | bytes 8388608
  44.7 8.1 %slice-start.11 = ((s8[14680064]{0:T(1024)(128)(4,1)}), s8[2097152]{0:T(1024)(128)(4,1)S(1)}, s32[]{:S(2)}) async-start(s8[14680064]{0:T(1024)(128)(4,1)} %bitcast.8), calls=%async_computation.11 | async-start | bytes 4194304
  46.7 1.8 %collective-permute-start.20 = (bf16[8,3584]{1,0:T(8,128)(2,1)S(1)}, bf16[8,3584]{1,0:T(8,128)(2,1)S(1)}, u32[]{:S(2)}, u32[]{:S(2)}) collective-permute-start(bf16[8,3584]{1,0:T(8,128)(2,1)S(1)} %second_gate_up.1.first_ref), channel_id=1, source_target_pairs={{0,1},{1,0},{2,3},{3,2},{4,5},{5,4},{6,7},{7,6},{8,9},{9,8},{10,11... | collective-permute-start | bytes 172040 | tf_op jit(solution)/shard_map/ppermute | solution.py:31
  47.2 5.6 %collective-permute-start.19 = (bf16[8,3712]{1,0:T(8,128)(2,1)S(1)}, bf16[8,3712]{1,0:T(8,128)(2,1)S(1)}, u32[]{:S(2)}, u32[]{:S(2)}) collective-permute-start(bf16[8,3712]{1,0:T(8,128)(2,1)S(1)} %pair_sum.2.one_near), channel_id=1, source_target_pairs={{0,2},{1,3},{2,0},{3,1},{4,6},{5,7},{6,4},{7,5},{8,10},{9,11},{10,... | collective-permute-start | bytes 178184 | tf_op jit(solution)/shard_map/ppermute | solution.py:31
  48.5 4.2 %collective-permute-start.21 = (bf16[8,3584]{1,0:T(8,128)(2,1)S(1)}, bf16[8,3584]{1,0:T(8,128)(2,1)S(1)}, u32[]{:S(2)}, u32[]{:S(2)}) collective-permute-start(bf16[8,3584]{1,0:T(8,128)(2,1)S(1)} %pair_sum.3.two_near), channel_id=1, source_target_pairs={{0,2},{1,3},{2,0},{3,1},{4,6},{5,7},{6,4},{7,5},{8,10},{9,11},{10,... | collective-permute-start | bytes 172040 | tf_op jit(solution)/shard_map/ppermute | solution.py:31
  55.1 5.5 %collective-permute-start.22 = (bf16[2,2048]{1,0:T(2,128)(2,1)S(1)}, bf16[2,2048]{1,0:T(2,128)(2,1)S(1)}, u32[]{:S(2)}, u32[]{:S(2)}) collective-permute-start(bf16[2,2048]{1,0:T(2,128)(2,1)S(1)} %get-tuple-element.79), channel_id=1, source_target_pairs={{0,12},{1,13},{2,14},{3,15},{4,8},{5,9},{6,10},{7,11},{8,4},{9,5},... | collective-permute-start | bytes 24584 | tf_op jit(solution)/shard_map/ppermute | solution.py:50
  57.1 4.5 %collective-permute-start.23 = (bf16[2,2048]{1,0:T(2,128)(2,1)S(1)}, bf16[2,2048]{1,0:T(2,128)(2,1)S(1)}, u32[]{:S(2)}, u32[]{:S(2)}) collective-permute-start(bf16[2,2048]{1,0:T(2,128)(2,1)S(1)} %get-tuple-element.80), channel_id=1, source_target_pairs={{0,8},{1,9},{2,10},{3,11},{4,12},{5,13},{6,14},{7,15},{8,0},{9,1},... | collective-permute-start | bytes 24584 | tf_op jit(solution)/shard_map/ppermute | solution.py:50
  57.9 3.7 %collective-permute-start.24 = (bf16[2,2048]{1,0:T(2,128)(2,1)S(1)}, bf16[2,2048]{1,0:T(2,128)(2,1)S(1)}, u32[]{:S(2)}, u32[]{:S(2)}) collective-permute-start(bf16[2,2048]{1,0:T(2,128)(2,1)S(1)} %get-tuple-element.81), channel_id=1, source_target_pairs={{0,4},{1,5},{2,6},{3,7},{4,0},{5,1},{6,2},{7,3},{8,12},{9,13},{10,... | collective-permute-start | bytes 24584 | tf_op jit(solution)/shard_map/ppermute | solution.py:50

commit v13 on v12

--- a/solution.py
+++ b/solution.py
@@ -15,7 +15,7 @@
 GROUP = HEADS // KV_HEADS
 LANES = 128
 MIB = 2**20
-COPIES = 4
+COPIES = 8
 STATS = 8
 
 epsilon = 1e-05
@@ -49,6 +49,30 @@
         ]
         got.append(lax.ppermute(pieces[k], ("tensor", "inner"), pairs))
     return got
+
+
+def joint_permute(value, route):
+    width = lax.axis_size("inner")
+    pairs = []
+    for t in range(lax.axis_size("tensor")):
+        for i in range(width):
+            to_t, to_i = route(t, i)
+            pairs.append((t * width + i, to_t * width + to_i))
+    return lax.ppermute(value, ("tensor", "inner"), pairs)
+
+
+def shared_slots(pieces, swap):
+    count = len(pieces)
+    pairs = [(k, count - k) for k in range(1, (count + 1) // 2)]
+    first = [
+        joint_permute(
+            operand, lambda t, i, low=low, high=high: (t ^ (high if i % 2 else low), i ^ 1)
+        )
+        for (low, high), operand in zip(pairs, swap)
+    ]
+    direct = [joint_permute(pieces[count // 2], lambda t, i: (t ^ (count // 2), i ^ 1))]
+    second = [swap_with(value, "inner", 1) for value in first]
+    return direct, first, second
 
 
 def steps_up(count):
@@ -378,17 +402,29 @@
             mixed = mixed + factor * mixture[j * all_rows : (j + 1) * all_rows]
             denominator = denominator + factor * whole(block, 4)
         out_s[:, j * HEAD_DIM : (j + 1) * HEAD_DIM] = mixed / denominator
-    part_rows(out_s, refs[-1 - slots : -1])
+    pairs = (slots - 1) // 2
+    part_rows(out_s, refs[-1 - slots - pairs : -1 - pairs])
+    rows = all_rows // slots
+    odd = lax.axis_index("inner") % 2 == 1
+    for n in range(pairs):
+        low, high = n + 1, slots - n - 1
+        sent = jnp.where(
+            odd,
+            out_s[high * rows : (high + 1) * rows, :],
+            out_s[low * rows : (low + 1) * rows, :],
+        )
+        refs[-1 - pairs + n][...] = sent.astype(jnp.bfloat16)
 
 
 def combine(parts, later, all_rows, slots):
     count = len(parts)
     columns = HEADS // slots * HEAD_DIM
+    outs = slots + (slots - 1) // 2
     return pl.pallas_call(
         functools.partial(combine_kernel, count, slots),
-        out_shape=(jax.ShapeDtypeStruct((all_rows // slots, columns), jnp.bfloat16),) * slots,
+        out_shape=(jax.ShapeDtypeStruct((all_rows // slots, columns), jnp.bfloat16),) * outs,
         in_specs=[in_vmem] * count + [in_place] * len(later),
-        out_specs=(in_vmem,) * slots,
+        out_specs=(in_vmem,) * outs,
         scratch_shapes=[pltpu.VMEM((all_rows, columns), jnp.float32)],
         compiler_params=params(2),
         name="combine",
@@ -406,13 +442,28 @@
     )
 
 
-def out_kernel(slots, later, weight_ref, *refs):
-    pieces = refs[:slots][::-1]
-    outs = refs[slots + later : 2 * slots + later]
+def out_kernel(slots, later, weight_ref, own_ref, *refs):
+    pairs = (slots - 1) // 2
+    direct_ref = refs[0]
+    first = refs[1 : 1 + pairs]
+    second = refs[1 + pairs : 1 + 2 * pairs]
+    outs = refs[1 + 2 * pairs + later : 1 + 2 * pairs + later + slots]
     left_s = refs[-1]
-    own_rows = pieces[0].shape[0]
+    own_rows = own_ref.shape[0]
     rows = left_s.shape[0]
-    lefts = [join_rows(pieces, left_s)]
+
+    def put(slot, value):
+        left_s[slot * own_rows : (slot + 1) * own_rows, :] = value
+
+    put(0, own_ref[...].astype(jnp.float32))
+    put(slots // 2, direct_ref[...].astype(jnp.float32))
+    odd = lax.axis_index("inner") % 2 == 1
+    for n in range(pairs):
+        one = first[n][...].astype(jnp.float32)
+        two = second[n][...].astype(jnp.float32)
+        put(n + 1, jnp.where(odd, one, two))
+        put(slots - n - 1, jnp.where(odd, two, one))
+    lefts = [left_s[...]]
     for k in range(1, slots):
         low = k & -k
         lefts.append(turned(lefts[k ^ low], low, own_rows))
@@ -425,19 +476,19 @@
     product_tiles(left, weight_ref, store)
 
 
-def project_out(pieces, weight, later):
-    slots = len(pieces)
-    own_rows, depth = pieces[0].shape
+def project_out(own, direct, first, second, weight, later, slots):
+    own_rows, depth = own.shape
     shape = jax.ShapeDtypeStruct((own_rows * slots, weight.shape[1]), jnp.bfloat16)
+    ins = 3 + len(first) + len(second)
     return pl.pallas_call(
         functools.partial(out_kernel, slots, len(later)),
         out_shape=(shape,) * slots,
-        in_specs=[in_vmem] * (1 + slots) + [in_place] * len(later),
+        in_specs=[in_vmem] * ins + [in_place] * len(later),
         out_specs=(in_vmem,) * slots,
         scratch_shapes=[pltpu.VMEM((own_rows * slots, depth), jnp.float32)],
         compiler_params=params(3),
         name="project_out",
-    )(resident(weight), *pieces[::-1], *[resident(w) for w in later])
+    )(resident(weight), own, direct, *first, *second, *[resident(w) for w in later])
 
 
 def pair_kernel(first_ref, second_ref, out_ref):
@@ -632,7 +683,9 @@
     (w_out,) = load(w_out, after=shard)
     shards, w_out = lax.optimization_barrier((exchange(shard, "inner")[::-1], w_out))
     pieces = combine(shards[::-1], [w_gate], all_rows, slots)
-    parts = scatter_slots(project_out(scatter_slots(pieces, 1), w_out, [w_up]), 0)
+    (direct,), first, second = shared_slots(pieces[:slots], pieces[slots:])
+    parts = project_out(pieces[0], direct, first, second, w_out, [w_up], slots)
+    parts = scatter_slots(parts, 0)
 
     tiles = w_gate.shape[1] // LANES
     first = (tiles + 1) // 2 * LANES

time: 62.4 us -> 63.5 us (1.018)
  waiting for transfers between devices: 13.1 us -> 15.6 us
  starting transfers between devices: 29.3 us -> 27 us
  Pallas kernels: 19.2 us -> 20.1 us
    ppermute x0 -> x2, waiting for transfers between devices: none -> 3.69 us  [joint_permute(): return lax.ppermute(value, ('tensor', 'inner'), pairs)]
    ppermute x12 -> x9, starting transfers between devices: 15.6 us -> 12.1 us  [scatter_slots(): got.append(lax.ppermute(pieces[k], ('tensor', 'inner'), pairs))]
    ppermute x12 -> x9, waiting for transfers between devices: 7.03 us -> 5.07 us  [scatter_slots(): got.append(lax.ppermute(pieces[k], ('tensor', 'inner'), pairs))]
    ppermute x0 -> x2, starting transfers between devices: none -> 1.15 us  [joint_permute(): return lax.ppermute(value, ('tensor', 'inner'), pairs)]
    ppermute x13 -> x14, waiting for transfers between devices: 6.02 us -> 6.84 us  [swap_with(): return lax.ppermute(value, axis, [(i, i ^ step) for i in range(count)])]
    ppermute x13 -> x14, starting transfers between devices: 13.7 us -> 13.7 us  [swap_with(): return lax.ppermute(value, axis, [(i, i ^ step) for i in range(count)])]
where the time goes in v13:
time: 63.5 us; the launch traced here: 63.3 us
  starting transfers between devices  27 us (43%)
  Pallas kernels  20.1 us (32%)
  waiting for transfers between devices  15.6 us (25%)
    ppermute x14, starting transfers between devices, swap_with(): return lax.ppermute(value, axis, [(i, i ^ step) for i in range(count)])  13.7 us
    ppermute x9, starting transfers between devices, scatter_slots(): got.append(lax.ppermute(pieces[k], ('tensor', 'inner'), pairs))  12.1 us
    pallas_call x4, Pallas kernels, load(): pl.pallas_call(functools.partial(load_kernel, spans), out_shape=tuple((pl...  8.8 us
    ppermute x14, waiting for transfers between devices, swap_with(): return lax.ppermute(value, axis, [(i, i ^ step) for i in range(count)])  6.84 us
    ppermute x9, waiting for transfers between devices, scatter_slots(): got.append(lax.ppermute(pieces[k], ('tensor', 'inner'), pairs))  5.07 us
    ppermute x2, waiting for transfers between devices, joint_permute(): return lax.ppermute(value, ('tensor', 'inner'), pairs)  3.69 us
    pallas_call x1, Pallas kernels, project_down(): pl.pallas_call(down_kernel, out_shape=(jax.ShapeDtypeStruct((rows // slot...  2.28 us
    pallas_call x1, Pallas kernels, first_gate_up(): pl.pallas_call(functools.partial(first_gate_up_kernel, slots, count), out...  2 us
  transfers between devices with their start and end apart: 25, of which 11 were waited for; matrix products, arithmetic and copies ran while one was open for 0% of the time, Pallas kernels for 17%

profile of v13, /device:TPU:0, one launch (start us, length us, event | category | flops | bytes accessed | tf_op | source)
XLA Modules:
  0.0 63.3 jit_solution(17810084568824399767)
XLA Ops:
  0.0 5.0 %collective-permute-start = (bf16[2,2048]{1,0:T(2,128)(2,1)}, bf16[2,2048]{1,0:T(2,128)(2,1)S(1)}, u32[]{:S(2)}, u32[]{:S(2)}) collective-permute-start(bf16[2,2048]{1,0:T(2,128)(2,1)} %refs_5_.1), channel_id=1, source_target_pairs={{0,12},{4,8},{8,4},{12,0},{1,13},{5,9},{9,5},{13,1},{2,14},{6,10},... | collective-permute-start | bytes 24584 | tf_op jit(solution)/shard_map/ppermute | solution.py:31
  5.0 0.0 collective-permute-start.1
  5.1 0.6 collective-permute-start.2
  5.6 3.1 %load.4 = (bf16[2,2048]{1,0:T(2,128)(2,1)S(1)}, bf16[2048]{0:T(1024)(128)(2,1)S(1)}, bf16[2048]{0:T(1024)(128)(2,1)S(1)}, bf16[2048,256]{1,0:T(8,128)(2,1)S(1)}, bf16[2048,1024]{1,0:T(8,128)(2,1)S(1)}) custom-call(bf16[2,2048]{1,0:T(2,128)(2,1)} %refs_5_.1, bf16[2048]{0:T(1024)(128)(2,1)} %refs_1_.1, bf16[2048]{0:T(1024)(128)(2,1)} %refs_2_.1, ...), custom_call_target="tpu_custom_call" | custom-call | bytes 5259264 | tf_op jit(solution)/shard_map/load/pallas_call | solution.py:169
  8.8 0.0 collective-permute-done.refs_0_
  8.8 1.0 %collective-permute-done.1.refs_1_ = bf16[2,2048]{1,0:T(2,128)(2,1)S(1)} collective-permute-done((bf16[2,2048]{1,0:T(2,128)(2,1)}, bf16[2,2048]{1,0:T(2,128)(2,1)S(1)}, u32[]{:S(2)}, u32[]{:S(2)}) %collective-permute-start.1) | collective-permute-done | bytes 8224 | tf_op jit(solution)/shard_map/ppermute | solution.py:31
  9.8 0.0 collective-permute-done.2.refs_2_
  9.8 0.8 %project_qkv.1 = (f32[8,2048]{1,0:T(8,128)S(1)}, bf16[2,1408]{1,0:T(2,128)(2,1)S(1)}, bf16[2,1408]{1,0:T(2,128)(2,1)S(1)}, bf16[2,1408]{1,0:T(2,128)(2,1)S(1)}, bf16[2,1408]{1,0:T(2,128)(2,1)S(1)}) custom-call(bf16[2048]{0:T(1024)(128)(2,1)S(1)} %get-tuple-element.43.gain_ref, bf16[2048,1024]{1,0:T(8,128)(2,1)S(1)} %get-tuple-element.44.wq_ref, ...), custom_call_target="tpu_custom_call" | custom-call | tf_op jit(solution)/shard_map/project_qkv/pallas_call | solution.py:222
  10.6 1.5 %collective-permute-start.3 = (bf16[2,1408]{1,0:T(2,128)(2,1)S(1)}, bf16[2,1408]{1,0:T(2,128)(2,1)S(1)}, u32[]{:S(2)}, u32[]{:S(2)}) collective-permute-start(bf16[2,1408]{1,0:T(2,128)(2,1)S(1)} %get-tuple-element.51), channel_id=1, source_target_pairs={{0,13},{1,12},{2,15},{3,14},{4,9},{5,8},{6,11},{7,10},{8,5},{9,4},... | collective-permute-start | bytes 16904 | tf_op jit(solution)/shard_map/ppermute | solution.py:50
  12.1 0.2 collective-permute-start.4
  12.4 1.5 %collective-permute-start.5 = (bf16[2,1408]{1,0:T(2,128)(2,1)S(1)}, bf16[2,1408]{1,0:T(2,128)(2,1)S(1)}, u32[]{:S(2)}, u32[]{:S(2)}) collective-permute-start(bf16[2,1408]{1,0:T(2,128)(2,1)S(1)} %get-tuple-element.53), channel_id=1, source_target_pairs={{0,5},{1,4},{2,7},{3,6},{4,1},{5,0},{6,3},{7,2},{8,13},{9,12},{10,... | collective-permute-start | bytes 16904 | tf_op jit(solution)/shard_map/ppermute | solution.py:50
  13.9 0.1 fusion.4
  14.0 1.7 %load.5.key_ref = bf16[2,4096,128]{2,1,0:T(8,128)(2,1)S(1)} custom-call(bf16[2,4096,128]{2,1,0:T(8,128)(2,1)} %bitcast.12, f32[8,2048]{1,0:T(8,128)S(1)} %get-tuple-element.48.refs_1_.rows_ref), custom_call_target="tpu_custom_call" | custom-call | bytes 2097152 | tf_op jit(solution)/shard_map/load/pallas_call | solution.py:169
  15.6 0.4 collective-permute-done.4.refs_1_
  16.1 0.0 collective-permute-done.5.refs_2_
  16.1 2.7 %collective-permute-start.6 = (bf16[8,1408]{1,0:T(8,128)(2,1)S(1)}, bf16[8,1408]{1,0:T(8,128)(2,1)S(1)}, u32[]{:S(2)}, u32[]{:S(2)}) collective-permute-start(bf16[8,1408]{1,0:T(8,128)(2,1)S(1)} %stack.1.refs_1_.refs_0_), channel_id=1, source_target_pairs={{0,3},{1,2},{2,1},{3,0},{4,7},{5,6},{6,5},{7,4},{8,11},{9,10},{10,... | collective-permute-start | bytes 67592 | tf_op jit(solution)/shard_map/ppermute | solution.py:31
  18.8 0.5 collective-permute-start.7
  19.3 0.0 collective-permute-start.8
  19.3 0.1 fusion
  19.4 0.0 slice-start.2
  19.4 0.0 slice-start.5
  19.5 1.8 %load.6.value_ref = bf16[2,4096,128]{2,1,0:T(8,128)(2,1)S(1)} custom-call(bf16[2,4096,128]{2,1,0:T(8,128)(2,1)} %bitcast.13, bf16[8,1408]{1,0:T(8,128)(2,1)S(1)} %stack.1.refs_1_.refs_0_), custom_call_target="tpu_custom_call" | custom-call | bytes 2097152 | tf_op jit(solution)/shard_map/load/pallas_call | solution.py:169
  21.3 1.3 %collective-permute-done.7.refs_2_ = bf16[8,1408]{1,0:T(8,128)(2,1)S(1)} collective-permute-done((bf16[8,1408]{1,0:T(8,128)(2,1)S(1)}, bf16[8,1408]{1,0:T(8,128)(2,1)S(1)}, u32[]{:S(2)}, u32[]{:S(2)}) %collective-permute-start.7) | collective-permute-done | bytes 22560 | tf_op jit(solution)/shard_map/ppermute | solution.py:31
  22.6 0.0 collective-permute-done.8.refs_1_
  22.6 0.1 broadcast_in_dim.10.lengths_ref
  22.7 1.7 %attend.1.refs_1_.refs_3_ = bf16[80,128]{1,0:T(8,128)(2,1)S(1)} custom-call(s32[2,128]{1,0:T(2,128)S(1)} %broadcast_in_dim.10.lengths_ref, f32[8,128]{1,0:T(8,128)S(1)} %bitcast.10, f32[8,128]{1,0:T(8,128)S(1)} %bitcast.11, bf16[2,4096,128]{2,1,0:T(8,128)(2,1)S(1)} %load.5.key_ref, bf16[2,4096,128]{2,1,0:T(8,128)(2,1)S(1)} %load.6.value_ref, ...), custom_call_target="tpu_custom_call" | custom-call | tf_op jit(solution)/shard_map/attend/pallas_call | solution.py:364
  24.4 0.0 slice-start.3
  24.4 0.0 slice-start.6
  24.4 0.6 collective-permute-start.10
  25.0 0.0 collective-permute-start.11
  25.0 1.6 %collective-permute-start.9 = (bf16[80,128]{1,0:T(8,128)(2,1)S(1)}, bf16[80,128]{1,0:T(8,128)(2,1)S(1)}, u32[]{:S(2)}, u32[]{:S(2)}) collective-permute-start(bf16[80,128]{1,0:T(8,128)(2,1)S(1)} %attend.1.refs_1_.refs_3_), channel_id=1, source_target_pairs={{0,3},{1,2},{2,1},{3,0},{4,7},{5,6},{6,5},{7,4},{8,11},{9,10},{10,... | collective-permute-start | bytes 61448 | tf_op jit(solution)/shard_map/ppermute | solution.py:31
  26.6 2.2 %load.7.weight_ref = bf16[1024,2048]{1,0:T(8,128)(2,1)S(1)} custom-call(bf16[1024,2048]{1,0:T(8,128)(2,1)} %refs_0_.3, bf16[80,128]{1,0:T(8,128)(2,1)S(1)} %attend.1.refs_1_.refs_3_), custom_call_target="tpu_custom_call" | custom-call | bytes 4194304 | tf_op jit(solution)/shard_map/load/pallas_call | solution.py:169
  28.9 0.0 slice-start.7
  28.9 0.0 collective-permute-done.9.refs_0_
  29.0 0.9 %combine.1 = (bf16[2,1024]{1,0:T(2,128)(2,1)S(1)}, bf16[2,1024]{1,0:T(2,128)(2,1)}, bf16[2,1024]{1,0:T(2,128)(2,1)S(1)}, bf16[2,1024]{1,0:T(2,128)(2,1)}, bf16[2,1024]{1,0:T(2,128)(2,1)S(1)}) custom-call(bf16[80,128]{1,0:T(8,128)(2,1)S(1)} %collective-permute-done.9.refs_0_, bf16[80,128]{1,0:T(8,128)(2,1)S(1)} %collective-permute-done.10.refs_1_, ...), custom_call_target="tpu_custom_call" | custom-call | tf_op jit(solution)/shard_map/combine/pallas_call | solution.py:423
  29.8 0.0 collective-permute-start.13
  29.8 1.1 %collective-permute-start.12 = (bf16[2,1024]{1,0:T(2,128)(2,1)S(1)}, bf16[2,1024]{1,0:T(2,128)(2,1)S(1)}, u32[]{:S(2)}, u32[]{:S(2)}) collective-permute-start(bf16[2,1024]{1,0:T(2,128)(2,1)S(1)} %get-tuple-element.68), channel_id=1, source_target_pairs={{0,9},{1,8},{2,11},{3,10},{4,13},{5,12},{6,15},{7,14},{8,1},{9,0},... | collective-permute-start | bytes 12296 | tf_op jit(solution)/shard_map/ppermute | solution.py:61
  31.0 3.7 %collective-permute-done.13.refs_1_ = bf16[2,1024]{1,0:T(2,128)(2,1)S(1)} collective-permute-done((bf16[2,1024]{1,0:T(2,128)(2,1)S(1)}, bf16[2,1024]{1,0:T(2,128)(2,1)S(1)}, u32[]{:S(2)}, u32[]{:S(2)}) %collective-permute-start.13) | collective-permute-done | bytes 4128 | tf_op jit(solution)/shard_map/ppermute | solution.py:61
  34.7 1.2 %collective-permute-done.14.refs_2_ = bf16[2,1024]{1,0:T(2,128)(2,1)S(1)} collective-permute-done((bf16[2,1024]{1,0:T(2,128)(2,1)S(1)}, bf16[2,1024]{1,0:T(2,128)(2,1)S(1)}, u32[]{:S(2)}, u32[]{:S(2)}) %collective-permute-start.14) | collective-permute-done | bytes 4128 | tf_op jit(solution)/shard_map/ppermute | solution.py:31
  35.8 1.0 %project_out.1 = (bf16[8,2048]{1,0:T(8,128)(2,1)S(1)}, bf16[8,2048]{1,0:T(8,128)(2,1)S(1)}, bf16[8,2048]{1,0:T(8,128)(2,1)S(1)}, bf16[8,2048]{1,0:T(8,128)(2,1)S(1)}) custom-call(bf16[1024,2048]{1,0:T(8,128)(2,1)S(1)} %load.7.weight_ref, bf16[2,1024]{1,0:T(2,128)(2,1)S(1)} %get-tuple-element.67.own_ref, bf16[2,1024]{1,0:T(2,128)(2,1)S(1)} %collective-permute-done.12.refs_0_, ...), custom_call_target="tpu_custom_call" | custom-call | tf_op jit(solution)/shard_map/project_out/pallas_call | solution.py:483
  36.8 2.0 %collective-permute-start.15 = (bf16[8,2048]{1,0:T(8,128)(2,1)S(1)}, bf16[8,2048]{1,0:T(8,128)(2,1)S(1)}, u32[]{:S(2)}, u32[]{:S(2)}) collective-permute-start(bf16[8,2048]{1,0:T(8,128)(2,1)S(1)} %get-tuple-element.70), channel_id=1, source_target_pairs={{0,12},{1,13},{2,14},{3,15},{4,8},{5,9},{6,10},{7,11},{8,4},{9,5},... | collective-permute-start | bytes 98312 | tf_op jit(solution)/shard_map/ppermute | solution.py:50
  38.8 2.4 %collective-permute-start.17 = (bf16[8,2048]{1,0:T(8,128)(2,1)S(1)}, bf16[8,2048]{1,0:T(8,128)(2,1)S(1)}, u32[]{:S(2)}, u32[]{:S(2)}) collective-permute-start(bf16[8,2048]{1,0:T(8,128)(2,1)S(1)} %get-tuple-element.72), channel_id=1, source_target_pairs={{0,4},{1,5},{2,6},{3,7},{4,0},{5,1},{6,2},{7,3},{8,12},{9,13},{10,... | collective-permute-start | bytes 98312 | tf_op jit(solution)/shard_map/ppermute | solution.py:50
  41.2 1.4 %collective-permute-done.15.refs_0_ = bf16[8,2048]{1,0:T(8,128)(2,1)S(1)} collective-permute-done((bf16[8,2048]{1,0:T(8,128)(2,1)S(1)}, bf16[8,2048]{1,0:T(8,128)(2,1)S(1)}, u32[]{:S(2)}, u32[]{:S(2)}) %collective-permute-start.15) | collective-permute-done | bytes 32800 | tf_op jit(solution)/shard_map/ppermute | solution.py:50
  42.6 1.0 %collective-permute-done.16.refs_1_ = bf16[8,2048]{1,0:T(8,128)(2,1)S(1)} collective-permute-done((bf16[8,2048]{1,0:T(8,128)(2,1)S(1)}, bf16[8,2048]{1,0:T(8,128)(2,1)S(1)}, u32[]{:S(2)}, u32[]{:S(2)}) %collective-permute-start.16) | collective-permute-done | bytes 32800 | tf_op jit(solution)/shard_map/ppermute | solution.py:50
  43.6 0.0 collective-permute-done.17.refs_2_
  43.7 2.0 %first_gate_up.1 = (bf16[8,3712]{1,0:T(8,128)(2,1)S(1)}, f32[2,2048]{1,0:T(2,128)S(1)}, bf16[8,2048]{1,0:T(8,128)(2,1)S(1)}) custom-call(f32[8,2048]{1,0:T(8,128)S(1)} %get-tuple-element.48.refs_1_.rows_ref, bf16[2048]{0:T(1024)(128)(2,1)S(1)} %get-tuple-element.49.gain_ref, bf16[2048,3584]{1,0:T(8,128)(2,1)S(1)} %bitcast.5, bf16[2048,3584]{1,0:T(8,128)(2,1)S(1)} %bitcast.7, ...), custom_call_target="tpu_custom_call" | custom-call | flops 117440512 | bytes 14680064 | tf_op jit(solution)/shard_map/first_gate_up/pallas_call | solution.py:539
  45.7 0.0 collective-permute-start.18
  45.7 0.0 slice-start.9
  45.7 2.0 %second_gate_up.1.first_ref = bf16[8,3584]{1,0:T(8,128)(2,1)S(1)} custom-call(bf16[8,2048]{1,0:T(8,128)(2,1)S(1)} %get-tuple-element.76.scaled_ref, bf16[2048,3584]{1,0:T(8,128)(2,1)S(1)} %bitcast.5, bf16[2048,3584]{1,0:T(8,128)(2,1)S(1)} %bitcast.7), custom_call_target="tpu_custom_call" | custom-call | flops 117440512 | bytes 14680064 | tf_op jit(solution)/shard_map/second_gate_up/pallas_call | solution.py:561
  47.7 0.5 collective-permute-start.20
  48.2 0.0 collective-permute-done.18.second_ref
  48.2 0.9 %collective-permute-start.19 = (bf16[8,3712]{1,0:T(8,128)(2,1)S(1)}, bf16[8,3712]{1,0:T(8,128)(2,1)S(1)}, u32[]{:S(2)}, u32[]{:S(2)}) collective-permute-start(bf16[8,3712]{1,0:T(8,128)(2,1)S(1)} %pair_sum.2.one_near), channel_id=1, source_target_pairs={{0,2},{1,3},{2,0},{3,1},{4,6},{5,7},{6,4},{7,5},{8,10},{9,11},{10,... | collective-permute-start | bytes 178184 | tf_op jit(solution)/shard_map/ppermute | solution.py:31
  49.1 0.0 collective-permute-done.20.second_ref
  49.1 1.3 %collective-permute-start.21 = (bf16[8,3584]{1,0:T(8,128)(2,1)S(1)}, bf16[8,3584]{1,0:T(8,128)(2,1)S(1)}, u32[]{:S(2)}, u32[]{:S(2)}) collective-permute-start(bf16[8,3584]{1,0:T(8,128)(2,1)S(1)} %pair_sum.3.two_near), channel_id=1, source_target_pairs={{0,2},{1,3},{2,0},{3,1},{4,6},{5,7},{6,4},{7,5},{8,10},{9,11},{10,... | collective-permute-start | bytes 172040 | tf_op jit(solution)/shard_map/ppermute | solution.py:31
  50.4 3.3 %collective-permute-done.21.two_far = bf16[8,3584]{1,0:T(8,128)(2,1)S(1)} collective-permute-done((bf16[8,3584]{1,0:T(8,128)(2,1)S(1)}, bf16[8,3584]{1,0:T(8,128)(2,1)S(1)}, u32[]{:S(2)}, u32[]{:S(2)}) %collective-permute-start.21) | collective-permute-done | bytes 57376 | tf_op jit(solution)/shard_map/ppermute | solution.py:31
  53.7 0.0 collective-permute-done.19.one_far
  53.8 2.3 %project_down.1 = (bf16[2,2048]{1,0:T(2,128)(2,1)S(1)}, bf16[2,2048]{1,0:T(2,128)(2,1)S(1)}, bf16[2,2048]{1,0:T(2,128)(2,1)S(1)}, bf16[2,2048]{1,0:T(2,128)(2,1)S(1)}) custom-call(bf16[8,3712]{1,0:T(8,128)(2,1)S(1)} %pair_sum.2.one_near, bf16[8,3712]{1,0:T(8,128)(2,1)S(1)} %collective-permute-done.19.one_far, bf16[8,3584]{1,0:T(8,128)(2,1)S(1)} %pair_sum.3.two_near, ...), custom_call_target="tpu_custom_call" | custom-call | tf_op jit(solution)/shard_map/project_down/pallas_call | solution.py:604
  56.0 1.9 %collective-permute-start.22 = (bf16[2,2048]{1,0:T(2,128)(2,1)S(1)}, bf16[2,2048]{1,0:T(2,128)(2,1)S(1)}, u32[]{:S(2)}, u32[]{:S(2)}) collective-permute-start(bf16[2,2048]{1,0:T(2,128)(2,1)S(1)} %get-tuple-element.77), channel_id=1, source_target_pairs={{0,12},{1,13},{2,14},{3,15},{4,8},{5,9},{6,10},{7,11},{8,4},{9,5},... | collective-permute-start | bytes 24584 | tf_op jit(solution)/shard_map/ppermute | solution.py:50
  58.0 1.1 %collective-permute-start.23 = (bf16[2,2048]{1,0:T(2,128)(2,1)S(1)}, bf16[2,2048]{1,0:T(2,128)(2,1)S(1)}, u32[]{:S(2)}, u32[]{:S(2)}) collective-permute-start(bf16[2,2048]{1,0:T(2,128)(2,1)S(1)} %get-tuple-element.78), channel_id=1, source_target_pairs={{0,8},{1,9},{2,10},{3,11},{4,12},{5,13},{6,14},{7,15},{8,0},{9,1},... | collective-permute-start | bytes 24584 | tf_op jit(solution)/shard_map/ppermute | solution.py:50
  59.0 1.5 %collective-permute-start.24 = (bf16[2,2048]{1,0:T(2,128)(2,1)S(1)}, bf16[2,2048]{1,0:T(2,128)(2,1)S(1)}, u32[]{:S(2)}, u32[]{:S(2)}) collective-permute-start(bf16[2,2048]{1,0:T(2,128)(2,1)S(1)} %get-tuple-element.79), channel_id=1, source_target_pairs={{0,4},{1,5},{2,6},{3,7},{4,0},{5,1},{6,2},{7,3},{8,12},{9,13},{10,... | collective-permute-start | bytes 24584 | tf_op jit(solution)/shard_map/ppermute | solution.py:50
  60.5 1.1 %collective-permute-done.22.refs_0_ = bf16[2,2048]{1,0:T(2,128)(2,1)S(1)} collective-permute-done((bf16[2,2048]{1,0:T(2,128)(2,1)S(1)}, bf16[2,2048]{1,0:T(2,128)(2,1)S(1)}, u32[]{:S(2)}, u32[]{:S(2)}) %collective-permute-start.22) | collective-permute-done | bytes 8224 | tf_op jit(solution)/shard_map/ppermute | solution.py:50
  61.6 1.0 %collective-permute-done.23.refs_1_ = bf16[2,2048]{1,0:T(2,128)(2,1)S(1)} collective-permute-done((bf16[2,2048]{1,0:T(2,128)(2,1)S(1)}, bf16[2,2048]{1,0:T(2,128)(2,1)S(1)}, u32[]{:S(2)}, u32[]{:S(2)}) %collective-permute-start.23) | collective-permute-done | bytes 8224 | tf_op jit(solution)/shard_map/ppermute | solution.py:50
  62.6 0.1 collective-permute-done.24.refs_2_
  62.7 0.6 finish.1
  (36 shorter events, 0.1 us)
Async XLA Ops:
  0.0 8.8 %collective-permute-start = (bf16[2,2048]{1,0:T(2,128)(2,1)}, bf16[2,2048]{1,0:T(2,128)(2,1)S(1)}, u32[]{:S(2)}, u32[]{:S(2)}) collective-permute-start(bf16[2,2048]{1,0:T(2,128)(2,1)} %refs_5_.1), channel_id=1, source_target_pairs={{0,12},{4,8},{8,4},{12,0},{1,13},{5,9},{9,5},{13,1},{2,14},{6,10},... | collective-permute-start | bytes 24584 | tf_op jit(solution)/shard_map/ppermute | solution.py:31
  5.0 4.8 %collective-permute-start.1 = (bf16[2,2048]{1,0:T(2,128)(2,1)}, bf16[2,2048]{1,0:T(2,128)(2,1)S(1)}, u32[]{:S(2)}, u32[]{:S(2)}) collective-permute-start(bf16[2,2048]{1,0:T(2,128)(2,1)} %refs_5_.1), channel_id=1, source_target_pairs={{0,8},{4,12},{8,0},{12,4},{1,9},{5,13},{9,1},{13,5},{2,10},{6,14},... | collective-permute-start | bytes 24584 | tf_op jit(solution)/shard_map/ppermute | solution.py:31
  5.1 4.8 %collective-permute-start.2 = (bf16[2,2048]{1,0:T(2,128)(2,1)}, bf16[2,2048]{1,0:T(2,128)(2,1)S(1)}, u32[]{:S(2)}, u32[]{:S(2)}) collective-permute-start(bf16[2,2048]{1,0:T(2,128)(2,1)} %refs_5_.1), channel_id=1, source_target_pairs={{0,4},{4,0},{8,12},{12,8},{1,5},{5,1},{9,13},{13,9},{2,6},{6,2},{1... | collective-permute-start | bytes 24584 | tf_op jit(solution)/shard_map/ppermute | solution.py:31
  5.6 8.3 %copy-start = (s32[8]{0:T(128)S(1)}, s32[8]{0:T(128)}, u32[]{:S(2)}) copy-start(s32[8]{0:T(128)} %param.23) | copy-start | bytes 100
  5.6 23.3 %slice-start = ((s8[14680064]{0:T(1024)(128)(4,1)}), s8[4194304]{0:T(1024)(128)(4,1)S(1)}, s32[]{:S(2)}) async-start(s8[14680064]{0:T(1024)(128)(4,1)} %bitcast.4), calls=%async_computation | async-start | bytes 8388608
  9.8 19.1 %slice-start.1 = ((s8[14680064]{0:T(1024)(128)(4,1)}), s8[4194304]{0:T(1024)(128)(4,1)S(1)}, s32[]{:S(2)}) async-start(s8[14680064]{0:T(1024)(128)(4,1)} %bitcast.4), calls=%async_computation.1 | async-start | bytes 8388608
  9.8 26.0 %slice-start.4 = ((s8[14680064]{0:T(1024)(128)(4,1)}), s8[4194304]{0:T(1024)(128)(4,1)S(1)}, s32[]{:S(2)}) async-start(s8[14680064]{0:T(1024)(128)(4,1)} %bitcast.6), calls=%async_computation.4 | async-start | bytes 8388608
  10.6 5.0 %collective-permute-start.3 = (bf16[2,1408]{1,0:T(2,128)(2,1)S(1)}, bf16[2,1408]{1,0:T(2,128)(2,1)S(1)}, u32[]{:S(2)}, u32[]{:S(2)}) collective-permute-start(bf16[2,1408]{1,0:T(2,128)(2,1)S(1)} %get-tuple-element.51), channel_id=1, source_target_pairs={{0,13},{1,12},{2,15},{3,14},{4,9},{5,8},{6,11},{7,10},{8,5},{9,4},... | collective-permute-start | bytes 16904 | tf_op jit(solution)/shard_map/ppermute | solution.py:50
  12.1 3.9 %collective-permute-start.4 = (bf16[2,1408]{1,0:T(2,128)(2,1)S(1)}, bf16[2,1408]{1,0:T(2,128)(2,1)S(1)}, u32[]{:S(2)}, u32[]{:S(2)}) collective-permute-start(bf16[2,1408]{1,0:T(2,128)(2,1)S(1)} %get-tuple-element.52), channel_id=1, source_target_pairs={{0,9},{1,8},{2,11},{3,10},{4,13},{5,12},{6,15},{7,14},{8,1},{9,0},... | collective-permute-start | bytes 16904 | tf_op jit(solution)/shard_map/ppermute | solution.py:50
  12.4 3.7 %collective-permute-start.5 = (bf16[2,1408]{1,0:T(2,128)(2,1)S(1)}, bf16[2,1408]{1,0:T(2,128)(2,1)S(1)}, u32[]{:S(2)}, u32[]{:S(2)}) collective-permute-start(bf16[2,1408]{1,0:T(2,128)(2,1)S(1)} %get-tuple-element.53), channel_id=1, source_target_pairs={{0,5},{1,4},{2,7},{3,6},{4,1},{5,0},{6,3},{7,2},{8,13},{9,12},{10,... | collective-permute-start | bytes 16904 | tf_op jit(solution)/shard_map/ppermute | solution.py:50
  16.1 5.2 %collective-permute-start.6 = (bf16[8,1408]{1,0:T(8,128)(2,1)S(1)}, bf16[8,1408]{1,0:T(8,128)(2,1)S(1)}, u32[]{:S(2)}, u32[]{:S(2)}) collective-permute-start(bf16[8,1408]{1,0:T(8,128)(2,1)S(1)} %stack.1.refs_1_.refs_0_), channel_id=1, source_target_pairs={{0,3},{1,2},{2,1},{3,0},{4,7},{5,6},{6,5},{7,4},{8,11},{9,10},{10,... | collective-permute-start | bytes 67592 | tf_op jit(solution)/shard_map/ppermute | solution.py:31
  18.8 3.8 %collective-permute-start.7 = (bf16[8,1408]{1,0:T(8,128)(2,1)S(1)}, bf16[8,1408]{1,0:T(8,128)(2,1)S(1)}, u32[]{:S(2)}, u32[]{:S(2)}) collective-permute-start(bf16[8,1408]{1,0:T(8,128)(2,1)S(1)} %stack.1.refs_1_.refs_0_), channel_id=1, source_target_pairs={{0,2},{1,3},{2,0},{3,1},{4,6},{5,7},{6,4},{7,5},{8,10},{9,11},{10,... | collective-permute-start | bytes 67592 | tf_op jit(solution)/shard_map/ppermute | solution.py:31
  19.3 3.3 %collective-permute-start.8 = (bf16[8,1408]{1,0:T(8,128)(2,1)S(1)}, bf16[8,1408]{1,0:T(8,128)(2,1)S(1)}, u32[]{:S(2)}, u32[]{:S(2)}) collective-permute-start(bf16[8,1408]{1,0:T(8,128)(2,1)S(1)} %stack.1.refs_1_.refs_0_), channel_id=1, source_target_pairs={{0,1},{1,0},{2,3},{3,2},{4,5},{5,4},{6,7},{7,6},{8,9},{9,8},{10,11... | collective-permute-start | bytes 67592 | tf_op jit(solution)/shard_map/ppermute | solution.py:31
  19.4 9.5 %slice-start.2 = ((s8[14680064]{0:T(1024)(128)(4,1)}), s8[4194304]{0:T(1024)(128)(4,1)S(1)}, s32[]{:S(2)}) async-start(s8[14680064]{0:T(1024)(128)(4,1)} %bitcast.4), calls=%async_computation.2 | async-start | bytes 8388608
  19.4 16.4 %slice-start.5 = ((s8[14680064]{0:T(1024)(128)(4,1)}), s8[4194304]{0:T(1024)(128)(4,1)S(1)}, s32[]{:S(2)}) async-start(s8[14680064]{0:T(1024)(128)(4,1)} %bitcast.6), calls=%async_computation.5 | async-start | bytes 8388608
  24.4 4.5 %slice-start.3 = ((s8[14680064]{0:T(1024)(128)(4,1)}), s8[2097152]{0:T(1024)(128)(4,1)S(1)}, s32[]{:S(2)}) async-start(s8[14680064]{0:T(1024)(128)(4,1)} %bitcast.4), calls=%async_computation.3 | async-start | bytes 4194304
  24.4 11.4 %slice-start.6 = ((s8[14680064]{0:T(1024)(128)(4,1)}), s8[4194304]{0:T(1024)(128)(4,1)S(1)}, s32[]{:S(2)}) async-start(s8[14680064]{0:T(1024)(128)(4,1)} %bitcast.6), calls=%async_computation.6 | async-start | bytes 8388608
  24.4 4.4 %collective-permute-start.10 = (bf16[80,128]{1,0:T(8,128)(2,1)S(1)}, bf16[80,128]{1,0:T(8,128)(2,1)S(1)}, u32[]{:S(2)}, u32[]{:S(2)}) collective-permute-start(bf16[80,128]{1,0:T(8,128)(2,1)S(1)} %attend.1.refs_1_.refs_3_), channel_id=1, source_target_pairs={{0,2},{1,3},{2,0},{3,1},{4,6},{5,7},{6,4},{7,5},{8,10},{9,11},{10,... | collective-permute-start | bytes 61448 | tf_op jit(solution)/shard_map/ppermute | solution.py:31
  25.0 3.9 %collective-permute-start.11 = (bf16[80,128]{1,0:T(8,128)(2,1)S(1)}, bf16[80,128]{1,0:T(8,128)(2,1)S(1)}, u32[]{:S(2)}, u32[]{:S(2)}) collective-permute-start(bf16[80,128]{1,0:T(8,128)(2,1)S(1)} %attend.1.refs_1_.refs_3_), channel_id=1, source_target_pairs={{0,1},{1,0},{2,3},{3,2},{4,5},{5,4},{6,7},{7,6},{8,9},{9,8},{10,11... | collective-permute-start | bytes 61448 | tf_op jit(solution)/shard_map/ppermute | solution.py:31
  25.0 3.9 %collective-permute-start.9 = (bf16[80,128]{1,0:T(8,128)(2,1)S(1)}, bf16[80,128]{1,0:T(8,128)(2,1)S(1)}, u32[]{:S(2)}, u32[]{:S(2)}) collective-permute-start(bf16[80,128]{1,0:T(8,128)(2,1)S(1)} %attend.1.refs_1_.refs_3_), channel_id=1, source_target_pairs={{0,3},{1,2},{2,1},{3,0},{4,7},{5,6},{6,5},{7,4},{8,11},{9,10},{10,... | collective-permute-start | bytes 61448 | tf_op jit(solution)/shard_map/ppermute | solution.py:31
  28.9 7.0 %slice-start.7 = ((s8[14680064]{0:T(1024)(128)(4,1)}), s8[2097152]{0:T(1024)(128)(4,1)S(1)}, s32[]{:S(2)}) async-start(s8[14680064]{0:T(1024)(128)(4,1)} %bitcast.6), calls=%async_computation.7 | async-start | bytes 4194304
  29.8 4.8 %collective-permute-start.13 = (bf16[2,1024]{1,0:T(2,128)(2,1)S(1)}, bf16[2,1024]{1,0:T(2,128)(2,1)S(1)}, u32[]{:S(2)}, u32[]{:S(2)}) collective-permute-start(bf16[2,1024]{1,0:T(2,128)(2,1)S(1)} %get-tuple-element.69), channel_id=1, source_target_pairs={{0,5},{1,12},{2,7},{3,14},{4,1},{5,8},{6,3},{7,10},{8,13},{9,4},{1... | collective-permute-start | bytes 12296 | tf_op jit(solution)/shard_map/ppermute | solution.py:61
  29.8 4.8 %collective-permute-start.12 = (bf16[2,1024]{1,0:T(2,128)(2,1)S(1)}, bf16[2,1024]{1,0:T(2,128)(2,1)S(1)}, u32[]{:S(2)}, u32[]{:S(2)}) collective-permute-start(bf16[2,1024]{1,0:T(2,128)(2,1)S(1)} %get-tuple-element.68), channel_id=1, source_target_pairs={{0,9},{1,8},{2,11},{3,10},{4,13},{5,12},{6,15},{7,14},{8,1},{9,0},... | collective-permute-start | bytes 12296 | tf_op jit(solution)/shard_map/ppermute | solution.py:61
  34.6 1.2 %collective-permute-start.14 = (bf16[2,1024]{1,0:T(2,128)(2,1)S(1)}, bf16[2,1024]{1,0:T(2,128)(2,1)S(1)}, u32[]{:S(2)}, u32[]{:S(2)}) collective-permute-start(bf16[2,1024]{1,0:T(2,128)(2,1)S(1)} %collective-permute-done.13.refs_1_), channel_id=1, source_target_pairs={{0,1},{1,0},{2,3},{3,2},{4,5},{5,4},{6,7},{7,6},{8,9},{9,8},{10,11... | collective-permute-start | bytes 12296 | tf_op jit(solution)/shard_map/ppermute | solution.py:31
  36.8 5.8 %collective-permute-start.15 = (bf16[8,2048]{1,0:T(8,128)(2,1)S(1)}, bf16[8,2048]{1,0:T(8,128)(2,1)S(1)}, u32[]{:S(2)}, u32[]{:S(2)}) collective-permute-start(bf16[8,2048]{1,0:T(8,128)(2,1)S(1)} %get-tuple-element.70), channel_id=1, source_target_pairs={{0,12},{1,13},{2,14},{3,15},{4,8},{5,9},{6,10},{7,11},{8,4},{9,5},... | collective-permute-start | bytes 98312 | tf_op jit(solution)/shard_map/ppermute | solution.py:50
  38.8 4.9 %collective-permute-start.16 = (bf16[8,2048]{1,0:T(8,128)(2,1)S(1)}, bf16[8,2048]{1,0:T(8,128)(2,1)S(1)}, u32[]{:S(2)}, u32[]{:S(2)}) collective-permute-start(bf16[8,2048]{1,0:T(8,128)(2,1)S(1)} %get-tuple-element.71), channel_id=1, source_target_pairs={{0,8},{1,9},{2,10},{3,11},{4,12},{5,13},{6,14},{7,15},{8,0},{9,1},... | collective-permute-start | bytes 98312 | tf_op jit(solution)/shard_map/ppermute | solution.py:50
  38.8 4.9 %collective-permute-start.17 = (bf16[8,2048]{1,0:T(8,128)(2,1)S(1)}, bf16[8,2048]{1,0:T(8,128)(2,1)S(1)}, u32[]{:S(2)}, u32[]{:S(2)}) collective-permute-start(bf16[8,2048]{1,0:T(8,128)(2,1)S(1)} %get-tuple-element.72), channel_id=1, source_target_pairs={{0,4},{1,5},{2,6},{3,7},{4,0},{5,1},{6,2},{7,3},{8,12},{9,13},{10,... | collective-permute-start | bytes 98312 | tf_op jit(solution)/shard_map/ppermute | solution.py:50
  45.7 2.6 %collective-permute-start.18 = (bf16[8,3712]{1,0:T(8,128)(2,1)S(1)}, bf16[8,3712]{1,0:T(8,128)(2,1)S(1)}, u32[]{:S(2)}, u32[]{:S(2)}) collective-permute-start(bf16[8,3712]{1,0:T(8,128)(2,1)S(1)} %get-tuple-element.75.first_ref), channel_id=1, source_target_pairs={{0,1},{1,0},{2,3},{3,2},{4,5},{5,4},{6,7},{7,6},{8,9},{9,8},{10,11... | collective-permute-start | bytes 178184 | tf_op jit(solution)/shard_map/ppermute | solution.py:31
  45.7 8.1 %slice-start.8 = ((s8[14680064]{0:T(1024)(128)(4,1)}), s8[4194304]{0:T(1024)(128)(4,1)S(1)}, s32[]{:S(2)}) async-start(s8[14680064]{0:T(1024)(128)(4,1)} %bitcast.8), calls=%async_computation.8 | async-start | bytes 8388608
  45.7 8.1 %slice-start.9 = ((s8[14680064]{0:T(1024)(128)(4,1)}), s8[4194304]{0:T(1024)(128)(4,1)S(1)}, s32[]{:S(2)}) async-start(s8[14680064]{0:T(1024)(128)(4,1)} %bitcast.8), calls=%async_computation.9 | async-start | bytes 8388608
  45.7 8.1 %slice-start.10 = ((s8[14680064]{0:T(1024)(128)(4,1)}), s8[4194304]{0:T(1024)(128)(4,1)S(1)}, s32[]{:S(2)}) async-start(s8[14680064]{0:T(1024)(128)(4,1)} %bitcast.8), calls=%async_computation.10 | async-start | bytes 8388608
  45.7 8.1 %slice-start.11 = ((s8[14680064]{0:T(1024)(128)(4,1)}), s8[2097152]{0:T(1024)(128)(4,1)S(1)}, s32[]{:S(2)}) async-start(s8[14680064]{0:T(1024)(128)(4,1)} %bitcast.8), calls=%async_computation.11 | async-start | bytes 4194304
  47.7 1.4 %collective-permute-start.20 = (bf16[8,3584]{1,0:T(8,128)(2,1)S(1)}, bf16[8,3584]{1,0:T(8,128)(2,1)S(1)}, u32[]{:S(2)}, u32[]{:S(2)}) collective-permute-start(bf16[8,3584]{1,0:T(8,128)(2,1)S(1)} %second_gate_up.1.first_ref), channel_id=1, source_target_pairs={{0,1},{1,0},{2,3},{3,2},{4,5},{5,4},{6,7},{7,6},{8,9},{9,8},{10,11... | collective-permute-start | bytes 172040 | tf_op jit(solution)/shard_map/ppermute | solution.py:31
  48.2 5.5 %collective-permute-start.19 = (bf16[8,3712]{1,0:T(8,128)(2,1)S(1)}, bf16[8,3712]{1,0:T(8,128)(2,1)S(1)}, u32[]{:S(2)}, u32[]{:S(2)}) collective-permute-start(bf16[8,3712]{1,0:T(8,128)(2,1)S(1)} %pair_sum.2.one_near), channel_id=1, source_target_pairs={{0,2},{1,3},{2,0},{3,1},{4,6},{5,7},{6,4},{7,5},{8,10},{9,11},{10,... | collective-permute-start | bytes 178184 | tf_op jit(solution)/shard_map/ppermute | solution.py:31
  49.1 4.6 %collective-permute-start.21 = (bf16[8,3584]{1,0:T(8,128)(2,1)S(1)}, bf16[8,3584]{1,0:T(8,128)(2,1)S(1)}, u32[]{:S(2)}, u32[]{:S(2)}) collective-permute-start(bf16[8,3584]{1,0:T(8,128)(2,1)S(1)} %pair_sum.3.two_near), channel_id=1, source_target_pairs={{0,2},{1,3},{2,0},{3,1},{4,6},{5,7},{6,4},{7,5},{8,10},{9,11},{10,... | collective-permute-start | bytes 172040 | tf_op jit(solution)/shard_map/ppermute | solution.py:31
  56.0 5.5 %collective-permute-start.22 = (bf16[2,2048]{1,0:T(2,128)(2,1)S(1)}, bf16[2,2048]{1,0:T(2,128)(2,1)S(1)}, u32[]{:S(2)}, u32[]{:S(2)}) collective-permute-start(bf16[2,2048]{1,0:T(2,128)(2,1)S(1)} %get-tuple-element.77), channel_id=1, source_target_pairs={{0,12},{1,13},{2,14},{3,15},{4,8},{5,9},{6,10},{7,11},{8,4},{9,5},... | collective-permute-start | bytes 24584 | tf_op jit(solution)/shard_map/ppermute | solution.py:50
  58.0 4.6 %collective-permute-start.23 = (bf16[2,2048]{1,0:T(2,128)(2,1)S(1)}, bf16[2,2048]{1,0:T(2,128)(2,1)S(1)}, u32[]{:S(2)}, u32[]{:S(2)}) collective-permute-start(bf16[2,2048]{1,0:T(2,128)(2,1)S(1)} %get-tuple-element.78), channel_id=1, source_target_pairs={{0,8},{1,9},{2,10},{3,11},{4,12},{5,13},{6,14},{7,15},{8,0},{9,1},... | collective-permute-start | bytes 24584 | tf_op jit(solution)/shard_map/ppermute | solution.py:50
  59.0 3.7 %collective-permute-start.24 = (bf16[2,2048]{1,0:T(2,128)(2,1)S(1)}, bf16[2,2048]{1,0:T(2,128)(2,1)S(1)}, u32[]{:S(2)}, u32[]{:S(2)}) collective-permute-start(bf16[2,2048]{1,0:T(2,128)(2,1)S(1)} %get-tuple-element.79), channel_id=1, source_target_pairs={{0,4},{1,5},{2,6},{3,7},{4,0},{5,1},{6,2},{7,3},{8,12},{9,13},{10,... | collective-permute-start | bytes 24584 | tf_op jit(solution)/shard_map/ppermute | solution.py:50

commit v14 on v12

--- a/solution.py
+++ b/solution.py
@@ -15,7 +15,7 @@
 GROUP = HEADS // KV_HEADS
 LANES = 128
 MIB = 2**20
-COPIES = 4
+COPIES = 1
 STATS = 8
 
 epsilon = 1e-05
@@ -109,9 +109,8 @@
     return out
 
 
-def squares_block(total):
-    lanes = lax.broadcasted_iota(jnp.int32, (total.shape[0], LANES), 1)
-    return spread(three_parts(total), lanes, lax.axis_index("inner") * 4)
+def squares_block(total, lanes):
+    return spread(three_parts(total), lanes, 0)
 
 
 def copies_of(source, start, target, sems):
@@ -169,7 +168,7 @@
         ref[...] = source[n * rows : (n + 1) * rows, :].astype(ref.dtype)
 
 
-def qkv_kernel(slots, gain_ref, wq_ref, wkv_ref, *refs):
+def qkv_kernel(slots, lanes_ref, gain_ref, wq_ref, wkv_ref, *refs):
     rows_ref = refs[slots]
     out_s, rows_s = refs[-2:]
     wide = join_rows(refs[:slots][::-1], rows_s)
@@ -187,11 +186,11 @@
     out_s[:, query_cols : query_cols + kv_cols] = jnp.dot(
         scaled, wkv_ref[...], preferred_element_type=jnp.float32
     )
-    out_s[:, query_cols + kv_cols :] = squares_block(total)
+    out_s[:, query_cols + kv_cols :] = squares_block(total, lanes_ref[...])
     part_rows(out_s, refs[slots + 1 : 2 * slots + 1])
 
 
-def project_qkv(rows, gain, w_query, w_kv):
+def project_qkv(lanes, rows, gain, w_query, w_kv):
     slots = len(rows)
     own_rows, depth = rows[0].shape
     columns = w_query.shape[1] + w_kv.shape[1] + LANES
@@ -201,7 +200,7 @@
             jax.ShapeDtypeStruct((own_rows * slots, depth), jnp.float32),
             *[jax.ShapeDtypeStruct((own_rows, columns), jnp.bfloat16)] * slots,
         ),
-        in_specs=[in_vmem] * (3 + slots),
+        in_specs=[in_vmem] * (4 + slots),
         out_specs=(in_vmem,) * (1 + slots),
         scratch_shapes=[
             pltpu.VMEM((own_rows * slots, columns), jnp.float32),
@@ -209,7 +208,7 @@
         ],
         compiler_params=params(2),
         name="project_qkv",
-    )(gain, resident(w_query), resident(w_kv), *rows[::-1])
+    )(lanes, gain, resident(w_query), resident(w_kv), *rows[::-1])
 
 
 def stack_kernel(*refs):
@@ -232,7 +231,8 @@
 def attend_kernel(
     slots,
     shards,
-    lengths_ref,
+    marks_ref,
+    kv_head_ref,
     cosine_ref,
     sine_ref,
     key_ref,
@@ -247,8 +247,6 @@
     query_cols = here * HEAD_DIM
     kv_cols = 2 * KV_HEADS * HEAD_DIM // slots
     columns = query_cols + kv_cols
-    tensor_index = lax.axis_index("tensor")
-    inner_index = lax.axis_index("inner")
     positions = key_ref.shape[1] // KV_HEADS
 
     joined = functools.reduce(jnp.add, [ref[...].astype(jnp.float32) for ref in parts])
@@ -268,10 +266,14 @@
     for j in range(here):
         block = rotate(joined[:, j * HEAD_DIM : (j + 1) * HEAD_DIM])
         query_s[j * all_rows : (j + 1) * all_rows, :] = block
-    for s in range(slots):
-        kv_s[s] = joined[s * own_rows : (s + 1) * own_rows, query_cols:]
+    block = joined[:, query_cols:]
+    for n in range(slots.bit_length() - 1):
+        bit = marks_ref[own_rows + 1 + n : own_rows + 2 + n, 0:1]
+        block = jnp.where(bit != 0, turned(block, 1 << n, own_rows), block)
+    kv_s[...] = block
     for d in range(slots):
-        kv_wide_s[:, d * kv_cols : (d + 1) * kv_cols] = kv_s[d ^ tensor_index]
+        rows = kv_s[d * own_rows : (d + 1) * own_rows, :]
+        kv_wide_s[:, d * kv_cols : (d + 1) * kv_cols] = rows
     new_keys = []
     new_values = []
     for g in range(KV_HEADS):
@@ -281,11 +283,9 @@
         new_values.append(block.astype(jnp.bfloat16).astype(jnp.float32))
 
     score_scale = HEAD_DIM ** (-0.5)
-    row = lax.broadcasted_iota(jnp.int32, (HEADS, 1), 0)
-    head = ((row % slots) ^ tensor_index) * here + row // slots
-    kv_head = head // GROUP
+    kv_head = kv_head_ref[:, 0:1]
     column = lax.broadcasted_iota(jnp.int32, (1, positions * KV_HEADS), 1)
-    place = column // KV_HEADS + inner_index * positions
+    place = column // KV_HEADS
     column_head = column % KV_HEADS
     lanes = lax.broadcasted_iota(jnp.int32, (HEADS, LANES), 1)
     for r in range(own_rows):
@@ -299,7 +299,7 @@
             )
             * score_scale
         )
-        used = jnp.where(place < lengths_ref[r : r + 1, 0:1], column_head, -1)
+        used = jnp.where(place < marks_ref[r : r + 1, 0:1], column_head, -1)
         masked = jnp.where(used == kv_head, scores, -1e30)
         key_rows = 0.0
         value_rows = 0.0
@@ -309,7 +309,7 @@
         new_score = (
             jnp.sum(queries.astype(jnp.float32) * key_rows, axis=1, keepdims=True) * score_scale
         )
-        new_score = jnp.where(inner_index == 0, new_score, -1e30)
+        new_score = jnp.where(marks_ref[own_rows : own_rows + 1, 0:1] != 0, new_score, -1e30)
         peak = jnp.maximum(jnp.max(masked, axis=1, keepdims=True), new_score)
         weights = jnp.exp(masked - peak)
         new_weight = jnp.exp(new_score - peak)
@@ -334,7 +334,7 @@
     out_ref[heads:, :] = packed.astype(jnp.bfloat16)
 
 
-def attend(lengths, cosine, sine, parts, keys, values, later, slots):
+def attend(marks, kv_head, cosine, sine, parts, keys, values, later, slots):
     own_rows = parts[0].shape[0] // slots
     kv_cols = 2 * KV_HEADS * HEAD_DIM // slots
     return pl.pallas_call(
@@ -342,18 +342,18 @@
         out_shape=jax.ShapeDtypeStruct(
             (own_rows * HEADS + max(16, own_rows * slots), HEAD_DIM), jnp.bfloat16
         ),
-        in_specs=[in_vmem] * (5 + len(parts)) + [in_place] * len(later),
+        in_specs=[in_vmem] * (6 + len(parts)) + [in_place] * len(later),
         out_specs=in_vmem,
         scratch_shapes=[
             pltpu.VMEM((own_rows * HEADS, HEAD_DIM), jnp.float32),
-            pltpu.VMEM((slots, own_rows, kv_cols), jnp.float32),
+            pltpu.VMEM((slots * own_rows, kv_cols), jnp.float32),
             pltpu.VMEM((own_rows, slots * kv_cols), jnp.float32),
             pltpu.VMEM((own_rows * HEADS, HEAD_DIM), jnp.float32),
             pltpu.VMEM((own_rows * HEADS, LANES), jnp.float32),
         ],
         compiler_params=params(6),
         name="attend",
-    )(lengths, cosine, sine, resident(keys), resident(values), *parts[::-1], *[resident(w) for w in later])
+    )(marks, kv_head, cosine, sine, resident(keys), resident(values), *parts[::-1], *[resident(w) for w in later])
 
 
 def combine_kernel(shards, slots, *refs):
@@ -468,7 +468,7 @@
     product_tiles(scaled, up_ref, store(count), first, count)
 
 
-def first_gate_up_kernel(slots, count, rows_ref, gain_ref, gate_ref, up_ref, *refs):
+def first_gate_up_kernel(slots, count, lanes_ref, rows_ref, gain_ref, gate_ref, up_ref, *refs):
     parts = refs[:slots]
     out_ref, updated_ref, scaled_ref = refs[-3:]
     own_rows = updated_ref.shape[0]
@@ -477,13 +477,13 @@
     wide = updated.astype(jnp.float32)
     updated_ref[...] = wide[:own_rows]
     squares = jnp.sum(wide * wide, axis=1, keepdims=True)
-    out_ref[:, 2 * count :] = squares_block(squares).astype(jnp.bfloat16)
+    out_ref[:, 2 * count :] = squares_block(squares, lanes_ref[...]).astype(jnp.bfloat16)
     scaled = (wide * gain_ref[...].astype(jnp.float32)[None, :]).astype(jnp.bfloat16)
     scaled_ref[...] = scaled
     gate_up_tiles(scaled, gate_ref, up_ref, out_ref, 0, count)
 
 
-def first_gate_up(rows, gain, parts, w_gate, w_up, later, count, own_rows):
+def first_gate_up(lanes, rows, gain, parts, w_gate, w_up, later, count, own_rows):
     slots = len(parts)
     return pl.pallas_call(
         functools.partial(first_gate_up_kernel, slots, count),
@@ -492,12 +492,12 @@
             jax.ShapeDtypeStruct((own_rows, rows.shape[1]), jnp.float32),
             jax.ShapeDtypeStruct(rows.shape, jnp.bfloat16),
         ),
-        in_specs=[in_vmem] * (4 + slots) + [in_place] * len(later),
+        in_specs=[in_vmem] * (5 + slots) + [in_place] * len(later),
         out_specs=(in_vmem,) * 3,
         compiler_params=params(3),
         cost_estimate=product_cost(w_gate.shape[0], 2 * count),
         name="first_gate_up",
-    )(rows, gain, resident(w_gate), resident(w_up), *parts[::-1], *[resident(w) for w in later])
+    )(lanes, rows, gain, resident(w_gate), resident(w_up), *parts[::-1], *[resident(w) for w in later])
 
 
 def second_gate_up_kernel(first, count, scaled_ref, gate_ref, up_ref, *refs):
@@ -578,6 +578,17 @@
         compiler_params=params(1),
         name="finish",
     )(updated, *parts[::-1])
+
+
+def attend_tables(lengths, tensor_index, inner_index, slots, positions):
+    bits = [(tensor_index >> n) & 1 for n in range(slots.bit_length() - 1)]
+    marks = jnp.concatenate(
+        [lengths - inner_index * positions, jnp.stack([(inner_index == 0).astype(jnp.int32), *bits])]
+    )
+    row = jnp.arange(HEADS)
+    head = ((row % slots) ^ tensor_index) * (HEADS // slots) + row // slots
+    wide = lambda column: jnp.broadcast_to(column[:, None], (column.shape[0], LANES))
+    return wide(marks.astype(jnp.int32)), wide((head // GROUP).astype(jnp.int32))
 
 
 def rotation_tables(positions, repeats):
@@ -608,26 +619,28 @@
 ):
     tensor_index = lax.axis_index("tensor")
     slots = lax.axis_size("tensor")
+    inner_index = lax.axis_index("inner")
     own_rows = states.shape[0]
     all_rows = own_rows * slots
 
     got = exchange(states, "tensor")
-    own, attn_gain, ffn_gain, w_kv, w_query = load(
-        states, attn_gain, ffn_gain, w_kv, w_query, after=states
-    )
-    rows, *pieces = project_qkv([own] + got[1:], attn_gain, w_query, w_kv)
+    own, w_kv, w_query = load(states, w_kv, w_query, after=states)
+    lanes = lax.broadcasted_iota(jnp.int32, (all_rows, LANES), 1) - 4 * inner_index
+    rows, *pieces = project_qkv(lanes, [own] + got[1:], attn_gain, w_query, w_kv)
 
     rows, lengths = lax.optimization_barrier((rows, lengths))
     my_lengths = lax.dynamic_slice_in_dim(lengths, tensor_index * own_rows, own_rows, 0)
     cosine, sine = rotation_tables(my_lengths.astype(jnp.float32), slots)
-    my_lengths = jnp.broadcast_to(my_lengths[:, None], (own_rows, LANES))
+    marks, kv_head = attend_tables(
+        my_lengths, tensor_index, inner_index, slots, key_cache.shape[1]
+    )
     flat = (own_rows, key_cache.shape[1] * KV_HEADS, HEAD_DIM)
     (keys,) = load(key_cache.reshape(flat), after=rows)
     joined = stack(scatter_slots(pieces, 1))
     joined, keys = lax.optimization_barrier((joined, keys))
     (values,) = load(value_cache.reshape(flat), after=joined)
     parts, values = lax.optimization_barrier((exchange(joined, "inner")[::-1], values))
-    shard = attend(my_lengths, cosine, sine, parts, keys, values, [], slots)
+    shard = attend(marks, kv_head, cosine, sine, parts, keys, values, [], slots)
 
     (w_out,) = load(w_out, after=shard)
     shards, w_out = lax.optimization_barrier((exchange(shard, "inner")[::-1], w_out))
@@ -637,7 +650,7 @@
     tiles = w_gate.shape[1] // LANES
     first = (tiles + 1) // 2 * LANES
     one, updated, scaled = first_gate_up(
-        rows, ffn_gain, parts, w_gate, w_up, [], first, own_rows
+        lanes, rows, ffn_gain, parts, w_gate, w_up, [], first, own_rows
     )
     two = second_gate_up(scaled, w_gate, w_up, [], first)
     steps = steps_up(lax.axis_size("inner"))

time: 62.4 us -> 66.9 us (1.072)
  local copies, waits for them, and re-layouts: 0.15 us -> 4.37 us
  starting transfers between devices: 29.3 us -> 30.6 us
  waiting for transfers between devices: 13.1 us -> 12 us
    unnamed x26 -> x28, local copies, waits for them, and re-layouts: 0.08 us -> 4.22 us
    ppermute x13, waiting for transfers between devices: 6.02 us -> 4.76 us  [swap_with(): return lax.ppermute(value, axis, [(i, i ^ step) for i in range(count)])]
    ppermute x12, starting transfers between devices: 15.6 us -> 16.8 us  [scatter_slots(): got.append(lax.ppermute(pieces[k], ('tensor', 'inner'), pairs))]
  transfers between devices with their start and end apart: 25 -> 25, of which waited for: 11 -> 9; matrix products, arithmetic and copies ran while one was open for 0% -> 0% of each run, Pallas kernels for 17% -> 15%
where the time goes in v14:
time: 66.9 us; the launch traced here: 66.7 us
  starting transfers between devices  30.6 us (46%)
  Pallas kernels  19.2 us (29%)
  waiting for transfers between devices  12 us (18%)
  local copies, waits for them, and re-layouts  4.37 us (7%)
    ppermute x12, starting transfers between devices, scatter_slots(): got.append(lax.ppermute(pieces[k], ('tensor', 'inner'), pairs))  16.8 us
    ppermute x13, starting transfers between devices, swap_with(): return lax.ppermute(value, axis, [(i, i ^ step) for i in range(count)])  13.7 us
    pallas_call x4, Pallas kernels, load(): pl.pallas_call(functools.partial(load_kernel, spans), out_shape=tuple((pl...  8.25 us
    ppermute x12, waiting for transfers between devices, scatter_slots(): got.append(lax.ppermute(pieces[k], ('tensor', 'inner'), pairs))  7.22 us
    ppermute x13, waiting for transfers between devices, swap_with(): return lax.ppermute(value, axis, [(i, i ^ step) for i in range(count)])  4.76 us
    unnamed x28, local copies, waits for them, and re-layouts  4.22 us
    pallas_call x1, Pallas kernels, project_down(): pl.pallas_call(down_kernel, out_shape=(jax.ShapeDtypeStruct((rows // slot...  2.28 us
    pallas_call x1, Pallas kernels, first_gate_up(): pl.pallas_call(functools.partial(first_gate_up_kernel, slots, count), out...  2 us
  transfers between devices with their start and end apart: 25, of which 9 were waited for; matrix products, arithmetic and copies ran while one was open for 0% of the time, Pallas kernels for 15%

profile of v14, /device:TPU:0, one launch (start us, length us, event | category | flops | bytes accessed | tf_op | source)
XLA Modules:
  0.0 66.7 jit_solution(14318954712626603474)
XLA Ops:
  0.0 5.0 %collective-permute-start = (bf16[2,2048]{1,0:T(2,128)(2,1)}, bf16[2,2048]{1,0:T(2,128)(2,1)S(1)}, u32[]{:S(2)}, u32[]{:S(2)}) collective-permute-start(bf16[2,2048]{1,0:T(2,128)(2,1)} %refs_3_.1), channel_id=1, source_target_pairs={{0,12},{4,8},{8,4},{12,0},{1,13},{5,9},{9,5},{13,1},{2,14},{6,10},... | collective-permute-start | bytes 24584 | tf_op jit(solution)/shard_map/ppermute | solution.py:31
  5.1 0.0 collective-permute-start.1
  5.1 0.6 collective-permute-start.2
  5.7 0.0 copy-start.5
  5.7 0.0 slice-start
  5.8 2.7 %load.4 = (bf16[2,2048]{1,0:T(2,128)(2,1)S(1)}, bf16[2048,256]{1,0:T(8,128)(2,1)S(1)}, bf16[2048,1024]{1,0:T(8,128)(2,1)S(1)}) custom-call(bf16[2,2048]{1,0:T(2,128)(2,1)} %refs_3_.1, bf16[2048,256]{1,0:T(8,128)(2,1)} %refs_1_.1, bf16[2048,1024]{1,0:T(8,128)(2,1)} %refs_2_.1, bf16[2,2048]{1,0:T(2,128)(2,1)} %refs_3_.1), custom_call_target="tpu_custom_call" | custom-call | bytes 5251072 | tf_op jit(solution)/shard_map/load/pallas_call | solution.py:144
  8.5 2.0 %copy-done.1 = bf16[2048,1024]{1,0:T(8,128)(2,1)} copy-done((bf16[2048,1024]{1,0:T(8,128)(2,1)}, bf16[2048,1024]{1,0:T(8,128)(2,1)S(1)}, u32[]{:S(2)}) %copy-start.1) | copy-done | bytes 4194328
  10.4 0.0 collective-permute-done.refs_0_
  10.4 0.0 collective-permute-done.1.refs_1_
  10.4 0.0 collective-permute-done.2.refs_2_
  10.5 2.2 %copy-done.2 = bf16[2048,1024]{1,0:T(8,128)(2,1)S(1)} copy-done((bf16[2048,1024]{1,0:T(8,128)(2,1)S(1)}, bf16[2048,1024]{1,0:T(8,128)(2,1)}, u32[]{:S(2)}) %copy-start.2) | copy-done | bytes 4194328
  12.7 0.8 %project_qkv.1 = (f32[8,2048]{1,0:T(8,128)S(1)}, bf16[2,1408]{1,0:T(2,128)(2,1)S(1)}, bf16[2,1408]{1,0:T(2,128)(2,1)S(1)}, bf16[2,1408]{1,0:T(2,128)(2,1)S(1)}, bf16[2,1408]{1,0:T(2,128)(2,1)S(1)}) custom-call(s32[8,128]{1,0:T(8,128)S(1)} %iota.24.lanes_ref, bf16[2048]{0:T(1024)(128)(2,1)S(1)} %copy-done.3, bf16[2048,1024]{1,0:T(8,128)(2,1)S(1)} %copy-done.2, ...), custom_call_target="tpu_custom_call" | custom-call | tf_op jit(solution)/shard_map/project_qkv/pallas_call | solution.py:197
  13.5 2.4 %collective-permute-start.3 = (bf16[2,1408]{1,0:T(2,128)(2,1)S(1)}, bf16[2,1408]{1,0:T(2,128)(2,1)S(1)}, u32[]{:S(2)}, u32[]{:S(2)}) collective-permute-start(bf16[2,1408]{1,0:T(2,128)(2,1)S(1)} %get-tuple-element.48), channel_id=1, source_target_pairs={{0,13},{1,12},{2,15},{3,14},{4,9},{5,8},{6,11},{7,10},{8,5},{9,4},... | collective-permute-start | bytes 16904 | tf_op jit(solution)/shard_map/ppermute | solution.py:50
  15.9 0.2 collective-permute-start.4
  16.2 1.6 %collective-permute-start.5 = (bf16[2,1408]{1,0:T(2,128)(2,1)S(1)}, bf16[2,1408]{1,0:T(2,128)(2,1)S(1)}, u32[]{:S(2)}, u32[]{:S(2)}) collective-permute-start(bf16[2,1408]{1,0:T(2,128)(2,1)S(1)} %get-tuple-element.50), channel_id=1, source_target_pairs={{0,5},{1,4},{2,7},{3,6},{4,1},{5,0},{6,3},{7,2},{8,13},{9,12},{10,... | collective-permute-start | bytes 16904 | tf_op jit(solution)/shard_map/ppermute | solution.py:50
  17.7 0.1 dynamic-slice_convert_fusion
  17.8 0.1 fusion
  17.9 1.6 %load.5.key_ref = bf16[2,4096,128]{2,1,0:T(8,128)(2,1)S(1)} custom-call(bf16[2,4096,128]{2,1,0:T(8,128)(2,1)} %bitcast.13, f32[8,2048]{1,0:T(8,128)S(1)} %get-tuple-element.46.refs_1_.rows_ref), custom_call_target="tpu_custom_call" | custom-call | bytes 2097152 | tf_op jit(solution)/shard_map/load/pallas_call | solution.py:144
  19.5 0.0 collective-permute-done.3.refs_0_
  19.5 0.4 collective-permute-done.4.refs_1_
  19.9 2.7 %collective-permute-start.6 = (bf16[8,1408]{1,0:T(8,128)(2,1)S(1)}, bf16[8,1408]{1,0:T(8,128)(2,1)S(1)}, u32[]{:S(2)}, u32[]{:S(2)}) collective-permute-start(bf16[8,1408]{1,0:T(8,128)(2,1)S(1)} %stack.18.refs_1_.refs_0_), channel_id=1, source_target_pairs={{0,3},{1,2},{2,1},{3,0},{4,7},{5,6},{6,5},{7,4},{8,11},{9,10},{10,... | collective-permute-start | bytes 67592 | tf_op jit(solution)/shard_map/ppermute | solution.py:31
  22.6 0.5 collective-permute-start.7
  23.1 0.1 pad_add_fusion
  23.2 1.8 %load.6.value_ref = bf16[2,4096,128]{2,1,0:T(8,128)(2,1)S(1)} custom-call(bf16[2,4096,128]{2,1,0:T(8,128)(2,1)} %bitcast.14, bf16[8,1408]{1,0:T(8,128)(2,1)S(1)} %stack.18.refs_1_.refs_0_), custom_call_target="tpu_custom_call" | custom-call | bytes 2097152 | tf_op jit(solution)/shard_map/load/pallas_call | solution.py:144
  25.0 0.0 collective-permute-done.6.refs_3_
  25.0 1.4 %collective-permute-done.7.refs_2_ = bf16[8,1408]{1,0:T(8,128)(2,1)S(1)} collective-permute-done((bf16[8,1408]{1,0:T(8,128)(2,1)S(1)}, bf16[8,1408]{1,0:T(8,128)(2,1)S(1)}, u32[]{:S(2)}, u32[]{:S(2)}) %collective-permute-start.7) | collective-permute-done | bytes 22560 | tf_op jit(solution)/shard_map/ppermute | solution.py:31
  26.4 0.1 broadcast_in_dim.12.marks_ref
  26.5 0.1 broadcast_in_dim.13.kv_head_ref
  26.5 1.9 %attend.1.refs_1_.refs_3_ = bf16[80,128]{1,0:T(8,128)(2,1)S(1)} custom-call(s32[5,128]{1,0:T(8,128)S(1)} %broadcast_in_dim.12.marks_ref, s32[32,128]{1,0:T(8,128)S(1)} %broadcast_in_dim.13.kv_head_ref, f32[8,128]{1,0:T(8,128)S(1)} %bitcast.11, f32[8,128]{1,0:T(8,128)S(1)} %bitcast.12, bf16[2,4096,128]{2,1,0:T(8,128)(2,1)S(1)} %load.5.key_ref, ...), custom_call_target="tpu_custom_call" | custom-call | tf_op jit(solution)/shard_map/attend/pallas_call | solution.py:340
  28.5 0.6 collective-permute-start.10
  29.1 0.0 collective-permute-start.11
  29.1 1.6 %collective-permute-start.9 = (bf16[80,128]{1,0:T(8,128)(2,1)S(1)}, bf16[80,128]{1,0:T(8,128)(2,1)S(1)}, u32[]{:S(2)}, u32[]{:S(2)}) collective-permute-start(bf16[80,128]{1,0:T(8,128)(2,1)S(1)} %attend.1.refs_1_.refs_3_), channel_id=1, source_target_pairs={{0,3},{1,2},{2,1},{3,0},{4,7},{5,6},{6,5},{7,4},{8,11},{9,10},{10,... | collective-permute-start | bytes 61448 | tf_op jit(solution)/shard_map/ppermute | solution.py:31
  30.7 2.2 %load.7.weight_ref = bf16[1024,2048]{1,0:T(8,128)(2,1)S(1)} custom-call(bf16[1024,2048]{1,0:T(8,128)(2,1)} %refs_0_.3, bf16[80,128]{1,0:T(8,128)(2,1)S(1)} %attend.1.refs_1_.refs_3_), custom_call_target="tpu_custom_call" | custom-call | bytes 4194304 | tf_op jit(solution)/shard_map/load/pallas_call | solution.py:144
  32.9 0.0 copy-start
  32.9 0.0 collective-permute-done.10.refs_1_
  32.9 0.0 collective-permute-done.11.refs_2_
  33.0 0.3 combine.1
  33.2 1.7 %collective-permute-start.12 = (bf16[2,1024]{1,0:T(2,128)(2,1)S(1)}, bf16[2,1024]{1,0:T(2,128)(2,1)S(1)}, u32[]{:S(2)}, u32[]{:S(2)}) collective-permute-start(bf16[2,1024]{1,0:T(2,128)(2,1)S(1)} %get-tuple-element.64), channel_id=1, source_target_pairs={{0,13},{1,12},{2,15},{3,14},{4,9},{5,8},{6,11},{7,10},{8,5},{9,4},... | collective-permute-start | bytes 12296 | tf_op jit(solution)/shard_map/ppermute | solution.py:50
  34.9 0.0 collective-permute-start.13
  34.9 2.1 %collective-permute-start.14 = (bf16[2,1024]{1,0:T(2,128)(2,1)S(1)}, bf16[2,1024]{1,0:T(2,128)(2,1)S(1)}, u32[]{:S(2)}, u32[]{:S(2)}) collective-permute-start(bf16[2,1024]{1,0:T(2,128)(2,1)S(1)} %get-tuple-element.66), channel_id=1, source_target_pairs={{0,5},{1,4},{2,7},{3,6},{4,1},{5,0},{6,3},{7,2},{8,13},{9,12},{10,... | collective-permute-start | bytes 12296 | tf_op jit(solution)/shard_map/ppermute | solution.py:50
  37.0 1.1 %collective-permute-done.12.refs_0_ = bf16[2,1024]{1,0:T(2,128)(2,1)S(1)} collective-permute-done((bf16[2,1024]{1,0:T(2,128)(2,1)S(1)}, bf16[2,1024]{1,0:T(2,128)(2,1)S(1)}, u32[]{:S(2)}, u32[]{:S(2)}) %collective-permute-start.12) | collective-permute-done | bytes 4128 | tf_op jit(solution)/shard_map/ppermute | solution.py:50
  38.1 0.7 %collective-permute-done.13.refs_1_ = bf16[2,1024]{1,0:T(2,128)(2,1)S(1)} collective-permute-done((bf16[2,1024]{1,0:T(2,128)(2,1)S(1)}, bf16[2,1024]{1,0:T(2,128)(2,1)S(1)}, u32[]{:S(2)}, u32[]{:S(2)}) %collective-permute-start.13) | collective-permute-done | bytes 4128 | tf_op jit(solution)/shard_map/ppermute | solution.py:50
  38.8 1.0 %project_out.1 = (bf16[8,2048]{1,0:T(8,128)(2,1)S(1)}, bf16[8,2048]{1,0:T(8,128)(2,1)S(1)}, bf16[8,2048]{1,0:T(8,128)(2,1)S(1)}, bf16[8,2048]{1,0:T(8,128)(2,1)S(1)}) custom-call(bf16[1024,2048]{1,0:T(8,128)(2,1)S(1)} %load.7.weight_ref, bf16[2,1024]{1,0:T(2,128)(2,1)S(1)} %collective-permute-done.12.refs_0_, ...), custom_call_target="tpu_custom_call" | custom-call | tf_op jit(solution)/shard_map/project_out/pallas_call | solution.py:432
  39.8 1.9 %collective-permute-start.15 = (bf16[8,2048]{1,0:T(8,128)(2,1)S(1)}, bf16[8,2048]{1,0:T(8,128)(2,1)S(1)}, u32[]{:S(2)}, u32[]{:S(2)}) collective-permute-start(bf16[8,2048]{1,0:T(8,128)(2,1)S(1)} %get-tuple-element.68), channel_id=1, source_target_pairs={{0,12},{1,13},{2,14},{3,15},{4,8},{5,9},{6,10},{7,11},{8,4},{9,5},... | collective-permute-start | bytes 98312 | tf_op jit(solution)/shard_map/ppermute | solution.py:50
  41.6 1.2 %collective-permute-start.16 = (bf16[8,2048]{1,0:T(8,128)(2,1)S(1)}, bf16[8,2048]{1,0:T(8,128)(2,1)S(1)}, u32[]{:S(2)}, u32[]{:S(2)}) collective-permute-start(bf16[8,2048]{1,0:T(8,128)(2,1)S(1)} %get-tuple-element.69), channel_id=1, source_target_pairs={{0,8},{1,9},{2,10},{3,11},{4,12},{5,13},{6,14},{7,15},{8,0},{9,1},... | collective-permute-start | bytes 98312 | tf_op jit(solution)/shard_map/ppermute | solution.py:50
  42.9 1.3 %collective-permute-start.17 = (bf16[8,2048]{1,0:T(8,128)(2,1)S(1)}, bf16[8,2048]{1,0:T(8,128)(2,1)S(1)}, u32[]{:S(2)}, u32[]{:S(2)}) collective-permute-start(bf16[8,2048]{1,0:T(8,128)(2,1)S(1)} %get-tuple-element.70), channel_id=1, source_target_pairs={{0,4},{1,5},{2,6},{3,7},{4,0},{5,1},{6,2},{7,3},{8,12},{9,13},{10,... | collective-permute-start | bytes 98312 | tf_op jit(solution)/shard_map/ppermute | solution.py:50
  44.2 1.6 %collective-permute-done.15.refs_0_ = bf16[8,2048]{1,0:T(8,128)(2,1)S(1)} collective-permute-done((bf16[8,2048]{1,0:T(8,128)(2,1)S(1)}, bf16[8,2048]{1,0:T(8,128)(2,1)S(1)}, u32[]{:S(2)}, u32[]{:S(2)}) %collective-permute-start.15) | collective-permute-done | bytes 32800 | tf_op jit(solution)/shard_map/ppermute | solution.py:50
  45.8 1.1 %collective-permute-done.16.refs_1_ = bf16[8,2048]{1,0:T(8,128)(2,1)S(1)} collective-permute-done((bf16[8,2048]{1,0:T(8,128)(2,1)S(1)}, bf16[8,2048]{1,0:T(8,128)(2,1)S(1)}, u32[]{:S(2)}, u32[]{:S(2)}) %collective-permute-start.16) | collective-permute-done | bytes 32800 | tf_op jit(solution)/shard_map/ppermute | solution.py:50
  46.9 0.0 collective-permute-done.17.refs_2_
  46.9 2.0 %first_gate_up.1 = (bf16[8,3712]{1,0:T(8,128)(2,1)S(1)}, f32[2,2048]{1,0:T(2,128)S(1)}, bf16[8,2048]{1,0:T(8,128)(2,1)S(1)}) custom-call(s32[8,128]{1,0:T(8,128)S(1)} %iota.24.lanes_ref, f32[8,2048]{1,0:T(8,128)S(1)} %get-tuple-element.46.refs_1_.rows_ref, bf16[2048]{0:T(1024)(128)(2,1)S(1)} %copy-done.4, bf16[2048,3584]{1,0:T(8,128)(2,1)S(1)} %bitcast.8, ...), custom_call_target="tpu_custom_call" | custom-call | flops 117440512 | bytes 14680064 | tf_op jit(solution)/shard_map/first_gate_up/pallas_call | solution.py:488
  48.9 0.0 slice-start.5
  49.0 0.0 slice-start.6
  49.0 2.0 %second_gate_up.1.first_ref = bf16[8,3584]{1,0:T(8,128)(2,1)S(1)} custom-call(bf16[8,2048]{1,0:T(8,128)(2,1)S(1)} %get-tuple-element.74.scaled_ref, bf16[2048,3584]{1,0:T(8,128)(2,1)S(1)} %bitcast.8, bf16[2048,3584]{1,0:T(8,128)(2,1)S(1)} %copy-done), custom_call_target="tpu_custom_call" | custom-call | flops 117440512 | bytes 14680064 | tf_op jit(solution)/shard_map/second_gate_up/pallas_call | solution.py:510
  51.0 0.5 collective-permute-start.20
  51.5 1.2 %collective-permute-start.19 = (bf16[8,3712]{1,0:T(8,128)(2,1)S(1)}, bf16[8,3712]{1,0:T(8,128)(2,1)S(1)}, u32[]{:S(2)}, u32[]{:S(2)}) collective-permute-start(bf16[8,3712]{1,0:T(8,128)(2,1)S(1)} %pair_sum.2.one_near), channel_id=1, source_target_pairs={{0,2},{1,3},{2,0},{3,1},{4,6},{5,7},{6,4},{7,5},{8,10},{9,11},{10,... | collective-permute-start | bytes 178184 | tf_op jit(solution)/shard_map/ppermute | solution.py:31
  52.7 1.0 %collective-permute-start.21 = (bf16[8,3584]{1,0:T(8,128)(2,1)S(1)}, bf16[8,3584]{1,0:T(8,128)(2,1)S(1)}, u32[]{:S(2)}, u32[]{:S(2)}) collective-permute-start(bf16[8,3584]{1,0:T(8,128)(2,1)S(1)} %pair_sum.3.two_near), channel_id=1, source_target_pairs={{0,2},{1,3},{2,0},{3,1},{4,6},{5,7},{6,4},{7,5},{8,10},{9,11},{10,... | collective-permute-start | bytes 172040 | tf_op jit(solution)/shard_map/ppermute | solution.py:31
  53.7 3.3 %collective-permute-done.21.two_far = bf16[8,3584]{1,0:T(8,128)(2,1)S(1)} collective-permute-done((bf16[8,3584]{1,0:T(8,128)(2,1)S(1)}, bf16[8,3584]{1,0:T(8,128)(2,1)S(1)}, u32[]{:S(2)}, u32[]{:S(2)}) %collective-permute-start.21) | collective-permute-done | bytes 57376 | tf_op jit(solution)/shard_map/ppermute | solution.py:31
  57.0 2.3 %project_down.1 = (bf16[2,2048]{1,0:T(2,128)(2,1)S(1)}, bf16[2,2048]{1,0:T(2,128)(2,1)S(1)}, bf16[2,2048]{1,0:T(2,128)(2,1)S(1)}, bf16[2,2048]{1,0:T(2,128)(2,1)S(1)}) custom-call(bf16[8,3712]{1,0:T(8,128)(2,1)S(1)} %pair_sum.2.one_near, bf16[8,3712]{1,0:T(8,128)(2,1)S(1)} %collective-permute-done.19.one_far, bf16[8,3584]{1,0:T(8,128)(2,1)S(1)} %pair_sum.3.two_near, ...), custom_call_target="tpu_custom_call" | custom-call | tf_op jit(solution)/shard_map/project_down/pallas_call | solution.py:553
  59.3 2.2 %collective-permute-start.22 = (bf16[2,2048]{1,0:T(2,128)(2,1)S(1)}, bf16[2,2048]{1,0:T(2,128)(2,1)S(1)}, u32[]{:S(2)}, u32[]{:S(2)}) collective-permute-start(bf16[2,2048]{1,0:T(2,128)(2,1)S(1)} %get-tuple-element.75), channel_id=1, source_target_pairs={{0,12},{1,13},{2,14},{3,15},{4,8},{5,9},{6,10},{7,11},{8,4},{9,5},... | collective-permute-start | bytes 24584 | tf_op jit(solution)/shard_map/ppermute | solution.py:50
  61.5 0.7 %collective-permute-start.23 = (bf16[2,2048]{1,0:T(2,128)(2,1)S(1)}, bf16[2,2048]{1,0:T(2,128)(2,1)S(1)}, u32[]{:S(2)}, u32[]{:S(2)}) collective-permute-start(bf16[2,2048]{1,0:T(2,128)(2,1)S(1)} %get-tuple-element.76), channel_id=1, source_target_pairs={{0,8},{1,9},{2,10},{3,11},{4,12},{5,13},{6,14},{7,15},{8,0},{9,1},... | collective-permute-start | bytes 24584 | tf_op jit(solution)/shard_map/ppermute | solution.py:50
  62.2 1.6 %collective-permute-start.24 = (bf16[2,2048]{1,0:T(2,128)(2,1)S(1)}, bf16[2,2048]{1,0:T(2,128)(2,1)S(1)}, u32[]{:S(2)}, u32[]{:S(2)}) collective-permute-start(bf16[2,2048]{1,0:T(2,128)(2,1)S(1)} %get-tuple-element.77), channel_id=1, source_target_pairs={{0,4},{1,5},{2,6},{3,7},{4,0},{5,1},{6,2},{7,3},{8,12},{9,13},{10,... | collective-permute-start | bytes 24584 | tf_op jit(solution)/shard_map/ppermute | solution.py:50
  63.8 1.1 %collective-permute-done.22.refs_0_ = bf16[2,2048]{1,0:T(2,128)(2,1)S(1)} collective-permute-done((bf16[2,2048]{1,0:T(2,128)(2,1)S(1)}, bf16[2,2048]{1,0:T(2,128)(2,1)S(1)}, u32[]{:S(2)}, u32[]{:S(2)}) %collective-permute-start.22) | collective-permute-done | bytes 8224 | tf_op jit(solution)/shard_map/ppermute | solution.py:50
  64.8 1.2 %collective-permute-done.23.refs_1_ = bf16[2,2048]{1,0:T(2,128)(2,1)S(1)} collective-permute-done((bf16[2,2048]{1,0:T(2,128)(2,1)S(1)}, bf16[2,2048]{1,0:T(2,128)(2,1)S(1)}, u32[]{:S(2)}, u32[]{:S(2)}) %collective-permute-start.23) | collective-permute-done | bytes 8224 | tf_op jit(solution)/shard_map/ppermute | solution.py:50
  66.1 0.6 finish.1
  (42 shorter events, 0.2 us)
Async XLA Ops:
  0.0 10.5 %copy-start.3 = (bf16[2048]{0:T(1024)(128)(2,1)S(1)}, bf16[2048]{0:T(1024)(128)(2,1)}, u32[]{:S(2)}) copy-start(bf16[2048]{0:T(1024)(128)(2,1)} %gain_ref.2) | copy-start | bytes 12292
  0.0 10.4 %collective-permute-start = (bf16[2,2048]{1,0:T(2,128)(2,1)}, bf16[2,2048]{1,0:T(2,128)(2,1)S(1)}, u32[]{:S(2)}, u32[]{:S(2)}) collective-permute-start(bf16[2,2048]{1,0:T(2,128)(2,1)} %refs_3_.1), channel_id=1, source_target_pairs={{0,12},{4,8},{8,4},{12,0},{1,13},{5,9},{9,5},{13,1},{2,14},{6,10},... | collective-permute-start | bytes 24584 | tf_op jit(solution)/shard_map/ppermute | solution.py:31
  5.1 5.4 %collective-permute-start.1 = (bf16[2,2048]{1,0:T(2,128)(2,1)}, bf16[2,2048]{1,0:T(2,128)(2,1)S(1)}, u32[]{:S(2)}, u32[]{:S(2)}) collective-permute-start(bf16[2,2048]{1,0:T(2,128)(2,1)} %refs_3_.1), channel_id=1, source_target_pairs={{0,8},{4,12},{8,0},{12,4},{1,9},{5,13},{9,1},{13,5},{2,10},{6,14},... | collective-permute-start | bytes 24584 | tf_op jit(solution)/shard_map/ppermute | solution.py:31
  5.1 5.4 %collective-permute-start.2 = (bf16[2,2048]{1,0:T(2,128)(2,1)}, bf16[2,2048]{1,0:T(2,128)(2,1)S(1)}, u32[]{:S(2)}, u32[]{:S(2)}) collective-permute-start(bf16[2,2048]{1,0:T(2,128)(2,1)} %refs_3_.1), channel_id=1, source_target_pairs={{0,4},{4,0},{8,12},{12,8},{1,5},{5,1},{9,13},{13,9},{2,6},{6,2},{1... | collective-permute-start | bytes 24584 | tf_op jit(solution)/shard_map/ppermute | solution.py:31
  5.7 12.0 %copy-start.5 = (s32[8]{0:T(128)S(1)}, s32[8]{0:T(128)}, u32[]{:S(2)}) copy-start(s32[8]{0:T(128)} %param.23) | copy-start | bytes 100
  5.7 27.2 %slice-start = ((s8[14680064]{0:T(1024)(128)(4,1)}), s8[2097152]{0:T(1024)(128)(4,1)S(1)}, s32[]{:S(2)}) async-start(s8[14680064]{0:T(1024)(128)(4,1)} %bitcast.7), calls=%async_computation | async-start | bytes 4194304
  8.5 2.0 %copy-start.1 = (bf16[2048,1024]{1,0:T(8,128)(2,1)}, bf16[2048,1024]{1,0:T(8,128)(2,1)S(1)}, u32[]{:S(2)}) copy-start(bf16[2048,1024]{1,0:T(8,128)(2,1)S(1)} %get-tuple-element.42.wq_ref) | copy-start | bytes 12582916
  10.5 2.2 %copy-start.2 = (bf16[2048,1024]{1,0:T(8,128)(2,1)S(1)}, bf16[2048,1024]{1,0:T(8,128)(2,1)}, u32[]{:S(2)}) copy-start(bf16[2048,1024]{1,0:T(8,128)(2,1)} %copy-done.1) | copy-start | bytes 12582916
  12.7 20.3 %slice-start.1 = ((s8[14680064]{0:T(1024)(128)(4,1)}), s8[4194304]{0:T(1024)(128)(4,1)S(1)}, s32[]{:S(2)}) async-start(s8[14680064]{0:T(1024)(128)(4,1)} %bitcast.7), calls=%async_computation.1 | async-start | bytes 8388608
  13.5 6.0 %collective-permute-start.3 = (bf16[2,1408]{1,0:T(2,128)(2,1)S(1)}, bf16[2,1408]{1,0:T(2,128)(2,1)S(1)}, u32[]{:S(2)}, u32[]{:S(2)}) collective-permute-start(bf16[2,1408]{1,0:T(2,128)(2,1)S(1)} %get-tuple-element.48), channel_id=1, source_target_pairs={{0,13},{1,12},{2,15},{3,14},{4,9},{5,8},{6,11},{7,10},{8,5},{9,4},... | collective-permute-start | bytes 16904 | tf_op jit(solution)/shard_map/ppermute | solution.py:50
  15.9 3.9 %collective-permute-start.4 = (bf16[2,1408]{1,0:T(2,128)(2,1)S(1)}, bf16[2,1408]{1,0:T(2,128)(2,1)S(1)}, u32[]{:S(2)}, u32[]{:S(2)}) collective-permute-start(bf16[2,1408]{1,0:T(2,128)(2,1)S(1)} %get-tuple-element.49), channel_id=1, source_target_pairs={{0,9},{1,8},{2,11},{3,10},{4,13},{5,12},{6,15},{7,14},{8,1},{9,0},... | collective-permute-start | bytes 16904 | tf_op jit(solution)/shard_map/ppermute | solution.py:50
  16.2 3.7 %collective-permute-start.5 = (bf16[2,1408]{1,0:T(2,128)(2,1)S(1)}, bf16[2,1408]{1,0:T(2,128)(2,1)S(1)}, u32[]{:S(2)}, u32[]{:S(2)}) collective-permute-start(bf16[2,1408]{1,0:T(2,128)(2,1)S(1)} %get-tuple-element.50), channel_id=1, source_target_pairs={{0,5},{1,4},{2,7},{3,6},{4,1},{5,0},{6,3},{7,2},{8,13},{9,12},{10,... | collective-permute-start | bytes 16904 | tf_op jit(solution)/shard_map/ppermute | solution.py:50
  19.9 5.1 %collective-permute-start.6 = (bf16[8,1408]{1,0:T(8,128)(2,1)S(1)}, bf16[8,1408]{1,0:T(8,128)(2,1)S(1)}, u32[]{:S(2)}, u32[]{:S(2)}) collective-permute-start(bf16[8,1408]{1,0:T(8,128)(2,1)S(1)} %stack.18.refs_1_.refs_0_), channel_id=1, source_target_pairs={{0,3},{1,2},{2,1},{3,0},{4,7},{5,6},{6,5},{7,4},{8,11},{9,10},{10,... | collective-permute-start | bytes 67592 | tf_op jit(solution)/shard_map/ppermute | solution.py:31
  22.6 3.8 %collective-permute-start.7 = (bf16[8,1408]{1,0:T(8,128)(2,1)S(1)}, bf16[8,1408]{1,0:T(8,128)(2,1)S(1)}, u32[]{:S(2)}, u32[]{:S(2)}) collective-permute-start(bf16[8,1408]{1,0:T(8,128)(2,1)S(1)} %stack.18.refs_1_.refs_0_), channel_id=1, source_target_pairs={{0,2},{1,3},{2,0},{3,1},{4,6},{5,7},{6,4},{7,5},{8,10},{9,11},{10,... | collective-permute-start | bytes 67592 | tf_op jit(solution)/shard_map/ppermute | solution.py:31
  23.1 3.3 %collective-permute-start.8 = (bf16[8,1408]{1,0:T(8,128)(2,1)S(1)}, bf16[8,1408]{1,0:T(8,128)(2,1)S(1)}, u32[]{:S(2)}, u32[]{:S(2)}) collective-permute-start(bf16[8,1408]{1,0:T(8,128)(2,1)S(1)} %stack.18.refs_1_.refs_0_), channel_id=1, source_target_pairs={{0,1},{1,0},{2,3},{3,2},{4,5},{5,4},{6,7},{7,6},{8,9},{9,8},{10,11... | collective-permute-start | bytes 67592 | tf_op jit(solution)/shard_map/ppermute | solution.py:31
  23.2 9.7 %slice-start.2 = ((s8[14680064]{0:T(1024)(128)(4,1)}), s8[4194304]{0:T(1024)(128)(4,1)S(1)}, s32[]{:S(2)}) async-start(s8[14680064]{0:T(1024)(128)(4,1)} %bitcast.7), calls=%async_computation.2 | async-start | bytes 8388608
  28.5 4.5 %slice-start.3 = ((s8[14680064]{0:T(1024)(128)(4,1)}), s8[4194304]{0:T(1024)(128)(4,1)S(1)}, s32[]{:S(2)}) async-start(s8[14680064]{0:T(1024)(128)(4,1)} %bitcast.7), calls=%async_computation.3 | async-start | bytes 8388608
  28.5 4.4 %collective-permute-start.10 = (bf16[80,128]{1,0:T(8,128)(2,1)S(1)}, bf16[80,128]{1,0:T(8,128)(2,1)S(1)}, u32[]{:S(2)}, u32[]{:S(2)}) collective-permute-start(bf16[80,128]{1,0:T(8,128)(2,1)S(1)} %attend.1.refs_1_.refs_3_), channel_id=1, source_target_pairs={{0,2},{1,3},{2,0},{3,1},{4,6},{5,7},{6,4},{7,5},{8,10},{9,11},{10,... | collective-permute-start | bytes 61448 | tf_op jit(solution)/shard_map/ppermute | solution.py:31
  29.1 3.8 %collective-permute-start.11 = (bf16[80,128]{1,0:T(8,128)(2,1)S(1)}, bf16[80,128]{1,0:T(8,128)(2,1)S(1)}, u32[]{:S(2)}, u32[]{:S(2)}) collective-permute-start(bf16[80,128]{1,0:T(8,128)(2,1)S(1)} %attend.1.refs_1_.refs_3_), channel_id=1, source_target_pairs={{0,1},{1,0},{2,3},{3,2},{4,5},{5,4},{6,7},{7,6},{8,9},{9,8},{10,11... | collective-permute-start | bytes 61448 | tf_op jit(solution)/shard_map/ppermute | solution.py:31
  29.1 3.8 %collective-permute-start.9 = (bf16[80,128]{1,0:T(8,128)(2,1)S(1)}, bf16[80,128]{1,0:T(8,128)(2,1)S(1)}, u32[]{:S(2)}, u32[]{:S(2)}) collective-permute-start(bf16[80,128]{1,0:T(8,128)(2,1)S(1)} %attend.1.refs_1_.refs_3_), channel_id=1, source_target_pairs={{0,3},{1,2},{2,1},{3,0},{4,7},{5,6},{6,5},{7,4},{8,11},{9,10},{10,... | collective-permute-start | bytes 61448 | tf_op jit(solution)/shard_map/ppermute | solution.py:31
  32.9 6.0 %copy-start = (bf16[2048,3584]{1,0:T(8,128)(2,1)S(1)}, bf16[2048,3584]{1,0:T(8,128)(2,1)}, u32[]{:S(2)}) copy-start(bf16[2048,3584]{1,0:T(8,128)(2,1)} %up_ref.3) | copy-start | bytes 44040196
  33.2 4.9 %collective-permute-start.12 = (bf16[2,1024]{1,0:T(2,128)(2,1)S(1)}, bf16[2,1024]{1,0:T(2,128)(2,1)S(1)}, u32[]{:S(2)}, u32[]{:S(2)}) collective-permute-start(bf16[2,1024]{1,0:T(2,128)(2,1)S(1)} %get-tuple-element.64), channel_id=1, source_target_pairs={{0,13},{1,12},{2,15},{3,14},{4,9},{5,8},{6,11},{7,10},{8,5},{9,4},... | collective-permute-start | bytes 12296 | tf_op jit(solution)/shard_map/ppermute | solution.py:50
  34.9 3.9 %collective-permute-start.13 = (bf16[2,1024]{1,0:T(2,128)(2,1)S(1)}, bf16[2,1024]{1,0:T(2,128)(2,1)S(1)}, u32[]{:S(2)}, u32[]{:S(2)}) collective-permute-start(bf16[2,1024]{1,0:T(2,128)(2,1)S(1)} %get-tuple-element.65), channel_id=1, source_target_pairs={{0,9},{1,8},{2,11},{3,10},{4,13},{5,12},{6,15},{7,14},{8,1},{9,0},... | collective-permute-start | bytes 12296 | tf_op jit(solution)/shard_map/ppermute | solution.py:50
  34.9 3.9 %collective-permute-start.14 = (bf16[2,1024]{1,0:T(2,128)(2,1)S(1)}, bf16[2,1024]{1,0:T(2,128)(2,1)S(1)}, u32[]{:S(2)}, u32[]{:S(2)}) collective-permute-start(bf16[2,1024]{1,0:T(2,128)(2,1)S(1)} %get-tuple-element.66), channel_id=1, source_target_pairs={{0,5},{1,4},{2,7},{3,6},{4,1},{5,0},{6,3},{7,2},{8,13},{9,12},{10,... | collective-permute-start | bytes 12296 | tf_op jit(solution)/shard_map/ppermute | solution.py:50
  38.8 8.1 %copy-start.4 = (bf16[2048]{0:T(1024)(128)(2,1)S(1)}, bf16[2048]{0:T(1024)(128)(2,1)}, u32[]{:S(2)}) copy-start(bf16[2048]{0:T(1024)(128)(2,1)} %gain_ref.3) | copy-start | bytes 12292
  39.8 6.0 %collective-permute-start.15 = (bf16[8,2048]{1,0:T(8,128)(2,1)S(1)}, bf16[8,2048]{1,0:T(8,128)(2,1)S(1)}, u32[]{:S(2)}, u32[]{:S(2)}) collective-permute-start(bf16[8,2048]{1,0:T(8,128)(2,1)S(1)} %get-tuple-element.68), channel_id=1, source_target_pairs={{0,12},{1,13},{2,14},{3,15},{4,8},{5,9},{6,10},{7,11},{8,4},{9,5},... | collective-permute-start | bytes 98312 | tf_op jit(solution)/shard_map/ppermute | solution.py:50
  41.6 5.2 %collective-permute-start.16 = (bf16[8,2048]{1,0:T(8,128)(2,1)S(1)}, bf16[8,2048]{1,0:T(8,128)(2,1)S(1)}, u32[]{:S(2)}, u32[]{:S(2)}) collective-permute-start(bf16[8,2048]{1,0:T(8,128)(2,1)S(1)} %get-tuple-element.69), channel_id=1, source_target_pairs={{0,8},{1,9},{2,10},{3,11},{4,12},{5,13},{6,14},{7,15},{8,0},{9,1},... | collective-permute-start | bytes 98312 | tf_op jit(solution)/shard_map/ppermute | solution.py:50
  42.9 4.1 %collective-permute-start.17 = (bf16[8,2048]{1,0:T(8,128)(2,1)S(1)}, bf16[8,2048]{1,0:T(8,128)(2,1)S(1)}, u32[]{:S(2)}, u32[]{:S(2)}) collective-permute-start(bf16[8,2048]{1,0:T(8,128)(2,1)S(1)} %get-tuple-element.70), channel_id=1, source_target_pairs={{0,4},{1,5},{2,6},{3,7},{4,0},{5,1},{6,2},{7,3},{8,12},{9,13},{10,... | collective-permute-start | bytes 98312 | tf_op jit(solution)/shard_map/ppermute | solution.py:50
  48.9 2.6 %collective-permute-start.18 = (bf16[8,3712]{1,0:T(8,128)(2,1)S(1)}, bf16[8,3712]{1,0:T(8,128)(2,1)S(1)}, u32[]{:S(2)}, u32[]{:S(2)}) collective-permute-start(bf16[8,3712]{1,0:T(8,128)(2,1)S(1)} %get-tuple-element.73.first_ref), channel_id=1, source_target_pairs={{0,1},{1,0},{2,3},{3,2},{4,5},{5,4},{6,7},{7,6},{8,9},{9,8},{10,11... | collective-permute-start | bytes 178184 | tf_op jit(solution)/shard_map/ppermute | solution.py:31
  48.9 8.1 %slice-start.4 = ((s8[14680064]{0:T(1024)(128)(4,1)}), s8[4194304]{0:T(1024)(128)(4,1)S(1)}, s32[]{:S(2)}) async-start(s8[14680064]{0:T(1024)(128)(4,1)} %bitcast.9), calls=%async_computation.4 | async-start | bytes 8388608
  48.9 8.1 %slice-start.5 = ((s8[14680064]{0:T(1024)(128)(4,1)}), s8[4194304]{0:T(1024)(128)(4,1)S(1)}, s32[]{:S(2)}) async-start(s8[14680064]{0:T(1024)(128)(4,1)} %bitcast.9), calls=%async_computation.5 | async-start | bytes 8388608
  49.0 8.1 %slice-start.6 = ((s8[14680064]{0:T(1024)(128)(4,1)}), s8[4194304]{0:T(1024)(128)(4,1)S(1)}, s32[]{:S(2)}) async-start(s8[14680064]{0:T(1024)(128)(4,1)} %bitcast.9), calls=%async_computation.6 | async-start | bytes 8388608
  49.0 8.1 %slice-start.7 = ((s8[14680064]{0:T(1024)(128)(4,1)}), s8[2097152]{0:T(1024)(128)(4,1)S(1)}, s32[]{:S(2)}) async-start(s8[14680064]{0:T(1024)(128)(4,1)} %bitcast.9), calls=%async_computation.7 | async-start | bytes 4194304
  51.0 1.7 %collective-permute-start.20 = (bf16[8,3584]{1,0:T(8,128)(2,1)S(1)}, bf16[8,3584]{1,0:T(8,128)(2,1)S(1)}, u32[]{:S(2)}, u32[]{:S(2)}) collective-permute-start(bf16[8,3584]{1,0:T(8,128)(2,1)S(1)} %second_gate_up.1.first_ref), channel_id=1, source_target_pairs={{0,1},{1,0},{2,3},{3,2},{4,5},{5,4},{6,7},{7,6},{8,9},{9,8},{10,11... | collective-permute-start | bytes 172040 | tf_op jit(solution)/shard_map/ppermute | solution.py:31
  51.5 5.5 %collective-permute-start.19 = (bf16[8,3712]{1,0:T(8,128)(2,1)S(1)}, bf16[8,3712]{1,0:T(8,128)(2,1)S(1)}, u32[]{:S(2)}, u32[]{:S(2)}) collective-permute-start(bf16[8,3712]{1,0:T(8,128)(2,1)S(1)} %pair_sum.2.one_near), channel_id=1, source_target_pairs={{0,2},{1,3},{2,0},{3,1},{4,6},{5,7},{6,4},{7,5},{8,10},{9,11},{10,... | collective-permute-start | bytes 178184 | tf_op jit(solution)/shard_map/ppermute | solution.py:31
  52.7 4.3 %collective-permute-start.21 = (bf16[8,3584]{1,0:T(8,128)(2,1)S(1)}, bf16[8,3584]{1,0:T(8,128)(2,1)S(1)}, u32[]{:S(2)}, u32[]{:S(2)}) collective-permute-start(bf16[8,3584]{1,0:T(8,128)(2,1)S(1)} %pair_sum.3.two_near), channel_id=1, source_target_pairs={{0,2},{1,3},{2,0},{3,1},{4,6},{5,7},{6,4},{7,5},{8,10},{9,11},{10,... | collective-permute-start | bytes 172040 | tf_op jit(solution)/shard_map/ppermute | solution.py:31
  59.3 5.5 %collective-permute-start.22 = (bf16[2,2048]{1,0:T(2,128)(2,1)S(1)}, bf16[2,2048]{1,0:T(2,128)(2,1)S(1)}, u32[]{:S(2)}, u32[]{:S(2)}) collective-permute-start(bf16[2,2048]{1,0:T(2,128)(2,1)S(1)} %get-tuple-element.75), channel_id=1, source_target_pairs={{0,12},{1,13},{2,14},{3,15},{4,8},{5,9},{6,10},{7,11},{8,4},{9,5},... | collective-permute-start | bytes 24584 | tf_op jit(solution)/shard_map/ppermute | solution.py:50
  61.5 4.5 %collective-permute-start.23 = (bf16[2,2048]{1,0:T(2,128)(2,1)S(1)}, bf16[2,2048]{1,0:T(2,128)(2,1)S(1)}, u32[]{:S(2)}, u32[]{:S(2)}) collective-permute-start(bf16[2,2048]{1,0:T(2,128)(2,1)S(1)} %get-tuple-element.76), channel_id=1, source_target_pairs={{0,8},{1,9},{2,10},{3,11},{4,12},{5,13},{6,14},{7,15},{8,0},{9,1},... | collective-permute-start | bytes 24584 | tf_op jit(solution)/shard_map/ppermute | solution.py:50
  62.2 3.9 %collective-permute-start.24 = (bf16[2,2048]{1,0:T(2,128)(2,1)S(1)}, bf16[2,2048]{1,0:T(2,128)(2,1)S(1)}, u32[]{:S(2)}, u32[]{:S(2)}) collective-permute-start(bf16[2,2048]{1,0:T(2,128)(2,1)S(1)} %get-tuple-element.77), channel_id=1, source_target_pairs={{0,4},{1,5},{2,6},{3,7},{4,0},{5,1},{6,2},{7,3},{8,12},{9,13},{10,... | collective-permute-start | bytes 24584 | tf_op jit(solution)/shard_map/ppermute | solution.py:50

commit v15 on v12

--- a/solution.py
+++ b/solution.py
@@ -406,12 +406,13 @@
     )
 
 
-def out_kernel(slots, later, weight_ref, *refs):
+def out_kernel(slots, later, upper_ref, lower_ref, *refs):
     pieces = refs[:slots][::-1]
     outs = refs[slots + later : 2 * slots + later]
     left_s = refs[-1]
     own_rows = pieces[0].shape[0]
     rows = left_s.shape[0]
+    cut = upper_ref.shape[0]
     lefts = [join_rows(pieces, left_s)]
     for k in range(1, slots):
         low = k & -k
@@ -419,25 +420,29 @@
     left = jnp.concatenate(lefts, axis=0).astype(jnp.bfloat16)
 
     def store(start, size, value):
+        span = pl.ds(start, size)
+        value = value + jnp.dot(
+            left[:, cut:], lower_ref[:, span], preferred_element_type=jnp.float32
+        )
         for k, ref in enumerate(outs):
-            ref[:, pl.ds(start, size)] = value[k * rows : (k + 1) * rows].astype(jnp.bfloat16)
-
-    product_tiles(left, weight_ref, store)
-
-
-def project_out(pieces, weight, later):
+            ref[:, span] = value[k * rows : (k + 1) * rows].astype(jnp.bfloat16)
+
+    product_tiles(left[:, :cut], upper_ref, store)
+
+
+def project_out(pieces, upper, lower, later):
     slots = len(pieces)
     own_rows, depth = pieces[0].shape
-    shape = jax.ShapeDtypeStruct((own_rows * slots, weight.shape[1]), jnp.bfloat16)
+    shape = jax.ShapeDtypeStruct((own_rows * slots, upper.shape[1]), jnp.bfloat16)
     return pl.pallas_call(
         functools.partial(out_kernel, slots, len(later)),
         out_shape=(shape,) * slots,
-        in_specs=[in_vmem] * (1 + slots) + [in_place] * len(later),
+        in_specs=[in_vmem] * (2 + slots) + [in_place] * len(later),
         out_specs=(in_vmem,) * slots,
         scratch_shapes=[pltpu.VMEM((own_rows * slots, depth), jnp.float32)],
         compiler_params=params(3),
         name="project_out",
-    )(resident(weight), *pieces[::-1], *[resident(w) for w in later])
+    )(resident(upper), resident(lower), *pieces[::-1], *[resident(w) for w in later])
 
 
 def pair_kernel(first_ref, second_ref, out_ref):
@@ -629,10 +634,13 @@
     parts, values = lax.optimization_barrier((exchange(joined, "inner")[::-1], values))
     shard = attend(my_lengths, cosine, sine, parts, keys, values, [], slots)
 
-    (w_out,) = load(w_out, after=shard)
-    shards, w_out = lax.optimization_barrier((exchange(shard, "inner")[::-1], w_out))
+    cut = w_out.shape[0] // 2
+    (out_upper,) = load(w_out, after=shard, spans=[(0, cut)])
+    shards, out_upper = lax.optimization_barrier((exchange(shard, "inner")[::-1], out_upper))
     pieces = combine(shards[::-1], [w_gate], all_rows, slots)
-    parts = scatter_slots(project_out(scatter_slots(pieces, 1), w_out, [w_up]), 0)
+    (out_lower,) = load(w_out, after=pieces[0], spans=[(cut, w_out.shape[0] - cut)])
+    pieces, out_lower = lax.optimization_barrier((scatter_slots(pieces, 1)[::-1], out_lower))
+    parts = scatter_slots(project_out(pieces[::-1], out_upper, out_lower, [w_up]), 0)
 
     tiles = w_gate.shape[1] // LANES
     first = (tiles + 1) // 2 * LANES

time: 62.4 us -> 62.2 us (level)
  waiting for transfers between devices: 13.1 us -> 12 us
  Pallas kernels: 19.2 us -> 19.9 us
    ppermute x12, waiting for transfers between devices: 7.03 us -> 5.55 us  [scatter_slots(): got.append(lax.ppermute(pieces[k], ('tensor', 'inner'), pairs))]
    pallas_call x4 -> x5, Pallas kernels: 8.48 us -> 9.23 us  [load(): pl.pallas_call(functools.partial(load_kernel, spans), out_shape=tuple((pl...]
  transfers between devices with their start and end apart: 25 -> 25, of which waited for: 11 -> 11; matrix products, arithmetic and copies ran while one was open for 0% -> 0% of each run, Pallas kernels for 17% -> 18%
where the time goes in v15:
time: 62.2 us; the launch traced here: 62 us
  starting transfers between devices  29.5 us (47%)
  Pallas kernels  19.9 us (32%)
  waiting for transfers between devices  12 us (19%)
    ppermute x12, starting transfers between devices, scatter_slots(): got.append(lax.ppermute(pieces[k], ('tensor', 'inner'), pairs))  15.7 us
    ppermute x13, starting transfers between devices, swap_with(): return lax.ppermute(value, axis, [(i, i ^ step) for i in range(count)])  13.8 us
    pallas_call x5, Pallas kernels, load(): pl.pallas_call(functools.partial(load_kernel, spans), out_shape=tuple((pl...  9.23 us
    ppermute x13, waiting for transfers between devices, swap_with(): return lax.ppermute(value, axis, [(i, i ^ step) for i in range(count)])  6.45 us
    ppermute x12, waiting for transfers between devices, scatter_slots(): got.append(lax.ppermute(pieces[k], ('tensor', 'inner'), pairs))  5.55 us
    pallas_call x1, Pallas kernels, project_down(): pl.pallas_call(down_kernel, out_shape=(jax.ShapeDtypeStruct((rows // slot...  2.28 us
    pallas_call x1, Pallas kernels, first_gate_up(): pl.pallas_call(functools.partial(first_gate_up_kernel, slots, count), out...  2 us
    pallas_call x1, Pallas kernels, second_gate_up(): pl.pallas_call(functools.partial(second_gate_up_kernel, first, count), ou...  2 us
  transfers between devices with their start and end apart: 25, of which 11 were waited for; matrix products, arithmetic and copies ran while one was open for 0% of the time, Pallas kernels for 18%

profile of v15, /device:TPU:0, one launch (start us, length us, event | category | flops | bytes accessed | tf_op | source)
XLA Modules:
  0.0 62.0 jit_solution(18370791916443937879)
XLA Ops:
  0.0 5.0 %collective-permute-start = (bf16[2,2048]{1,0:T(2,128)(2,1)}, bf16[2,2048]{1,0:T(2,128)(2,1)S(1)}, u32[]{:S(2)}, u32[]{:S(2)}) collective-permute-start(bf16[2,2048]{1,0:T(2,128)(2,1)} %refs_5_.1), channel_id=1, source_target_pairs={{0,12},{4,8},{8,4},{12,0},{1,13},{5,9},{9,5},{13,1},{2,14},{6,10},... | collective-permute-start | bytes 24584 | tf_op jit(solution)/shard_map/ppermute | solution.py:31
  5.0 0.0 collective-permute-start.1
  5.1 0.6 collective-permute-start.2
  5.6 2.7 %load.5 = (bf16[2,2048]{1,0:T(2,128)(2,1)S(1)}, bf16[2048]{0:T(1024)(128)(2,1)S(1)}, bf16[2048]{0:T(1024)(128)(2,1)S(1)}, bf16[2048,256]{1,0:T(8,128)(2,1)S(1)}, bf16[2048,1024]{1,0:T(8,128)(2,1)S(1)}) custom-call(bf16[2,2048]{1,0:T(2,128)(2,1)} %refs_5_.1, bf16[2048]{0:T(1024)(128)(2,1)} %refs_1_.1, bf16[2048]{0:T(1024)(128)(2,1)} %refs_2_.1, ...), custom_call_target="tpu_custom_call" | custom-call | bytes 5259264 | tf_op jit(solution)/shard_map/load/pallas_call | solution.py:145
  8.4 0.0 collective-permute-done.refs_0_
  8.4 1.4 %collective-permute-done.1.refs_1_ = bf16[2,2048]{1,0:T(2,128)(2,1)S(1)} collective-permute-done((bf16[2,2048]{1,0:T(2,128)(2,1)}, bf16[2,2048]{1,0:T(2,128)(2,1)S(1)}, u32[]{:S(2)}, u32[]{:S(2)}) %collective-permute-start.1) | collective-permute-done | bytes 8224 | tf_op jit(solution)/shard_map/ppermute | solution.py:31
  9.8 0.8 %project_qkv.1 = (f32[8,2048]{1,0:T(8,128)S(1)}, bf16[2,1408]{1,0:T(2,128)(2,1)S(1)}, bf16[2,1408]{1,0:T(2,128)(2,1)S(1)}, bf16[2,1408]{1,0:T(2,128)(2,1)S(1)}, bf16[2,1408]{1,0:T(2,128)(2,1)S(1)}) custom-call(bf16[2048]{0:T(1024)(128)(2,1)S(1)} %get-tuple-element.49.gain_ref, bf16[2048,1024]{1,0:T(8,128)(2,1)S(1)} %get-tuple-element.50.wq_ref, ...), custom_call_target="tpu_custom_call" | custom-call | tf_op jit(solution)/shard_map/project_qkv/pallas_call | solution.py:198
  10.6 1.1 %collective-permute-start.3 = (bf16[2,1408]{1,0:T(2,128)(2,1)S(1)}, bf16[2,1408]{1,0:T(2,128)(2,1)S(1)}, u32[]{:S(2)}, u32[]{:S(2)}) collective-permute-start(bf16[2,1408]{1,0:T(2,128)(2,1)S(1)} %get-tuple-element.57), channel_id=1, source_target_pairs={{0,13},{1,12},{2,15},{3,14},{4,9},{5,8},{6,11},{7,10},{8,5},{9,4},... | collective-permute-start | bytes 16904 | tf_op jit(solution)/shard_map/ppermute | solution.py:50
  11.7 0.2 collective-permute-start.4
  11.9 1.5 %collective-permute-start.5 = (bf16[2,1408]{1,0:T(2,128)(2,1)S(1)}, bf16[2,1408]{1,0:T(2,128)(2,1)S(1)}, u32[]{:S(2)}, u32[]{:S(2)}) collective-permute-start(bf16[2,1408]{1,0:T(2,128)(2,1)S(1)} %get-tuple-element.59), channel_id=1, source_target_pairs={{0,5},{1,4},{2,7},{3,6},{4,1},{5,0},{6,3},{7,2},{8,13},{9,12},{10,... | collective-permute-start | bytes 16904 | tf_op jit(solution)/shard_map/ppermute | solution.py:50
  13.5 0.1 fusion.4
  13.6 1.6 %load.6.key_ref = bf16[2,4096,128]{2,1,0:T(8,128)(2,1)S(1)} custom-call(bf16[2,4096,128]{2,1,0:T(8,128)(2,1)} %bitcast.8, f32[8,2048]{1,0:T(8,128)S(1)} %get-tuple-element.54.refs_1_.rows_ref), custom_call_target="tpu_custom_call" | custom-call | bytes 2097152 | tf_op jit(solution)/shard_map/load/pallas_call | solution.py:145
  15.2 0.4 collective-permute-done.3.refs_0_
  15.6 0.1 collective-permute-done.4.refs_1_
  15.7 0.0 collective-permute-done.5.refs_2_
  15.7 2.7 %collective-permute-start.6 = (bf16[8,1408]{1,0:T(8,128)(2,1)S(1)}, bf16[8,1408]{1,0:T(8,128)(2,1)S(1)}, u32[]{:S(2)}, u32[]{:S(2)}) collective-permute-start(bf16[8,1408]{1,0:T(8,128)(2,1)S(1)} %stack.1.refs_1_.refs_0_), channel_id=1, source_target_pairs={{0,3},{1,2},{2,1},{3,0},{4,7},{5,6},{6,5},{7,4},{8,11},{9,10},{10,... | collective-permute-start | bytes 67592 | tf_op jit(solution)/shard_map/ppermute | solution.py:31
  18.4 0.5 collective-permute-start.7
  18.9 0.0 collective-permute-start.8
  18.9 0.1 fusion
  19.0 0.0 copy-start
  19.0 1.8 %load.7.value_ref = bf16[2,4096,128]{2,1,0:T(8,128)(2,1)S(1)} custom-call(bf16[2,4096,128]{2,1,0:T(8,128)(2,1)} %bitcast.9, bf16[8,1408]{1,0:T(8,128)(2,1)S(1)} %stack.1.refs_1_.refs_0_), custom_call_target="tpu_custom_call" | custom-call | bytes 2097152 | tf_op jit(solution)/shard_map/load/pallas_call | solution.py:145
  20.8 0.0 collective-permute-done.6.refs_3_
  20.8 1.3 %collective-permute-done.7.refs_2_ = bf16[8,1408]{1,0:T(8,128)(2,1)S(1)} collective-permute-done((bf16[8,1408]{1,0:T(8,128)(2,1)S(1)}, bf16[8,1408]{1,0:T(8,128)(2,1)S(1)}, u32[]{:S(2)}, u32[]{:S(2)}) %collective-permute-start.7) | collective-permute-done | bytes 22560 | tf_op jit(solution)/shard_map/ppermute | solution.py:31
  22.2 0.0 collective-permute-done.8.refs_1_
  22.2 0.1 broadcast_in_dim.10.lengths_ref
  22.3 1.7 %attend.1.refs_1_.refs_3_ = bf16[80,128]{1,0:T(8,128)(2,1)S(1)} custom-call(s32[2,128]{1,0:T(2,128)S(1)} %broadcast_in_dim.10.lengths_ref, f32[8,128]{1,0:T(8,128)S(1)} %bitcast.6, f32[8,128]{1,0:T(8,128)S(1)} %bitcast.7, bf16[2,4096,128]{2,1,0:T(8,128)(2,1)S(1)} %load.6.key_ref, bf16[2,4096,128]{2,1,0:T(8,128)(2,1)S(1)} %load.7.value_ref, ...), custom_call_target="tpu_custom_call" | custom-call | tf_op jit(solution)/shard_map/attend/pallas_call | solution.py:340
  24.0 0.6 collective-permute-start.10
  24.6 0.0 collective-permute-start.11
  24.6 1.6 %collective-permute-start.9 = (bf16[80,128]{1,0:T(8,128)(2,1)S(1)}, bf16[80,128]{1,0:T(8,128)(2,1)S(1)}, u32[]{:S(2)}, u32[]{:S(2)}) collective-permute-start(bf16[80,128]{1,0:T(8,128)(2,1)S(1)} %attend.1.refs_1_.refs_3_), channel_id=1, source_target_pairs={{0,3},{1,2},{2,1},{3,0},{4,7},{5,6},{6,5},{7,4},{8,11},{9,10},{10,... | collective-permute-start | bytes 61448 | tf_op jit(solution)/shard_map/ppermute | solution.py:31
  26.2 1.5 %load.8.upper_ref = bf16[512,2048]{1,0:T(8,128)(2,1)S(1)} custom-call(bf16[1024,2048]{1,0:T(8,128)(2,1)} %refs_0_.5, bf16[80,128]{1,0:T(8,128)(2,1)S(1)} %attend.1.refs_1_.refs_3_), custom_call_target="tpu_custom_call" | custom-call | bytes 2097152 | tf_op jit(solution)/shard_map/load/pallas_call | solution.py:145
  27.8 0.3 collective-permute-done.10.refs_1_
  28.0 0.0 copy-start.1
  28.0 0.3 combine.1
  28.3 1.8 %collective-permute-start.12 = (bf16[2,1024]{1,0:T(2,128)(2,1)S(1)}, bf16[2,1024]{1,0:T(2,128)(2,1)S(1)}, u32[]{:S(2)}, u32[]{:S(2)}) collective-permute-start(bf16[2,1024]{1,0:T(2,128)(2,1)S(1)} %get-tuple-element.73), channel_id=1, source_target_pairs={{0,13},{1,12},{2,15},{3,14},{4,9},{5,8},{6,11},{7,10},{8,5},{9,4},... | collective-permute-start | bytes 12296 | tf_op jit(solution)/shard_map/ppermute | solution.py:50
  30.2 2.2 %collective-permute-start.14 = (bf16[2,1024]{1,0:T(2,128)(2,1)S(1)}, bf16[2,1024]{1,0:T(2,128)(2,1)S(1)}, u32[]{:S(2)}, u32[]{:S(2)}) collective-permute-start(bf16[2,1024]{1,0:T(2,128)(2,1)S(1)} %get-tuple-element.75), channel_id=1, source_target_pairs={{0,5},{1,4},{2,7},{3,6},{4,1},{5,0},{6,3},{7,2},{8,13},{9,12},{10,... | collective-permute-start | bytes 12296 | tf_op jit(solution)/shard_map/ppermute | solution.py:50
  32.4 1.5 %load.9.lower_ref = bf16[512,2048]{1,0:T(8,128)(2,1)S(1)} custom-call(bf16[1024,2048]{1,0:T(8,128)(2,1)} %refs_0_.5, bf16[2,1024]{1,0:T(2,128)(2,1)S(1)} %get-tuple-element.81.refs_1_.refs_3_), custom_call_target="tpu_custom_call" | custom-call | bytes 2097152 | tf_op jit(solution)/shard_map/load/pallas_call | solution.py:145
  33.9 0.0 collective-permute-done.12.refs_0_
  33.9 0.2 collective-permute-done.13.refs_1_
  34.1 0.0 collective-permute-done.14.refs_2_
  34.1 0.9 %project_out.1 = (bf16[8,2048]{1,0:T(8,128)(2,1)S(1)}, bf16[8,2048]{1,0:T(8,128)(2,1)S(1)}, bf16[8,2048]{1,0:T(8,128)(2,1)S(1)}, bf16[8,2048]{1,0:T(8,128)(2,1)S(1)}) custom-call(bf16[512,2048]{1,0:T(8,128)(2,1)S(1)} %load.8.upper_ref, bf16[512,2048]{1,0:T(8,128)(2,1)S(1)} %load.9.lower_ref, bf16[2,1024]{1,0:T(2,128)(2,1)S(1)} %collective-permute-done.12.refs_0_, ...), custom_call_target="tpu_custom_call" | custom-call | tf_op jit(solution)/shard_map/project_out/pallas_call | solution.py:437
  35.0 1.9 %collective-permute-start.15 = (bf16[8,2048]{1,0:T(8,128)(2,1)S(1)}, bf16[8,2048]{1,0:T(8,128)(2,1)S(1)}, u32[]{:S(2)}, u32[]{:S(2)}) collective-permute-start(bf16[8,2048]{1,0:T(8,128)(2,1)S(1)} %get-tuple-element.82), channel_id=1, source_target_pairs={{0,12},{1,13},{2,14},{3,15},{4,8},{5,9},{6,10},{7,11},{8,4},{9,5},... | collective-permute-start | bytes 98312 | tf_op jit(solution)/shard_map/ppermute | solution.py:50
  37.0 1.0 %collective-permute-start.16 = (bf16[8,2048]{1,0:T(8,128)(2,1)S(1)}, bf16[8,2048]{1,0:T(8,128)(2,1)S(1)}, u32[]{:S(2)}, u32[]{:S(2)}) collective-permute-start(bf16[8,2048]{1,0:T(8,128)(2,1)S(1)} %get-tuple-element.83), channel_id=1, source_target_pairs={{0,8},{1,9},{2,10},{3,11},{4,12},{5,13},{6,14},{7,15},{8,0},{9,1},... | collective-permute-start | bytes 98312 | tf_op jit(solution)/shard_map/ppermute | solution.py:50
  37.9 1.5 %collective-permute-start.17 = (bf16[8,2048]{1,0:T(8,128)(2,1)S(1)}, bf16[8,2048]{1,0:T(8,128)(2,1)S(1)}, u32[]{:S(2)}, u32[]{:S(2)}) collective-permute-start(bf16[8,2048]{1,0:T(8,128)(2,1)S(1)} %get-tuple-element.84), channel_id=1, source_target_pairs={{0,4},{1,5},{2,6},{3,7},{4,0},{5,1},{6,2},{7,3},{8,12},{9,13},{10,... | collective-permute-start | bytes 98312 | tf_op jit(solution)/shard_map/ppermute | solution.py:50
  39.4 1.7 %collective-permute-done.15.refs_0_ = bf16[8,2048]{1,0:T(8,128)(2,1)S(1)} collective-permute-done((bf16[8,2048]{1,0:T(8,128)(2,1)S(1)}, bf16[8,2048]{1,0:T(8,128)(2,1)S(1)}, u32[]{:S(2)}, u32[]{:S(2)}) %collective-permute-start.15) | collective-permute-done | bytes 32800 | tf_op jit(solution)/shard_map/ppermute | solution.py:50
  41.1 1.2 %collective-permute-done.16.refs_1_ = bf16[8,2048]{1,0:T(8,128)(2,1)S(1)} collective-permute-done((bf16[8,2048]{1,0:T(8,128)(2,1)S(1)}, bf16[8,2048]{1,0:T(8,128)(2,1)S(1)}, u32[]{:S(2)}, u32[]{:S(2)}) %collective-permute-start.16) | collective-permute-done | bytes 32800 | tf_op jit(solution)/shard_map/ppermute | solution.py:50
  42.3 0.0 collective-permute-done.17.refs_2_
  42.3 2.0 %first_gate_up.1 = (bf16[8,3712]{1,0:T(8,128)(2,1)S(1)}, f32[2,2048]{1,0:T(2,128)S(1)}, bf16[8,2048]{1,0:T(8,128)(2,1)S(1)}) custom-call(f32[8,2048]{1,0:T(8,128)S(1)} %get-tuple-element.54.refs_1_.rows_ref, bf16[2048]{0:T(1024)(128)(2,1)S(1)} %get-tuple-element.55.gain_ref, bf16[2048,3584]{1,0:T(8,128)(2,1)S(1)} %copy-done, ...), custom_call_target="tpu_custom_call" | custom-call | flops 117440512 | bytes 14680064 | tf_op jit(solution)/shard_map/first_gate_up/pallas_call | solution.py:493
  44.3 0.0 collective-permute-start.18
  44.3 0.0 slice-start.1
  44.3 2.0 %second_gate_up.1.first_ref = bf16[8,3584]{1,0:T(8,128)(2,1)S(1)} custom-call(bf16[8,2048]{1,0:T(8,128)(2,1)S(1)} %get-tuple-element.88.scaled_ref, bf16[2048,3584]{1,0:T(8,128)(2,1)S(1)} %copy-done, bf16[2048,3584]{1,0:T(8,128)(2,1)S(1)} %copy-done.1), custom_call_target="tpu_custom_call" | custom-call | flops 117440512 | bytes 14680064 | tf_op jit(solution)/shard_map/second_gate_up/pallas_call | solution.py:515
  46.3 0.5 collective-permute-start.20
  46.8 0.0 collective-permute-done.18.second_ref
  46.9 1.4 %collective-permute-start.19 = (bf16[8,3712]{1,0:T(8,128)(2,1)S(1)}, bf16[8,3712]{1,0:T(8,128)(2,1)S(1)}, u32[]{:S(2)}, u32[]{:S(2)}) collective-permute-start(bf16[8,3712]{1,0:T(8,128)(2,1)S(1)} %pair_sum.2.one_near), channel_id=1, source_target_pairs={{0,2},{1,3},{2,0},{3,1},{4,6},{5,7},{6,4},{7,5},{8,10},{9,11},{10,... | collective-permute-start | bytes 178184 | tf_op jit(solution)/shard_map/ppermute | solution.py:31
  48.3 0.9 %collective-permute-start.21 = (bf16[8,3584]{1,0:T(8,128)(2,1)S(1)}, bf16[8,3584]{1,0:T(8,128)(2,1)S(1)}, u32[]{:S(2)}, u32[]{:S(2)}) collective-permute-start(bf16[8,3584]{1,0:T(8,128)(2,1)S(1)} %pair_sum.3.two_near), channel_id=1, source_target_pairs={{0,2},{1,3},{2,0},{3,1},{4,6},{5,7},{6,4},{7,5},{8,10},{9,11},{10,... | collective-permute-start | bytes 172040 | tf_op jit(solution)/shard_map/ppermute | solution.py:31
  49.1 3.4 %collective-permute-done.21.two_far = bf16[8,3584]{1,0:T(8,128)(2,1)S(1)} collective-permute-done((bf16[8,3584]{1,0:T(8,128)(2,1)S(1)}, bf16[8,3584]{1,0:T(8,128)(2,1)S(1)}, u32[]{:S(2)}, u32[]{:S(2)}) %collective-permute-start.21) | collective-permute-done | bytes 57376 | tf_op jit(solution)/shard_map/ppermute | solution.py:31
  52.5 0.0 collective-permute-done.19.one_far
  52.6 2.3 %project_down.1 = (bf16[2,2048]{1,0:T(2,128)(2,1)S(1)}, bf16[2,2048]{1,0:T(2,128)(2,1)S(1)}, bf16[2,2048]{1,0:T(2,128)(2,1)S(1)}, bf16[2,2048]{1,0:T(2,128)(2,1)S(1)}) custom-call(bf16[8,3712]{1,0:T(8,128)(2,1)S(1)} %pair_sum.2.one_near, bf16[8,3712]{1,0:T(8,128)(2,1)S(1)} %collective-permute-done.19.one_far, bf16[8,3584]{1,0:T(8,128)(2,1)S(1)} %pair_sum.3.two_near, ...), custom_call_target="tpu_custom_call" | custom-call | tf_op jit(solution)/shard_map/project_down/pallas_call | solution.py:558
  54.9 2.0 %collective-permute-start.22 = (bf16[2,2048]{1,0:T(2,128)(2,1)S(1)}, bf16[2,2048]{1,0:T(2,128)(2,1)S(1)}, u32[]{:S(2)}, u32[]{:S(2)}) collective-permute-start(bf16[2,2048]{1,0:T(2,128)(2,1)S(1)} %get-tuple-element.89), channel_id=1, source_target_pairs={{0,12},{1,13},{2,14},{3,15},{4,8},{5,9},{6,10},{7,11},{8,4},{9,5},... | collective-permute-start | bytes 24584 | tf_op jit(solution)/shard_map/ppermute | solution.py:50
  56.8 0.8 %collective-permute-start.23 = (bf16[2,2048]{1,0:T(2,128)(2,1)S(1)}, bf16[2,2048]{1,0:T(2,128)(2,1)S(1)}, u32[]{:S(2)}, u32[]{:S(2)}) collective-permute-start(bf16[2,2048]{1,0:T(2,128)(2,1)S(1)} %get-tuple-element.90), channel_id=1, source_target_pairs={{0,8},{1,9},{2,10},{3,11},{4,12},{5,13},{6,14},{7,15},{8,0},{9,1},... | collective-permute-start | bytes 24584 | tf_op jit(solution)/shard_map/ppermute | solution.py:50
  57.6 1.7 %collective-permute-start.24 = (bf16[2,2048]{1,0:T(2,128)(2,1)S(1)}, bf16[2,2048]{1,0:T(2,128)(2,1)S(1)}, u32[]{:S(2)}, u32[]{:S(2)}) collective-permute-start(bf16[2,2048]{1,0:T(2,128)(2,1)S(1)} %get-tuple-element.91), channel_id=1, source_target_pairs={{0,4},{1,5},{2,6},{3,7},{4,0},{5,1},{6,2},{7,3},{8,12},{9,13},{10,... | collective-permute-start | bytes 24584 | tf_op jit(solution)/shard_map/ppermute | solution.py:50
  59.3 1.1 %collective-permute-done.22.refs_0_ = bf16[2,2048]{1,0:T(2,128)(2,1)S(1)} collective-permute-done((bf16[2,2048]{1,0:T(2,128)(2,1)S(1)}, bf16[2,2048]{1,0:T(2,128)(2,1)S(1)}, u32[]{:S(2)}, u32[]{:S(2)}) %collective-permute-start.22) | collective-permute-done | bytes 8224 | tf_op jit(solution)/shard_map/ppermute | solution.py:50
  60.4 0.9 %collective-permute-done.23.refs_1_ = bf16[2,2048]{1,0:T(2,128)(2,1)S(1)} collective-permute-done((bf16[2,2048]{1,0:T(2,128)(2,1)S(1)}, bf16[2,2048]{1,0:T(2,128)(2,1)S(1)}, u32[]{:S(2)}, u32[]{:S(2)}) %collective-permute-start.23) | collective-permute-done | bytes 8224 | tf_op jit(solution)/shard_map/ppermute | solution.py:50
  61.4 0.0 collective-permute-done.24.refs_2_
  61.4 0.6 finish.1
  (23 shorter events, 0.1 us)
Async XLA Ops:
  0.0 8.4 %collective-permute-start = (bf16[2,2048]{1,0:T(2,128)(2,1)}, bf16[2,2048]{1,0:T(2,128)(2,1)S(1)}, u32[]{:S(2)}, u32[]{:S(2)}) collective-permute-start(bf16[2,2048]{1,0:T(2,128)(2,1)} %refs_5_.1), channel_id=1, source_target_pairs={{0,12},{4,8},{8,4},{12,0},{1,13},{5,9},{9,5},{13,1},{2,14},{6,10},... | collective-permute-start | bytes 24584 | tf_op jit(solution)/shard_map/ppermute | solution.py:31
  5.0 4.8 %collective-permute-start.1 = (bf16[2,2048]{1,0:T(2,128)(2,1)}, bf16[2,2048]{1,0:T(2,128)(2,1)S(1)}, u32[]{:S(2)}, u32[]{:S(2)}) collective-permute-start(bf16[2,2048]{1,0:T(2,128)(2,1)} %refs_5_.1), channel_id=1, source_target_pairs={{0,8},{4,12},{8,0},{12,4},{1,9},{5,13},{9,1},{13,5},{2,10},{6,14},... | collective-permute-start | bytes 24584 | tf_op jit(solution)/shard_map/ppermute | solution.py:31
  5.1 4.8 %collective-permute-start.2 = (bf16[2,2048]{1,0:T(2,128)(2,1)}, bf16[2,2048]{1,0:T(2,128)(2,1)S(1)}, u32[]{:S(2)}, u32[]{:S(2)}) collective-permute-start(bf16[2,2048]{1,0:T(2,128)(2,1)} %refs_5_.1), channel_id=1, source_target_pairs={{0,4},{4,0},{8,12},{12,8},{1,5},{5,1},{9,13},{13,9},{2,6},{6,2},{1... | collective-permute-start | bytes 24584 | tf_op jit(solution)/shard_map/ppermute | solution.py:31
  5.6 7.9 %copy-start.2 = (s32[8]{0:T(128)S(1)}, s32[8]{0:T(128)}, u32[]{:S(2)}) copy-start(s32[8]{0:T(128)} %param.23) | copy-start | bytes 100
  10.6 4.9 %collective-permute-start.3 = (bf16[2,1408]{1,0:T(2,128)(2,1)S(1)}, bf16[2,1408]{1,0:T(2,128)(2,1)S(1)}, u32[]{:S(2)}, u32[]{:S(2)}) collective-permute-start(bf16[2,1408]{1,0:T(2,128)(2,1)S(1)} %get-tuple-element.57), channel_id=1, source_target_pairs={{0,13},{1,12},{2,15},{3,14},{4,9},{5,8},{6,11},{7,10},{8,5},{9,4},... | collective-permute-start | bytes 16904 | tf_op jit(solution)/shard_map/ppermute | solution.py:50
  11.7 4.0 %collective-permute-start.4 = (bf16[2,1408]{1,0:T(2,128)(2,1)S(1)}, bf16[2,1408]{1,0:T(2,128)(2,1)S(1)}, u32[]{:S(2)}, u32[]{:S(2)}) collective-permute-start(bf16[2,1408]{1,0:T(2,128)(2,1)S(1)} %get-tuple-element.58), channel_id=1, source_target_pairs={{0,9},{1,8},{2,11},{3,10},{4,13},{5,12},{6,15},{7,14},{8,1},{9,0},... | collective-permute-start | bytes 16904 | tf_op jit(solution)/shard_map/ppermute | solution.py:50
  11.9 3.7 %collective-permute-start.5 = (bf16[2,1408]{1,0:T(2,128)(2,1)S(1)}, bf16[2,1408]{1,0:T(2,128)(2,1)S(1)}, u32[]{:S(2)}, u32[]{:S(2)}) collective-permute-start(bf16[2,1408]{1,0:T(2,128)(2,1)S(1)} %get-tuple-element.59), channel_id=1, source_target_pairs={{0,5},{1,4},{2,7},{3,6},{4,1},{5,0},{6,3},{7,2},{8,13},{9,12},{10,... | collective-permute-start | bytes 16904 | tf_op jit(solution)/shard_map/ppermute | solution.py:50
  15.7 5.1 %collective-permute-start.6 = (bf16[8,1408]{1,0:T(8,128)(2,1)S(1)}, bf16[8,1408]{1,0:T(8,128)(2,1)S(1)}, u32[]{:S(2)}, u32[]{:S(2)}) collective-permute-start(bf16[8,1408]{1,0:T(8,128)(2,1)S(1)} %stack.1.refs_1_.refs_0_), channel_id=1, source_target_pairs={{0,3},{1,2},{2,1},{3,0},{4,7},{5,6},{6,5},{7,4},{8,11},{9,10},{10,... | collective-permute-start | bytes 67592 | tf_op jit(solution)/shard_map/ppermute | solution.py:31
  18.4 3.8 %collective-permute-start.7 = (bf16[8,1408]{1,0:T(8,128)(2,1)S(1)}, bf16[8,1408]{1,0:T(8,128)(2,1)S(1)}, u32[]{:S(2)}, u32[]{:S(2)}) collective-permute-start(bf16[8,1408]{1,0:T(8,128)(2,1)S(1)} %stack.1.refs_1_.refs_0_), channel_id=1, source_target_pairs={{0,2},{1,3},{2,0},{3,1},{4,6},{5,7},{6,4},{7,5},{8,10},{9,11},{10,... | collective-permute-start | bytes 67592 | tf_op jit(solution)/shard_map/ppermute | solution.py:31
  18.9 3.3 %collective-permute-start.8 = (bf16[8,1408]{1,0:T(8,128)(2,1)S(1)}, bf16[8,1408]{1,0:T(8,128)(2,1)S(1)}, u32[]{:S(2)}, u32[]{:S(2)}) collective-permute-start(bf16[8,1408]{1,0:T(8,128)(2,1)S(1)} %stack.1.refs_1_.refs_0_), channel_id=1, source_target_pairs={{0,1},{1,0},{2,3},{3,2},{4,5},{5,4},{6,7},{7,6},{8,9},{9,8},{10,11... | collective-permute-start | bytes 67592 | tf_op jit(solution)/shard_map/ppermute | solution.py:31
  19.0 9.0 %copy-start = (bf16[2048,3584]{1,0:T(8,128)(2,1)S(1)}, bf16[2048,3584]{1,0:T(8,128)(2,1)}, u32[]{:S(2)}) copy-start(bf16[2048,3584]{1,0:T(8,128)(2,1)} %gate_ref.3) | copy-start | bytes 44040196
  24.0 4.0 %collective-permute-start.10 = (bf16[80,128]{1,0:T(8,128)(2,1)S(1)}, bf16[80,128]{1,0:T(8,128)(2,1)S(1)}, u32[]{:S(2)}, u32[]{:S(2)}) collective-permute-start(bf16[80,128]{1,0:T(8,128)(2,1)S(1)} %attend.1.refs_1_.refs_3_), channel_id=1, source_target_pairs={{0,2},{1,3},{2,0},{3,1},{4,6},{5,7},{6,4},{7,5},{8,10},{9,11},{10,... | collective-permute-start | bytes 61448 | tf_op jit(solution)/shard_map/ppermute | solution.py:31
  24.6 3.4 %collective-permute-start.11 = (bf16[80,128]{1,0:T(8,128)(2,1)S(1)}, bf16[80,128]{1,0:T(8,128)(2,1)S(1)}, u32[]{:S(2)}, u32[]{:S(2)}) collective-permute-start(bf16[80,128]{1,0:T(8,128)(2,1)S(1)} %attend.1.refs_1_.refs_3_), channel_id=1, source_target_pairs={{0,1},{1,0},{2,3},{3,2},{4,5},{5,4},{6,7},{7,6},{8,9},{9,8},{10,11... | collective-permute-start | bytes 61448 | tf_op jit(solution)/shard_map/ppermute | solution.py:31
  24.6 3.4 %collective-permute-start.9 = (bf16[80,128]{1,0:T(8,128)(2,1)S(1)}, bf16[80,128]{1,0:T(8,128)(2,1)S(1)}, u32[]{:S(2)}, u32[]{:S(2)}) collective-permute-start(bf16[80,128]{1,0:T(8,128)(2,1)S(1)} %attend.1.refs_1_.refs_3_), channel_id=1, source_target_pairs={{0,3},{1,2},{2,1},{3,0},{4,7},{5,6},{6,5},{7,4},{8,11},{9,10},{10,... | collective-permute-start | bytes 61448 | tf_op jit(solution)/shard_map/ppermute | solution.py:31
  28.0 6.1 %copy-start.1 = (bf16[2048,3584]{1,0:T(8,128)(2,1)S(1)}, bf16[2048,3584]{1,0:T(8,128)(2,1)}, u32[]{:S(2)}) copy-start(bf16[2048,3584]{1,0:T(8,128)(2,1)} %up_ref.3) | copy-start | bytes 44040196
  28.3 5.6 %collective-permute-start.12 = (bf16[2,1024]{1,0:T(2,128)(2,1)S(1)}, bf16[2,1024]{1,0:T(2,128)(2,1)S(1)}, u32[]{:S(2)}, u32[]{:S(2)}) collective-permute-start(bf16[2,1024]{1,0:T(2,128)(2,1)S(1)} %get-tuple-element.73), channel_id=1, source_target_pairs={{0,13},{1,12},{2,15},{3,14},{4,9},{5,8},{6,11},{7,10},{8,5},{9,4},... | collective-permute-start | bytes 12296 | tf_op jit(solution)/shard_map/ppermute | solution.py:50
  30.2 3.9 %collective-permute-start.13 = (bf16[2,1024]{1,0:T(2,128)(2,1)S(1)}, bf16[2,1024]{1,0:T(2,128)(2,1)S(1)}, u32[]{:S(2)}, u32[]{:S(2)}) collective-permute-start(bf16[2,1024]{1,0:T(2,128)(2,1)S(1)} %get-tuple-element.74), channel_id=1, source_target_pairs={{0,9},{1,8},{2,11},{3,10},{4,13},{5,12},{6,15},{7,14},{8,1},{9,0},... | collective-permute-start | bytes 12296 | tf_op jit(solution)/shard_map/ppermute | solution.py:50
  30.2 3.9 %collective-permute-start.14 = (bf16[2,1024]{1,0:T(2,128)(2,1)S(1)}, bf16[2,1024]{1,0:T(2,128)(2,1)S(1)}, u32[]{:S(2)}, u32[]{:S(2)}) collective-permute-start(bf16[2,1024]{1,0:T(2,128)(2,1)S(1)} %get-tuple-element.75), channel_id=1, source_target_pairs={{0,5},{1,4},{2,7},{3,6},{4,1},{5,0},{6,3},{7,2},{8,13},{9,12},{10,... | collective-permute-start | bytes 12296 | tf_op jit(solution)/shard_map/ppermute | solution.py:50
  35.0 6.1 %collective-permute-start.15 = (bf16[8,2048]{1,0:T(8,128)(2,1)S(1)}, bf16[8,2048]{1,0:T(8,128)(2,1)S(1)}, u32[]{:S(2)}, u32[]{:S(2)}) collective-permute-start(bf16[8,2048]{1,0:T(8,128)(2,1)S(1)} %get-tuple-element.82), channel_id=1, source_target_pairs={{0,12},{1,13},{2,14},{3,15},{4,8},{5,9},{6,10},{7,11},{8,4},{9,5},... | collective-permute-start | bytes 98312 | tf_op jit(solution)/shard_map/ppermute | solution.py:50
  37.0 5.3 %collective-permute-start.16 = (bf16[8,2048]{1,0:T(8,128)(2,1)S(1)}, bf16[8,2048]{1,0:T(8,128)(2,1)S(1)}, u32[]{:S(2)}, u32[]{:S(2)}) collective-permute-start(bf16[8,2048]{1,0:T(8,128)(2,1)S(1)} %get-tuple-element.83), channel_id=1, source_target_pairs={{0,8},{1,9},{2,10},{3,11},{4,12},{5,13},{6,14},{7,15},{8,0},{9,1},... | collective-permute-start | bytes 98312 | tf_op jit(solution)/shard_map/ppermute | solution.py:50
  37.9 4.3 %collective-permute-start.17 = (bf16[8,2048]{1,0:T(8,128)(2,1)S(1)}, bf16[8,2048]{1,0:T(8,128)(2,1)S(1)}, u32[]{:S(2)}, u32[]{:S(2)}) collective-permute-start(bf16[8,2048]{1,0:T(8,128)(2,1)S(1)} %get-tuple-element.84), channel_id=1, source_target_pairs={{0,4},{1,5},{2,6},{3,7},{4,0},{5,1},{6,2},{7,3},{8,12},{9,13},{10,... | collective-permute-start | bytes 98312 | tf_op jit(solution)/shard_map/ppermute | solution.py:50
  44.3 2.6 %collective-permute-start.18 = (bf16[8,3712]{1,0:T(8,128)(2,1)S(1)}, bf16[8,3712]{1,0:T(8,128)(2,1)S(1)}, u32[]{:S(2)}, u32[]{:S(2)}) collective-permute-start(bf16[8,3712]{1,0:T(8,128)(2,1)S(1)} %get-tuple-element.87.first_ref), channel_id=1, source_target_pairs={{0,1},{1,0},{2,3},{3,2},{4,5},{5,4},{6,7},{7,6},{8,9},{9,8},{10,11... | collective-permute-start | bytes 178184 | tf_op jit(solution)/shard_map/ppermute | solution.py:31
  44.3 8.2 %slice-start = ((s8[14680064]{0:T(1024)(128)(4,1)}), s8[4194304]{0:T(1024)(128)(4,1)S(1)}, s32[]{:S(2)}) async-start(s8[14680064]{0:T(1024)(128)(4,1)} %bitcast.4), calls=%async_computation | async-start | bytes 8388608
  44.3 8.2 %slice-start.1 = ((s8[14680064]{0:T(1024)(128)(4,1)}), s8[4194304]{0:T(1024)(128)(4,1)S(1)}, s32[]{:S(2)}) async-start(s8[14680064]{0:T(1024)(128)(4,1)} %bitcast.4), calls=%async_computation.1 | async-start | bytes 8388608
  44.3 8.2 %slice-start.2 = ((s8[14680064]{0:T(1024)(128)(4,1)}), s8[4194304]{0:T(1024)(128)(4,1)S(1)}, s32[]{:S(2)}) async-start(s8[14680064]{0:T(1024)(128)(4,1)} %bitcast.4), calls=%async_computation.2 | async-start | bytes 8388608
  44.3 8.2 %slice-start.3 = ((s8[14680064]{0:T(1024)(128)(4,1)}), s8[2097152]{0:T(1024)(128)(4,1)S(1)}, s32[]{:S(2)}) async-start(s8[14680064]{0:T(1024)(128)(4,1)} %bitcast.4), calls=%async_computation.3 | async-start | bytes 4194304
  46.3 1.9 %collective-permute-start.20 = (bf16[8,3584]{1,0:T(8,128)(2,1)S(1)}, bf16[8,3584]{1,0:T(8,128)(2,1)S(1)}, u32[]{:S(2)}, u32[]{:S(2)}) collective-permute-start(bf16[8,3584]{1,0:T(8,128)(2,1)S(1)} %second_gate_up.1.first_ref), channel_id=1, source_target_pairs={{0,1},{1,0},{2,3},{3,2},{4,5},{5,4},{6,7},{7,6},{8,9},{9,8},{10,11... | collective-permute-start | bytes 172040 | tf_op jit(solution)/shard_map/ppermute | solution.py:31
  46.9 5.7 %collective-permute-start.19 = (bf16[8,3712]{1,0:T(8,128)(2,1)S(1)}, bf16[8,3712]{1,0:T(8,128)(2,1)S(1)}, u32[]{:S(2)}, u32[]{:S(2)}) collective-permute-start(bf16[8,3712]{1,0:T(8,128)(2,1)S(1)} %pair_sum.2.one_near), channel_id=1, source_target_pairs={{0,2},{1,3},{2,0},{3,1},{4,6},{5,7},{6,4},{7,5},{8,10},{9,11},{10,... | collective-permute-start | bytes 178184 | tf_op jit(solution)/shard_map/ppermute | solution.py:31
  48.3 4.2 %collective-permute-start.21 = (bf16[8,3584]{1,0:T(8,128)(2,1)S(1)}, bf16[8,3584]{1,0:T(8,128)(2,1)S(1)}, u32[]{:S(2)}, u32[]{:S(2)}) collective-permute-start(bf16[8,3584]{1,0:T(8,128)(2,1)S(1)} %pair_sum.3.two_near), channel_id=1, source_target_pairs={{0,2},{1,3},{2,0},{3,1},{4,6},{5,7},{6,4},{7,5},{8,10},{9,11},{10,... | collective-permute-start | bytes 172040 | tf_op jit(solution)/shard_map/ppermute | solution.py:31
  54.9 5.6 %collective-permute-start.22 = (bf16[2,2048]{1,0:T(2,128)(2,1)S(1)}, bf16[2,2048]{1,0:T(2,128)(2,1)S(1)}, u32[]{:S(2)}, u32[]{:S(2)}) collective-permute-start(bf16[2,2048]{1,0:T(2,128)(2,1)S(1)} %get-tuple-element.89), channel_id=1, source_target_pairs={{0,12},{1,13},{2,14},{3,15},{4,8},{5,9},{6,10},{7,11},{8,4},{9,5},... | collective-permute-start | bytes 24584 | tf_op jit(solution)/shard_map/ppermute | solution.py:50
  56.8 4.5 %collective-permute-start.23 = (bf16[2,2048]{1,0:T(2,128)(2,1)S(1)}, bf16[2,2048]{1,0:T(2,128)(2,1)S(1)}, u32[]{:S(2)}, u32[]{:S(2)}) collective-permute-start(bf16[2,2048]{1,0:T(2,128)(2,1)S(1)} %get-tuple-element.90), channel_id=1, source_target_pairs={{0,8},{1,9},{2,10},{3,11},{4,12},{5,13},{6,14},{7,15},{8,0},{9,1},... | collective-permute-start | bytes 24584 | tf_op jit(solution)/shard_map/ppermute | solution.py:50
  57.6 3.7 %collective-permute-start.24 = (bf16[2,2048]{1,0:T(2,128)(2,1)S(1)}, bf16[2,2048]{1,0:T(2,128)(2,1)S(1)}, u32[]{:S(2)}, u32[]{:S(2)}) collective-permute-start(bf16[2,2048]{1,0:T(2,128)(2,1)S(1)} %get-tuple-element.91), channel_id=1, source_target_pairs={{0,4},{1,5},{2,6},{3,7},{4,0},{5,1},{6,2},{7,3},{8,12},{9,13},{10,... | collective-permute-start | bytes 24584 | tf_op jit(solution)/shard_map/ppermute | solution.py:50

commit v16 on v15

--- a/solution.py
+++ b/solution.py
@@ -532,41 +532,79 @@
     return (gate / (1.0 + jnp.exp(-gate)) * total(count)).astype(jnp.bfloat16)
 
 
-def down_kernel(one_near, one_far, two_near, two_far, weight_ref, *refs):
-    hidden_s, out_s = refs[-2:]
-    first = (one_near.shape[1] - LANES) // 2
-    second = two_near.shape[1] // 2
+def first_down_kernel(count, near_ref, far_ref, weight_ref, token_ref, out_ref, scale_ref):
+    del token_ref
     squares = jnp.sum(
-        one_near[:, 2 * first :].astype(jnp.float32) + one_far[:, 2 * first :].astype(jnp.float32),
+        near_ref[:, 2 * count :].astype(jnp.float32) + far_ref[:, 2 * count :].astype(jnp.float32),
         axis=1,
         keepdims=True,
     )
     scale = lax.rsqrt(squares / D + epsilon)
-    hidden_s[:, :first] = hidden_of(one_near, one_far, scale, first)
-    hidden_s[:, first:] = hidden_of(two_near, two_far, scale, second)
+    scale_ref[...] = jnp.broadcast_to(scale, scale_ref.shape)
 
     def store(start, size, value):
-        out_s[:, pl.ds(start, size)] = value
-
-    product_tiles(hidden_s[...], weight_ref, store)
-    part_rows(out_s, refs[:-2])
-
-
-def project_down(one, two, weight, slots):
-    rows = one[0].shape[0]
-    depth, columns = weight.shape
-    return pl.pallas_call(
-        down_kernel,
+        out_ref[:, pl.ds(start, size)] = value
+
+    product_tiles(hidden_of(near_ref, far_ref, scale, count), weight_ref.at[:count], store)
+
+
+def first_down(near, far, weight, token, count):
+    rows = near.shape[0]
+    return pl.pallas_call(
+        functools.partial(first_down_kernel, count),
+        out_shape=(
+            jax.ShapeDtypeStruct((rows, weight.shape[1]), jnp.float32),
+            jax.ShapeDtypeStruct((rows, LANES), jnp.float32),
+        ),
+        in_specs=[in_vmem] * 3 + [in_place],
+        out_specs=(in_vmem,) * 2,
+        compiler_params=params(3),
+        cost_estimate=product_cost(count, weight.shape[1]),
+        name="first_down",
+    )(near, far, resident(weight), token)
+
+
+def second_down_kernel(count, near_ref, far_ref, weight_ref, part_ref, scale_ref, *refs):
+    out_s = refs[-1]
+    first = weight_ref.shape[0] - count
+
+    def store(start, size, value):
+        span = pl.ds(start, size)
+        out_s[:, span] = part_ref[:, span] + value
+
+    hidden = hidden_of(near_ref, far_ref, scale_ref[:, 0:1], count)
+    product_tiles(hidden, weight_ref.at[first:], store)
+    part_rows(out_s, refs[:-1])
+
+
+def second_down(near, far, weight, part, scale, slots):
+    rows, columns = part.shape
+    count = near.shape[1] // 2
+    return pl.pallas_call(
+        functools.partial(second_down_kernel, count),
         out_shape=(jax.ShapeDtypeStruct((rows // slots, columns), jnp.bfloat16),) * slots,
         in_specs=[in_vmem] * 5,
         out_specs=(in_vmem,) * slots,
-        scratch_shapes=[
-            pltpu.VMEM((rows, depth), jnp.bfloat16),
-            pltpu.VMEM((rows, columns), jnp.float32),
-        ],
+        scratch_shapes=[pltpu.VMEM(part.shape, jnp.float32)],
         compiler_params=params(3),
-        name="project_down",
-    )(*one, *two, resident(weight))
+        name="second_down",
+    )(near, far, resident(weight), part, scale)
+
+
+def hold_kernel(after_ref, weight_ref, out_ref):
+    del after_ref, weight_ref
+    out_ref[...] = jnp.zeros_like(out_ref)
+
+
+def hold(after, weight):
+    return pl.pallas_call(
+        hold_kernel,
+        out_shape=jax.ShapeDtypeStruct((8, LANES), jnp.float32),
+        in_specs=[in_place, in_place],
+        out_specs=in_vmem,
+        compiler_params=params(1),
+        name="hold",
+    )(after, resident(weight))
 
 
 def finish_kernel(updated_ref, *refs):
@@ -652,9 +690,9 @@
     for step in steps[:-1]:
         one = pair_sum(one, swap_with(one, "inner", step))
         two = pair_sum(two, swap_with(two, "inner", step))
-    one = (one, swap_with(one, "inner", steps[-1]))
-    two = (two, swap_with(two, "inner", steps[-1]))
-    pieces = project_down(one, two, w_down, slots)
+    token = hold(two, w_down)
+    part, scale = first_down(one, swap_with(one, "inner", steps[-1]), w_down, token, first)
+    pieces = second_down(two, swap_with(two, "inner", steps[-1]), w_down, part, scale, slots)
     parts = scatter_slots(pieces, 0)
     return finish(updated, parts)
 

time: 62.2 us -> 61.4 us (0.987)
  waiting for transfers between devices: 12 us -> 10.6 us
    ppermute x13, waiting for transfers between devices: 6.45 us -> 5 us  [swap_with(): return lax.ppermute(value, axis, [(i, i ^ step) for i in range(count)])]
    pallas_call x1 -> x3, Pallas kernels: 2.28 us -> 2.6 us  [the longest x1 1.32 us: second_down(): pl.pallas_call(functools.partial(second_down_kernel, count), out_shape=(j...]
  transfers between devices with their start and end apart: 25 -> 25, of which waited for: 11 -> 11; matrix products, arithmetic and copies ran while one was open for 0% -> 0% of each run, Pallas kernels for 18% -> 20%
where the time goes in v16:
time: 61.4 us; the launch traced here: 61.3 us
  starting transfers between devices  29.5 us (48%)
  Pallas kernels  20.3 us (33%)
  waiting for transfers between devices  10.6 us (17%)
    ppermute x12, starting transfers between devices, scatter_slots(): got.append(lax.ppermute(pieces[k], ('tensor', 'inner'), pairs))  15.7 us
    ppermute x13, starting transfers between devices, swap_with(): return lax.ppermute(value, axis, [(i, i ^ step) for i in range(count)])  13.8 us
    pallas_call x5, Pallas kernels, load(): pl.pallas_call(functools.partial(load_kernel, spans), out_shape=tuple((pl...  9.23 us
    ppermute x12, waiting for transfers between devices, scatter_slots(): got.append(lax.ppermute(pieces[k], ('tensor', 'inner'), pairs))  5.56 us
    ppermute x13, waiting for transfers between devices, swap_with(): return lax.ppermute(value, axis, [(i, i ^ step) for i in range(count)])  5 us
    pallas_call x1, Pallas kernels, first_gate_up(): pl.pallas_call(functools.partial(first_gate_up_kernel, slots, count), out...  2 us
    pallas_call x1, Pallas kernels, second_gate_up(): pl.pallas_call(functools.partial(second_gate_up_kernel, first, count), ou...  2 us
    pallas_call x1, Pallas kernels, attend(): pl.pallas_call(functools.partial(attend_kernel, slots, len(parts)), out_s...  1.73 us
  transfers between devices with their start and end apart: 25, of which 11 were waited for; matrix products, arithmetic and copies ran while one was open for 0% of the time, Pallas kernels for 20%

profile of v16, /device:TPU:0, one launch (start us, length us, event | category | flops | bytes accessed | tf_op | source)
XLA Modules:
  0.0 61.3 jit_solution(631249795029771927)
XLA Ops:
  0.0 5.0 %collective-permute-start = (bf16[2,2048]{1,0:T(2,128)(2,1)}, bf16[2,2048]{1,0:T(2,128)(2,1)S(1)}, u32[]{:S(2)}, u32[]{:S(2)}) collective-permute-start(bf16[2,2048]{1,0:T(2,128)(2,1)} %refs_5_.1), channel_id=1, source_target_pairs={{0,12},{4,8},{8,4},{12,0},{1,13},{5,9},{9,5},{13,1},{2,14},{6,10},... | collective-permute-start | bytes 24584 | tf_op jit(solution)/shard_map/ppermute | solution.py:31
  5.0 0.0 collective-permute-start.1
  5.1 0.6 collective-permute-start.2
  5.6 2.7 %load.5 = (bf16[2,2048]{1,0:T(2,128)(2,1)S(1)}, bf16[2048]{0:T(1024)(128)(2,1)S(1)}, bf16[2048]{0:T(1024)(128)(2,1)S(1)}, bf16[2048,256]{1,0:T(8,128)(2,1)S(1)}, bf16[2048,1024]{1,0:T(8,128)(2,1)S(1)}) custom-call(bf16[2,2048]{1,0:T(2,128)(2,1)} %refs_5_.1, bf16[2048]{0:T(1024)(128)(2,1)} %refs_1_.1, bf16[2048]{0:T(1024)(128)(2,1)} %refs_2_.1, ...), custom_call_target="tpu_custom_call" | custom-call | bytes 5259264 | tf_op jit(solution)/shard_map/load/pallas_call | solution.py:145
  8.4 0.0 collective-permute-done.refs_0_
  8.4 1.4 %collective-permute-done.1.refs_1_ = bf16[2,2048]{1,0:T(2,128)(2,1)S(1)} collective-permute-done((bf16[2,2048]{1,0:T(2,128)(2,1)}, bf16[2,2048]{1,0:T(2,128)(2,1)S(1)}, u32[]{:S(2)}, u32[]{:S(2)}) %collective-permute-start.1) | collective-permute-done | bytes 8224 | tf_op jit(solution)/shard_map/ppermute | solution.py:31
  9.8 0.0 collective-permute-done.2.refs_2_
  9.8 0.8 %project_qkv.1 = (f32[8,2048]{1,0:T(8,128)S(1)}, bf16[2,1408]{1,0:T(2,128)(2,1)S(1)}, bf16[2,1408]{1,0:T(2,128)(2,1)S(1)}, bf16[2,1408]{1,0:T(2,128)(2,1)S(1)}, bf16[2,1408]{1,0:T(2,128)(2,1)S(1)}) custom-call(bf16[2048]{0:T(1024)(128)(2,1)S(1)} %get-tuple-element.51.gain_ref, bf16[2048,1024]{1,0:T(8,128)(2,1)S(1)} %get-tuple-element.52.wq_ref, ...), custom_call_target="tpu_custom_call" | custom-call | tf_op jit(solution)/shard_map/project_qkv/pallas_call | solution.py:198
  10.6 1.1 %collective-permute-start.3 = (bf16[2,1408]{1,0:T(2,128)(2,1)S(1)}, bf16[2,1408]{1,0:T(2,128)(2,1)S(1)}, u32[]{:S(2)}, u32[]{:S(2)}) collective-permute-start(bf16[2,1408]{1,0:T(2,128)(2,1)S(1)} %get-tuple-element.59), channel_id=1, source_target_pairs={{0,13},{1,12},{2,15},{3,14},{4,9},{5,8},{6,11},{7,10},{8,5},{9,4},... | collective-permute-start | bytes 16904 | tf_op jit(solution)/shard_map/ppermute | solution.py:50
  11.7 0.2 collective-permute-start.4
  11.9 1.5 %collective-permute-start.5 = (bf16[2,1408]{1,0:T(2,128)(2,1)S(1)}, bf16[2,1408]{1,0:T(2,128)(2,1)S(1)}, u32[]{:S(2)}, u32[]{:S(2)}) collective-permute-start(bf16[2,1408]{1,0:T(2,128)(2,1)S(1)} %get-tuple-element.61), channel_id=1, source_target_pairs={{0,5},{1,4},{2,7},{3,6},{4,1},{5,0},{6,3},{7,2},{8,13},{9,12},{10,... | collective-permute-start | bytes 16904 | tf_op jit(solution)/shard_map/ppermute | solution.py:50
  13.5 0.1 fusion.4
  13.6 1.6 %load.6.key_ref = bf16[2,4096,128]{2,1,0:T(8,128)(2,1)S(1)} custom-call(bf16[2,4096,128]{2,1,0:T(8,128)(2,1)} %bitcast.8, f32[8,2048]{1,0:T(8,128)S(1)} %get-tuple-element.56.refs_1_.rows_ref), custom_call_target="tpu_custom_call" | custom-call | bytes 2097152 | tf_op jit(solution)/shard_map/load/pallas_call | solution.py:145
  15.2 0.4 collective-permute-done.3.refs_0_
  15.6 0.1 collective-permute-done.4.refs_1_
  15.7 2.7 %collective-permute-start.6 = (bf16[8,1408]{1,0:T(8,128)(2,1)S(1)}, bf16[8,1408]{1,0:T(8,128)(2,1)S(1)}, u32[]{:S(2)}, u32[]{:S(2)}) collective-permute-start(bf16[8,1408]{1,0:T(8,128)(2,1)S(1)} %stack.1.refs_1_.refs_0_), channel_id=1, source_target_pairs={{0,3},{1,2},{2,1},{3,0},{4,7},{5,6},{6,5},{7,4},{8,11},{9,10},{10,... | collective-permute-start | bytes 67592 | tf_op jit(solution)/shard_map/ppermute | solution.py:31
  18.4 0.5 collective-permute-start.7
  18.9 0.1 fusion
  19.0 0.0 copy-start
  19.0 1.8 %load.7.value_ref = bf16[2,4096,128]{2,1,0:T(8,128)(2,1)S(1)} custom-call(bf16[2,4096,128]{2,1,0:T(8,128)(2,1)} %bitcast.9, bf16[8,1408]{1,0:T(8,128)(2,1)S(1)} %stack.1.refs_1_.refs_0_), custom_call_target="tpu_custom_call" | custom-call | bytes 2097152 | tf_op jit(solution)/shard_map/load/pallas_call | solution.py:145
  20.8 1.3 %collective-permute-done.7.refs_2_ = bf16[8,1408]{1,0:T(8,128)(2,1)S(1)} collective-permute-done((bf16[8,1408]{1,0:T(8,128)(2,1)S(1)}, bf16[8,1408]{1,0:T(8,128)(2,1)S(1)}, u32[]{:S(2)}, u32[]{:S(2)}) %collective-permute-start.7) | collective-permute-done | bytes 22560 | tf_op jit(solution)/shard_map/ppermute | solution.py:31
  22.2 0.1 broadcast_in_dim.10.lengths_ref
  22.3 1.7 %attend.1.refs_1_.refs_3_ = bf16[80,128]{1,0:T(8,128)(2,1)S(1)} custom-call(s32[2,128]{1,0:T(2,128)S(1)} %broadcast_in_dim.10.lengths_ref, f32[8,128]{1,0:T(8,128)S(1)} %bitcast.6, f32[8,128]{1,0:T(8,128)S(1)} %bitcast.7, bf16[2,4096,128]{2,1,0:T(8,128)(2,1)S(1)} %load.6.key_ref, bf16[2,4096,128]{2,1,0:T(8,128)(2,1)S(1)} %load.7.value_ref, ...), custom_call_target="tpu_custom_call" | custom-call | tf_op jit(solution)/shard_map/attend/pallas_call | solution.py:340
  24.0 0.6 collective-permute-start.10
  24.6 0.0 collective-permute-start.11
  24.6 1.6 %collective-permute-start.9 = (bf16[80,128]{1,0:T(8,128)(2,1)S(1)}, bf16[80,128]{1,0:T(8,128)(2,1)S(1)}, u32[]{:S(2)}, u32[]{:S(2)}) collective-permute-start(bf16[80,128]{1,0:T(8,128)(2,1)S(1)} %attend.1.refs_1_.refs_3_), channel_id=1, source_target_pairs={{0,3},{1,2},{2,1},{3,0},{4,7},{5,6},{6,5},{7,4},{8,11},{9,10},{10,... | collective-permute-start | bytes 61448 | tf_op jit(solution)/shard_map/ppermute | solution.py:31
  26.2 1.5 %load.8.upper_ref = bf16[512,2048]{1,0:T(8,128)(2,1)S(1)} custom-call(bf16[1024,2048]{1,0:T(8,128)(2,1)} %refs_0_.5, bf16[80,128]{1,0:T(8,128)(2,1)S(1)} %attend.1.refs_1_.refs_3_), custom_call_target="tpu_custom_call" | custom-call | bytes 2097152 | tf_op jit(solution)/shard_map/load/pallas_call | solution.py:145
  27.8 0.3 collective-permute-done.10.refs_1_
  28.0 0.0 copy-start.1
  28.0 0.3 combine.1
  28.3 1.8 %collective-permute-start.12 = (bf16[2,1024]{1,0:T(2,128)(2,1)S(1)}, bf16[2,1024]{1,0:T(2,128)(2,1)S(1)}, u32[]{:S(2)}, u32[]{:S(2)}) collective-permute-start(bf16[2,1024]{1,0:T(2,128)(2,1)S(1)} %get-tuple-element.75), channel_id=1, source_target_pairs={{0,13},{1,12},{2,15},{3,14},{4,9},{5,8},{6,11},{7,10},{8,5},{9,4},... | collective-permute-start | bytes 12296 | tf_op jit(solution)/shard_map/ppermute | solution.py:50
  30.2 2.2 %collective-permute-start.14 = (bf16[2,1024]{1,0:T(2,128)(2,1)S(1)}, bf16[2,1024]{1,0:T(2,128)(2,1)S(1)}, u32[]{:S(2)}, u32[]{:S(2)}) collective-permute-start(bf16[2,1024]{1,0:T(2,128)(2,1)S(1)} %get-tuple-element.77), channel_id=1, source_target_pairs={{0,5},{1,4},{2,7},{3,6},{4,1},{5,0},{6,3},{7,2},{8,13},{9,12},{10,... | collective-permute-start | bytes 12296 | tf_op jit(solution)/shard_map/ppermute | solution.py:50
  32.4 1.5 %load.9.lower_ref = bf16[512,2048]{1,0:T(8,128)(2,1)S(1)} custom-call(bf16[1024,2048]{1,0:T(8,128)(2,1)} %refs_0_.5, bf16[2,1024]{1,0:T(2,128)(2,1)S(1)} %get-tuple-element.83.refs_1_.refs_3_), custom_call_target="tpu_custom_call" | custom-call | bytes 2097152 | tf_op jit(solution)/shard_map/load/pallas_call | solution.py:145
  33.9 0.0 collective-permute-done.12.refs_0_
  33.9 0.2 collective-permute-done.13.refs_1_
  34.1 0.0 collective-permute-done.14.refs_2_
  34.1 0.9 %project_out.1 = (bf16[8,2048]{1,0:T(8,128)(2,1)S(1)}, bf16[8,2048]{1,0:T(8,128)(2,1)S(1)}, bf16[8,2048]{1,0:T(8,128)(2,1)S(1)}, bf16[8,2048]{1,0:T(8,128)(2,1)S(1)}) custom-call(bf16[512,2048]{1,0:T(8,128)(2,1)S(1)} %load.8.upper_ref, bf16[512,2048]{1,0:T(8,128)(2,1)S(1)} %load.9.lower_ref, bf16[2,1024]{1,0:T(2,128)(2,1)S(1)} %collective-permute-done.12.refs_0_, ...), custom_call_target="tpu_custom_call" | custom-call | tf_op jit(solution)/shard_map/project_out/pallas_call | solution.py:437
  35.0 1.9 %collective-permute-start.15 = (bf16[8,2048]{1,0:T(8,128)(2,1)S(1)}, bf16[8,2048]{1,0:T(8,128)(2,1)S(1)}, u32[]{:S(2)}, u32[]{:S(2)}) collective-permute-start(bf16[8,2048]{1,0:T(8,128)(2,1)S(1)} %get-tuple-element.84), channel_id=1, source_target_pairs={{0,12},{1,13},{2,14},{3,15},{4,8},{5,9},{6,10},{7,11},{8,4},{9,5},... | collective-permute-start | bytes 98312 | tf_op jit(solution)/shard_map/ppermute | solution.py:50
  37.0 1.0 %collective-permute-start.16 = (bf16[8,2048]{1,0:T(8,128)(2,1)S(1)}, bf16[8,2048]{1,0:T(8,128)(2,1)S(1)}, u32[]{:S(2)}, u32[]{:S(2)}) collective-permute-start(bf16[8,2048]{1,0:T(8,128)(2,1)S(1)} %get-tuple-element.85), channel_id=1, source_target_pairs={{0,8},{1,9},{2,10},{3,11},{4,12},{5,13},{6,14},{7,15},{8,0},{9,1},... | collective-permute-start | bytes 98312 | tf_op jit(solution)/shard_map/ppermute | solution.py:50
  38.0 1.5 %collective-permute-start.17 = (bf16[8,2048]{1,0:T(8,128)(2,1)S(1)}, bf16[8,2048]{1,0:T(8,128)(2,1)S(1)}, u32[]{:S(2)}, u32[]{:S(2)}) collective-permute-start(bf16[8,2048]{1,0:T(8,128)(2,1)S(1)} %get-tuple-element.86), channel_id=1, source_target_pairs={{0,4},{1,5},{2,6},{3,7},{4,0},{5,1},{6,2},{7,3},{8,12},{9,13},{10,... | collective-permute-start | bytes 98312 | tf_op jit(solution)/shard_map/ppermute | solution.py:50
  39.5 1.7 %collective-permute-done.15.refs_0_ = bf16[8,2048]{1,0:T(8,128)(2,1)S(1)} collective-permute-done((bf16[8,2048]{1,0:T(8,128)(2,1)S(1)}, bf16[8,2048]{1,0:T(8,128)(2,1)S(1)}, u32[]{:S(2)}, u32[]{:S(2)}) %collective-permute-start.15) | collective-permute-done | bytes 32800 | tf_op jit(solution)/shard_map/ppermute | solution.py:50
  41.1 1.2 %collective-permute-done.16.refs_1_ = bf16[8,2048]{1,0:T(8,128)(2,1)S(1)} collective-permute-done((bf16[8,2048]{1,0:T(8,128)(2,1)S(1)}, bf16[8,2048]{1,0:T(8,128)(2,1)S(1)}, u32[]{:S(2)}, u32[]{:S(2)}) %collective-permute-start.16) | collective-permute-done | bytes 32800 | tf_op jit(solution)/shard_map/ppermute | solution.py:50
  42.3 0.0 collective-permute-done.17.refs_2_
  42.3 2.0 %first_gate_up.1 = (bf16[8,3712]{1,0:T(8,128)(2,1)S(1)}, f32[2,2048]{1,0:T(2,128)S(1)}, bf16[8,2048]{1,0:T(8,128)(2,1)S(1)}) custom-call(f32[8,2048]{1,0:T(8,128)S(1)} %get-tuple-element.56.refs_1_.rows_ref, bf16[2048]{0:T(1024)(128)(2,1)S(1)} %get-tuple-element.57.gain_ref, bf16[2048,3584]{1,0:T(8,128)(2,1)S(1)} %copy-done, ...), custom_call_target="tpu_custom_call" | custom-call | flops 117440512 | bytes 14680064 | tf_op jit(solution)/shard_map/first_gate_up/pallas_call | solution.py:493
  44.3 0.0 collective-permute-start.20
  44.3 0.0 slice-start.1
  44.3 2.0 %second_gate_up.1.first_ref = bf16[8,3584]{1,0:T(8,128)(2,1)S(1)} custom-call(bf16[8,2048]{1,0:T(8,128)(2,1)S(1)} %get-tuple-element.89.scaled_ref, bf16[2048,3584]{1,0:T(8,128)(2,1)S(1)} %copy-done, bf16[2048,3584]{1,0:T(8,128)(2,1)S(1)} %copy-done.2), custom_call_target="tpu_custom_call" | custom-call | flops 117440512 | bytes 14680064 | tf_op jit(solution)/shard_map/second_gate_up/pallas_call | solution.py:515
  46.3 0.5 collective-permute-start.18
  46.8 0.0 collective-permute-done.20.second_ref
  46.9 1.4 %collective-permute-start.21 = (bf16[8,3712]{1,0:T(8,128)(2,1)S(1)}, bf16[8,3712]{1,0:T(8,128)(2,1)S(1)}, u32[]{:S(2)}, u32[]{:S(2)}) collective-permute-start(bf16[8,3712]{1,0:T(8,128)(2,1)S(1)} %pair_sum.3.near_ref), channel_id=1, source_target_pairs={{0,2},{1,3},{2,0},{3,1},{4,6},{5,7},{6,4},{7,5},{8,10},{9,11},{10,... | collective-permute-start | bytes 178184 | tf_op jit(solution)/shard_map/ppermute | solution.py:31
  48.3 0.0 collective-permute-done.18.second_ref
  48.3 0.9 %collective-permute-start.19 = (bf16[8,3584]{1,0:T(8,128)(2,1)S(1)}, bf16[8,3584]{1,0:T(8,128)(2,1)S(1)}, u32[]{:S(2)}, u32[]{:S(2)}) collective-permute-start(bf16[8,3584]{1,0:T(8,128)(2,1)S(1)} %pair_sum.2.after_ref.near_ref), channel_id=1, source_target_pairs={{0,2},{1,3},{2,0},{3,1},{4,6},{5,7},{6,4},{7,5},{8,10},{9,11},{10,... | collective-permute-start | bytes 172040 | tf_op jit(solution)/shard_map/ppermute | solution.py:31
  49.2 0.4 slice-done.3
  49.6 1.9 %collective-permute-done.21.far_ref = bf16[8,3712]{1,0:T(8,128)(2,1)S(1)} collective-permute-done((bf16[8,3712]{1,0:T(8,128)(2,1)S(1)}, bf16[8,3712]{1,0:T(8,128)(2,1)S(1)}, u32[]{:S(2)}, u32[]{:S(2)}) %collective-permute-start.21) | collective-permute-done | bytes 59424 | tf_op jit(solution)/shard_map/ppermute | solution.py:31
  51.5 1.3 %first_down.1 = (f32[8,2048]{1,0:T(8,128)S(1)}, f32[8,128]{1,0:T(8,128)S(1)}) custom-call(bf16[8,3712]{1,0:T(8,128)(2,1)S(1)} %pair_sum.3.near_ref, bf16[8,3712]{1,0:T(8,128)(2,1)S(1)} %collective-permute-done.21.far_ref, bf16[3584,2048]{1,0:T(8,128)(2,1)S(1)} %bitcast.5, f32[8,128]{1,0:T(8,128)S(1)} %hold.1.token_ref), custom_call_target="tpu_custom_call" | custom-call | flops 58720256 | bytes 7340032 | tf_op jit(solution)/shard_map/first_down/pallas_call | solution.py:553
  52.8 0.0 collective-permute-done.19.far_ref
  52.8 1.3 %second_down.1 = (bf16[2,2048]{1,0:T(2,128)(2,1)S(1)}, bf16[2,2048]{1,0:T(2,128)(2,1)S(1)}, bf16[2,2048]{1,0:T(2,128)(2,1)S(1)}, bf16[2,2048]{1,0:T(2,128)(2,1)S(1)}) custom-call(bf16[8,3584]{1,0:T(8,128)(2,1)S(1)} %pair_sum.2.after_ref.near_ref, bf16[8,3584]{1,0:T(8,128)(2,1)S(1)} %collective-permute-done.19.far_ref, bf16[3584,2048]{1,0:T(8,128)(2,1)S(1)} %bitcast.5, ...), custom_call_target="tpu_custom_call" | custom-call | tf_op jit(solution)/shard_map/second_down/pallas_call | solution.py:583
  54.1 2.0 %collective-permute-start.22 = (bf16[2,2048]{1,0:T(2,128)(2,1)S(1)}, bf16[2,2048]{1,0:T(2,128)(2,1)S(1)}, u32[]{:S(2)}, u32[]{:S(2)}) collective-permute-start(bf16[2,2048]{1,0:T(2,128)(2,1)S(1)} %get-tuple-element.93), channel_id=1, source_target_pairs={{0,12},{1,13},{2,14},{3,15},{4,8},{5,9},{6,10},{7,11},{8,4},{9,5},... | collective-permute-start | bytes 24584 | tf_op jit(solution)/shard_map/ppermute | solution.py:50
  56.1 0.7 %collective-permute-start.23 = (bf16[2,2048]{1,0:T(2,128)(2,1)S(1)}, bf16[2,2048]{1,0:T(2,128)(2,1)S(1)}, u32[]{:S(2)}, u32[]{:S(2)}) collective-permute-start(bf16[2,2048]{1,0:T(2,128)(2,1)S(1)} %get-tuple-element.94), channel_id=1, source_target_pairs={{0,8},{1,9},{2,10},{3,11},{4,12},{5,13},{6,14},{7,15},{8,0},{9,1},... | collective-permute-start | bytes 24584 | tf_op jit(solution)/shard_map/ppermute | solution.py:50
  56.7 1.8 %collective-permute-start.24 = (bf16[2,2048]{1,0:T(2,128)(2,1)S(1)}, bf16[2,2048]{1,0:T(2,128)(2,1)S(1)}, u32[]{:S(2)}, u32[]{:S(2)}) collective-permute-start(bf16[2,2048]{1,0:T(2,128)(2,1)S(1)} %get-tuple-element.95), channel_id=1, source_target_pairs={{0,4},{1,5},{2,6},{3,7},{4,0},{5,1},{6,2},{7,3},{8,12},{9,13},{10,... | collective-permute-start | bytes 24584 | tf_op jit(solution)/shard_map/ppermute | solution.py:50
  58.6 1.1 %collective-permute-done.22.refs_0_ = bf16[2,2048]{1,0:T(2,128)(2,1)S(1)} collective-permute-done((bf16[2,2048]{1,0:T(2,128)(2,1)S(1)}, bf16[2,2048]{1,0:T(2,128)(2,1)S(1)}, u32[]{:S(2)}, u32[]{:S(2)}) %collective-permute-start.22) | collective-permute-done | bytes 8224 | tf_op jit(solution)/shard_map/ppermute | solution.py:50
  59.6 1.0 %collective-permute-done.23.refs_1_ = bf16[2,2048]{1,0:T(2,128)(2,1)S(1)} collective-permute-done((bf16[2,2048]{1,0:T(2,128)(2,1)S(1)}, bf16[2,2048]{1,0:T(2,128)(2,1)S(1)}, u32[]{:S(2)}, u32[]{:S(2)}) %collective-permute-start.23) | collective-permute-done | bytes 8224 | tf_op jit(solution)/shard_map/ppermute | solution.py:50
  60.6 0.0 collective-permute-done.24.refs_2_
  60.6 0.6 %finish.1 = bf16[2,2048]{1,0:T(2,128)(2,1)} custom-call(f32[2,2048]{1,0:T(2,128)S(1)} %get-tuple-element.88.updated_ref, bf16[2,2048]{1,0:T(2,128)(2,1)S(1)} %collective-permute-done.22.refs_0_, bf16[2,2048]{1,0:T(2,128)(2,1)S(1)} %collective-permute-done.23.refs_1_, bf16[2,2048]{1,0:T(2,128)(2,1)S(1)} %collective-permute-done.24.refs_2_, ...), custom_call_target="tpu_custom_call" | custom-call | tf_op jit(solution)/shard_map/finish/pallas_call | solution.py:616
  (27 shorter events, 0.1 us)
Async XLA Ops:
  0.0 8.4 %collective-permute-start = (bf16[2,2048]{1,0:T(2,128)(2,1)}, bf16[2,2048]{1,0:T(2,128)(2,1)S(1)}, u32[]{:S(2)}, u32[]{:S(2)}) collective-permute-start(bf16[2,2048]{1,0:T(2,128)(2,1)} %refs_5_.1), channel_id=1, source_target_pairs={{0,12},{4,8},{8,4},{12,0},{1,13},{5,9},{9,5},{13,1},{2,14},{6,10},... | collective-permute-start | bytes 24584 | tf_op jit(solution)/shard_map/ppermute | solution.py:31
  5.0 4.8 %collective-permute-start.1 = (bf16[2,2048]{1,0:T(2,128)(2,1)}, bf16[2,2048]{1,0:T(2,128)(2,1)S(1)}, u32[]{:S(2)}, u32[]{:S(2)}) collective-permute-start(bf16[2,2048]{1,0:T(2,128)(2,1)} %refs_5_.1), channel_id=1, source_target_pairs={{0,8},{4,12},{8,0},{12,4},{1,9},{5,13},{9,1},{13,5},{2,10},{6,14},... | collective-permute-start | bytes 24584 | tf_op jit(solution)/shard_map/ppermute | solution.py:31
  5.1 4.8 %collective-permute-start.2 = (bf16[2,2048]{1,0:T(2,128)(2,1)}, bf16[2,2048]{1,0:T(2,128)(2,1)S(1)}, u32[]{:S(2)}, u32[]{:S(2)}) collective-permute-start(bf16[2,2048]{1,0:T(2,128)(2,1)} %refs_5_.1), channel_id=1, source_target_pairs={{0,4},{4,0},{8,12},{12,8},{1,5},{5,1},{9,13},{13,9},{2,6},{6,2},{1... | collective-permute-start | bytes 24584 | tf_op jit(solution)/shard_map/ppermute | solution.py:31
  5.6 7.8 %copy-start.3 = (s32[8]{0:T(128)S(1)}, s32[8]{0:T(128)}, u32[]{:S(2)}) copy-start(s32[8]{0:T(128)} %param.23) | copy-start | bytes 100
  10.6 4.9 %collective-permute-start.3 = (bf16[2,1408]{1,0:T(2,128)(2,1)S(1)}, bf16[2,1408]{1,0:T(2,128)(2,1)S(1)}, u32[]{:S(2)}, u32[]{:S(2)}) collective-permute-start(bf16[2,1408]{1,0:T(2,128)(2,1)S(1)} %get-tuple-element.59), channel_id=1, source_target_pairs={{0,13},{1,12},{2,15},{3,14},{4,9},{5,8},{6,11},{7,10},{8,5},{9,4},... | collective-permute-start | bytes 16904 | tf_op jit(solution)/shard_map/ppermute | solution.py:50
  11.7 4.0 %collective-permute-start.4 = (bf16[2,1408]{1,0:T(2,128)(2,1)S(1)}, bf16[2,1408]{1,0:T(2,128)(2,1)S(1)}, u32[]{:S(2)}, u32[]{:S(2)}) collective-permute-start(bf16[2,1408]{1,0:T(2,128)(2,1)S(1)} %get-tuple-element.60), channel_id=1, source_target_pairs={{0,9},{1,8},{2,11},{3,10},{4,13},{5,12},{6,15},{7,14},{8,1},{9,0},... | collective-permute-start | bytes 16904 | tf_op jit(solution)/shard_map/ppermute | solution.py:50
  11.9 3.7 %collective-permute-start.5 = (bf16[2,1408]{1,0:T(2,128)(2,1)S(1)}, bf16[2,1408]{1,0:T(2,128)(2,1)S(1)}, u32[]{:S(2)}, u32[]{:S(2)}) collective-permute-start(bf16[2,1408]{1,0:T(2,128)(2,1)S(1)} %get-tuple-element.61), channel_id=1, source_target_pairs={{0,5},{1,4},{2,7},{3,6},{4,1},{5,0},{6,3},{7,2},{8,13},{9,12},{10,... | collective-permute-start | bytes 16904 | tf_op jit(solution)/shard_map/ppermute | solution.py:50
  15.7 5.1 %collective-permute-start.6 = (bf16[8,1408]{1,0:T(8,128)(2,1)S(1)}, bf16[8,1408]{1,0:T(8,128)(2,1)S(1)}, u32[]{:S(2)}, u32[]{:S(2)}) collective-permute-start(bf16[8,1408]{1,0:T(8,128)(2,1)S(1)} %stack.1.refs_1_.refs_0_), channel_id=1, source_target_pairs={{0,3},{1,2},{2,1},{3,0},{4,7},{5,6},{6,5},{7,4},{8,11},{9,10},{10,... | collective-permute-start | bytes 67592 | tf_op jit(solution)/shard_map/ppermute | solution.py:31
  18.4 3.8 %collective-permute-start.7 = (bf16[8,1408]{1,0:T(8,128)(2,1)S(1)}, bf16[8,1408]{1,0:T(8,128)(2,1)S(1)}, u32[]{:S(2)}, u32[]{:S(2)}) collective-permute-start(bf16[8,1408]{1,0:T(8,128)(2,1)S(1)} %stack.1.refs_1_.refs_0_), channel_id=1, source_target_pairs={{0,2},{1,3},{2,0},{3,1},{4,6},{5,7},{6,4},{7,5},{8,10},{9,11},{10,... | collective-permute-start | bytes 67592 | tf_op jit(solution)/shard_map/ppermute | solution.py:31
  18.9 3.3 %collective-permute-start.8 = (bf16[8,1408]{1,0:T(8,128)(2,1)S(1)}, bf16[8,1408]{1,0:T(8,128)(2,1)S(1)}, u32[]{:S(2)}, u32[]{:S(2)}) collective-permute-start(bf16[8,1408]{1,0:T(8,128)(2,1)S(1)} %stack.1.refs_1_.refs_0_), channel_id=1, source_target_pairs={{0,1},{1,0},{2,3},{3,2},{4,5},{5,4},{6,7},{7,6},{8,9},{9,8},{10,11... | collective-permute-start | bytes 67592 | tf_op jit(solution)/shard_map/ppermute | solution.py:31
  19.0 9.0 %copy-start = (bf16[2048,3584]{1,0:T(8,128)(2,1)S(1)}, bf16[2048,3584]{1,0:T(8,128)(2,1)}, u32[]{:S(2)}) copy-start(bf16[2048,3584]{1,0:T(8,128)(2,1)} %gate_ref.3) | copy-start | bytes 44040196
  24.0 4.0 %collective-permute-start.10 = (bf16[80,128]{1,0:T(8,128)(2,1)S(1)}, bf16[80,128]{1,0:T(8,128)(2,1)S(1)}, u32[]{:S(2)}, u32[]{:S(2)}) collective-permute-start(bf16[80,128]{1,0:T(8,128)(2,1)S(1)} %attend.1.refs_1_.refs_3_), channel_id=1, source_target_pairs={{0,2},{1,3},{2,0},{3,1},{4,6},{5,7},{6,4},{7,5},{8,10},{9,11},{10,... | collective-permute-start | bytes 61448 | tf_op jit(solution)/shard_map/ppermute | solution.py:31
  24.6 3.4 %collective-permute-start.11 = (bf16[80,128]{1,0:T(8,128)(2,1)S(1)}, bf16[80,128]{1,0:T(8,128)(2,1)S(1)}, u32[]{:S(2)}, u32[]{:S(2)}) collective-permute-start(bf16[80,128]{1,0:T(8,128)(2,1)S(1)} %attend.1.refs_1_.refs_3_), channel_id=1, source_target_pairs={{0,1},{1,0},{2,3},{3,2},{4,5},{5,4},{6,7},{7,6},{8,9},{9,8},{10,11... | collective-permute-start | bytes 61448 | tf_op jit(solution)/shard_map/ppermute | solution.py:31
  24.6 3.4 %collective-permute-start.9 = (bf16[80,128]{1,0:T(8,128)(2,1)S(1)}, bf16[80,128]{1,0:T(8,128)(2,1)S(1)}, u32[]{:S(2)}, u32[]{:S(2)}) collective-permute-start(bf16[80,128]{1,0:T(8,128)(2,1)S(1)} %attend.1.refs_1_.refs_3_), channel_id=1, source_target_pairs={{0,3},{1,2},{2,1},{3,0},{4,7},{5,6},{6,5},{7,4},{8,11},{9,10},{10,... | collective-permute-start | bytes 61448 | tf_op jit(solution)/shard_map/ppermute | solution.py:31
  28.0 6.1 %copy-start.1 = (bf16[2048,3584]{1,0:T(8,128)(2,1)S(1)}, bf16[2048,3584]{1,0:T(8,128)(2,1)}, u32[]{:S(2)}) copy-start(bf16[2048,3584]{1,0:T(8,128)(2,1)} %up_ref.3) | copy-start | bytes 44040196
  28.3 5.6 %collective-permute-start.12 = (bf16[2,1024]{1,0:T(2,128)(2,1)S(1)}, bf16[2,1024]{1,0:T(2,128)(2,1)S(1)}, u32[]{:S(2)}, u32[]{:S(2)}) collective-permute-start(bf16[2,1024]{1,0:T(2,128)(2,1)S(1)} %get-tuple-element.75), channel_id=1, source_target_pairs={{0,13},{1,12},{2,15},{3,14},{4,9},{5,8},{6,11},{7,10},{8,5},{9,4},... | collective-permute-start | bytes 12296 | tf_op jit(solution)/shard_map/ppermute | solution.py:50
  30.2 3.9 %collective-permute-start.13 = (bf16[2,1024]{1,0:T(2,128)(2,1)S(1)}, bf16[2,1024]{1,0:T(2,128)(2,1)S(1)}, u32[]{:S(2)}, u32[]{:S(2)}) collective-permute-start(bf16[2,1024]{1,0:T(2,128)(2,1)S(1)} %get-tuple-element.76), channel_id=1, source_target_pairs={{0,9},{1,8},{2,11},{3,10},{4,13},{5,12},{6,15},{7,14},{8,1},{9,0},... | collective-permute-start | bytes 12296 | tf_op jit(solution)/shard_map/ppermute | solution.py:50
  30.2 3.9 %collective-permute-start.14 = (bf16[2,1024]{1,0:T(2,128)(2,1)S(1)}, bf16[2,1024]{1,0:T(2,128)(2,1)S(1)}, u32[]{:S(2)}, u32[]{:S(2)}) collective-permute-start(bf16[2,1024]{1,0:T(2,128)(2,1)S(1)} %get-tuple-element.77), channel_id=1, source_target_pairs={{0,5},{1,4},{2,7},{3,6},{4,1},{5,0},{6,3},{7,2},{8,13},{9,12},{10,... | collective-permute-start | bytes 12296 | tf_op jit(solution)/shard_map/ppermute | solution.py:50
  34.1 8.2 %copy-start.2 = (bf16[2048,3584]{1,0:T(8,128)(2,1)S(1)}, bf16[2048,3584]{1,0:T(8,128)(2,1)}, u32[]{:S(2)}) copy-start(bf16[2048,3584]{1,0:T(8,128)(2,1)} %up_ref.3) | copy-start | bytes 44040196
  35.0 6.1 %collective-permute-start.15 = (bf16[8,2048]{1,0:T(8,128)(2,1)S(1)}, bf16[8,2048]{1,0:T(8,128)(2,1)S(1)}, u32[]{:S(2)}, u32[]{:S(2)}) collective-permute-start(bf16[8,2048]{1,0:T(8,128)(2,1)S(1)} %get-tuple-element.84), channel_id=1, source_target_pairs={{0,12},{1,13},{2,14},{3,15},{4,8},{5,9},{6,10},{7,11},{8,4},{9,5},... | collective-permute-start | bytes 98312 | tf_op jit(solution)/shard_map/ppermute | solution.py:50
  37.0 5.3 %collective-permute-start.16 = (bf16[8,2048]{1,0:T(8,128)(2,1)S(1)}, bf16[8,2048]{1,0:T(8,128)(2,1)S(1)}, u32[]{:S(2)}, u32[]{:S(2)}) collective-permute-start(bf16[8,2048]{1,0:T(8,128)(2,1)S(1)} %get-tuple-element.85), channel_id=1, source_target_pairs={{0,8},{1,9},{2,10},{3,11},{4,12},{5,13},{6,14},{7,15},{8,0},{9,1},... | collective-permute-start | bytes 98312 | tf_op jit(solution)/shard_map/ppermute | solution.py:50
  38.0 4.3 %collective-permute-start.17 = (bf16[8,2048]{1,0:T(8,128)(2,1)S(1)}, bf16[8,2048]{1,0:T(8,128)(2,1)S(1)}, u32[]{:S(2)}, u32[]{:S(2)}) collective-permute-start(bf16[8,2048]{1,0:T(8,128)(2,1)S(1)} %get-tuple-element.86), channel_id=1, source_target_pairs={{0,4},{1,5},{2,6},{3,7},{4,0},{5,1},{6,2},{7,3},{8,12},{9,13},{10,... | collective-permute-start | bytes 98312 | tf_op jit(solution)/shard_map/ppermute | solution.py:50
  44.3 2.6 %collective-permute-start.20 = (bf16[8,3712]{1,0:T(8,128)(2,1)S(1)}, bf16[8,3712]{1,0:T(8,128)(2,1)S(1)}, u32[]{:S(2)}, u32[]{:S(2)}) collective-permute-start(bf16[8,3712]{1,0:T(8,128)(2,1)S(1)} %get-tuple-element.90.first_ref), channel_id=1, source_target_pairs={{0,1},{1,0},{2,3},{3,2},{4,5},{5,4},{6,7},{7,6},{8,9},{9,8},{10,11... | collective-permute-start | bytes 178184 | tf_op jit(solution)/shard_map/ppermute | solution.py:31
  44.3 4.9 %slice-start = ((s8[14680064]{0:T(1024)(128)(4,1)}), s8[4194304]{0:T(1024)(128)(4,1)S(1)}, s32[]{:S(2)}) async-start(s8[14680064]{0:T(1024)(128)(4,1)} %bitcast.4), calls=%async_computation | async-start | bytes 8388608
  44.3 4.9 %slice-start.1 = ((s8[14680064]{0:T(1024)(128)(4,1)}), s8[4194304]{0:T(1024)(128)(4,1)S(1)}, s32[]{:S(2)}) async-start(s8[14680064]{0:T(1024)(128)(4,1)} %bitcast.4), calls=%async_computation.1 | async-start | bytes 8388608
  44.3 4.8 %slice-start.2 = ((s8[14680064]{0:T(1024)(128)(4,1)}), s8[4194304]{0:T(1024)(128)(4,1)S(1)}, s32[]{:S(2)}) async-start(s8[14680064]{0:T(1024)(128)(4,1)} %bitcast.4), calls=%async_computation.2 | async-start | bytes 8388608
  44.3 5.2 %slice-start.3 = ((s8[14680064]{0:T(1024)(128)(4,1)}), s8[2097152]{0:T(1024)(128)(4,1)S(1)}, s32[]{:S(2)}) async-start(s8[14680064]{0:T(1024)(128)(4,1)} %bitcast.4), calls=%async_computation.3 | async-start | bytes 4194304
  46.3 1.9 %collective-permute-start.18 = (bf16[8,3584]{1,0:T(8,128)(2,1)S(1)}, bf16[8,3584]{1,0:T(8,128)(2,1)S(1)}, u32[]{:S(2)}, u32[]{:S(2)}) collective-permute-start(bf16[8,3584]{1,0:T(8,128)(2,1)S(1)} %second_gate_up.1.first_ref), channel_id=1, source_target_pairs={{0,1},{1,0},{2,3},{3,2},{4,5},{5,4},{6,7},{7,6},{8,9},{9,8},{10,11... | collective-permute-start | bytes 172040 | tf_op jit(solution)/shard_map/ppermute | solution.py:31
  46.9 4.6 %collective-permute-start.21 = (bf16[8,3712]{1,0:T(8,128)(2,1)S(1)}, bf16[8,3712]{1,0:T(8,128)(2,1)S(1)}, u32[]{:S(2)}, u32[]{:S(2)}) collective-permute-start(bf16[8,3712]{1,0:T(8,128)(2,1)S(1)} %pair_sum.3.near_ref), channel_id=1, source_target_pairs={{0,2},{1,3},{2,0},{3,1},{4,6},{5,7},{6,4},{7,5},{8,10},{9,11},{10,... | collective-permute-start | bytes 178184 | tf_op jit(solution)/shard_map/ppermute | solution.py:31
  48.3 4.5 %collective-permute-start.19 = (bf16[8,3584]{1,0:T(8,128)(2,1)S(1)}, bf16[8,3584]{1,0:T(8,128)(2,1)S(1)}, u32[]{:S(2)}, u32[]{:S(2)}) collective-permute-start(bf16[8,3584]{1,0:T(8,128)(2,1)S(1)} %pair_sum.2.after_ref.near_ref), channel_id=1, source_target_pairs={{0,2},{1,3},{2,0},{3,1},{4,6},{5,7},{6,4},{7,5},{8,10},{9,11},{10,... | collective-permute-start | bytes 172040 | tf_op jit(solution)/shard_map/ppermute | solution.py:31
  54.1 5.5 %collective-permute-start.22 = (bf16[2,2048]{1,0:T(2,128)(2,1)S(1)}, bf16[2,2048]{1,0:T(2,128)(2,1)S(1)}, u32[]{:S(2)}, u32[]{:S(2)}) collective-permute-start(bf16[2,2048]{1,0:T(2,128)(2,1)S(1)} %get-tuple-element.93), channel_id=1, source_target_pairs={{0,12},{1,13},{2,14},{3,15},{4,8},{5,9},{6,10},{7,11},{8,4},{9,5},... | collective-permute-start | bytes 24584 | tf_op jit(solution)/shard_map/ppermute | solution.py:50
  56.1 4.5 %collective-permute-start.23 = (bf16[2,2048]{1,0:T(2,128)(2,1)S(1)}, bf16[2,2048]{1,0:T(2,128)(2,1)S(1)}, u32[]{:S(2)}, u32[]{:S(2)}) collective-permute-start(bf16[2,2048]{1,0:T(2,128)(2,1)S(1)} %get-tuple-element.94), channel_id=1, source_target_pairs={{0,8},{1,9},{2,10},{3,11},{4,12},{5,13},{6,14},{7,15},{8,0},{9,1},... | collective-permute-start | bytes 24584 | tf_op jit(solution)/shard_map/ppermute | solution.py:50
  56.7 3.9 %collective-permute-start.24 = (bf16[2,2048]{1,0:T(2,128)(2,1)S(1)}, bf16[2,2048]{1,0:T(2,128)(2,1)S(1)}, u32[]{:S(2)}, u32[]{:S(2)}) collective-permute-start(bf16[2,2048]{1,0:T(2,128)(2,1)S(1)} %get-tuple-element.95), channel_id=1, source_target_pairs={{0,4},{1,5},{2,6},{3,7},{4,0},{5,1},{6,2},{7,3},{8,12},{9,13},{10,... | collective-permute-start | bytes 24584 | tf_op jit(solution)/shard_map/ppermute | solution.py:50

commit v17 on v16

--- a/solution.py
+++ b/solution.py
@@ -288,40 +288,42 @@
     place = column // KV_HEADS + inner_index * positions
     column_head = column % KV_HEADS
     lanes = lax.broadcasted_iota(jnp.int32, (HEADS, LANES), 1)
+    queries = [
+        query_s[pl.ds(r, HEADS, stride=own_rows), :].astype(jnp.bfloat16) for r in range(own_rows)
+    ]
+    scores = [
+        lax.dot_general(
+            queries[r], key_ref[r], (((1,), (1,)), ((), ())), preferred_element_type=jnp.float32
+        )
+        for r in range(own_rows)
+    ]
+    weights = []
+    mixtures = []
     for r in range(own_rows):
-        queries = query_s[pl.ds(r, HEADS, stride=own_rows), :].astype(jnp.bfloat16)
-        scores = (
-            lax.dot_general(
-                queries,
-                key_ref[r],
-                (((1,), (1,)), ((), ())),
-                preferred_element_type=jnp.float32,
-            )
-            * score_scale
-        )
         used = jnp.where(place < lengths_ref[r : r + 1, 0:1], column_head, -1)
-        masked = jnp.where(used == kv_head, scores, -1e30)
+        masked = jnp.where(used == kv_head, scores[r] * score_scale, -1e30)
         key_rows = 0.0
         value_rows = 0.0
         for g in range(KV_HEADS):
             key_rows = key_rows + jnp.where(kv_head == g, new_keys[g][r : r + 1], 0.0)
             value_rows = value_rows + jnp.where(kv_head == g, new_values[g][r : r + 1], 0.0)
         new_score = (
-            jnp.sum(queries.astype(jnp.float32) * key_rows, axis=1, keepdims=True) * score_scale
+            jnp.sum(queries[r].astype(jnp.float32) * key_rows, axis=1, keepdims=True) * score_scale
         )
         new_score = jnp.where(inner_index == 0, new_score, -1e30)
         peak = jnp.maximum(jnp.max(masked, axis=1, keepdims=True), new_score)
-        weights = jnp.exp(masked - peak)
+        weight = jnp.exp(masked - peak)
         new_weight = jnp.exp(new_score - peak)
-        totals = jnp.sum(weights, axis=1, keepdims=True) + new_weight
-        mixture = jnp.dot(
-            weights.astype(jnp.bfloat16), value_ref[r], preferred_element_type=jnp.float32
-        )
-        mixture = mixture + new_weight.astype(jnp.bfloat16).astype(jnp.float32) * value_rows
-        mixed_s[pl.ds(r, HEADS, stride=own_rows), :] = mixture
+        totals = jnp.sum(weight, axis=1, keepdims=True) + new_weight
+        weights.append(weight.astype(jnp.bfloat16))
+        mixtures.append(new_weight.astype(jnp.bfloat16).astype(jnp.float32) * value_rows)
         stats_s[pl.ds(r, HEADS, stride=own_rows), :] = spread(
             three_parts(peak), lanes, 0
         ) + spread(three_parts(totals), lanes, 4)
+    for r in range(own_rows):
+        mixed_s[pl.ds(r, HEADS, stride=own_rows), :] = mixtures[r] + jnp.dot(
+            weights[r], value_ref[r], preferred_element_type=jnp.float32
+        )
     heads = own_rows * HEADS
     out_ref[:heads, :] = mixed_s[...].astype(jnp.bfloat16)
     packed = stats_s[:all_rows, :]
@@ -674,8 +676,8 @@
 
     cut = w_out.shape[0] // 2
     (out_upper,) = load(w_out, after=shard, spans=[(0, cut)])
-    shards, out_upper = lax.optimization_barrier((exchange(shard, "inner")[::-1], out_upper))
-    pieces = combine(shards[::-1], [w_gate], all_rows, slots)
+    shards, out_upper = lax.optimization_barrier((exchange(shard, "inner"), out_upper))
+    pieces = combine(shards, [w_gate], all_rows, slots)
     (out_lower,) = load(w_out, after=pieces[0], spans=[(cut, w_out.shape[0] - cut)])
     pieces, out_lower = lax.optimization_barrier((scatter_slots(pieces, 1)[::-1], out_lower))
     parts = scatter_slots(project_out(pieces[::-1], out_upper, out_lower, [w_up]), 0)

time: 61.4 us -> 60.9 us (level)
  transfers between devices with their start and end apart: 25 -> 25, of which waited for: 11 -> 11; matrix products, arithmetic and copies ran while one was open for 0% -> 0% of each run, Pallas kernels for 20% -> 21%
where the time goes in v17:
time: 60.9 us; the launch traced here: 60.7 us
  starting transfers between devices  29.3 us (48%)
  Pallas kernels  20 us (33%)
  waiting for transfers between devices  10.4 us (17%)
  local copies, waits for them, and re-layouts  0.63 us (1%)
    ppermute x12, starting transfers between devices, scatter_slots(): got.append(lax.ppermute(pieces[k], ('tensor', 'inner'), pairs))  15.6 us
    ppermute x13, starting transfers between devices, swap_with(): return lax.ppermute(value, axis, [(i, i ^ step) for i in range(count)])  13.7 us
    pallas_call x5, Pallas kernels, load(): pl.pallas_call(functools.partial(load_kernel, spans), out_shape=tuple((pl...  9.26 us
    ppermute x12, waiting for transfers between devices, scatter_slots(): got.append(lax.ppermute(pieces[k], ('tensor', 'inner'), pairs))  5.45 us
    ppermute x13, waiting for transfers between devices, swap_with(): return lax.ppermute(value, axis, [(i, i ^ step) for i in range(count)])  5 us
    pallas_call x1, Pallas kernels, first_gate_up(): pl.pallas_call(functools.partial(first_gate_up_kernel, slots, count), out...  2 us
    pallas_call x1, Pallas kernels, second_gate_up(): pl.pallas_call(functools.partial(second_gate_up_kernel, first, count), ou...  2 us
    pallas_call x1, Pallas kernels, attend(): pl.pallas_call(functools.partial(attend_kernel, slots, len(parts)), out_s...  1.47 us
  transfers between devices with their start and end apart: 25, of which 11 were waited for; matrix products, arithmetic and copies ran while one was open for 0% of the time, Pallas kernels for 21%

profile of v17, /device:TPU:0, one launch (start us, length us, event | category | flops | bytes accessed | tf_op | source)
XLA Modules:
  0.0 60.7 jit_solution(8083260793738883069)
XLA Ops:
  0.0 5.0 %collective-permute-start = (bf16[2,2048]{1,0:T(2,128)(2,1)}, bf16[2,2048]{1,0:T(2,128)(2,1)S(1)}, u32[]{:S(2)}, u32[]{:S(2)}) collective-permute-start(bf16[2,2048]{1,0:T(2,128)(2,1)} %refs_5_.1), channel_id=1, source_target_pairs={{0,12},{4,8},{8,4},{12,0},{1,13},{5,9},{9,5},{13,1},{2,14},{6,10},... | collective-permute-start | bytes 24584 | tf_op jit(solution)/shard_map/ppermute | solution.py:31
  5.0 0.0 collective-permute-start.1
  5.1 0.6 collective-permute-start.2
  5.6 2.7 %load.5 = (bf16[2,2048]{1,0:T(2,128)(2,1)S(1)}, bf16[2048]{0:T(1024)(128)(2,1)S(1)}, bf16[2048]{0:T(1024)(128)(2,1)S(1)}, bf16[2048,256]{1,0:T(8,128)(2,1)S(1)}, bf16[2048,1024]{1,0:T(8,128)(2,1)S(1)}) custom-call(bf16[2,2048]{1,0:T(2,128)(2,1)} %refs_5_.1, bf16[2048]{0:T(1024)(128)(2,1)} %refs_1_.1, bf16[2048]{0:T(1024)(128)(2,1)} %refs_2_.1, ...), custom_call_target="tpu_custom_call" | custom-call | bytes 5259264 | tf_op jit(solution)/shard_map/load/pallas_call | solution.py:145
  8.4 0.0 collective-permute-done.refs_0_
  8.4 1.4 %collective-permute-done.1.refs_1_ = bf16[2,2048]{1,0:T(2,128)(2,1)S(1)} collective-permute-done((bf16[2,2048]{1,0:T(2,128)(2,1)}, bf16[2,2048]{1,0:T(2,128)(2,1)S(1)}, u32[]{:S(2)}, u32[]{:S(2)}) %collective-permute-start.1) | collective-permute-done | bytes 8224 | tf_op jit(solution)/shard_map/ppermute | solution.py:31
  9.8 0.0 collective-permute-done.2.refs_2_
  9.8 0.8 %project_qkv.1 = (f32[8,2048]{1,0:T(8,128)S(1)}, bf16[2,1408]{1,0:T(2,128)(2,1)S(1)}, bf16[2,1408]{1,0:T(2,128)(2,1)S(1)}, bf16[2,1408]{1,0:T(2,128)(2,1)S(1)}, bf16[2,1408]{1,0:T(2,128)(2,1)S(1)}) custom-call(bf16[2048]{0:T(1024)(128)(2,1)S(1)} %get-tuple-element.51.gain_ref, bf16[2048,1024]{1,0:T(8,128)(2,1)S(1)} %get-tuple-element.52.wq_ref, ...), custom_call_target="tpu_custom_call" | custom-call | tf_op jit(solution)/shard_map/project_qkv/pallas_call | solution.py:198
  10.6 1.1 %collective-permute-start.3 = (bf16[2,1408]{1,0:T(2,128)(2,1)S(1)}, bf16[2,1408]{1,0:T(2,128)(2,1)S(1)}, u32[]{:S(2)}, u32[]{:S(2)}) collective-permute-start(bf16[2,1408]{1,0:T(2,128)(2,1)S(1)} %get-tuple-element.59), channel_id=1, source_target_pairs={{0,13},{1,12},{2,15},{3,14},{4,9},{5,8},{6,11},{7,10},{8,5},{9,4},... | collective-permute-start | bytes 16904 | tf_op jit(solution)/shard_map/ppermute | solution.py:50
  11.7 0.2 collective-permute-start.4
  11.9 1.5 %collective-permute-start.5 = (bf16[2,1408]{1,0:T(2,128)(2,1)S(1)}, bf16[2,1408]{1,0:T(2,128)(2,1)S(1)}, u32[]{:S(2)}, u32[]{:S(2)}) collective-permute-start(bf16[2,1408]{1,0:T(2,128)(2,1)S(1)} %get-tuple-element.61), channel_id=1, source_target_pairs={{0,5},{1,4},{2,7},{3,6},{4,1},{5,0},{6,3},{7,2},{8,13},{9,12},{10,... | collective-permute-start | bytes 16904 | tf_op jit(solution)/shard_map/ppermute | solution.py:50
  13.5 0.1 fusion.4
  13.6 1.6 %load.6.key_ref = bf16[2,4096,128]{2,1,0:T(8,128)(2,1)S(1)} custom-call(bf16[2,4096,128]{2,1,0:T(8,128)(2,1)} %bitcast.8, f32[8,2048]{1,0:T(8,128)S(1)} %get-tuple-element.56.refs_1_.rows_ref), custom_call_target="tpu_custom_call" | custom-call | bytes 2097152 | tf_op jit(solution)/shard_map/load/pallas_call | solution.py:145
  15.2 0.4 collective-permute-done.3.refs_0_
  15.6 0.1 collective-permute-done.4.refs_1_
  15.7 0.0 collective-permute-done.5.refs_2_
  15.7 2.7 %collective-permute-start.6 = (bf16[8,1408]{1,0:T(8,128)(2,1)S(1)}, bf16[8,1408]{1,0:T(8,128)(2,1)S(1)}, u32[]{:S(2)}, u32[]{:S(2)}) collective-permute-start(bf16[8,1408]{1,0:T(8,128)(2,1)S(1)} %stack.1.refs_1_.refs_0_), channel_id=1, source_target_pairs={{0,3},{1,2},{2,1},{3,0},{4,7},{5,6},{6,5},{7,4},{8,11},{9,10},{10,... | collective-permute-start | bytes 67592 | tf_op jit(solution)/shard_map/ppermute | solution.py:31
  18.4 0.5 collective-permute-start.7
  18.9 0.0 collective-permute-start.8
  18.9 0.1 fusion
  19.0 0.0 copy-start
  19.0 1.8 %load.7.value_ref = bf16[2,4096,128]{2,1,0:T(8,128)(2,1)S(1)} custom-call(bf16[2,4096,128]{2,1,0:T(8,128)(2,1)} %bitcast.9, bf16[8,1408]{1,0:T(8,128)(2,1)S(1)} %stack.1.refs_1_.refs_0_), custom_call_target="tpu_custom_call" | custom-call | bytes 2097152 | tf_op jit(solution)/shard_map/load/pallas_call | solution.py:145
  20.8 0.0 collective-permute-done.6.refs_3_
  20.8 1.3 %collective-permute-done.7.refs_2_ = bf16[8,1408]{1,0:T(8,128)(2,1)S(1)} collective-permute-done((bf16[8,1408]{1,0:T(8,128)(2,1)S(1)}, bf16[8,1408]{1,0:T(8,128)(2,1)S(1)}, u32[]{:S(2)}, u32[]{:S(2)}) %collective-permute-start.7) | collective-permute-done | bytes 22560 | tf_op jit(solution)/shard_map/ppermute | solution.py:31
  22.2 0.0 collective-permute-done.8.refs_1_
  22.2 0.1 broadcast_in_dim.10.lengths_ref
  22.3 1.5 %attend.1.refs_1_.refs_3_ = bf16[80,128]{1,0:T(8,128)(2,1)S(1)} custom-call(s32[2,128]{1,0:T(2,128)S(1)} %broadcast_in_dim.10.lengths_ref, f32[8,128]{1,0:T(8,128)S(1)} %bitcast.6, f32[8,128]{1,0:T(8,128)S(1)} %bitcast.7, bf16[2,4096,128]{2,1,0:T(8,128)(2,1)S(1)} %load.6.key_ref, bf16[2,4096,128]{2,1,0:T(8,128)(2,1)S(1)} %load.7.value_ref, ...), custom_call_target="tpu_custom_call" | custom-call | tf_op jit(solution)/shard_map/attend/pallas_call | solution.py:342
  23.7 0.6 collective-permute-start.10
  24.3 0.0 collective-permute-start.11
  24.4 1.6 %collective-permute-start.9 = (bf16[80,128]{1,0:T(8,128)(2,1)S(1)}, bf16[80,128]{1,0:T(8,128)(2,1)S(1)}, u32[]{:S(2)}, u32[]{:S(2)}) collective-permute-start(bf16[80,128]{1,0:T(8,128)(2,1)S(1)} %attend.1.refs_1_.refs_3_), channel_id=1, source_target_pairs={{0,1},{1,0},{2,3},{3,2},{4,5},{5,4},{6,7},{7,6},{8,9},{9,8},{10,11... | collective-permute-start | bytes 61448 | tf_op jit(solution)/shard_map/ppermute | solution.py:31
  25.9 1.5 %load.8.upper_ref = bf16[512,2048]{1,0:T(8,128)(2,1)S(1)} custom-call(bf16[1024,2048]{1,0:T(8,128)(2,1)} %refs_0_.5, bf16[80,128]{1,0:T(8,128)(2,1)S(1)} %attend.1.refs_1_.refs_3_), custom_call_target="tpu_custom_call" | custom-call | bytes 2097152 | tf_op jit(solution)/shard_map/load/pallas_call | solution.py:145
  27.5 0.3 collective-permute-done.10.refs_1_
  27.8 0.0 copy-start.1
  27.8 0.3 combine.1
  28.0 1.7 %collective-permute-start.12 = (bf16[2,1024]{1,0:T(2,128)(2,1)S(1)}, bf16[2,1024]{1,0:T(2,128)(2,1)S(1)}, u32[]{:S(2)}, u32[]{:S(2)}) collective-permute-start(bf16[2,1024]{1,0:T(2,128)(2,1)S(1)} %get-tuple-element.75), channel_id=1, source_target_pairs={{0,13},{1,12},{2,15},{3,14},{4,9},{5,8},{6,11},{7,10},{8,5},{9,4},... | collective-permute-start | bytes 12296 | tf_op jit(solution)/shard_map/ppermute | solution.py:50
  29.7 0.2 collective-permute-start.13
  29.9 2.0 %collective-permute-start.14 = (bf16[2,1024]{1,0:T(2,128)(2,1)S(1)}, bf16[2,1024]{1,0:T(2,128)(2,1)S(1)}, u32[]{:S(2)}, u32[]{:S(2)}) collective-permute-start(bf16[2,1024]{1,0:T(2,128)(2,1)S(1)} %get-tuple-element.77), channel_id=1, source_target_pairs={{0,5},{1,4},{2,7},{3,6},{4,1},{5,0},{6,3},{7,2},{8,13},{9,12},{10,... | collective-permute-start | bytes 12296 | tf_op jit(solution)/shard_map/ppermute | solution.py:50
  31.9 1.6 %load.9.lower_ref = bf16[512,2048]{1,0:T(8,128)(2,1)S(1)} custom-call(bf16[1024,2048]{1,0:T(8,128)(2,1)} %refs_0_.5, bf16[2,1024]{1,0:T(2,128)(2,1)S(1)} %get-tuple-element.83.refs_1_.refs_3_), custom_call_target="tpu_custom_call" | custom-call | bytes 2097152 | tf_op jit(solution)/shard_map/load/pallas_call | solution.py:145
  33.5 0.1 collective-permute-done.13.refs_1_
  33.7 0.0 collective-permute-done.14.refs_2_
  33.7 0.9 %project_out.1 = (bf16[8,2048]{1,0:T(8,128)(2,1)S(1)}, bf16[8,2048]{1,0:T(8,128)(2,1)S(1)}, bf16[8,2048]{1,0:T(8,128)(2,1)S(1)}, bf16[8,2048]{1,0:T(8,128)(2,1)S(1)}) custom-call(bf16[512,2048]{1,0:T(8,128)(2,1)S(1)} %load.8.upper_ref, bf16[512,2048]{1,0:T(8,128)(2,1)S(1)} %load.9.lower_ref, bf16[2,1024]{1,0:T(2,128)(2,1)S(1)} %collective-permute-done.12.refs_0_, ...), custom_call_target="tpu_custom_call" | custom-call | tf_op jit(solution)/shard_map/project_out/pallas_call | solution.py:439
  34.6 1.9 %collective-permute-start.15 = (bf16[8,2048]{1,0:T(8,128)(2,1)S(1)}, bf16[8,2048]{1,0:T(8,128)(2,1)S(1)}, u32[]{:S(2)}, u32[]{:S(2)}) collective-permute-start(bf16[8,2048]{1,0:T(8,128)(2,1)S(1)} %get-tuple-element.84), channel_id=1, source_target_pairs={{0,12},{1,13},{2,14},{3,15},{4,8},{5,9},{6,10},{7,11},{8,4},{9,5},... | collective-permute-start | bytes 98312 | tf_op jit(solution)/shard_map/ppermute | solution.py:50
  36.6 1.2 %collective-permute-start.16 = (bf16[8,2048]{1,0:T(8,128)(2,1)S(1)}, bf16[8,2048]{1,0:T(8,128)(2,1)S(1)}, u32[]{:S(2)}, u32[]{:S(2)}) collective-permute-start(bf16[8,2048]{1,0:T(8,128)(2,1)S(1)} %get-tuple-element.85), channel_id=1, source_target_pairs={{0,8},{1,9},{2,10},{3,11},{4,12},{5,13},{6,14},{7,15},{8,0},{9,1},... | collective-permute-start | bytes 98312 | tf_op jit(solution)/shard_map/ppermute | solution.py:50
  37.7 1.3 %collective-permute-start.17 = (bf16[8,2048]{1,0:T(8,128)(2,1)S(1)}, bf16[8,2048]{1,0:T(8,128)(2,1)S(1)}, u32[]{:S(2)}, u32[]{:S(2)}) collective-permute-start(bf16[8,2048]{1,0:T(8,128)(2,1)S(1)} %get-tuple-element.86), channel_id=1, source_target_pairs={{0,4},{1,5},{2,6},{3,7},{4,0},{5,1},{6,2},{7,3},{8,12},{9,13},{10,... | collective-permute-start | bytes 98312 | tf_op jit(solution)/shard_map/ppermute | solution.py:50
  39.0 1.7 %collective-permute-done.15.refs_0_ = bf16[8,2048]{1,0:T(8,128)(2,1)S(1)} collective-permute-done((bf16[8,2048]{1,0:T(8,128)(2,1)S(1)}, bf16[8,2048]{1,0:T(8,128)(2,1)S(1)}, u32[]{:S(2)}, u32[]{:S(2)}) %collective-permute-start.15) | collective-permute-done | bytes 32800 | tf_op jit(solution)/shard_map/ppermute | solution.py:50
  40.7 1.1 %collective-permute-done.16.refs_1_ = bf16[8,2048]{1,0:T(8,128)(2,1)S(1)} collective-permute-done((bf16[8,2048]{1,0:T(8,128)(2,1)S(1)}, bf16[8,2048]{1,0:T(8,128)(2,1)S(1)}, u32[]{:S(2)}, u32[]{:S(2)}) %collective-permute-start.16) | collective-permute-done | bytes 32800 | tf_op jit(solution)/shard_map/ppermute | solution.py:50
  41.8 0.0 collective-permute-done.17.refs_2_
  41.8 2.0 %first_gate_up.1 = (bf16[8,3712]{1,0:T(8,128)(2,1)S(1)}, f32[2,2048]{1,0:T(2,128)S(1)}, bf16[8,2048]{1,0:T(8,128)(2,1)S(1)}) custom-call(f32[8,2048]{1,0:T(8,128)S(1)} %get-tuple-element.56.refs_1_.rows_ref, bf16[2048]{0:T(1024)(128)(2,1)S(1)} %get-tuple-element.57.gain_ref, bf16[2048,3584]{1,0:T(8,128)(2,1)S(1)} %copy-done, ...), custom_call_target="tpu_custom_call" | custom-call | flops 117440512 | bytes 14680064 | tf_op jit(solution)/shard_map/first_gate_up/pallas_call | solution.py:495
  43.8 0.0 collective-permute-start.20
  43.8 0.0 slice-start.1
  43.8 2.0 %second_gate_up.1.first_ref = bf16[8,3584]{1,0:T(8,128)(2,1)S(1)} custom-call(bf16[8,2048]{1,0:T(8,128)(2,1)S(1)} %get-tuple-element.89.scaled_ref, bf16[2048,3584]{1,0:T(8,128)(2,1)S(1)} %copy-done, bf16[2048,3584]{1,0:T(8,128)(2,1)S(1)} %copy-done.2), custom_call_target="tpu_custom_call" | custom-call | flops 117440512 | bytes 14680064 | tf_op jit(solution)/shard_map/second_gate_up/pallas_call | solution.py:517
  45.8 0.5 collective-permute-start.18
  46.3 1.3 %collective-permute-start.21 = (bf16[8,3712]{1,0:T(8,128)(2,1)S(1)}, bf16[8,3712]{1,0:T(8,128)(2,1)S(1)}, u32[]{:S(2)}, u32[]{:S(2)}) collective-permute-start(bf16[8,3712]{1,0:T(8,128)(2,1)S(1)} %pair_sum.3.near_ref), channel_id=1, source_target_pairs={{0,2},{1,3},{2,0},{3,1},{4,6},{5,7},{6,4},{7,5},{8,10},{9,11},{10,... | collective-permute-start | bytes 178184 | tf_op jit(solution)/shard_map/ppermute | solution.py:31
  47.6 0.9 %collective-permute-start.19 = (bf16[8,3584]{1,0:T(8,128)(2,1)S(1)}, bf16[8,3584]{1,0:T(8,128)(2,1)S(1)}, u32[]{:S(2)}, u32[]{:S(2)}) collective-permute-start(bf16[8,3584]{1,0:T(8,128)(2,1)S(1)} %pair_sum.2.after_ref.near_ref), channel_id=1, source_target_pairs={{0,2},{1,3},{2,0},{3,1},{4,6},{5,7},{6,4},{7,5},{8,10},{9,11},{10,... | collective-permute-start | bytes 172040 | tf_op jit(solution)/shard_map/ppermute | solution.py:31
  48.5 0.5 slice-done.3
  49.1 1.9 %collective-permute-done.21.far_ref = bf16[8,3712]{1,0:T(8,128)(2,1)S(1)} collective-permute-done((bf16[8,3712]{1,0:T(8,128)(2,1)S(1)}, bf16[8,3712]{1,0:T(8,128)(2,1)S(1)}, u32[]{:S(2)}, u32[]{:S(2)}) %collective-permute-start.21) | collective-permute-done | bytes 59424 | tf_op jit(solution)/shard_map/ppermute | solution.py:31
  51.0 1.3 %first_down.1 = (f32[8,2048]{1,0:T(8,128)S(1)}, f32[8,128]{1,0:T(8,128)S(1)}) custom-call(bf16[8,3712]{1,0:T(8,128)(2,1)S(1)} %pair_sum.3.near_ref, bf16[8,3712]{1,0:T(8,128)(2,1)S(1)} %collective-permute-done.21.far_ref, bf16[3584,2048]{1,0:T(8,128)(2,1)S(1)} %bitcast.5, f32[8,128]{1,0:T(8,128)S(1)} %hold.1.token_ref), custom_call_target="tpu_custom_call" | custom-call | flops 58720256 | bytes 7340032 | tf_op jit(solution)/shard_map/first_down/pallas_call | solution.py:555
  52.3 1.3 %second_down.1 = (bf16[2,2048]{1,0:T(2,128)(2,1)S(1)}, bf16[2,2048]{1,0:T(2,128)(2,1)S(1)}, bf16[2,2048]{1,0:T(2,128)(2,1)S(1)}, bf16[2,2048]{1,0:T(2,128)(2,1)S(1)}) custom-call(bf16[8,3584]{1,0:T(8,128)(2,1)S(1)} %pair_sum.2.after_ref.near_ref, bf16[8,3584]{1,0:T(8,128)(2,1)S(1)} %collective-permute-done.19.far_ref, bf16[3584,2048]{1,0:T(8,128)(2,1)S(1)} %bitcast.5, ...), custom_call_target="tpu_custom_call" | custom-call | tf_op jit(solution)/shard_map/second_down/pallas_call | solution.py:585
  53.6 2.0 %collective-permute-start.22 = (bf16[2,2048]{1,0:T(2,128)(2,1)S(1)}, bf16[2,2048]{1,0:T(2,128)(2,1)S(1)}, u32[]{:S(2)}, u32[]{:S(2)}) collective-permute-start(bf16[2,2048]{1,0:T(2,128)(2,1)S(1)} %get-tuple-element.93), channel_id=1, source_target_pairs={{0,12},{1,13},{2,14},{3,15},{4,8},{5,9},{6,10},{7,11},{8,4},{9,5},... | collective-permute-start | bytes 24584 | tf_op jit(solution)/shard_map/ppermute | solution.py:50
  55.6 0.7 %collective-permute-start.23 = (bf16[2,2048]{1,0:T(2,128)(2,1)S(1)}, bf16[2,2048]{1,0:T(2,128)(2,1)S(1)}, u32[]{:S(2)}, u32[]{:S(2)}) collective-permute-start(bf16[2,2048]{1,0:T(2,128)(2,1)S(1)} %get-tuple-element.94), channel_id=1, source_target_pairs={{0,8},{1,9},{2,10},{3,11},{4,12},{5,13},{6,14},{7,15},{8,0},{9,1},... | collective-permute-start | bytes 24584 | tf_op jit(solution)/shard_map/ppermute | solution.py:50
  56.3 1.8 %collective-permute-start.24 = (bf16[2,2048]{1,0:T(2,128)(2,1)S(1)}, bf16[2,2048]{1,0:T(2,128)(2,1)S(1)}, u32[]{:S(2)}, u32[]{:S(2)}) collective-permute-start(bf16[2,2048]{1,0:T(2,128)(2,1)S(1)} %get-tuple-element.95), channel_id=1, source_target_pairs={{0,4},{1,5},{2,6},{3,7},{4,0},{5,1},{6,2},{7,3},{8,12},{9,13},{10,... | collective-permute-start | bytes 24584 | tf_op jit(solution)/shard_map/ppermute | solution.py:50
  58.0 1.1 %collective-permute-done.22.refs_0_ = bf16[2,2048]{1,0:T(2,128)(2,1)S(1)} collective-permute-done((bf16[2,2048]{1,0:T(2,128)(2,1)S(1)}, bf16[2,2048]{1,0:T(2,128)(2,1)S(1)}, u32[]{:S(2)}, u32[]{:S(2)}) %collective-permute-start.22) | collective-permute-done | bytes 8224 | tf_op jit(solution)/shard_map/ppermute | solution.py:50
  59.1 1.0 %collective-permute-done.23.refs_1_ = bf16[2,2048]{1,0:T(2,128)(2,1)S(1)} collective-permute-done((bf16[2,2048]{1,0:T(2,128)(2,1)S(1)}, bf16[2,2048]{1,0:T(2,128)(2,1)S(1)}, u32[]{:S(2)}, u32[]{:S(2)}) %collective-permute-start.23) | collective-permute-done | bytes 8224 | tf_op jit(solution)/shard_map/ppermute | solution.py:50
  60.1 0.6 %finish.1 = bf16[2,2048]{1,0:T(2,128)(2,1)} custom-call(f32[2,2048]{1,0:T(2,128)S(1)} %get-tuple-element.88.updated_ref, bf16[2,2048]{1,0:T(2,128)(2,1)S(1)} %collective-permute-done.22.refs_0_, bf16[2,2048]{1,0:T(2,128)(2,1)S(1)} %collective-permute-done.23.refs_1_, bf16[2,2048]{1,0:T(2,128)(2,1)S(1)} %collective-permute-done.24.refs_2_, ...), custom_call_target="tpu_custom_call" | custom-call | tf_op jit(solution)/shard_map/finish/pallas_call | solution.py:618
  (27 shorter events, 0.1 us)
Async XLA Ops:
  0.0 8.4 %collective-permute-start = (bf16[2,2048]{1,0:T(2,128)(2,1)}, bf16[2,2048]{1,0:T(2,128)(2,1)S(1)}, u32[]{:S(2)}, u32[]{:S(2)}) collective-permute-start(bf16[2,2048]{1,0:T(2,128)(2,1)} %refs_5_.1), channel_id=1, source_target_pairs={{0,12},{4,8},{8,4},{12,0},{1,13},{5,9},{9,5},{13,1},{2,14},{6,10},... | collective-permute-start | bytes 24584 | tf_op jit(solution)/shard_map/ppermute | solution.py:31
  5.0 4.8 %collective-permute-start.1 = (bf16[2,2048]{1,0:T(2,128)(2,1)}, bf16[2,2048]{1,0:T(2,128)(2,1)S(1)}, u32[]{:S(2)}, u32[]{:S(2)}) collective-permute-start(bf16[2,2048]{1,0:T(2,128)(2,1)} %refs_5_.1), channel_id=1, source_target_pairs={{0,8},{4,12},{8,0},{12,4},{1,9},{5,13},{9,1},{13,5},{2,10},{6,14},... | collective-permute-start | bytes 24584 | tf_op jit(solution)/shard_map/ppermute | solution.py:31
  5.1 4.8 %collective-permute-start.2 = (bf16[2,2048]{1,0:T(2,128)(2,1)}, bf16[2,2048]{1,0:T(2,128)(2,1)S(1)}, u32[]{:S(2)}, u32[]{:S(2)}) collective-permute-start(bf16[2,2048]{1,0:T(2,128)(2,1)} %refs_5_.1), channel_id=1, source_target_pairs={{0,4},{4,0},{8,12},{12,8},{1,5},{5,1},{9,13},{13,9},{2,6},{6,2},{1... | collective-permute-start | bytes 24584 | tf_op jit(solution)/shard_map/ppermute | solution.py:31
  5.6 7.8 %copy-start.3 = (s32[8]{0:T(128)S(1)}, s32[8]{0:T(128)}, u32[]{:S(2)}) copy-start(s32[8]{0:T(128)} %param.23) | copy-start | bytes 100
  10.6 4.9 %collective-permute-start.3 = (bf16[2,1408]{1,0:T(2,128)(2,1)S(1)}, bf16[2,1408]{1,0:T(2,128)(2,1)S(1)}, u32[]{:S(2)}, u32[]{:S(2)}) collective-permute-start(bf16[2,1408]{1,0:T(2,128)(2,1)S(1)} %get-tuple-element.59), channel_id=1, source_target_pairs={{0,13},{1,12},{2,15},{3,14},{4,9},{5,8},{6,11},{7,10},{8,5},{9,4},... | collective-permute-start | bytes 16904 | tf_op jit(solution)/shard_map/ppermute | solution.py:50
  11.7 4.0 %collective-permute-start.4 = (bf16[2,1408]{1,0:T(2,128)(2,1)S(1)}, bf16[2,1408]{1,0:T(2,128)(2,1)S(1)}, u32[]{:S(2)}, u32[]{:S(2)}) collective-permute-start(bf16[2,1408]{1,0:T(2,128)(2,1)S(1)} %get-tuple-element.60), channel_id=1, source_target_pairs={{0,9},{1,8},{2,11},{3,10},{4,13},{5,12},{6,15},{7,14},{8,1},{9,0},... | collective-permute-start | bytes 16904 | tf_op jit(solution)/shard_map/ppermute | solution.py:50
  11.9 3.7 %collective-permute-start.5 = (bf16[2,1408]{1,0:T(2,128)(2,1)S(1)}, bf16[2,1408]{1,0:T(2,128)(2,1)S(1)}, u32[]{:S(2)}, u32[]{:S(2)}) collective-permute-start(bf16[2,1408]{1,0:T(2,128)(2,1)S(1)} %get-tuple-element.61), channel_id=1, source_target_pairs={{0,5},{1,4},{2,7},{3,6},{4,1},{5,0},{6,3},{7,2},{8,13},{9,12},{10,... | collective-permute-start | bytes 16904 | tf_op jit(solution)/shard_map/ppermute | solution.py:50
  15.7 5.1 %collective-permute-start.6 = (bf16[8,1408]{1,0:T(8,128)(2,1)S(1)}, bf16[8,1408]{1,0:T(8,128)(2,1)S(1)}, u32[]{:S(2)}, u32[]{:S(2)}) collective-permute-start(bf16[8,1408]{1,0:T(8,128)(2,1)S(1)} %stack.1.refs_1_.refs_0_), channel_id=1, source_target_pairs={{0,3},{1,2},{2,1},{3,0},{4,7},{5,6},{6,5},{7,4},{8,11},{9,10},{10,... | collective-permute-start | bytes 67592 | tf_op jit(solution)/shard_map/ppermute | solution.py:31
  18.4 3.8 %collective-permute-start.7 = (bf16[8,1408]{1,0:T(8,128)(2,1)S(1)}, bf16[8,1408]{1,0:T(8,128)(2,1)S(1)}, u32[]{:S(2)}, u32[]{:S(2)}) collective-permute-start(bf16[8,1408]{1,0:T(8,128)(2,1)S(1)} %stack.1.refs_1_.refs_0_), channel_id=1, source_target_pairs={{0,2},{1,3},{2,0},{3,1},{4,6},{5,7},{6,4},{7,5},{8,10},{9,11},{10,... | collective-permute-start | bytes 67592 | tf_op jit(solution)/shard_map/ppermute | solution.py:31
  18.9 3.3 %collective-permute-start.8 = (bf16[8,1408]{1,0:T(8,128)(2,1)S(1)}, bf16[8,1408]{1,0:T(8,128)(2,1)S(1)}, u32[]{:S(2)}, u32[]{:S(2)}) collective-permute-start(bf16[8,1408]{1,0:T(8,128)(2,1)S(1)} %stack.1.refs_1_.refs_0_), channel_id=1, source_target_pairs={{0,1},{1,0},{2,3},{3,2},{4,5},{5,4},{6,7},{7,6},{8,9},{9,8},{10,11... | collective-permute-start | bytes 67592 | tf_op jit(solution)/shard_map/ppermute | solution.py:31
  19.0 8.8 %copy-start = (bf16[2048,3584]{1,0:T(8,128)(2,1)S(1)}, bf16[2048,3584]{1,0:T(8,128)(2,1)}, u32[]{:S(2)}) copy-start(bf16[2048,3584]{1,0:T(8,128)(2,1)} %gate_ref.3) | copy-start | bytes 44040196
  23.7 4.0 %collective-permute-start.10 = (bf16[80,128]{1,0:T(8,128)(2,1)S(1)}, bf16[80,128]{1,0:T(8,128)(2,1)S(1)}, u32[]{:S(2)}, u32[]{:S(2)}) collective-permute-start(bf16[80,128]{1,0:T(8,128)(2,1)S(1)} %attend.1.refs_1_.refs_3_), channel_id=1, source_target_pairs={{0,2},{1,3},{2,0},{3,1},{4,6},{5,7},{6,4},{7,5},{8,10},{9,11},{10,... | collective-permute-start | bytes 61448 | tf_op jit(solution)/shard_map/ppermute | solution.py:31
  24.3 3.4 %collective-permute-start.11 = (bf16[80,128]{1,0:T(8,128)(2,1)S(1)}, bf16[80,128]{1,0:T(8,128)(2,1)S(1)}, u32[]{:S(2)}, u32[]{:S(2)}) collective-permute-start(bf16[80,128]{1,0:T(8,128)(2,1)S(1)} %attend.1.refs_1_.refs_3_), channel_id=1, source_target_pairs={{0,3},{1,2},{2,1},{3,0},{4,7},{5,6},{6,5},{7,4},{8,11},{9,10},{10,... | collective-permute-start | bytes 61448 | tf_op jit(solution)/shard_map/ppermute | solution.py:31
  24.4 3.4 %collective-permute-start.9 = (bf16[80,128]{1,0:T(8,128)(2,1)S(1)}, bf16[80,128]{1,0:T(8,128)(2,1)S(1)}, u32[]{:S(2)}, u32[]{:S(2)}) collective-permute-start(bf16[80,128]{1,0:T(8,128)(2,1)S(1)} %attend.1.refs_1_.refs_3_), channel_id=1, source_target_pairs={{0,1},{1,0},{2,3},{3,2},{4,5},{5,4},{6,7},{7,6},{8,9},{9,8},{10,11... | collective-permute-start | bytes 61448 | tf_op jit(solution)/shard_map/ppermute | solution.py:31
  27.8 5.9 %copy-start.1 = (bf16[2048,3584]{1,0:T(8,128)(2,1)S(1)}, bf16[2048,3584]{1,0:T(8,128)(2,1)}, u32[]{:S(2)}) copy-start(bf16[2048,3584]{1,0:T(8,128)(2,1)} %up_ref.3) | copy-start | bytes 44040196
  28.0 5.5 %collective-permute-start.12 = (bf16[2,1024]{1,0:T(2,128)(2,1)S(1)}, bf16[2,1024]{1,0:T(2,128)(2,1)S(1)}, u32[]{:S(2)}, u32[]{:S(2)}) collective-permute-start(bf16[2,1024]{1,0:T(2,128)(2,1)S(1)} %get-tuple-element.75), channel_id=1, source_target_pairs={{0,13},{1,12},{2,15},{3,14},{4,9},{5,8},{6,11},{7,10},{8,5},{9,4},... | collective-permute-start | bytes 12296 | tf_op jit(solution)/shard_map/ppermute | solution.py:50
  29.7 3.9 %collective-permute-start.13 = (bf16[2,1024]{1,0:T(2,128)(2,1)S(1)}, bf16[2,1024]{1,0:T(2,128)(2,1)S(1)}, u32[]{:S(2)}, u32[]{:S(2)}) collective-permute-start(bf16[2,1024]{1,0:T(2,128)(2,1)S(1)} %get-tuple-element.76), channel_id=1, source_target_pairs={{0,9},{1,8},{2,11},{3,10},{4,13},{5,12},{6,15},{7,14},{8,1},{9,0},... | collective-permute-start | bytes 12296 | tf_op jit(solution)/shard_map/ppermute | solution.py:50
  29.9 3.7 %collective-permute-start.14 = (bf16[2,1024]{1,0:T(2,128)(2,1)S(1)}, bf16[2,1024]{1,0:T(2,128)(2,1)S(1)}, u32[]{:S(2)}, u32[]{:S(2)}) collective-permute-start(bf16[2,1024]{1,0:T(2,128)(2,1)S(1)} %get-tuple-element.77), channel_id=1, source_target_pairs={{0,5},{1,4},{2,7},{3,6},{4,1},{5,0},{6,3},{7,2},{8,13},{9,12},{10,... | collective-permute-start | bytes 12296 | tf_op jit(solution)/shard_map/ppermute | solution.py:50
  33.7 8.1 %copy-start.2 = (bf16[2048,3584]{1,0:T(8,128)(2,1)S(1)}, bf16[2048,3584]{1,0:T(8,128)(2,1)}, u32[]{:S(2)}) copy-start(bf16[2048,3584]{1,0:T(8,128)(2,1)} %up_ref.3) | copy-start | bytes 44040196
  34.6 6.1 %collective-permute-start.15 = (bf16[8,2048]{1,0:T(8,128)(2,1)S(1)}, bf16[8,2048]{1,0:T(8,128)(2,1)S(1)}, u32[]{:S(2)}, u32[]{:S(2)}) collective-permute-start(bf16[8,2048]{1,0:T(8,128)(2,1)S(1)} %get-tuple-element.84), channel_id=1, source_target_pairs={{0,12},{1,13},{2,14},{3,15},{4,8},{5,9},{6,10},{7,11},{8,4},{9,5},... | collective-permute-start | bytes 98312 | tf_op jit(solution)/shard_map/ppermute | solution.py:50
  36.6 5.2 %collective-permute-start.16 = (bf16[8,2048]{1,0:T(8,128)(2,1)S(1)}, bf16[8,2048]{1,0:T(8,128)(2,1)S(1)}, u32[]{:S(2)}, u32[]{:S(2)}) collective-permute-start(bf16[8,2048]{1,0:T(8,128)(2,1)S(1)} %get-tuple-element.85), channel_id=1, source_target_pairs={{0,8},{1,9},{2,10},{3,11},{4,12},{5,13},{6,14},{7,15},{8,0},{9,1},... | collective-permute-start | bytes 98312 | tf_op jit(solution)/shard_map/ppermute | solution.py:50
  37.7 4.1 %collective-permute-start.17 = (bf16[8,2048]{1,0:T(8,128)(2,1)S(1)}, bf16[8,2048]{1,0:T(8,128)(2,1)S(1)}, u32[]{:S(2)}, u32[]{:S(2)}) collective-permute-start(bf16[8,2048]{1,0:T(8,128)(2,1)S(1)} %get-tuple-element.86), channel_id=1, source_target_pairs={{0,4},{1,5},{2,6},{3,7},{4,0},{5,1},{6,2},{7,3},{8,12},{9,13},{10,... | collective-permute-start | bytes 98312 | tf_op jit(solution)/shard_map/ppermute | solution.py:50
  43.8 2.6 %collective-permute-start.20 = (bf16[8,3712]{1,0:T(8,128)(2,1)S(1)}, bf16[8,3712]{1,0:T(8,128)(2,1)S(1)}, u32[]{:S(2)}, u32[]{:S(2)}) collective-permute-start(bf16[8,3712]{1,0:T(8,128)(2,1)S(1)} %get-tuple-element.90.first_ref), channel_id=1, source_target_pairs={{0,1},{1,0},{2,3},{3,2},{4,5},{5,4},{6,7},{7,6},{8,9},{9,8},{10,11... | collective-permute-start | bytes 178184 | tf_op jit(solution)/shard_map/ppermute | solution.py:31
  43.8 4.8 %slice-start = ((s8[14680064]{0:T(1024)(128)(4,1)}), s8[4194304]{0:T(1024)(128)(4,1)S(1)}, s32[]{:S(2)}) async-start(s8[14680064]{0:T(1024)(128)(4,1)} %bitcast.4), calls=%async_computation | async-start | bytes 8388608
  43.8 4.8 %slice-start.1 = ((s8[14680064]{0:T(1024)(128)(4,1)}), s8[4194304]{0:T(1024)(128)(4,1)S(1)}, s32[]{:S(2)}) async-start(s8[14680064]{0:T(1024)(128)(4,1)} %bitcast.4), calls=%async_computation.1 | async-start | bytes 8388608
  43.8 4.7 %slice-start.2 = ((s8[14680064]{0:T(1024)(128)(4,1)}), s8[4194304]{0:T(1024)(128)(4,1)S(1)}, s32[]{:S(2)}) async-start(s8[14680064]{0:T(1024)(128)(4,1)} %bitcast.4), calls=%async_computation.2 | async-start | bytes 8388608
  43.8 5.2 %slice-start.3 = ((s8[14680064]{0:T(1024)(128)(4,1)}), s8[2097152]{0:T(1024)(128)(4,1)S(1)}, s32[]{:S(2)}) async-start(s8[14680064]{0:T(1024)(128)(4,1)} %bitcast.4), calls=%async_computation.3 | async-start | bytes 4194304
  45.8 1.8 %collective-permute-start.18 = (bf16[8,3584]{1,0:T(8,128)(2,1)S(1)}, bf16[8,3584]{1,0:T(8,128)(2,1)S(1)}, u32[]{:S(2)}, u32[]{:S(2)}) collective-permute-start(bf16[8,3584]{1,0:T(8,128)(2,1)S(1)} %second_gate_up.1.first_ref), channel_id=1, source_target_pairs={{0,1},{1,0},{2,3},{3,2},{4,5},{5,4},{6,7},{7,6},{8,9},{9,8},{10,11... | collective-permute-start | bytes 172040 | tf_op jit(solution)/shard_map/ppermute | solution.py:31
  46.3 4.6 %collective-permute-start.21 = (bf16[8,3712]{1,0:T(8,128)(2,1)S(1)}, bf16[8,3712]{1,0:T(8,128)(2,1)S(1)}, u32[]{:S(2)}, u32[]{:S(2)}) collective-permute-start(bf16[8,3712]{1,0:T(8,128)(2,1)S(1)} %pair_sum.3.near_ref), channel_id=1, source_target_pairs={{0,2},{1,3},{2,0},{3,1},{4,6},{5,7},{6,4},{7,5},{8,10},{9,11},{10,... | collective-permute-start | bytes 178184 | tf_op jit(solution)/shard_map/ppermute | solution.py:31
  47.6 4.6 %collective-permute-start.19 = (bf16[8,3584]{1,0:T(8,128)(2,1)S(1)}, bf16[8,3584]{1,0:T(8,128)(2,1)S(1)}, u32[]{:S(2)}, u32[]{:S(2)}) collective-permute-start(bf16[8,3584]{1,0:T(8,128)(2,1)S(1)} %pair_sum.2.after_ref.near_ref), channel_id=1, source_target_pairs={{0,2},{1,3},{2,0},{3,1},{4,6},{5,7},{6,4},{7,5},{8,10},{9,11},{10,... | collective-permute-start | bytes 172040 | tf_op jit(solution)/shard_map/ppermute | solution.py:31
  53.6 5.5 %collective-permute-start.22 = (bf16[2,2048]{1,0:T(2,128)(2,1)S(1)}, bf16[2,2048]{1,0:T(2,128)(2,1)S(1)}, u32[]{:S(2)}, u32[]{:S(2)}) collective-permute-start(bf16[2,2048]{1,0:T(2,128)(2,1)S(1)} %get-tuple-element.93), channel_id=1, source_target_pairs={{0,12},{1,13},{2,14},{3,15},{4,8},{5,9},{6,10},{7,11},{8,4},{9,5},... | collective-permute-start | bytes 24584 | tf_op jit(solution)/shard_map/ppermute | solution.py:50
  55.6 4.5 %collective-permute-start.23 = (bf16[2,2048]{1,0:T(2,128)(2,1)S(1)}, bf16[2,2048]{1,0:T(2,128)(2,1)S(1)}, u32[]{:S(2)}, u32[]{:S(2)}) collective-permute-start(bf16[2,2048]{1,0:T(2,128)(2,1)S(1)} %get-tuple-element.94), channel_id=1, source_target_pairs={{0,8},{1,9},{2,10},{3,11},{4,12},{5,13},{6,14},{7,15},{8,0},{9,1},... | collective-permute-start | bytes 24584 | tf_op jit(solution)/shard_map/ppermute | solution.py:50
  56.3 3.8 %collective-permute-start.24 = (bf16[2,2048]{1,0:T(2,128)(2,1)S(1)}, bf16[2,2048]{1,0:T(2,128)(2,1)S(1)}, u32[]{:S(2)}, u32[]{:S(2)}) collective-permute-start(bf16[2,2048]{1,0:T(2,128)(2,1)S(1)} %get-tuple-element.95), channel_id=1, source_target_pairs={{0,4},{1,5},{2,6},{3,7},{4,0},{5,1},{6,2},{7,3},{8,12},{9,13},{10,... | collective-permute-start | bytes 24584 | tf_op jit(solution)/shard_map/ppermute | solution.py:50

commit v18 on v17

--- a/solution.py
+++ b/solution.py
@@ -51,6 +51,20 @@
     return got
 
 
+def start_order(count):
+    half = count // 2
+    return [half] + [k for k in reversed(range(1, count)) if k != half] + [0]
+
+
+def in_start_order(slots):
+    return [slots[k] for k in start_order(len(slots))]
+
+
+def in_slot_order(refs):
+    order = start_order(len(refs))
+    return [refs[order.index(k)] for k in range(len(refs))]
+
+
 def steps_up(count):
     return [1 << n for n in range(count.bit_length() - 1)]
 
@@ -172,7 +186,7 @@
 def qkv_kernel(slots, gain_ref, wq_ref, wkv_ref, *refs):
     rows_ref = refs[slots]
     out_s, rows_s = refs[-2:]
-    wide = join_rows(refs[:slots][::-1], rows_s)
+    wide = join_rows(in_slot_order(refs[:slots]), rows_s)
     rows_ref[...] = wide
     total = jnp.sum(wide * wide, axis=1, keepdims=True)
     gain = gain_ref[...].astype(jnp.float32)[None, :]
@@ -209,7 +223,7 @@
         ],
         compiler_params=params(2),
         name="project_qkv",
-    )(gain, resident(w_query), resident(w_kv), *rows[::-1])
+    )(gain, resident(w_query), resident(w_kv), *in_start_order(rows))
 
 
 def stack_kernel(*refs):
@@ -281,6 +295,7 @@
         new_values.append(block.astype(jnp.bfloat16).astype(jnp.float32))
 
     score_scale = HEAD_DIM ** (-0.5)
+    two_scale = score_scale * math.log2(math.e)
     row = lax.broadcasted_iota(jnp.int32, (HEADS, 1), 0)
     head = ((row % slots) ^ tensor_index) * here + row // slots
     kv_head = head // GROUP
@@ -301,19 +316,18 @@
     mixtures = []
     for r in range(own_rows):
         used = jnp.where(place < lengths_ref[r : r + 1, 0:1], column_head, -1)
-        masked = jnp.where(used == kv_head, scores[r] * score_scale, -1e30)
+        masked = jnp.where(used == kv_head, scores[r], -1e30)
         key_rows = 0.0
         value_rows = 0.0
         for g in range(KV_HEADS):
             key_rows = key_rows + jnp.where(kv_head == g, new_keys[g][r : r + 1], 0.0)
             value_rows = value_rows + jnp.where(kv_head == g, new_values[g][r : r + 1], 0.0)
-        new_score = (
-            jnp.sum(queries[r].astype(jnp.float32) * key_rows, axis=1, keepdims=True) * score_scale
-        )
+        new_score = jnp.sum(queries[r].astype(jnp.float32) * key_rows, axis=1, keepdims=True)
         new_score = jnp.where(inner_index == 0, new_score, -1e30)
         peak = jnp.maximum(jnp.max(masked, axis=1, keepdims=True), new_score)
-        weight = jnp.exp(masked - peak)
-        new_weight = jnp.exp(new_score - peak)
+        weight = jnp.exp2((masked - peak) * two_scale)
+        new_weight = jnp.exp2((new_score - peak) * two_scale)
+        peak = peak * score_scale
         totals = jnp.sum(weight, axis=1, keepdims=True) + new_weight
         weights.append(weight.astype(jnp.bfloat16))
         mixtures.append(new_weight.astype(jnp.bfloat16).astype(jnp.float32) * value_rows)
@@ -504,7 +518,14 @@
         compiler_params=params(3),
         cost_estimate=product_cost(w_gate.shape[0], 2 * count),
         name="first_gate_up",
-    )(rows, gain, resident(w_gate), resident(w_up), *parts[::-1], *[resident(w) for w in later])
+    )(
+        rows,
+        gain,
+        resident(w_gate),
+        resident(w_up),
+        *in_start_order(parts),
+        *[resident(w) for w in later],
+    )
 
 
 def second_gate_up_kernel(first, count, scaled_ref, gate_ref, up_ref, *refs):
@@ -622,7 +643,7 @@
         out_specs=in_vmem,
         compiler_params=params(1),
         name="finish",
-    )(updated, *parts[::-1])
+    )(updated, *in_start_order(parts))
 
 
 def rotation_tables(positions, repeats):

time: 60.9 us -> 61.1 us (level)
  waiting for transfers between devices: 10.4 us -> 12.5 us
  starting transfers between devices: 29.3 us -> 27.3 us
    ppermute x12, waiting for transfers between devices: 5.45 us -> 7.67 us  [scatter_slots(): got.append(lax.ppermute(pieces[k], ('tensor', 'inner'), pairs))]
    ppermute x12, starting transfers between devices: 15.6 us -> 13.9 us  [scatter_slots(): got.append(lax.ppermute(pieces[k], ('tensor', 'inner'), pairs))]
  transfers between devices with their start and end apart: 25 -> 25, of which waited for: 11 -> 12; matrix products, arithmetic and copies ran while one was open for 0% -> 0% of each run, Pallas kernels for 21% -> 21%
where the time goes in v18:
time: 61.1 us; the launch traced here: 60.9 us
  starting transfers between devices  27.3 us (45%)
  Pallas kernels  20 us (33%)
  waiting for transfers between devices  12.5 us (20%)
  local copies, waits for them, and re-layouts  0.62 us (1%)
    ppermute x12, starting transfers between devices, scatter_slots(): got.append(lax.ppermute(pieces[k], ('tensor', 'inner'), pairs))  13.9 us
    ppermute x13, starting transfers between devices, swap_with(): return lax.ppermute(value, axis, [(i, i ^ step) for i in range(count)])  13.4 us
    pallas_call x5, Pallas kernels, load(): pl.pallas_call(functools.partial(load_kernel, spans), out_shape=tuple((pl...  9.26 us
    ppermute x12, waiting for transfers between devices, scatter_slots(): got.append(lax.ppermute(pieces[k], ('tensor', 'inner'), pairs))  7.67 us
    ppermute x13, waiting for transfers between devices, swap_with(): return lax.ppermute(value, axis, [(i, i ^ step) for i in range(count)])  4.88 us
    pallas_call x1, Pallas kernels, first_gate_up(): pl.pallas_call(functools.partial(first_gate_up_kernel, slots, count), out...  2 us
    pallas_call x1, Pallas kernels, second_gate_up(): pl.pallas_call(functools.partial(second_gate_up_kernel, first, count), ou...  2 us
    pallas_call x1, Pallas kernels, attend(): pl.pallas_call(functools.partial(attend_kernel, slots, len(parts)), out_s...  1.49 us
  transfers between devices with their start and end apart: 25, of which 12 were waited for; matrix products, arithmetic and copies ran while one was open for 0% of the time, Pallas kernels for 21%

profile of v18, /device:TPU:0, one launch (start us, length us, event | category | flops | bytes accessed | tf_op | source)
XLA Modules:
  0.0 60.9 jit_solution(14056022918876563508)
XLA Ops:
  0.0 4.0 %collective-permute-start = (bf16[2,2048]{1,0:T(2,128)(2,1)}, bf16[2,2048]{1,0:T(2,128)(2,1)S(1)}, u32[]{:S(2)}, u32[]{:S(2)}) collective-permute-start(bf16[2,2048]{1,0:T(2,128)(2,1)} %refs_5_.1), channel_id=1, source_target_pairs={{0,8},{4,12},{8,0},{12,4},{1,9},{5,13},{9,1},{13,5},{2,10},{6,14},... | collective-permute-start | bytes 24584 | tf_op jit(solution)/shard_map/ppermute | solution.py:31
  4.0 1.3 %collective-permute-start.1 = (bf16[2,2048]{1,0:T(2,128)(2,1)}, bf16[2,2048]{1,0:T(2,128)(2,1)S(1)}, u32[]{:S(2)}, u32[]{:S(2)}) collective-permute-start(bf16[2,2048]{1,0:T(2,128)(2,1)} %refs_5_.1), channel_id=1, source_target_pairs={{0,12},{4,8},{8,4},{12,0},{1,13},{5,9},{9,5},{13,1},{2,14},{6,10},... | collective-permute-start | bytes 24584 | tf_op jit(solution)/shard_map/ppermute | solution.py:31
  5.4 0.2 collective-permute-start.2
  5.6 2.7 %load.5 = (bf16[2,2048]{1,0:T(2,128)(2,1)S(1)}, bf16[2048]{0:T(1024)(128)(2,1)S(1)}, bf16[2048]{0:T(1024)(128)(2,1)S(1)}, bf16[2048,256]{1,0:T(8,128)(2,1)S(1)}, bf16[2048,1024]{1,0:T(8,128)(2,1)S(1)}) custom-call(bf16[2,2048]{1,0:T(2,128)(2,1)} %refs_5_.1, bf16[2048]{0:T(1024)(128)(2,1)} %refs_1_.1, bf16[2048]{0:T(1024)(128)(2,1)} %refs_2_.1, ...), custom_call_target="tpu_custom_call" | custom-call | bytes 5259264 | tf_op jit(solution)/shard_map/load/pallas_call | solution.py:159
  8.4 0.0 collective-permute-done.refs_0_
  8.4 1.3 %collective-permute-done.1.refs_1_ = bf16[2,2048]{1,0:T(2,128)(2,1)S(1)} collective-permute-done((bf16[2,2048]{1,0:T(2,128)(2,1)}, bf16[2,2048]{1,0:T(2,128)(2,1)S(1)}, u32[]{:S(2)}, u32[]{:S(2)}) %collective-permute-start.1) | collective-permute-done | bytes 8224 | tf_op jit(solution)/shard_map/ppermute | solution.py:31
  9.7 0.0 collective-permute-done.2.refs_2_
  9.7 0.8 %project_qkv.1 = (f32[8,2048]{1,0:T(8,128)S(1)}, bf16[2,1408]{1,0:T(2,128)(2,1)S(1)}, bf16[2,1408]{1,0:T(2,128)(2,1)S(1)}, bf16[2,1408]{1,0:T(2,128)(2,1)S(1)}, bf16[2,1408]{1,0:T(2,128)(2,1)S(1)}) custom-call(bf16[2048]{0:T(1024)(128)(2,1)S(1)} %get-tuple-element.51.gain_ref, bf16[2048,1024]{1,0:T(8,128)(2,1)S(1)} %get-tuple-element.52.wq_ref, ...), custom_call_target="tpu_custom_call" | custom-call | tf_op jit(solution)/shard_map/project_qkv/pallas_call | solution.py:212
  10.5 0.3 collective-permute-start.3
  10.8 1.5 %collective-permute-start.4 = (bf16[2,1408]{1,0:T(2,128)(2,1)S(1)}, bf16[2,1408]{1,0:T(2,128)(2,1)S(1)}, u32[]{:S(2)}, u32[]{:S(2)}) collective-permute-start(bf16[2,1408]{1,0:T(2,128)(2,1)S(1)} %get-tuple-element.60), channel_id=1, source_target_pairs={{0,9},{1,8},{2,11},{3,10},{4,13},{5,12},{6,15},{7,14},{8,1},{9,0},... | collective-permute-start | bytes 16904 | tf_op jit(solution)/shard_map/ppermute | solution.py:50
  12.3 0.7 %collective-permute-start.5 = (bf16[2,1408]{1,0:T(2,128)(2,1)S(1)}, bf16[2,1408]{1,0:T(2,128)(2,1)S(1)}, u32[]{:S(2)}, u32[]{:S(2)}) collective-permute-start(bf16[2,1408]{1,0:T(2,128)(2,1)S(1)} %get-tuple-element.61), channel_id=1, source_target_pairs={{0,5},{1,4},{2,7},{3,6},{4,1},{5,0},{6,3},{7,2},{8,13},{9,12},{10,... | collective-permute-start | bytes 16904 | tf_op jit(solution)/shard_map/ppermute | solution.py:50
  13.0 0.1 fusion.4
  13.1 1.6 %load.6.key_ref = bf16[2,4096,128]{2,1,0:T(8,128)(2,1)S(1)} custom-call(bf16[2,4096,128]{2,1,0:T(8,128)(2,1)} %bitcast.8, f32[8,2048]{1,0:T(8,128)S(1)} %get-tuple-element.56.refs_1_.rows_ref), custom_call_target="tpu_custom_call" | custom-call | bytes 2097152 | tf_op jit(solution)/shard_map/load/pallas_call | solution.py:159
  14.7 0.7 %collective-permute-done.3.refs_0_ = bf16[2,1408]{1,0:T(2,128)(2,1)S(1)} collective-permute-done((bf16[2,1408]{1,0:T(2,128)(2,1)S(1)}, bf16[2,1408]{1,0:T(2,128)(2,1)S(1)}, u32[]{:S(2)}, u32[]{:S(2)}) %collective-permute-start.3) | collective-permute-done | bytes 5664 | tf_op jit(solution)/shard_map/ppermute | solution.py:50
  15.4 0.0 collective-permute-done.4.refs_1_
  15.4 0.0 collective-permute-done.5.refs_2_
  15.5 2.4 %collective-permute-start.6 = (bf16[8,1408]{1,0:T(8,128)(2,1)S(1)}, bf16[8,1408]{1,0:T(8,128)(2,1)S(1)}, u32[]{:S(2)}, u32[]{:S(2)}) collective-permute-start(bf16[8,1408]{1,0:T(8,128)(2,1)S(1)} %stack.1.refs_1_.refs_0_), channel_id=1, source_target_pairs={{0,3},{1,2},{2,1},{3,0},{4,7},{5,6},{6,5},{7,4},{8,11},{9,10},{10,... | collective-permute-start | bytes 67592 | tf_op jit(solution)/shard_map/ppermute | solution.py:31
  17.9 0.5 collective-permute-start.7
  18.4 0.1 fusion
  18.5 0.0 copy-start
  18.5 1.8 %load.7.value_ref = bf16[2,4096,128]{2,1,0:T(8,128)(2,1)S(1)} custom-call(bf16[2,4096,128]{2,1,0:T(8,128)(2,1)} %bitcast.9, bf16[8,1408]{1,0:T(8,128)(2,1)S(1)} %stack.1.refs_1_.refs_0_), custom_call_target="tpu_custom_call" | custom-call | bytes 2097152 | tf_op jit(solution)/shard_map/load/pallas_call | solution.py:159
  20.3 1.3 %collective-permute-done.7.refs_2_ = bf16[8,1408]{1,0:T(8,128)(2,1)S(1)} collective-permute-done((bf16[8,1408]{1,0:T(8,128)(2,1)S(1)}, bf16[8,1408]{1,0:T(8,128)(2,1)S(1)}, u32[]{:S(2)}, u32[]{:S(2)}) %collective-permute-start.7) | collective-permute-done | bytes 22560 | tf_op jit(solution)/shard_map/ppermute | solution.py:31
  21.7 0.1 broadcast_in_dim.10.lengths_ref
  21.8 1.5 %attend.1.refs_1_.refs_3_ = bf16[80,128]{1,0:T(8,128)(2,1)S(1)} custom-call(s32[2,128]{1,0:T(2,128)S(1)} %broadcast_in_dim.10.lengths_ref, f32[8,128]{1,0:T(8,128)S(1)} %bitcast.6, f32[8,128]{1,0:T(8,128)S(1)} %bitcast.7, bf16[2,4096,128]{2,1,0:T(8,128)(2,1)S(1)} %load.6.key_ref, bf16[2,4096,128]{2,1,0:T(8,128)(2,1)S(1)} %load.7.value_ref, ...), custom_call_target="tpu_custom_call" | custom-call | tf_op jit(solution)/shard_map/attend/pallas_call | solution.py:356
  23.2 0.6 collective-permute-start.10
  23.8 0.0 collective-permute-start.11
  23.9 1.6 %collective-permute-start.9 = (bf16[80,128]{1,0:T(8,128)(2,1)S(1)}, bf16[80,128]{1,0:T(8,128)(2,1)S(1)}, u32[]{:S(2)}, u32[]{:S(2)}) collective-permute-start(bf16[80,128]{1,0:T(8,128)(2,1)S(1)} %attend.1.refs_1_.refs_3_), channel_id=1, source_target_pairs={{0,1},{1,0},{2,3},{3,2},{4,5},{5,4},{6,7},{7,6},{8,9},{9,8},{10,11... | collective-permute-start | bytes 61448 | tf_op jit(solution)/shard_map/ppermute | solution.py:31
  25.5 1.5 %load.8.upper_ref = bf16[512,2048]{1,0:T(8,128)(2,1)S(1)} custom-call(bf16[1024,2048]{1,0:T(8,128)(2,1)} %refs_0_.5, bf16[80,128]{1,0:T(8,128)(2,1)S(1)} %attend.1.refs_1_.refs_3_), custom_call_target="tpu_custom_call" | custom-call | bytes 2097152 | tf_op jit(solution)/shard_map/load/pallas_call | solution.py:159
  27.0 0.3 collective-permute-done.10.refs_1_
  27.3 0.0 collective-permute-done.11.refs_0_
  27.3 0.0 collective-permute-done.9.refs_2_
  27.3 0.0 copy-start.1
  27.3 0.3 combine.1
  27.6 1.7 %collective-permute-start.12 = (bf16[2,1024]{1,0:T(2,128)(2,1)S(1)}, bf16[2,1024]{1,0:T(2,128)(2,1)S(1)}, u32[]{:S(2)}, u32[]{:S(2)}) collective-permute-start(bf16[2,1024]{1,0:T(2,128)(2,1)S(1)} %get-tuple-element.75), channel_id=1, source_target_pairs={{0,13},{1,12},{2,15},{3,14},{4,9},{5,8},{6,11},{7,10},{8,5},{9,4},... | collective-permute-start | bytes 12296 | tf_op jit(solution)/shard_map/ppermute | solution.py:50
  29.2 0.4 collective-permute-start.13
  29.6 1.8 %collective-permute-start.14 = (bf16[2,1024]{1,0:T(2,128)(2,1)S(1)}, bf16[2,1024]{1,0:T(2,128)(2,1)S(1)}, u32[]{:S(2)}, u32[]{:S(2)}) collective-permute-start(bf16[2,1024]{1,0:T(2,128)(2,1)S(1)} %get-tuple-element.77), channel_id=1, source_target_pairs={{0,5},{1,4},{2,7},{3,6},{4,1},{5,0},{6,3},{7,2},{8,13},{9,12},{10,... | collective-permute-start | bytes 12296 | tf_op jit(solution)/shard_map/ppermute | solution.py:50
  31.4 1.6 %load.9.lower_ref = bf16[512,2048]{1,0:T(8,128)(2,1)S(1)} custom-call(bf16[1024,2048]{1,0:T(8,128)(2,1)} %refs_0_.5, bf16[2,1024]{1,0:T(2,128)(2,1)S(1)} %get-tuple-element.83.refs_1_.refs_3_), custom_call_target="tpu_custom_call" | custom-call | bytes 2097152 | tf_op jit(solution)/shard_map/load/pallas_call | solution.py:159
  33.0 0.1 collective-permute-done.13.refs_1_
  33.2 0.9 %project_out.1 = (bf16[8,2048]{1,0:T(8,128)(2,1)S(1)}, bf16[8,2048]{1,0:T(8,128)(2,1)S(1)}, bf16[8,2048]{1,0:T(8,128)(2,1)S(1)}, bf16[8,2048]{1,0:T(8,128)(2,1)S(1)}) custom-call(bf16[512,2048]{1,0:T(8,128)(2,1)S(1)} %load.8.upper_ref, bf16[512,2048]{1,0:T(8,128)(2,1)S(1)} %load.9.lower_ref, bf16[2,1024]{1,0:T(2,128)(2,1)S(1)} %collective-permute-done.12.refs_0_, ...), custom_call_target="tpu_custom_call" | custom-call | tf_op jit(solution)/shard_map/project_out/pallas_call | solution.py:453
  34.1 2.1 %collective-permute-start.15 = (bf16[8,2048]{1,0:T(8,128)(2,1)S(1)}, bf16[8,2048]{1,0:T(8,128)(2,1)S(1)}, u32[]{:S(2)}, u32[]{:S(2)}) collective-permute-start(bf16[8,2048]{1,0:T(8,128)(2,1)S(1)} %get-tuple-element.84), channel_id=1, source_target_pairs={{0,8},{1,9},{2,10},{3,11},{4,12},{5,13},{6,14},{7,15},{8,0},{9,1},... | collective-permute-start | bytes 98312 | tf_op jit(solution)/shard_map/ppermute | solution.py:50
  36.2 1.9 %collective-permute-start.16 = (bf16[8,2048]{1,0:T(8,128)(2,1)S(1)}, bf16[8,2048]{1,0:T(8,128)(2,1)S(1)}, u32[]{:S(2)}, u32[]{:S(2)}) collective-permute-start(bf16[8,2048]{1,0:T(8,128)(2,1)S(1)} %get-tuple-element.85), channel_id=1, source_target_pairs={{0,12},{1,13},{2,14},{3,15},{4,8},{5,9},{6,10},{7,11},{8,4},{9,5},... | collective-permute-start | bytes 98312 | tf_op jit(solution)/shard_map/ppermute | solution.py:50
  38.1 0.0 collective-permute-start.17
  38.1 1.3 %collective-permute-done.15.refs_0_ = bf16[8,2048]{1,0:T(8,128)(2,1)S(1)} collective-permute-done((bf16[8,2048]{1,0:T(8,128)(2,1)S(1)}, bf16[8,2048]{1,0:T(8,128)(2,1)S(1)}, u32[]{:S(2)}, u32[]{:S(2)}) %collective-permute-start.15) | collective-permute-done | bytes 32800 | tf_op jit(solution)/shard_map/ppermute | solution.py:50
  39.5 2.5 %collective-permute-done.16.refs_1_ = bf16[8,2048]{1,0:T(8,128)(2,1)S(1)} collective-permute-done((bf16[8,2048]{1,0:T(8,128)(2,1)S(1)}, bf16[8,2048]{1,0:T(8,128)(2,1)S(1)}, u32[]{:S(2)}, u32[]{:S(2)}) %collective-permute-start.16) | collective-permute-done | bytes 32800 | tf_op jit(solution)/shard_map/ppermute | solution.py:50
  41.9 0.3 collective-permute-done.17.refs_2_
  42.3 2.0 %first_gate_up.1 = (bf16[8,3712]{1,0:T(8,128)(2,1)S(1)}, f32[2,2048]{1,0:T(2,128)S(1)}, bf16[8,2048]{1,0:T(8,128)(2,1)S(1)}) custom-call(f32[8,2048]{1,0:T(8,128)S(1)} %get-tuple-element.56.refs_1_.rows_ref, bf16[2048]{0:T(1024)(128)(2,1)S(1)} %get-tuple-element.57.gain_ref, bf16[2048,3584]{1,0:T(8,128)(2,1)S(1)} %copy-done, ...), custom_call_target="tpu_custom_call" | custom-call | flops 117440512 | bytes 14680064 | tf_op jit(solution)/shard_map/first_gate_up/pallas_call | solution.py:509
  44.3 0.0 collective-permute-start.20
  44.3 0.0 slice-start.1
  44.3 0.0 slice-start.2
  44.3 2.0 %second_gate_up.1.first_ref = bf16[8,3584]{1,0:T(8,128)(2,1)S(1)} custom-call(bf16[8,2048]{1,0:T(8,128)(2,1)S(1)} %get-tuple-element.89.scaled_ref, bf16[2048,3584]{1,0:T(8,128)(2,1)S(1)} %copy-done, bf16[2048,3584]{1,0:T(8,128)(2,1)S(1)} %copy-done.2), custom_call_target="tpu_custom_call" | custom-call | flops 117440512 | bytes 14680064 | tf_op jit(solution)/shard_map/second_gate_up/pallas_call | solution.py:538
  46.3 0.5 collective-permute-start.18
  46.8 1.3 %collective-permute-start.21 = (bf16[8,3712]{1,0:T(8,128)(2,1)S(1)}, bf16[8,3712]{1,0:T(8,128)(2,1)S(1)}, u32[]{:S(2)}, u32[]{:S(2)}) collective-permute-start(bf16[8,3712]{1,0:T(8,128)(2,1)S(1)} %pair_sum.3.near_ref), channel_id=1, source_target_pairs={{0,2},{1,3},{2,0},{3,1},{4,6},{5,7},{6,4},{7,5},{8,10},{9,11},{10,... | collective-permute-start | bytes 178184 | tf_op jit(solution)/shard_map/ppermute | solution.py:31
  48.2 0.9 %collective-permute-start.19 = (bf16[8,3584]{1,0:T(8,128)(2,1)S(1)}, bf16[8,3584]{1,0:T(8,128)(2,1)S(1)}, u32[]{:S(2)}, u32[]{:S(2)}) collective-permute-start(bf16[8,3584]{1,0:T(8,128)(2,1)S(1)} %pair_sum.2.after_ref.near_ref), channel_id=1, source_target_pairs={{0,2},{1,3},{2,0},{3,1},{4,6},{5,7},{6,4},{7,5},{8,10},{9,11},{10,... | collective-permute-start | bytes 172040 | tf_op jit(solution)/shard_map/ppermute | solution.py:31
  49.0 0.5 slice-done.3
  49.5 1.9 %collective-permute-done.21.far_ref = bf16[8,3712]{1,0:T(8,128)(2,1)S(1)} collective-permute-done((bf16[8,3712]{1,0:T(8,128)(2,1)S(1)}, bf16[8,3712]{1,0:T(8,128)(2,1)S(1)}, u32[]{:S(2)}, u32[]{:S(2)}) %collective-permute-start.21) | collective-permute-done | bytes 59424 | tf_op jit(solution)/shard_map/ppermute | solution.py:31
  51.5 1.3 %first_down.1 = (f32[8,2048]{1,0:T(8,128)S(1)}, f32[8,128]{1,0:T(8,128)S(1)}) custom-call(bf16[8,3712]{1,0:T(8,128)(2,1)S(1)} %pair_sum.3.near_ref, bf16[8,3712]{1,0:T(8,128)(2,1)S(1)} %collective-permute-done.21.far_ref, bf16[3584,2048]{1,0:T(8,128)(2,1)S(1)} %bitcast.5, f32[8,128]{1,0:T(8,128)S(1)} %hold.1.token_ref), custom_call_target="tpu_custom_call" | custom-call | flops 58720256 | bytes 7340032 | tf_op jit(solution)/shard_map/first_down/pallas_call | solution.py:576
  52.8 1.3 %second_down.1 = (bf16[2,2048]{1,0:T(2,128)(2,1)S(1)}, bf16[2,2048]{1,0:T(2,128)(2,1)S(1)}, bf16[2,2048]{1,0:T(2,128)(2,1)S(1)}, bf16[2,2048]{1,0:T(2,128)(2,1)S(1)}) custom-call(bf16[8,3584]{1,0:T(8,128)(2,1)S(1)} %pair_sum.2.after_ref.near_ref, bf16[8,3584]{1,0:T(8,128)(2,1)S(1)} %collective-permute-done.19.far_ref, bf16[3584,2048]{1,0:T(8,128)(2,1)S(1)} %bitcast.5, ...), custom_call_target="tpu_custom_call" | custom-call | tf_op jit(solution)/shard_map/second_down/pallas_call | solution.py:606
  54.1 0.6 %collective-permute-start.22 = (bf16[2,2048]{1,0:T(2,128)(2,1)S(1)}, bf16[2,2048]{1,0:T(2,128)(2,1)S(1)}, u32[]{:S(2)}, u32[]{:S(2)}) collective-permute-start(bf16[2,2048]{1,0:T(2,128)(2,1)S(1)} %get-tuple-element.93), channel_id=1, source_target_pairs={{0,8},{1,9},{2,10},{3,11},{4,12},{5,13},{6,14},{7,15},{8,0},{9,1},... | collective-permute-start | bytes 24584 | tf_op jit(solution)/shard_map/ppermute | solution.py:50
  54.7 1.9 %collective-permute-start.23 = (bf16[2,2048]{1,0:T(2,128)(2,1)S(1)}, bf16[2,2048]{1,0:T(2,128)(2,1)S(1)}, u32[]{:S(2)}, u32[]{:S(2)}) collective-permute-start(bf16[2,2048]{1,0:T(2,128)(2,1)S(1)} %get-tuple-element.94), channel_id=1, source_target_pairs={{0,12},{1,13},{2,14},{3,15},{4,8},{5,9},{6,10},{7,11},{8,4},{9,5},... | collective-permute-start | bytes 24584 | tf_op jit(solution)/shard_map/ppermute | solution.py:50
  56.6 1.0 %collective-permute-start.24 = (bf16[2,2048]{1,0:T(2,128)(2,1)S(1)}, bf16[2,2048]{1,0:T(2,128)(2,1)S(1)}, u32[]{:S(2)}, u32[]{:S(2)}) collective-permute-start(bf16[2,2048]{1,0:T(2,128)(2,1)S(1)} %get-tuple-element.95), channel_id=1, source_target_pairs={{0,4},{1,5},{2,6},{3,7},{4,0},{5,1},{6,2},{7,3},{8,12},{9,13},{10,... | collective-permute-start | bytes 24584 | tf_op jit(solution)/shard_map/ppermute | solution.py:50
  57.6 1.1 %collective-permute-done.22.refs_0_ = bf16[2,2048]{1,0:T(2,128)(2,1)S(1)} collective-permute-done((bf16[2,2048]{1,0:T(2,128)(2,1)S(1)}, bf16[2,2048]{1,0:T(2,128)(2,1)S(1)}, u32[]{:S(2)}, u32[]{:S(2)}) %collective-permute-start.22) | collective-permute-done | bytes 8224 | tf_op jit(solution)/shard_map/ppermute | solution.py:50
  58.7 1.5 %collective-permute-done.23.refs_1_ = bf16[2,2048]{1,0:T(2,128)(2,1)S(1)} collective-permute-done((bf16[2,2048]{1,0:T(2,128)(2,1)S(1)}, bf16[2,2048]{1,0:T(2,128)(2,1)S(1)}, u32[]{:S(2)}, u32[]{:S(2)}) %collective-permute-start.23) | collective-permute-done | bytes 8224 | tf_op jit(solution)/shard_map/ppermute | solution.py:50
  60.2 0.1 collective-permute-done.24.refs_2_
  60.3 0.6 %finish.1 = bf16[2,2048]{1,0:T(2,128)(2,1)} custom-call(f32[2,2048]{1,0:T(2,128)S(1)} %get-tuple-element.88.updated_ref, bf16[2,2048]{1,0:T(2,128)(2,1)S(1)} %collective-permute-done.22.refs_0_, bf16[2,2048]{1,0:T(2,128)(2,1)S(1)} %collective-permute-done.23.refs_1_, bf16[2,2048]{1,0:T(2,128)(2,1)S(1)} %collective-permute-done.24.refs_2_, ...), custom_call_target="tpu_custom_call" | custom-call | tf_op jit(solution)/shard_map/finish/pallas_call | solution.py:639
  (27 shorter events, 0.1 us)
Async XLA Ops:
  0.0 8.4 %collective-permute-start = (bf16[2,2048]{1,0:T(2,128)(2,1)}, bf16[2,2048]{1,0:T(2,128)(2,1)S(1)}, u32[]{:S(2)}, u32[]{:S(2)}) collective-permute-start(bf16[2,2048]{1,0:T(2,128)(2,1)} %refs_5_.1), channel_id=1, source_target_pairs={{0,8},{4,12},{8,0},{12,4},{1,9},{5,13},{9,1},{13,5},{2,10},{6,14},... | collective-permute-start | bytes 24584 | tf_op jit(solution)/shard_map/ppermute | solution.py:31
  4.0 5.7 %collective-permute-start.1 = (bf16[2,2048]{1,0:T(2,128)(2,1)}, bf16[2,2048]{1,0:T(2,128)(2,1)S(1)}, u32[]{:S(2)}, u32[]{:S(2)}) collective-permute-start(bf16[2,2048]{1,0:T(2,128)(2,1)} %refs_5_.1), channel_id=1, source_target_pairs={{0,12},{4,8},{8,4},{12,0},{1,13},{5,9},{9,5},{13,1},{2,14},{6,10},... | collective-permute-start | bytes 24584 | tf_op jit(solution)/shard_map/ppermute | solution.py:31
  5.4 4.3 %collective-permute-start.2 = (bf16[2,2048]{1,0:T(2,128)(2,1)}, bf16[2,2048]{1,0:T(2,128)(2,1)S(1)}, u32[]{:S(2)}, u32[]{:S(2)}) collective-permute-start(bf16[2,2048]{1,0:T(2,128)(2,1)} %refs_5_.1), channel_id=1, source_target_pairs={{0,4},{4,0},{8,12},{12,8},{1,5},{5,1},{9,13},{13,9},{2,6},{6,2},{1... | collective-permute-start | bytes 24584 | tf_op jit(solution)/shard_map/ppermute | solution.py:31
  5.6 7.4 %copy-start.3 = (s32[8]{0:T(128)S(1)}, s32[8]{0:T(128)}, u32[]{:S(2)}) copy-start(s32[8]{0:T(128)} %param.23) | copy-start | bytes 100
  10.5 4.9 %collective-permute-start.3 = (bf16[2,1408]{1,0:T(2,128)(2,1)S(1)}, bf16[2,1408]{1,0:T(2,128)(2,1)S(1)}, u32[]{:S(2)}, u32[]{:S(2)}) collective-permute-start(bf16[2,1408]{1,0:T(2,128)(2,1)S(1)} %get-tuple-element.59), channel_id=1, source_target_pairs={{0,13},{1,12},{2,15},{3,14},{4,9},{5,8},{6,11},{7,10},{8,5},{9,4},... | collective-permute-start | bytes 16904 | tf_op jit(solution)/shard_map/ppermute | solution.py:50
  10.8 4.6 %collective-permute-start.4 = (bf16[2,1408]{1,0:T(2,128)(2,1)S(1)}, bf16[2,1408]{1,0:T(2,128)(2,1)S(1)}, u32[]{:S(2)}, u32[]{:S(2)}) collective-permute-start(bf16[2,1408]{1,0:T(2,128)(2,1)S(1)} %get-tuple-element.60), channel_id=1, source_target_pairs={{0,9},{1,8},{2,11},{3,10},{4,13},{5,12},{6,15},{7,14},{8,1},{9,0},... | collective-permute-start | bytes 16904 | tf_op jit(solution)/shard_map/ppermute | solution.py:50
  12.3 3.2 %collective-permute-start.5 = (bf16[2,1408]{1,0:T(2,128)(2,1)S(1)}, bf16[2,1408]{1,0:T(2,128)(2,1)S(1)}, u32[]{:S(2)}, u32[]{:S(2)}) collective-permute-start(bf16[2,1408]{1,0:T(2,128)(2,1)S(1)} %get-tuple-element.61), channel_id=1, source_target_pairs={{0,5},{1,4},{2,7},{3,6},{4,1},{5,0},{6,3},{7,2},{8,13},{9,12},{10,... | collective-permute-start | bytes 16904 | tf_op jit(solution)/shard_map/ppermute | solution.py:50
  15.5 4.8 %collective-permute-start.6 = (bf16[8,1408]{1,0:T(8,128)(2,1)S(1)}, bf16[8,1408]{1,0:T(8,128)(2,1)S(1)}, u32[]{:S(2)}, u32[]{:S(2)}) collective-permute-start(bf16[8,1408]{1,0:T(8,128)(2,1)S(1)} %stack.1.refs_1_.refs_0_), channel_id=1, source_target_pairs={{0,3},{1,2},{2,1},{3,0},{4,7},{5,6},{6,5},{7,4},{8,11},{9,10},{10,... | collective-permute-start | bytes 67592 | tf_op jit(solution)/shard_map/ppermute | solution.py:31
  17.9 3.8 %collective-permute-start.7 = (bf16[8,1408]{1,0:T(8,128)(2,1)S(1)}, bf16[8,1408]{1,0:T(8,128)(2,1)S(1)}, u32[]{:S(2)}, u32[]{:S(2)}) collective-permute-start(bf16[8,1408]{1,0:T(8,128)(2,1)S(1)} %stack.1.refs_1_.refs_0_), channel_id=1, source_target_pairs={{0,2},{1,3},{2,0},{3,1},{4,6},{5,7},{6,4},{7,5},{8,10},{9,11},{10,... | collective-permute-start | bytes 67592 | tf_op jit(solution)/shard_map/ppermute | solution.py:31
  18.4 3.3 %collective-permute-start.8 = (bf16[8,1408]{1,0:T(8,128)(2,1)S(1)}, bf16[8,1408]{1,0:T(8,128)(2,1)S(1)}, u32[]{:S(2)}, u32[]{:S(2)}) collective-permute-start(bf16[8,1408]{1,0:T(8,128)(2,1)S(1)} %stack.1.refs_1_.refs_0_), channel_id=1, source_target_pairs={{0,1},{1,0},{2,3},{3,2},{4,5},{5,4},{6,7},{7,6},{8,9},{9,8},{10,11... | collective-permute-start | bytes 67592 | tf_op jit(solution)/shard_map/ppermute | solution.py:31
  18.5 8.8 %copy-start = (bf16[2048,3584]{1,0:T(8,128)(2,1)S(1)}, bf16[2048,3584]{1,0:T(8,128)(2,1)}, u32[]{:S(2)}) copy-start(bf16[2048,3584]{1,0:T(8,128)(2,1)} %gate_ref.3) | copy-start | bytes 44040196
  23.2 4.0 %collective-permute-start.10 = (bf16[80,128]{1,0:T(8,128)(2,1)S(1)}, bf16[80,128]{1,0:T(8,128)(2,1)S(1)}, u32[]{:S(2)}, u32[]{:S(2)}) collective-permute-start(bf16[80,128]{1,0:T(8,128)(2,1)S(1)} %attend.1.refs_1_.refs_3_), channel_id=1, source_target_pairs={{0,2},{1,3},{2,0},{3,1},{4,6},{5,7},{6,4},{7,5},{8,10},{9,11},{10,... | collective-permute-start | bytes 61448 | tf_op jit(solution)/shard_map/ppermute | solution.py:31
  23.8 3.4 %collective-permute-start.11 = (bf16[80,128]{1,0:T(8,128)(2,1)S(1)}, bf16[80,128]{1,0:T(8,128)(2,1)S(1)}, u32[]{:S(2)}, u32[]{:S(2)}) collective-permute-start(bf16[80,128]{1,0:T(8,128)(2,1)S(1)} %attend.1.refs_1_.refs_3_), channel_id=1, source_target_pairs={{0,3},{1,2},{2,1},{3,0},{4,7},{5,6},{6,5},{7,4},{8,11},{9,10},{10,... | collective-permute-start | bytes 61448 | tf_op jit(solution)/shard_map/ppermute | solution.py:31
  23.9 3.4 %collective-permute-start.9 = (bf16[80,128]{1,0:T(8,128)(2,1)S(1)}, bf16[80,128]{1,0:T(8,128)(2,1)S(1)}, u32[]{:S(2)}, u32[]{:S(2)}) collective-permute-start(bf16[80,128]{1,0:T(8,128)(2,1)S(1)} %attend.1.refs_1_.refs_3_), channel_id=1, source_target_pairs={{0,1},{1,0},{2,3},{3,2},{4,5},{5,4},{6,7},{7,6},{8,9},{9,8},{10,11... | collective-permute-start | bytes 61448 | tf_op jit(solution)/shard_map/ppermute | solution.py:31
  27.3 5.9 %copy-start.1 = (bf16[2048,3584]{1,0:T(8,128)(2,1)S(1)}, bf16[2048,3584]{1,0:T(8,128)(2,1)}, u32[]{:S(2)}) copy-start(bf16[2048,3584]{1,0:T(8,128)(2,1)} %up_ref.3) | copy-start | bytes 44040196
  27.6 5.5 %collective-permute-start.12 = (bf16[2,1024]{1,0:T(2,128)(2,1)S(1)}, bf16[2,1024]{1,0:T(2,128)(2,1)S(1)}, u32[]{:S(2)}, u32[]{:S(2)}) collective-permute-start(bf16[2,1024]{1,0:T(2,128)(2,1)S(1)} %get-tuple-element.75), channel_id=1, source_target_pairs={{0,13},{1,12},{2,15},{3,14},{4,9},{5,8},{6,11},{7,10},{8,5},{9,4},... | collective-permute-start | bytes 12296 | tf_op jit(solution)/shard_map/ppermute | solution.py:50
  29.2 3.9 %collective-permute-start.13 = (bf16[2,1024]{1,0:T(2,128)(2,1)S(1)}, bf16[2,1024]{1,0:T(2,128)(2,1)S(1)}, u32[]{:S(2)}, u32[]{:S(2)}) collective-permute-start(bf16[2,1024]{1,0:T(2,128)(2,1)S(1)} %get-tuple-element.76), channel_id=1, source_target_pairs={{0,9},{1,8},{2,11},{3,10},{4,13},{5,12},{6,15},{7,14},{8,1},{9,0},... | collective-permute-start | bytes 12296 | tf_op jit(solution)/shard_map/ppermute | solution.py:50
  29.6 3.5 %collective-permute-start.14 = (bf16[2,1024]{1,0:T(2,128)(2,1)S(1)}, bf16[2,1024]{1,0:T(2,128)(2,1)S(1)}, u32[]{:S(2)}, u32[]{:S(2)}) collective-permute-start(bf16[2,1024]{1,0:T(2,128)(2,1)S(1)} %get-tuple-element.77), channel_id=1, source_target_pairs={{0,5},{1,4},{2,7},{3,6},{4,1},{5,0},{6,3},{7,2},{8,13},{9,12},{10,... | collective-permute-start | bytes 12296 | tf_op jit(solution)/shard_map/ppermute | solution.py:50
  33.2 9.1 %copy-start.2 = (bf16[2048,3584]{1,0:T(8,128)(2,1)S(1)}, bf16[2048,3584]{1,0:T(8,128)(2,1)}, u32[]{:S(2)}) copy-start(bf16[2048,3584]{1,0:T(8,128)(2,1)} %up_ref.3) | copy-start | bytes 44040196
  34.1 5.3 %collective-permute-start.15 = (bf16[8,2048]{1,0:T(8,128)(2,1)S(1)}, bf16[8,2048]{1,0:T(8,128)(2,1)S(1)}, u32[]{:S(2)}, u32[]{:S(2)}) collective-permute-start(bf16[8,2048]{1,0:T(8,128)(2,1)S(1)} %get-tuple-element.84), channel_id=1, source_target_pairs={{0,8},{1,9},{2,10},{3,11},{4,12},{5,13},{6,14},{7,15},{8,0},{9,1},... | collective-permute-start | bytes 98312 | tf_op jit(solution)/shard_map/ppermute | solution.py:50
  36.2 5.7 %collective-permute-start.16 = (bf16[8,2048]{1,0:T(8,128)(2,1)S(1)}, bf16[8,2048]{1,0:T(8,128)(2,1)S(1)}, u32[]{:S(2)}, u32[]{:S(2)}) collective-permute-start(bf16[8,2048]{1,0:T(8,128)(2,1)S(1)} %get-tuple-element.85), channel_id=1, source_target_pairs={{0,12},{1,13},{2,14},{3,15},{4,8},{5,9},{6,10},{7,11},{8,4},{9,5},... | collective-permute-start | bytes 98312 | tf_op jit(solution)/shard_map/ppermute | solution.py:50
  38.1 4.1 %collective-permute-start.17 = (bf16[8,2048]{1,0:T(8,128)(2,1)S(1)}, bf16[8,2048]{1,0:T(8,128)(2,1)S(1)}, u32[]{:S(2)}, u32[]{:S(2)}) collective-permute-start(bf16[8,2048]{1,0:T(8,128)(2,1)S(1)} %get-tuple-element.86), channel_id=1, source_target_pairs={{0,4},{1,5},{2,6},{3,7},{4,0},{5,1},{6,2},{7,3},{8,12},{9,13},{10,... | collective-permute-start | bytes 98312 | tf_op jit(solution)/shard_map/ppermute | solution.py:50
  44.3 2.6 %collective-permute-start.20 = (bf16[8,3712]{1,0:T(8,128)(2,1)S(1)}, bf16[8,3712]{1,0:T(8,128)(2,1)S(1)}, u32[]{:S(2)}, u32[]{:S(2)}) collective-permute-start(bf16[8,3712]{1,0:T(8,128)(2,1)S(1)} %get-tuple-element.90.first_ref), channel_id=1, source_target_pairs={{0,1},{1,0},{2,3},{3,2},{4,5},{5,4},{6,7},{7,6},{8,9},{9,8},{10,11... | collective-permute-start | bytes 178184 | tf_op jit(solution)/shard_map/ppermute | solution.py:31
  44.3 4.8 %slice-start = ((s8[14680064]{0:T(1024)(128)(4,1)}), s8[4194304]{0:T(1024)(128)(4,1)S(1)}, s32[]{:S(2)}) async-start(s8[14680064]{0:T(1024)(128)(4,1)} %bitcast.4), calls=%async_computation | async-start | bytes 8388608
  44.3 4.8 %slice-start.1 = ((s8[14680064]{0:T(1024)(128)(4,1)}), s8[4194304]{0:T(1024)(128)(4,1)S(1)}, s32[]{:S(2)}) async-start(s8[14680064]{0:T(1024)(128)(4,1)} %bitcast.4), calls=%async_computation.1 | async-start | bytes 8388608
  44.3 4.8 %slice-start.2 = ((s8[14680064]{0:T(1024)(128)(4,1)}), s8[4194304]{0:T(1024)(128)(4,1)S(1)}, s32[]{:S(2)}) async-start(s8[14680064]{0:T(1024)(128)(4,1)} %bitcast.4), calls=%async_computation.2 | async-start | bytes 8388608
  44.3 5.2 %slice-start.3 = ((s8[14680064]{0:T(1024)(128)(4,1)}), s8[2097152]{0:T(1024)(128)(4,1)S(1)}, s32[]{:S(2)}) async-start(s8[14680064]{0:T(1024)(128)(4,1)} %bitcast.4), calls=%async_computation.3 | async-start | bytes 4194304
  46.3 1.8 %collective-permute-start.18 = (bf16[8,3584]{1,0:T(8,128)(2,1)S(1)}, bf16[8,3584]{1,0:T(8,128)(2,1)S(1)}, u32[]{:S(2)}, u32[]{:S(2)}) collective-permute-start(bf16[8,3584]{1,0:T(8,128)(2,1)S(1)} %second_gate_up.1.first_ref), channel_id=1, source_target_pairs={{0,1},{1,0},{2,3},{3,2},{4,5},{5,4},{6,7},{7,6},{8,9},{9,8},{10,11... | collective-permute-start | bytes 172040 | tf_op jit(solution)/shard_map/ppermute | solution.py:31
  46.8 4.6 %collective-permute-start.21 = (bf16[8,3712]{1,0:T(8,128)(2,1)S(1)}, bf16[8,3712]{1,0:T(8,128)(2,1)S(1)}, u32[]{:S(2)}, u32[]{:S(2)}) collective-permute-start(bf16[8,3712]{1,0:T(8,128)(2,1)S(1)} %pair_sum.3.near_ref), channel_id=1, source_target_pairs={{0,2},{1,3},{2,0},{3,1},{4,6},{5,7},{6,4},{7,5},{8,10},{9,11},{10,... | collective-permute-start | bytes 178184 | tf_op jit(solution)/shard_map/ppermute | solution.py:31
  48.2 4.6 %collective-permute-start.19 = (bf16[8,3584]{1,0:T(8,128)(2,1)S(1)}, bf16[8,3584]{1,0:T(8,128)(2,1)S(1)}, u32[]{:S(2)}, u32[]{:S(2)}) collective-permute-start(bf16[8,3584]{1,0:T(8,128)(2,1)S(1)} %pair_sum.2.after_ref.near_ref), channel_id=1, source_target_pairs={{0,2},{1,3},{2,0},{3,1},{4,6},{5,7},{6,4},{7,5},{8,10},{9,11},{10,... | collective-permute-start | bytes 172040 | tf_op jit(solution)/shard_map/ppermute | solution.py:31
  54.1 4.6 %collective-permute-start.22 = (bf16[2,2048]{1,0:T(2,128)(2,1)S(1)}, bf16[2,2048]{1,0:T(2,128)(2,1)S(1)}, u32[]{:S(2)}, u32[]{:S(2)}) collective-permute-start(bf16[2,2048]{1,0:T(2,128)(2,1)S(1)} %get-tuple-element.93), channel_id=1, source_target_pairs={{0,8},{1,9},{2,10},{3,11},{4,12},{5,13},{6,14},{7,15},{8,0},{9,1},... | collective-permute-start | bytes 24584 | tf_op jit(solution)/shard_map/ppermute | solution.py:50
  54.7 5.4 %collective-permute-start.23 = (bf16[2,2048]{1,0:T(2,128)(2,1)S(1)}, bf16[2,2048]{1,0:T(2,128)(2,1)S(1)}, u32[]{:S(2)}, u32[]{:S(2)}) collective-permute-start(bf16[2,2048]{1,0:T(2,128)(2,1)S(1)} %get-tuple-element.94), channel_id=1, source_target_pairs={{0,12},{1,13},{2,14},{3,15},{4,8},{5,9},{6,10},{7,11},{8,4},{9,5},... | collective-permute-start | bytes 24584 | tf_op jit(solution)/shard_map/ppermute | solution.py:50
  56.6 3.7 %collective-permute-start.24 = (bf16[2,2048]{1,0:T(2,128)(2,1)S(1)}, bf16[2,2048]{1,0:T(2,128)(2,1)S(1)}, u32[]{:S(2)}, u32[]{:S(2)}) collective-permute-start(bf16[2,2048]{1,0:T(2,128)(2,1)S(1)} %get-tuple-element.95), channel_id=1, source_target_pairs={{0,4},{1,5},{2,6},{3,7},{4,0},{5,1},{6,2},{7,3},{8,12},{9,13},{10,... | collective-permute-start | bytes 24584 | tf_op jit(solution)/shard_map/ppermute | solution.py:50

commit v19 on v18

--- a/solution.py
+++ b/solution.py
@@ -523,7 +523,7 @@
         gain,
         resident(w_gate),
         resident(w_up),
-        *in_start_order(parts),
+        *parts[::-1],
         *[resident(w) for w in later],
     )
 

time: 61.1 us -> 61.1 us (level)
  transfers between devices with their start and end apart: 25 -> 25, of which waited for: 12 -> 11; matrix products, arithmetic and copies ran while one was open for 0% -> 0% of each run, Pallas kernels for 21% -> 21%
where the time goes in v19:
time: 61.1 us; the launch traced here: 61 us
  starting transfers between devices  27.8 us (45%)
  Pallas kernels  20 us (33%)
  waiting for transfers between devices  12.2 us (20%)
  local copies, waits for them, and re-layouts  0.63 us (1%)
    ppermute x12, starting transfers between devices, scatter_slots(): got.append(lax.ppermute(pieces[k], ('tensor', 'inner'), pairs))  14.3 us
    ppermute x13, starting transfers between devices, swap_with(): return lax.ppermute(value, axis, [(i, i ^ step) for i in range(count)])  13.4 us
    pallas_call x5, Pallas kernels, load(): pl.pallas_call(functools.partial(load_kernel, spans), out_shape=tuple((pl...  9.26 us
    ppermute x12, waiting for transfers between devices, scatter_slots(): got.append(lax.ppermute(pieces[k], ('tensor', 'inner'), pairs))  7.28 us
    ppermute x13, waiting for transfers between devices, swap_with(): return lax.ppermute(value, axis, [(i, i ^ step) for i in range(count)])  4.88 us
    pallas_call x1, Pallas kernels, first_gate_up(): pl.pallas_call(functools.partial(first_gate_up_kernel, slots, count), out...  2 us
    pallas_call x1, Pallas kernels, second_gate_up(): pl.pallas_call(functools.partial(second_gate_up_kernel, first, count), ou...  2 us
    pallas_call x1, Pallas kernels, attend(): pl.pallas_call(functools.partial(attend_kernel, slots, len(parts)), out_s...  1.49 us
  transfers between devices with their start and end apart: 25, of which 11 were waited for; matrix products, arithmetic and copies ran while one was open for 0% of the time, Pallas kernels for 21%

profile of v19, /device:TPU:0, one launch (start us, length us, event | category | flops | bytes accessed | tf_op | source)
XLA Modules:
  0.0 61.0 jit_solution(3010625036294612399)
XLA Ops:
  0.0 4.0 %collective-permute-start = (bf16[2,2048]{1,0:T(2,128)(2,1)}, bf16[2,2048]{1,0:T(2,128)(2,1)S(1)}, u32[]{:S(2)}, u32[]{:S(2)}) collective-permute-start(bf16[2,2048]{1,0:T(2,128)(2,1)} %refs_5_.1), channel_id=1, source_target_pairs={{0,8},{4,12},{8,0},{12,4},{1,9},{5,13},{9,1},{13,5},{2,10},{6,14},... | collective-permute-start | bytes 24584 | tf_op jit(solution)/shard_map/ppermute | solution.py:31
  4.0 1.3 %collective-permute-start.1 = (bf16[2,2048]{1,0:T(2,128)(2,1)}, bf16[2,2048]{1,0:T(2,128)(2,1)S(1)}, u32[]{:S(2)}, u32[]{:S(2)}) collective-permute-start(bf16[2,2048]{1,0:T(2,128)(2,1)} %refs_5_.1), channel_id=1, source_target_pairs={{0,12},{4,8},{8,4},{12,0},{1,13},{5,9},{9,5},{13,1},{2,14},{6,10},... | collective-permute-start | bytes 24584 | tf_op jit(solution)/shard_map/ppermute | solution.py:31
  5.4 0.2 collective-permute-start.2
  5.6 2.7 %load.5 = (bf16[2,2048]{1,0:T(2,128)(2,1)S(1)}, bf16[2048]{0:T(1024)(128)(2,1)S(1)}, bf16[2048]{0:T(1024)(128)(2,1)S(1)}, bf16[2048,256]{1,0:T(8,128)(2,1)S(1)}, bf16[2048,1024]{1,0:T(8,128)(2,1)S(1)}) custom-call(bf16[2,2048]{1,0:T(2,128)(2,1)} %refs_5_.1, bf16[2048]{0:T(1024)(128)(2,1)} %refs_1_.1, bf16[2048]{0:T(1024)(128)(2,1)} %refs_2_.1, ...), custom_call_target="tpu_custom_call" | custom-call | bytes 5259264 | tf_op jit(solution)/shard_map/load/pallas_call | solution.py:159
  8.4 1.3 %collective-permute-done.1.refs_1_ = bf16[2,2048]{1,0:T(2,128)(2,1)S(1)} collective-permute-done((bf16[2,2048]{1,0:T(2,128)(2,1)}, bf16[2,2048]{1,0:T(2,128)(2,1)S(1)}, u32[]{:S(2)}, u32[]{:S(2)}) %collective-permute-start.1) | collective-permute-done | bytes 8224 | tf_op jit(solution)/shard_map/ppermute | solution.py:31
  9.7 0.8 %project_qkv.1 = (f32[8,2048]{1,0:T(8,128)S(1)}, bf16[2,1408]{1,0:T(2,128)(2,1)S(1)}, bf16[2,1408]{1,0:T(2,128)(2,1)S(1)}, bf16[2,1408]{1,0:T(2,128)(2,1)S(1)}, bf16[2,1408]{1,0:T(2,128)(2,1)S(1)}) custom-call(bf16[2048]{0:T(1024)(128)(2,1)S(1)} %get-tuple-element.51.gain_ref, bf16[2048,1024]{1,0:T(8,128)(2,1)S(1)} %get-tuple-element.52.wq_ref, ...), custom_call_target="tpu_custom_call" | custom-call | tf_op jit(solution)/shard_map/project_qkv/pallas_call | solution.py:212
  10.5 0.3 collective-permute-start.3
  10.8 1.5 %collective-permute-start.4 = (bf16[2,1408]{1,0:T(2,128)(2,1)S(1)}, bf16[2,1408]{1,0:T(2,128)(2,1)S(1)}, u32[]{:S(2)}, u32[]{:S(2)}) collective-permute-start(bf16[2,1408]{1,0:T(2,128)(2,1)S(1)} %get-tuple-element.60), channel_id=1, source_target_pairs={{0,9},{1,8},{2,11},{3,10},{4,13},{5,12},{6,15},{7,14},{8,1},{9,0},... | collective-permute-start | bytes 16904 | tf_op jit(solution)/shard_map/ppermute | solution.py:50
  12.3 0.7 %collective-permute-start.5 = (bf16[2,1408]{1,0:T(2,128)(2,1)S(1)}, bf16[2,1408]{1,0:T(2,128)(2,1)S(1)}, u32[]{:S(2)}, u32[]{:S(2)}) collective-permute-start(bf16[2,1408]{1,0:T(2,128)(2,1)S(1)} %get-tuple-element.61), channel_id=1, source_target_pairs={{0,5},{1,4},{2,7},{3,6},{4,1},{5,0},{6,3},{7,2},{8,13},{9,12},{10,... | collective-permute-start | bytes 16904 | tf_op jit(solution)/shard_map/ppermute | solution.py:50
  13.0 0.1 fusion.4
  13.1 1.6 %load.6.key_ref = bf16[2,4096,128]{2,1,0:T(8,128)(2,1)S(1)} custom-call(bf16[2,4096,128]{2,1,0:T(8,128)(2,1)} %bitcast.8, f32[8,2048]{1,0:T(8,128)S(1)} %get-tuple-element.56.refs_1_.rows_ref), custom_call_target="tpu_custom_call" | custom-call | bytes 2097152 | tf_op jit(solution)/shard_map/load/pallas_call | solution.py:159
  14.7 0.7 %collective-permute-done.3.refs_0_ = bf16[2,1408]{1,0:T(2,128)(2,1)S(1)} collective-permute-done((bf16[2,1408]{1,0:T(2,128)(2,1)S(1)}, bf16[2,1408]{1,0:T(2,128)(2,1)S(1)}, u32[]{:S(2)}, u32[]{:S(2)}) %collective-permute-start.3) | collective-permute-done | bytes 5664 | tf_op jit(solution)/shard_map/ppermute | solution.py:50
  15.4 0.0 collective-permute-done.4.refs_1_
  15.4 0.0 collective-permute-done.5.refs_2_
  15.5 2.4 %collective-permute-start.6 = (bf16[8,1408]{1,0:T(8,128)(2,1)S(1)}, bf16[8,1408]{1,0:T(8,128)(2,1)S(1)}, u32[]{:S(2)}, u32[]{:S(2)}) collective-permute-start(bf16[8,1408]{1,0:T(8,128)(2,1)S(1)} %stack.1.refs_1_.refs_0_), channel_id=1, source_target_pairs={{0,3},{1,2},{2,1},{3,0},{4,7},{5,6},{6,5},{7,4},{8,11},{9,10},{10,... | collective-permute-start | bytes 67592 | tf_op jit(solution)/shard_map/ppermute | solution.py:31
  17.9 0.5 collective-permute-start.7
  18.4 0.0 collective-permute-start.8
  18.4 0.1 fusion
  18.5 0.0 copy-start
  18.5 1.8 %load.7.value_ref = bf16[2,4096,128]{2,1,0:T(8,128)(2,1)S(1)} custom-call(bf16[2,4096,128]{2,1,0:T(8,128)(2,1)} %bitcast.9, bf16[8,1408]{1,0:T(8,128)(2,1)S(1)} %stack.1.refs_1_.refs_0_), custom_call_target="tpu_custom_call" | custom-call | bytes 2097152 | tf_op jit(solution)/shard_map/load/pallas_call | solution.py:159
  20.3 0.0 collective-permute-done.6.refs_3_
  20.3 1.3 %collective-permute-done.7.refs_2_ = bf16[8,1408]{1,0:T(8,128)(2,1)S(1)} collective-permute-done((bf16[8,1408]{1,0:T(8,128)(2,1)S(1)}, bf16[8,1408]{1,0:T(8,128)(2,1)S(1)}, u32[]{:S(2)}, u32[]{:S(2)}) %collective-permute-start.7) | collective-permute-done | bytes 22560 | tf_op jit(solution)/shard_map/ppermute | solution.py:31
  21.7 0.0 collective-permute-done.8.refs_1_
  21.7 0.1 broadcast_in_dim.10.lengths_ref
  21.8 1.5 %attend.1.refs_1_.refs_3_ = bf16[80,128]{1,0:T(8,128)(2,1)S(1)} custom-call(s32[2,128]{1,0:T(2,128)S(1)} %broadcast_in_dim.10.lengths_ref, f32[8,128]{1,0:T(8,128)S(1)} %bitcast.6, f32[8,128]{1,0:T(8,128)S(1)} %bitcast.7, bf16[2,4096,128]{2,1,0:T(8,128)(2,1)S(1)} %load.6.key_ref, bf16[2,4096,128]{2,1,0:T(8,128)(2,1)S(1)} %load.7.value_ref, ...), custom_call_target="tpu_custom_call" | custom-call | tf_op jit(solution)/shard_map/attend/pallas_call | solution.py:356
  23.2 0.6 collective-permute-start.10
  23.8 0.0 collective-permute-start.11
  23.9 1.6 %collective-permute-start.9 = (bf16[80,128]{1,0:T(8,128)(2,1)S(1)}, bf16[80,128]{1,0:T(8,128)(2,1)S(1)}, u32[]{:S(2)}, u32[]{:S(2)}) collective-permute-start(bf16[80,128]{1,0:T(8,128)(2,1)S(1)} %attend.1.refs_1_.refs_3_), channel_id=1, source_target_pairs={{0,1},{1,0},{2,3},{3,2},{4,5},{5,4},{6,7},{7,6},{8,9},{9,8},{10,11... | collective-permute-start | bytes 61448 | tf_op jit(solution)/shard_map/ppermute | solution.py:31
  25.5 1.5 %load.8.upper_ref = bf16[512,2048]{1,0:T(8,128)(2,1)S(1)} custom-call(bf16[1024,2048]{1,0:T(8,128)(2,1)} %refs_0_.5, bf16[80,128]{1,0:T(8,128)(2,1)S(1)} %attend.1.refs_1_.refs_3_), custom_call_target="tpu_custom_call" | custom-call | bytes 2097152 | tf_op jit(solution)/shard_map/load/pallas_call | solution.py:159
  27.0 0.3 collective-permute-done.10.refs_1_
  27.3 0.0 collective-permute-done.11.refs_0_
  27.3 0.0 collective-permute-done.9.refs_2_
  27.3 0.0 copy-start.1
  27.3 0.3 combine.1
  27.6 1.7 %collective-permute-start.12 = (bf16[2,1024]{1,0:T(2,128)(2,1)S(1)}, bf16[2,1024]{1,0:T(2,128)(2,1)S(1)}, u32[]{:S(2)}, u32[]{:S(2)}) collective-permute-start(bf16[2,1024]{1,0:T(2,128)(2,1)S(1)} %get-tuple-element.75), channel_id=1, source_target_pairs={{0,13},{1,12},{2,15},{3,14},{4,9},{5,8},{6,11},{7,10},{8,5},{9,4},... | collective-permute-start | bytes 12296 | tf_op jit(solution)/shard_map/ppermute | solution.py:50
  29.2 0.4 collective-permute-start.13
  29.6 1.8 %collective-permute-start.14 = (bf16[2,1024]{1,0:T(2,128)(2,1)S(1)}, bf16[2,1024]{1,0:T(2,128)(2,1)S(1)}, u32[]{:S(2)}, u32[]{:S(2)}) collective-permute-start(bf16[2,1024]{1,0:T(2,128)(2,1)S(1)} %get-tuple-element.77), channel_id=1, source_target_pairs={{0,5},{1,4},{2,7},{3,6},{4,1},{5,0},{6,3},{7,2},{8,13},{9,12},{10,... | collective-permute-start | bytes 12296 | tf_op jit(solution)/shard_map/ppermute | solution.py:50
  31.4 1.6 %load.9.lower_ref = bf16[512,2048]{1,0:T(8,128)(2,1)S(1)} custom-call(bf16[1024,2048]{1,0:T(8,128)(2,1)} %refs_0_.5, bf16[2,1024]{1,0:T(2,128)(2,1)S(1)} %get-tuple-element.83.refs_1_.refs_3_), custom_call_target="tpu_custom_call" | custom-call | bytes 2097152 | tf_op jit(solution)/shard_map/load/pallas_call | solution.py:159
  33.0 0.0 collective-permute-done.12.refs_0_
  33.0 0.1 collective-permute-done.13.refs_1_
  33.2 0.0 collective-permute-done.14.refs_2_
  33.2 0.9 %project_out.1 = (bf16[8,2048]{1,0:T(8,128)(2,1)S(1)}, bf16[8,2048]{1,0:T(8,128)(2,1)S(1)}, bf16[8,2048]{1,0:T(8,128)(2,1)S(1)}, bf16[8,2048]{1,0:T(8,128)(2,1)S(1)}) custom-call(bf16[512,2048]{1,0:T(8,128)(2,1)S(1)} %load.8.upper_ref, bf16[512,2048]{1,0:T(8,128)(2,1)S(1)} %load.9.lower_ref, bf16[2,1024]{1,0:T(2,128)(2,1)S(1)} %collective-permute-done.12.refs_0_, ...), custom_call_target="tpu_custom_call" | custom-call | tf_op jit(solution)/shard_map/project_out/pallas_call | solution.py:453
  34.1 1.9 %collective-permute-start.15 = (bf16[8,2048]{1,0:T(8,128)(2,1)S(1)}, bf16[8,2048]{1,0:T(8,128)(2,1)S(1)}, u32[]{:S(2)}, u32[]{:S(2)}) collective-permute-start(bf16[8,2048]{1,0:T(8,128)(2,1)S(1)} %get-tuple-element.84), channel_id=1, source_target_pairs={{0,12},{1,13},{2,14},{3,15},{4,8},{5,9},{6,10},{7,11},{8,4},{9,5},... | collective-permute-start | bytes 98312 | tf_op jit(solution)/shard_map/ppermute | solution.py:50
  36.1 1.2 %collective-permute-start.16 = (bf16[8,2048]{1,0:T(8,128)(2,1)S(1)}, bf16[8,2048]{1,0:T(8,128)(2,1)S(1)}, u32[]{:S(2)}, u32[]{:S(2)}) collective-permute-start(bf16[8,2048]{1,0:T(8,128)(2,1)S(1)} %get-tuple-element.85), channel_id=1, source_target_pairs={{0,8},{1,9},{2,10},{3,11},{4,12},{5,13},{6,14},{7,15},{8,0},{9,1},... | collective-permute-start | bytes 98312 | tf_op jit(solution)/shard_map/ppermute | solution.py:50
  37.2 1.3 %collective-permute-start.17 = (bf16[8,2048]{1,0:T(8,128)(2,1)S(1)}, bf16[8,2048]{1,0:T(8,128)(2,1)S(1)}, u32[]{:S(2)}, u32[]{:S(2)}) collective-permute-start(bf16[8,2048]{1,0:T(8,128)(2,1)S(1)} %get-tuple-element.86), channel_id=1, source_target_pairs={{0,4},{1,5},{2,6},{3,7},{4,0},{5,1},{6,2},{7,3},{8,12},{9,13},{10,... | collective-permute-start | bytes 98312 | tf_op jit(solution)/shard_map/ppermute | solution.py:50
  38.5 1.7 %collective-permute-done.15.refs_0_ = bf16[8,2048]{1,0:T(8,128)(2,1)S(1)} collective-permute-done((bf16[8,2048]{1,0:T(8,128)(2,1)S(1)}, bf16[8,2048]{1,0:T(8,128)(2,1)S(1)}, u32[]{:S(2)}, u32[]{:S(2)}) %collective-permute-start.15) | collective-permute-done | bytes 32800 | tf_op jit(solution)/shard_map/ppermute | solution.py:50
  40.2 1.1 %collective-permute-done.16.refs_1_ = bf16[8,2048]{1,0:T(8,128)(2,1)S(1)} collective-permute-done((bf16[8,2048]{1,0:T(8,128)(2,1)S(1)}, bf16[8,2048]{1,0:T(8,128)(2,1)S(1)}, u32[]{:S(2)}, u32[]{:S(2)}) %collective-permute-start.16) | collective-permute-done | bytes 32800 | tf_op jit(solution)/shard_map/ppermute | solution.py:50
  41.3 0.0 collective-permute-done.17.refs_2_
  41.3 2.0 %first_gate_up.1 = (bf16[8,3712]{1,0:T(8,128)(2,1)S(1)}, f32[2,2048]{1,0:T(2,128)S(1)}, bf16[8,2048]{1,0:T(8,128)(2,1)S(1)}) custom-call(f32[8,2048]{1,0:T(8,128)S(1)} %get-tuple-element.56.refs_1_.rows_ref, bf16[2048]{0:T(1024)(128)(2,1)S(1)} %get-tuple-element.57.gain_ref, bf16[2048,3584]{1,0:T(8,128)(2,1)S(1)} %copy-done, ...), custom_call_target="tpu_custom_call" | custom-call | flops 117440512 | bytes 14680064 | tf_op jit(solution)/shard_map/first_gate_up/pallas_call | solution.py:509
  43.3 0.0 slice-start.1
  43.3 2.0 %second_gate_up.1.first_ref = bf16[8,3584]{1,0:T(8,128)(2,1)S(1)} custom-call(bf16[8,2048]{1,0:T(8,128)(2,1)S(1)} %get-tuple-element.89.scaled_ref, bf16[2048,3584]{1,0:T(8,128)(2,1)S(1)} %copy-done, bf16[2048,3584]{1,0:T(8,128)(2,1)S(1)} %copy-done.2), custom_call_target="tpu_custom_call" | custom-call | flops 117440512 | bytes 14680064 | tf_op jit(solution)/shard_map/second_gate_up/pallas_call | solution.py:538
  45.3 0.5 collective-permute-start.18
  45.9 1.3 %collective-permute-start.21 = (bf16[8,3712]{1,0:T(8,128)(2,1)S(1)}, bf16[8,3712]{1,0:T(8,128)(2,1)S(1)}, u32[]{:S(2)}, u32[]{:S(2)}) collective-permute-start(bf16[8,3712]{1,0:T(8,128)(2,1)S(1)} %pair_sum.3.near_ref), channel_id=1, source_target_pairs={{0,2},{1,3},{2,0},{3,1},{4,6},{5,7},{6,4},{7,5},{8,10},{9,11},{10,... | collective-permute-start | bytes 178184 | tf_op jit(solution)/shard_map/ppermute | solution.py:31
  47.1 0.9 %collective-permute-start.19 = (bf16[8,3584]{1,0:T(8,128)(2,1)S(1)}, bf16[8,3584]{1,0:T(8,128)(2,1)S(1)}, u32[]{:S(2)}, u32[]{:S(2)}) collective-permute-start(bf16[8,3584]{1,0:T(8,128)(2,1)S(1)} %pair_sum.2.after_ref.near_ref), channel_id=1, source_target_pairs={{0,2},{1,3},{2,0},{3,1},{4,6},{5,7},{6,4},{7,5},{8,10},{9,11},{10,... | collective-permute-start | bytes 172040 | tf_op jit(solution)/shard_map/ppermute | solution.py:31
  48.0 0.5 slice-done.3
  48.6 1.9 %collective-permute-done.21.far_ref = bf16[8,3712]{1,0:T(8,128)(2,1)S(1)} collective-permute-done((bf16[8,3712]{1,0:T(8,128)(2,1)S(1)}, bf16[8,3712]{1,0:T(8,128)(2,1)S(1)}, u32[]{:S(2)}, u32[]{:S(2)}) %collective-permute-start.21) | collective-permute-done | bytes 59424 | tf_op jit(solution)/shard_map/ppermute | solution.py:31
  50.5 1.3 %first_down.1 = (f32[8,2048]{1,0:T(8,128)S(1)}, f32[8,128]{1,0:T(8,128)S(1)}) custom-call(bf16[8,3712]{1,0:T(8,128)(2,1)S(1)} %pair_sum.3.near_ref, bf16[8,3712]{1,0:T(8,128)(2,1)S(1)} %collective-permute-done.21.far_ref, bf16[3584,2048]{1,0:T(8,128)(2,1)S(1)} %bitcast.5, f32[8,128]{1,0:T(8,128)S(1)} %hold.1.token_ref), custom_call_target="tpu_custom_call" | custom-call | flops 58720256 | bytes 7340032 | tf_op jit(solution)/shard_map/first_down/pallas_call | solution.py:576
  51.8 1.3 %second_down.1 = (bf16[2,2048]{1,0:T(2,128)(2,1)S(1)}, bf16[2,2048]{1,0:T(2,128)(2,1)S(1)}, bf16[2,2048]{1,0:T(2,128)(2,1)S(1)}, bf16[2,2048]{1,0:T(2,128)(2,1)S(1)}) custom-call(bf16[8,3584]{1,0:T(8,128)(2,1)S(1)} %pair_sum.2.after_ref.near_ref, bf16[8,3584]{1,0:T(8,128)(2,1)S(1)} %collective-permute-done.19.far_ref, bf16[3584,2048]{1,0:T(8,128)(2,1)S(1)} %bitcast.5, ...), custom_call_target="tpu_custom_call" | custom-call | tf_op jit(solution)/shard_map/second_down/pallas_call | solution.py:606
  53.1 1.7 %collective-permute-start.22 = (bf16[2,2048]{1,0:T(2,128)(2,1)S(1)}, bf16[2,2048]{1,0:T(2,128)(2,1)S(1)}, u32[]{:S(2)}, u32[]{:S(2)}) collective-permute-start(bf16[2,2048]{1,0:T(2,128)(2,1)S(1)} %get-tuple-element.93), channel_id=1, source_target_pairs={{0,8},{1,9},{2,10},{3,11},{4,12},{5,13},{6,14},{7,15},{8,0},{9,1},... | collective-permute-start | bytes 24584 | tf_op jit(solution)/shard_map/ppermute | solution.py:50
  54.8 1.9 %collective-permute-start.23 = (bf16[2,2048]{1,0:T(2,128)(2,1)S(1)}, bf16[2,2048]{1,0:T(2,128)(2,1)S(1)}, u32[]{:S(2)}, u32[]{:S(2)}) collective-permute-start(bf16[2,2048]{1,0:T(2,128)(2,1)S(1)} %get-tuple-element.94), channel_id=1, source_target_pairs={{0,12},{1,13},{2,14},{3,15},{4,8},{5,9},{6,10},{7,11},{8,4},{9,5},... | collective-permute-start | bytes 24584 | tf_op jit(solution)/shard_map/ppermute | solution.py:50
  56.7 1.0 %collective-permute-done.22.refs_0_ = bf16[2,2048]{1,0:T(2,128)(2,1)S(1)} collective-permute-done((bf16[2,2048]{1,0:T(2,128)(2,1)S(1)}, bf16[2,2048]{1,0:T(2,128)(2,1)S(1)}, u32[]{:S(2)}, u32[]{:S(2)}) %collective-permute-start.22) | collective-permute-done | bytes 8224 | tf_op jit(solution)/shard_map/ppermute | solution.py:50
  57.7 2.5 %collective-permute-done.23.refs_1_ = bf16[2,2048]{1,0:T(2,128)(2,1)S(1)} collective-permute-done((bf16[2,2048]{1,0:T(2,128)(2,1)S(1)}, bf16[2,2048]{1,0:T(2,128)(2,1)S(1)}, u32[]{:S(2)}, u32[]{:S(2)}) %collective-permute-start.23) | collective-permute-done | bytes 8224 | tf_op jit(solution)/shard_map/ppermute | solution.py:50
  60.2 0.1 collective-permute-done.24.refs_2_
  60.3 0.6 %finish.1 = bf16[2,2048]{1,0:T(2,128)(2,1)} custom-call(f32[2,2048]{1,0:T(2,128)S(1)} %get-tuple-element.88.updated_ref, bf16[2,2048]{1,0:T(2,128)(2,1)S(1)} %collective-permute-done.22.refs_0_, bf16[2,2048]{1,0:T(2,128)(2,1)S(1)} %collective-permute-done.23.refs_1_, bf16[2,2048]{1,0:T(2,128)(2,1)S(1)} %collective-permute-done.24.refs_2_, ...), custom_call_target="tpu_custom_call" | custom-call | tf_op jit(solution)/shard_map/finish/pallas_call | solution.py:639
  (27 shorter events, 0.1 us)
Async XLA Ops:
  0.0 8.4 %collective-permute-start = (bf16[2,2048]{1,0:T(2,128)(2,1)}, bf16[2,2048]{1,0:T(2,128)(2,1)S(1)}, u32[]{:S(2)}, u32[]{:S(2)}) collective-permute-start(bf16[2,2048]{1,0:T(2,128)(2,1)} %refs_5_.1), channel_id=1, source_target_pairs={{0,8},{4,12},{8,0},{12,4},{1,9},{5,13},{9,1},{13,5},{2,10},{6,14},... | collective-permute-start | bytes 24584 | tf_op jit(solution)/shard_map/ppermute | solution.py:31
  4.0 5.7 %collective-permute-start.1 = (bf16[2,2048]{1,0:T(2,128)(2,1)}, bf16[2,2048]{1,0:T(2,128)(2,1)S(1)}, u32[]{:S(2)}, u32[]{:S(2)}) collective-permute-start(bf16[2,2048]{1,0:T(2,128)(2,1)} %refs_5_.1), channel_id=1, source_target_pairs={{0,12},{4,8},{8,4},{12,0},{1,13},{5,9},{9,5},{13,1},{2,14},{6,10},... | collective-permute-start | bytes 24584 | tf_op jit(solution)/shard_map/ppermute | solution.py:31
  5.4 4.3 %collective-permute-start.2 = (bf16[2,2048]{1,0:T(2,128)(2,1)}, bf16[2,2048]{1,0:T(2,128)(2,1)S(1)}, u32[]{:S(2)}, u32[]{:S(2)}) collective-permute-start(bf16[2,2048]{1,0:T(2,128)(2,1)} %refs_5_.1), channel_id=1, source_target_pairs={{0,4},{4,0},{8,12},{12,8},{1,5},{5,1},{9,13},{13,9},{2,6},{6,2},{1... | collective-permute-start | bytes 24584 | tf_op jit(solution)/shard_map/ppermute | solution.py:31
  5.6 7.4 %copy-start.3 = (s32[8]{0:T(128)S(1)}, s32[8]{0:T(128)}, u32[]{:S(2)}) copy-start(s32[8]{0:T(128)} %param.23) | copy-start | bytes 100
  10.5 4.9 %collective-permute-start.3 = (bf16[2,1408]{1,0:T(2,128)(2,1)S(1)}, bf16[2,1408]{1,0:T(2,128)(2,1)S(1)}, u32[]{:S(2)}, u32[]{:S(2)}) collective-permute-start(bf16[2,1408]{1,0:T(2,128)(2,1)S(1)} %get-tuple-element.59), channel_id=1, source_target_pairs={{0,13},{1,12},{2,15},{3,14},{4,9},{5,8},{6,11},{7,10},{8,5},{9,4},... | collective-permute-start | bytes 16904 | tf_op jit(solution)/shard_map/ppermute | solution.py:50
  10.8 4.6 %collective-permute-start.4 = (bf16[2,1408]{1,0:T(2,128)(2,1)S(1)}, bf16[2,1408]{1,0:T(2,128)(2,1)S(1)}, u32[]{:S(2)}, u32[]{:S(2)}) collective-permute-start(bf16[2,1408]{1,0:T(2,128)(2,1)S(1)} %get-tuple-element.60), channel_id=1, source_target_pairs={{0,9},{1,8},{2,11},{3,10},{4,13},{5,12},{6,15},{7,14},{8,1},{9,0},... | collective-permute-start | bytes 16904 | tf_op jit(solution)/shard_map/ppermute | solution.py:50
  12.3 3.2 %collective-permute-start.5 = (bf16[2,1408]{1,0:T(2,128)(2,1)S(1)}, bf16[2,1408]{1,0:T(2,128)(2,1)S(1)}, u32[]{:S(2)}, u32[]{:S(2)}) collective-permute-start(bf16[2,1408]{1,0:T(2,128)(2,1)S(1)} %get-tuple-element.61), channel_id=1, source_target_pairs={{0,5},{1,4},{2,7},{3,6},{4,1},{5,0},{6,3},{7,2},{8,13},{9,12},{10,... | collective-permute-start | bytes 16904 | tf_op jit(solution)/shard_map/ppermute | solution.py:50
  15.5 4.8 %collective-permute-start.6 = (bf16[8,1408]{1,0:T(8,128)(2,1)S(1)}, bf16[8,1408]{1,0:T(8,128)(2,1)S(1)}, u32[]{:S(2)}, u32[]{:S(2)}) collective-permute-start(bf16[8,1408]{1,0:T(8,128)(2,1)S(1)} %stack.1.refs_1_.refs_0_), channel_id=1, source_target_pairs={{0,3},{1,2},{2,1},{3,0},{4,7},{5,6},{6,5},{7,4},{8,11},{9,10},{10,... | collective-permute-start | bytes 67592 | tf_op jit(solution)/shard_map/ppermute | solution.py:31
  17.9 3.8 %collective-permute-start.7 = (bf16[8,1408]{1,0:T(8,128)(2,1)S(1)}, bf16[8,1408]{1,0:T(8,128)(2,1)S(1)}, u32[]{:S(2)}, u32[]{:S(2)}) collective-permute-start(bf16[8,1408]{1,0:T(8,128)(2,1)S(1)} %stack.1.refs_1_.refs_0_), channel_id=1, source_target_pairs={{0,2},{1,3},{2,0},{3,1},{4,6},{5,7},{6,4},{7,5},{8,10},{9,11},{10,... | collective-permute-start | bytes 67592 | tf_op jit(solution)/shard_map/ppermute | solution.py:31
  18.4 3.3 %collective-permute-start.8 = (bf16[8,1408]{1,0:T(8,128)(2,1)S(1)}, bf16[8,1408]{1,0:T(8,128)(2,1)S(1)}, u32[]{:S(2)}, u32[]{:S(2)}) collective-permute-start(bf16[8,1408]{1,0:T(8,128)(2,1)S(1)} %stack.1.refs_1_.refs_0_), channel_id=1, source_target_pairs={{0,1},{1,0},{2,3},{3,2},{4,5},{5,4},{6,7},{7,6},{8,9},{9,8},{10,11... | collective-permute-start | bytes 67592 | tf_op jit(solution)/shard_map/ppermute | solution.py:31
  18.5 8.8 %copy-start = (bf16[2048,3584]{1,0:T(8,128)(2,1)S(1)}, bf16[2048,3584]{1,0:T(8,128)(2,1)}, u32[]{:S(2)}) copy-start(bf16[2048,3584]{1,0:T(8,128)(2,1)} %gate_ref.3) | copy-start | bytes 44040196
  23.2 4.0 %collective-permute-start.10 = (bf16[80,128]{1,0:T(8,128)(2,1)S(1)}, bf16[80,128]{1,0:T(8,128)(2,1)S(1)}, u32[]{:S(2)}, u32[]{:S(2)}) collective-permute-start(bf16[80,128]{1,0:T(8,128)(2,1)S(1)} %attend.1.refs_1_.refs_3_), channel_id=1, source_target_pairs={{0,2},{1,3},{2,0},{3,1},{4,6},{5,7},{6,4},{7,5},{8,10},{9,11},{10,... | collective-permute-start | bytes 61448 | tf_op jit(solution)/shard_map/ppermute | solution.py:31
  23.8 3.4 %collective-permute-start.11 = (bf16[80,128]{1,0:T(8,128)(2,1)S(1)}, bf16[80,128]{1,0:T(8,128)(2,1)S(1)}, u32[]{:S(2)}, u32[]{:S(2)}) collective-permute-start(bf16[80,128]{1,0:T(8,128)(2,1)S(1)} %attend.1.refs_1_.refs_3_), channel_id=1, source_target_pairs={{0,3},{1,2},{2,1},{3,0},{4,7},{5,6},{6,5},{7,4},{8,11},{9,10},{10,... | collective-permute-start | bytes 61448 | tf_op jit(solution)/shard_map/ppermute | solution.py:31
  23.9 3.4 %collective-permute-start.9 = (bf16[80,128]{1,0:T(8,128)(2,1)S(1)}, bf16[80,128]{1,0:T(8,128)(2,1)S(1)}, u32[]{:S(2)}, u32[]{:S(2)}) collective-permute-start(bf16[80,128]{1,0:T(8,128)(2,1)S(1)} %attend.1.refs_1_.refs_3_), channel_id=1, source_target_pairs={{0,1},{1,0},{2,3},{3,2},{4,5},{5,4},{6,7},{7,6},{8,9},{9,8},{10,11... | collective-permute-start | bytes 61448 | tf_op jit(solution)/shard_map/ppermute | solution.py:31
  27.3 5.9 %copy-start.1 = (bf16[2048,3584]{1,0:T(8,128)(2,1)S(1)}, bf16[2048,3584]{1,0:T(8,128)(2,1)}, u32[]{:S(2)}) copy-start(bf16[2048,3584]{1,0:T(8,128)(2,1)} %up_ref.3) | copy-start | bytes 44040196
  27.6 5.5 %collective-permute-start.12 = (bf16[2,1024]{1,0:T(2,128)(2,1)S(1)}, bf16[2,1024]{1,0:T(2,128)(2,1)S(1)}, u32[]{:S(2)}, u32[]{:S(2)}) collective-permute-start(bf16[2,1024]{1,0:T(2,128)(2,1)S(1)} %get-tuple-element.75), channel_id=1, source_target_pairs={{0,13},{1,12},{2,15},{3,14},{4,9},{5,8},{6,11},{7,10},{8,5},{9,4},... | collective-permute-start | bytes 12296 | tf_op jit(solution)/shard_map/ppermute | solution.py:50
  29.2 3.9 %collective-permute-start.13 = (bf16[2,1024]{1,0:T(2,128)(2,1)S(1)}, bf16[2,1024]{1,0:T(2,128)(2,1)S(1)}, u32[]{:S(2)}, u32[]{:S(2)}) collective-permute-start(bf16[2,1024]{1,0:T(2,128)(2,1)S(1)} %get-tuple-element.76), channel_id=1, source_target_pairs={{0,9},{1,8},{2,11},{3,10},{4,13},{5,12},{6,15},{7,14},{8,1},{9,0},... | collective-permute-start | bytes 12296 | tf_op jit(solution)/shard_map/ppermute | solution.py:50
  29.6 3.5 %collective-permute-start.14 = (bf16[2,1024]{1,0:T(2,128)(2,1)S(1)}, bf16[2,1024]{1,0:T(2,128)(2,1)S(1)}, u32[]{:S(2)}, u32[]{:S(2)}) collective-permute-start(bf16[2,1024]{1,0:T(2,128)(2,1)S(1)} %get-tuple-element.77), channel_id=1, source_target_pairs={{0,5},{1,4},{2,7},{3,6},{4,1},{5,0},{6,3},{7,2},{8,13},{9,12},{10,... | collective-permute-start | bytes 12296 | tf_op jit(solution)/shard_map/ppermute | solution.py:50
  33.2 8.1 %copy-start.2 = (bf16[2048,3584]{1,0:T(8,128)(2,1)S(1)}, bf16[2048,3584]{1,0:T(8,128)(2,1)}, u32[]{:S(2)}) copy-start(bf16[2048,3584]{1,0:T(8,128)(2,1)} %up_ref.3) | copy-start | bytes 44040196
  34.1 6.1 %collective-permute-start.15 = (bf16[8,2048]{1,0:T(8,128)(2,1)S(1)}, bf16[8,2048]{1,0:T(8,128)(2,1)S(1)}, u32[]{:S(2)}, u32[]{:S(2)}) collective-permute-start(bf16[8,2048]{1,0:T(8,128)(2,1)S(1)} %get-tuple-element.84), channel_id=1, source_target_pairs={{0,12},{1,13},{2,14},{3,15},{4,8},{5,9},{6,10},{7,11},{8,4},{9,5},... | collective-permute-start | bytes 98312 | tf_op jit(solution)/shard_map/ppermute | solution.py:50
  36.1 5.2 %collective-permute-start.16 = (bf16[8,2048]{1,0:T(8,128)(2,1)S(1)}, bf16[8,2048]{1,0:T(8,128)(2,1)S(1)}, u32[]{:S(2)}, u32[]{:S(2)}) collective-permute-start(bf16[8,2048]{1,0:T(8,128)(2,1)S(1)} %get-tuple-element.85), channel_id=1, source_target_pairs={{0,8},{1,9},{2,10},{3,11},{4,12},{5,13},{6,14},{7,15},{8,0},{9,1},... | collective-permute-start | bytes 98312 | tf_op jit(solution)/shard_map/ppermute | solution.py:50
  37.2 4.1 %collective-permute-start.17 = (bf16[8,2048]{1,0:T(8,128)(2,1)S(1)}, bf16[8,2048]{1,0:T(8,128)(2,1)S(1)}, u32[]{:S(2)}, u32[]{:S(2)}) collective-permute-start(bf16[8,2048]{1,0:T(8,128)(2,1)S(1)} %get-tuple-element.86), channel_id=1, source_target_pairs={{0,4},{1,5},{2,6},{3,7},{4,0},{5,1},{6,2},{7,3},{8,12},{9,13},{10,... | collective-permute-start | bytes 98312 | tf_op jit(solution)/shard_map/ppermute | solution.py:50
  43.3 2.6 %collective-permute-start.20 = (bf16[8,3712]{1,0:T(8,128)(2,1)S(1)}, bf16[8,3712]{1,0:T(8,128)(2,1)S(1)}, u32[]{:S(2)}, u32[]{:S(2)}) collective-permute-start(bf16[8,3712]{1,0:T(8,128)(2,1)S(1)} %get-tuple-element.90.first_ref), channel_id=1, source_target_pairs={{0,1},{1,0},{2,3},{3,2},{4,5},{5,4},{6,7},{7,6},{8,9},{9,8},{10,11... | collective-permute-start | bytes 178184 | tf_op jit(solution)/shard_map/ppermute | solution.py:31
  43.3 4.8 %slice-start = ((s8[14680064]{0:T(1024)(128)(4,1)}), s8[4194304]{0:T(1024)(128)(4,1)S(1)}, s32[]{:S(2)}) async-start(s8[14680064]{0:T(1024)(128)(4,1)} %bitcast.4), calls=%async_computation | async-start | bytes 8388608
  43.3 4.8 %slice-start.1 = ((s8[14680064]{0:T(1024)(128)(4,1)}), s8[4194304]{0:T(1024)(128)(4,1)S(1)}, s32[]{:S(2)}) async-start(s8[14680064]{0:T(1024)(128)(4,1)} %bitcast.4), calls=%async_computation.1 | async-start | bytes 8388608
  43.3 4.7 %slice-start.2 = ((s8[14680064]{0:T(1024)(128)(4,1)}), s8[4194304]{0:T(1024)(128)(4,1)S(1)}, s32[]{:S(2)}) async-start(s8[14680064]{0:T(1024)(128)(4,1)} %bitcast.4), calls=%async_computation.2 | async-start | bytes 8388608
  43.3 5.2 %slice-start.3 = ((s8[14680064]{0:T(1024)(128)(4,1)}), s8[2097152]{0:T(1024)(128)(4,1)S(1)}, s32[]{:S(2)}) async-start(s8[14680064]{0:T(1024)(128)(4,1)} %bitcast.4), calls=%async_computation.3 | async-start | bytes 4194304
  45.3 1.8 %collective-permute-start.18 = (bf16[8,3584]{1,0:T(8,128)(2,1)S(1)}, bf16[8,3584]{1,0:T(8,128)(2,1)S(1)}, u32[]{:S(2)}, u32[]{:S(2)}) collective-permute-start(bf16[8,3584]{1,0:T(8,128)(2,1)S(1)} %second_gate_up.1.first_ref), channel_id=1, source_target_pairs={{0,1},{1,0},{2,3},{3,2},{4,5},{5,4},{6,7},{7,6},{8,9},{9,8},{10,11... | collective-permute-start | bytes 172040 | tf_op jit(solution)/shard_map/ppermute | solution.py:31
  45.9 4.6 %collective-permute-start.21 = (bf16[8,3712]{1,0:T(8,128)(2,1)S(1)}, bf16[8,3712]{1,0:T(8,128)(2,1)S(1)}, u32[]{:S(2)}, u32[]{:S(2)}) collective-permute-start(bf16[8,3712]{1,0:T(8,128)(2,1)S(1)} %pair_sum.3.near_ref), channel_id=1, source_target_pairs={{0,2},{1,3},{2,0},{3,1},{4,6},{5,7},{6,4},{7,5},{8,10},{9,11},{10,... | collective-permute-start | bytes 178184 | tf_op jit(solution)/shard_map/ppermute | solution.py:31
  47.1 4.6 %collective-permute-start.19 = (bf16[8,3584]{1,0:T(8,128)(2,1)S(1)}, bf16[8,3584]{1,0:T(8,128)(2,1)S(1)}, u32[]{:S(2)}, u32[]{:S(2)}) collective-permute-start(bf16[8,3584]{1,0:T(8,128)(2,1)S(1)} %pair_sum.2.after_ref.near_ref), channel_id=1, source_target_pairs={{0,2},{1,3},{2,0},{3,1},{4,6},{5,7},{6,4},{7,5},{8,10},{9,11},{10,... | collective-permute-start | bytes 172040 | tf_op jit(solution)/shard_map/ppermute | solution.py:31
  53.1 4.6 %collective-permute-start.22 = (bf16[2,2048]{1,0:T(2,128)(2,1)S(1)}, bf16[2,2048]{1,0:T(2,128)(2,1)S(1)}, u32[]{:S(2)}, u32[]{:S(2)}) collective-permute-start(bf16[2,2048]{1,0:T(2,128)(2,1)S(1)} %get-tuple-element.93), channel_id=1, source_target_pairs={{0,8},{1,9},{2,10},{3,11},{4,12},{5,13},{6,14},{7,15},{8,0},{9,1},... | collective-permute-start | bytes 24584 | tf_op jit(solution)/shard_map/ppermute | solution.py:50
  54.8 5.4 %collective-permute-start.23 = (bf16[2,2048]{1,0:T(2,128)(2,1)S(1)}, bf16[2,2048]{1,0:T(2,128)(2,1)S(1)}, u32[]{:S(2)}, u32[]{:S(2)}) collective-permute-start(bf16[2,2048]{1,0:T(2,128)(2,1)S(1)} %get-tuple-element.94), channel_id=1, source_target_pairs={{0,12},{1,13},{2,14},{3,15},{4,8},{5,9},{6,10},{7,11},{8,4},{9,5},... | collective-permute-start | bytes 24584 | tf_op jit(solution)/shard_map/ppermute | solution.py:50
  56.7 3.7 %collective-permute-start.24 = (bf16[2,2048]{1,0:T(2,128)(2,1)S(1)}, bf16[2,2048]{1,0:T(2,128)(2,1)S(1)}, u32[]{:S(2)}, u32[]{:S(2)}) collective-permute-start(bf16[2,2048]{1,0:T(2,128)(2,1)S(1)} %get-tuple-element.95), channel_id=1, source_target_pairs={{0,4},{1,5},{2,6},{3,7},{4,0},{5,1},{6,2},{7,3},{8,12},{9,13},{10,... | collective-permute-start | bytes 24584 | tf_op jit(solution)/shard_map/ppermute | solution.py:50

commit v20 on v19

--- a/solution.py
+++ b/solution.py
@@ -227,7 +227,7 @@
 
 
 def stack_kernel(*refs):
-    refs[-2][...] = join_rows(refs[:-2][::-1], refs[-1]).astype(refs[-2].dtype)
+    refs[-2][...] = join_rows(in_slot_order(refs[:-2]), refs[-1]).astype(refs[-2].dtype)
 
 
 def stack(pieces):
@@ -240,7 +240,7 @@
         scratch_shapes=[pltpu.VMEM(shape, jnp.float32)],
         compiler_params=params(1),
         name="stack",
-    )(*pieces[::-1])
+    )(*in_start_order(pieces))
 
 
 def attend_kernel(
@@ -643,7 +643,7 @@
         out_specs=in_vmem,
         compiler_params=params(1),
         name="finish",
-    )(updated, *in_start_order(parts))
+    )(updated, *parts[::-1])
 
 
 def rotation_tables(positions, repeats):

time: 61.1 us -> 60.8 us (level)
  waiting for transfers between devices: 12.2 us -> 11.1 us
    ppermute x12, starting transfers between devices: 14.3 us -> 15.4 us  [scatter_slots(): got.append(lax.ppermute(pieces[k], ('tensor', 'inner'), pairs))]
    ppermute x12, waiting for transfers between devices: 7.28 us -> 6.24 us  [scatter_slots(): got.append(lax.ppermute(pieces[k], ('tensor', 'inner'), pairs))]
where the time goes in v20:
time: 60.8 us; the launch traced here: 60.6 us
  starting transfers between devices  28.4 us (47%)
  Pallas kernels  20 us (33%)
  waiting for transfers between devices  11.1 us (18%)
  local copies, waits for them, and re-layouts  0.63 us (1%)
    ppermute x12, starting transfers between devices, scatter_slots(): got.append(lax.ppermute(pieces[k], ('tensor', 'inner'), pairs))  15.4 us
    ppermute x13, starting transfers between devices, swap_with(): return lax.ppermute(value, axis, [(i, i ^ step) for i in range(count)])  13 us
    pallas_call x5, Pallas kernels, load(): pl.pallas_call(functools.partial(load_kernel, spans), out_shape=tuple((pl...  9.26 us
    ppermute x12, waiting for transfers between devices, scatter_slots(): got.append(lax.ppermute(pieces[k], ('tensor', 'inner'), pairs))  6.24 us
    ppermute x13, waiting for transfers between devices, swap_with(): return lax.ppermute(value, axis, [(i, i ^ step) for i in range(count)])  4.89 us
    pallas_call x1, Pallas kernels, first_gate_up(): pl.pallas_call(functools.partial(first_gate_up_kernel, slots, count), out...  2 us
    pallas_call x1, Pallas kernels, second_gate_up(): pl.pallas_call(functools.partial(second_gate_up_kernel, first, count), ou...  2 us
    pallas_call x1, Pallas kernels, attend(): pl.pallas_call(functools.partial(attend_kernel, slots, len(parts)), out_s...  1.48 us
  transfers between devices with their start and end apart: 25, of which 11 were waited for; matrix products, arithmetic and copies ran while one was open for 0% of the time, Pallas kernels for 21%

profile of v20, /device:TPU:0, one launch (start us, length us, event | category | flops | bytes accessed | tf_op | source)
XLA Modules:
  0.0 60.6 jit_solution(6732932909299491244)
XLA Ops:
  0.0 4.0 %collective-permute-start = (bf16[2,2048]{1,0:T(2,128)(2,1)}, bf16[2,2048]{1,0:T(2,128)(2,1)S(1)}, u32[]{:S(2)}, u32[]{:S(2)}) collective-permute-start(bf16[2,2048]{1,0:T(2,128)(2,1)} %refs_5_.1), channel_id=1, source_target_pairs={{0,8},{4,12},{8,0},{12,4},{1,9},{5,13},{9,1},{13,5},{2,10},{6,14},... | collective-permute-start | bytes 24584 | tf_op jit(solution)/shard_map/ppermute | solution.py:31
  4.0 1.3 %collective-permute-start.1 = (bf16[2,2048]{1,0:T(2,128)(2,1)}, bf16[2,2048]{1,0:T(2,128)(2,1)S(1)}, u32[]{:S(2)}, u32[]{:S(2)}) collective-permute-start(bf16[2,2048]{1,0:T(2,128)(2,1)} %refs_5_.1), channel_id=1, source_target_pairs={{0,12},{4,8},{8,4},{12,0},{1,13},{5,9},{9,5},{13,1},{2,14},{6,10},... | collective-permute-start | bytes 24584 | tf_op jit(solution)/shard_map/ppermute | solution.py:31
  5.4 0.2 collective-permute-start.2
  5.6 2.7 %load.5 = (bf16[2,2048]{1,0:T(2,128)(2,1)S(1)}, bf16[2048]{0:T(1024)(128)(2,1)S(1)}, bf16[2048]{0:T(1024)(128)(2,1)S(1)}, bf16[2048,256]{1,0:T(8,128)(2,1)S(1)}, bf16[2048,1024]{1,0:T(8,128)(2,1)S(1)}) custom-call(bf16[2,2048]{1,0:T(2,128)(2,1)} %refs_5_.1, bf16[2048]{0:T(1024)(128)(2,1)} %refs_1_.1, bf16[2048]{0:T(1024)(128)(2,1)} %refs_2_.1, ...), custom_call_target="tpu_custom_call" | custom-call | bytes 5259264 | tf_op jit(solution)/shard_map/load/pallas_call | solution.py:159
  8.4 1.3 %collective-permute-done.1.refs_1_ = bf16[2,2048]{1,0:T(2,128)(2,1)S(1)} collective-permute-done((bf16[2,2048]{1,0:T(2,128)(2,1)}, bf16[2,2048]{1,0:T(2,128)(2,1)S(1)}, u32[]{:S(2)}, u32[]{:S(2)}) %collective-permute-start.1) | collective-permute-done | bytes 8224 | tf_op jit(solution)/shard_map/ppermute | solution.py:31
  9.7 0.8 %project_qkv.1 = (f32[8,2048]{1,0:T(8,128)S(1)}, bf16[2,1408]{1,0:T(2,128)(2,1)S(1)}, bf16[2,1408]{1,0:T(2,128)(2,1)S(1)}, bf16[2,1408]{1,0:T(2,128)(2,1)S(1)}, bf16[2,1408]{1,0:T(2,128)(2,1)S(1)}) custom-call(bf16[2048]{0:T(1024)(128)(2,1)S(1)} %get-tuple-element.51.gain_ref, bf16[2048,1024]{1,0:T(8,128)(2,1)S(1)} %get-tuple-element.52.wq_ref, ...), custom_call_target="tpu_custom_call" | custom-call | tf_op jit(solution)/shard_map/project_qkv/pallas_call | solution.py:212
  10.5 0.2 collective-permute-start.3
  10.7 2.5 %collective-permute-start.4 = (bf16[2,1408]{1,0:T(2,128)(2,1)S(1)}, bf16[2,1408]{1,0:T(2,128)(2,1)S(1)}, u32[]{:S(2)}, u32[]{:S(2)}) collective-permute-start(bf16[2,1408]{1,0:T(2,128)(2,1)S(1)} %get-tuple-element.60), channel_id=1, source_target_pairs={{0,13},{1,12},{2,15},{3,14},{4,9},{5,8},{6,11},{7,10},{8,5},{9,4},... | collective-permute-start | bytes 16904 | tf_op jit(solution)/shard_map/ppermute | solution.py:50
  13.2 0.1 fusion.4
  13.2 1.6 %load.6.key_ref = bf16[2,4096,128]{2,1,0:T(8,128)(2,1)S(1)} custom-call(bf16[2,4096,128]{2,1,0:T(8,128)(2,1)} %bitcast.8, f32[8,2048]{1,0:T(8,128)S(1)} %get-tuple-element.56.refs_1_.rows_ref), custom_call_target="tpu_custom_call" | custom-call | bytes 2097152 | tf_op jit(solution)/shard_map/load/pallas_call | solution.py:159
  14.9 0.0 collective-permute-done.3.refs_0_
  14.9 0.7 %collective-permute-done.4.refs_1_ = bf16[2,1408]{1,0:T(2,128)(2,1)S(1)} collective-permute-done((bf16[2,1408]{1,0:T(2,128)(2,1)S(1)}, bf16[2,1408]{1,0:T(2,128)(2,1)S(1)}, u32[]{:S(2)}, u32[]{:S(2)}) %collective-permute-start.4) | collective-permute-done | bytes 5664 | tf_op jit(solution)/shard_map/ppermute | solution.py:50
  15.5 0.7 %collective-permute-done.5.refs_2_ = bf16[2,1408]{1,0:T(2,128)(2,1)S(1)} collective-permute-done((bf16[2,1408]{1,0:T(2,128)(2,1)S(1)}, bf16[2,1408]{1,0:T(2,128)(2,1)S(1)}, u32[]{:S(2)}, u32[]{:S(2)}) %collective-permute-start.5) | collective-permute-done | bytes 5664 | tf_op jit(solution)/shard_map/ppermute | solution.py:50
  16.2 2.0 %collective-permute-start.6 = (bf16[8,1408]{1,0:T(8,128)(2,1)S(1)}, bf16[8,1408]{1,0:T(8,128)(2,1)S(1)}, u32[]{:S(2)}, u32[]{:S(2)}) collective-permute-start(bf16[8,1408]{1,0:T(8,128)(2,1)S(1)} %stack.1.refs_1_.refs_0_), channel_id=1, source_target_pairs={{0,3},{1,2},{2,1},{3,0},{4,7},{5,6},{6,5},{7,4},{8,11},{9,10},{10,... | collective-permute-start | bytes 67592 | tf_op jit(solution)/shard_map/ppermute | solution.py:31
  18.3 0.5 collective-permute-start.7
  18.8 0.0 collective-permute-start.8
  18.8 0.1 fusion
  18.9 0.0 copy-start
  18.9 1.8 %load.7.value_ref = bf16[2,4096,128]{2,1,0:T(8,128)(2,1)S(1)} custom-call(bf16[2,4096,128]{2,1,0:T(8,128)(2,1)} %bitcast.9, bf16[8,1408]{1,0:T(8,128)(2,1)S(1)} %stack.1.refs_1_.refs_0_), custom_call_target="tpu_custom_call" | custom-call | bytes 2097152 | tf_op jit(solution)/shard_map/load/pallas_call | solution.py:159
  20.7 0.0 collective-permute-done.6.refs_3_
  20.7 1.3 %collective-permute-done.7.refs_2_ = bf16[8,1408]{1,0:T(8,128)(2,1)S(1)} collective-permute-done((bf16[8,1408]{1,0:T(8,128)(2,1)S(1)}, bf16[8,1408]{1,0:T(8,128)(2,1)S(1)}, u32[]{:S(2)}, u32[]{:S(2)}) %collective-permute-start.7) | collective-permute-done | bytes 22560 | tf_op jit(solution)/shard_map/ppermute | solution.py:31
  22.1 0.0 collective-permute-done.8.refs_1_
  22.1 0.1 broadcast_in_dim.10.lengths_ref
  22.1 1.5 %attend.1.refs_1_.refs_3_ = bf16[80,128]{1,0:T(8,128)(2,1)S(1)} custom-call(s32[2,128]{1,0:T(2,128)S(1)} %broadcast_in_dim.10.lengths_ref, f32[8,128]{1,0:T(8,128)S(1)} %bitcast.6, f32[8,128]{1,0:T(8,128)S(1)} %bitcast.7, bf16[2,4096,128]{2,1,0:T(8,128)(2,1)S(1)} %load.6.key_ref, bf16[2,4096,128]{2,1,0:T(8,128)(2,1)S(1)} %load.7.value_ref, ...), custom_call_target="tpu_custom_call" | custom-call | tf_op jit(solution)/shard_map/attend/pallas_call | solution.py:356
  23.6 0.6 collective-permute-start.10
  24.2 0.0 collective-permute-start.11
  24.3 1.6 %collective-permute-start.9 = (bf16[80,128]{1,0:T(8,128)(2,1)S(1)}, bf16[80,128]{1,0:T(8,128)(2,1)S(1)}, u32[]{:S(2)}, u32[]{:S(2)}) collective-permute-start(bf16[80,128]{1,0:T(8,128)(2,1)S(1)} %attend.1.refs_1_.refs_3_), channel_id=1, source_target_pairs={{0,1},{1,0},{2,3},{3,2},{4,5},{5,4},{6,7},{7,6},{8,9},{9,8},{10,11... | collective-permute-start | bytes 61448 | tf_op jit(solution)/shard_map/ppermute | solution.py:31
  25.8 1.5 %load.8.upper_ref = bf16[512,2048]{1,0:T(8,128)(2,1)S(1)} custom-call(bf16[1024,2048]{1,0:T(8,128)(2,1)} %refs_0_.5, bf16[80,128]{1,0:T(8,128)(2,1)S(1)} %attend.1.refs_1_.refs_3_), custom_call_target="tpu_custom_call" | custom-call | bytes 2097152 | tf_op jit(solution)/shard_map/load/pallas_call | solution.py:159
  27.4 0.3 collective-permute-done.10.refs_1_
  27.7 0.0 collective-permute-done.11.refs_0_
  27.7 0.0 collective-permute-done.9.refs_2_
  27.7 0.0 copy-start.1
  27.7 0.3 combine.1
  27.9 1.3 %collective-permute-start.12 = (bf16[2,1024]{1,0:T(2,128)(2,1)S(1)}, bf16[2,1024]{1,0:T(2,128)(2,1)S(1)}, u32[]{:S(2)}, u32[]{:S(2)}) collective-permute-start(bf16[2,1024]{1,0:T(2,128)(2,1)S(1)} %get-tuple-element.75), channel_id=1, source_target_pairs={{0,13},{1,12},{2,15},{3,14},{4,9},{5,8},{6,11},{7,10},{8,5},{9,4},... | collective-permute-start | bytes 12296 | tf_op jit(solution)/shard_map/ppermute | solution.py:50
  29.3 0.0 collective-permute-start.13
  29.3 2.5 %collective-permute-start.14 = (bf16[2,1024]{1,0:T(2,128)(2,1)S(1)}, bf16[2,1024]{1,0:T(2,128)(2,1)S(1)}, u32[]{:S(2)}, u32[]{:S(2)}) collective-permute-start(bf16[2,1024]{1,0:T(2,128)(2,1)S(1)} %get-tuple-element.77), channel_id=1, source_target_pairs={{0,5},{1,4},{2,7},{3,6},{4,1},{5,0},{6,3},{7,2},{8,13},{9,12},{10,... | collective-permute-start | bytes 12296 | tf_op jit(solution)/shard_map/ppermute | solution.py:50
  31.8 1.6 %load.9.lower_ref = bf16[512,2048]{1,0:T(8,128)(2,1)S(1)} custom-call(bf16[1024,2048]{1,0:T(8,128)(2,1)} %refs_0_.5, bf16[2,1024]{1,0:T(2,128)(2,1)S(1)} %get-tuple-element.83.refs_1_.refs_3_), custom_call_target="tpu_custom_call" | custom-call | bytes 2097152 | tf_op jit(solution)/shard_map/load/pallas_call | solution.py:159
  33.4 0.0 collective-permute-done.13.refs_1_
  33.5 0.0 copy-start.2
  33.5 0.9 %project_out.1 = (bf16[8,2048]{1,0:T(8,128)(2,1)S(1)}, bf16[8,2048]{1,0:T(8,128)(2,1)S(1)}, bf16[8,2048]{1,0:T(8,128)(2,1)S(1)}, bf16[8,2048]{1,0:T(8,128)(2,1)S(1)}) custom-call(bf16[512,2048]{1,0:T(8,128)(2,1)S(1)} %load.8.upper_ref, bf16[512,2048]{1,0:T(8,128)(2,1)S(1)} %load.9.lower_ref, bf16[2,1024]{1,0:T(2,128)(2,1)S(1)} %collective-permute-done.12.refs_0_, ...), custom_call_target="tpu_custom_call" | custom-call | tf_op jit(solution)/shard_map/project_out/pallas_call | solution.py:453
  34.4 2.0 %collective-permute-start.15 = (bf16[8,2048]{1,0:T(8,128)(2,1)S(1)}, bf16[8,2048]{1,0:T(8,128)(2,1)S(1)}, u32[]{:S(2)}, u32[]{:S(2)}) collective-permute-start(bf16[8,2048]{1,0:T(8,128)(2,1)S(1)} %get-tuple-element.84), channel_id=1, source_target_pairs={{0,12},{1,13},{2,14},{3,15},{4,8},{5,9},{6,10},{7,11},{8,4},{9,5},... | collective-permute-start | bytes 98312 | tf_op jit(solution)/shard_map/ppermute | solution.py:50
  36.4 1.2 %collective-permute-start.16 = (bf16[8,2048]{1,0:T(8,128)(2,1)S(1)}, bf16[8,2048]{1,0:T(8,128)(2,1)S(1)}, u32[]{:S(2)}, u32[]{:S(2)}) collective-permute-start(bf16[8,2048]{1,0:T(8,128)(2,1)S(1)} %get-tuple-element.85), channel_id=1, source_target_pairs={{0,8},{1,9},{2,10},{3,11},{4,12},{5,13},{6,14},{7,15},{8,0},{9,1},... | collective-permute-start | bytes 98312 | tf_op jit(solution)/shard_map/ppermute | solution.py:50
  37.6 1.2 %collective-permute-start.17 = (bf16[8,2048]{1,0:T(8,128)(2,1)S(1)}, bf16[8,2048]{1,0:T(8,128)(2,1)S(1)}, u32[]{:S(2)}, u32[]{:S(2)}) collective-permute-start(bf16[8,2048]{1,0:T(8,128)(2,1)S(1)} %get-tuple-element.86), channel_id=1, source_target_pairs={{0,4},{1,5},{2,6},{3,7},{4,0},{5,1},{6,2},{7,3},{8,12},{9,13},{10,... | collective-permute-start | bytes 98312 | tf_op jit(solution)/shard_map/ppermute | solution.py:50
  38.8 1.6 %collective-permute-done.15.refs_0_ = bf16[8,2048]{1,0:T(8,128)(2,1)S(1)} collective-permute-done((bf16[8,2048]{1,0:T(8,128)(2,1)S(1)}, bf16[8,2048]{1,0:T(8,128)(2,1)S(1)}, u32[]{:S(2)}, u32[]{:S(2)}) %collective-permute-start.15) | collective-permute-done | bytes 32800 | tf_op jit(solution)/shard_map/ppermute | solution.py:50
  40.4 1.2 %collective-permute-done.16.refs_1_ = bf16[8,2048]{1,0:T(8,128)(2,1)S(1)} collective-permute-done((bf16[8,2048]{1,0:T(8,128)(2,1)S(1)}, bf16[8,2048]{1,0:T(8,128)(2,1)S(1)}, u32[]{:S(2)}, u32[]{:S(2)}) %collective-permute-start.16) | collective-permute-done | bytes 32800 | tf_op jit(solution)/shard_map/ppermute | solution.py:50
  41.6 0.3 collective-permute-done.17.refs_2_
  42.0 2.0 %first_gate_up.1 = (bf16[8,3712]{1,0:T(8,128)(2,1)S(1)}, f32[2,2048]{1,0:T(2,128)S(1)}, bf16[8,2048]{1,0:T(8,128)(2,1)S(1)}) custom-call(f32[8,2048]{1,0:T(8,128)S(1)} %get-tuple-element.56.refs_1_.rows_ref, bf16[2048]{0:T(1024)(128)(2,1)S(1)} %get-tuple-element.57.gain_ref, bf16[2048,3584]{1,0:T(8,128)(2,1)S(1)} %copy-done, ...), custom_call_target="tpu_custom_call" | custom-call | flops 117440512 | bytes 14680064 | tf_op jit(solution)/shard_map/first_gate_up/pallas_call | solution.py:509
  43.9 0.0 collective-permute-start.20
  44.0 0.0 slice-start.1
  44.0 0.0 slice-start.2
  44.0 2.0 %second_gate_up.1.first_ref = bf16[8,3584]{1,0:T(8,128)(2,1)S(1)} custom-call(bf16[8,2048]{1,0:T(8,128)(2,1)S(1)} %get-tuple-element.89.scaled_ref, bf16[2048,3584]{1,0:T(8,128)(2,1)S(1)} %copy-done, bf16[2048,3584]{1,0:T(8,128)(2,1)S(1)} %copy-done.2), custom_call_target="tpu_custom_call" | custom-call | flops 117440512 | bytes 14680064 | tf_op jit(solution)/shard_map/second_gate_up/pallas_call | solution.py:538
  46.0 0.5 collective-permute-start.18
  46.5 1.3 %collective-permute-start.21 = (bf16[8,3712]{1,0:T(8,128)(2,1)S(1)}, bf16[8,3712]{1,0:T(8,128)(2,1)S(1)}, u32[]{:S(2)}, u32[]{:S(2)}) collective-permute-start(bf16[8,3712]{1,0:T(8,128)(2,1)S(1)} %pair_sum.3.near_ref), channel_id=1, source_target_pairs={{0,2},{1,3},{2,0},{3,1},{4,6},{5,7},{6,4},{7,5},{8,10},{9,11},{10,... | collective-permute-start | bytes 178184 | tf_op jit(solution)/shard_map/ppermute | solution.py:31
  47.9 0.9 %collective-permute-start.19 = (bf16[8,3584]{1,0:T(8,128)(2,1)S(1)}, bf16[8,3584]{1,0:T(8,128)(2,1)S(1)}, u32[]{:S(2)}, u32[]{:S(2)}) collective-permute-start(bf16[8,3584]{1,0:T(8,128)(2,1)S(1)} %pair_sum.2.after_ref.near_ref), channel_id=1, source_target_pairs={{0,2},{1,3},{2,0},{3,1},{4,6},{5,7},{6,4},{7,5},{8,10},{9,11},{10,... | collective-permute-start | bytes 172040 | tf_op jit(solution)/shard_map/ppermute | solution.py:31
  48.7 0.5 slice-done.3
  49.2 1.9 %collective-permute-done.21.far_ref = bf16[8,3712]{1,0:T(8,128)(2,1)S(1)} collective-permute-done((bf16[8,3712]{1,0:T(8,128)(2,1)S(1)}, bf16[8,3712]{1,0:T(8,128)(2,1)S(1)}, u32[]{:S(2)}, u32[]{:S(2)}) %collective-permute-start.21) | collective-permute-done | bytes 59424 | tf_op jit(solution)/shard_map/ppermute | solution.py:31
  51.2 1.3 %first_down.1 = (f32[8,2048]{1,0:T(8,128)S(1)}, f32[8,128]{1,0:T(8,128)S(1)}) custom-call(bf16[8,3712]{1,0:T(8,128)(2,1)S(1)} %pair_sum.3.near_ref, bf16[8,3712]{1,0:T(8,128)(2,1)S(1)} %collective-permute-done.21.far_ref, bf16[3584,2048]{1,0:T(8,128)(2,1)S(1)} %bitcast.5, f32[8,128]{1,0:T(8,128)S(1)} %hold.1.token_ref), custom_call_target="tpu_custom_call" | custom-call | flops 58720256 | bytes 7340032 | tf_op jit(solution)/shard_map/first_down/pallas_call | solution.py:576
  52.4 1.3 %second_down.1 = (bf16[2,2048]{1,0:T(2,128)(2,1)S(1)}, bf16[2,2048]{1,0:T(2,128)(2,1)S(1)}, bf16[2,2048]{1,0:T(2,128)(2,1)S(1)}, bf16[2,2048]{1,0:T(2,128)(2,1)S(1)}) custom-call(bf16[8,3584]{1,0:T(8,128)(2,1)S(1)} %pair_sum.2.after_ref.near_ref, bf16[8,3584]{1,0:T(8,128)(2,1)S(1)} %collective-permute-done.19.far_ref, bf16[3584,2048]{1,0:T(8,128)(2,1)S(1)} %bitcast.5, ...), custom_call_target="tpu_custom_call" | custom-call | tf_op jit(solution)/shard_map/second_down/pallas_call | solution.py:606
  53.8 1.7 %collective-permute-start.22 = (bf16[2,2048]{1,0:T(2,128)(2,1)S(1)}, bf16[2,2048]{1,0:T(2,128)(2,1)S(1)}, u32[]{:S(2)}, u32[]{:S(2)}) collective-permute-start(bf16[2,2048]{1,0:T(2,128)(2,1)S(1)} %get-tuple-element.93), channel_id=1, source_target_pairs={{0,12},{1,13},{2,14},{3,15},{4,8},{5,9},{6,10},{7,11},{8,4},{9,5},... | collective-permute-start | bytes 24584 | tf_op jit(solution)/shard_map/ppermute | solution.py:50
  55.5 0.6 %collective-permute-start.23 = (bf16[2,2048]{1,0:T(2,128)(2,1)S(1)}, bf16[2,2048]{1,0:T(2,128)(2,1)S(1)}, u32[]{:S(2)}, u32[]{:S(2)}) collective-permute-start(bf16[2,2048]{1,0:T(2,128)(2,1)S(1)} %get-tuple-element.94), channel_id=1, source_target_pairs={{0,8},{1,9},{2,10},{3,11},{4,12},{5,13},{6,14},{7,15},{8,0},{9,1},... | collective-permute-start | bytes 24584 | tf_op jit(solution)/shard_map/ppermute | solution.py:50
  56.1 2.1 %collective-permute-start.24 = (bf16[2,2048]{1,0:T(2,128)(2,1)S(1)}, bf16[2,2048]{1,0:T(2,128)(2,1)S(1)}, u32[]{:S(2)}, u32[]{:S(2)}) collective-permute-start(bf16[2,2048]{1,0:T(2,128)(2,1)S(1)} %get-tuple-element.95), channel_id=1, source_target_pairs={{0,4},{1,5},{2,6},{3,7},{4,0},{5,1},{6,2},{7,3},{8,12},{9,13},{10,... | collective-permute-start | bytes 24584 | tf_op jit(solution)/shard_map/ppermute | solution.py:50
  58.2 1.1 %collective-permute-done.22.refs_0_ = bf16[2,2048]{1,0:T(2,128)(2,1)S(1)} collective-permute-done((bf16[2,2048]{1,0:T(2,128)(2,1)S(1)}, bf16[2,2048]{1,0:T(2,128)(2,1)S(1)}, u32[]{:S(2)}, u32[]{:S(2)}) %collective-permute-start.22) | collective-permute-done | bytes 8224 | tf_op jit(solution)/shard_map/ppermute | solution.py:50
  59.3 0.7 %collective-permute-done.23.refs_1_ = bf16[2,2048]{1,0:T(2,128)(2,1)S(1)} collective-permute-done((bf16[2,2048]{1,0:T(2,128)(2,1)S(1)}, bf16[2,2048]{1,0:T(2,128)(2,1)S(1)}, u32[]{:S(2)}, u32[]{:S(2)}) %collective-permute-start.23) | collective-permute-done | bytes 8224 | tf_op jit(solution)/shard_map/ppermute | solution.py:50
  60.0 0.6 %finish.1 = bf16[2,2048]{1,0:T(2,128)(2,1)} custom-call(f32[2,2048]{1,0:T(2,128)S(1)} %get-tuple-element.88.updated_ref, bf16[2,2048]{1,0:T(2,128)(2,1)S(1)} %collective-permute-done.22.refs_0_, bf16[2,2048]{1,0:T(2,128)(2,1)S(1)} %collective-permute-done.23.refs_1_, bf16[2,2048]{1,0:T(2,128)(2,1)S(1)} %collective-permute-done.24.refs_2_, ...), custom_call_target="tpu_custom_call" | custom-call | tf_op jit(solution)/shard_map/finish/pallas_call | solution.py:639
  (27 shorter events, 0.1 us)
Async XLA Ops:
  0.0 8.4 %collective-permute-start = (bf16[2,2048]{1,0:T(2,128)(2,1)}, bf16[2,2048]{1,0:T(2,128)(2,1)S(1)}, u32[]{:S(2)}, u32[]{:S(2)}) collective-permute-start(bf16[2,2048]{1,0:T(2,128)(2,1)} %refs_5_.1), channel_id=1, source_target_pairs={{0,8},{4,12},{8,0},{12,4},{1,9},{5,13},{9,1},{13,5},{2,10},{6,14},... | collective-permute-start | bytes 24584 | tf_op jit(solution)/shard_map/ppermute | solution.py:31
  4.0 5.7 %collective-permute-start.1 = (bf16[2,2048]{1,0:T(2,128)(2,1)}, bf16[2,2048]{1,0:T(2,128)(2,1)S(1)}, u32[]{:S(2)}, u32[]{:S(2)}) collective-permute-start(bf16[2,2048]{1,0:T(2,128)(2,1)} %refs_5_.1), channel_id=1, source_target_pairs={{0,12},{4,8},{8,4},{12,0},{1,13},{5,9},{9,5},{13,1},{2,14},{6,10},... | collective-permute-start | bytes 24584 | tf_op jit(solution)/shard_map/ppermute | solution.py:31
  5.4 4.3 %collective-permute-start.2 = (bf16[2,2048]{1,0:T(2,128)(2,1)}, bf16[2,2048]{1,0:T(2,128)(2,1)S(1)}, u32[]{:S(2)}, u32[]{:S(2)}) collective-permute-start(bf16[2,2048]{1,0:T(2,128)(2,1)} %refs_5_.1), channel_id=1, source_target_pairs={{0,4},{4,0},{8,12},{12,8},{1,5},{5,1},{9,13},{13,9},{2,6},{6,2},{1... | collective-permute-start | bytes 24584 | tf_op jit(solution)/shard_map/ppermute | solution.py:31
  5.6 7.5 %copy-start.3 = (s32[8]{0:T(128)S(1)}, s32[8]{0:T(128)}, u32[]{:S(2)}) copy-start(s32[8]{0:T(128)} %param.23) | copy-start | bytes 100
  10.5 4.4 %collective-permute-start.3 = (bf16[2,1408]{1,0:T(2,128)(2,1)S(1)}, bf16[2,1408]{1,0:T(2,128)(2,1)S(1)}, u32[]{:S(2)}, u32[]{:S(2)}) collective-permute-start(bf16[2,1408]{1,0:T(2,128)(2,1)S(1)} %get-tuple-element.59), channel_id=1, source_target_pairs={{0,9},{1,8},{2,11},{3,10},{4,13},{5,12},{6,15},{7,14},{8,1},{9,0},... | collective-permute-start | bytes 16904 | tf_op jit(solution)/shard_map/ppermute | solution.py:50
  10.7 4.8 %collective-permute-start.4 = (bf16[2,1408]{1,0:T(2,128)(2,1)S(1)}, bf16[2,1408]{1,0:T(2,128)(2,1)S(1)}, u32[]{:S(2)}, u32[]{:S(2)}) collective-permute-start(bf16[2,1408]{1,0:T(2,128)(2,1)S(1)} %get-tuple-element.60), channel_id=1, source_target_pairs={{0,13},{1,12},{2,15},{3,14},{4,9},{5,8},{6,11},{7,10},{8,5},{9,4},... | collective-permute-start | bytes 16904 | tf_op jit(solution)/shard_map/ppermute | solution.py:50
  13.2 3.0 %collective-permute-start.5 = (bf16[2,1408]{1,0:T(2,128)(2,1)S(1)}, bf16[2,1408]{1,0:T(2,128)(2,1)S(1)}, u32[]{:S(2)}, u32[]{:S(2)}) collective-permute-start(bf16[2,1408]{1,0:T(2,128)(2,1)S(1)} %get-tuple-element.61), channel_id=1, source_target_pairs={{0,5},{1,4},{2,7},{3,6},{4,1},{5,0},{6,3},{7,2},{8,13},{9,12},{10,... | collective-permute-start | bytes 16904 | tf_op jit(solution)/shard_map/ppermute | solution.py:50
  16.2 4.5 %collective-permute-start.6 = (bf16[8,1408]{1,0:T(8,128)(2,1)S(1)}, bf16[8,1408]{1,0:T(8,128)(2,1)S(1)}, u32[]{:S(2)}, u32[]{:S(2)}) collective-permute-start(bf16[8,1408]{1,0:T(8,128)(2,1)S(1)} %stack.1.refs_1_.refs_0_), channel_id=1, source_target_pairs={{0,3},{1,2},{2,1},{3,0},{4,7},{5,6},{6,5},{7,4},{8,11},{9,10},{10,... | collective-permute-start | bytes 67592 | tf_op jit(solution)/shard_map/ppermute | solution.py:31
  18.3 3.8 %collective-permute-start.7 = (bf16[8,1408]{1,0:T(8,128)(2,1)S(1)}, bf16[8,1408]{1,0:T(8,128)(2,1)S(1)}, u32[]{:S(2)}, u32[]{:S(2)}) collective-permute-start(bf16[8,1408]{1,0:T(8,128)(2,1)S(1)} %stack.1.refs_1_.refs_0_), channel_id=1, source_target_pairs={{0,2},{1,3},{2,0},{3,1},{4,6},{5,7},{6,4},{7,5},{8,10},{9,11},{10,... | collective-permute-start | bytes 67592 | tf_op jit(solution)/shard_map/ppermute | solution.py:31
  18.8 3.3 %collective-permute-start.8 = (bf16[8,1408]{1,0:T(8,128)(2,1)S(1)}, bf16[8,1408]{1,0:T(8,128)(2,1)S(1)}, u32[]{:S(2)}, u32[]{:S(2)}) collective-permute-start(bf16[8,1408]{1,0:T(8,128)(2,1)S(1)} %stack.1.refs_1_.refs_0_), channel_id=1, source_target_pairs={{0,1},{1,0},{2,3},{3,2},{4,5},{5,4},{6,7},{7,6},{8,9},{9,8},{10,11... | collective-permute-start | bytes 67592 | tf_op jit(solution)/shard_map/ppermute | solution.py:31
  18.9 8.8 %copy-start = (bf16[2048,3584]{1,0:T(8,128)(2,1)S(1)}, bf16[2048,3584]{1,0:T(8,128)(2,1)}, u32[]{:S(2)}) copy-start(bf16[2048,3584]{1,0:T(8,128)(2,1)} %gate_ref.3) | copy-start | bytes 44040196
  23.6 4.0 %collective-permute-start.10 = (bf16[80,128]{1,0:T(8,128)(2,1)S(1)}, bf16[80,128]{1,0:T(8,128)(2,1)S(1)}, u32[]{:S(2)}, u32[]{:S(2)}) collective-permute-start(bf16[80,128]{1,0:T(8,128)(2,1)S(1)} %attend.1.refs_1_.refs_3_), channel_id=1, source_target_pairs={{0,2},{1,3},{2,0},{3,1},{4,6},{5,7},{6,4},{7,5},{8,10},{9,11},{10,... | collective-permute-start | bytes 61448 | tf_op jit(solution)/shard_map/ppermute | solution.py:31
  24.2 3.4 %collective-permute-start.11 = (bf16[80,128]{1,0:T(8,128)(2,1)S(1)}, bf16[80,128]{1,0:T(8,128)(2,1)S(1)}, u32[]{:S(2)}, u32[]{:S(2)}) collective-permute-start(bf16[80,128]{1,0:T(8,128)(2,1)S(1)} %attend.1.refs_1_.refs_3_), channel_id=1, source_target_pairs={{0,3},{1,2},{2,1},{3,0},{4,7},{5,6},{6,5},{7,4},{8,11},{9,10},{10,... | collective-permute-start | bytes 61448 | tf_op jit(solution)/shard_map/ppermute | solution.py:31
  24.3 3.4 %collective-permute-start.9 = (bf16[80,128]{1,0:T(8,128)(2,1)S(1)}, bf16[80,128]{1,0:T(8,128)(2,1)S(1)}, u32[]{:S(2)}, u32[]{:S(2)}) collective-permute-start(bf16[80,128]{1,0:T(8,128)(2,1)S(1)} %attend.1.refs_1_.refs_3_), channel_id=1, source_target_pairs={{0,1},{1,0},{2,3},{3,2},{4,5},{5,4},{6,7},{7,6},{8,9},{9,8},{10,11... | collective-permute-start | bytes 61448 | tf_op jit(solution)/shard_map/ppermute | solution.py:31
  27.7 5.8 %copy-start.1 = (bf16[2048,3584]{1,0:T(8,128)(2,1)S(1)}, bf16[2048,3584]{1,0:T(8,128)(2,1)}, u32[]{:S(2)}) copy-start(bf16[2048,3584]{1,0:T(8,128)(2,1)} %up_ref.3) | copy-start | bytes 44040196
  27.9 5.5 %collective-permute-start.12 = (bf16[2,1024]{1,0:T(2,128)(2,1)S(1)}, bf16[2,1024]{1,0:T(2,128)(2,1)S(1)}, u32[]{:S(2)}, u32[]{:S(2)}) collective-permute-start(bf16[2,1024]{1,0:T(2,128)(2,1)S(1)} %get-tuple-element.75), channel_id=1, source_target_pairs={{0,13},{1,12},{2,15},{3,14},{4,9},{5,8},{6,11},{7,10},{8,5},{9,4},... | collective-permute-start | bytes 12296 | tf_op jit(solution)/shard_map/ppermute | solution.py:50
  29.3 4.1 %collective-permute-start.13 = (bf16[2,1024]{1,0:T(2,128)(2,1)S(1)}, bf16[2,1024]{1,0:T(2,128)(2,1)S(1)}, u32[]{:S(2)}, u32[]{:S(2)}) collective-permute-start(bf16[2,1024]{1,0:T(2,128)(2,1)S(1)} %get-tuple-element.76), channel_id=1, source_target_pairs={{0,9},{1,8},{2,11},{3,10},{4,13},{5,12},{6,15},{7,14},{8,1},{9,0},... | collective-permute-start | bytes 12296 | tf_op jit(solution)/shard_map/ppermute | solution.py:50
  29.3 4.2 %collective-permute-start.14 = (bf16[2,1024]{1,0:T(2,128)(2,1)S(1)}, bf16[2,1024]{1,0:T(2,128)(2,1)S(1)}, u32[]{:S(2)}, u32[]{:S(2)}) collective-permute-start(bf16[2,1024]{1,0:T(2,128)(2,1)S(1)} %get-tuple-element.77), channel_id=1, source_target_pairs={{0,5},{1,4},{2,7},{3,6},{4,1},{5,0},{6,3},{7,2},{8,13},{9,12},{10,... | collective-permute-start | bytes 12296 | tf_op jit(solution)/shard_map/ppermute | solution.py:50
  33.5 8.5 %copy-start.2 = (bf16[2048,3584]{1,0:T(8,128)(2,1)S(1)}, bf16[2048,3584]{1,0:T(8,128)(2,1)}, u32[]{:S(2)}) copy-start(bf16[2048,3584]{1,0:T(8,128)(2,1)} %up_ref.3) | copy-start | bytes 44040196
  34.4 6.0 %collective-permute-start.15 = (bf16[8,2048]{1,0:T(8,128)(2,1)S(1)}, bf16[8,2048]{1,0:T(8,128)(2,1)S(1)}, u32[]{:S(2)}, u32[]{:S(2)}) collective-permute-start(bf16[8,2048]{1,0:T(8,128)(2,1)S(1)} %get-tuple-element.84), channel_id=1, source_target_pairs={{0,12},{1,13},{2,14},{3,15},{4,8},{5,9},{6,10},{7,11},{8,4},{9,5},... | collective-permute-start | bytes 98312 | tf_op jit(solution)/shard_map/ppermute | solution.py:50
  36.4 5.2 %collective-permute-start.16 = (bf16[8,2048]{1,0:T(8,128)(2,1)S(1)}, bf16[8,2048]{1,0:T(8,128)(2,1)S(1)}, u32[]{:S(2)}, u32[]{:S(2)}) collective-permute-start(bf16[8,2048]{1,0:T(8,128)(2,1)S(1)} %get-tuple-element.85), channel_id=1, source_target_pairs={{0,8},{1,9},{2,10},{3,11},{4,12},{5,13},{6,14},{7,15},{8,0},{9,1},... | collective-permute-start | bytes 98312 | tf_op jit(solution)/shard_map/ppermute | solution.py:50
  37.6 4.3 %collective-permute-start.17 = (bf16[8,2048]{1,0:T(8,128)(2,1)S(1)}, bf16[8,2048]{1,0:T(8,128)(2,1)S(1)}, u32[]{:S(2)}, u32[]{:S(2)}) collective-permute-start(bf16[8,2048]{1,0:T(8,128)(2,1)S(1)} %get-tuple-element.86), channel_id=1, source_target_pairs={{0,4},{1,5},{2,6},{3,7},{4,0},{5,1},{6,2},{7,3},{8,12},{9,13},{10,... | collective-permute-start | bytes 98312 | tf_op jit(solution)/shard_map/ppermute | solution.py:50
  43.9 2.6 %collective-permute-start.20 = (bf16[8,3712]{1,0:T(8,128)(2,1)S(1)}, bf16[8,3712]{1,0:T(8,128)(2,1)S(1)}, u32[]{:S(2)}, u32[]{:S(2)}) collective-permute-start(bf16[8,3712]{1,0:T(8,128)(2,1)S(1)} %get-tuple-element.90.first_ref), channel_id=1, source_target_pairs={{0,1},{1,0},{2,3},{3,2},{4,5},{5,4},{6,7},{7,6},{8,9},{9,8},{10,11... | collective-permute-start | bytes 178184 | tf_op jit(solution)/shard_map/ppermute | solution.py:31
  44.0 4.8 %slice-start = ((s8[14680064]{0:T(1024)(128)(4,1)}), s8[4194304]{0:T(1024)(128)(4,1)S(1)}, s32[]{:S(2)}) async-start(s8[14680064]{0:T(1024)(128)(4,1)} %bitcast.4), calls=%async_computation | async-start | bytes 8388608
  44.0 4.8 %slice-start.1 = ((s8[14680064]{0:T(1024)(128)(4,1)}), s8[4194304]{0:T(1024)(128)(4,1)S(1)}, s32[]{:S(2)}) async-start(s8[14680064]{0:T(1024)(128)(4,1)} %bitcast.4), calls=%async_computation.1 | async-start | bytes 8388608
  44.0 4.7 %slice-start.2 = ((s8[14680064]{0:T(1024)(128)(4,1)}), s8[4194304]{0:T(1024)(128)(4,1)S(1)}, s32[]{:S(2)}) async-start(s8[14680064]{0:T(1024)(128)(4,1)} %bitcast.4), calls=%async_computation.2 | async-start | bytes 8388608
  44.0 5.2 %slice-start.3 = ((s8[14680064]{0:T(1024)(128)(4,1)}), s8[2097152]{0:T(1024)(128)(4,1)S(1)}, s32[]{:S(2)}) async-start(s8[14680064]{0:T(1024)(128)(4,1)} %bitcast.4), calls=%async_computation.3 | async-start | bytes 4194304
  46.0 1.8 %collective-permute-start.18 = (bf16[8,3584]{1,0:T(8,128)(2,1)S(1)}, bf16[8,3584]{1,0:T(8,128)(2,1)S(1)}, u32[]{:S(2)}, u32[]{:S(2)}) collective-permute-start(bf16[8,3584]{1,0:T(8,128)(2,1)S(1)} %second_gate_up.1.first_ref), channel_id=1, source_target_pairs={{0,1},{1,0},{2,3},{3,2},{4,5},{5,4},{6,7},{7,6},{8,9},{9,8},{10,11... | collective-permute-start | bytes 172040 | tf_op jit(solution)/shard_map/ppermute | solution.py:31
  46.5 4.6 %collective-permute-start.21 = (bf16[8,3712]{1,0:T(8,128)(2,1)S(1)}, bf16[8,3712]{1,0:T(8,128)(2,1)S(1)}, u32[]{:S(2)}, u32[]{:S(2)}) collective-permute-start(bf16[8,3712]{1,0:T(8,128)(2,1)S(1)} %pair_sum.3.near_ref), channel_id=1, source_target_pairs={{0,2},{1,3},{2,0},{3,1},{4,6},{5,7},{6,4},{7,5},{8,10},{9,11},{10,... | collective-permute-start | bytes 178184 | tf_op jit(solution)/shard_map/ppermute | solution.py:31
  47.9 4.6 %collective-permute-start.19 = (bf16[8,3584]{1,0:T(8,128)(2,1)S(1)}, bf16[8,3584]{1,0:T(8,128)(2,1)S(1)}, u32[]{:S(2)}, u32[]{:S(2)}) collective-permute-start(bf16[8,3584]{1,0:T(8,128)(2,1)S(1)} %pair_sum.2.after_ref.near_ref), channel_id=1, source_target_pairs={{0,2},{1,3},{2,0},{3,1},{4,6},{5,7},{6,4},{7,5},{8,10},{9,11},{10,... | collective-permute-start | bytes 172040 | tf_op jit(solution)/shard_map/ppermute | solution.py:31
  53.8 5.5 %collective-permute-start.22 = (bf16[2,2048]{1,0:T(2,128)(2,1)S(1)}, bf16[2,2048]{1,0:T(2,128)(2,1)S(1)}, u32[]{:S(2)}, u32[]{:S(2)}) collective-permute-start(bf16[2,2048]{1,0:T(2,128)(2,1)S(1)} %get-tuple-element.93), channel_id=1, source_target_pairs={{0,12},{1,13},{2,14},{3,15},{4,8},{5,9},{6,10},{7,11},{8,4},{9,5},... | collective-permute-start | bytes 24584 | tf_op jit(solution)/shard_map/ppermute | solution.py:50
  55.5 4.5 %collective-permute-start.23 = (bf16[2,2048]{1,0:T(2,128)(2,1)S(1)}, bf16[2,2048]{1,0:T(2,128)(2,1)S(1)}, u32[]{:S(2)}, u32[]{:S(2)}) collective-permute-start(bf16[2,2048]{1,0:T(2,128)(2,1)S(1)} %get-tuple-element.94), channel_id=1, source_target_pairs={{0,8},{1,9},{2,10},{3,11},{4,12},{5,13},{6,14},{7,15},{8,0},{9,1},... | collective-permute-start | bytes 24584 | tf_op jit(solution)/shard_map/ppermute | solution.py:50
  56.1 3.9 %collective-permute-start.24 = (bf16[2,2048]{1,0:T(2,128)(2,1)S(1)}, bf16[2,2048]{1,0:T(2,128)(2,1)S(1)}, u32[]{:S(2)}, u32[]{:S(2)}) collective-permute-start(bf16[2,2048]{1,0:T(2,128)(2,1)S(1)} %get-tuple-element.95), channel_id=1, source_target_pairs={{0,4},{1,5},{2,6},{3,7},{4,0},{5,1},{6,2},{7,3},{8,12},{9,13},{10,... | collective-permute-start | bytes 24584 | tf_op jit(solution)/shard_map/ppermute | solution.py:50

commit v21 on v19

--- a/solution.py
+++ b/solution.py
@@ -643,7 +643,7 @@
         out_specs=in_vmem,
         compiler_params=params(1),
         name="finish",
-    )(updated, *in_start_order(parts))
+    )(updated, *parts[::-1])
 
 
 def rotation_tables(positions, repeats):

time: 61.1 us -> 60.4 us (0.989)
  waiting for transfers between devices: 12.2 us -> 10.6 us
  starting transfers between devices: 27.8 us -> 28.6 us
    ppermute x12, waiting for transfers between devices: 7.28 us -> 5.71 us  [scatter_slots(): got.append(lax.ppermute(pieces[k], ('tensor', 'inner'), pairs))]
    ppermute x12, starting transfers between devices: 14.3 us -> 15.2 us  [scatter_slots(): got.append(lax.ppermute(pieces[k], ('tensor', 'inner'), pairs))]
  transfers between devices with their start and end apart: 25 -> 25, of which waited for: 11 -> 10; matrix products, arithmetic and copies ran while one was open for 0% -> 0% of each run, Pallas kernels for 21% -> 21%
where the time goes in v21:
time: 60.4 us; the launch traced here: 60.3 us
  starting transfers between devices  28.6 us (47%)
  Pallas kernels  20 us (33%)
  waiting for transfers between devices  10.6 us (18%)
  local copies, waits for them, and re-layouts  0.63 us (1%)
    ppermute x12, starting transfers between devices, scatter_slots(): got.append(lax.ppermute(pieces[k], ('tensor', 'inner'), pairs))  15.2 us
    ppermute x13, starting transfers between devices, swap_with(): return lax.ppermute(value, axis, [(i, i ^ step) for i in range(count)])  13.4 us
    pallas_call x5, Pallas kernels, load(): pl.pallas_call(functools.partial(load_kernel, spans), out_shape=tuple((pl...  9.26 us
    ppermute x12, waiting for transfers between devices, scatter_slots(): got.append(lax.ppermute(pieces[k], ('tensor', 'inner'), pairs))  5.71 us
    ppermute x13, waiting for transfers between devices, swap_with(): return lax.ppermute(value, axis, [(i, i ^ step) for i in range(count)])  4.88 us
    pallas_call x1, Pallas kernels, first_gate_up(): pl.pallas_call(functools.partial(first_gate_up_kernel, slots, count), out...  2 us
    pallas_call x1, Pallas kernels, second_gate_up(): pl.pallas_call(functools.partial(second_gate_up_kernel, first, count), ou...  2 us
    pallas_call x1, Pallas kernels, attend(): pl.pallas_call(functools.partial(attend_kernel, slots, len(parts)), out_s...  1.49 us
  transfers between devices with their start and end apart: 25, of which 10 were waited for; matrix products, arithmetic and copies ran while one was open for 0% of the time, Pallas kernels for 21%

profile of v21, /device:TPU:0, one launch (start us, length us, event | category | flops | bytes accessed | tf_op | source)
XLA Modules:
  0.0 60.3 jit_solution(11915086366234578076)
XLA Ops:
  0.0 4.0 %collective-permute-start = (bf16[2,2048]{1,0:T(2,128)(2,1)}, bf16[2,2048]{1,0:T(2,128)(2,1)S(1)}, u32[]{:S(2)}, u32[]{:S(2)}) collective-permute-start(bf16[2,2048]{1,0:T(2,128)(2,1)} %refs_5_.1), channel_id=1, source_target_pairs={{0,8},{4,12},{8,0},{12,4},{1,9},{5,13},{9,1},{13,5},{2,10},{6,14},... | collective-permute-start | bytes 24584 | tf_op jit(solution)/shard_map/ppermute | solution.py:31
  4.0 1.3 %collective-permute-start.1 = (bf16[2,2048]{1,0:T(2,128)(2,1)}, bf16[2,2048]{1,0:T(2,128)(2,1)S(1)}, u32[]{:S(2)}, u32[]{:S(2)}) collective-permute-start(bf16[2,2048]{1,0:T(2,128)(2,1)} %refs_5_.1), channel_id=1, source_target_pairs={{0,12},{4,8},{8,4},{12,0},{1,13},{5,9},{9,5},{13,1},{2,14},{6,10},... | collective-permute-start | bytes 24584 | tf_op jit(solution)/shard_map/ppermute | solution.py:31
  5.4 0.2 collective-permute-start.2
  5.6 2.7 %load.5 = (bf16[2,2048]{1,0:T(2,128)(2,1)S(1)}, bf16[2048]{0:T(1024)(128)(2,1)S(1)}, bf16[2048]{0:T(1024)(128)(2,1)S(1)}, bf16[2048,256]{1,0:T(8,128)(2,1)S(1)}, bf16[2048,1024]{1,0:T(8,128)(2,1)S(1)}) custom-call(bf16[2,2048]{1,0:T(2,128)(2,1)} %refs_5_.1, bf16[2048]{0:T(1024)(128)(2,1)} %refs_1_.1, bf16[2048]{0:T(1024)(128)(2,1)} %refs_2_.1, ...), custom_call_target="tpu_custom_call" | custom-call | bytes 5259264 | tf_op jit(solution)/shard_map/load/pallas_call | solution.py:159
  8.4 0.0 collective-permute-done.refs_0_
  8.4 1.3 %collective-permute-done.1.refs_1_ = bf16[2,2048]{1,0:T(2,128)(2,1)S(1)} collective-permute-done((bf16[2,2048]{1,0:T(2,128)(2,1)}, bf16[2,2048]{1,0:T(2,128)(2,1)S(1)}, u32[]{:S(2)}, u32[]{:S(2)}) %collective-permute-start.1) | collective-permute-done | bytes 8224 | tf_op jit(solution)/shard_map/ppermute | solution.py:31
  9.7 0.0 collective-permute-done.2.refs_2_
  9.7 0.8 %project_qkv.1 = (f32[8,2048]{1,0:T(8,128)S(1)}, bf16[2,1408]{1,0:T(2,128)(2,1)S(1)}, bf16[2,1408]{1,0:T(2,128)(2,1)S(1)}, bf16[2,1408]{1,0:T(2,128)(2,1)S(1)}, bf16[2,1408]{1,0:T(2,128)(2,1)S(1)}) custom-call(bf16[2048]{0:T(1024)(128)(2,1)S(1)} %get-tuple-element.51.gain_ref, bf16[2048,1024]{1,0:T(8,128)(2,1)S(1)} %get-tuple-element.52.wq_ref, ...), custom_call_target="tpu_custom_call" | custom-call | tf_op jit(solution)/shard_map/project_qkv/pallas_call | solution.py:212
  10.5 0.3 collective-permute-start.3
  10.8 1.5 %collective-permute-start.4 = (bf16[2,1408]{1,0:T(2,128)(2,1)S(1)}, bf16[2,1408]{1,0:T(2,128)(2,1)S(1)}, u32[]{:S(2)}, u32[]{:S(2)}) collective-permute-start(bf16[2,1408]{1,0:T(2,128)(2,1)S(1)} %get-tuple-element.60), channel_id=1, source_target_pairs={{0,9},{1,8},{2,11},{3,10},{4,13},{5,12},{6,15},{7,14},{8,1},{9,0},... | collective-permute-start | bytes 16904 | tf_op jit(solution)/shard_map/ppermute | solution.py:50
  12.3 0.7 %collective-permute-start.5 = (bf16[2,1408]{1,0:T(2,128)(2,1)S(1)}, bf16[2,1408]{1,0:T(2,128)(2,1)S(1)}, u32[]{:S(2)}, u32[]{:S(2)}) collective-permute-start(bf16[2,1408]{1,0:T(2,128)(2,1)S(1)} %get-tuple-element.61), channel_id=1, source_target_pairs={{0,5},{1,4},{2,7},{3,6},{4,1},{5,0},{6,3},{7,2},{8,13},{9,12},{10,... | collective-permute-start | bytes 16904 | tf_op jit(solution)/shard_map/ppermute | solution.py:50
  13.0 0.1 fusion.4
  13.1 1.6 %load.6.key_ref = bf16[2,4096,128]{2,1,0:T(8,128)(2,1)S(1)} custom-call(bf16[2,4096,128]{2,1,0:T(8,128)(2,1)} %bitcast.8, f32[8,2048]{1,0:T(8,128)S(1)} %get-tuple-element.56.refs_1_.rows_ref), custom_call_target="tpu_custom_call" | custom-call | bytes 2097152 | tf_op jit(solution)/shard_map/load/pallas_call | solution.py:159
  14.7 0.7 %collective-permute-done.3.refs_0_ = bf16[2,1408]{1,0:T(2,128)(2,1)S(1)} collective-permute-done((bf16[2,1408]{1,0:T(2,128)(2,1)S(1)}, bf16[2,1408]{1,0:T(2,128)(2,1)S(1)}, u32[]{:S(2)}, u32[]{:S(2)}) %collective-permute-start.3) | collective-permute-done | bytes 5664 | tf_op jit(solution)/shard_map/ppermute | solution.py:50
  15.4 0.0 collective-permute-done.4.refs_1_
  15.4 0.0 collective-permute-done.5.refs_2_
  15.5 2.4 %collective-permute-start.6 = (bf16[8,1408]{1,0:T(8,128)(2,1)S(1)}, bf16[8,1408]{1,0:T(8,128)(2,1)S(1)}, u32[]{:S(2)}, u32[]{:S(2)}) collective-permute-start(bf16[8,1408]{1,0:T(8,128)(2,1)S(1)} %stack.1.refs_1_.refs_0_), channel_id=1, source_target_pairs={{0,3},{1,2},{2,1},{3,0},{4,7},{5,6},{6,5},{7,4},{8,11},{9,10},{10,... | collective-permute-start | bytes 67592 | tf_op jit(solution)/shard_map/ppermute | solution.py:31
  17.9 0.5 collective-permute-start.7
  18.4 0.0 collective-permute-start.8
  18.4 0.1 fusion
  18.5 0.0 copy-start
  18.5 1.8 %load.7.value_ref = bf16[2,4096,128]{2,1,0:T(8,128)(2,1)S(1)} custom-call(bf16[2,4096,128]{2,1,0:T(8,128)(2,1)} %bitcast.9, bf16[8,1408]{1,0:T(8,128)(2,1)S(1)} %stack.1.refs_1_.refs_0_), custom_call_target="tpu_custom_call" | custom-call | bytes 2097152 | tf_op jit(solution)/shard_map/load/pallas_call | solution.py:159
  20.3 1.3 %collective-permute-done.7.refs_2_ = bf16[8,1408]{1,0:T(8,128)(2,1)S(1)} collective-permute-done((bf16[8,1408]{1,0:T(8,128)(2,1)S(1)}, bf16[8,1408]{1,0:T(8,128)(2,1)S(1)}, u32[]{:S(2)}, u32[]{:S(2)}) %collective-permute-start.7) | collective-permute-done | bytes 22560 | tf_op jit(solution)/shard_map/ppermute | solution.py:31
  21.7 0.1 broadcast_in_dim.10.lengths_ref
  21.8 1.5 %attend.1.refs_1_.refs_3_ = bf16[80,128]{1,0:T(8,128)(2,1)S(1)} custom-call(s32[2,128]{1,0:T(2,128)S(1)} %broadcast_in_dim.10.lengths_ref, f32[8,128]{1,0:T(8,128)S(1)} %bitcast.6, f32[8,128]{1,0:T(8,128)S(1)} %bitcast.7, bf16[2,4096,128]{2,1,0:T(8,128)(2,1)S(1)} %load.6.key_ref, bf16[2,4096,128]{2,1,0:T(8,128)(2,1)S(1)} %load.7.value_ref, ...), custom_call_target="tpu_custom_call" | custom-call | tf_op jit(solution)/shard_map/attend/pallas_call | solution.py:356
  23.2 0.6 collective-permute-start.10
  23.8 0.0 collective-permute-start.11
  23.9 1.6 %collective-permute-start.9 = (bf16[80,128]{1,0:T(8,128)(2,1)S(1)}, bf16[80,128]{1,0:T(8,128)(2,1)S(1)}, u32[]{:S(2)}, u32[]{:S(2)}) collective-permute-start(bf16[80,128]{1,0:T(8,128)(2,1)S(1)} %attend.1.refs_1_.refs_3_), channel_id=1, source_target_pairs={{0,1},{1,0},{2,3},{3,2},{4,5},{5,4},{6,7},{7,6},{8,9},{9,8},{10,11... | collective-permute-start | bytes 61448 | tf_op jit(solution)/shard_map/ppermute | solution.py:31
  25.5 1.5 %load.8.upper_ref = bf16[512,2048]{1,0:T(8,128)(2,1)S(1)} custom-call(bf16[1024,2048]{1,0:T(8,128)(2,1)} %refs_0_.5, bf16[80,128]{1,0:T(8,128)(2,1)S(1)} %attend.1.refs_1_.refs_3_), custom_call_target="tpu_custom_call" | custom-call | bytes 2097152 | tf_op jit(solution)/shard_map/load/pallas_call | solution.py:159
  27.0 0.3 collective-permute-done.10.refs_1_
  27.3 0.0 copy-start.1
  27.3 0.3 combine.1
  27.6 1.7 %collective-permute-start.12 = (bf16[2,1024]{1,0:T(2,128)(2,1)S(1)}, bf16[2,1024]{1,0:T(2,128)(2,1)S(1)}, u32[]{:S(2)}, u32[]{:S(2)}) collective-permute-start(bf16[2,1024]{1,0:T(2,128)(2,1)S(1)} %get-tuple-element.75), channel_id=1, source_target_pairs={{0,13},{1,12},{2,15},{3,14},{4,9},{5,8},{6,11},{7,10},{8,5},{9,4},... | collective-permute-start | bytes 12296 | tf_op jit(solution)/shard_map/ppermute | solution.py:50
  29.2 0.4 collective-permute-start.13
  29.6 1.8 %collective-permute-start.14 = (bf16[2,1024]{1,0:T(2,128)(2,1)S(1)}, bf16[2,1024]{1,0:T(2,128)(2,1)S(1)}, u32[]{:S(2)}, u32[]{:S(2)}) collective-permute-start(bf16[2,1024]{1,0:T(2,128)(2,1)S(1)} %get-tuple-element.77), channel_id=1, source_target_pairs={{0,5},{1,4},{2,7},{3,6},{4,1},{5,0},{6,3},{7,2},{8,13},{9,12},{10,... | collective-permute-start | bytes 12296 | tf_op jit(solution)/shard_map/ppermute | solution.py:50
  31.4 1.6 %load.9.lower_ref = bf16[512,2048]{1,0:T(8,128)(2,1)S(1)} custom-call(bf16[1024,2048]{1,0:T(8,128)(2,1)} %refs_0_.5, bf16[2,1024]{1,0:T(2,128)(2,1)S(1)} %get-tuple-element.83.refs_1_.refs_3_), custom_call_target="tpu_custom_call" | custom-call | bytes 2097152 | tf_op jit(solution)/shard_map/load/pallas_call | solution.py:159
  33.0 0.1 collective-permute-done.13.refs_1_
  33.2 0.0 collective-permute-done.14.refs_2_
  33.2 0.9 %project_out.1 = (bf16[8,2048]{1,0:T(8,128)(2,1)S(1)}, bf16[8,2048]{1,0:T(8,128)(2,1)S(1)}, bf16[8,2048]{1,0:T(8,128)(2,1)S(1)}, bf16[8,2048]{1,0:T(8,128)(2,1)S(1)}) custom-call(bf16[512,2048]{1,0:T(8,128)(2,1)S(1)} %load.8.upper_ref, bf16[512,2048]{1,0:T(8,128)(2,1)S(1)} %load.9.lower_ref, bf16[2,1024]{1,0:T(2,128)(2,1)S(1)} %collective-permute-done.12.refs_0_, ...), custom_call_target="tpu_custom_call" | custom-call | tf_op jit(solution)/shard_map/project_out/pallas_call | solution.py:453
  34.1 1.9 %collective-permute-start.15 = (bf16[8,2048]{1,0:T(8,128)(2,1)S(1)}, bf16[8,2048]{1,0:T(8,128)(2,1)S(1)}, u32[]{:S(2)}, u32[]{:S(2)}) collective-permute-start(bf16[8,2048]{1,0:T(8,128)(2,1)S(1)} %get-tuple-element.84), channel_id=1, source_target_pairs={{0,12},{1,13},{2,14},{3,15},{4,8},{5,9},{6,10},{7,11},{8,4},{9,5},... | collective-permute-start | bytes 98312 | tf_op jit(solution)/shard_map/ppermute | solution.py:50
  36.1 1.2 %collective-permute-start.16 = (bf16[8,2048]{1,0:T(8,128)(2,1)S(1)}, bf16[8,2048]{1,0:T(8,128)(2,1)S(1)}, u32[]{:S(2)}, u32[]{:S(2)}) collective-permute-start(bf16[8,2048]{1,0:T(8,128)(2,1)S(1)} %get-tuple-element.85), channel_id=1, source_target_pairs={{0,8},{1,9},{2,10},{3,11},{4,12},{5,13},{6,14},{7,15},{8,0},{9,1},... | collective-permute-start | bytes 98312 | tf_op jit(solution)/shard_map/ppermute | solution.py:50
  37.2 1.3 %collective-permute-start.17 = (bf16[8,2048]{1,0:T(8,128)(2,1)S(1)}, bf16[8,2048]{1,0:T(8,128)(2,1)S(1)}, u32[]{:S(2)}, u32[]{:S(2)}) collective-permute-start(bf16[8,2048]{1,0:T(8,128)(2,1)S(1)} %get-tuple-element.86), channel_id=1, source_target_pairs={{0,4},{1,5},{2,6},{3,7},{4,0},{5,1},{6,2},{7,3},{8,12},{9,13},{10,... | collective-permute-start | bytes 98312 | tf_op jit(solution)/shard_map/ppermute | solution.py:50
  38.5 1.7 %collective-permute-done.15.refs_0_ = bf16[8,2048]{1,0:T(8,128)(2,1)S(1)} collective-permute-done((bf16[8,2048]{1,0:T(8,128)(2,1)S(1)}, bf16[8,2048]{1,0:T(8,128)(2,1)S(1)}, u32[]{:S(2)}, u32[]{:S(2)}) %collective-permute-start.15) | collective-permute-done | bytes 32800 | tf_op jit(solution)/shard_map/ppermute | solution.py:50
  40.2 1.1 %collective-permute-done.16.refs_1_ = bf16[8,2048]{1,0:T(8,128)(2,1)S(1)} collective-permute-done((bf16[8,2048]{1,0:T(8,128)(2,1)S(1)}, bf16[8,2048]{1,0:T(8,128)(2,1)S(1)}, u32[]{:S(2)}, u32[]{:S(2)}) %collective-permute-start.16) | collective-permute-done | bytes 32800 | tf_op jit(solution)/shard_map/ppermute | solution.py:50
  41.3 0.0 collective-permute-done.17.refs_2_
  41.3 2.0 %first_gate_up.1 = (bf16[8,3712]{1,0:T(8,128)(2,1)S(1)}, f32[2,2048]{1,0:T(2,128)S(1)}, bf16[8,2048]{1,0:T(8,128)(2,1)S(1)}) custom-call(f32[8,2048]{1,0:T(8,128)S(1)} %get-tuple-element.56.refs_1_.rows_ref, bf16[2048]{0:T(1024)(128)(2,1)S(1)} %get-tuple-element.57.gain_ref, bf16[2048,3584]{1,0:T(8,128)(2,1)S(1)} %copy-done, ...), custom_call_target="tpu_custom_call" | custom-call | flops 117440512 | bytes 14680064 | tf_op jit(solution)/shard_map/first_gate_up/pallas_call | solution.py:509
  43.3 0.0 collective-permute-start.20
  43.3 0.0 slice-start.1
  43.3 0.0 slice-start.2
  43.3 2.0 %second_gate_up.1.first_ref = bf16[8,3584]{1,0:T(8,128)(2,1)S(1)} custom-call(bf16[8,2048]{1,0:T(8,128)(2,1)S(1)} %get-tuple-element.89.scaled_ref, bf16[2048,3584]{1,0:T(8,128)(2,1)S(1)} %copy-done, bf16[2048,3584]{1,0:T(8,128)(2,1)S(1)} %copy-done.2), custom_call_target="tpu_custom_call" | custom-call | flops 117440512 | bytes 14680064 | tf_op jit(solution)/shard_map/second_gate_up/pallas_call | solution.py:538
  45.3 0.5 collective-permute-start.18
  45.9 1.3 %collective-permute-start.21 = (bf16[8,3712]{1,0:T(8,128)(2,1)S(1)}, bf16[8,3712]{1,0:T(8,128)(2,1)S(1)}, u32[]{:S(2)}, u32[]{:S(2)}) collective-permute-start(bf16[8,3712]{1,0:T(8,128)(2,1)S(1)} %pair_sum.3.near_ref), channel_id=1, source_target_pairs={{0,2},{1,3},{2,0},{3,1},{4,6},{5,7},{6,4},{7,5},{8,10},{9,11},{10,... | collective-permute-start | bytes 178184 | tf_op jit(solution)/shard_map/ppermute | solution.py:31
  47.1 0.0 collective-permute-done.18.second_ref
  47.1 0.9 %collective-permute-start.19 = (bf16[8,3584]{1,0:T(8,128)(2,1)S(1)}, bf16[8,3584]{1,0:T(8,128)(2,1)S(1)}, u32[]{:S(2)}, u32[]{:S(2)}) collective-permute-start(bf16[8,3584]{1,0:T(8,128)(2,1)S(1)} %pair_sum.2.after_ref.near_ref), channel_id=1, source_target_pairs={{0,2},{1,3},{2,0},{3,1},{4,6},{5,7},{6,4},{7,5},{8,10},{9,11},{10,... | collective-permute-start | bytes 172040 | tf_op jit(solution)/shard_map/ppermute | solution.py:31
  48.0 0.5 slice-done.3
  48.6 1.9 %collective-permute-done.21.far_ref = bf16[8,3712]{1,0:T(8,128)(2,1)S(1)} collective-permute-done((bf16[8,3712]{1,0:T(8,128)(2,1)S(1)}, bf16[8,3712]{1,0:T(8,128)(2,1)S(1)}, u32[]{:S(2)}, u32[]{:S(2)}) %collective-permute-start.21) | collective-permute-done | bytes 59424 | tf_op jit(solution)/shard_map/ppermute | solution.py:31
  50.5 1.3 %first_down.1 = (f32[8,2048]{1,0:T(8,128)S(1)}, f32[8,128]{1,0:T(8,128)S(1)}) custom-call(bf16[8,3712]{1,0:T(8,128)(2,1)S(1)} %pair_sum.3.near_ref, bf16[8,3712]{1,0:T(8,128)(2,1)S(1)} %collective-permute-done.21.far_ref, bf16[3584,2048]{1,0:T(8,128)(2,1)S(1)} %bitcast.5, f32[8,128]{1,0:T(8,128)S(1)} %hold.1.token_ref), custom_call_target="tpu_custom_call" | custom-call | flops 58720256 | bytes 7340032 | tf_op jit(solution)/shard_map/first_down/pallas_call | solution.py:576
  51.8 1.3 %second_down.1 = (bf16[2,2048]{1,0:T(2,128)(2,1)S(1)}, bf16[2,2048]{1,0:T(2,128)(2,1)S(1)}, bf16[2,2048]{1,0:T(2,128)(2,1)S(1)}, bf16[2,2048]{1,0:T(2,128)(2,1)S(1)}) custom-call(bf16[8,3584]{1,0:T(8,128)(2,1)S(1)} %pair_sum.2.after_ref.near_ref, bf16[8,3584]{1,0:T(8,128)(2,1)S(1)} %collective-permute-done.19.far_ref, bf16[3584,2048]{1,0:T(8,128)(2,1)S(1)} %bitcast.5, ...), custom_call_target="tpu_custom_call" | custom-call | tf_op jit(solution)/shard_map/second_down/pallas_call | solution.py:606
  53.1 2.0 %collective-permute-start.22 = (bf16[2,2048]{1,0:T(2,128)(2,1)S(1)}, bf16[2,2048]{1,0:T(2,128)(2,1)S(1)}, u32[]{:S(2)}, u32[]{:S(2)}) collective-permute-start(bf16[2,2048]{1,0:T(2,128)(2,1)S(1)} %get-tuple-element.93), channel_id=1, source_target_pairs={{0,12},{1,13},{2,14},{3,15},{4,8},{5,9},{6,10},{7,11},{8,4},{9,5},... | collective-permute-start | bytes 24584 | tf_op jit(solution)/shard_map/ppermute | solution.py:50
  55.1 0.7 %collective-permute-start.23 = (bf16[2,2048]{1,0:T(2,128)(2,1)S(1)}, bf16[2,2048]{1,0:T(2,128)(2,1)S(1)}, u32[]{:S(2)}, u32[]{:S(2)}) collective-permute-start(bf16[2,2048]{1,0:T(2,128)(2,1)S(1)} %get-tuple-element.94), channel_id=1, source_target_pairs={{0,8},{1,9},{2,10},{3,11},{4,12},{5,13},{6,14},{7,15},{8,0},{9,1},... | collective-permute-start | bytes 24584 | tf_op jit(solution)/shard_map/ppermute | solution.py:50
  55.8 1.8 %collective-permute-start.24 = (bf16[2,2048]{1,0:T(2,128)(2,1)S(1)}, bf16[2,2048]{1,0:T(2,128)(2,1)S(1)}, u32[]{:S(2)}, u32[]{:S(2)}) collective-permute-start(bf16[2,2048]{1,0:T(2,128)(2,1)S(1)} %get-tuple-element.95), channel_id=1, source_target_pairs={{0,4},{1,5},{2,6},{3,7},{4,0},{5,1},{6,2},{7,3},{8,12},{9,13},{10,... | collective-permute-start | bytes 24584 | tf_op jit(solution)/shard_map/ppermute | solution.py:50
  57.6 1.1 %collective-permute-done.22.refs_0_ = bf16[2,2048]{1,0:T(2,128)(2,1)S(1)} collective-permute-done((bf16[2,2048]{1,0:T(2,128)(2,1)S(1)}, bf16[2,2048]{1,0:T(2,128)(2,1)S(1)}, u32[]{:S(2)}, u32[]{:S(2)}) %collective-permute-start.22) | collective-permute-done | bytes 8224 | tf_op jit(solution)/shard_map/ppermute | solution.py:50
  58.6 1.0 %collective-permute-done.23.refs_1_ = bf16[2,2048]{1,0:T(2,128)(2,1)S(1)} collective-permute-done((bf16[2,2048]{1,0:T(2,128)(2,1)S(1)}, bf16[2,2048]{1,0:T(2,128)(2,1)S(1)}, u32[]{:S(2)}, u32[]{:S(2)}) %collective-permute-start.23) | collective-permute-done | bytes 8224 | tf_op jit(solution)/shard_map/ppermute | solution.py:50
  59.6 0.6 %finish.1 = bf16[2,2048]{1,0:T(2,128)(2,1)} custom-call(f32[2,2048]{1,0:T(2,128)S(1)} %get-tuple-element.88.updated_ref, bf16[2,2048]{1,0:T(2,128)(2,1)S(1)} %collective-permute-done.22.refs_0_, bf16[2,2048]{1,0:T(2,128)(2,1)S(1)} %collective-permute-done.23.refs_1_, bf16[2,2048]{1,0:T(2,128)(2,1)S(1)} %collective-permute-done.24.refs_2_, ...), custom_call_target="tpu_custom_call" | custom-call | tf_op jit(solution)/shard_map/finish/pallas_call | solution.py:639
  (27 shorter events, 0.1 us)
Async XLA Ops:
  0.0 8.4 %collective-permute-start = (bf16[2,2048]{1,0:T(2,128)(2,1)}, bf16[2,2048]{1,0:T(2,128)(2,1)S(1)}, u32[]{:S(2)}, u32[]{:S(2)}) collective-permute-start(bf16[2,2048]{1,0:T(2,128)(2,1)} %refs_5_.1), channel_id=1, source_target_pairs={{0,8},{4,12},{8,0},{12,4},{1,9},{5,13},{9,1},{13,5},{2,10},{6,14},... | collective-permute-start | bytes 24584 | tf_op jit(solution)/shard_map/ppermute | solution.py:31
  4.0 5.7 %collective-permute-start.1 = (bf16[2,2048]{1,0:T(2,128)(2,1)}, bf16[2,2048]{1,0:T(2,128)(2,1)S(1)}, u32[]{:S(2)}, u32[]{:S(2)}) collective-permute-start(bf16[2,2048]{1,0:T(2,128)(2,1)} %refs_5_.1), channel_id=1, source_target_pairs={{0,12},{4,8},{8,4},{12,0},{1,13},{5,9},{9,5},{13,1},{2,14},{6,10},... | collective-permute-start | bytes 24584 | tf_op jit(solution)/shard_map/ppermute | solution.py:31
  5.4 4.3 %collective-permute-start.2 = (bf16[2,2048]{1,0:T(2,128)(2,1)}, bf16[2,2048]{1,0:T(2,128)(2,1)S(1)}, u32[]{:S(2)}, u32[]{:S(2)}) collective-permute-start(bf16[2,2048]{1,0:T(2,128)(2,1)} %refs_5_.1), channel_id=1, source_target_pairs={{0,4},{4,0},{8,12},{12,8},{1,5},{5,1},{9,13},{13,9},{2,6},{6,2},{1... | collective-permute-start | bytes 24584 | tf_op jit(solution)/shard_map/ppermute | solution.py:31
  5.6 7.4 %copy-start.3 = (s32[8]{0:T(128)S(1)}, s32[8]{0:T(128)}, u32[]{:S(2)}) copy-start(s32[8]{0:T(128)} %param.23) | copy-start | bytes 100
  10.5 4.9 %collective-permute-start.3 = (bf16[2,1408]{1,0:T(2,128)(2,1)S(1)}, bf16[2,1408]{1,0:T(2,128)(2,1)S(1)}, u32[]{:S(2)}, u32[]{:S(2)}) collective-permute-start(bf16[2,1408]{1,0:T(2,128)(2,1)S(1)} %get-tuple-element.59), channel_id=1, source_target_pairs={{0,13},{1,12},{2,15},{3,14},{4,9},{5,8},{6,11},{7,10},{8,5},{9,4},... | collective-permute-start | bytes 16904 | tf_op jit(solution)/shard_map/ppermute | solution.py:50
  10.8 4.6 %collective-permute-start.4 = (bf16[2,1408]{1,0:T(2,128)(2,1)S(1)}, bf16[2,1408]{1,0:T(2,128)(2,1)S(1)}, u32[]{:S(2)}, u32[]{:S(2)}) collective-permute-start(bf16[2,1408]{1,0:T(2,128)(2,1)S(1)} %get-tuple-element.60), channel_id=1, source_target_pairs={{0,9},{1,8},{2,11},{3,10},{4,13},{5,12},{6,15},{7,14},{8,1},{9,0},... | collective-permute-start | bytes 16904 | tf_op jit(solution)/shard_map/ppermute | solution.py:50
  12.3 3.2 %collective-permute-start.5 = (bf16[2,1408]{1,0:T(2,128)(2,1)S(1)}, bf16[2,1408]{1,0:T(2,128)(2,1)S(1)}, u32[]{:S(2)}, u32[]{:S(2)}) collective-permute-start(bf16[2,1408]{1,0:T(2,128)(2,1)S(1)} %get-tuple-element.61), channel_id=1, source_target_pairs={{0,5},{1,4},{2,7},{3,6},{4,1},{5,0},{6,3},{7,2},{8,13},{9,12},{10,... | collective-permute-start | bytes 16904 | tf_op jit(solution)/shard_map/ppermute | solution.py:50
  15.5 4.8 %collective-permute-start.6 = (bf16[8,1408]{1,0:T(8,128)(2,1)S(1)}, bf16[8,1408]{1,0:T(8,128)(2,1)S(1)}, u32[]{:S(2)}, u32[]{:S(2)}) collective-permute-start(bf16[8,1408]{1,0:T(8,128)(2,1)S(1)} %stack.1.refs_1_.refs_0_), channel_id=1, source_target_pairs={{0,3},{1,2},{2,1},{3,0},{4,7},{5,6},{6,5},{7,4},{8,11},{9,10},{10,... | collective-permute-start | bytes 67592 | tf_op jit(solution)/shard_map/ppermute | solution.py:31
  17.9 3.8 %collective-permute-start.7 = (bf16[8,1408]{1,0:T(8,128)(2,1)S(1)}, bf16[8,1408]{1,0:T(8,128)(2,1)S(1)}, u32[]{:S(2)}, u32[]{:S(2)}) collective-permute-start(bf16[8,1408]{1,0:T(8,128)(2,1)S(1)} %stack.1.refs_1_.refs_0_), channel_id=1, source_target_pairs={{0,2},{1,3},{2,0},{3,1},{4,6},{5,7},{6,4},{7,5},{8,10},{9,11},{10,... | collective-permute-start | bytes 67592 | tf_op jit(solution)/shard_map/ppermute | solution.py:31
  18.4 3.3 %collective-permute-start.8 = (bf16[8,1408]{1,0:T(8,128)(2,1)S(1)}, bf16[8,1408]{1,0:T(8,128)(2,1)S(1)}, u32[]{:S(2)}, u32[]{:S(2)}) collective-permute-start(bf16[8,1408]{1,0:T(8,128)(2,1)S(1)} %stack.1.refs_1_.refs_0_), channel_id=1, source_target_pairs={{0,1},{1,0},{2,3},{3,2},{4,5},{5,4},{6,7},{7,6},{8,9},{9,8},{10,11... | collective-permute-start | bytes 67592 | tf_op jit(solution)/shard_map/ppermute | solution.py:31
  18.5 8.8 %copy-start = (bf16[2048,3584]{1,0:T(8,128)(2,1)S(1)}, bf16[2048,3584]{1,0:T(8,128)(2,1)}, u32[]{:S(2)}) copy-start(bf16[2048,3584]{1,0:T(8,128)(2,1)} %gate_ref.3) | copy-start | bytes 44040196
  23.2 4.0 %collective-permute-start.10 = (bf16[80,128]{1,0:T(8,128)(2,1)S(1)}, bf16[80,128]{1,0:T(8,128)(2,1)S(1)}, u32[]{:S(2)}, u32[]{:S(2)}) collective-permute-start(bf16[80,128]{1,0:T(8,128)(2,1)S(1)} %attend.1.refs_1_.refs_3_), channel_id=1, source_target_pairs={{0,2},{1,3},{2,0},{3,1},{4,6},{5,7},{6,4},{7,5},{8,10},{9,11},{10,... | collective-permute-start | bytes 61448 | tf_op jit(solution)/shard_map/ppermute | solution.py:31
  23.8 3.4 %collective-permute-start.11 = (bf16[80,128]{1,0:T(8,128)(2,1)S(1)}, bf16[80,128]{1,0:T(8,128)(2,1)S(1)}, u32[]{:S(2)}, u32[]{:S(2)}) collective-permute-start(bf16[80,128]{1,0:T(8,128)(2,1)S(1)} %attend.1.refs_1_.refs_3_), channel_id=1, source_target_pairs={{0,3},{1,2},{2,1},{3,0},{4,7},{5,6},{6,5},{7,4},{8,11},{9,10},{10,... | collective-permute-start | bytes 61448 | tf_op jit(solution)/shard_map/ppermute | solution.py:31
  23.9 3.4 %collective-permute-start.9 = (bf16[80,128]{1,0:T(8,128)(2,1)S(1)}, bf16[80,128]{1,0:T(8,128)(2,1)S(1)}, u32[]{:S(2)}, u32[]{:S(2)}) collective-permute-start(bf16[80,128]{1,0:T(8,128)(2,1)S(1)} %attend.1.refs_1_.refs_3_), channel_id=1, source_target_pairs={{0,1},{1,0},{2,3},{3,2},{4,5},{5,4},{6,7},{7,6},{8,9},{9,8},{10,11... | collective-permute-start | bytes 61448 | tf_op jit(solution)/shard_map/ppermute | solution.py:31
  27.3 5.9 %copy-start.1 = (bf16[2048,3584]{1,0:T(8,128)(2,1)S(1)}, bf16[2048,3584]{1,0:T(8,128)(2,1)}, u32[]{:S(2)}) copy-start(bf16[2048,3584]{1,0:T(8,128)(2,1)} %up_ref.3) | copy-start | bytes 44040196
  27.6 5.5 %collective-permute-start.12 = (bf16[2,1024]{1,0:T(2,128)(2,1)S(1)}, bf16[2,1024]{1,0:T(2,128)(2,1)S(1)}, u32[]{:S(2)}, u32[]{:S(2)}) collective-permute-start(bf16[2,1024]{1,0:T(2,128)(2,1)S(1)} %get-tuple-element.75), channel_id=1, source_target_pairs={{0,13},{1,12},{2,15},{3,14},{4,9},{5,8},{6,11},{7,10},{8,5},{9,4},... | collective-permute-start | bytes 12296 | tf_op jit(solution)/shard_map/ppermute | solution.py:50
  29.2 3.9 %collective-permute-start.13 = (bf16[2,1024]{1,0:T(2,128)(2,1)S(1)}, bf16[2,1024]{1,0:T(2,128)(2,1)S(1)}, u32[]{:S(2)}, u32[]{:S(2)}) collective-permute-start(bf16[2,1024]{1,0:T(2,128)(2,1)S(1)} %get-tuple-element.76), channel_id=1, source_target_pairs={{0,9},{1,8},{2,11},{3,10},{4,13},{5,12},{6,15},{7,14},{8,1},{9,0},... | collective-permute-start | bytes 12296 | tf_op jit(solution)/shard_map/ppermute | solution.py:50
  29.6 3.5 %collective-permute-start.14 = (bf16[2,1024]{1,0:T(2,128)(2,1)S(1)}, bf16[2,1024]{1,0:T(2,128)(2,1)S(1)}, u32[]{:S(2)}, u32[]{:S(2)}) collective-permute-start(bf16[2,1024]{1,0:T(2,128)(2,1)S(1)} %get-tuple-element.77), channel_id=1, source_target_pairs={{0,5},{1,4},{2,7},{3,6},{4,1},{5,0},{6,3},{7,2},{8,13},{9,12},{10,... | collective-permute-start | bytes 12296 | tf_op jit(solution)/shard_map/ppermute | solution.py:50
  33.2 8.1 %copy-start.2 = (bf16[2048,3584]{1,0:T(8,128)(2,1)S(1)}, bf16[2048,3584]{1,0:T(8,128)(2,1)}, u32[]{:S(2)}) copy-start(bf16[2048,3584]{1,0:T(8,128)(2,1)} %up_ref.3) | copy-start | bytes 44040196
  34.1 6.1 %collective-permute-start.15 = (bf16[8,2048]{1,0:T(8,128)(2,1)S(1)}, bf16[8,2048]{1,0:T(8,128)(2,1)S(1)}, u32[]{:S(2)}, u32[]{:S(2)}) collective-permute-start(bf16[8,2048]{1,0:T(8,128)(2,1)S(1)} %get-tuple-element.84), channel_id=1, source_target_pairs={{0,12},{1,13},{2,14},{3,15},{4,8},{5,9},{6,10},{7,11},{8,4},{9,5},... | collective-permute-start | bytes 98312 | tf_op jit(solution)/shard_map/ppermute | solution.py:50
  36.1 5.2 %collective-permute-start.16 = (bf16[8,2048]{1,0:T(8,128)(2,1)S(1)}, bf16[8,2048]{1,0:T(8,128)(2,1)S(1)}, u32[]{:S(2)}, u32[]{:S(2)}) collective-permute-start(bf16[8,2048]{1,0:T(8,128)(2,1)S(1)} %get-tuple-element.85), channel_id=1, source_target_pairs={{0,8},{1,9},{2,10},{3,11},{4,12},{5,13},{6,14},{7,15},{8,0},{9,1},... | collective-permute-start | bytes 98312 | tf_op jit(solution)/shard_map/ppermute | solution.py:50
  37.2 4.1 %collective-permute-start.17 = (bf16[8,2048]{1,0:T(8,128)(2,1)S(1)}, bf16[8,2048]{1,0:T(8,128)(2,1)S(1)}, u32[]{:S(2)}, u32[]{:S(2)}) collective-permute-start(bf16[8,2048]{1,0:T(8,128)(2,1)S(1)} %get-tuple-element.86), channel_id=1, source_target_pairs={{0,4},{1,5},{2,6},{3,7},{4,0},{5,1},{6,2},{7,3},{8,12},{9,13},{10,... | collective-permute-start | bytes 98312 | tf_op jit(solution)/shard_map/ppermute | solution.py:50
  43.3 2.6 %collective-permute-start.20 = (bf16[8,3712]{1,0:T(8,128)(2,1)S(1)}, bf16[8,3712]{1,0:T(8,128)(2,1)S(1)}, u32[]{:S(2)}, u32[]{:S(2)}) collective-permute-start(bf16[8,3712]{1,0:T(8,128)(2,1)S(1)} %get-tuple-element.90.first_ref), channel_id=1, source_target_pairs={{0,1},{1,0},{2,3},{3,2},{4,5},{5,4},{6,7},{7,6},{8,9},{9,8},{10,11... | collective-permute-start | bytes 178184 | tf_op jit(solution)/shard_map/ppermute | solution.py:31
  43.3 4.8 %slice-start = ((s8[14680064]{0:T(1024)(128)(4,1)}), s8[4194304]{0:T(1024)(128)(4,1)S(1)}, s32[]{:S(2)}) async-start(s8[14680064]{0:T(1024)(128)(4,1)} %bitcast.4), calls=%async_computation | async-start | bytes 8388608
  43.3 4.8 %slice-start.1 = ((s8[14680064]{0:T(1024)(128)(4,1)}), s8[4194304]{0:T(1024)(128)(4,1)S(1)}, s32[]{:S(2)}) async-start(s8[14680064]{0:T(1024)(128)(4,1)} %bitcast.4), calls=%async_computation.1 | async-start | bytes 8388608
  43.3 4.7 %slice-start.2 = ((s8[14680064]{0:T(1024)(128)(4,1)}), s8[4194304]{0:T(1024)(128)(4,1)S(1)}, s32[]{:S(2)}) async-start(s8[14680064]{0:T(1024)(128)(4,1)} %bitcast.4), calls=%async_computation.2 | async-start | bytes 8388608
  43.3 5.2 %slice-start.3 = ((s8[14680064]{0:T(1024)(128)(4,1)}), s8[2097152]{0:T(1024)(128)(4,1)S(1)}, s32[]{:S(2)}) async-start(s8[14680064]{0:T(1024)(128)(4,1)} %bitcast.4), calls=%async_computation.3 | async-start | bytes 4194304
  45.3 1.8 %collective-permute-start.18 = (bf16[8,3584]{1,0:T(8,128)(2,1)S(1)}, bf16[8,3584]{1,0:T(8,128)(2,1)S(1)}, u32[]{:S(2)}, u32[]{:S(2)}) collective-permute-start(bf16[8,3584]{1,0:T(8,128)(2,1)S(1)} %second_gate_up.1.first_ref), channel_id=1, source_target_pairs={{0,1},{1,0},{2,3},{3,2},{4,5},{5,4},{6,7},{7,6},{8,9},{9,8},{10,11... | collective-permute-start | bytes 172040 | tf_op jit(solution)/shard_map/ppermute | solution.py:31
  45.9 4.6 %collective-permute-start.21 = (bf16[8,3712]{1,0:T(8,128)(2,1)S(1)}, bf16[8,3712]{1,0:T(8,128)(2,1)S(1)}, u32[]{:S(2)}, u32[]{:S(2)}) collective-permute-start(bf16[8,3712]{1,0:T(8,128)(2,1)S(1)} %pair_sum.3.near_ref), channel_id=1, source_target_pairs={{0,2},{1,3},{2,0},{3,1},{4,6},{5,7},{6,4},{7,5},{8,10},{9,11},{10,... | collective-permute-start | bytes 178184 | tf_op jit(solution)/shard_map/ppermute | solution.py:31
  47.1 4.6 %collective-permute-start.19 = (bf16[8,3584]{1,0:T(8,128)(2,1)S(1)}, bf16[8,3584]{1,0:T(8,128)(2,1)S(1)}, u32[]{:S(2)}, u32[]{:S(2)}) collective-permute-start(bf16[8,3584]{1,0:T(8,128)(2,1)S(1)} %pair_sum.2.after_ref.near_ref), channel_id=1, source_target_pairs={{0,2},{1,3},{2,0},{3,1},{4,6},{5,7},{6,4},{7,5},{8,10},{9,11},{10,... | collective-permute-start | bytes 172040 | tf_op jit(solution)/shard_map/ppermute | solution.py:31
  53.1 5.5 %collective-permute-start.22 = (bf16[2,2048]{1,0:T(2,128)(2,1)S(1)}, bf16[2,2048]{1,0:T(2,128)(2,1)S(1)}, u32[]{:S(2)}, u32[]{:S(2)}) collective-permute-start(bf16[2,2048]{1,0:T(2,128)(2,1)S(1)} %get-tuple-element.93), channel_id=1, source_target_pairs={{0,12},{1,13},{2,14},{3,15},{4,8},{5,9},{6,10},{7,11},{8,4},{9,5},... | collective-permute-start | bytes 24584 | tf_op jit(solution)/shard_map/ppermute | solution.py:50
  55.1 4.5 %collective-permute-start.23 = (bf16[2,2048]{1,0:T(2,128)(2,1)S(1)}, bf16[2,2048]{1,0:T(2,128)(2,1)S(1)}, u32[]{:S(2)}, u32[]{:S(2)}) collective-permute-start(bf16[2,2048]{1,0:T(2,128)(2,1)S(1)} %get-tuple-element.94), channel_id=1, source_target_pairs={{0,8},{1,9},{2,10},{3,11},{4,12},{5,13},{6,14},{7,15},{8,0},{9,1},... | collective-permute-start | bytes 24584 | tf_op jit(solution)/shard_map/ppermute | solution.py:50
  55.8 3.8 %collective-permute-start.24 = (bf16[2,2048]{1,0:T(2,128)(2,1)S(1)}, bf16[2,2048]{1,0:T(2,128)(2,1)S(1)}, u32[]{:S(2)}, u32[]{:S(2)}) collective-permute-start(bf16[2,2048]{1,0:T(2,128)(2,1)S(1)} %get-tuple-element.95), channel_id=1, source_target_pairs={{0,4},{1,5},{2,6},{3,7},{4,0},{5,1},{6,2},{7,3},{8,12},{9,13},{10,... | collective-permute-start | bytes 24584 | tf_op jit(solution)/shard_map/ppermute | solution.py:50

commit v22 on v21

--- a/solution.py
+++ b/solution.py
@@ -423,7 +423,7 @@
 
 
 def out_kernel(slots, later, upper_ref, lower_ref, *refs):
-    pieces = refs[:slots][::-1]
+    pieces = in_slot_order(refs[:slots])
     outs = refs[slots + later : 2 * slots + later]
     left_s = refs[-1]
     own_rows = pieces[0].shape[0]
@@ -458,7 +458,12 @@
         scratch_shapes=[pltpu.VMEM((own_rows * slots, depth), jnp.float32)],
         compiler_params=params(3),
         name="project_out",
-    )(resident(upper), resident(lower), *pieces[::-1], *[resident(w) for w in later])
+    )(
+        resident(upper),
+        resident(lower),
+        *in_start_order(pieces),
+        *[resident(w) for w in later],
+    )
 
 
 def pair_kernel(first_ref, second_ref, out_ref):
@@ -700,8 +705,12 @@
     shards, out_upper = lax.optimization_barrier((exchange(shard, "inner"), out_upper))
     pieces = combine(shards, [w_gate], all_rows, slots)
     (out_lower,) = load(w_out, after=pieces[0], spans=[(cut, w_out.shape[0] - cut)])
-    pieces, out_lower = lax.optimization_barrier((scatter_slots(pieces, 1)[::-1], out_lower))
-    parts = scatter_slots(project_out(pieces[::-1], out_upper, out_lower, [w_up]), 0)
+    pieces, out_lower = lax.optimization_barrier(
+        (in_start_order(scatter_slots(pieces, 1)), out_lower)
+    )
+    parts = scatter_slots(
+        project_out(in_slot_order(pieces), out_upper, out_lower, [w_up]), 0
+    )
 
     tiles = w_gate.shape[1] // LANES
     first = (tiles + 1) // 2 * LANES

time: 60.4 us -> 60.7 us (level)
  starting transfers between devices: 28.6 us -> 27.7 us
  Pallas kernels: 20 us -> 20.8 us
    ppermute x12, starting transfers between devices: 15.2 us -> 14.3 us  [scatter_slots(): got.append(lax.ppermute(pieces[k], ('tensor', 'inner'), pairs))]
    pallas_call x5, Pallas kernels: 9.26 us -> 9.98 us  [load(): pl.pallas_call(functools.partial(load_kernel, spans), out_shape=tuple((pl...]
  transfers between devices with their start and end apart: 25 -> 25, of which waited for: 10 -> 11; matrix products, arithmetic and copies ran while one was open for 0% -> 0% of each run, Pallas kernels for 21% -> 22%
where the time goes in v22:
time: 60.7 us; the launch traced here: 60.6 us
  starting transfers between devices  27.7 us (46%)
  Pallas kernels  20.8 us (34%)
  waiting for transfers between devices  11.1 us (18%)
  local copies, waits for them, and re-layouts  0.63 us (1%)
    ppermute x12, starting transfers between devices, scatter_slots(): got.append(lax.ppermute(pieces[k], ('tensor', 'inner'), pairs))  14.3 us
    ppermute x13, starting transfers between devices, swap_with(): return lax.ppermute(value, axis, [(i, i ^ step) for i in range(count)])  13.4 us
    pallas_call x5, Pallas kernels, load(): pl.pallas_call(functools.partial(load_kernel, spans), out_shape=tuple((pl...  9.98 us
    ppermute x12, waiting for transfers between devices, scatter_slots(): got.append(lax.ppermute(pieces[k], ('tensor', 'inner'), pairs))  6.2 us
    ppermute x13, waiting for transfers between devices, swap_with(): return lax.ppermute(value, axis, [(i, i ^ step) for i in range(count)])  4.88 us
    pallas_call x1, Pallas kernels, first_gate_up(): pl.pallas_call(functools.partial(first_gate_up_kernel, slots, count), out...  2 us
    pallas_call x1, Pallas kernels, second_gate_up(): pl.pallas_call(functools.partial(second_gate_up_kernel, first, count), ou...  2 us
    pallas_call x1, Pallas kernels, attend(): pl.pallas_call(functools.partial(attend_kernel, slots, len(parts)), out_s...  1.49 us
  transfers between devices with their start and end apart: 25, of which 11 were waited for; matrix products, arithmetic and copies ran while one was open for 0% of the time, Pallas kernels for 22%

profile of v22, /device:TPU:0, one launch (start us, length us, event | category | flops | bytes accessed | tf_op | source)
XLA Modules:
  0.0 60.6 jit_solution(12462607884122945920)
XLA Ops:
  0.0 4.0 %collective-permute-start = (bf16[2,2048]{1,0:T(2,128)(2,1)}, bf16[2,2048]{1,0:T(2,128)(2,1)S(1)}, u32[]{:S(2)}, u32[]{:S(2)}) collective-permute-start(bf16[2,2048]{1,0:T(2,128)(2,1)} %refs_5_.1), channel_id=1, source_target_pairs={{0,8},{4,12},{8,0},{12,4},{1,9},{5,13},{9,1},{13,5},{2,10},{6,14},... | collective-permute-start | bytes 24584 | tf_op jit(solution)/shard_map/ppermute | solution.py:31
  4.0 1.3 %collective-permute-start.1 = (bf16[2,2048]{1,0:T(2,128)(2,1)}, bf16[2,2048]{1,0:T(2,128)(2,1)S(1)}, u32[]{:S(2)}, u32[]{:S(2)}) collective-permute-start(bf16[2,2048]{1,0:T(2,128)(2,1)} %refs_5_.1), channel_id=1, source_target_pairs={{0,12},{4,8},{8,4},{12,0},{1,13},{5,9},{9,5},{13,1},{2,14},{6,10},... | collective-permute-start | bytes 24584 | tf_op jit(solution)/shard_map/ppermute | solution.py:31
  5.4 0.2 collective-permute-start.2
  5.6 2.7 %load.5 = (bf16[2,2048]{1,0:T(2,128)(2,1)S(1)}, bf16[2048]{0:T(1024)(128)(2,1)S(1)}, bf16[2048]{0:T(1024)(128)(2,1)S(1)}, bf16[2048,256]{1,0:T(8,128)(2,1)S(1)}, bf16[2048,1024]{1,0:T(8,128)(2,1)S(1)}) custom-call(bf16[2,2048]{1,0:T(2,128)(2,1)} %refs_5_.1, bf16[2048]{0:T(1024)(128)(2,1)} %refs_1_.1, bf16[2048]{0:T(1024)(128)(2,1)} %refs_2_.1, ...), custom_call_target="tpu_custom_call" | custom-call | bytes 5259264 | tf_op jit(solution)/shard_map/load/pallas_call | solution.py:159
  8.4 1.3 %collective-permute-done.1.refs_1_ = bf16[2,2048]{1,0:T(2,128)(2,1)S(1)} collective-permute-done((bf16[2,2048]{1,0:T(2,128)(2,1)}, bf16[2,2048]{1,0:T(2,128)(2,1)S(1)}, u32[]{:S(2)}, u32[]{:S(2)}) %collective-permute-start.1) | collective-permute-done | bytes 8224 | tf_op jit(solution)/shard_map/ppermute | solution.py:31
  9.7 0.0 collective-permute-done.2.refs_2_
  9.7 0.8 %project_qkv.1 = (f32[8,2048]{1,0:T(8,128)S(1)}, bf16[2,1408]{1,0:T(2,128)(2,1)S(1)}, bf16[2,1408]{1,0:T(2,128)(2,1)S(1)}, bf16[2,1408]{1,0:T(2,128)(2,1)S(1)}, bf16[2,1408]{1,0:T(2,128)(2,1)S(1)}) custom-call(bf16[2048]{0:T(1024)(128)(2,1)S(1)} %get-tuple-element.51.gain_ref, bf16[2048,1024]{1,0:T(8,128)(2,1)S(1)} %get-tuple-element.52.wq_ref, ...), custom_call_target="tpu_custom_call" | custom-call | tf_op jit(solution)/shard_map/project_qkv/pallas_call | solution.py:212
  10.5 0.3 collective-permute-start.3
  10.8 1.5 %collective-permute-start.4 = (bf16[2,1408]{1,0:T(2,128)(2,1)S(1)}, bf16[2,1408]{1,0:T(2,128)(2,1)S(1)}, u32[]{:S(2)}, u32[]{:S(2)}) collective-permute-start(bf16[2,1408]{1,0:T(2,128)(2,1)S(1)} %get-tuple-element.60), channel_id=1, source_target_pairs={{0,9},{1,8},{2,11},{3,10},{4,13},{5,12},{6,15},{7,14},{8,1},{9,0},... | collective-permute-start | bytes 16904 | tf_op jit(solution)/shard_map/ppermute | solution.py:50
  12.3 0.7 %collective-permute-start.5 = (bf16[2,1408]{1,0:T(2,128)(2,1)S(1)}, bf16[2,1408]{1,0:T(2,128)(2,1)S(1)}, u32[]{:S(2)}, u32[]{:S(2)}) collective-permute-start(bf16[2,1408]{1,0:T(2,128)(2,1)S(1)} %get-tuple-element.61), channel_id=1, source_target_pairs={{0,5},{1,4},{2,7},{3,6},{4,1},{5,0},{6,3},{7,2},{8,13},{9,12},{10,... | collective-permute-start | bytes 16904 | tf_op jit(solution)/shard_map/ppermute | solution.py:50
  13.0 0.1 fusion.4
  13.1 1.6 %load.6.key_ref = bf16[2,4096,128]{2,1,0:T(8,128)(2,1)S(1)} custom-call(bf16[2,4096,128]{2,1,0:T(8,128)(2,1)} %bitcast.8, f32[8,2048]{1,0:T(8,128)S(1)} %get-tuple-element.56.refs_1_.rows_ref), custom_call_target="tpu_custom_call" | custom-call | bytes 2097152 | tf_op jit(solution)/shard_map/load/pallas_call | solution.py:159
  14.7 0.7 %collective-permute-done.3.refs_0_ = bf16[2,1408]{1,0:T(2,128)(2,1)S(1)} collective-permute-done((bf16[2,1408]{1,0:T(2,128)(2,1)S(1)}, bf16[2,1408]{1,0:T(2,128)(2,1)S(1)}, u32[]{:S(2)}, u32[]{:S(2)}) %collective-permute-start.3) | collective-permute-done | bytes 5664 | tf_op jit(solution)/shard_map/ppermute | solution.py:50
  15.4 0.0 collective-permute-done.4.refs_1_
  15.4 0.0 collective-permute-done.5.refs_2_
  15.5 2.4 %collective-permute-start.6 = (bf16[8,1408]{1,0:T(8,128)(2,1)S(1)}, bf16[8,1408]{1,0:T(8,128)(2,1)S(1)}, u32[]{:S(2)}, u32[]{:S(2)}) collective-permute-start(bf16[8,1408]{1,0:T(8,128)(2,1)S(1)} %stack.1.refs_1_.refs_0_), channel_id=1, source_target_pairs={{0,3},{1,2},{2,1},{3,0},{4,7},{5,6},{6,5},{7,4},{8,11},{9,10},{10,... | collective-permute-start | bytes 67592 | tf_op jit(solution)/shard_map/ppermute | solution.py:31
  17.9 0.5 collective-permute-start.7
  18.4 0.0 collective-permute-start.8
  18.4 0.1 fusion
  18.5 0.0 copy-start
  18.5 1.8 %load.7.value_ref = bf16[2,4096,128]{2,1,0:T(8,128)(2,1)S(1)} custom-call(bf16[2,4096,128]{2,1,0:T(8,128)(2,1)} %bitcast.9, bf16[8,1408]{1,0:T(8,128)(2,1)S(1)} %stack.1.refs_1_.refs_0_), custom_call_target="tpu_custom_call" | custom-call | bytes 2097152 | tf_op jit(solution)/shard_map/load/pallas_call | solution.py:159
  20.3 0.0 collective-permute-done.6.refs_3_
  20.3 1.3 %collective-permute-done.7.refs_2_ = bf16[8,1408]{1,0:T(8,128)(2,1)S(1)} collective-permute-done((bf16[8,1408]{1,0:T(8,128)(2,1)S(1)}, bf16[8,1408]{1,0:T(8,128)(2,1)S(1)}, u32[]{:S(2)}, u32[]{:S(2)}) %collective-permute-start.7) | collective-permute-done | bytes 22560 | tf_op jit(solution)/shard_map/ppermute | solution.py:31
  21.7 0.0 collective-permute-done.8.refs_1_
  21.7 0.1 broadcast_in_dim.10.lengths_ref
  21.8 1.5 %attend.1.refs_1_.refs_3_ = bf16[80,128]{1,0:T(8,128)(2,1)S(1)} custom-call(s32[2,128]{1,0:T(2,128)S(1)} %broadcast_in_dim.10.lengths_ref, f32[8,128]{1,0:T(8,128)S(1)} %bitcast.6, f32[8,128]{1,0:T(8,128)S(1)} %bitcast.7, bf16[2,4096,128]{2,1,0:T(8,128)(2,1)S(1)} %load.6.key_ref, bf16[2,4096,128]{2,1,0:T(8,128)(2,1)S(1)} %load.7.value_ref, ...), custom_call_target="tpu_custom_call" | custom-call | tf_op jit(solution)/shard_map/attend/pallas_call | solution.py:356
  23.2 0.6 collective-permute-start.10
  23.8 0.0 collective-permute-start.11
  23.9 1.6 %collective-permute-start.9 = (bf16[80,128]{1,0:T(8,128)(2,1)S(1)}, bf16[80,128]{1,0:T(8,128)(2,1)S(1)}, u32[]{:S(2)}, u32[]{:S(2)}) collective-permute-start(bf16[80,128]{1,0:T(8,128)(2,1)S(1)} %attend.1.refs_1_.refs_3_), channel_id=1, source_target_pairs={{0,1},{1,0},{2,3},{3,2},{4,5},{5,4},{6,7},{7,6},{8,9},{9,8},{10,11... | collective-permute-start | bytes 61448 | tf_op jit(solution)/shard_map/ppermute | solution.py:31
  25.5 1.5 %load.8.upper_ref = bf16[512,2048]{1,0:T(8,128)(2,1)S(1)} custom-call(bf16[1024,2048]{1,0:T(8,128)(2,1)} %refs_0_.5, bf16[80,128]{1,0:T(8,128)(2,1)S(1)} %attend.1.refs_1_.refs_3_), custom_call_target="tpu_custom_call" | custom-call | bytes 2097152 | tf_op jit(solution)/shard_map/load/pallas_call | solution.py:159
  27.0 0.3 collective-permute-done.10.refs_1_
  27.3 0.0 collective-permute-done.11.refs_0_
  27.3 0.0 collective-permute-done.9.refs_2_
  27.3 0.0 copy-start.1
  27.3 0.3 combine.1
  27.6 1.0 %collective-permute-start.12 = (bf16[2,1024]{1,0:T(2,128)(2,1)S(1)}, bf16[2,1024]{1,0:T(2,128)(2,1)S(1)}, u32[]{:S(2)}, u32[]{:S(2)}) collective-permute-start(bf16[2,1024]{1,0:T(2,128)(2,1)S(1)} %get-tuple-element.75), channel_id=1, source_target_pairs={{0,9},{1,8},{2,11},{3,10},{4,13},{5,12},{6,15},{7,14},{8,1},{9,0},... | collective-permute-start | bytes 12296 | tf_op jit(solution)/shard_map/ppermute | solution.py:50
  28.6 2.0 %collective-permute-start.13 = (bf16[2,1024]{1,0:T(2,128)(2,1)S(1)}, bf16[2,1024]{1,0:T(2,128)(2,1)S(1)}, u32[]{:S(2)}, u32[]{:S(2)}) collective-permute-start(bf16[2,1024]{1,0:T(2,128)(2,1)S(1)} %get-tuple-element.76), channel_id=1, source_target_pairs={{0,13},{1,12},{2,15},{3,14},{4,9},{5,8},{6,11},{7,10},{8,5},{9,4},... | collective-permute-start | bytes 12296 | tf_op jit(solution)/shard_map/ppermute | solution.py:50
  30.5 0.0 collective-permute-start.14
  30.5 2.3 %load.9.lower_ref = bf16[512,2048]{1,0:T(8,128)(2,1)S(1)} custom-call(bf16[1024,2048]{1,0:T(8,128)(2,1)} %refs_0_.5, bf16[2,1024]{1,0:T(2,128)(2,1)S(1)} %get-tuple-element.83.refs_1_.refs_3_), custom_call_target="tpu_custom_call" | custom-call | bytes 2097152 | tf_op jit(solution)/shard_map/load/pallas_call | solution.py:159
  32.8 0.0 collective-permute-done.12.refs_0_
  32.8 0.5 collective-permute-done.13.refs_1_
  33.4 0.2 collective-permute-done.14.refs_2_
  33.6 0.9 %project_out.1 = (bf16[8,2048]{1,0:T(8,128)(2,1)S(1)}, bf16[8,2048]{1,0:T(8,128)(2,1)S(1)}, bf16[8,2048]{1,0:T(8,128)(2,1)S(1)}, bf16[8,2048]{1,0:T(8,128)(2,1)S(1)}) custom-call(bf16[512,2048]{1,0:T(8,128)(2,1)S(1)} %load.8.upper_ref, bf16[512,2048]{1,0:T(8,128)(2,1)S(1)} %load.9.lower_ref, bf16[2,1024]{1,0:T(2,128)(2,1)S(1)} %collective-permute-done.12.refs_0_, ...), custom_call_target="tpu_custom_call" | custom-call | tf_op jit(solution)/shard_map/project_out/pallas_call | solution.py:453
  34.5 2.0 %collective-permute-start.15 = (bf16[8,2048]{1,0:T(8,128)(2,1)S(1)}, bf16[8,2048]{1,0:T(8,128)(2,1)S(1)}, u32[]{:S(2)}, u32[]{:S(2)}) collective-permute-start(bf16[8,2048]{1,0:T(8,128)(2,1)S(1)} %get-tuple-element.84), channel_id=1, source_target_pairs={{0,12},{1,13},{2,14},{3,15},{4,8},{5,9},{6,10},{7,11},{8,4},{9,5},... | collective-permute-start | bytes 98312 | tf_op jit(solution)/shard_map/ppermute | solution.py:50
  36.6 2.4 %collective-permute-start.17 = (bf16[8,2048]{1,0:T(8,128)(2,1)S(1)}, bf16[8,2048]{1,0:T(8,128)(2,1)S(1)}, u32[]{:S(2)}, u32[]{:S(2)}) collective-permute-start(bf16[8,2048]{1,0:T(8,128)(2,1)S(1)} %get-tuple-element.86), channel_id=1, source_target_pairs={{0,4},{1,5},{2,6},{3,7},{4,0},{5,1},{6,2},{7,3},{8,12},{9,13},{10,... | collective-permute-start | bytes 98312 | tf_op jit(solution)/shard_map/ppermute | solution.py:50
  38.9 1.5 %collective-permute-done.15.refs_0_ = bf16[8,2048]{1,0:T(8,128)(2,1)S(1)} collective-permute-done((bf16[8,2048]{1,0:T(8,128)(2,1)S(1)}, bf16[8,2048]{1,0:T(8,128)(2,1)S(1)}, u32[]{:S(2)}, u32[]{:S(2)}) %collective-permute-start.15) | collective-permute-done | bytes 32800 | tf_op jit(solution)/shard_map/ppermute | solution.py:50
  40.5 1.0 %collective-permute-done.16.refs_1_ = bf16[8,2048]{1,0:T(8,128)(2,1)S(1)} collective-permute-done((bf16[8,2048]{1,0:T(8,128)(2,1)S(1)}, bf16[8,2048]{1,0:T(8,128)(2,1)S(1)}, u32[]{:S(2)}, u32[]{:S(2)}) %collective-permute-start.16) | collective-permute-done | bytes 32800 | tf_op jit(solution)/shard_map/ppermute | solution.py:50
  41.5 2.0 %first_gate_up.1 = (bf16[8,3712]{1,0:T(8,128)(2,1)S(1)}, f32[2,2048]{1,0:T(2,128)S(1)}, bf16[8,2048]{1,0:T(8,128)(2,1)S(1)}) custom-call(f32[8,2048]{1,0:T(8,128)S(1)} %get-tuple-element.56.refs_1_.rows_ref, bf16[2048]{0:T(1024)(128)(2,1)S(1)} %get-tuple-element.57.gain_ref, bf16[2048,3584]{1,0:T(8,128)(2,1)S(1)} %copy-done, ...), custom_call_target="tpu_custom_call" | custom-call | flops 117440512 | bytes 14680064 | tf_op jit(solution)/shard_map/first_gate_up/pallas_call | solution.py:514
  43.5 0.0 slice-start.1
  43.5 2.0 %second_gate_up.1.first_ref = bf16[8,3584]{1,0:T(8,128)(2,1)S(1)} custom-call(bf16[8,2048]{1,0:T(8,128)(2,1)S(1)} %get-tuple-element.89.scaled_ref, bf16[2048,3584]{1,0:T(8,128)(2,1)S(1)} %copy-done, bf16[2048,3584]{1,0:T(8,128)(2,1)S(1)} %copy-done.2), custom_call_target="tpu_custom_call" | custom-call | flops 117440512 | bytes 14680064 | tf_op jit(solution)/shard_map/second_gate_up/pallas_call | solution.py:543
  45.5 0.5 collective-permute-start.18
  46.0 0.9 %collective-permute-start.21 = (bf16[8,3712]{1,0:T(8,128)(2,1)S(1)}, bf16[8,3712]{1,0:T(8,128)(2,1)S(1)}, u32[]{:S(2)}, u32[]{:S(2)}) collective-permute-start(bf16[8,3712]{1,0:T(8,128)(2,1)S(1)} %pair_sum.3.near_ref), channel_id=1, source_target_pairs={{0,2},{1,3},{2,0},{3,1},{4,6},{5,7},{6,4},{7,5},{8,10},{9,11},{10,... | collective-permute-start | bytes 178184 | tf_op jit(solution)/shard_map/ppermute | solution.py:31
  46.9 0.0 collective-permute-done.18.second_ref
  46.9 1.3 %collective-permute-start.19 = (bf16[8,3584]{1,0:T(8,128)(2,1)S(1)}, bf16[8,3584]{1,0:T(8,128)(2,1)S(1)}, u32[]{:S(2)}, u32[]{:S(2)}) collective-permute-start(bf16[8,3584]{1,0:T(8,128)(2,1)S(1)} %pair_sum.2.after_ref.near_ref), channel_id=1, source_target_pairs={{0,2},{1,3},{2,0},{3,1},{4,6},{5,7},{6,4},{7,5},{8,10},{9,11},{10,... | collective-permute-start | bytes 172040 | tf_op jit(solution)/shard_map/ppermute | solution.py:31
  48.2 0.5 slice-done.3
  48.8 1.9 %collective-permute-done.21.far_ref = bf16[8,3712]{1,0:T(8,128)(2,1)S(1)} collective-permute-done((bf16[8,3712]{1,0:T(8,128)(2,1)S(1)}, bf16[8,3712]{1,0:T(8,128)(2,1)S(1)}, u32[]{:S(2)}, u32[]{:S(2)}) %collective-permute-start.21) | collective-permute-done | bytes 59424 | tf_op jit(solution)/shard_map/ppermute | solution.py:31
  50.7 1.3 %first_down.1 = (f32[8,2048]{1,0:T(8,128)S(1)}, f32[8,128]{1,0:T(8,128)S(1)}) custom-call(bf16[8,3712]{1,0:T(8,128)(2,1)S(1)} %pair_sum.3.near_ref, bf16[8,3712]{1,0:T(8,128)(2,1)S(1)} %collective-permute-done.21.far_ref, bf16[3584,2048]{1,0:T(8,128)(2,1)S(1)} %bitcast.5, f32[8,128]{1,0:T(8,128)S(1)} %hold.1.token_ref), custom_call_target="tpu_custom_call" | custom-call | flops 58720256 | bytes 7340032 | tf_op jit(solution)/shard_map/first_down/pallas_call | solution.py:581
  52.0 1.3 %second_down.1 = (bf16[2,2048]{1,0:T(2,128)(2,1)S(1)}, bf16[2,2048]{1,0:T(2,128)(2,1)S(1)}, bf16[2,2048]{1,0:T(2,128)(2,1)S(1)}, bf16[2,2048]{1,0:T(2,128)(2,1)S(1)}) custom-call(bf16[8,3584]{1,0:T(8,128)(2,1)S(1)} %pair_sum.2.after_ref.near_ref, bf16[8,3584]{1,0:T(8,128)(2,1)S(1)} %collective-permute-done.19.far_ref, bf16[3584,2048]{1,0:T(8,128)(2,1)S(1)} %bitcast.5, ...), custom_call_target="tpu_custom_call" | custom-call | tf_op jit(solution)/shard_map/second_down/pallas_call | solution.py:611
  53.3 2.1 %collective-permute-start.22 = (bf16[2,2048]{1,0:T(2,128)(2,1)S(1)}, bf16[2,2048]{1,0:T(2,128)(2,1)S(1)}, u32[]{:S(2)}, u32[]{:S(2)}) collective-permute-start(bf16[2,2048]{1,0:T(2,128)(2,1)S(1)} %get-tuple-element.93), channel_id=1, source_target_pairs={{0,12},{1,13},{2,14},{3,15},{4,8},{5,9},{6,10},{7,11},{8,4},{9,5},... | collective-permute-start | bytes 24584 | tf_op jit(solution)/shard_map/ppermute | solution.py:50
  55.4 0.8 %collective-permute-start.23 = (bf16[2,2048]{1,0:T(2,128)(2,1)S(1)}, bf16[2,2048]{1,0:T(2,128)(2,1)S(1)}, u32[]{:S(2)}, u32[]{:S(2)}) collective-permute-start(bf16[2,2048]{1,0:T(2,128)(2,1)S(1)} %get-tuple-element.94), channel_id=1, source_target_pairs={{0,8},{1,9},{2,10},{3,11},{4,12},{5,13},{6,14},{7,15},{8,0},{9,1},... | collective-permute-start | bytes 24584 | tf_op jit(solution)/shard_map/ppermute | solution.py:50
  56.2 1.6 %collective-permute-start.24 = (bf16[2,2048]{1,0:T(2,128)(2,1)S(1)}, bf16[2,2048]{1,0:T(2,128)(2,1)S(1)}, u32[]{:S(2)}, u32[]{:S(2)}) collective-permute-start(bf16[2,2048]{1,0:T(2,128)(2,1)S(1)} %get-tuple-element.95), channel_id=1, source_target_pairs={{0,4},{1,5},{2,6},{3,7},{4,0},{5,1},{6,2},{7,3},{8,12},{9,13},{10,... | collective-permute-start | bytes 24584 | tf_op jit(solution)/shard_map/ppermute | solution.py:50
  57.7 1.1 %collective-permute-done.22.refs_0_ = bf16[2,2048]{1,0:T(2,128)(2,1)S(1)} collective-permute-done((bf16[2,2048]{1,0:T(2,128)(2,1)S(1)}, bf16[2,2048]{1,0:T(2,128)(2,1)S(1)}, u32[]{:S(2)}, u32[]{:S(2)}) %collective-permute-start.22) | collective-permute-done | bytes 8224 | tf_op jit(solution)/shard_map/ppermute | solution.py:50
  58.8 1.1 %collective-permute-done.23.refs_1_ = bf16[2,2048]{1,0:T(2,128)(2,1)S(1)} collective-permute-done((bf16[2,2048]{1,0:T(2,128)(2,1)S(1)}, bf16[2,2048]{1,0:T(2,128)(2,1)S(1)}, u32[]{:S(2)}, u32[]{:S(2)}) %collective-permute-start.23) | collective-permute-done | bytes 8224 | tf_op jit(solution)/shard_map/ppermute | solution.py:50
  59.9 0.6 %finish.1 = bf16[2,2048]{1,0:T(2,128)(2,1)} custom-call(f32[2,2048]{1,0:T(2,128)S(1)} %get-tuple-element.88.updated_ref, bf16[2,2048]{1,0:T(2,128)(2,1)S(1)} %collective-permute-done.22.refs_0_, bf16[2,2048]{1,0:T(2,128)(2,1)S(1)} %collective-permute-done.23.refs_1_, bf16[2,2048]{1,0:T(2,128)(2,1)S(1)} %collective-permute-done.24.refs_2_, ...), custom_call_target="tpu_custom_call" | custom-call | tf_op jit(solution)/shard_map/finish/pallas_call | solution.py:644
  (27 shorter events, 0.1 us)
Async XLA Ops:
  0.0 8.4 %collective-permute-start = (bf16[2,2048]{1,0:T(2,128)(2,1)}, bf16[2,2048]{1,0:T(2,128)(2,1)S(1)}, u32[]{:S(2)}, u32[]{:S(2)}) collective-permute-start(bf16[2,2048]{1,0:T(2,128)(2,1)} %refs_5_.1), channel_id=1, source_target_pairs={{0,8},{4,12},{8,0},{12,4},{1,9},{5,13},{9,1},{13,5},{2,10},{6,14},... | collective-permute-start | bytes 24584 | tf_op jit(solution)/shard_map/ppermute | solution.py:31
  4.0 5.7 %collective-permute-start.1 = (bf16[2,2048]{1,0:T(2,128)(2,1)}, bf16[2,2048]{1,0:T(2,128)(2,1)S(1)}, u32[]{:S(2)}, u32[]{:S(2)}) collective-permute-start(bf16[2,2048]{1,0:T(2,128)(2,1)} %refs_5_.1), channel_id=1, source_target_pairs={{0,12},{4,8},{8,4},{12,0},{1,13},{5,9},{9,5},{13,1},{2,14},{6,10},... | collective-permute-start | bytes 24584 | tf_op jit(solution)/shard_map/ppermute | solution.py:31
  5.4 4.3 %collective-permute-start.2 = (bf16[2,2048]{1,0:T(2,128)(2,1)}, bf16[2,2048]{1,0:T(2,128)(2,1)S(1)}, u32[]{:S(2)}, u32[]{:S(2)}) collective-permute-start(bf16[2,2048]{1,0:T(2,128)(2,1)} %refs_5_.1), channel_id=1, source_target_pairs={{0,4},{4,0},{8,12},{12,8},{1,5},{5,1},{9,13},{13,9},{2,6},{6,2},{1... | collective-permute-start | bytes 24584 | tf_op jit(solution)/shard_map/ppermute | solution.py:31
  5.6 7.4 %copy-start.3 = (s32[8]{0:T(128)S(1)}, s32[8]{0:T(128)}, u32[]{:S(2)}) copy-start(s32[8]{0:T(128)} %param.23) | copy-start | bytes 100
  10.5 4.9 %collective-permute-start.3 = (bf16[2,1408]{1,0:T(2,128)(2,1)S(1)}, bf16[2,1408]{1,0:T(2,128)(2,1)S(1)}, u32[]{:S(2)}, u32[]{:S(2)}) collective-permute-start(bf16[2,1408]{1,0:T(2,128)(2,1)S(1)} %get-tuple-element.59), channel_id=1, source_target_pairs={{0,13},{1,12},{2,15},{3,14},{4,9},{5,8},{6,11},{7,10},{8,5},{9,4},... | collective-permute-start | bytes 16904 | tf_op jit(solution)/shard_map/ppermute | solution.py:50
  10.8 4.6 %collective-permute-start.4 = (bf16[2,1408]{1,0:T(2,128)(2,1)S(1)}, bf16[2,1408]{1,0:T(2,128)(2,1)S(1)}, u32[]{:S(2)}, u32[]{:S(2)}) collective-permute-start(bf16[2,1408]{1,0:T(2,128)(2,1)S(1)} %get-tuple-element.60), channel_id=1, source_target_pairs={{0,9},{1,8},{2,11},{3,10},{4,13},{5,12},{6,15},{7,14},{8,1},{9,0},... | collective-permute-start | bytes 16904 | tf_op jit(solution)/shard_map/ppermute | solution.py:50
  12.3 3.2 %collective-permute-start.5 = (bf16[2,1408]{1,0:T(2,128)(2,1)S(1)}, bf16[2,1408]{1,0:T(2,128)(2,1)S(1)}, u32[]{:S(2)}, u32[]{:S(2)}) collective-permute-start(bf16[2,1408]{1,0:T(2,128)(2,1)S(1)} %get-tuple-element.61), channel_id=1, source_target_pairs={{0,5},{1,4},{2,7},{3,6},{4,1},{5,0},{6,3},{7,2},{8,13},{9,12},{10,... | collective-permute-start | bytes 16904 | tf_op jit(solution)/shard_map/ppermute | solution.py:50
  15.5 4.8 %collective-permute-start.6 = (bf16[8,1408]{1,0:T(8,128)(2,1)S(1)}, bf16[8,1408]{1,0:T(8,128)(2,1)S(1)}, u32[]{:S(2)}, u32[]{:S(2)}) collective-permute-start(bf16[8,1408]{1,0:T(8,128)(2,1)S(1)} %stack.1.refs_1_.refs_0_), channel_id=1, source_target_pairs={{0,3},{1,2},{2,1},{3,0},{4,7},{5,6},{6,5},{7,4},{8,11},{9,10},{10,... | collective-permute-start | bytes 67592 | tf_op jit(solution)/shard_map/ppermute | solution.py:31
  17.9 3.8 %collective-permute-start.7 = (bf16[8,1408]{1,0:T(8,128)(2,1)S(1)}, bf16[8,1408]{1,0:T(8,128)(2,1)S(1)}, u32[]{:S(2)}, u32[]{:S(2)}) collective-permute-start(bf16[8,1408]{1,0:T(8,128)(2,1)S(1)} %stack.1.refs_1_.refs_0_), channel_id=1, source_target_pairs={{0,2},{1,3},{2,0},{3,1},{4,6},{5,7},{6,4},{7,5},{8,10},{9,11},{10,... | collective-permute-start | bytes 67592 | tf_op jit(solution)/shard_map/ppermute | solution.py:31
  18.4 3.3 %collective-permute-start.8 = (bf16[8,1408]{1,0:T(8,128)(2,1)S(1)}, bf16[8,1408]{1,0:T(8,128)(2,1)S(1)}, u32[]{:S(2)}, u32[]{:S(2)}) collective-permute-start(bf16[8,1408]{1,0:T(8,128)(2,1)S(1)} %stack.1.refs_1_.refs_0_), channel_id=1, source_target_pairs={{0,1},{1,0},{2,3},{3,2},{4,5},{5,4},{6,7},{7,6},{8,9},{9,8},{10,11... | collective-permute-start | bytes 67592 | tf_op jit(solution)/shard_map/ppermute | solution.py:31
  18.5 8.8 %copy-start = (bf16[2048,3584]{1,0:T(8,128)(2,1)S(1)}, bf16[2048,3584]{1,0:T(8,128)(2,1)}, u32[]{:S(2)}) copy-start(bf16[2048,3584]{1,0:T(8,128)(2,1)} %gate_ref.3) | copy-start | bytes 44040196
  23.2 4.0 %collective-permute-start.10 = (bf16[80,128]{1,0:T(8,128)(2,1)S(1)}, bf16[80,128]{1,0:T(8,128)(2,1)S(1)}, u32[]{:S(2)}, u32[]{:S(2)}) collective-permute-start(bf16[80,128]{1,0:T(8,128)(2,1)S(1)} %attend.1.refs_1_.refs_3_), channel_id=1, source_target_pairs={{0,2},{1,3},{2,0},{3,1},{4,6},{5,7},{6,4},{7,5},{8,10},{9,11},{10,... | collective-permute-start | bytes 61448 | tf_op jit(solution)/shard_map/ppermute | solution.py:31
  23.8 3.4 %collective-permute-start.11 = (bf16[80,128]{1,0:T(8,128)(2,1)S(1)}, bf16[80,128]{1,0:T(8,128)(2,1)S(1)}, u32[]{:S(2)}, u32[]{:S(2)}) collective-permute-start(bf16[80,128]{1,0:T(8,128)(2,1)S(1)} %attend.1.refs_1_.refs_3_), channel_id=1, source_target_pairs={{0,3},{1,2},{2,1},{3,0},{4,7},{5,6},{6,5},{7,4},{8,11},{9,10},{10,... | collective-permute-start | bytes 61448 | tf_op jit(solution)/shard_map/ppermute | solution.py:31
  23.9 3.4 %collective-permute-start.9 = (bf16[80,128]{1,0:T(8,128)(2,1)S(1)}, bf16[80,128]{1,0:T(8,128)(2,1)S(1)}, u32[]{:S(2)}, u32[]{:S(2)}) collective-permute-start(bf16[80,128]{1,0:T(8,128)(2,1)S(1)} %attend.1.refs_1_.refs_3_), channel_id=1, source_target_pairs={{0,1},{1,0},{2,3},{3,2},{4,5},{5,4},{6,7},{7,6},{8,9},{9,8},{10,11... | collective-permute-start | bytes 61448 | tf_op jit(solution)/shard_map/ppermute | solution.py:31
  27.3 6.3 %copy-start.1 = (bf16[2048,3584]{1,0:T(8,128)(2,1)S(1)}, bf16[2048,3584]{1,0:T(8,128)(2,1)}, u32[]{:S(2)}) copy-start(bf16[2048,3584]{1,0:T(8,128)(2,1)} %up_ref.3) | copy-start | bytes 44040196
  27.6 5.3 %collective-permute-start.12 = (bf16[2,1024]{1,0:T(2,128)(2,1)S(1)}, bf16[2,1024]{1,0:T(2,128)(2,1)S(1)}, u32[]{:S(2)}, u32[]{:S(2)}) collective-permute-start(bf16[2,1024]{1,0:T(2,128)(2,1)S(1)} %get-tuple-element.75), channel_id=1, source_target_pairs={{0,9},{1,8},{2,11},{3,10},{4,13},{5,12},{6,15},{7,14},{8,1},{9,0},... | collective-permute-start | bytes 12296 | tf_op jit(solution)/shard_map/ppermute | solution.py:50
  28.6 4.8 %collective-permute-start.13 = (bf16[2,1024]{1,0:T(2,128)(2,1)S(1)}, bf16[2,1024]{1,0:T(2,128)(2,1)S(1)}, u32[]{:S(2)}, u32[]{:S(2)}) collective-permute-start(bf16[2,1024]{1,0:T(2,128)(2,1)S(1)} %get-tuple-element.76), channel_id=1, source_target_pairs={{0,13},{1,12},{2,15},{3,14},{4,9},{5,8},{6,11},{7,10},{8,5},{9,4},... | collective-permute-start | bytes 12296 | tf_op jit(solution)/shard_map/ppermute | solution.py:50
  30.5 3.0 %collective-permute-start.14 = (bf16[2,1024]{1,0:T(2,128)(2,1)S(1)}, bf16[2,1024]{1,0:T(2,128)(2,1)S(1)}, u32[]{:S(2)}, u32[]{:S(2)}) collective-permute-start(bf16[2,1024]{1,0:T(2,128)(2,1)S(1)} %get-tuple-element.77), channel_id=1, source_target_pairs={{0,5},{1,4},{2,7},{3,6},{4,1},{5,0},{6,3},{7,2},{8,13},{9,12},{10,... | collective-permute-start | bytes 12296 | tf_op jit(solution)/shard_map/ppermute | solution.py:50
  33.6 7.9 %copy-start.2 = (bf16[2048,3584]{1,0:T(8,128)(2,1)S(1)}, bf16[2048,3584]{1,0:T(8,128)(2,1)}, u32[]{:S(2)}) copy-start(bf16[2048,3584]{1,0:T(8,128)(2,1)} %up_ref.3) | copy-start | bytes 44040196
  34.5 5.9 %collective-permute-start.15 = (bf16[8,2048]{1,0:T(8,128)(2,1)S(1)}, bf16[8,2048]{1,0:T(8,128)(2,1)S(1)}, u32[]{:S(2)}, u32[]{:S(2)}) collective-permute-start(bf16[8,2048]{1,0:T(8,128)(2,1)S(1)} %get-tuple-element.84), channel_id=1, source_target_pairs={{0,12},{1,13},{2,14},{3,15},{4,8},{5,9},{6,10},{7,11},{8,4},{9,5},... | collective-permute-start | bytes 98312 | tf_op jit(solution)/shard_map/ppermute | solution.py:50
  36.6 4.9 %collective-permute-start.16 = (bf16[8,2048]{1,0:T(8,128)(2,1)S(1)}, bf16[8,2048]{1,0:T(8,128)(2,1)S(1)}, u32[]{:S(2)}, u32[]{:S(2)}) collective-permute-start(bf16[8,2048]{1,0:T(8,128)(2,1)S(1)} %get-tuple-element.85), channel_id=1, source_target_pairs={{0,8},{1,9},{2,10},{3,11},{4,12},{5,13},{6,14},{7,15},{8,0},{9,1},... | collective-permute-start | bytes 98312 | tf_op jit(solution)/shard_map/ppermute | solution.py:50
  36.6 4.9 %collective-permute-start.17 = (bf16[8,2048]{1,0:T(8,128)(2,1)S(1)}, bf16[8,2048]{1,0:T(8,128)(2,1)S(1)}, u32[]{:S(2)}, u32[]{:S(2)}) collective-permute-start(bf16[8,2048]{1,0:T(8,128)(2,1)S(1)} %get-tuple-element.86), channel_id=1, source_target_pairs={{0,4},{1,5},{2,6},{3,7},{4,0},{5,1},{6,2},{7,3},{8,12},{9,13},{10,... | collective-permute-start | bytes 98312 | tf_op jit(solution)/shard_map/ppermute | solution.py:50
  43.5 2.6 %collective-permute-start.20 = (bf16[8,3712]{1,0:T(8,128)(2,1)S(1)}, bf16[8,3712]{1,0:T(8,128)(2,1)S(1)}, u32[]{:S(2)}, u32[]{:S(2)}) collective-permute-start(bf16[8,3712]{1,0:T(8,128)(2,1)S(1)} %get-tuple-element.90.first_ref), channel_id=1, source_target_pairs={{0,1},{1,0},{2,3},{3,2},{4,5},{5,4},{6,7},{7,6},{8,9},{9,8},{10,11... | collective-permute-start | bytes 178184 | tf_op jit(solution)/shard_map/ppermute | solution.py:31
  43.5 4.8 %slice-start = ((s8[14680064]{0:T(1024)(128)(4,1)}), s8[4194304]{0:T(1024)(128)(4,1)S(1)}, s32[]{:S(2)}) async-start(s8[14680064]{0:T(1024)(128)(4,1)} %bitcast.4), calls=%async_computation | async-start | bytes 8388608
  43.5 4.8 %slice-start.1 = ((s8[14680064]{0:T(1024)(128)(4,1)}), s8[4194304]{0:T(1024)(128)(4,1)S(1)}, s32[]{:S(2)}) async-start(s8[14680064]{0:T(1024)(128)(4,1)} %bitcast.4), calls=%async_computation.1 | async-start | bytes 8388608
  43.5 4.7 %slice-start.2 = ((s8[14680064]{0:T(1024)(128)(4,1)}), s8[4194304]{0:T(1024)(128)(4,1)S(1)}, s32[]{:S(2)}) async-start(s8[14680064]{0:T(1024)(128)(4,1)} %bitcast.4), calls=%async_computation.2 | async-start | bytes 8388608
  43.5 5.2 %slice-start.3 = ((s8[14680064]{0:T(1024)(128)(4,1)}), s8[2097152]{0:T(1024)(128)(4,1)S(1)}, s32[]{:S(2)}) async-start(s8[14680064]{0:T(1024)(128)(4,1)} %bitcast.4), calls=%async_computation.3 | async-start | bytes 4194304
  45.5 1.4 %collective-permute-start.18 = (bf16[8,3584]{1,0:T(8,128)(2,1)S(1)}, bf16[8,3584]{1,0:T(8,128)(2,1)S(1)}, u32[]{:S(2)}, u32[]{:S(2)}) collective-permute-start(bf16[8,3584]{1,0:T(8,128)(2,1)S(1)} %second_gate_up.1.first_ref), channel_id=1, source_target_pairs={{0,1},{1,0},{2,3},{3,2},{4,5},{5,4},{6,7},{7,6},{8,9},{9,8},{10,11... | collective-permute-start | bytes 172040 | tf_op jit(solution)/shard_map/ppermute | solution.py:31
  46.0 4.6 %collective-permute-start.21 = (bf16[8,3712]{1,0:T(8,128)(2,1)S(1)}, bf16[8,3712]{1,0:T(8,128)(2,1)S(1)}, u32[]{:S(2)}, u32[]{:S(2)}) collective-permute-start(bf16[8,3712]{1,0:T(8,128)(2,1)S(1)} %pair_sum.3.near_ref), channel_id=1, source_target_pairs={{0,2},{1,3},{2,0},{3,1},{4,6},{5,7},{6,4},{7,5},{8,10},{9,11},{10,... | collective-permute-start | bytes 178184 | tf_op jit(solution)/shard_map/ppermute | solution.py:31
  46.9 5.0 %collective-permute-start.19 = (bf16[8,3584]{1,0:T(8,128)(2,1)S(1)}, bf16[8,3584]{1,0:T(8,128)(2,1)S(1)}, u32[]{:S(2)}, u32[]{:S(2)}) collective-permute-start(bf16[8,3584]{1,0:T(8,128)(2,1)S(1)} %pair_sum.2.after_ref.near_ref), channel_id=1, source_target_pairs={{0,2},{1,3},{2,0},{3,1},{4,6},{5,7},{6,4},{7,5},{8,10},{9,11},{10,... | collective-permute-start | bytes 172040 | tf_op jit(solution)/shard_map/ppermute | solution.py:31
  53.3 5.5 %collective-permute-start.22 = (bf16[2,2048]{1,0:T(2,128)(2,1)S(1)}, bf16[2,2048]{1,0:T(2,128)(2,1)S(1)}, u32[]{:S(2)}, u32[]{:S(2)}) collective-permute-start(bf16[2,2048]{1,0:T(2,128)(2,1)S(1)} %get-tuple-element.93), channel_id=1, source_target_pairs={{0,12},{1,13},{2,14},{3,15},{4,8},{5,9},{6,10},{7,11},{8,4},{9,5},... | collective-permute-start | bytes 24584 | tf_op jit(solution)/shard_map/ppermute | solution.py:50
  55.4 4.5 %collective-permute-start.23 = (bf16[2,2048]{1,0:T(2,128)(2,1)S(1)}, bf16[2,2048]{1,0:T(2,128)(2,1)S(1)}, u32[]{:S(2)}, u32[]{:S(2)}) collective-permute-start(bf16[2,2048]{1,0:T(2,128)(2,1)S(1)} %get-tuple-element.94), channel_id=1, source_target_pairs={{0,8},{1,9},{2,10},{3,11},{4,12},{5,13},{6,14},{7,15},{8,0},{9,1},... | collective-permute-start | bytes 24584 | tf_op jit(solution)/shard_map/ppermute | solution.py:50
  56.2 3.7 %collective-permute-start.24 = (bf16[2,2048]{1,0:T(2,128)(2,1)S(1)}, bf16[2,2048]{1,0:T(2,128)(2,1)S(1)}, u32[]{:S(2)}, u32[]{:S(2)}) collective-permute-start(bf16[2,2048]{1,0:T(2,128)(2,1)S(1)} %get-tuple-element.95), channel_id=1, source_target_pairs={{0,4},{1,5},{2,6},{3,7},{4,0},{5,1},{6,2},{7,3},{8,12},{9,13},{10,... | collective-permute-start | bytes 24584 | tf_op jit(solution)/shard_map/ppermute | solution.py:50

commit v23 on v21

--- a/solution.py
+++ b/solution.py
@@ -88,7 +88,7 @@
 
 
 def tile_of(columns):
-    for tile in (1792, 1024, 896, 512, 256, 128):
+    for tile in (2048, 1792, 1024, 896, 512, 256, 128):
         if columns % tile == 0:
             return tile
     return columns

time: 60.4 us -> 60 us (level)
  no operation moved by 1% of the time
where the time goes in v23:
time: 60 us; the launch traced here: 59.8 us
  starting transfers between devices  28.6 us (48%)
  Pallas kernels  19.6 us (33%)
  waiting for transfers between devices  10.6 us (18%)
  local copies, waits for them, and re-layouts  0.63 us (1%)
    ppermute x12, starting transfers between devices, scatter_slots(): got.append(lax.ppermute(pieces[k], ('tensor', 'inner'), pairs))  15.2 us
    ppermute x13, starting transfers between devices, swap_with(): return lax.ppermute(value, axis, [(i, i ^ step) for i in range(count)])  13.4 us
    pallas_call x5, Pallas kernels, load(): pl.pallas_call(functools.partial(load_kernel, spans), out_shape=tuple((pl...  9.26 us
    ppermute x12, waiting for transfers between devices, scatter_slots(): got.append(lax.ppermute(pieces[k], ('tensor', 'inner'), pairs))  5.71 us
    ppermute x13, waiting for transfers between devices, swap_with(): return lax.ppermute(value, axis, [(i, i ^ step) for i in range(count)])  4.88 us
    pallas_call x1, Pallas kernels, first_gate_up(): pl.pallas_call(functools.partial(first_gate_up_kernel, slots, count), out...  2 us
    pallas_call x1, Pallas kernels, second_gate_up(): pl.pallas_call(functools.partial(second_gate_up_kernel, first, count), ou...  2 us
    pallas_call x1, Pallas kernels, attend(): pl.pallas_call(functools.partial(attend_kernel, slots, len(parts)), out_s...  1.49 us
  transfers between devices with their start and end apart: 25, of which 10 were waited for; matrix products, arithmetic and copies ran while one was open for 0% of the time, Pallas kernels for 21%

profile of v23, /device:TPU:0, one launch (start us, length us, event | category | flops | bytes accessed | tf_op | source)
XLA Modules:
  0.0 59.8 jit_solution(2279706275283831208)
XLA Ops:
  0.0 4.0 %collective-permute-start = (bf16[2,2048]{1,0:T(2,128)(2,1)}, bf16[2,2048]{1,0:T(2,128)(2,1)S(1)}, u32[]{:S(2)}, u32[]{:S(2)}) collective-permute-start(bf16[2,2048]{1,0:T(2,128)(2,1)} %refs_5_.1), channel_id=1, source_target_pairs={{0,8},{4,12},{8,0},{12,4},{1,9},{5,13},{9,1},{13,5},{2,10},{6,14},... | collective-permute-start | bytes 24584 | tf_op jit(solution)/shard_map/ppermute | solution.py:31
  4.0 1.3 %collective-permute-start.1 = (bf16[2,2048]{1,0:T(2,128)(2,1)}, bf16[2,2048]{1,0:T(2,128)(2,1)S(1)}, u32[]{:S(2)}, u32[]{:S(2)}) collective-permute-start(bf16[2,2048]{1,0:T(2,128)(2,1)} %refs_5_.1), channel_id=1, source_target_pairs={{0,12},{4,8},{8,4},{12,0},{1,13},{5,9},{9,5},{13,1},{2,14},{6,10},... | collective-permute-start | bytes 24584 | tf_op jit(solution)/shard_map/ppermute | solution.py:31
  5.4 0.2 collective-permute-start.2
  5.6 2.7 %load.5 = (bf16[2,2048]{1,0:T(2,128)(2,1)S(1)}, bf16[2048]{0:T(1024)(128)(2,1)S(1)}, bf16[2048]{0:T(1024)(128)(2,1)S(1)}, bf16[2048,256]{1,0:T(8,128)(2,1)S(1)}, bf16[2048,1024]{1,0:T(8,128)(2,1)S(1)}) custom-call(bf16[2,2048]{1,0:T(2,128)(2,1)} %refs_5_.1, bf16[2048]{0:T(1024)(128)(2,1)} %refs_1_.1, bf16[2048]{0:T(1024)(128)(2,1)} %refs_2_.1, ...), custom_call_target="tpu_custom_call" | custom-call | bytes 5259264 | tf_op jit(solution)/shard_map/load/pallas_call | solution.py:159
  8.4 0.0 collective-permute-done.refs_0_
  8.4 1.3 %collective-permute-done.1.refs_1_ = bf16[2,2048]{1,0:T(2,128)(2,1)S(1)} collective-permute-done((bf16[2,2048]{1,0:T(2,128)(2,1)}, bf16[2,2048]{1,0:T(2,128)(2,1)S(1)}, u32[]{:S(2)}, u32[]{:S(2)}) %collective-permute-start.1) | collective-permute-done | bytes 8224 | tf_op jit(solution)/shard_map/ppermute | solution.py:31
  9.7 0.0 collective-permute-done.2.refs_2_
  9.7 0.8 %project_qkv.1 = (f32[8,2048]{1,0:T(8,128)S(1)}, bf16[2,1408]{1,0:T(2,128)(2,1)S(1)}, bf16[2,1408]{1,0:T(2,128)(2,1)S(1)}, bf16[2,1408]{1,0:T(2,128)(2,1)S(1)}, bf16[2,1408]{1,0:T(2,128)(2,1)S(1)}) custom-call(bf16[2048]{0:T(1024)(128)(2,1)S(1)} %get-tuple-element.51.gain_ref, bf16[2048,1024]{1,0:T(8,128)(2,1)S(1)} %get-tuple-element.52.wq_ref, ...), custom_call_target="tpu_custom_call" | custom-call | tf_op jit(solution)/shard_map/project_qkv/pallas_call | solution.py:212
  10.5 0.3 collective-permute-start.3
  10.8 1.5 %collective-permute-start.4 = (bf16[2,1408]{1,0:T(2,128)(2,1)S(1)}, bf16[2,1408]{1,0:T(2,128)(2,1)S(1)}, u32[]{:S(2)}, u32[]{:S(2)}) collective-permute-start(bf16[2,1408]{1,0:T(2,128)(2,1)S(1)} %get-tuple-element.60), channel_id=1, source_target_pairs={{0,9},{1,8},{2,11},{3,10},{4,13},{5,12},{6,15},{7,14},{8,1},{9,0},... | collective-permute-start | bytes 16904 | tf_op jit(solution)/shard_map/ppermute | solution.py:50
  12.3 0.7 %collective-permute-start.5 = (bf16[2,1408]{1,0:T(2,128)(2,1)S(1)}, bf16[2,1408]{1,0:T(2,128)(2,1)S(1)}, u32[]{:S(2)}, u32[]{:S(2)}) collective-permute-start(bf16[2,1408]{1,0:T(2,128)(2,1)S(1)} %get-tuple-element.61), channel_id=1, source_target_pairs={{0,5},{1,4},{2,7},{3,6},{4,1},{5,0},{6,3},{7,2},{8,13},{9,12},{10,... | collective-permute-start | bytes 16904 | tf_op jit(solution)/shard_map/ppermute | solution.py:50
  13.0 0.1 fusion.4
  13.1 1.6 %load.6.key_ref = bf16[2,4096,128]{2,1,0:T(8,128)(2,1)S(1)} custom-call(bf16[2,4096,128]{2,1,0:T(8,128)(2,1)} %bitcast.8, f32[8,2048]{1,0:T(8,128)S(1)} %get-tuple-element.56.refs_1_.rows_ref), custom_call_target="tpu_custom_call" | custom-call | bytes 2097152 | tf_op jit(solution)/shard_map/load/pallas_call | solution.py:159
  14.7 0.7 %collective-permute-done.3.refs_0_ = bf16[2,1408]{1,0:T(2,128)(2,1)S(1)} collective-permute-done((bf16[2,1408]{1,0:T(2,128)(2,1)S(1)}, bf16[2,1408]{1,0:T(2,128)(2,1)S(1)}, u32[]{:S(2)}, u32[]{:S(2)}) %collective-permute-start.3) | collective-permute-done | bytes 5664 | tf_op jit(solution)/shard_map/ppermute | solution.py:50
  15.4 0.0 collective-permute-done.4.refs_1_
  15.4 0.0 collective-permute-done.5.refs_2_
  15.5 2.4 %collective-permute-start.6 = (bf16[8,1408]{1,0:T(8,128)(2,1)S(1)}, bf16[8,1408]{1,0:T(8,128)(2,1)S(1)}, u32[]{:S(2)}, u32[]{:S(2)}) collective-permute-start(bf16[8,1408]{1,0:T(8,128)(2,1)S(1)} %stack.1.refs_1_.refs_0_), channel_id=1, source_target_pairs={{0,3},{1,2},{2,1},{3,0},{4,7},{5,6},{6,5},{7,4},{8,11},{9,10},{10,... | collective-permute-start | bytes 67592 | tf_op jit(solution)/shard_map/ppermute | solution.py:31
  17.9 0.5 collective-permute-start.7
  18.4 0.0 collective-permute-start.8
  18.4 0.1 fusion
  18.5 0.0 copy-start
  18.5 1.8 %load.7.value_ref = bf16[2,4096,128]{2,1,0:T(8,128)(2,1)S(1)} custom-call(bf16[2,4096,128]{2,1,0:T(8,128)(2,1)} %bitcast.9, bf16[8,1408]{1,0:T(8,128)(2,1)S(1)} %stack.1.refs_1_.refs_0_), custom_call_target="tpu_custom_call" | custom-call | bytes 2097152 | tf_op jit(solution)/shard_map/load/pallas_call | solution.py:159
  20.3 1.3 %collective-permute-done.7.refs_2_ = bf16[8,1408]{1,0:T(8,128)(2,1)S(1)} collective-permute-done((bf16[8,1408]{1,0:T(8,128)(2,1)S(1)}, bf16[8,1408]{1,0:T(8,128)(2,1)S(1)}, u32[]{:S(2)}, u32[]{:S(2)}) %collective-permute-start.7) | collective-permute-done | bytes 22560 | tf_op jit(solution)/shard_map/ppermute | solution.py:31
  21.7 0.1 broadcast_in_dim.10.lengths_ref
  21.8 1.5 %attend.1.refs_1_.refs_3_ = bf16[80,128]{1,0:T(8,128)(2,1)S(1)} custom-call(s32[2,128]{1,0:T(2,128)S(1)} %broadcast_in_dim.10.lengths_ref, f32[8,128]{1,0:T(8,128)S(1)} %bitcast.6, f32[8,128]{1,0:T(8,128)S(1)} %bitcast.7, bf16[2,4096,128]{2,1,0:T(8,128)(2,1)S(1)} %load.6.key_ref, bf16[2,4096,128]{2,1,0:T(8,128)(2,1)S(1)} %load.7.value_ref, ...), custom_call_target="tpu_custom_call" | custom-call | tf_op jit(solution)/shard_map/attend/pallas_call | solution.py:356
  23.2 0.6 collective-permute-start.10
  23.8 0.0 collective-permute-start.11
  23.9 1.6 %collective-permute-start.9 = (bf16[80,128]{1,0:T(8,128)(2,1)S(1)}, bf16[80,128]{1,0:T(8,128)(2,1)S(1)}, u32[]{:S(2)}, u32[]{:S(2)}) collective-permute-start(bf16[80,128]{1,0:T(8,128)(2,1)S(1)} %attend.1.refs_1_.refs_3_), channel_id=1, source_target_pairs={{0,1},{1,0},{2,3},{3,2},{4,5},{5,4},{6,7},{7,6},{8,9},{9,8},{10,11... | collective-permute-start | bytes 61448 | tf_op jit(solution)/shard_map/ppermute | solution.py:31
  25.5 1.5 %load.8.upper_ref = bf16[512,2048]{1,0:T(8,128)(2,1)S(1)} custom-call(bf16[1024,2048]{1,0:T(8,128)(2,1)} %refs_0_.5, bf16[80,128]{1,0:T(8,128)(2,1)S(1)} %attend.1.refs_1_.refs_3_), custom_call_target="tpu_custom_call" | custom-call | bytes 2097152 | tf_op jit(solution)/shard_map/load/pallas_call | solution.py:159
  27.0 0.3 collective-permute-done.10.refs_1_
  27.3 0.0 copy-start.1
  27.3 0.3 combine.1
  27.6 1.7 %collective-permute-start.12 = (bf16[2,1024]{1,0:T(2,128)(2,1)S(1)}, bf16[2,1024]{1,0:T(2,128)(2,1)S(1)}, u32[]{:S(2)}, u32[]{:S(2)}) collective-permute-start(bf16[2,1024]{1,0:T(2,128)(2,1)S(1)} %get-tuple-element.75), channel_id=1, source_target_pairs={{0,13},{1,12},{2,15},{3,14},{4,9},{5,8},{6,11},{7,10},{8,5},{9,4},... | collective-permute-start | bytes 12296 | tf_op jit(solution)/shard_map/ppermute | solution.py:50
  29.2 0.4 collective-permute-start.13
  29.6 1.8 %collective-permute-start.14 = (bf16[2,1024]{1,0:T(2,128)(2,1)S(1)}, bf16[2,1024]{1,0:T(2,128)(2,1)S(1)}, u32[]{:S(2)}, u32[]{:S(2)}) collective-permute-start(bf16[2,1024]{1,0:T(2,128)(2,1)S(1)} %get-tuple-element.77), channel_id=1, source_target_pairs={{0,5},{1,4},{2,7},{3,6},{4,1},{5,0},{6,3},{7,2},{8,13},{9,12},{10,... | collective-permute-start | bytes 12296 | tf_op jit(solution)/shard_map/ppermute | solution.py:50
  31.4 1.6 %load.9.lower_ref = bf16[512,2048]{1,0:T(8,128)(2,1)S(1)} custom-call(bf16[1024,2048]{1,0:T(8,128)(2,1)} %refs_0_.5, bf16[2,1024]{1,0:T(2,128)(2,1)S(1)} %get-tuple-element.83.refs_1_.refs_3_), custom_call_target="tpu_custom_call" | custom-call | bytes 2097152 | tf_op jit(solution)/shard_map/load/pallas_call | solution.py:159
  33.0 0.1 collective-permute-done.13.refs_1_
  33.2 0.0 collective-permute-done.14.refs_2_
  33.2 0.8 %project_out.1 = (bf16[8,2048]{1,0:T(8,128)(2,1)S(1)}, bf16[8,2048]{1,0:T(8,128)(2,1)S(1)}, bf16[8,2048]{1,0:T(8,128)(2,1)S(1)}, bf16[8,2048]{1,0:T(8,128)(2,1)S(1)}) custom-call(bf16[512,2048]{1,0:T(8,128)(2,1)S(1)} %load.8.upper_ref, bf16[512,2048]{1,0:T(8,128)(2,1)S(1)} %load.9.lower_ref, bf16[2,1024]{1,0:T(2,128)(2,1)S(1)} %collective-permute-done.12.refs_0_, ...), custom_call_target="tpu_custom_call" | custom-call | tf_op jit(solution)/shard_map/project_out/pallas_call | solution.py:453
  34.0 1.9 %collective-permute-start.15 = (bf16[8,2048]{1,0:T(8,128)(2,1)S(1)}, bf16[8,2048]{1,0:T(8,128)(2,1)S(1)}, u32[]{:S(2)}, u32[]{:S(2)}) collective-permute-start(bf16[8,2048]{1,0:T(8,128)(2,1)S(1)} %get-tuple-element.84), channel_id=1, source_target_pairs={{0,12},{1,13},{2,14},{3,15},{4,8},{5,9},{6,10},{7,11},{8,4},{9,5},... | collective-permute-start | bytes 98312 | tf_op jit(solution)/shard_map/ppermute | solution.py:50
  35.9 1.2 %collective-permute-start.16 = (bf16[8,2048]{1,0:T(8,128)(2,1)S(1)}, bf16[8,2048]{1,0:T(8,128)(2,1)S(1)}, u32[]{:S(2)}, u32[]{:S(2)}) collective-permute-start(bf16[8,2048]{1,0:T(8,128)(2,1)S(1)} %get-tuple-element.85), channel_id=1, source_target_pairs={{0,8},{1,9},{2,10},{3,11},{4,12},{5,13},{6,14},{7,15},{8,0},{9,1},... | collective-permute-start | bytes 98312 | tf_op jit(solution)/shard_map/ppermute | solution.py:50
  37.1 1.3 %collective-permute-start.17 = (bf16[8,2048]{1,0:T(8,128)(2,1)S(1)}, bf16[8,2048]{1,0:T(8,128)(2,1)S(1)}, u32[]{:S(2)}, u32[]{:S(2)}) collective-permute-start(bf16[8,2048]{1,0:T(8,128)(2,1)S(1)} %get-tuple-element.86), channel_id=1, source_target_pairs={{0,4},{1,5},{2,6},{3,7},{4,0},{5,1},{6,2},{7,3},{8,12},{9,13},{10,... | collective-permute-start | bytes 98312 | tf_op jit(solution)/shard_map/ppermute | solution.py:50
  38.4 1.7 %collective-permute-done.15.refs_0_ = bf16[8,2048]{1,0:T(8,128)(2,1)S(1)} collective-permute-done((bf16[8,2048]{1,0:T(8,128)(2,1)S(1)}, bf16[8,2048]{1,0:T(8,128)(2,1)S(1)}, u32[]{:S(2)}, u32[]{:S(2)}) %collective-permute-start.15) | collective-permute-done | bytes 32800 | tf_op jit(solution)/shard_map/ppermute | solution.py:50
  40.1 1.1 %collective-permute-done.16.refs_1_ = bf16[8,2048]{1,0:T(8,128)(2,1)S(1)} collective-permute-done((bf16[8,2048]{1,0:T(8,128)(2,1)S(1)}, bf16[8,2048]{1,0:T(8,128)(2,1)S(1)}, u32[]{:S(2)}, u32[]{:S(2)}) %collective-permute-start.16) | collective-permute-done | bytes 32800 | tf_op jit(solution)/shard_map/ppermute | solution.py:50
  41.1 0.0 collective-permute-done.17.refs_2_
  41.2 2.0 %first_gate_up.1 = (bf16[8,3712]{1,0:T(8,128)(2,1)S(1)}, f32[2,2048]{1,0:T(2,128)S(1)}, bf16[8,2048]{1,0:T(8,128)(2,1)S(1)}) custom-call(f32[8,2048]{1,0:T(8,128)S(1)} %get-tuple-element.56.refs_1_.rows_ref, bf16[2048]{0:T(1024)(128)(2,1)S(1)} %get-tuple-element.57.gain_ref, bf16[2048,3584]{1,0:T(8,128)(2,1)S(1)} %copy-done, ...), custom_call_target="tpu_custom_call" | custom-call | flops 117440512 | bytes 14680064 | tf_op jit(solution)/shard_map/first_gate_up/pallas_call | solution.py:509
  43.2 0.0 slice-start.1
  43.2 0.0 slice-start.3
  43.2 2.0 %second_gate_up.1.first_ref = bf16[8,3584]{1,0:T(8,128)(2,1)S(1)} custom-call(bf16[8,2048]{1,0:T(8,128)(2,1)S(1)} %get-tuple-element.89.scaled_ref, bf16[2048,3584]{1,0:T(8,128)(2,1)S(1)} %copy-done, bf16[2048,3584]{1,0:T(8,128)(2,1)S(1)} %copy-done.2), custom_call_target="tpu_custom_call" | custom-call | flops 117440512 | bytes 14680064 | tf_op jit(solution)/shard_map/second_gate_up/pallas_call | solution.py:538
  45.2 0.5 collective-permute-start.18
  45.7 0.0 collective-permute-done.20.second_ref
  45.7 1.3 %collective-permute-start.21 = (bf16[8,3712]{1,0:T(8,128)(2,1)S(1)}, bf16[8,3712]{1,0:T(8,128)(2,1)S(1)}, u32[]{:S(2)}, u32[]{:S(2)}) collective-permute-start(bf16[8,3712]{1,0:T(8,128)(2,1)S(1)} %pair_sum.3.near_ref), channel_id=1, source_target_pairs={{0,2},{1,3},{2,0},{3,1},{4,6},{5,7},{6,4},{7,5},{8,10},{9,11},{10,... | collective-permute-start | bytes 178184 | tf_op jit(solution)/shard_map/ppermute | solution.py:31
  47.0 0.9 %collective-permute-start.19 = (bf16[8,3584]{1,0:T(8,128)(2,1)S(1)}, bf16[8,3584]{1,0:T(8,128)(2,1)S(1)}, u32[]{:S(2)}, u32[]{:S(2)}) collective-permute-start(bf16[8,3584]{1,0:T(8,128)(2,1)S(1)} %pair_sum.2.after_ref.near_ref), channel_id=1, source_target_pairs={{0,2},{1,3},{2,0},{3,1},{4,6},{5,7},{6,4},{7,5},{8,10},{9,11},{10,... | collective-permute-start | bytes 172040 | tf_op jit(solution)/shard_map/ppermute | solution.py:31
  47.9 0.5 slice-done.3
  48.4 1.9 %collective-permute-done.21.far_ref = bf16[8,3712]{1,0:T(8,128)(2,1)S(1)} collective-permute-done((bf16[8,3712]{1,0:T(8,128)(2,1)S(1)}, bf16[8,3712]{1,0:T(8,128)(2,1)S(1)}, u32[]{:S(2)}, u32[]{:S(2)}) %collective-permute-start.21) | collective-permute-done | bytes 59424 | tf_op jit(solution)/shard_map/ppermute | solution.py:31
  50.4 1.1 %first_down.1 = (f32[8,2048]{1,0:T(8,128)S(1)}, f32[8,128]{1,0:T(8,128)S(1)}) custom-call(bf16[8,3712]{1,0:T(8,128)(2,1)S(1)} %pair_sum.3.near_ref, bf16[8,3712]{1,0:T(8,128)(2,1)S(1)} %collective-permute-done.21.far_ref, bf16[3584,2048]{1,0:T(8,128)(2,1)S(1)} %bitcast.5, f32[8,128]{1,0:T(8,128)S(1)} %hold.1.token_ref), custom_call_target="tpu_custom_call" | custom-call | flops 58720256 | bytes 7340032 | tf_op jit(solution)/shard_map/first_down/pallas_call | solution.py:576
  51.5 1.1 %second_down.1 = (bf16[2,2048]{1,0:T(2,128)(2,1)S(1)}, bf16[2,2048]{1,0:T(2,128)(2,1)S(1)}, bf16[2,2048]{1,0:T(2,128)(2,1)S(1)}, bf16[2,2048]{1,0:T(2,128)(2,1)S(1)}) custom-call(bf16[8,3584]{1,0:T(8,128)(2,1)S(1)} %pair_sum.2.after_ref.near_ref, bf16[8,3584]{1,0:T(8,128)(2,1)S(1)} %collective-permute-done.19.far_ref, bf16[3584,2048]{1,0:T(8,128)(2,1)S(1)} %bitcast.5, ...), custom_call_target="tpu_custom_call" | custom-call | tf_op jit(solution)/shard_map/second_down/pallas_call | solution.py:606
  52.6 2.0 %collective-permute-start.22 = (bf16[2,2048]{1,0:T(2,128)(2,1)S(1)}, bf16[2,2048]{1,0:T(2,128)(2,1)S(1)}, u32[]{:S(2)}, u32[]{:S(2)}) collective-permute-start(bf16[2,2048]{1,0:T(2,128)(2,1)S(1)} %get-tuple-element.93), channel_id=1, source_target_pairs={{0,12},{1,13},{2,14},{3,15},{4,8},{5,9},{6,10},{7,11},{8,4},{9,5},... | collective-permute-start | bytes 24584 | tf_op jit(solution)/shard_map/ppermute | solution.py:50
  54.6 0.7 %collective-permute-start.23 = (bf16[2,2048]{1,0:T(2,128)(2,1)S(1)}, bf16[2,2048]{1,0:T(2,128)(2,1)S(1)}, u32[]{:S(2)}, u32[]{:S(2)}) collective-permute-start(bf16[2,2048]{1,0:T(2,128)(2,1)S(1)} %get-tuple-element.94), channel_id=1, source_target_pairs={{0,8},{1,9},{2,10},{3,11},{4,12},{5,13},{6,14},{7,15},{8,0},{9,1},... | collective-permute-start | bytes 24584 | tf_op jit(solution)/shard_map/ppermute | solution.py:50
  55.3 1.8 %collective-permute-start.24 = (bf16[2,2048]{1,0:T(2,128)(2,1)S(1)}, bf16[2,2048]{1,0:T(2,128)(2,1)S(1)}, u32[]{:S(2)}, u32[]{:S(2)}) collective-permute-start(bf16[2,2048]{1,0:T(2,128)(2,1)S(1)} %get-tuple-element.95), channel_id=1, source_target_pairs={{0,4},{1,5},{2,6},{3,7},{4,0},{5,1},{6,2},{7,3},{8,12},{9,13},{10,... | collective-permute-start | bytes 24584 | tf_op jit(solution)/shard_map/ppermute | solution.py:50
  57.1 1.1 %collective-permute-done.22.refs_0_ = bf16[2,2048]{1,0:T(2,128)(2,1)S(1)} collective-permute-done((bf16[2,2048]{1,0:T(2,128)(2,1)S(1)}, bf16[2,2048]{1,0:T(2,128)(2,1)S(1)}, u32[]{:S(2)}, u32[]{:S(2)}) %collective-permute-start.22) | collective-permute-done | bytes 8224 | tf_op jit(solution)/shard_map/ppermute | solution.py:50
  58.2 1.0 %collective-permute-done.23.refs_1_ = bf16[2,2048]{1,0:T(2,128)(2,1)S(1)} collective-permute-done((bf16[2,2048]{1,0:T(2,128)(2,1)S(1)}, bf16[2,2048]{1,0:T(2,128)(2,1)S(1)}, u32[]{:S(2)}, u32[]{:S(2)}) %collective-permute-start.23) | collective-permute-done | bytes 8224 | tf_op jit(solution)/shard_map/ppermute | solution.py:50
  59.2 0.0 collective-permute-done.24.refs_2_
  59.2 0.6 %finish.1 = bf16[2,2048]{1,0:T(2,128)(2,1)} custom-call(f32[2,2048]{1,0:T(2,128)S(1)} %get-tuple-element.88.updated_ref, bf16[2,2048]{1,0:T(2,128)(2,1)S(1)} %collective-permute-done.22.refs_0_, bf16[2,2048]{1,0:T(2,128)(2,1)S(1)} %collective-permute-done.23.refs_1_, bf16[2,2048]{1,0:T(2,128)(2,1)S(1)} %collective-permute-done.24.refs_2_, ...), custom_call_target="tpu_custom_call" | custom-call | tf_op jit(solution)/shard_map/finish/pallas_call | solution.py:639
  (27 shorter events, 0.1 us)
Async XLA Ops:
  0.0 8.4 %collective-permute-start = (bf16[2,2048]{1,0:T(2,128)(2,1)}, bf16[2,2048]{1,0:T(2,128)(2,1)S(1)}, u32[]{:S(2)}, u32[]{:S(2)}) collective-permute-start(bf16[2,2048]{1,0:T(2,128)(2,1)} %refs_5_.1), channel_id=1, source_target_pairs={{0,8},{4,12},{8,0},{12,4},{1,9},{5,13},{9,1},{13,5},{2,10},{6,14},... | collective-permute-start | bytes 24584 | tf_op jit(solution)/shard_map/ppermute | solution.py:31
  4.0 5.7 %collective-permute-start.1 = (bf16[2,2048]{1,0:T(2,128)(2,1)}, bf16[2,2048]{1,0:T(2,128)(2,1)S(1)}, u32[]{:S(2)}, u32[]{:S(2)}) collective-permute-start(bf16[2,2048]{1,0:T(2,128)(2,1)} %refs_5_.1), channel_id=1, source_target_pairs={{0,12},{4,8},{8,4},{12,0},{1,13},{5,9},{9,5},{13,1},{2,14},{6,10},... | collective-permute-start | bytes 24584 | tf_op jit(solution)/shard_map/ppermute | solution.py:31
  5.4 4.3 %collective-permute-start.2 = (bf16[2,2048]{1,0:T(2,128)(2,1)}, bf16[2,2048]{1,0:T(2,128)(2,1)S(1)}, u32[]{:S(2)}, u32[]{:S(2)}) collective-permute-start(bf16[2,2048]{1,0:T(2,128)(2,1)} %refs_5_.1), channel_id=1, source_target_pairs={{0,4},{4,0},{8,12},{12,8},{1,5},{5,1},{9,13},{13,9},{2,6},{6,2},{1... | collective-permute-start | bytes 24584 | tf_op jit(solution)/shard_map/ppermute | solution.py:31
  5.6 7.4 %copy-start.3 = (s32[8]{0:T(128)S(1)}, s32[8]{0:T(128)}, u32[]{:S(2)}) copy-start(s32[8]{0:T(128)} %param.23) | copy-start | bytes 100
  10.5 4.9 %collective-permute-start.3 = (bf16[2,1408]{1,0:T(2,128)(2,1)S(1)}, bf16[2,1408]{1,0:T(2,128)(2,1)S(1)}, u32[]{:S(2)}, u32[]{:S(2)}) collective-permute-start(bf16[2,1408]{1,0:T(2,128)(2,1)S(1)} %get-tuple-element.59), channel_id=1, source_target_pairs={{0,13},{1,12},{2,15},{3,14},{4,9},{5,8},{6,11},{7,10},{8,5},{9,4},... | collective-permute-start | bytes 16904 | tf_op jit(solution)/shard_map/ppermute | solution.py:50
  10.8 4.6 %collective-permute-start.4 = (bf16[2,1408]{1,0:T(2,128)(2,1)S(1)}, bf16[2,1408]{1,0:T(2,128)(2,1)S(1)}, u32[]{:S(2)}, u32[]{:S(2)}) collective-permute-start(bf16[2,1408]{1,0:T(2,128)(2,1)S(1)} %get-tuple-element.60), channel_id=1, source_target_pairs={{0,9},{1,8},{2,11},{3,10},{4,13},{5,12},{6,15},{7,14},{8,1},{9,0},... | collective-permute-start | bytes 16904 | tf_op jit(solution)/shard_map/ppermute | solution.py:50
  12.3 3.2 %collective-permute-start.5 = (bf16[2,1408]{1,0:T(2,128)(2,1)S(1)}, bf16[2,1408]{1,0:T(2,128)(2,1)S(1)}, u32[]{:S(2)}, u32[]{:S(2)}) collective-permute-start(bf16[2,1408]{1,0:T(2,128)(2,1)S(1)} %get-tuple-element.61), channel_id=1, source_target_pairs={{0,5},{1,4},{2,7},{3,6},{4,1},{5,0},{6,3},{7,2},{8,13},{9,12},{10,... | collective-permute-start | bytes 16904 | tf_op jit(solution)/shard_map/ppermute | solution.py:50
  15.5 4.8 %collective-permute-start.6 = (bf16[8,1408]{1,0:T(8,128)(2,1)S(1)}, bf16[8,1408]{1,0:T(8,128)(2,1)S(1)}, u32[]{:S(2)}, u32[]{:S(2)}) collective-permute-start(bf16[8,1408]{1,0:T(8,128)(2,1)S(1)} %stack.1.refs_1_.refs_0_), channel_id=1, source_target_pairs={{0,3},{1,2},{2,1},{3,0},{4,7},{5,6},{6,5},{7,4},{8,11},{9,10},{10,... | collective-permute-start | bytes 67592 | tf_op jit(solution)/shard_map/ppermute | solution.py:31
  17.9 3.8 %collective-permute-start.7 = (bf16[8,1408]{1,0:T(8,128)(2,1)S(1)}, bf16[8,1408]{1,0:T(8,128)(2,1)S(1)}, u32[]{:S(2)}, u32[]{:S(2)}) collective-permute-start(bf16[8,1408]{1,0:T(8,128)(2,1)S(1)} %stack.1.refs_1_.refs_0_), channel_id=1, source_target_pairs={{0,2},{1,3},{2,0},{3,1},{4,6},{5,7},{6,4},{7,5},{8,10},{9,11},{10,... | collective-permute-start | bytes 67592 | tf_op jit(solution)/shard_map/ppermute | solution.py:31
  18.4 3.3 %collective-permute-start.8 = (bf16[8,1408]{1,0:T(8,128)(2,1)S(1)}, bf16[8,1408]{1,0:T(8,128)(2,1)S(1)}, u32[]{:S(2)}, u32[]{:S(2)}) collective-permute-start(bf16[8,1408]{1,0:T(8,128)(2,1)S(1)} %stack.1.refs_1_.refs_0_), channel_id=1, source_target_pairs={{0,1},{1,0},{2,3},{3,2},{4,5},{5,4},{6,7},{7,6},{8,9},{9,8},{10,11... | collective-permute-start | bytes 67592 | tf_op jit(solution)/shard_map/ppermute | solution.py:31
  18.5 8.8 %copy-start = (bf16[2048,3584]{1,0:T(8,128)(2,1)S(1)}, bf16[2048,3584]{1,0:T(8,128)(2,1)}, u32[]{:S(2)}) copy-start(bf16[2048,3584]{1,0:T(8,128)(2,1)} %gate_ref.3) | copy-start | bytes 44040196
  23.2 4.0 %collective-permute-start.10 = (bf16[80,128]{1,0:T(8,128)(2,1)S(1)}, bf16[80,128]{1,0:T(8,128)(2,1)S(1)}, u32[]{:S(2)}, u32[]{:S(2)}) collective-permute-start(bf16[80,128]{1,0:T(8,128)(2,1)S(1)} %attend.1.refs_1_.refs_3_), channel_id=1, source_target_pairs={{0,2},{1,3},{2,0},{3,1},{4,6},{5,7},{6,4},{7,5},{8,10},{9,11},{10,... | collective-permute-start | bytes 61448 | tf_op jit(solution)/shard_map/ppermute | solution.py:31
  23.8 3.4 %collective-permute-start.11 = (bf16[80,128]{1,0:T(8,128)(2,1)S(1)}, bf16[80,128]{1,0:T(8,128)(2,1)S(1)}, u32[]{:S(2)}, u32[]{:S(2)}) collective-permute-start(bf16[80,128]{1,0:T(8,128)(2,1)S(1)} %attend.1.refs_1_.refs_3_), channel_id=1, source_target_pairs={{0,3},{1,2},{2,1},{3,0},{4,7},{5,6},{6,5},{7,4},{8,11},{9,10},{10,... | collective-permute-start | bytes 61448 | tf_op jit(solution)/shard_map/ppermute | solution.py:31
  23.9 3.4 %collective-permute-start.9 = (bf16[80,128]{1,0:T(8,128)(2,1)S(1)}, bf16[80,128]{1,0:T(8,128)(2,1)S(1)}, u32[]{:S(2)}, u32[]{:S(2)}) collective-permute-start(bf16[80,128]{1,0:T(8,128)(2,1)S(1)} %attend.1.refs_1_.refs_3_), channel_id=1, source_target_pairs={{0,1},{1,0},{2,3},{3,2},{4,5},{5,4},{6,7},{7,6},{8,9},{9,8},{10,11... | collective-permute-start | bytes 61448 | tf_op jit(solution)/shard_map/ppermute | solution.py:31
  27.3 5.9 %copy-start.1 = (bf16[2048,3584]{1,0:T(8,128)(2,1)S(1)}, bf16[2048,3584]{1,0:T(8,128)(2,1)}, u32[]{:S(2)}) copy-start(bf16[2048,3584]{1,0:T(8,128)(2,1)} %up_ref.3) | copy-start | bytes 44040196
  27.6 5.5 %collective-permute-start.12 = (bf16[2,1024]{1,0:T(2,128)(2,1)S(1)}, bf16[2,1024]{1,0:T(2,128)(2,1)S(1)}, u32[]{:S(2)}, u32[]{:S(2)}) collective-permute-start(bf16[2,1024]{1,0:T(2,128)(2,1)S(1)} %get-tuple-element.75), channel_id=1, source_target_pairs={{0,13},{1,12},{2,15},{3,14},{4,9},{5,8},{6,11},{7,10},{8,5},{9,4},... | collective-permute-start | bytes 12296 | tf_op jit(solution)/shard_map/ppermute | solution.py:50
  29.2 3.9 %collective-permute-start.13 = (bf16[2,1024]{1,0:T(2,128)(2,1)S(1)}, bf16[2,1024]{1,0:T(2,128)(2,1)S(1)}, u32[]{:S(2)}, u32[]{:S(2)}) collective-permute-start(bf16[2,1024]{1,0:T(2,128)(2,1)S(1)} %get-tuple-element.76), channel_id=1, source_target_pairs={{0,9},{1,8},{2,11},{3,10},{4,13},{5,12},{6,15},{7,14},{8,1},{9,0},... | collective-permute-start | bytes 12296 | tf_op jit(solution)/shard_map/ppermute | solution.py:50
  29.6 3.5 %collective-permute-start.14 = (bf16[2,1024]{1,0:T(2,128)(2,1)S(1)}, bf16[2,1024]{1,0:T(2,128)(2,1)S(1)}, u32[]{:S(2)}, u32[]{:S(2)}) collective-permute-start(bf16[2,1024]{1,0:T(2,128)(2,1)S(1)} %get-tuple-element.77), channel_id=1, source_target_pairs={{0,5},{1,4},{2,7},{3,6},{4,1},{5,0},{6,3},{7,2},{8,13},{9,12},{10,... | collective-permute-start | bytes 12296 | tf_op jit(solution)/shard_map/ppermute | solution.py:50
  33.2 8.0 %copy-start.2 = (bf16[2048,3584]{1,0:T(8,128)(2,1)S(1)}, bf16[2048,3584]{1,0:T(8,128)(2,1)}, u32[]{:S(2)}) copy-start(bf16[2048,3584]{1,0:T(8,128)(2,1)} %up_ref.3) | copy-start | bytes 44040196
  34.0 6.1 %collective-permute-start.15 = (bf16[8,2048]{1,0:T(8,128)(2,1)S(1)}, bf16[8,2048]{1,0:T(8,128)(2,1)S(1)}, u32[]{:S(2)}, u32[]{:S(2)}) collective-permute-start(bf16[8,2048]{1,0:T(8,128)(2,1)S(1)} %get-tuple-element.84), channel_id=1, source_target_pairs={{0,12},{1,13},{2,14},{3,15},{4,8},{5,9},{6,10},{7,11},{8,4},{9,5},... | collective-permute-start | bytes 98312 | tf_op jit(solution)/shard_map/ppermute | solution.py:50
  35.9 5.2 %collective-permute-start.16 = (bf16[8,2048]{1,0:T(8,128)(2,1)S(1)}, bf16[8,2048]{1,0:T(8,128)(2,1)S(1)}, u32[]{:S(2)}, u32[]{:S(2)}) collective-permute-start(bf16[8,2048]{1,0:T(8,128)(2,1)S(1)} %get-tuple-element.85), channel_id=1, source_target_pairs={{0,8},{1,9},{2,10},{3,11},{4,12},{5,13},{6,14},{7,15},{8,0},{9,1},... | collective-permute-start | bytes 98312 | tf_op jit(solution)/shard_map/ppermute | solution.py:50
  37.1 4.1 %collective-permute-start.17 = (bf16[8,2048]{1,0:T(8,128)(2,1)S(1)}, bf16[8,2048]{1,0:T(8,128)(2,1)S(1)}, u32[]{:S(2)}, u32[]{:S(2)}) collective-permute-start(bf16[8,2048]{1,0:T(8,128)(2,1)S(1)} %get-tuple-element.86), channel_id=1, source_target_pairs={{0,4},{1,5},{2,6},{3,7},{4,0},{5,1},{6,2},{7,3},{8,12},{9,13},{10,... | collective-permute-start | bytes 98312 | tf_op jit(solution)/shard_map/ppermute | solution.py:50
  43.1 2.6 %collective-permute-start.20 = (bf16[8,3712]{1,0:T(8,128)(2,1)S(1)}, bf16[8,3712]{1,0:T(8,128)(2,1)S(1)}, u32[]{:S(2)}, u32[]{:S(2)}) collective-permute-start(bf16[8,3712]{1,0:T(8,128)(2,1)S(1)} %get-tuple-element.90.first_ref), channel_id=1, source_target_pairs={{0,1},{1,0},{2,3},{3,2},{4,5},{5,4},{6,7},{7,6},{8,9},{9,8},{10,11... | collective-permute-start | bytes 178184 | tf_op jit(solution)/shard_map/ppermute | solution.py:31
  43.2 4.8 %slice-start = ((s8[14680064]{0:T(1024)(128)(4,1)}), s8[4194304]{0:T(1024)(128)(4,1)S(1)}, s32[]{:S(2)}) async-start(s8[14680064]{0:T(1024)(128)(4,1)} %bitcast.4), calls=%async_computation | async-start | bytes 8388608
  43.2 4.8 %slice-start.1 = ((s8[14680064]{0:T(1024)(128)(4,1)}), s8[4194304]{0:T(1024)(128)(4,1)S(1)}, s32[]{:S(2)}) async-start(s8[14680064]{0:T(1024)(128)(4,1)} %bitcast.4), calls=%async_computation.1 | async-start | bytes 8388608
  43.2 4.7 %slice-start.2 = ((s8[14680064]{0:T(1024)(128)(4,1)}), s8[4194304]{0:T(1024)(128)(4,1)S(1)}, s32[]{:S(2)}) async-start(s8[14680064]{0:T(1024)(128)(4,1)} %bitcast.4), calls=%async_computation.2 | async-start | bytes 8388608
  43.2 5.2 %slice-start.3 = ((s8[14680064]{0:T(1024)(128)(4,1)}), s8[2097152]{0:T(1024)(128)(4,1)S(1)}, s32[]{:S(2)}) async-start(s8[14680064]{0:T(1024)(128)(4,1)} %bitcast.4), calls=%async_computation.3 | async-start | bytes 4194304
  45.2 1.8 %collective-permute-start.18 = (bf16[8,3584]{1,0:T(8,128)(2,1)S(1)}, bf16[8,3584]{1,0:T(8,128)(2,1)S(1)}, u32[]{:S(2)}, u32[]{:S(2)}) collective-permute-start(bf16[8,3584]{1,0:T(8,128)(2,1)S(1)} %second_gate_up.1.first_ref), channel_id=1, source_target_pairs={{0,1},{1,0},{2,3},{3,2},{4,5},{5,4},{6,7},{7,6},{8,9},{9,8},{10,11... | collective-permute-start | bytes 172040 | tf_op jit(solution)/shard_map/ppermute | solution.py:31
  45.7 4.6 %collective-permute-start.21 = (bf16[8,3712]{1,0:T(8,128)(2,1)S(1)}, bf16[8,3712]{1,0:T(8,128)(2,1)S(1)}, u32[]{:S(2)}, u32[]{:S(2)}) collective-permute-start(bf16[8,3712]{1,0:T(8,128)(2,1)S(1)} %pair_sum.3.near_ref), channel_id=1, source_target_pairs={{0,2},{1,3},{2,0},{3,1},{4,6},{5,7},{6,4},{7,5},{8,10},{9,11},{10,... | collective-permute-start | bytes 178184 | tf_op jit(solution)/shard_map/ppermute | solution.py:31
  47.0 4.5 %collective-permute-start.19 = (bf16[8,3584]{1,0:T(8,128)(2,1)S(1)}, bf16[8,3584]{1,0:T(8,128)(2,1)S(1)}, u32[]{:S(2)}, u32[]{:S(2)}) collective-permute-start(bf16[8,3584]{1,0:T(8,128)(2,1)S(1)} %pair_sum.2.after_ref.near_ref), channel_id=1, source_target_pairs={{0,2},{1,3},{2,0},{3,1},{4,6},{5,7},{6,4},{7,5},{8,10},{9,11},{10,... | collective-permute-start | bytes 172040 | tf_op jit(solution)/shard_map/ppermute | solution.py:31
  52.6 5.5 %collective-permute-start.22 = (bf16[2,2048]{1,0:T(2,128)(2,1)S(1)}, bf16[2,2048]{1,0:T(2,128)(2,1)S(1)}, u32[]{:S(2)}, u32[]{:S(2)}) collective-permute-start(bf16[2,2048]{1,0:T(2,128)(2,1)S(1)} %get-tuple-element.93), channel_id=1, source_target_pairs={{0,12},{1,13},{2,14},{3,15},{4,8},{5,9},{6,10},{7,11},{8,4},{9,5},... | collective-permute-start | bytes 24584 | tf_op jit(solution)/shard_map/ppermute | solution.py:50
  54.6 4.5 %collective-permute-start.23 = (bf16[2,2048]{1,0:T(2,128)(2,1)S(1)}, bf16[2,2048]{1,0:T(2,128)(2,1)S(1)}, u32[]{:S(2)}, u32[]{:S(2)}) collective-permute-start(bf16[2,2048]{1,0:T(2,128)(2,1)S(1)} %get-tuple-element.94), channel_id=1, source_target_pairs={{0,8},{1,9},{2,10},{3,11},{4,12},{5,13},{6,14},{7,15},{8,0},{9,1},... | collective-permute-start | bytes 24584 | tf_op jit(solution)/shard_map/ppermute | solution.py:50
  55.3 3.8 %collective-permute-start.24 = (bf16[2,2048]{1,0:T(2,128)(2,1)S(1)}, bf16[2,2048]{1,0:T(2,128)(2,1)S(1)}, u32[]{:S(2)}, u32[]{:S(2)}) collective-permute-start(bf16[2,2048]{1,0:T(2,128)(2,1)S(1)} %get-tuple-element.95), channel_id=1, source_target_pairs={{0,4},{1,5},{2,6},{3,7},{4,0},{5,1},{6,2},{7,3},{8,12},{9,13},{10,... | collective-permute-start | bytes 24584 | tf_op jit(solution)/shard_map/ppermute | solution.py:50
